TPU v7x, 32 devices: a whole 2x2x4 slice. The times are simulated.
32 devices in a mesh: dp: 8 (over z, x), tensor: 4 (over y, core).
Axes of the slice: x: 2, y: 2, z: 4, core: 2. Of those that a mesh axis runs over, the one named last changes fastest.
Arguments:
- tokens: bfloat16 [8192, 768], P(('dp', 'tensor')), may hold values from -6 to 6
- node_counts: int32 [64], P('dp'), may hold values from 4 to 42
- edge_counts: int32 [64], P('dp'), may hold values from 0 to 84
- ln1_gain: float32 [768], replicated, may hold values from 0.25 to 1.75
- ln1_bias: float32 [768], replicated, may hold values from -3 to 3
- qkv_weight: bfloat16 [3, 768, 768], P(None, 'tensor'), may hold values from -0.3125 to 0.3125
- out_weight: bfloat16 [768, 768], P('tensor'), may hold values from -0.875 to 0.875
- ln2_gain: float32 [768], replicated, may hold values from 0.25 to 1.75
- ln2_bias: float32 [768], replicated, may hold values from -3 to 3
- fc1_weight: bfloat16 [768, 768], P('tensor'), may hold values from -0.21875 to 0.21875
- fc1_bias: bfloat16 [768], P('tensor'), may hold values from -3 to 3
- fc2_weight: bfloat16 [768, 768], P('tensor'), may hold values from -0.3125 to 0.3125
- out_grad: bfloat16 [8192, 768], P(('dp', 'tensor')), may hold values from -6 to 6
Outputs:
- result: bfloat16 [8192, 768], P(('dp', 'tensor'))
- grad_tokens: bfloat16 [8192, 768], P(('dp', 'tensor'))
- grad_ln1_gain: float32 [768], replicated
- grad_ln1_bias: float32 [768], replicated
- grad_qkv_weight: float32 [3, 768, 768], P(None, 'tensor')
- grad_out_weight: float32 [768, 768], P('tensor')
- grad_ln2_gain: float32 [768], replicated
- grad_ln2_bias: float32 [768], replicated
- grad_fc1_weight: float32 [768, 768], P('tensor')
- grad_fc1_bias: float32 [768], P('tensor')
- grad_fc2_weight: float32 [768, 768], P('tensor')
All inputs are finite; a program needn't handle non-finite values.
Results may differ from a plain program's by a relative error of at most 0.019.
Values may be sent and summed in bfloat16 or wider, within the bound.
No kernel may reach another device: no remote copies, remote signals or barrier semaphores. Data moves between devices by JAX's collectives and lax.ppermute only.
A program may use at most 64 MiB of HBM per device.

v0:
```python
import jax
import jax.numpy as jnp
from jax import lax
from jax.sharding import PartitionSpec as P

HEAD_DIM = 24
LEN = 128


EPSILON = 1e-05


def layer_norm(values, gain_values, shifts):
    average = jnp.mean(values, axis=-1, keepdims=True)
    centered = values - average
    variance = jnp.mean(centered * centered, axis=-1, keepdims=True)
    return centered * lax.rsqrt(variance + EPSILON) * gain_values + shifts


def gelu_exact(values):
    return jax.nn.gelu(values, approximate=False)


def contract_rows(left_side, right_side):
    return lax.dot_general(
        left_side, right_side, (((0,), (0,)), ((), ())), preferred_element_type=jnp.float32
    )


def contract_cols(left_side, right_side):
    return lax.dot_general(
        left_side, right_side, (((1,), (1,)), ((), ())), preferred_element_type=jnp.float32
    )


def masked_scores(queries, key_rows, valid_keys, score_scale):
    scores = (
        jnp.einsum("mqhd,mkhd->mhqk", queries, key_rows, preferred_element_type=jnp.float32)
        * score_scale
    )
    return jnp.where(valid_keys[:, None, None, :], scores, -1000000000.0)


def attention_forward(queries, key_rows, value_rows, valid_keys, score_scale):
    scores = masked_scores(queries, key_rows, valid_keys, score_scale)
    largest = jnp.max(scores, axis=-1, keepdims=True)
    weights = jnp.exp(scores - largest)
    totals = jnp.sum(weights, axis=-1, keepdims=True)
    probabilities = (weights / totals).astype(jnp.bfloat16)
    attended = jnp.einsum(
        "mhqk,mkhd->mqhd", probabilities, value_rows, preferred_element_type=jnp.float32
    )
    return (attended, largest + jnp.log(totals))


def attention_backward(
    queries, key_rows, value_rows, valid_keys, score_scale, log_totals, grad_attended
):
    scores = masked_scores(queries, key_rows, valid_keys, score_scale)
    probabilities = jnp.exp(scores - log_totals)
    grad_weights = jnp.einsum(
        "mqhd,mkhd->mhqk", grad_attended, value_rows, preferred_element_type=jnp.float32
    )
    grad_values = jnp.einsum(
        "mhqk,mqhd->mkhd",
        probabilities.astype(jnp.bfloat16),
        grad_attended,
        preferred_element_type=jnp.float32,
    )
    grad_scores = probabilities * (
        grad_weights - jnp.sum(grad_weights * probabilities, axis=-1, keepdims=True)
    )
    grad_scores = grad_scores.astype(jnp.bfloat16)
    grad_queries = (
        jnp.einsum("mhqk,mkhd->mqhd", grad_scores, key_rows, preferred_element_type=jnp.float32)
        * score_scale
    )
    grad_keys = (
        jnp.einsum("mhqk,mqhd->mkhd", grad_scores, queries, preferred_element_type=jnp.float32)
        * score_scale
    )
    return (grad_queries, grad_keys, grad_values)


def local(
    tokens,
    node_counts,
    edge_counts,
    ln1_gain,
    ln1_bias,
    qkv_weight,
    out_weight,
    ln2_gain,
    ln2_bias,
    fc1_weight,
    fc1_bias,
    fc2_weight,
    out_grad,
):
    molecules = node_counts.shape[0]
    local_heads = qkv_weight.shape[1] // HEAD_DIM
    score_scale = HEAD_DIM ** (-0.5)
    positions = lax.broadcasted_iota(jnp.int32, (molecules, LEN), 1)
    valid_keys = positions < (1 + node_counts + edge_counts)[:, None]
    inputs = tokens.astype(jnp.float32)
    normed_one = layer_norm(inputs, ln1_gain, ln1_bias).astype(jnp.bfloat16)
    gathered_one = lax.all_gather(normed_one, "tensor", axis=0, tiled=True)
    projected = jnp.einsum(
        "td,ced->cte", gathered_one, qkv_weight, preferred_element_type=jnp.float32
    ).astype(jnp.bfloat16)
    shaped = projected.reshape(3, molecules, LEN, local_heads, HEAD_DIM)
    queries, key_rows, value_rows = (shaped[0], shaped[1], shaped[2])
    attended, log_totals = attention_forward(queries, key_rows, value_rows, valid_keys, score_scale)
    attended_rows = attended.reshape(molecules * LEN, local_heads * HEAD_DIM).astype(jnp.bfloat16)
    row_piece = attended_rows
    branch_one = lax.psum_scatter(
        jnp.dot(row_piece, out_weight, preferred_element_type=jnp.float32).astype(jnp.bfloat16),
        "tensor",
        scatter_dimension=0,
        tiled=True,
    ).astype(jnp.float32)
    hidden = inputs + branch_one
    normed_two = layer_norm(hidden, ln2_gain, ln2_bias).astype(jnp.bfloat16)
    ffn_rows = lax.all_gather(normed_two, "tensor", axis=0, tiled=True)
    inner_values = contract_cols(ffn_rows, fc1_weight) + fc1_bias.astype(jnp.float32)
    activated = gelu_exact(inner_values).astype(jnp.bfloat16)
    row_piece = activated
    branch_two = lax.psum_scatter(
        jnp.dot(row_piece, fc2_weight, preferred_element_type=jnp.float32).astype(jnp.bfloat16),
        "tensor",
        scatter_dimension=0,
        tiled=True,
    ).astype(jnp.float32)
    result = (hidden + branch_two).astype(jnp.bfloat16)
    grad_rows = lax.all_gather(out_grad, "tensor", axis=0, tiled=True)
    grad_activated = contract_cols(grad_rows, fc2_weight)
    grad_fc2 = contract_rows(activated, grad_rows)
    grad_inner = jax.vjp(gelu_exact, inner_values)[1](grad_activated)[0].astype(jnp.bfloat16)
    grad_fc1 = contract_rows(grad_inner, ffn_rows)
    grad_fc1_bias = jnp.sum(grad_inner.astype(jnp.float32), axis=0)
    row_piece = grad_inner
    grad_normed_two = lax.psum_scatter(
        jnp.dot(row_piece, fc1_weight, preferred_element_type=jnp.float32).astype(jnp.bfloat16),
        "tensor",
        scatter_dimension=0,
        tiled=True,
    ).astype(jnp.float32)
    norm_back_two = jax.vjp(layer_norm, hidden, ln2_gain, ln2_bias)[1]
    hidden_part, grad_gain_two, grad_shift_two = norm_back_two(grad_normed_two)
    grad_hidden = out_grad.astype(jnp.float32) + hidden_part
    grad_rows_one = lax.all_gather(grad_hidden.astype(jnp.bfloat16), "tensor", axis=0, tiled=True)
    grad_attended = contract_cols(grad_rows_one, out_weight).astype(jnp.bfloat16)
    grad_out = contract_rows(attended_rows, grad_rows_one)
    grad_queries, grad_keys, grad_values = attention_backward(
        queries,
        key_rows,
        value_rows,
        valid_keys,
        score_scale,
        log_totals,
        grad_attended.reshape(molecules, LEN, local_heads, HEAD_DIM),
    )
    grad_projected = (
        jnp.stack([grad_queries, grad_keys, grad_values])
        .reshape(3, molecules * LEN, local_heads * HEAD_DIM)
        .astype(jnp.bfloat16)
    )
    grad_qkv = jnp.einsum(
        "cte,td->ced", grad_projected, gathered_one, preferred_element_type=jnp.float32
    )
    row_piece = grad_projected
    grad_normed_one = lax.psum_scatter(
        jnp.einsum("cte,ced->td", row_piece, qkv_weight, preferred_element_type=jnp.float32).astype(
            jnp.bfloat16
        ),
        "tensor",
        scatter_dimension=0,
        tiled=True,
    ).astype(jnp.float32)
    norm_back_one = jax.vjp(layer_norm, inputs, ln1_gain, ln1_bias)[1]
    input_part, grad_gain_one, grad_shift_one = norm_back_one(grad_normed_one)
    grad_tokens = (grad_hidden + input_part).astype(jnp.bfloat16)
    grad_qkv, grad_out, grad_fc1, grad_fc1_bias, grad_fc2 = lax.psum(
        (grad_qkv, grad_out, grad_fc1, grad_fc1_bias, grad_fc2), "dp"
    )
    grad_gain_one, grad_shift_one, grad_gain_two, grad_shift_two = lax.psum(
        (grad_gain_one, grad_shift_one, grad_gain_two, grad_shift_two), ("dp", "tensor")
    )
    return (
        result,
        grad_tokens,
        grad_gain_one,
        grad_shift_one,
        grad_qkv,
        grad_out,
        grad_gain_two,
        grad_shift_two,
        grad_fc1,
        grad_fc1_bias,
        grad_fc2,
    )


def solution(mesh):
    in_specs = (
        P(("dp", "tensor"), None),
        P("dp"),
        P("dp"),
        P(),
        P(),
        P(None, "tensor", None),
        P("tensor", None),
        P(),
        P(),
        P("tensor", None),
        P("tensor"),
        P("tensor", None),
        P(("dp", "tensor"), None),
    )
    out_specs = (
        P(("dp", "tensor"), None),
        P(("dp", "tensor"), None),
        P(),
        P(),
        P(None, "tensor", None),
        P("tensor", None),
        P(),
        P(),
        P("tensor", None),
        P("tensor"),
        P("tensor", None),
    )
    return jax.shard_map(local, mesh=mesh, in_specs=in_specs, out_specs=out_specs, check_vma=False)
```

profile of v0, /device:TPU:0, one launch (start us, length us, event | category | flops | bytes accessed | tf_op | source)
XLA Modules:
  0.0 419.9 jit_solution(10593481951313167642)
XLA Ops:
  7.3 1.2 convert_reduce_fusion.2
  8.5 1.2 fusion.40
  9.7 2.0 fusion.38
  11.9 22.4 %all-gather.5.cloned.1.call-done = bf16[1024,768]{1,0:T(8,128)(2,1)} async-done(((bf16[256,768]{1,0:T(8,128)(2,1)}), bf16[1024,768]{1,0:T(8,128)(2,1)}) %all-gather.5.cloned.1.call-update) | async-done | bytes 1572880 | tf_op jit(solution)/shard_map/all_gather | solution.py:107
  34.3 2.5 fusion.13
  37.2 1.3 fusion.72
  41.6 1.8 convolution_convert_fusion.2
  43.5 28.3 %reduce-scatter.5.cloned.1.call-done = bf16[256,768]{1,0:T(8,128)(2,1)} async-done(((bf16[1024,768]{1,0:T(8,128)(2,1)}), bf16[256,768]{1,0:T(8,128)(2,1)}) %reduce-scatter.5.cloned.1.call-update) | async-done | bytes 393232 | tf_op jit(solution)/shard_map/reduce_scatter | solution.py:116
  71.8 1.2 fusion.51
  73.0 1.2 multiply_reduce_fusion.1
  76.0 19.2 %all-gather.7.cloned.1.call-done = bf16[1024,768]{1,0:T(8,128)(2,1)} async-done(((bf16[256,768]{1,0:T(8,128)(2,1)}), bf16[1024,768]{1,0:T(8,128)(2,1)}) %all-gather.7.cloned.1.call-update) | async-done | bytes 1572880 | tf_op jit(solution)/shard_map/all_gather | solution.py:124
  95.2 2.1 convolution_add_fusion
  97.3 19.1 %all-gather.9.cloned.1.call-done = bf16[1024,768]{1,0:T(8,128)(2,1)} async-done(((bf16[256,768]{1,0:T(8,128)(2,1)}), bf16[1024,768]{1,0:T(8,128)(2,1)}) %all-gather.9.cloned.1.call-update) | async-done | bytes 1572880 | tf_op jit(solution)/shard_map/all_gather | solution.py:135
  116.3 5.1 %convert_reduce_fusion.3 = (f32[192]{0:T(256)}, bf16[1024,192]{0,1:T(8,128)(2,1)S(1)}, f32[1024,192]{0,1:T(8,128)}) fusion(f32[1024,192]{0,1:T(8,128)S(1)} %convolution_add_fusion, bf16[1024,768]{1,0:T(8,128)(2,1)} %all-gather.9.cloned.1.call-done, bf16[192,768]{1,0:T(8,128)(2,1)} %param.24), kind=kOutput, calls=%fused_computation.62 | convolution fusion | flops 316538688 | bytes 3834624 | tf_op jit(solution)/shard_map/dot_general | solution.py:31
  122.3 1.8 convolution_convert_fusion
  124.1 1.3 multiply_convert_fusion.1
  126.2 1.8 convolution_convert_fusion.1
  128.1 24.4 %reduce-scatter.9.cloned.1.call-done = bf16[256,768]{1,0:T(8,128)(2,1)} async-done(((bf16[1024,768]{1,0:T(8,128)(2,1)}), bf16[256,768]{1,0:T(8,128)(2,1)}) %reduce-scatter.9.cloned.1.call-update) | async-done | bytes 393232 | tf_op jit(solution)/shard_map/reduce_scatter | solution.py:142
  152.4 2.0 fusion.43
  155.0 28.0 %reduce-scatter.7.cloned.1.call-done = bf16[256,768]{1,0:T(8,128)(2,1)} async-done(((bf16[1024,768]{1,0:T(8,128)(2,1)}), bf16[256,768]{1,0:T(8,128)(2,1)}) %reduce-scatter.7.cloned.1.call-update) | async-done | bytes 393232 | tf_op jit(solution)/shard_map/reduce_scatter | solution.py:128
  183.0 2.3 fusion.71
  186.4 1.4 log_add_fusion
  187.9 18.2 %all-gather.11.cloned.1.call-done = bf16[1024,768]{1,0:T(8,128)(2,1)} async-done(((bf16[256,768]{1,0:T(8,128)(2,1)}), bf16[1024,768]{1,0:T(8,128)(2,1)}) %all-gather.11.cloned.1.call-update) | async-done | bytes 1572880 | tf_op jit(solution)/shard_map/all_gather | solution.py:151
  206.0 2.1 fusion.22
  208.2 3.5 fusion.26
  211.8 1.1 multiply_reduce_fusion
  212.9 1.2 multiply_convert_fusion
  214.1 2.0 fusion.24
  216.1 1.4 fusion.25
  218.5 1.2 stack.14
  219.7 2.0 copy.45
  221.7 1.9 stack.12
  223.6 2.0 copy.48
  225.6 1.9 stack.13
  227.5 1.0 constant_dynamic-update-slice_fusion.2
  228.5 1.0 constant_dynamic-update-slice_fusion.1
  230.6 2.6 bitcast_convert_fusion
  233.3 2.9 fusion.73
  236.2 1.3 fusion.74
  237.6 1.3 fusion.54
  239.2 2.3 fusion.6
  242.2 21.6 %psum.70 = f32[192]{0:T(256)} all-reduce(f32[192]{0:T(256)S(1)} %copy-done.40), channel_id=1, replica_groups=mesh['dp'=8,'tensor'=4] {'dp'}, use_global_device_ids=true, to_apply=%region_27.28 | all-reduce | flops 192 | bytes 1536 | tf_op jit(solution)/shard_map/psum | solution.py:183
  263.9 1.4 convert_reduce_fusion
  265.3 1.5 fusion.44
  266.8 42.0 %all-reduce = (f32[768]{0:T(1024)}, f32[768]{0:T(1024)}, f32[768]{0:T(1024)}, f32[768]{0:T(1024)}) all-reduce(f32[768]{0:T(1024)S(1)} %get-tuple-element.13, f32[768]{0:T(1024)S(1)} %get-tuple-element.16, f32[768]{0:T(1024)S(1)} %copy-done.31, f32[768]{0:T(1024)S(1)} %copy-done.32), channel_id=1, replica_groups=mesh['dp'=8,'tensor'=4] {'dp','tensor'}, use_global_device_ids=true, to_apply=%region_16.17 | all-reduce | flops 3072 | bytes 24576 | tf_op jit(solution)/shard_map/psum | solution.py:186
  308.8 1.1 add_convert_fusion
  309.9 98.0 %all-reduce.4.cloned.1.call-done = (f32[3,192,768]{2,1,0:T(8,128)}, f32[192,768]{1,0:T(8,128)}, f32[192,768]{1,0:T(8,128)}, f32[192,768]{1,0:T(8,128)}) async-done(((f32[3,192,768]{2,1,0:T(8,128)}, f32[192,768]{1,0:T(8,128)}, f32[192,768]{1,0:T(8,128)}, f32[192,768]{1,0:T(8,128)}), (f32[3,192,768]{2,1,0:T(8,128)}, f32[192,768]{1,0:T(8,128)}, f32[192,768]{1,0:T(8,128)}, ...) | async-done | bytes 3538960 | tf_op jit(solution)/shard_map/psum | solution.py:183
  408.0 2.9 copy.99
  (135 shorter events, 14.4 us)
Async XLA Ops:
  7.2 27.1 %copy-start = (bf16[3,192,768]{2,1,0:T(8,128)(2,1)S(1)}, bf16[3,192,768]{2,1,0:T(8,128)(2,1)}, u32[]{:S(2)}) copy-start(bf16[3,192,768]{2,1,0:T(8,128)(2,1)} %param.18) | copy-start | bytes 2654212
  7.2 4.6 %copy-start.42 = (s32[8]{0:T(128)S(1)}, s32[8]{0:T(128)}, u32[]{:S(2)}) copy-start(s32[8]{0:T(128)} %param.15) | copy-start | bytes 100
  7.2 4.6 %copy-start.43 = (s32[8]{0:T(128)S(1)}, s32[8]{0:T(128)}, u32[]{:S(2)}) copy-start(s32[8]{0:T(128)} %param.14) | copy-start | bytes 100
  7.2 27.1 %all-gather.5.cloned.1.call-start = ((), (), s32[]{:S(2)}) async-start(), calls=%async_computation.4 | async-start | bytes 1966080 | tf_op jit(solution)/shard_map/all_gather | solution.py:107
  9.7 27.1 %copy-start.35 = (f32[256]{0:T(256)}, f32[256]{0:T(256)S(1)}, u32[]{:S(2)}) copy-start(f32[256]{0:T(256)S(1)} %fusion.40) | copy-start | bytes 3076
  11.8 60.0 %reduce-scatter.5.cloned.1.call-start = ((), (), s32[]{:S(2)}) async-start(), calls=%async_computation.5 | async-start | bytes 1966080 | tf_op jit(solution)/shard_map/reduce_scatter | solution.py:116
  37.0 2.6 copy-start.14
  37.1 1.4 copy-start.10
  37.1 1.4 copy-start.12
  38.5 1.9 copy-start.1
  38.5 1.9 copy-start.24
  39.6 1.8 copy-start.26
  41.6 30.1 %copy-start.3 = (bf16[256,768]{1,0:T(8,128)(2,1)S(1)}, bf16[256,768]{1,0:T(8,128)(2,1)}, u32[]{:S(2)}) copy-start(bf16[256,768]{1,0:T(8,128)(2,1)} %param.13) | copy-start | bytes 1179652
  43.4 30.9 %copy-start.30 = (f32[768]{0:T(1024)S(1)}, f32[768]{0:T(1024)}, u32[]{:S(2)}) copy-start(f32[768]{0:T(1024)} %param.20) | copy-start | bytes 9220
  43.4 30.9 %copy-start.39 = (f32[768]{0:T(1024)S(1)}, f32[768]{0:T(1024)}, u32[]{:S(2)}) copy-start(f32[768]{0:T(1024)} %param.21) | copy-start | bytes 9220
  43.4 32.5 %copy-start.44 = (bf16[192]{0:T(256)(128)(2,1)S(1)}, bf16[192]{0:T(256)(128)(2,1)}, u32[]{:S(2)}) copy-start(bf16[192]{0:T(256)(128)(2,1)} %param.23) | copy-start | bytes 1156
  43.4 51.7 %copy-start.18 = (bf16[192,768]{1,0:T(8,128)(2,1)S(1)}, bf16[192,768]{1,0:T(8,128)(2,1)}, u32[]{:S(2)}) copy-start(bf16[192,768]{1,0:T(8,128)(2,1)} %param.22) | copy-start | bytes 884740
  43.4 51.7 %all-gather.7.cloned.1.call-start = ((), (), s32[]{:S(2)}) async-start(), calls=%async_computation.6 | async-start | bytes 1966080 | tf_op jit(solution)/shard_map/all_gather | solution.py:124
  71.8 2.6 copy-start.4
  74.3 23.0 %copy-start.37 = (f32[256]{0:T(256)}, f32[256]{0:T(256)S(1)}, u32[]{:S(2)}) copy-start(f32[256]{0:T(256)S(1)} %multiply_reduce_fusion.1) | copy-start | bytes 3076
  74.3 22.9 %copy-start.33 = (f32[256]{0:T(256)}, f32[256]{0:T(256)S(1)}, u32[]{:S(2)}) copy-start(f32[256]{0:T(256)S(1)} %fusion.69) | copy-start | bytes 3076
  75.3 41.0 %all-gather.9.cloned.1.call-start = ((), (), s32[]{:S(2)}) async-start(), calls=%async_computation.8 | async-start | bytes 1966080 | tf_op jit(solution)/shard_map/all_gather | solution.py:135
  75.9 76.5 %reduce-scatter.9.cloned.1.call-start = ((), (), s32[]{:S(2)}) async-start(), calls=%async_computation.9 | async-start | bytes 1966080 | tf_op jit(solution)/shard_map/reduce_scatter | solution.py:142
  124.0 2.1 copy-start.25
  124.1 59.0 %reduce-scatter.7.cloned.1.call-start = ((), (), s32[]{:S(2)}) async-start(), calls=%async_computation.7 | async-start | bytes 1966080 | tf_op jit(solution)/shard_map/reduce_scatter | solution.py:128
  126.2 26.2 %copy-start.34 = (f32[256]{0:T(256)S(1)}, f32[256]{0:T(256)}, u32[]{:S(2)}) copy-start(f32[256]{0:T(256)} %copy-done.33) | copy-start | bytes 3076
  128.0 26.4 %copy-start.38 = (f32[256]{0:T(256)S(1)}, f32[256]{0:T(256)}, u32[]{:S(2)}) copy-start(f32[256]{0:T(256)} %copy-done.37) | copy-start | bytes 3076
  128.0 57.3 %copy-start.7 = (bf16[256,768]{1,0:T(8,128)(2,1)S(1)}, bf16[256,768]{1,0:T(8,128)(2,1)}, u32[]{:S(2)}) copy-start(bf16[256,768]{1,0:T(8,128)(2,1)} %param.25) | copy-start | bytes 1179652
  128.0 78.0 %all-gather.11.cloned.1.call-start = ((), (), s32[]{:S(2)}) async-start(), calls=%async_computation.10 | async-start | bytes 1966080 | tf_op jit(solution)/shard_map/all_gather | solution.py:151
  186.2 77.6 %reduce-scatter.11.cloned.1.call-start = ((), (), s32[]{:S(2)}) async-start(), calls=%async_computation.11 | async-start | bytes 1966080 | tf_op jit(solution)/shard_map/reduce_scatter | solution.py:172
  206.0 2.2 copy-start.23
  208.2 3.6 copy-start.2
  208.2 3.6 copy-start.15
  214.1 2.0 copy-start.11
  233.2 3.0 copy-start.9
  233.2 174.8 %all-reduce.4.cloned.1.call-start = ((), (), s32[]{:S(2)}) async-start(), calls=%async_computation.12 | async-start | bytes 7077888 | tf_op jit(solution)/shard_map/psum | solution.py:183
  233.2 3.0 copy-start.16
  236.2 1.4 copy-start.5
  236.2 2.7 copy-start.41
  237.6 1.6 copy-start.28
  241.5 22.3 %copy-start.29 = (f32[768]{0:T(1024)S(1)}, f32[768]{0:T(1024)}, u32[]{:S(2)}) copy-start(f32[768]{0:T(1024)} %param.16) | copy-start | bytes 9220
  241.5 23.7 %copy-start.36 = (f32[256]{0:T(256)S(1)}, f32[256]{0:T(256)}, u32[]{:S(2)}) copy-start(f32[256]{0:T(256)} %copy-done.35) | copy-start | bytes 3076
  241.5 25.2 %copy-start.31 = (f32[768]{0:T(1024)S(1)}, f32[768]{0:T(1024)}, u32[]{:S(2)}) copy-start(f32[768]{0:T(1024)} %get-tuple-element.11) | copy-start | bytes 9220
  241.5 25.2 %copy-start.32 = (f32[768]{0:T(1024)S(1)}, f32[768]{0:T(1024)}, u32[]{:S(2)}) copy-start(f32[768]{0:T(1024)} %get-tuple-element.15) | copy-start | bytes 9220
  263.9 44.9 %copy-start.6 = (bf16[256,768]{1,0:T(8,128)(2,1)S(1)}, bf16[256,768]{1,0:T(8,128)(2,1)}, u32[]{:S(2)}) copy-start(bf16[256,768]{1,0:T(8,128)(2,1)} %reduce-scatter.11.cloned.1.call-done) | copy-start | bytes 1179652
  408.0 2.9 copy-start.22
  408.0 3.7 copy-start.21
  410.9 1.6 copy-start.20
  (6 other events, 5.6 us)
Sparse Core Ops, SparseCore 0:
  11.9 22.3 all-gather.4
  43.5 28.1 reduce-scatter.4
  75.5 19.6 all-gather.6
  96.6 19.6 all-gather.8
  124.2 28.1 reduce-scatter.8
  154.8 28.1 reduce-scatter.6
  186.3 19.6 all-gather.10
  233.3 28.1 reduce-scatter.10
  266.6 141.3 all-reduce.3
where the time goes:
time: 421 us; the launch traced here: 420 us
  waiting for transfers between devices  258 us (61%)
  blocking collectives  63.6 us (15%)
  matrix products  37.8 us (9%)
  local copies, waits for them, and re-layouts  22.7 us (5%)
  other arithmetic  22.7 us (5%)
  between operations  14.4 us (3%)
    psum x1, waiting for transfers between devices, local(): lax.psum((grad_qkv, grad_out, grad_fc1, grad_fc1_bias, grad_fc2), 'dp')  98 us
    psum x1, blocking collectives, local(): lax.psum((grad_gain_one, grad_shift_one, grad_gain_two, grad_shift_two),...  42 us
    reduce_scatter x1, waiting for transfers between devices, local(): lax.psum_scatter(jnp.dot(row_piece, out_weight, preferred_element_type=jn...  28.3 us
    reduce_scatter x1, waiting for transfers between devices, local(): lax.psum_scatter(jnp.dot(row_piece, fc2_weight, preferred_element_type=jn...  28 us
    reduce_scatter x1, waiting for transfers between devices, local(): lax.psum_scatter(jnp.dot(row_piece, fc1_weight, preferred_element_type=jn...  24.4 us
    all_gather x1, waiting for transfers between devices, local(): gathered_one = lax.all_gather(normed_one, 'tensor', axis=0, tiled=True)  22.4 us
    psum x1, blocking collectives, local(): lax.psum((grad_qkv, grad_out, grad_fc1, grad_fc1_bias, grad_fc2), 'dp')  21.6 us
    all_gather x1, waiting for transfers between devices, local(): ffn_rows = lax.all_gather(normed_two, 'tensor', axis=0, tiled=True)  19.2 us
  transfers between devices with their start and end apart: 9, of which 8 were waited for; matrix products, arithmetic and copies ran while one was open for 5% of the time, Pallas kernels for 0%

commit v1 on v0

v1 whole, which is shorter than its diff:
```python
import functools

import jax
import jax.numpy as jnp
from jax import lax
from jax.experimental import pallas as pl
from jax.experimental.pallas import tpu as pltpu
from jax.sharding import PartitionSpec as P

HEAD_DIM = 24
LEN = 128
PAIR = 2 * HEAD_DIM
EPSILON = 1e-05
SCALE = HEAD_DIM ** (-0.5)
LOG2E = 1.4426950408889634
F32 = jnp.float32
BF16 = jnp.bfloat16
VMEM_LIMIT = 48 * 1024 * 1024


def dot_nn(a, b):
    return lax.dot_general(a, b, (((1,), (0,)), ((), ())), preferred_element_type=F32)


def dot_nt(a, b):
    return lax.dot_general(a, b, (((1,), (1,)), ((), ())), preferred_element_type=F32)


def dot_tn(a, b):
    return lax.dot_general(a, b, (((0,), (0,)), ((), ())), preferred_element_type=F32)


def normalise(v):
    centered = v - jnp.mean(v, axis=-1, keepdims=True)
    r = lax.rsqrt(jnp.mean(centered * centered, axis=-1, keepdims=True) + EPSILON)
    return centered * r, r


def norm_back(da, gain, xh, r):
    e = da * gain
    return r * (
        e - jnp.mean(e, axis=-1, keepdims=True) - xh * jnp.mean(e * xh, axis=-1, keepdims=True)
    )


def pair_blocks(rows):
    none = jnp.zeros((HEAD_DIM, LEN), F32)
    left = jnp.concatenate([rows[:HEAD_DIM], none], axis=0)
    right = jnp.concatenate([none, rows[HEAD_DIM:]], axis=0)
    return jnp.concatenate([left, right], axis=1).astype(BF16)


def pair_window(i, width):
    low = (PAIR * i) // LEN * LEN
    low = min(low, width - 2 * LEN)
    return low, PAIR * i - low


def placed(block, before):
    parts = []
    if before:
        parts.append(jnp.zeros((before, 2 * LEN), BF16))
    parts.append(block)
    after = 2 * LEN - PAIR - before
    if after:
        parts.append(jnp.zeros((after, 2 * LEN), BF16))
    return jnp.concatenate(parts, axis=0)


def diagonal(both):
    return jnp.concatenate([both[:HEAD_DIM, :LEN], both[HEAD_DIM:, LEN:]], axis=0)


def attention_kernel(
    aliased, place_ref, nodes_ref, edges_ref, x_ref, gain_ref, bias_ref, w_ref, *refs
):
    a1_ref, qt_ref, kt_ref, v_ref, p_ref, ot_ref, o_ref = refs[aliased:]
    width = w_ref.shape[1]
    mol = place_ref[0] + pl.program_id(0)
    count = 1 + nodes_ref[mol] + edges_ref[mol]
    xh, _ = normalise(x_ref[...].astype(F32))
    a1 = (xh * gain_ref[...] + bias_ref[...]).astype(BF16)
    a1_ref[...] = a1
    qt = dot_nt(w_ref[0], a1).astype(BF16)
    vt = dot_nt(w_ref[2], a1).astype(BF16)
    keys = dot_nt(a1, w_ref[1]).astype(BF16)
    qt_ref[...] = qt
    kt_ref[...] = dot_nt(w_ref[1], a1).astype(BF16)
    v_ref[...] = dot_nt(a1, w_ref[2]).astype(BF16)
    valid = lax.broadcasted_iota(jnp.int32, (LEN, 2 * LEN), 0) < count
    for i in range(width // PAIR):
        low, before = pair_window(i, width)
        rows = slice(PAIR * i, PAIR * (i + 1))
        rhs = placed(pair_blocks(qt[rows].astype(F32)), before)
        s = dot_nn(keys[:, low : low + 2 * LEN], rhs)
        s = jnp.where(valid, s, -1e30)
        e = jnp.exp2((s - jnp.max(s, axis=0, keepdims=True)) * (SCALE * LOG2E))
        p = (e * (1.0 / jnp.sum(e, axis=0, keepdims=True))).astype(BF16)
        p_ref[0, i] = p
        ot_ref[rows, :] = diagonal(dot_nn(vt[rows], p)).astype(BF16)
    o_ref[...] = ot_ref[...].T


def attention(place, nodes, edges, x, gain, bias, w, kept, first, total):
    width, d = w.shape[1:]
    mols = x.shape[0] // LEN
    pairs = width // PAIR
    at = lambda i, *_: (first + i, 0)
    lanes = lambda i, *_: (0, first + i)
    fixed = lambda *_: (0, 0)
    outs = [
        (jax.ShapeDtypeStruct((total * LEN, d), BF16), pl.BlockSpec((LEN, d), at)),
        (jax.ShapeDtypeStruct((width, total * LEN), BF16), pl.BlockSpec((width, LEN), lanes)),
        (jax.ShapeDtypeStruct((width, total * LEN), BF16), pl.BlockSpec((width, LEN), lanes)),
        (jax.ShapeDtypeStruct((total * LEN, width), BF16), pl.BlockSpec((LEN, width), at)),
        (
            jax.ShapeDtypeStruct((total, pairs, LEN, 2 * LEN), BF16),
            pl.BlockSpec((1, pairs, LEN, 2 * LEN), lambda i, *_: (first + i, 0, 0, 0)),
        ),
        (jax.ShapeDtypeStruct((width, total * LEN), BF16), pl.BlockSpec((width, LEN), lanes)),
        (
            jax.ShapeDtypeStruct((mols * LEN, width), BF16),
            pl.BlockSpec((LEN, width), lambda i, *_: (i, 0)),
        ),
    ]
    return pl.pallas_call(
        functools.partial(attention_kernel, len(kept)),
        grid_spec=pltpu.PrefetchScalarGridSpec(
            num_scalar_prefetch=3,
            grid=(mols,),
            in_specs=[
                pl.BlockSpec((LEN, d), lambda i, *_: (i, 0)),
                pl.BlockSpec((1, d), fixed),
                pl.BlockSpec((1, d), fixed),
                pl.BlockSpec((3, width, d), lambda *_: (0, 0, 0)),
            ]
            + [pl.BlockSpec(memory_space=pl.ANY)] * len(kept),
            out_specs=[spec for _, spec in outs],
        ),
        out_shape=[shape for shape, _ in outs],
        input_output_aliases={7 + j: j for j in range(len(kept))},
        compiler_params=pltpu.CompilerParams(vmem_limit_bytes=VMEM_LIMIT),
        cost_estimate=pl.CostEstimate(
            flops=mols * LEN * width * (10 * d + 8 * LEN),
            bytes_accessed=w.size * 2 + mols * LEN * (d * 4 + width * 20),
            transcendentals=mols * pairs * 2 * LEN * LEN,
        ),
        name="attention_forward",
    )(place, nodes, edges, x, gain, bias, w, *kept)


def feed_kernel(
    half, x0, x1, oa0, oa1, ob0, ob1, g0, g1, wa_ref, wb_ref, gain_ref, bias_ref, fc1_ref, b1_ref,
    fc2_ref, h_ref, a2_ref, z_ref, du_ref,
):
    own = pl.program_id(0) < half

    def body(x, oa, ob, g):
        branch = dot_nn(oa[...], wa_ref[...]) + dot_nn(ob[...], wb_ref[...])
        h = x[...].astype(F32) + branch
        h_ref[...] = h
        xh, _ = normalise(h)
        a2 = (xh * gain_ref[...] + bias_ref[...]).astype(BF16)
        a2_ref[...] = a2
        u = dot_nt(a2, fc1_ref[...]) + b1_ref[...]
        phi = 0.5 * (1.0 + lax.erf(u * (0.5**0.5)))
        z_ref[...] = (u * phi).astype(BF16)
        slope = phi + u * (jnp.exp(-0.5 * u * u) * 0.3989422804014327)
        du_ref[...] = (dot_nt(g[...], fc2_ref[...]) * slope).astype(BF16)

    pl.when(own)(lambda: body(x0, oa0, ob0, g0))
    pl.when(jnp.logical_not(own))(lambda: body(x1, oa1, ob1, g1))


def feed(xs, oas, obs, gs, wa, wb, gain, bias, fc1, b1, fc2):
    rows, d = xs[0].shape
    width = wa.shape[0]
    block = LEN
    half = rows // block
    mine = lambda i: (jnp.minimum(i, half - 1), 0)
    theirs = lambda i: (jnp.maximum(i - half, 0), 0)
    fixed = lambda i: (0, 0)
    pair = lambda cols: [pl.BlockSpec((block, cols), mine), pl.BlockSpec((block, cols), theirs)]
    here = lambda cols: pl.BlockSpec((block, cols), lambda i: (i, 0))
    whole = lambda a: pl.BlockSpec(a.shape, fixed)
    return pl.pallas_call(
        functools.partial(feed_kernel, half),
        grid=(2 * half,),
        in_specs=pair(d) + pair(width) + pair(width) + pair(d)
        + [whole(a) for a in (wa, wb, gain, bias, fc1, b1, fc2)],
        out_specs=[here(d), here(d), here(width), here(width)],
        out_shape=[
            jax.ShapeDtypeStruct((2 * rows, d), F32),
            jax.ShapeDtypeStruct((2 * rows, d), BF16),
            jax.ShapeDtypeStruct((2 * rows, width), BF16),
            jax.ShapeDtypeStruct((2 * rows, width), BF16),
        ],
        compiler_params=pltpu.CompilerParams(vmem_limit_bytes=VMEM_LIMIT),
        cost_estimate=pl.CostEstimate(
            flops=2 * rows * d * width * 8, bytes_accessed=rows * d * 24, transcendentals=4 * rows * width
        ),
        name="feed_forward",
    )(*xs, *oas, *obs, *gs, wa, wb, gain, bias, fc1, b1, fc2)


def feed_grads_kernel(z_ref, du_ref, a2_ref, g0, g1, fc2_ref, h_ref, keep_ref, send_ref, sums_ref,
                      mine_ref, theirs_ref):
    rows = g0.shape[0]
    shard = fc2_ref.shape[0] // 2
    z = z_ref[...]
    du = du_ref[...]
    mine_ref[...] = h_ref[...] + dot_nn(z[:rows], fc2_ref[...])
    theirs_ref[...] = dot_nn(z[rows:], fc2_ref[...]).astype(BF16)
    first = dot_tn(du, a2_ref[...]).astype(BF16)
    keep_ref[:shard] = first[:shard]
    send_ref[:shard] = first[shard:]
    second = (dot_tn(z[:rows], g0[...]) + dot_tn(z[rows:], g1[...])).astype(BF16)
    keep_ref[shard:] = second[:shard]
    send_ref[shard:] = second[shard:]
    sums_ref[...] = jnp.sum(du.astype(F32), axis=0, keepdims=True)


def feed_grads(z, du, a2, gs, fc2, h):
    rows, d = gs[0].shape
    width = z.shape[1]
    whole = lambda a: pl.BlockSpec(a.shape, lambda i: (0, 0))
    shapes = [
        jax.ShapeDtypeStruct((width, d), BF16),
        jax.ShapeDtypeStruct((width, d), BF16),
        jax.ShapeDtypeStruct((1, width), F32),
        jax.ShapeDtypeStruct((rows, d), F32),
        jax.ShapeDtypeStruct((rows, d), BF16),
    ]
    return pl.pallas_call(
        feed_grads_kernel,
        grid=(1,),
        in_specs=[whole(z), whole(du), whole(a2), whole(gs[0]), whole(gs[1]), whole(fc2),
                  pl.BlockSpec((rows, d), lambda i: (0, 0))],
        out_specs=[whole(s) for s in shapes],
        out_shape=shapes,
        compiler_params=pltpu.CompilerParams(vmem_limit_bytes=VMEM_LIMIT),
        cost_estimate=pl.CostEstimate(
            flops=2 * rows * d * width * 6, bytes_accessed=rows * d * 18, transcendentals=0
        ),
        name="feed_grads",
    )(z, du, a2, *gs, fc2, h)


def backward_kernel(
    half, du0, du1, dr0, dr1, fa_ref, fb_ref, h_ref, g0, g1, gain_ref, wo_ref, ot_ref, p_ref, qt_ref,
    kt_ref, v_ref, a1_ref, w_ref, keep_ref, send_ref, dh_ref, sums_ref, mine_ref, theirs_ref,
    dp_ref, gh_ref,
):
    step = pl.program_id(0)
    own = step < half
    width = wo_ref.shape[0]
    shard = width // 2
    here = pl.ds(pl.multiple_of(step * LEN, LEN), LEN)

    @pl.when(step == 0)
    def _():
        sums_ref[...] = jnp.zeros_like(sums_ref)

    du = jnp.where(own, du0[...].astype(F32), du1[...].astype(F32)).astype(BF16)
    dr = jnp.where(own, dr0[...].astype(F32), dr1[...].astype(F32)).astype(BF16)
    g = jnp.where(own, g0[...].astype(F32), g1[...].astype(F32))
    da2 = dot_nn(du, fa_ref[...]) + dot_nn(dr, fb_ref[...])
    xh, r = normalise(h_ref[...])
    dh = g + norm_back(da2, gain_ref[...], xh, r)

    @pl.when(own)
    def _():
        dh_ref[...] = dh
        sums_ref[0:1] += jnp.sum(da2 * xh, axis=0, keepdims=True)
        sums_ref[1:2] += jnp.sum(da2, axis=0, keepdims=True)

    gh = dh.astype(BF16)
    gh_ref[here, :] = gh
    dot = dot_nt(wo_ref[...], gh).astype(BF16)
    for i in range(width // PAIR):
        low, before = pair_window(i, width)
        rows = slice(PAIR * i, PAIR * (i + 1))
        do_pair = pair_blocks(dot[rows].astype(F32))
        q_pair = pair_blocks(qt_ref[rows, :].astype(F32))
        pb = p_ref[0, i]
        p = pb.astype(F32)
        dp = dot_nn(v_ref[:, low : low + 2 * LEN], placed(do_pair, before)) * p
        ds = (dp - p * jnp.sum(dp, axis=0, keepdims=True)).astype(BF16)
        dq = diagonal(dot_nn(kt_ref[rows, :], ds)) * SCALE
        dk = dot_nt(q_pair, ds) * SCALE
        dv = dot_nt(do_pair, pb)
        dp_ref[pl.ds(PAIR * i, PAIR), here] = dq.astype(BF16)
        dp_ref[pl.ds(width + PAIR * i, PAIR), here] = dk.astype(BF16)
        dp_ref[pl.ds(2 * width + PAIR * i, PAIR), here] = dv.astype(BF16)
    da1 = dot_tn(dp_ref[:, here], w_ref[...])

    @pl.when(own)
    def _():
        mine_ref[...] = da1

    @pl.when(jnp.logical_not(own))
    def _():
        theirs_ref[...] = da1.astype(BF16)

    @pl.when(step == 2 * half - 1)
    def _():
        a1 = a1_ref[...]
        for c in range(3):
            for s, ref in enumerate((keep_ref, send_ref)):
                at = c * width + s * shard
                ref[c] = dot_nn(dp_ref[at : at + shard, :], a1).astype(BF16)
        for s, ref in enumerate((keep_ref, send_ref)):
            ref[3] = dot_nn(ot_ref[s * shard : (s + 1) * shard, :], gh_ref[...]).astype(BF16)


def backward(dus, drs, fa, fb, h, gs, gain, wo, ot, p, qt, kt, v, a1, w):
    rows, d = gs[0].shape
    width = wo.shape[0]
    half = rows // LEN
    pairs = width // PAIR
    mine = lambda i: (jnp.minimum(i, half - 1), 0)
    theirs = lambda i: (jnp.maximum(i - half, 0), 0)
    lanes = lambda i: (0, i)
    pair = lambda cols: [pl.BlockSpec((LEN, cols), mine), pl.BlockSpec((LEN, cols), theirs)]
    whole = lambda a: pl.BlockSpec(a.shape, lambda i, n=len(a.shape): (0,) * n)
    w = w.reshape(3 * width, d)
    shapes = [
        jax.ShapeDtypeStruct((4, width // 2, d), BF16),
        jax.ShapeDtypeStruct((4, width // 2, d), BF16),
        jax.ShapeDtypeStruct((rows, d), F32),
        jax.ShapeDtypeStruct((8, d), F32),
        jax.ShapeDtypeStruct((rows, d), F32),
        jax.ShapeDtypeStruct((rows, d), BF16),
    ]
    return pl.pallas_call(
        functools.partial(backward_kernel, half),
        grid=(2 * half,),
        in_specs=[
            pl.BlockSpec((LEN, width), mine),
            pl.BlockSpec((LEN, width), lambda i: (jnp.maximum(i, half), 0)),
            pl.BlockSpec((LEN, width), lambda i: (jnp.minimum(i, half - 1) + half, 0)),
            pl.BlockSpec((LEN, width), theirs),
            whole(fa),
            whole(fb),
            pl.BlockSpec((LEN, d), lambda i: (i, 0)),
        ]
        + pair(d)
        + [
            whole(gain),
            whole(wo),
            whole(ot),
            pl.BlockSpec((1, pairs, LEN, 2 * LEN), lambda i: (i, 0, 0, 0)),
            pl.BlockSpec((width, LEN), lanes),
            pl.BlockSpec((width, LEN), lanes),
            pl.BlockSpec((LEN, width), lambda i: (i, 0)),
            whole(a1),
            whole(w),
        ],
        out_specs=[
            whole(shapes[0]),
            whole(shapes[1]),
            pl.BlockSpec((LEN, d), mine),
            whole(shapes[3]),
            pl.BlockSpec((LEN, d), mine),
            pl.BlockSpec((LEN, d), theirs),
        ],
        out_shape=shapes,
        scratch_shapes=[
            pltpu.VMEM((3 * width, 2 * rows), BF16),
            pltpu.VMEM((2 * rows, d), BF16),
        ],
        compiler_params=pltpu.CompilerParams(vmem_limit_bytes=VMEM_LIMIT),
        cost_estimate=pl.CostEstimate(
            flops=2 * rows * d * width * 22, bytes_accessed=rows * d * 40, transcendentals=0
        ),
        name="attention_backward",
    )(dus, dus, drs, drs, fa, fb, h, *gs, gain, wo, ot, p, qt, kt, v, a1, w)


def input_norm_kernel(x_ref, gain_ref, mine_ref, got_ref, dh_ref, sums_ref, bias_ref, out_ref, vec_ref):
    xh, r = normalise(x_ref[...].astype(F32))
    da1 = mine_ref[...] + got_ref[...].astype(F32)
    out_ref[...] = (dh_ref[...] + norm_back(da1, gain_ref[...], xh, r)).astype(BF16)
    d = x_ref.shape[1]
    bias = bias_ref[...]
    rows = [
        jnp.sum(da1 * xh, axis=0, keepdims=True),
        jnp.sum(da1, axis=0, keepdims=True),
        sums_ref[0:2],
        jnp.concatenate([bias, jnp.zeros((1, d - bias.shape[1]), F32)], axis=1),
        jnp.zeros((11, d), F32),
    ]
    vec_ref[...] = jnp.concatenate(rows, axis=0).astype(BF16)


def input_norm(x, gain, mine, got, dh, sums, bias):
    rows, d = x.shape
    args = (x, gain, mine, got, dh, sums, bias)
    whole = lambda a: pl.BlockSpec(a.shape, lambda i: (0, 0))
    shapes = [jax.ShapeDtypeStruct((rows, d), BF16), jax.ShapeDtypeStruct((16, d), BF16)]
    return pl.pallas_call(
        input_norm_kernel,
        grid=(1,),
        in_specs=[whole(a) for a in args],
        out_specs=[whole(s) for s in shapes],
        out_shape=shapes,
        compiler_params=pltpu.CompilerParams(vmem_limit_bytes=VMEM_LIMIT),
        cost_estimate=pl.CostEstimate(
            flops=rows * d * 20, bytes_accessed=rows * d * 14, transcendentals=0
        ),
        name="input_norm",
    )(*args)


def add(a, b):
    return (a.astype(F32) + b.astype(F32)).astype(BF16)


def local(
    n_dp, n_tensor, tokens, node_counts, edge_counts, ln1_gain, ln1_bias, qkv_weight, out_weight,
    ln2_gain, ln2_bias, fc1_weight, fc1_bias, fc2_weight, out_grad,
):
    d = tokens.shape[1]
    mols = tokens.shape[0] // LEN
    dp_at = lax.axis_index("dp")
    tensor_at = lax.axis_index("tensor")

    def swap_core(a):
        return lax.ppermute(a, "tensor", [(t, t ^ 1) for t in range(n_tensor)])

    def swap_y(a):
        return lax.ppermute(a, "tensor", [(t, t ^ 2) for t in range(n_tensor)])

    def swap_dp(a, mask0, mask1):
        pairs = [
            (p * n_tensor + t, (p ^ (mask1 if t % 2 else mask0)) * n_tensor + t)
            for p in range(n_dp)
            for t in range(n_tensor)
        ]
        return lax.ppermute(a, ("dp", "tensor"), pairs)

    row = lambda v: v.reshape(1, -1).astype(F32)
    g1, b1, g2, b2 = row(ln1_gain), row(ln1_bias), row(ln2_gain), row(ln2_bias)

    both = lambda a, axis=0: jnp.concatenate([a, swap_core(a)], axis=axis)
    place = jnp.stack([tensor_at * mols, (tensor_at ^ 2) * mols]).astype(jnp.int32)

    x_got = swap_y(tokens)
    w_qkv = both(qkv_weight, 1)
    w_out = both(out_weight)
    w_fc1 = both(fc1_weight)
    w_fc2 = both(fc2_weight)
    b_fc1 = both(fc1_bias)

    total = 2 * mols
    kept = attention(place[:1], node_counts, edge_counts, tokens, g1, b1, w_qkv, (), 0, total)
    o_own = kept[6]
    x_got, g_src, w_src = lax.optimization_barrier(
        (x_got, out_grad, jnp.concatenate([out_weight, fc1_weight], axis=0))
    )
    o_own_got = swap_y(o_own)
    kept = attention(place[1:], node_counts, edge_counts, x_got, g1, b1, w_qkv, kept[:6], mols, total)
    a1, qt, kt, v, p, ot, o_theirs = kept
    o_theirs_got = swap_y(o_theirs)
    w_got = both(swap_y(w_src))
    shard = out_weight.shape[0]
    w_out_got = jnp.concatenate([w_got[:shard], w_got[2 * shard : 3 * shard]], axis=0)
    w_fc1_got = jnp.concatenate([w_got[shard : 2 * shard], w_got[3 * shard :]], axis=0)
    g_got = swap_y(g_src)

    gs = (out_grad, g_got)
    h, a2, z, du = feed(
        (tokens, x_got), (o_own, o_theirs), (o_theirs_got, o_own_got), gs, w_out, w_out_got, g2, b2,
        w_fc1, row(b_fc1), w_fc2,
    )
    du_got = swap_y(du)
    fc_keep, fc_send, bias_sums, res_mine, res_theirs = feed_grads(z, du, a2, gs, w_fc2, h)
    res_got = swap_y(res_theirs)
    result = (res_mine + res_got.astype(F32)).astype(BF16)

    keep, send, dh, sums, da1_mine, da1_theirs = backward(
        du, du_got, w_fc1, w_fc1_got, h, gs, g2, w_out, ot, p, qt, kt, v, a1, w_qkv
    )
    grad_tokens, vec = input_norm(tokens, g1, da1_mine, swap_y(da1_theirs), dh, sums, bias_sums)
    vec_got = swap_y(vec)
    same = lax.broadcasted_iota(jnp.int32, vec.shape, 0) < 4
    vec = jnp.where(same, add(vec, vec_got), vec)
    vec_got = swap_core(vec)
    turned = jnp.concatenate(
        [vec_got[:, shard : 2 * shard], vec_got[:, :shard], vec_got[:, 2 * shard :]], axis=1
    )
    vec = add(vec, jnp.where(same, vec_got, turned))

    core = tensor_at % 2
    bit0 = dp_at % 2
    bit1 = (dp_at // 2 + dp_at // 4) % 2
    first = jnp.where(core == 0, bit0, bit1)
    second = jnp.where(core == 0, bit1, bit0)

    def pick(a, at):
        return lax.dynamic_index_in_dim(a, at, 0, False)

    def ordered(at, here, there):
        return jnp.where(at == 0, jnp.stack([here, there]), jnp.stack([there, here]))

    def sum_dp(a, extra=None):
        a = a.reshape(2, 2, -1, d)
        s = add(pick(a, first), swap_dp(pick(a, 1 - first), 1, 2))
        s = add(pick(s, second), swap_dp(pick(s, 1 - second), 2, 1))
        size = s.shape[0]
        if extra is not None:
            s = jnp.concatenate([s, extra], axis=0)
        far = [(4 << k) for k in range(n_dp.bit_length()) if (4 << k) < n_dp]
        for bit in far:
            mask = 6 if bit == 4 else bit
            s = add(s, swap_dp(s, mask, mask))
        got = swap_dp(s, 2, 1)
        if extra is not None:
            extra = add(s[size:], got[size:])
            s, got = s[:size], got[:size]
        s = ordered(second, s, got)
        if extra is None:
            got = swap_dp(s, 1, 2)
        else:
            got = swap_dp(jnp.concatenate([s.reshape(2 * size, d), extra], axis=0), 1, 2)
            extra = add(extra, got[2 * size :])
            got = got[: 2 * size].reshape(2, size, d)
        return ordered(first, s, got).astype(F32), extra

    fc, _ = sum_dp(add(fc_keep, swap_core(fc_send)))
    fc = fc.reshape(2, shard, d)
    rest, vec = sum_dp(add(keep, swap_core(send)), vec)
    rest = rest.reshape(4, shard, d)
    vec = vec.astype(F32)
    return (
        result, grad_tokens, vec[0], vec[1], rest[:3], rest[3], vec[2], vec[3], fc[0], vec[4, :shard],
        fc[1],
    )


def solution(mesh):
    in_specs = (
        P(("dp", "tensor"), None),
        P("dp"),
        P("dp"),
        P(),
        P(),
        P(None, "tensor", None),
        P("tensor", None),
        P(),
        P(),
        P("tensor", None),
        P("tensor"),
        P("tensor", None),
        P(("dp", "tensor"), None),
    )
    out_specs = (
        P(("dp", "tensor"), None),
        P(("dp", "tensor"), None),
        P(),
        P(),
        P(None, "tensor", None),
        P("tensor", None),
        P(),
        P(),
        P("tensor", None),
        P("tensor"),
        P("tensor", None),
    )
    step = functools.partial(local, mesh.shape["dp"], mesh.shape["tensor"])
    return jax.shard_map(step, mesh=mesh, in_specs=in_specs, out_specs=out_specs, check_vma=False)
```

time: 421 us -> 171 us (0.41)
  waiting for transfers between devices: 258 us -> 66.5 us
  blocking collectives: 63.6 us -> 0 us
  Pallas kernels: 0 us -> 42.5 us
  matrix products: 37.8 us -> 0 us
  starting transfers between devices: 0.55 us -> 35.1 us
  other arithmetic: 22.7 us -> 8.4 us
  between operations: 14.4 us -> 1.16 us
  local copies, waits for them, and re-layouts: 22.7 us -> 17.1 us
    psum x1 -> x0, waiting for transfers between devices: 98 us -> none  [local(): lax.psum((grad_qkv, grad_out, grad_fc1, grad_fc1_bias, grad_fc2), 'dp')]
    reduce_scatter x4 -> x0, waiting for transfers between devices: 80.6 us -> none  [the longest x1 28.3 us: local(): lax.psum_scatter(jnp.dot(row_piece, out_weight, preferred_element_type=jn...]
    all_gather x4 -> x0, waiting for transfers between devices: 78.8 us -> none  [the longest x1 22.4 us: local(): gathered_one = lax.all_gather(normed_one, 'tensor', axis=0, tiled=True)]
    ppermute x0 -> x28, waiting for transfers between devices: none -> 66.5 us  [the longest x9 36.2 us: swap_y(): return lax.ppermute(a, 'tensor', [(t, t ^ 2) for t in range(n_tensor)])]
    psum x2 -> x0, blocking collectives: 63.6 us -> none  [the longest x1 42 us: local(): lax.psum((grad_gain_one, grad_shift_one, grad_gain_two, grad_shift_two),...]
    pallas_call x0 -> x6, Pallas kernels: none -> 42.5 us  [the longest x1 18.8 us: backward(): pl.pallas_call(functools.partial(backward_kernel, half), grid=(2 * half,)...]
    dot_general x18 -> x0, matrix products: 37.8 us -> none  [the longest x3 9.3 us: contract_cols(): lax.dot_general(left_side, right_side, (((1,), (1,)), ((), ())), preferre...]
    ppermute x0 -> x28, starting transfers between devices: none -> 35.1 us  [the longest x10 23.2 us: swap_dp(): return lax.ppermute(a, ('dp', 'tensor'), pairs)]
  transfers between devices with their start and end apart: 9 -> 28, of which waited for: 8 -> 12; matrix products, arithmetic and copies ran while one was open for 5% -> 12% of each run, Pallas kernels for 0% -> 22%
where the time goes in v1:
time: 171 us
  waiting for transfers between devices  66.5 us (39%)
  Pallas kernels  42.5 us (25%)
  starting transfers between devices  35.1 us (21%)
  local copies, waits for them, and re-layouts  17.1 us (10%)
  other arithmetic  8.4 us (5%)
    ppermute x9, waiting for transfers between devices, swap_y(): return lax.ppermute(a, 'tensor', [(t, t ^ 2) for t in range(n_tensor)])  36.2 us
    ppermute x10, waiting for transfers between devices, swap_dp(): return lax.ppermute(a, ('dp', 'tensor'), pairs)  30.3 us
    ppermute x10, starting transfers between devices, swap_dp(): return lax.ppermute(a, ('dp', 'tensor'), pairs)  23.2 us
    pallas_call x1, Pallas kernels, backward(): pl.pallas_call(functools.partial(backward_kernel, half), grid=(2 * half,)...  18.8 us
    pallas_call x2, Pallas kernels, attention(): pl.pallas_call(functools.partial(attention_kernel, len(kept)), grid_spec=...  13.5 us
    ppermute x9, starting transfers between devices, swap_y(): return lax.ppermute(a, 'tensor', [(t, t ^ 2) for t in range(n_tensor)])  10.7 us
    pallas_call x1, Pallas kernels, feed(): pl.pallas_call(functools.partial(feed_kernel, half), grid=(2 * half,), in...  5.77 us
    unnamed x50, local copies, waits for them, and re-layouts  4.98 us
  transfers between devices with their start and end apart: 28, of which 12 were waited for; matrix products, arithmetic and copies ran while one was open for 12% of the time, Pallas kernels for 22%

profile of v1, /device:TPU:0, one launch (start us, length us, event | category | flops | bytes accessed | tf_op | source)
XLA Modules:
  0.0 170.7 jit_solution(3743061464499480568)
XLA Ops:
  0.7 3.0 %collective-permute-start = (bf16[256,768]{1,0:T(8,128)(2,1)}, bf16[256,768]{1,0:T(8,128)(2,1)S(1)}, u32[]{:S(2)}, u32[]{:S(2)}) collective-permute-start(bf16[256,768]{1,0:T(8,128)(2,1)} %x_ref.3), channel_id=1, source_target_pairs={{0,2},{1,3},{2,0},{3,1},{4,6},{5,7},{6,4},{7,5},{8,10},{9,11},{10,... | collective-permute-start | bytes 1179656 | tf_op jit(solution)/shard_map/ppermute | solution.py:432
  4.7 1.9 %pad_maximum_fusion.1 = bf16[384,768]{1,0:T(8,128)(2,1)} fusion(bf16[192,768]{1,0:T(8,128)(2,1)} %param.22, bf16[192,768]{1,0:T(8,128)(2,1)} %param.19), kind=kLoop, calls=%fused_computation.10 | loop fusion | flops 1179648 | bytes 1179648 | tf_op jit(solution)/shard_map/concatenate | solution.py:459
  6.6 0.7 constant_dynamic-update-slice_fusion.3
  7.4 1.2 constant_dynamic-update-slice_fusion.1
  8.7 4.4 %collective-permute-done.x_ref.x1 = bf16[256,768]{1,0:T(8,128)(2,1)S(1)} collective-permute-done((bf16[256,768]{1,0:T(8,128)(2,1)}, bf16[256,768]{1,0:T(8,128)(2,1)S(1)}, u32[]{:S(2)}, u32[]{:S(2)}) %collective-permute-start) | collective-permute-done | bytes 393248 | tf_op jit(solution)/shard_map/ppermute | solution.py:432
  13.0 1.7 %collective-permute-start.6 = (bf16[384,768]{1,0:T(8,128)(2,1)}, bf16[384,768]{1,0:T(8,128)(2,1)}, u32[]{:S(2)}, u32[]{:S(2)}) collective-permute-start(bf16[384,768]{1,0:T(8,128)(2,1)} %pad_maximum_fusion.1), channel_id=1, source_target_pairs={{0,2},{1,3},{2,0},{3,1},{4,6},{5,7},{6,4},{7,5},{8,10},{9,11},{10,... | collective-permute-start | bytes 1769480 | tf_op jit(solution)/shard_map/ppermute | solution.py:432
  15.5 1.0 constant_dynamic-update-slice_fusion.7
  16.8 1.7 constant_dynamic-update-slice_fusion.2.wa_ref.wo_ref
  18.5 1.7 constant_dynamic-update-slice_fusion.4.fc1_ref.fa_ref
  20.2 7.7 %collective-permute-done.6 = bf16[384,768]{1,0:T(8,128)(2,1)} collective-permute-done((bf16[384,768]{1,0:T(8,128)(2,1)}, bf16[384,768]{1,0:T(8,128)(2,1)}, u32[]{:S(2)}, u32[]{:S(2)}) %collective-permute-start.6) | collective-permute-done | bytes 589856 | tf_op jit(solution)/shard_map/ppermute | solution.py:432
  27.9 1.5 collective-permute-start.4
  29.4 1.2 constant_dynamic-update-slice_fusion.w_ref
  30.7 6.8 %attention_forward.2 = (bf16[512,768]{1,0:T(8,128)(2,1)S(1)}, bf16[384,512]{1,0:T(8,128)(2,1)S(1)}, bf16[384,512]{1,0:T(8,128)(2,1)S(1)}, bf16[512,384]{1,0:T(8,...) custom-call(s32[1]{0:T(128)} %bitcast.place_ref, ...), custom_call_target="tpu_custom_call" | custom-call | flops 855638016 | bytes 4521984 | tf_op jit(solution)/shard_map/attention_forward/pallas_call | solution.py:126
  37.4 6.7 %attention_forward.3 = (bf16[512,768]{1,0:T(8,128)(2,1)S(1)}, bf16[384,512]{1,0:T(8,128)(2,1)S(1)}, bf16[384,512]{1,0:T(8,128)(2,1)S(1)}, bf16[512,384]{1,0:T(8,...) custom-call(s32[1]{0:T(128)} %bitcast.1.place_ref, ...), custom_call_target="tpu_custom_call", output_to_operand_aliasing={{0}: (7, {}), {1}: (8, {}), {2}: (9, {}), {3}: (10, {}), {4... | custom-call | flops 855638016 | bytes 4521984 | tf_op jit(solution)/shard_map/attention_forward/pallas_call | solution.py:126
  44.8 1.4 collective-permute-start.3
  46.2 1.1 fusion.8
  47.4 4.5 %collective-permute-done.2.ob0 = bf16[256,384]{1,0:T(8,128)(2,1)S(1)} collective-permute-done((bf16[256,384]{1,0:T(8,128)(2,1)S(1)}, bf16[256,384]{1,0:T(8,128)(2,1)S(1)}, u32[]{:S(2)}, u32[]{:S(2)}) %collective-permute-start.2) | collective-permute-done | bytes 196640 | tf_op jit(solution)/shard_map/ppermute | solution.py:432
  51.9 3.5 %collective-permute-done.3.ob1 = bf16[256,384]{1,0:T(8,128)(2,1)S(1)} collective-permute-done((bf16[256,384]{1,0:T(8,128)(2,1)S(1)}, bf16[256,384]{1,0:T(8,128)(2,1)S(1)}, u32[]{:S(2)}, u32[]{:S(2)}) %collective-permute-start.3) | collective-permute-done | bytes 196640 | tf_op jit(solution)/shard_map/ppermute | solution.py:432
  55.4 5.8 %feed_forward.1 = (f32[512,768]{1,0:T(8,128)}, bf16[512,768]{1,0:T(8,128)(2,1)}, bf16[512,384]{1,0:T(8,128)(2,1)S(1)}, bf16[512,384]{1,0:T(8,128)(2,1)S(1)}) custom-call(bf16[256,768]{1,0:T(8,128)(2,1)S(1)} %copy-done.2, bf16[256,768]{1,0:T(8,128)(2,1)S(1)} %collective-permute-done.x_ref.x1, bf16[256,384]{1,0:T(8,128)(2,1)S(1)} %get-tuple-element.46.oa0, ...), custom_call_target="tpu_custom_call" | custom-call | flops 1207959552 | bytes 4718592 | tf_op jit(solution)/shard_map/feed_forward/pallas_call | solution.py:186
  61.8 1.1 copy-done.7
  62.9 3.2 %feed_grads.1 = (bf16[384,768]{1,0:T(8,128)(2,1)S(1)}, bf16[384,768]{1,0:T(8,128)(2,1)}, f32[1,384]{1,0:T(1,128)S(1)}, f32[256,768]{1,0:T(8,128)S(1)}, bf16[256,768]{1,0:T(8,128)(2,1)S(1)}) custom-call(bf16[512,384]{1,0:T(8,128)(2,1)S(1)} %get-tuple-element.56.z_ref, bf16[512,384]{1,0:T(8,128)(2,1)S(1)} %get-tuple-element.57.du_ref.du0.du1, ...), custom_call_target="tpu_custom_call" | custom-call | flops 905969664 | bytes 3538944 | tf_op jit(solution)/shard_map/feed_grads/pallas_call | solution.py:234
  66.1 5.5 %collective-permute-done.12.dr0.dr1 = bf16[512,384]{1,0:T(8,128)(2,1)S(1)} collective-permute-done((bf16[512,384]{1,0:T(8,128)(2,1)S(1)}, bf16[512,384]{1,0:T(8,128)(2,1)S(1)}, u32[]{:S(2)}, u32[]{:S(2)}) %collective-permute-start.12) | collective-permute-done | bytes 393248 | tf_op jit(solution)/shard_map/ppermute | solution.py:432
  71.6 18.8 %attention_backward.1 = (bf16[4,192,768]{2,1,0:T(8,128)(2,1)}, bf16[4,192,768]{2,1,0:T(8,128)(2,1)}, f32[256,768]{1,0:T(8,128)S(1)}, f32[8,768]{1,0:T(8,128)S(1)...) custom-call(bf16[512,384]{1,0:T(8,128)(2,1)S(1)} %get-tuple-element.57.du_ref.du0.du1, ...), custom_call_target="tpu_custom_call" | custom-call | flops 3321888768 | bytes 7864320 | tf_op jit(solution)/shard_map/attention_backward/pallas_call | solution.py:335
  91.1 1.4 add_convert_fusion.1
  92.5 9.7 %collective-permute-done.13.got_ref = bf16[256,768]{1,0:T(8,128)(2,1)S(1)} collective-permute-done((bf16[256,768]{1,0:T(8,128)(2,1)}, bf16[256,768]{1,0:T(8,128)(2,1)S(1)}, u32[]{:S(2)}, u32[]{:S(2)}) %collective-permute-start.13) | collective-permute-done | bytes 393248 | tf_op jit(solution)/shard_map/ppermute | solution.py:432
  102.2 1.4 input_norm.1
  104.9 1.4 collective-permute-start.23
  106.3 1.1 collective-permute-done.17
  107.5 1.5 add_convert_fusion
  109.1 0.9 dynamic-slice_bitcast_fusion
  110.0 1.5 collective-permute-start.15
  112.2 1.6 collective-permute-start.24
  113.8 7.9 %collective-permute-done.15 = bf16[2,192,768]{2,1,0:T(8,128)(2,1)} collective-permute-done((bf16[2,192,768]{2,1,0:T(8,128)(2,1)}, bf16[2,192,768]{2,1,0:T(8,128)(2,1)}, u32[]{:S(2)}, u32[]{:S(2)}) %collective-permute-start.15) | collective-permute-done | bytes 589856 | tf_op jit(solution)/shard_map/ppermute | solution.py:440
  121.7 1.2 fusion
  123.0 1.6 collective-permute-start.16
  124.8 2.6 %collective-permute-start.25 = (bf16[96,768]{1,0:T(8,128)(2,1)S(1)}, bf16[96,768]{1,0:T(8,128)(2,1)S(1)}, u32[]{:S(2)}, u32[]{:S(2)}) collective-permute-start(bf16[96,768]{1,0:T(8,128)(2,1)S(1)} %fusion.4), channel_id=1, source_target_pairs={{0,24},{1,25},{2,26},{3,27},{4,28},{5,29},{6,30},{7,31},{8,16},{9,... | collective-permute-start | bytes 442376 | tf_op jit(solution)/shard_map/ppermute | solution.py:440
  127.3 3.7 %collective-permute-done.16 = bf16[192,768]{1,0:T(8,128)(2,1)S(1)} collective-permute-done((bf16[192,768]{1,0:T(8,128)(2,1)S(1)}, bf16[192,768]{1,0:T(8,128)(2,1)S(1)}, u32[]{:S(2)}, u32[]{:S(2)}) %collective-permute-start.16) | collective-permute-done | bytes 294944 | tf_op jit(solution)/shard_map/ppermute | solution.py:440
  131.2 5.5 %collective-permute-start.19 = (bf16[208,768]{1,0:T(8,128)(2,1)S(1)}, bf16[208,768]{1,0:T(8,128)(2,1)S(1)}, u32[]{:S(2)}, u32[]{:S(2)}) collective-permute-start(bf16[208,768]{1,0:T(8,128)(2,1)S(1)} %pad_maximum_fusion.4), channel_id=1, source_target_pairs={{0,24},{1,25},{2,26},{3,27},{4,28},{5,29},{6,30},{7,31},{8,16},{9,... | collective-permute-start | bytes 958472 | tf_op jit(solution)/shard_map/ppermute | solution.py:440
  136.7 0.8 add_convert_fusion.2
  137.6 4.2 %collective-permute-done.19 = bf16[208,768]{1,0:T(8,128)(2,1)S(1)} collective-permute-done((bf16[208,768]{1,0:T(8,128)(2,1)S(1)}, bf16[208,768]{1,0:T(8,128)(2,1)S(1)}, u32[]{:S(2)}, u32[]{:S(2)}) %collective-permute-start.19) | collective-permute-done | bytes 319520 | tf_op jit(solution)/shard_map/ppermute | solution.py:440
  142.0 6.5 %collective-permute-start.20 = (bf16[208,768]{1,0:T(8,128)(2,1)S(1)}, bf16[208,768]{1,0:T(8,128)(2,1)S(1)}, u32[]{:S(2)}, u32[]{:S(2)}) collective-permute-start(bf16[208,768]{1,0:T(8,128)(2,1)S(1)} %add_convert_fusion.3), channel_id=1, source_target_pairs={{0,8},{1,5},{2,10},{3,7},{4,12},{5,1},{6,14},{7,3},{8,0},{9,13},{1... | collective-permute-start | bytes 958472 | tf_op jit(solution)/shard_map/ppermute | solution.py:440
  148.5 1.4 collective-permute-start.27
  149.9 6.5 %collective-permute-done.20 = bf16[208,768]{1,0:T(8,128)(2,1)S(1)} collective-permute-done((bf16[208,768]{1,0:T(8,128)(2,1)S(1)}, bf16[208,768]{1,0:T(8,128)(2,1)S(1)}, u32[]{:S(2)}, u32[]{:S(2)}) %collective-permute-start.20) | collective-permute-done | bytes 319520 | tf_op jit(solution)/shard_map/ppermute | solution.py:440
  156.6 1.0 collective-permute-start.21
  157.8 1.1 fusion.7
  158.9 7.9 %collective-permute-done.21 = bf16[400,768]{1,0:T(8,128)(2,1)S(1)} collective-permute-done((bf16[400,768]{1,0:T(8,128)(2,1)S(1)}, bf16[400,768]{1,0:T(8,128)(2,1)S(1)}, u32[]{:S(2)}, u32[]{:S(2)}) %collective-permute-start.21) | collective-permute-done | bytes 614432 | tf_op jit(solution)/shard_map/ppermute | solution.py:440
  167.4 1.3 slice.105
  168.7 0.9 slice_bitcast_fusion
  (117 shorter events, 9.0 us)
Async XLA Ops:
  0.6 6.0 %copy-start.16 = (bf16[192,768]{1,0:T(8,128)(2,1)S(1)}, bf16[192,768]{1,0:T(8,128)(2,1)}, u32[]{:S(2)}) copy-start(bf16[192,768]{1,0:T(8,128)(2,1)} %param.19) | copy-start | bytes 884740
  0.7 6.7 %copy-start.22 = (bf16[192]{0:T(256)(128)(2,1)S(1)}, bf16[192]{0:T(256)(128)(2,1)}, u32[]{:S(2)}) copy-start(bf16[192]{0:T(256)(128)(2,1)} %param.23) | copy-start | bytes 1156
  0.7 6.7 %copy-start.18 = (f32[768]{0:T(1024)S(1)}, f32[768]{0:T(1024)}, u32[]{:S(2)}) copy-start(f32[768]{0:T(1024)} %param.16) | copy-start | bytes 9220
  0.7 12.4 %collective-permute-start = (bf16[256,768]{1,0:T(8,128)(2,1)}, bf16[256,768]{1,0:T(8,128)(2,1)S(1)}, u32[]{:S(2)}, u32[]{:S(2)}) collective-permute-start(bf16[256,768]{1,0:T(8,128)(2,1)} %x_ref.3), channel_id=1, source_target_pairs={{0,2},{1,3},{2,0},{3,1},{4,6},{5,7},{6,4},{7,5},{8,10},{9,11},{10,... | collective-permute-start | bytes 1179656 | tf_op jit(solution)/shard_map/ppermute | solution.py:432
  3.7 25.7 %collective-permute-start.1 = (bf16[3,192,768]{2,1,0:T(8,128)(2,1)}, bf16[3,192,768]{2,1,0:T(8,128)(2,1)}, u32[]{:S(2)}, u32[]{:S(2)}) collective-permute-start(bf16[3,192,768]{2,1,0:T(8,128)(2,1)} %param.18), channel_id=1, source_target_pairs={{0,1},{1,0},{2,3},{3,2},{4,5},{5,4},{6,7},{7,6},{8,9},{9,8},{10,11... | collective-permute-start | bytes 2654216 | tf_op jit(solution)/shard_map/ppermute | solution.py:429
  3.7 13.1 %collective-permute-start.5 = (bf16[192,768]{1,0:T(8,128)(2,1)}, bf16[192,768]{1,0:T(8,128)(2,1)}, u32[]{:S(2)}, u32[]{:S(2)}) collective-permute-start(bf16[192,768]{1,0:T(8,128)(2,1)} %param.19), channel_id=1, source_target_pairs={{0,1},{1,0},{2,3},{3,2},{4,5},{5,4},{6,7},{7,6},{8,9},{9,8},{10,11... | collective-permute-start | bytes 884744 | tf_op jit(solution)/shard_map/ppermute | solution.py:429
  4.2 14.3 %collective-permute-start.8 = (bf16[192,768]{1,0:T(8,128)(2,1)}, bf16[192,768]{1,0:T(8,128)(2,1)}, u32[]{:S(2)}, u32[]{:S(2)}) collective-permute-start(bf16[192,768]{1,0:T(8,128)(2,1)} %param.22), channel_id=1, source_target_pairs={{0,1},{1,0},{2,3},{3,2},{4,5},{5,4},{6,7},{7,6},{8,9},{9,8},{10,11... | collective-permute-start | bytes 884744 | tf_op jit(solution)/shard_map/ppermute | solution.py:429
  4.2 12.4 %collective-permute-start.9 = (bf16[192]{0:T(256)(128)(2,1)}, bf16[192]{0:T(256)(128)(2,1)S(1)}, u32[]{:S(2)}, u32[]{:S(2)}) collective-permute-start(bf16[192]{0:T(256)(128)(2,1)} %param.23), channel_id=1, source_target_pairs={{0,1},{1,0},{2,3},{3,2},{4,5},{5,4},{6,7},{7,6},{8,9},{9,8},{10,11... | collective-permute-start | bytes 1160 | tf_op jit(solution)/shard_map/ppermute | solution.py:429
  6.6 8.1 %copy-start.17 = (bf16[192,768]{1,0:T(8,128)(2,1)S(1)}, bf16[192,768]{1,0:T(8,128)(2,1)}, u32[]{:S(2)}) copy-start(bf16[192,768]{1,0:T(8,128)(2,1)} %param.22) | copy-start | bytes 884740
  7.4 9.2 %copy-start.19 = (f32[768]{0:T(1024)S(1)}, f32[768]{0:T(1024)}, u32[]{:S(2)}) copy-start(f32[768]{0:T(1024)} %param.17) | copy-start | bytes 9220
  7.4 9.2 %copy-start.20 = (f32[768]{0:T(1024)S(1)}, f32[768]{0:T(1024)}, u32[]{:S(2)}) copy-start(f32[768]{0:T(1024)} %param.20) | copy-start | bytes 9220
  7.4 9.2 %copy-start.21 = (f32[768]{0:T(1024)S(1)}, f32[768]{0:T(1024)}, u32[]{:S(2)}) copy-start(f32[768]{0:T(1024)} %param.21) | copy-start | bytes 9220
  13.0 14.8 %collective-permute-start.6 = (bf16[384,768]{1,0:T(8,128)(2,1)}, bf16[384,768]{1,0:T(8,128)(2,1)}, u32[]{:S(2)}, u32[]{:S(2)}) collective-permute-start(bf16[384,768]{1,0:T(8,128)(2,1)} %pad_maximum_fusion.1), channel_id=1, source_target_pairs={{0,2},{1,3},{2,0},{3,1},{4,6},{5,7},{6,4},{7,5},{8,10},{9,11},{10,... | collective-permute-start | bytes 1769480 | tf_op jit(solution)/shard_map/ppermute | solution.py:432
  15.5 12.4 %copy-start.1 = (bf16[256,768]{1,0:T(8,128)(2,1)S(1)}, bf16[256,768]{1,0:T(8,128)(2,1)}, u32[]{:S(2)}) copy-start(bf16[256,768]{1,0:T(8,128)(2,1)} %g0.5) | copy-start | bytes 1179652
  16.6 11.2 %collective-permute-start.10 = (bf16[192,768]{1,0:T(8,128)(2,1)}, bf16[192,768]{1,0:T(8,128)(2,1)S(1)}, u32[]{:S(2)}, u32[]{:S(2)}) collective-permute-start(bf16[192,768]{1,0:T(8,128)(2,1)} %param.24), channel_id=1, source_target_pairs={{0,1},{1,0},{2,3},{3,2},{4,5},{5,4},{6,7},{7,6},{8,9},{9,8},{10,11... | collective-permute-start | bytes 884744 | tf_op jit(solution)/shard_map/ppermute | solution.py:429
  20.2 10.4 %copy-start.2 = (bf16[256,768]{1,0:T(8,128)(2,1)S(1)}, bf16[256,768]{1,0:T(8,128)(2,1)}, u32[]{:S(2)}) copy-start(bf16[256,768]{1,0:T(8,128)(2,1)} %x_ref.3) | copy-start | bytes 1179652
  20.2 10.5 %copy-start.9 = (s32[8]{0:T(128)S(1)}, s32[8]{0:T(128)}, u32[]{:S(2)}) copy-start(s32[8]{0:T(128)} %nodes_ref.3) | copy-start | bytes 100
  20.2 10.5 %copy-start.10 = (s32[8]{0:T(128)S(1)}, s32[8]{0:T(128)}, u32[]{:S(2)}) copy-start(s32[8]{0:T(128)} %edges_ref.3) | copy-start | bytes 100
  27.9 19.4 %collective-permute-start.7 = (bf16[384,768]{1,0:T(8,128)(2,1)}, bf16[384,768]{1,0:T(8,128)(2,1)S(1)}, u32[]{:S(2)}, u32[]{:S(2)}) collective-permute-start(bf16[384,768]{1,0:T(8,128)(2,1)} %collective-permute-done.6), channel_id=1, source_target_pairs={{0,1},{1,0},{2,3},{3,2},{4,5},{5,4},{6,7},{7,6},{8,9},{9,8},{10,11... | collective-permute-start | bytes 1769480 | tf_op jit(solution)/shard_map/ppermute | solution.py:429
  27.9 19.5 %collective-permute-start.4 = (bf16[256,768]{1,0:T(8,128)(2,1)S(1)}, bf16[256,768]{1,0:T(8,128)(2,1)S(1)}, u32[]{:S(2)}, u32[]{:S(2)}) collective-permute-start(bf16[256,768]{1,0:T(8,128)(2,1)S(1)} %copy-done.1), channel_id=1, source_target_pairs={{0,2},{1,3},{2,0},{3,1},{4,6},{5,7},{6,4},{7,5},{8,10},{9,11},{10,... | collective-permute-start | bytes 1179656 | tf_op jit(solution)/shard_map/ppermute | solution.py:432
  30.6 6.8 %copy-start = (bf16[3,384,768]{2,1,0:T(8,128)(2,1)}, bf16[3,384,768]{2,1,0:T(8,128)(2,1)S(1)}, u32[]{:S(2)}) copy-start(bf16[3,384,768]{2,1,0:T(8,128)(2,1)S(1)} %constant_dynamic-update-slice_fusion.w_ref) | copy-start | bytes 5308420
  44.1 3.2 %copy-start.5 = (bf16[512,768]{1,0:T(8,128)(2,1)}, bf16[512,768]{1,0:T(8,128)(2,1)S(1)}, u32[]{:S(2)}) copy-start(bf16[512,768]{1,0:T(8,128)(2,1)S(1)} %get-tuple-element.67.a1_ref) | copy-start | bytes 2359300
  44.1 7.7 %collective-permute-start.2 = (bf16[256,384]{1,0:T(8,128)(2,1)S(1)}, bf16[256,384]{1,0:T(8,128)(2,1)S(1)}, u32[]{:S(2)}, u32[]{:S(2)}) collective-permute-start(bf16[256,384]{1,0:T(8,128)(2,1)S(1)} %get-tuple-element.53.oa1), channel_id=1, source_target_pairs={{0,2},{1,3},{2,0},{3,1},{4,6},{5,7},{6,4},{7,5},{8,10},{9,11},{10,... | collective-permute-start | bytes 589832 | tf_op jit(solution)/shard_map/ppermute | solution.py:432
  44.8 10.6 %collective-permute-start.3 = (bf16[256,384]{1,0:T(8,128)(2,1)S(1)}, bf16[256,384]{1,0:T(8,128)(2,1)S(1)}, u32[]{:S(2)}, u32[]{:S(2)}) collective-permute-start(bf16[256,384]{1,0:T(8,128)(2,1)S(1)} %get-tuple-element.46.oa0), channel_id=1, source_target_pairs={{0,2},{1,3},{2,0},{3,1},{4,6},{5,7},{6,4},{7,5},{8,10},{9,11},{10,... | collective-permute-start | bytes 589832 | tf_op jit(solution)/shard_map/ppermute | solution.py:432
  47.3 8.1 %copy-start.3 = (bf16[384,768]{1,0:T(8,128)(2,1)S(1)}, bf16[384,768]{1,0:T(8,128)(2,1)}, u32[]{:S(2)}) copy-start(bf16[384,768]{1,0:T(8,128)(2,1)} %constant_dynamic-update-slice_fusion.2.wa_ref.wo_ref) | copy-start | bytes 1769476
  47.3 8.1 %copy-start.4 = (bf16[384,768]{1,0:T(8,128)(2,1)S(1)}, bf16[384,768]{1,0:T(8,128)(2,1)}, u32[]{:S(2)}) copy-start(bf16[384,768]{1,0:T(8,128)(2,1)} %constant_dynamic-update-slice_fusion.4.fc1_ref.fa_ref) | copy-start | bytes 1769476
  61.2 10.4 %collective-permute-start.12 = (bf16[512,384]{1,0:T(8,128)(2,1)S(1)}, bf16[512,384]{1,0:T(8,128)(2,1)S(1)}, u32[]{:S(2)}, u32[]{:S(2)}) collective-permute-start(bf16[512,384]{1,0:T(8,128)(2,1)S(1)} %get-tuple-element.57.du_ref.du0.du1), channel_id=1, source_target_pairs={{0,2},{1,3},{2,0},{3,1},{4,6},{5,7},{6,4},{7,5},{8,10},{9,11},{10,... | collective-permute-start | bytes 1179656 | tf_op jit(solution)/shard_map/ppermute | solution.py:432
  66.1 5.5 %copy-start.11 = (bf16[256,768]{1,0:T(8,128)(2,1)}, bf16[256,768]{1,0:T(8,128)(2,1)S(1)}, u32[]{:S(2)}) copy-start(bf16[256,768]{1,0:T(8,128)(2,1)S(1)} %get-tuple-element.61) | copy-start | bytes 1179652
  66.1 24.3 %copy-start.8 = (bf16[384,768]{1,0:T(8,128)(2,1)}, bf16[384,768]{1,0:T(8,128)(2,1)S(1)}, u32[]{:S(2)}) copy-start(bf16[384,768]{1,0:T(8,128)(2,1)S(1)} %get-tuple-element.77) | copy-start | bytes 1769476
  66.1 25.1 %collective-permute-start.22 = (bf16[384,768]{1,0:T(8,128)(2,1)}, bf16[384,768]{1,0:T(8,128)(2,1)}, u32[]{:S(2)}, u32[]{:S(2)}) collective-permute-start(bf16[384,768]{1,0:T(8,128)(2,1)} %get-tuple-element.78), channel_id=1, source_target_pairs={{0,1},{1,0},{2,3},{3,2},{4,5},{5,4},{6,7},{7,6},{8,9},{9,8},{10,11... | collective-permute-start | bytes 1769480 | tf_op jit(solution)/shard_map/ppermute | solution.py:429
  90.4 11.8 %copy-start.6 = (f32[256,768]{1,0:T(8,128)S(1)}, f32[256,768]{1,0:T(8,128)}, u32[]{:S(2)}) copy-start(f32[256,768]{1,0:T(8,128)} %get-tuple-element.68.mine_ref) | copy-start | bytes 2359300
  90.4 17.1 %collective-permute-start.14 = (bf16[4,192,768]{2,1,0:T(8,128)(2,1)}, bf16[4,192,768]{2,1,0:T(8,128)(2,1)}, u32[]{:S(2)}, u32[]{:S(2)}) collective-permute-start(bf16[4,192,768]{2,1,0:T(8,128)(2,1)} %get-tuple-element.75), channel_id=1, source_target_pairs={{0,1},{1,0},{2,3},{3,2},{4,5},{5,4},{6,7},{7,6},{8,9},{9,8},{10,11... | collective-permute-start | bytes 3538952 | tf_op jit(solution)/shard_map/ppermute | solution.py:429
  90.5 11.7 %collective-permute-start.13 = (bf16[256,768]{1,0:T(8,128)(2,1)}, bf16[256,768]{1,0:T(8,128)(2,1)S(1)}, u32[]{:S(2)}, u32[]{:S(2)}) collective-permute-start(bf16[256,768]{1,0:T(8,128)(2,1)} %get-tuple-element.69), channel_id=1, source_target_pairs={{0,2},{1,3},{2,0},{3,1},{4,6},{5,7},{6,4},{7,5},{8,10},{9,11},{10,... | collective-permute-start | bytes 1179656 | tf_op jit(solution)/shard_map/ppermute | solution.py:432
  92.5 11.7 %copy-start.13 = (bf16[384,768]{1,0:T(8,128)(2,1)}, bf16[384,768]{1,0:T(8,128)(2,1)S(1)}, u32[]{:S(2)}) copy-start(bf16[384,768]{1,0:T(8,128)(2,1)S(1)} %add_convert_fusion.1) | copy-start | bytes 1769476
  102.2 5.3 %copy-start.15 = (bf16[4,192,768]{2,1,0:T(8,128)(2,1)S(1)}, bf16[4,192,768]{2,1,0:T(8,128)(2,1)}, u32[]{:S(2)}) copy-start(bf16[4,192,768]{2,1,0:T(8,128)(2,1)} %get-tuple-element.74) | copy-start | bytes 3538948
  103.6 3.8 %collective-permute-start.17 = (bf16[16,768]{1,0:T(8,128)(2,1)S(1)}, bf16[16,768]{1,0:T(8,128)(2,1)S(1)}, u32[]{:S(2)}, u32[]{:S(2)}) collective-permute-start(bf16[16,768]{1,0:T(8,128)(2,1)S(1)} %get-tuple-element.76), channel_id=1, source_target_pairs={{0,2},{1,3},{2,0},{3,1},{4,6},{5,7},{6,4},{7,5},{8,10},{9,11},{10,... | collective-permute-start | bytes 73736 | tf_op jit(solution)/shard_map/ppermute | solution.py:432
  104.9 7.1 %collective-permute-start.23 = (bf16[2,96,768]{2,1,0:T(8,128)(2,1)}, bf16[2,96,768]{2,1,0:T(8,128)(2,1)S(1)}, u32[]{:S(2)}, u32[]{:S(2)}) collective-permute-start(bf16[2,96,768]{2,1,0:T(8,128)(2,1)} %dynamic-slice_bitcast_fusion.1), channel_id=1, source_target_pairs={{0,4},{1,9},{2,6},{3,11},{4,0},{5,13},{6,2},{7,15},{8,12},{9,1},{1... | collective-permute-start | bytes 884744 | tf_op jit(solution)/shard_map/ppermute | solution.py:440
  107.5 4.5 %collective-permute-start.18 = (bf16[16,768]{1,0:T(8,128)(2,1)S(1)}, bf16[16,768]{1,0:T(8,128)(2,1)S(1)}, u32[]{:S(2)}, u32[]{:S(2)}) collective-permute-start(bf16[16,768]{1,0:T(8,128)(2,1)S(1)} %fusion.5), channel_id=1, source_target_pairs={{0,1},{1,0},{2,3},{3,2},{4,5},{5,4},{6,7},{7,6},{8,9},{9,8},{10,11... | collective-permute-start | bytes 73736 | tf_op jit(solution)/shard_map/ppermute | solution.py:429
  110.0 11.8 %collective-permute-start.15 = (bf16[2,192,768]{2,1,0:T(8,128)(2,1)}, bf16[2,192,768]{2,1,0:T(8,128)(2,1)}, u32[]{:S(2)}, u32[]{:S(2)}) collective-permute-start(bf16[2,192,768]{2,1,0:T(8,128)(2,1)} %dynamic-slice_bitcast_fusion), channel_id=1, source_target_pairs={{0,4},{1,9},{2,6},{3,11},{4,0},{5,13},{6,2},{7,15},{8,12},{9,1},{1... | collective-permute-start | bytes 1769480 | tf_op jit(solution)/shard_map/ppermute | solution.py:440
  111.4 25.3 %collective-permute-start.11 = (bf16[256,768]{1,0:T(8,128)(2,1)S(1)}, bf16[256,768]{1,0:T(8,128)(2,1)S(1)}, u32[]{:S(2)}, u32[]{:S(2)}) collective-permute-start(bf16[256,768]{1,0:T(8,128)(2,1)S(1)} %copy-done.12), channel_id=1, source_target_pairs={{0,2},{1,3},{2,0},{3,1},{4,6},{5,7},{6,4},{7,5},{8,10},{9,11},{10,... | collective-permute-start | bytes 1179656 | tf_op jit(solution)/shard_map/ppermute | solution.py:432
  112.2 12.5 %collective-permute-start.24 = (bf16[96,768]{1,0:T(8,128)(2,1)S(1)}, bf16[96,768]{1,0:T(8,128)(2,1)S(1)}, u32[]{:S(2)}, u32[]{:S(2)}) collective-permute-start(bf16[96,768]{1,0:T(8,128)(2,1)S(1)} %dynamic-slice_bitcast_fusion.3), channel_id=1, source_target_pairs={{0,8},{1,5},{2,10},{3,7},{4,12},{5,1},{6,14},{7,3},{8,0},{9,13},{1... | collective-permute-start | bytes 442376 | tf_op jit(solution)/shard_map/ppermute | solution.py:440
  123.0 8.1 %collective-permute-start.16 = (bf16[192,768]{1,0:T(8,128)(2,1)S(1)}, bf16[192,768]{1,0:T(8,128)(2,1)S(1)}, u32[]{:S(2)}, u32[]{:S(2)}) collective-permute-start(bf16[192,768]{1,0:T(8,128)(2,1)S(1)} %dynamic-slice_bitcast_fusion.2), channel_id=1, source_target_pairs={{0,8},{1,5},{2,10},{3,7},{4,12},{5,1},{6,14},{7,3},{8,0},{9,13},{1... | collective-permute-start | bytes 884744 | tf_op jit(solution)/shard_map/ppermute | solution.py:440
  124.8 12.8 %collective-permute-start.25 = (bf16[96,768]{1,0:T(8,128)(2,1)S(1)}, bf16[96,768]{1,0:T(8,128)(2,1)S(1)}, u32[]{:S(2)}, u32[]{:S(2)}) collective-permute-start(bf16[96,768]{1,0:T(8,128)(2,1)S(1)} %fusion.4), channel_id=1, source_target_pairs={{0,24},{1,25},{2,26},{3,27},{4,28},{5,29},{6,30},{7,31},{8,16},{9,... | collective-permute-start | bytes 442376 | tf_op jit(solution)/shard_map/ppermute | solution.py:440
  131.2 10.7 %collective-permute-start.19 = (bf16[208,768]{1,0:T(8,128)(2,1)S(1)}, bf16[208,768]{1,0:T(8,128)(2,1)S(1)}, u32[]{:S(2)}, u32[]{:S(2)}) collective-permute-start(bf16[208,768]{1,0:T(8,128)(2,1)S(1)} %pad_maximum_fusion.4), channel_id=1, source_target_pairs={{0,24},{1,25},{2,26},{3,27},{4,28},{5,29},{6,30},{7,31},{8,16},{9,... | collective-permute-start | bytes 958472 | tf_op jit(solution)/shard_map/ppermute | solution.py:440
  137.6 10.9 %collective-permute-start.26 = (bf16[96,768]{1,0:T(8,128)(2,1)S(1)}, bf16[96,768]{1,0:T(8,128)(2,1)S(1)}, u32[]{:S(2)}, u32[]{:S(2)}) collective-permute-start(bf16[96,768]{1,0:T(8,128)(2,1)S(1)} %add_convert_fusion.4), channel_id=1, source_target_pairs={{0,8},{1,5},{2,10},{3,7},{4,12},{5,1},{6,14},{7,3},{8,0},{9,13},{1... | collective-permute-start | bytes 442376 | tf_op jit(solution)/shard_map/ppermute | solution.py:440
  142.0 14.5 %collective-permute-start.20 = (bf16[208,768]{1,0:T(8,128)(2,1)S(1)}, bf16[208,768]{1,0:T(8,128)(2,1)S(1)}, u32[]{:S(2)}, u32[]{:S(2)}) collective-permute-start(bf16[208,768]{1,0:T(8,128)(2,1)S(1)} %add_convert_fusion.3), channel_id=1, source_target_pairs={{0,8},{1,5},{2,10},{3,7},{4,12},{5,1},{6,14},{7,3},{8,0},{9,13},{1... | collective-permute-start | bytes 958472 | tf_op jit(solution)/shard_map/ppermute | solution.py:440
  148.5 9.2 %collective-permute-start.27 = (bf16[2,96,768]{2,1,0:T(8,128)(2,1)S(1)}, bf16[2,96,768]{2,1,0:T(8,128)(2,1)S(1)}, u32[]{:S(2)}, u32[]{:S(2)}) collective-permute-start(bf16[2,96,768]{2,1,0:T(8,128)(2,1)S(1)} %maximum_select_fusion.5), channel_id=1, source_target_pairs={{0,4},{1,9},{2,6},{3,11},{4,0},{5,13},{6,2},{7,15},{8,12},{9,1},{1... | collective-permute-start | bytes 884744 | tf_op jit(solution)/shard_map/ppermute | solution.py:440
  156.6 10.2 %collective-permute-start.21 = (bf16[400,768]{1,0:T(8,128)(2,1)S(1)}, bf16[400,768]{1,0:T(8,128)(2,1)S(1)}, u32[]{:S(2)}, u32[]{:S(2)}) collective-permute-start(bf16[400,768]{1,0:T(8,128)(2,1)S(1)} %pad_maximum_fusion), channel_id=1, source_target_pairs={{0,4},{1,9},{2,6},{3,11},{4,0},{5,13},{6,2},{7,15},{8,12},{9,1},{1... | collective-permute-start | bytes 1843208 | tf_op jit(solution)/shard_map/ppermute | solution.py:440
  (3 other events, 6.5 us)

commit v2 on v0

v2 whole, which is shorter than its diff:
```python
import functools

import jax
import jax.numpy as jnp
from jax import lax
from jax.experimental import pallas as pl
from jax.experimental.pallas import tpu as pltpu
from jax.sharding import PartitionSpec as P

HEAD_DIM = 24
LEN = 128
PAIR = 2 * HEAD_DIM
EPSILON = 1e-05
SCALE = HEAD_DIM ** (-0.5)
LOG2E = 1.4426950408889634
F32 = jnp.float32
BF16 = jnp.bfloat16
VMEM_LIMIT = 24 * 1024 * 1024


def dot_nn(a, b):
    return lax.dot_general(a, b, (((1,), (0,)), ((), ())), preferred_element_type=F32)


def dot_nt(a, b):
    return lax.dot_general(a, b, (((1,), (1,)), ((), ())), preferred_element_type=F32)


def dot_tn(a, b):
    return lax.dot_general(a, b, (((0,), (0,)), ((), ())), preferred_element_type=F32)


def normalise(v):
    centered = v - jnp.mean(v, axis=-1, keepdims=True)
    r = lax.rsqrt(jnp.mean(centered * centered, axis=-1, keepdims=True) + EPSILON)
    return centered * r, r


def norm_back(da, gain, xh, r):
    e = da * gain
    return r * (
        e - jnp.mean(e, axis=-1, keepdims=True) - xh * jnp.mean(e * xh, axis=-1, keepdims=True)
    )


def pair_blocks(rows):
    rows = rows.astype(F32)
    none = jnp.zeros((HEAD_DIM, LEN), F32)
    left = jnp.concatenate([rows[:HEAD_DIM], none], axis=0)
    right = jnp.concatenate([none, rows[HEAD_DIM:]], axis=0)
    return jnp.concatenate([left, right], axis=1).astype(BF16)


def pair_window(i, width):
    low = min(PAIR * i // LEN * LEN, width - 2 * LEN)
    return low, PAIR * i - low


def placed(block, before):
    parts = []
    if before:
        parts.append(jnp.zeros((before, 2 * LEN), BF16))
    parts.append(block)
    after = 2 * LEN - PAIR - before
    if after:
        parts.append(jnp.zeros((after, 2 * LEN), BF16))
    return jnp.concatenate(parts, axis=0)


def diagonal(both):
    return jnp.concatenate([both[:HEAD_DIM, :LEN], both[HEAD_DIM:, LEN:]], axis=0)


def call(kernel, name, args, shapes, flops, scalars=0, scratch=()):
    size = lambda a: a.size * a.dtype.itemsize
    return pl.pallas_call(
        kernel,
        in_specs=[
            pl.BlockSpec(memory_space=pltpu.SMEM if j < scalars else pltpu.VMEM)
            for j in range(len(args))
        ],
        out_specs=[pl.BlockSpec(memory_space=pltpu.VMEM) for _ in shapes],
        out_shape=shapes,
        scratch_shapes=list(scratch),
        compiler_params=pltpu.CompilerParams(vmem_limit_bytes=VMEM_LIMIT),
        cost_estimate=pl.CostEstimate(
            flops=flops,
            bytes_accessed=sum(map(size, args)) + sum(map(size, shapes)),
            transcendentals=0,
        ),
        name=name,
    )(*args)


def attention_body(place_ref, nodes_ref, edges_ref, x_ref, gain_ref, bias_ref, w_ref, outs):
    a1_ref, qt_ref, kt_ref, v_ref, p_ref, ot_ref, o_ref = outs
    width = w_ref.shape[1]
    mols = x_ref.shape[0] // LEN
    pairs = width // PAIR
    xh, _ = normalise(x_ref[...].astype(F32))
    a1 = (xh * gain_ref[...] + bias_ref[...]).astype(BF16)
    a1_ref[...] = a1
    qt = dot_nt(w_ref[0], a1).astype(BF16)
    keys = dot_nt(a1, w_ref[1]).astype(BF16)
    vt = dot_nt(w_ref[2], a1).astype(BF16)
    qt_ref[...] = qt
    every = [(m, i) for m in range(mols) for i in range(pairs)]
    lanes = lambda m: slice(LEN * m, LEN * (m + 1))
    rows = lambda i: slice(PAIR * i, PAIR * (i + 1))
    scores, probs = {}, {}
    for m, i in every:
        low, before = pair_window(i, width)
        rhs = placed(pair_blocks(qt[rows(i), lanes(m)]), before)
        scores[m, i] = dot_nn(keys[lanes(m), low : low + 2 * LEN], rhs)
    for m in range(mols):
        mol = place_ref[0] + m
        count = 1 + nodes_ref[mol] + edges_ref[mol]
        valid = lax.broadcasted_iota(jnp.int32, (LEN, 2 * LEN), 0) < count
        for i in range(pairs):
            s = jnp.where(valid, scores[m, i], -1e30)
            e = jnp.exp2((s - jnp.max(s, axis=0, keepdims=True)) * (SCALE * LOG2E))
            p = (e * (1.0 / jnp.sum(e, axis=0, keepdims=True))).astype(BF16)
            p_ref[m, i] = p
            probs[m, i] = p
    for m, i in every:
        both = dot_nn(vt[rows(i), lanes(m)], probs[m, i])
        ot_ref[rows(i), lanes(m)] = diagonal(both).astype(BF16)
    o_ref[...] = ot_ref[...].T
    kt_ref[...] = dot_nt(w_ref[1], a1).astype(BF16)
    v_ref[...] = dot_nt(a1, w_ref[2]).astype(BF16)


def attention(place, nodes, edges, x, gain, bias, w):
    rows, d = x.shape
    width = w.shape[1]
    pairs = width // PAIR
    shape = lambda *s: jax.ShapeDtypeStruct(s, BF16)

    def kernel(*refs):
        attention_body(*refs[:7], refs[7:])

    return call(
        kernel, "attention_forward", (place, nodes, edges, x, gain, bias, w),
        [shape(rows, d), shape(width, rows), shape(width, rows), shape(rows, width),
         shape(rows // LEN, pairs, LEN, 2 * LEN), shape(width, rows), shape(rows, width)],
        rows * width * (10 * d + 8 * LEN), scalars=3,
    )


def feed_body(x, oa, ob, g, wo_ref, gain_ref, bias_ref, fc1_ref, b1_ref, fc2_ref, h_ref, a2_ref, z_ref,
              du_ref):
    h = x.astype(F32) + dot_nn(jnp.concatenate([oa, ob], axis=1), wo_ref[...])
    h_ref[...] = h
    xh, _ = normalise(h)
    a2 = (xh * gain_ref[...] + bias_ref[...]).astype(BF16)
    a2_ref[...] = a2
    u = dot_nt(a2, fc1_ref[: fc2_ref.shape[0]]) + b1_ref[...]
    dz = dot_nt(g, fc2_ref[...])
    phi = 0.5 * (1.0 + lax.erf(u * (0.5**0.5)))
    slope = phi + u * (jnp.exp(-0.5 * u * u) * 0.3989422804014327)
    du_ref[...] = (dz * slope).astype(BF16)
    z_ref[...] = (u * phi).astype(BF16)


def feed(x, oa, got, wo, gain, bias, fc1, b1, fc2):
    rows, d = x.shape
    width = fc2.shape[0]
    got = got if isinstance(got, tuple) else (got,)

    def kernel(x_ref, oa_ref, *refs):
        if len(got) == 2:
            g, ob = refs[0][...], refs[1][...]
        else:
            g, ob = refs[0][:, :d], refs[0][:, d:]
        feed_body(x_ref[...], oa_ref[...], ob, g, *refs[len(got) :])

    shape = jax.ShapeDtypeStruct
    return call(
        kernel, "feed_forward", (x, oa, *got, wo, gain, bias, fc1, b1, fc2),
        [shape((rows, d), F32), shape((rows, d), BF16), shape((rows, width), BF16),
         shape((rows, width), BF16)],
        8 * rows * d * width,
    )


def backward_body(du_ref, dr_ref, fc1_ref, h_ref, g_ref, gain_ref, wo_ref, p_ref, qt_ref, kt_ref, v_ref,
                  gh_ref, dp_ref, dh_ref, sums_ref):
    width, d = kt_ref.shape[0], h_ref.shape[1]
    mols = h_ref.shape[0] // LEN
    pairs = width // PAIR
    du = jnp.concatenate([du_ref[...], dr_ref[...]], axis=1)
    da2 = dot_nn(du, fc1_ref[...])
    xh, r = normalise(h_ref[...])
    dh = g_ref[:, :d].astype(F32) + norm_back(da2, gain_ref[...], xh, r)
    if dh_ref is not None:
        dh_ref[...] = dh
        sums_ref[0:1] = jnp.sum(da2 * xh, axis=0, keepdims=True)
        sums_ref[1:2] = jnp.sum(da2, axis=0, keepdims=True)
    gh = dh.astype(BF16)
    gh_ref[...] = gh
    dot = dot_nt(wo_ref[:width], gh).astype(BF16)
    every = [(m, i) for m in range(mols) for i in range(pairs)]
    lanes = lambda m: slice(LEN * m, LEN * (m + 1))
    rows = lambda i: slice(PAIR * i, PAIR * (i + 1))
    dps, dss, dos = {}, {}, {}
    for m, i in every:
        low, before = pair_window(i, width)
        dos[m, i] = pair_blocks(dot[rows(i), lanes(m)])
        dps[m, i] = dot_nn(v_ref[lanes(m), low : low + 2 * LEN], placed(dos[m, i], before))
    for m, i in every:
        dp_ref[pl.ds(2 * width + PAIR * i, PAIR), lanes(m)] = dot_nt(dos[m, i], p_ref[m, i]).astype(BF16)
    for m, i in every:
        p = p_ref[m, i].astype(F32)
        t = dps[m, i] * p
        dss[m, i] = (t - p * jnp.sum(t, axis=0, keepdims=True)).astype(BF16)
    for m, i in every:
        dq = diagonal(dot_nn(kt_ref[rows(i), lanes(m)], dss[m, i])) * SCALE
        dp_ref[rows(i), lanes(m)] = dq.astype(BF16)
        dk = dot_nt(pair_blocks(qt_ref[rows(i), lanes(m)]), dss[m, i]) * SCALE
        dp_ref[pl.ds(width + PAIR * i, PAIR), lanes(m)] = dk.astype(BF16)


def pack_qkv_kernel(own_ref, got_ref, out_ref):
    shard = own_ref.shape[1]
    out_ref[:, :shard] = own_ref[...]
    out_ref[:, shard:] = got_ref[...]


def pack_qkv(own, got):
    c, shard, d = own.shape
    return call(
        pack_qkv_kernel, "pack_qkv", (own, got), [jax.ShapeDtypeStruct((c, 2 * shard, d), BF16)], 0
    )[0]


def pack_rest_kernel(bit_ref, wo0, wo1, fc10, fc11, fc20, fc21, y0, y1, x0, x1,
                     wo_ref, fc1_ref, fc2_ref):
    shard = wo0.shape[0]
    for at, (a, b, c) in enumerate(((wo0, fc10, fc20), (wo1, fc11, fc21))):
        rows = slice(at * shard, (at + 1) * shard)
        wo_ref[rows] = a[...]
        fc1_ref[rows] = b[...]
        fc2_ref[rows] = c[...]

    def far(a, b):
        for at, (u, v) in enumerate(zip(a, b)):
            rows = slice((2 + at) * shard, (3 + at) * shard)
            wo_ref[rows] = u[...]
            fc1_ref[rows] = v[...]

    @pl.when(bit_ref[0] == 0)
    def _():
        far((y0, y1), (x0, x1))

    @pl.when(bit_ref[0] != 0)
    def _():
        far((x0, x1), (y0, y1))


def pack_rest(bit, *parts):
    shard, d = parts[0].shape
    shape = lambda rows: jax.ShapeDtypeStruct((rows, d), BF16)
    return call(
        pack_rest_kernel, "pack_rest", (bit, *parts),
        [shape(4 * shard), shape(4 * shard), shape(2 * shard)], 0, scalars=1,
    )


def feed_grads_kernel(z0, z1, du0, du1, a0, a1, g0, g1, fc2_ref, h_ref,
                      keep_ref, send_ref, sums_ref, mine_ref, theirs_ref):
    shard = fc2_ref.shape[0] // 2
    d = h_ref.shape[1]
    first = dot_tn(du0[...], a0[...]) + dot_tn(du1[...], a1[...])
    second = dot_tn(z0[...], g0[...]) + dot_tn(z1[...], g1[:, :d])
    for at, ref in enumerate((keep_ref, send_ref)):
        rows = slice(at * shard, (at + 1) * shard)
        ref[0] = first[rows].astype(BF16)
        ref[1] = second[rows].astype(BF16)
    sums_ref[...] = jnp.sum(du0[...].astype(F32), axis=0, keepdims=True) + jnp.sum(
        du1[...].astype(F32), axis=0, keepdims=True
    )
    mine_ref[...] = h_ref[...] + dot_nn(z0[...], fc2_ref[...])
    theirs_ref[...] = dot_nn(z1[...], fc2_ref[...]).astype(BF16)


def feed_grads(zs, dus, a2s, gs, fc2, h):
    rows, d = h.shape
    width = fc2.shape[0]
    shape = jax.ShapeDtypeStruct
    return call(
        feed_grads_kernel, "feed_grads", (*zs, *dus, *a2s, *gs, fc2, h),
        [shape((2, width // 2, d), BF16), shape((2, width // 2, d), BF16), shape((1, width), F32),
         shape((rows, d), F32), shape((rows, d), BF16)],
        12 * rows * d * width,
    )


def out_grads_kernel(ot0, ot1, gh0, gh1, keep_ref, send_ref):
    shard = ot0.shape[0] // 2
    total = dot_nn(ot0[...], gh0[...]) + dot_nn(ot1[...], gh1[...])
    keep_ref[0] = total[:shard].astype(BF16)
    send_ref[0] = total[shard:].astype(BF16)


def out_grads(ots, ghs):
    width, d = ots[0].shape[0], ghs[0].shape[1]
    shape = jax.ShapeDtypeStruct((1, width // 2, d), BF16)
    return call(
        out_grads_kernel, "out_grads", (*ots, *ghs), [shape, shape], 4 * width * d * ghs[0].shape[0]
    )


def qkv_grads_kernel(dp0, dp1, a0, a1, keep_ref, send_ref):
    shard = keep_ref.shape[1]
    a = jnp.concatenate([a0[...], a1[...]], axis=0)
    for c in range(3):
        for at, ref in enumerate((keep_ref, send_ref)):
            rows = slice((2 * c + at) * shard, (2 * c + at + 1) * shard)
            dp = jnp.concatenate([dp0[rows], dp1[rows]], axis=1)
            ref[c] = dot_nn(dp, a).astype(BF16)


def qkv_grads(dps, a1s):
    width, d = dps[0].shape[0] // 3, a1s[0].shape[1]
    shape = jax.ShapeDtypeStruct((3, width // 2, d), BF16)
    return call(
        qkv_grads_kernel, "qkv_grads", (*dps, *a1s), [shape, shape], 12 * width * d * a1s[0].shape[0]
    )


def backward(du, dr, fc1, h, g, gain, wo, p, qt, kt, v, own):
    rows, d = h.shape
    width = kt.shape[0]
    shape = jax.ShapeDtypeStruct
    shapes = [shape((rows, d), BF16), shape((3 * width, rows), BF16)]
    if own:
        shapes += [shape((rows, d), F32), shape((8, d), F32)]

    def kernel(*refs):
        backward_body(*refs[:11], *refs[11:], *(() if own else (None, None)))

    return call(
        kernel, "attention_backward", (du, dr, fc1, h, g, gain, wo, p, qt, kt, v), shapes,
        rows * width * (6 * d + 16 * LEN),
    )


def input_grads_kernel(dp0, dp1, w_ref, mine_ref, theirs_ref):
    w = w_ref[...].reshape(dp0.shape[0], w_ref.shape[2])
    theirs_ref[...] = dot_tn(dp1[...], w).astype(BF16)
    mine_ref[...] = dot_tn(dp0[...], w)


def input_grads(dps, w):
    rows, d = dps[0].shape[1], w.shape[2]
    shape = jax.ShapeDtypeStruct
    return call(
        input_grads_kernel, "input_grads", (*dps, w), [shape((rows, d), F32), shape((rows, d), BF16)],
        4 * dps[0].size * d,
    )


def input_norm_kernel(x_ref, gain_ref, mine_ref, got_ref, dh_ref, sums_ref, bias_ref, out_ref, vec_ref):
    xh, r = normalise(x_ref[...].astype(F32))
    da1 = mine_ref[...] + got_ref[...].astype(F32)
    out_ref[...] = (dh_ref[...] + norm_back(da1, gain_ref[...], xh, r)).astype(BF16)
    d = x_ref.shape[1]
    bias = bias_ref[...]
    rows = [
        jnp.sum(da1 * xh, axis=0, keepdims=True),
        jnp.sum(da1, axis=0, keepdims=True),
        sums_ref[0:2],
        jnp.concatenate([bias, jnp.zeros((1, d - bias.shape[1]), F32)], axis=1),
        jnp.zeros((11, d), F32),
    ]
    vec_ref[...] = jnp.concatenate(rows, axis=0).astype(BF16)


def input_norm(x, gain, mine, got, dh, sums, bias):
    rows, d = x.shape
    return call(
        input_norm_kernel, "input_norm", (x, gain, mine, got, dh, sums, bias),
        [jax.ShapeDtypeStruct((rows, d), BF16), jax.ShapeDtypeStruct((16, d), BF16)], rows * d * 20,
    )


def plus(a, b):
    return (a.astype(F32) + b.astype(F32)).astype(BF16)


def halve_kernel(bits_ref, mine_ref, got_ref, keep_ref, send_ref):
    at = bits_ref[0]
    keep_ref[...] = plus(mine_ref[at], got_ref[at])
    send_ref[...] = plus(mine_ref[1 - at], got_ref[1 - at])


def halve(bit, mine, got):
    shape = jax.ShapeDtypeStruct(mine.shape[1:], BF16)
    return call(halve_kernel, "sum_halves", (bit, mine, got), [shape, shape], mine.size, scalars=1)


def sum_kernel(a_ref, b_ref, out_ref):
    out_ref[...] = plus(a_ref[...], b_ref[...])


def sum_two(a, b):
    return call(sum_kernel, "sum_two", (a, b), [jax.ShapeDtypeStruct(a.shape, BF16)], a.size)[0]


def join_kernel(bits_ref, mine_ref, got_ref, out_ref):
    at = bits_ref[0]
    out_ref[at] = mine_ref[...].astype(out_ref.dtype)
    out_ref[1 - at] = got_ref[...].astype(out_ref.dtype)


def join(bit, mine, got, dtype):
    shape = jax.ShapeDtypeStruct((2, *mine.shape), dtype)
    return call(join_kernel, "join_halves", (bit, mine, got), [shape], mine.size, scalars=1)[0]


def local(
    n_dp, n_tensor, tokens, node_counts, edge_counts, ln1_gain, ln1_bias, qkv_weight, out_weight,
    ln2_gain, ln2_bias, fc1_weight, fc1_bias, fc2_weight, out_grad,
):
    d = tokens.shape[1]
    shard = out_weight.shape[0]
    mols = tokens.shape[0] // LEN
    dp_at = lax.axis_index("dp")
    tensor_at = lax.axis_index("tensor")
    core = tensor_at % 2
    bit0 = dp_at % 2
    bit1 = (dp_at // 2 + dp_at // 4) % 2
    scalar = lambda v: v.reshape(1).astype(jnp.int32)
    first = scalar(jnp.where(core == 0, bit0, bit1))
    second = scalar(jnp.where(core == 0, bit1, bit0))

    def swap_core(a):
        return lax.ppermute(a, "tensor", [(t, t ^ 1) for t in range(n_tensor)])

    def swap_y(a):
        return lax.ppermute(a, "tensor", [(t, t ^ 2) for t in range(n_tensor)])

    def swap_dp(a, mask0, mask1):
        pairs = [
            (p * n_tensor + t, (p ^ (mask1 if t % 2 else mask0)) * n_tensor + t)
            for p in range(n_dp)
            for t in range(n_tensor)
        ]
        return lax.ppermute(a, ("dp", "tensor"), pairs)

    row = lambda v: v.reshape(1, -1).astype(F32)
    g1, b1, g2, b2 = row(ln1_gain), row(ln1_bias), row(ln2_gain), row(ln2_bias)

    x_got = swap_y(tokens)
    w_qkv = pack_qkv(qkv_weight, swap_core(qkv_weight))
    far_y = swap_y(jnp.where(bit0 == 0, out_weight, fc1_weight))
    far_x = swap_dp(far_y, 1, 1)
    bias = jnp.concatenate([fc1_bias, swap_core(fc1_bias)])

    place = lambda t: scalar(t * mols)
    fwd = lambda t, x: attention(place(t), node_counts, edge_counts, x, g1, b1, w_qkv)
    a1_0, qt_0, kt_0, v_0, p_0, ot_0, o_0 = fwd(tensor_at, tokens)
    packet = swap_y(jnp.concatenate([out_grad, o_0], axis=1))
    a1_1, qt_1, kt_1, v_1, p_1, ot_1, o_1 = fwd(tensor_at ^ 2, x_got)
    o_got = swap_y(o_1)
    wo, fc1, fc2 = pack_rest(
        scalar(bit0), out_weight, swap_core(out_weight), fc1_weight, swap_core(fc1_weight),
        fc2_weight, swap_core(fc2_weight), far_y, swap_core(far_y), far_x, swap_core(far_x),
    )

    h_1, a2_1, z_1, du_1 = feed(x_got, o_1, packet, wo, g2, b2, fc1, row(bias), fc2)
    dr_0 = swap_y(du_1)
    h_0, a2_0, z_0, du_0 = feed(tokens, o_0, (out_grad, o_got), wo, g2, b2, fc1, row(bias), fc2)
    dr_1 = swap_y(du_0)
    keep_fc, send_fc, bias_sums, res_mine, res_theirs = feed_grads(
        (z_0, z_1), (du_0, du_1), (a2_0, a2_1), (out_grad, packet), fc2, h_0
    )
    result = (res_mine + swap_y(res_theirs).astype(F32)).astype(BF16)

    gh_0, dp_0, dh, sums = backward(
        du_0, dr_0, fc1, h_0, out_grad, g2, wo, p_0, qt_0, kt_0, v_0, True
    )
    gh_1, dp_1 = backward(du_1, dr_1, fc1, h_1, packet, g2, wo, p_1, qt_1, kt_1, v_1, False)
    keep_out, send_out = out_grads((ot_0, ot_1), (gh_0, gh_1))
    keep_qkv, send_qkv = qkv_grads((dp_0, dp_1), (a1_0, a1_1))
    da1_mine, da1_theirs = input_grads((dp_0, dp_1), w_qkv)
    grad_tokens, vec = input_norm(tokens, g1, da1_mine, swap_y(da1_theirs), dh, sums, bias_sums)
    vec_got = swap_y(vec)
    same = lax.broadcasted_iota(jnp.int32, vec.shape, 0) < 4
    vec = jnp.where(same, plus(vec, vec_got), vec)
    vec_got = swap_core(vec)
    turned = jnp.concatenate(
        [vec_got[:, shard : 2 * shard], vec_got[:, :shard], vec_got[:, 2 * shard :]], axis=1
    )
    vec = plus(vec, jnp.where(same, vec_got, turned))

    def sum_dp(mine, got, extra=None):
        rows = mine.shape[0] * mine.shape[1]
        size = rows // 4
        view = lambda a: a.reshape(2, rows // 2, d)
        keep, send = halve(first, view(mine), view(got))
        split = lambda a: a.reshape(2, size, d)
        keep, send = halve(second, split(keep), split(swap_dp(send, 1, 2)))
        s = sum_two(keep, swap_dp(send, 2, 1))
        if extra is not None:
            s = jnp.concatenate([s, extra], axis=0)
        for k in range(2, n_dp.bit_length() - 1):
            mask = 6 if k == 2 else 1 << k
            s = sum_two(s, swap_dp(s, mask, mask))
        got = swap_dp(s, 2, 1)
        if extra is not None:
            extra = plus(s[size:], got[size:])
            s, got = s[:size], got[:size]
        s = join(second, s, got, BF16).reshape(2 * size, d)
        if extra is None:
            got = swap_dp(s, 1, 2)
        else:
            got = swap_dp(jnp.concatenate([s, extra], axis=0), 1, 2)
            extra = plus(extra, got[2 * size :])
            got = got[: 2 * size]
        return join(first, s, got, F32).reshape(mine.shape), extra

    keep_rest = jnp.concatenate([keep_fc, keep_out], axis=0)
    rest, _ = sum_dp(keep_rest, swap_core(jnp.concatenate([send_fc, send_out], axis=0)))
    qkv, vec = sum_dp(keep_qkv, swap_core(send_qkv), vec)
    vec = vec.astype(F32)
    return (
        result, grad_tokens, vec[0], vec[1], qkv, rest[2], vec[2], vec[3], rest[0], vec[4, :shard],
        rest[1],
    )


def solution(mesh):
    tokens = P(("dp", "tensor"), None)
    rows = P("tensor", None)
    qkv = P(None, "tensor", None)
    in_specs = (
        tokens, P("dp"), P("dp"), P(), P(), qkv, rows, P(), P(), rows, P("tensor"), rows, tokens,
    )
    out_specs = (tokens, tokens, P(), P(), qkv, rows, P(), P(), rows, P("tensor"), rows)
    step = functools.partial(local, mesh.shape["dp"], mesh.shape["tensor"])
    return jax.shard_map(step, mesh=mesh, in_specs=in_specs, out_specs=out_specs, check_vma=False)
```

time: 421 us -> 153 us (0.36)
  waiting for transfers between devices: 258 us -> 69.5 us
  blocking collectives: 63.6 us -> 0 us
  matrix products: 37.8 us -> 0 us
  starting transfers between devices: 0.55 us -> 34.2 us
  Pallas kernels: 0 us -> 27.8 us
  other arithmetic: 22.7 us -> 4.15 us
  between operations: 14.4 us -> 1.11 us
  local copies, waits for them, and re-layouts: 22.7 us -> 15.3 us
    psum x1 -> x0, waiting for transfers between devices: 98 us -> none  [local(): lax.psum((grad_qkv, grad_out, grad_fc1, grad_fc1_bias, grad_fc2), 'dp')]
    reduce_scatter x4 -> x0, waiting for transfers between devices: 80.6 us -> none  [the longest x1 28.3 us: local(): lax.psum_scatter(jnp.dot(row_piece, out_weight, preferred_element_type=jn...]
    all_gather x4 -> x0, waiting for transfers between devices: 78.8 us -> none  [the longest x1 22.4 us: local(): gathered_one = lax.all_gather(normed_one, 'tensor', axis=0, tiled=True)]
    ppermute x0 -> x30, waiting for transfers between devices: none -> 69.5 us  [the longest x11 38.5 us: swap_dp(): return lax.ppermute(a, ('dp', 'tensor'), pairs)]
    psum x2 -> x0, blocking collectives: 63.6 us -> none  [the longest x1 42 us: local(): lax.psum((grad_gain_one, grad_shift_one, grad_gain_two, grad_shift_two),...]
    dot_general x18 -> x0, matrix products: 37.8 us -> none  [the longest x3 9.3 us: contract_cols(): lax.dot_general(left_side, right_side, (((1,), (1,)), ((), ())), preferre...]
    ppermute x0 -> x30, starting transfers between devices: none -> 34.2 us  [the longest x11 20.5 us: swap_dp(): return lax.ppermute(a, ('dp', 'tensor'), pairs)]
    pallas_call x0 -> x25, Pallas kernels: none -> 27.8 us  [call(): pl.pallas_call(kernel, in_specs=[pl.BlockSpec(memory_space=pltpu.SMEM if...]
  transfers between devices with their start and end apart: 9 -> 30, of which waited for: 8 -> 13; matrix products, arithmetic and copies ran while one was open for 5% -> 4% of each run, Pallas kernels for 0% -> 16%
where the time goes in v2:
time: 153 us; the launch traced here: 152 us
  waiting for transfers between devices  69.5 us (45%)
  starting transfers between devices  34.2 us (22%)
  Pallas kernels  27.8 us (18%)
  local copies, waits for them, and re-layouts  15.3 us (10%)
  other arithmetic  4.15 us (3%)
    ppermute x11, waiting for transfers between devices, swap_dp(): return lax.ppermute(a, ('dp', 'tensor'), pairs)  38.5 us
    ppermute x9, waiting for transfers between devices, swap_y(): return lax.ppermute(a, 'tensor', [(t, t ^ 2) for t in range(n_tensor)])  29.8 us
    pallas_call x25, Pallas kernels, call(): pl.pallas_call(kernel, in_specs=[pl.BlockSpec(memory_space=pltpu.SMEM if...  27.8 us
    ppermute x11, starting transfers between devices, swap_dp(): return lax.ppermute(a, ('dp', 'tensor'), pairs)  20.5 us
    ppermute x9, starting transfers between devices, swap_y(): return lax.ppermute(a, 'tensor', [(t, t ^ 2) for t in range(n_tensor)])  11.5 us
    unnamed x72, local copies, waits for them, and re-layouts  11.3 us
  transfers between devices with their start and end apart: 30, of which 13 were waited for; matrix products, arithmetic and copies ran while one was open for 4% of the time, Pallas kernels for 16%

profile of v2, /device:TPU:0, one launch (start us, length us, event | category | flops | bytes accessed | tf_op | source)
XLA Modules:
  0.0 152.1 jit_solution(8475646162941260537)
XLA Ops:
  1.2 1.0 broadcast_select_fusion
  2.2 2.7 %collective-permute-start.6 = (bf16[192,768]{1,0:T(8,128)(2,1)S(1)}, bf16[192,768]{1,0:T(8,128)(2,1)}, u32[]{:S(2)}, u32[]{:S(2)}) collective-permute-start(bf16[192,768]{1,0:T(8,128)(2,1)S(1)} %broadcast_select_fusion), channel_id=1, source_target_pairs={{0,2},{1,3},{2,0},{3,1},{4,6},{5,7},{6,4},{7,5},{8,10},{9,11},{10,... | collective-permute-start | bytes 884744 | tf_op jit(solution)/shard_map/ppermute | solution.py:441
  6.8 6.0 %collective-permute-done.6.y0 = bf16[192,768]{1,0:T(8,128)(2,1)} collective-permute-done((bf16[192,768]{1,0:T(8,128)(2,1)S(1)}, bf16[192,768]{1,0:T(8,128)(2,1)}, u32[]{:S(2)}, u32[]{:S(2)}) %collective-permute-start.6) | collective-permute-done | bytes 294944 | tf_op jit(solution)/shard_map/ppermute | solution.py:441
  13.7 1.9 %collective-permute-start.8 = (bf16[192,768]{1,0:T(8,128)(2,1)}, bf16[192,768]{1,0:T(8,128)(2,1)}, u32[]{:S(2)}, u32[]{:S(2)}) collective-permute-start(bf16[192,768]{1,0:T(8,128)(2,1)} %collective-permute-done.6.y0), channel_id=1, source_target_pairs={{0,4},{1,5},{2,6},{3,7},{4,0},{5,1},{6,2},{7,3},{8,12},{9,13},{10,... | collective-permute-start | bytes 884744 | tf_op jit(solution)/shard_map/ppermute | solution.py:449
  15.7 1.2 copy-done.8
  17.0 2.7 %attention_forward.2 = (bf16[256,768]{1,0:T(8,128)(2,1)S(1)}, bf16[384,256]{1,0:T(8,128)(2,1)S(1)}, bf16[384,256]{1,0:T(8,128)(2,1)S(1)}, bf16[256,384]{1,0:T(8,...) custom-call(s32[1]{0:T(128)} %bitcast.refs_0_, ...), custom_call_target="tpu_custom_call" | custom-call | flops 855638016 | bytes 4593732 | tf_op jit(solution)/shard_map/attention_forward/pallas_call | solution.py:76
  22.5 0.9 pad_maximum_fusion.2
  24.1 1.5 collective-permute-start.11
  26.3 3.2 %attention_forward.3 = (bf16[256,768]{1,0:T(8,128)(2,1)S(1)}, bf16[384,256]{1,0:T(8,128)(2,1)S(1)}, bf16[384,256]{1,0:T(8,128)(2,1)S(1)}, bf16[256,384]{1,0:T(8,...) custom-call(s32[1]{0:T(128)} %bitcast.1.refs_0_, ...), custom_call_target="tpu_custom_call" | custom-call | flops 855638016 | bytes 4593732 | tf_op jit(solution)/shard_map/attention_forward/pallas_call | solution.py:76
  30.2 2.0 %pack_rest.1 = (bf16[768,768]{1,0:T(8,128)(2,1)S(1)}, bf16[768,768]{1,0:T(8,128)(2,1)S(1)}, bf16[384,768]{1,0:T(8,128)(2,1)S(1)}) custom-call(s32[1]{0:T(128)} %bitcast.2.bit_ref, bf16[192,768]{1,0:T(8,128)(2,1)S(1)} %copy-done.2, bf16[192,768]{1,0:T(8,128)(2,1)} %collective-permute-done.3.wo1, bf16[192,768]{1,0:T(8,128)(2,1)S(1)} %copy-done.3, ...), custom_call_target="tpu_custom_call" | custom-call | bytes 5898244 | tf_op jit(solution)/shard_map/pack_rest/pallas_call | solution.py:76
  32.2 11.8 %collective-permute-done.2.refs_1_ = bf16[256,384]{1,0:T(8,128)(2,1)S(1)} collective-permute-done((bf16[256,384]{1,0:T(8,128)(2,1)S(1)}, bf16[256,384]{1,0:T(8,128)(2,1)S(1)}, u32[]{:S(2)}, u32[]{:S(2)}) %collective-permute-start.2) | collective-permute-done | bytes 196640 | tf_op jit(solution)/shard_map/ppermute | solution.py:441
  44.0 1.2 feed_forward.2
  45.3 1.6 %collective-permute-start.14 = (bf16[256,384]{1,0:T(8,128)(2,1)S(1)}, bf16[256,384]{1,0:T(8,128)(2,1)S(1)}, u32[]{:S(2)}, u32[]{:S(2)}) collective-permute-start(bf16[256,384]{1,0:T(8,128)(2,1)S(1)} %get-tuple-element.70.du0.refs_0_), channel_id=1, source_target_pairs={{0,2},{1,3},{2,0},{3,1},{4,6},{5,7},{6,4},{7,5},{8,10},{9,11},{10,... | collective-permute-start | bytes 589832 | tf_op jit(solution)/shard_map/ppermute | solution.py:441
  46.9 2.2 %feed_forward.3 = (f32[256,768]{1,0:T(8,128)S(1)}, bf16[256,768]{1,0:T(8,128)(2,1)S(1)}, bf16[256,384]{1,0:T(8,128)(2,1)S(1)}, bf16[256,384]{1,0:T(8,128)(2,1)S(1)}) custom-call(bf16[256,768]{1,0:T(8,128)(2,1)} %collective-permute-done.1.refs_3_.x_ref, bf16[256,384]{1,0:T(8,128)(2,1)S(1)} %get-tuple-element.64.oa_ref, ...), custom_call_target="tpu_custom_call" | custom-call | flops 603979776 | bytes 5709312 | tf_op jit(solution)/shard_map/feed_forward/pallas_call | solution.py:76
  49.7 2.6 %collective-permute-done.14.refs_1_ = bf16[256,384]{1,0:T(8,128)(2,1)S(1)} collective-permute-done((bf16[256,384]{1,0:T(8,128)(2,1)S(1)}, bf16[256,384]{1,0:T(8,128)(2,1)S(1)}, u32[]{:S(2)}, u32[]{:S(2)}) %collective-permute-start.14) | collective-permute-done | bytes 196640 | tf_op jit(solution)/shard_map/ppermute | solution.py:441
  52.2 2.4 %attention_backward.3 = (bf16[256,768]{1,0:T(8,128)(2,1)S(1)}, bf16[1152,256]{1,0:T(8,128)(2,1)S(1)}) custom-call(bf16[256,384]{1,0:T(8,128)(2,1)S(1)} %get-tuple-element.71.du1.refs_0_, bf16[256,384]{1,0:T(8,128)(2,1)S(1)} %collective-permute-done.14.refs_1_, bf16[768,768]{1,0:T(8,128)(2,1)S(1)} %get-tuple-element.66.refs_5_.refs_4_.refs_2_, ...), custom_call_target="tpu_custom_call" | custom-call | flops 654311424 | bytes 6753280 | tf_op jit(solution)/shard_map/attention_backward/pallas_call | solution.py:76
  54.7 1.3 feed_grads.1
  58.4 2.4 %attention_backward.2 = (bf16[256,768]{1,0:T(8,128)(2,1)S(1)}, bf16[1152,256]{1,0:T(8,128)(2,1)S(1)}, f32[256,768]{1,0:T(8,128)S(1)}, f32[8,768]{1,0:T(8,128)S(1)}) custom-call(bf16[256,384]{1,0:T(8,128)(2,1)S(1)} %get-tuple-element.70.du0.refs_0_, bf16[256,384]{1,0:T(8,128)(2,1)S(1)} %collective-permute-done.13.refs_1_, ...), custom_call_target="tpu_custom_call" | custom-call | flops 654311424 | bytes 7367680 | tf_op jit(solution)/shard_map/attention_backward/pallas_call | solution.py:76
  61.3 1.0 pad_maximum_fusion.1
  62.4 2.0 %qkv_grads.1 = (bf16[3,192,768]{2,1,0:T(8,128)(2,1)S(1)}, bf16[3,192,768]{2,1,0:T(8,128)(2,1)}) custom-call(bf16[1152,256]{1,0:T(8,128)(2,1)S(1)} %get-tuple-element.81.dp0, bf16[1152,256]{1,0:T(8,128)(2,1)S(1)} %get-tuple-element.87.dp1, bf16[256,768]{1,0:T(8,128)(2,1)S(1)} %copy-done.30, bf16[256,768]{1,0:T(8,128)(2,1)S(1)} %get-tuple-element.95.a1), custom_call_target="tpu_custom_call" | custom-call | flops 905969664 | bytes 3735552 | tf_op jit(solution)/shard_map/qkv_grads/pallas_call | solution.py:76
  64.9 1.7 %input_grads.1 = (f32[256,768]{1,0:T(8,128)S(1)}, bf16[256,768]{1,0:T(8,128)(2,1)}) custom-call(bf16[1152,256]{1,0:T(8,128)(2,1)S(1)} %get-tuple-element.81.dp0, bf16[1152,256]{1,0:T(8,128)(2,1)S(1)} %get-tuple-element.87.dp1, bf16[3,384,768]{2,1,0:T(8,128)(2,1)S(1)} %pack_qkv.1.refs_6_.w_ref), custom_call_target="tpu_custom_call" | custom-call | flops 905969664 | bytes 4128768 | tf_op jit(solution)/shard_map/input_grads/pallas_call | solution.py:76
  66.6 0.9 copy-done.13
  67.5 2.5 %collective-permute-start.15 = (bf16[256,768]{1,0:T(8,128)(2,1)}, bf16[256,768]{1,0:T(8,128)(2,1)S(1)}, u32[]{:S(2)}, u32[]{:S(2)}) collective-permute-start(bf16[256,768]{1,0:T(8,128)(2,1)} %get-tuple-element.89), channel_id=1, source_target_pairs={{0,2},{1,3},{2,0},{3,1},{4,6},{5,7},{6,4},{7,5},{8,10},{9,11},{10,... | collective-permute-start | bytes 1179656 | tf_op jit(solution)/shard_map/ppermute | solution.py:441
  70.0 9.5 %collective-permute-done.15.got_ref = bf16[256,768]{1,0:T(8,128)(2,1)S(1)} collective-permute-done((bf16[256,768]{1,0:T(8,128)(2,1)}, bf16[256,768]{1,0:T(8,128)(2,1)S(1)}, u32[]{:S(2)}, u32[]{:S(2)}) %collective-permute-start.15) | collective-permute-done | bytes 393248 | tf_op jit(solution)/shard_map/ppermute | solution.py:441
  79.5 1.1 copy-done.12
  80.7 1.1 copy-done.14
  81.8 1.4 input_norm.1
  83.2 1.7 %collective-permute-start.19 = (bf16[16,768]{1,0:T(8,128)(2,1)S(1)}, bf16[16,768]{1,0:T(8,128)(2,1)S(1)}, u32[]{:S(2)}, u32[]{:S(2)}) collective-permute-start(bf16[16,768]{1,0:T(8,128)(2,1)S(1)} %get-tuple-element.102), channel_id=1, source_target_pairs={{0,2},{1,3},{2,0},{3,1},{4,6},{5,7},{6,4},{7,5},{8,10},{9,11},{10,... | collective-permute-start | bytes 73736 | tf_op jit(solution)/shard_map/ppermute | solution.py:441
  85.1 1.4 sum_halves.6
  87.0 1.4 sum_halves.4
  88.4 1.6 %collective-permute-start.17 = (bf16[288,768]{1,0:T(8,128)(2,1)S(1)}, bf16[288,768]{1,0:T(8,128)(2,1)S(1)}, u32[]{:S(2)}, u32[]{:S(2)}) collective-permute-start(bf16[288,768]{1,0:T(8,128)(2,1)S(1)} %get-tuple-element.99), channel_id=1, source_target_pairs={{0,4},{1,9},{2,6},{3,11},{4,0},{5,13},{6,2},{7,15},{8,12},{9,1},{1... | collective-permute-start | bytes 1327112 | tf_op jit(solution)/shard_map/ppermute | solution.py:449
  90.1 1.2 collective-permute-done.20
  91.3 3.5 %collective-permute-done.25 = bf16[288,768]{1,0:T(8,128)(2,1)S(1)} collective-permute-done((bf16[288,768]{1,0:T(8,128)(2,1)S(1)}, bf16[288,768]{1,0:T(8,128)(2,1)S(1)}, u32[]{:S(2)}, u32[]{:S(2)}) %collective-permute-start.25) | collective-permute-done | bytes 442400 | tf_op jit(solution)/shard_map/ppermute | solution.py:449
  94.9 1.6 %collective-permute-start.26 = (bf16[144,768]{1,0:T(8,128)(2,1)S(1)}, bf16[144,768]{1,0:T(8,128)(2,1)S(1)}, u32[]{:S(2)}, u32[]{:S(2)}) collective-permute-start(bf16[144,768]{1,0:T(8,128)(2,1)S(1)} %get-tuple-element.114), channel_id=1, source_target_pairs={{0,8},{1,5},{2,10},{3,7},{4,12},{5,1},{6,14},{7,3},{8,0},{9,13},{1... | collective-permute-start | bytes 663560 | tf_op jit(solution)/shard_map/ppermute | solution.py:449
  96.5 6.9 %collective-permute-done.17 = bf16[288,768]{1,0:T(8,128)(2,1)S(1)} collective-permute-done((bf16[288,768]{1,0:T(8,128)(2,1)S(1)}, bf16[288,768]{1,0:T(8,128)(2,1)S(1)}, u32[]{:S(2)}, u32[]{:S(2)}) %collective-permute-start.17) | collective-permute-done | bytes 442400 | tf_op jit(solution)/shard_map/ppermute | solution.py:449
  103.5 1.6 %collective-permute-start.18 = (bf16[144,768]{1,0:T(8,128)(2,1)S(1)}, bf16[144,768]{1,0:T(8,128)(2,1)S(1)}, u32[]{:S(2)}, u32[]{:S(2)}) collective-permute-start(bf16[144,768]{1,0:T(8,128)(2,1)S(1)} %get-tuple-element.101), channel_id=1, source_target_pairs={{0,8},{1,5},{2,10},{3,7},{4,12},{5,1},{6,14},{7,3},{8,0},{9,13},{1... | collective-permute-start | bytes 663560 | tf_op jit(solution)/shard_map/ppermute | solution.py:449
  105.2 5.5 %collective-permute-done.18.b_ref = bf16[144,768]{1,0:T(8,128)(2,1)S(1)} collective-permute-done((bf16[144,768]{1,0:T(8,128)(2,1)S(1)}, bf16[144,768]{1,0:T(8,128)(2,1)S(1)}, u32[]{:S(2)}, u32[]{:S(2)}) %collective-permute-start.18) | collective-permute-done | bytes 221216 | tf_op jit(solution)/shard_map/ppermute | solution.py:449
  110.8 7.5 %collective-permute-start.21 = (bf16[160,768]{1,0:T(8,128)(2,1)S(1)}, bf16[160,768]{1,0:T(8,128)(2,1)S(1)}, u32[]{:S(2)}, u32[]{:S(2)}) collective-permute-start(bf16[160,768]{1,0:T(8,128)(2,1)S(1)} %pad_maximum_fusion.4.a_ref), channel_id=1, source_target_pairs={{0,24},{1,25},{2,26},{3,27},{4,28},{5,29},{6,30},{7,31},{8,16},{9,... | collective-permute-start | bytes 737288 | tf_op jit(solution)/shard_map/ppermute | solution.py:449
  118.4 4.1 %collective-permute-done.21.b_ref = bf16[160,768]{1,0:T(8,128)(2,1)S(1)} collective-permute-done((bf16[160,768]{1,0:T(8,128)(2,1)S(1)}, bf16[160,768]{1,0:T(8,128)(2,1)S(1)}, u32[]{:S(2)}, u32[]{:S(2)}) %collective-permute-start.21) | collective-permute-done | bytes 245792 | tf_op jit(solution)/shard_map/ppermute | solution.py:449
  122.6 1.2 collective-permute-start.22
  123.8 2.4 %collective-permute-done.27.b_ref = bf16[144,768]{1,0:T(8,128)(2,1)S(1)} collective-permute-done((bf16[144,768]{1,0:T(8,128)(2,1)S(1)}, bf16[144,768]{1,0:T(8,128)(2,1)S(1)}, u32[]{:S(2)}, u32[]{:S(2)}) %collective-permute-start.27) | collective-permute-done | bytes 221216 | tf_op jit(solution)/shard_map/ppermute | solution.py:449
  126.3 2.3 %collective-permute-start.28 = (bf16[144,768]{1,0:T(8,128)(2,1)S(1)}, bf16[144,768]{1,0:T(8,128)(2,1)S(1)}, u32[]{:S(2)}, u32[]{:S(2)}) collective-permute-start(bf16[144,768]{1,0:T(8,128)(2,1)S(1)} %sum_two.7.mine_ref), channel_id=1, source_target_pairs={{0,8},{1,5},{2,10},{3,7},{4,12},{5,1},{6,14},{7,3},{8,0},{9,13},{1... | collective-permute-start | bytes 663560 | tf_op jit(solution)/shard_map/ppermute | solution.py:449
  128.9 7.2 %collective-permute-done.28.got_ref = bf16[144,768]{1,0:T(8,128)(2,1)S(1)} collective-permute-done((bf16[144,768]{1,0:T(8,128)(2,1)S(1)}, bf16[144,768]{1,0:T(8,128)(2,1)S(1)}, u32[]{:S(2)}, u32[]{:S(2)}) %collective-permute-start.28) | collective-permute-done | bytes 221216 | tf_op jit(solution)/shard_map/ppermute | solution.py:449
  136.9 1.6 %collective-permute-start.23 = (bf16[304,768]{1,0:T(8,128)(2,1)S(1)}, bf16[304,768]{1,0:T(8,128)(2,1)S(1)}, u32[]{:S(2)}, u32[]{:S(2)}) collective-permute-start(bf16[304,768]{1,0:T(8,128)(2,1)S(1)} %pad_maximum_fusion.3), channel_id=1, source_target_pairs={{0,4},{1,9},{2,6},{3,11},{4,0},{5,13},{6,2},{7,15},{8,12},{9,1},{1... | collective-permute-start | bytes 1400840 | tf_op jit(solution)/shard_map/ppermute | solution.py:449
  139.3 5.2 %collective-permute-done.29.got_ref = bf16[288,768]{1,0:T(8,128)(2,1)S(1)} collective-permute-done((bf16[288,768]{1,0:T(8,128)(2,1)S(1)}, bf16[288,768]{1,0:T(8,128)(2,1)S(1)}, u32[]{:S(2)}, u32[]{:S(2)}) %collective-permute-start.29) | collective-permute-done | bytes 442400 | tf_op jit(solution)/shard_map/ppermute | solution.py:449
  144.6 1.2 slice_bitcast_fusion
  145.9 3.6 %collective-permute-done.23 = bf16[304,768]{1,0:T(8,128)(2,1)S(1)} collective-permute-done((bf16[304,768]{1,0:T(8,128)(2,1)S(1)}, bf16[304,768]{1,0:T(8,128)(2,1)S(1)}, u32[]{:S(2)}, u32[]{:S(2)}) %collective-permute-start.23) | collective-permute-done | bytes 466976 | tf_op jit(solution)/shard_map/ppermute | solution.py:449
  150.8 1.3 join_halves.5
  (136 shorter events, 17.1 us)
Async XLA Ops:
  0.6 15.0 %copy-start.6 = (bf16[3,192,768]{2,1,0:T(8,128)(2,1)S(1)}, bf16[3,192,768]{2,1,0:T(8,128)(2,1)}, u32[]{:S(2)}) copy-start(bf16[3,192,768]{2,1,0:T(8,128)(2,1)} %own_ref.1) | copy-start | bytes 2654212
  0.7 12.2 %collective-permute-start = (bf16[3,192,768]{2,1,0:T(8,128)(2,1)}, bf16[3,192,768]{2,1,0:T(8,128)(2,1)S(1)}, u32[]{:S(2)}, u32[]{:S(2)}) collective-permute-start(bf16[3,192,768]{2,1,0:T(8,128)(2,1)} %own_ref.1), channel_id=1, source_target_pairs={{0,1},{1,0},{2,3},{3,2},{4,5},{5,4},{6,7},{7,6},{8,9},{9,8},{10,11... | collective-permute-start | bytes 2654216 | tf_op jit(solution)/shard_map/ppermute | solution.py:438
  2.2 10.6 %collective-permute-start.6 = (bf16[192,768]{1,0:T(8,128)(2,1)S(1)}, bf16[192,768]{1,0:T(8,128)(2,1)}, u32[]{:S(2)}, u32[]{:S(2)}) collective-permute-start(bf16[192,768]{1,0:T(8,128)(2,1)S(1)} %broadcast_select_fusion), channel_id=1, source_target_pairs={{0,2},{1,3},{2,0},{3,1},{4,6},{5,7},{6,4},{7,5},{8,10},{9,11},{10,... | collective-permute-start | bytes 884744 | tf_op jit(solution)/shard_map/ppermute | solution.py:441
  4.8 20.8 %collective-permute-start.3 = (bf16[192,768]{1,0:T(8,128)(2,1)}, bf16[192,768]{1,0:T(8,128)(2,1)}, u32[]{:S(2)}, u32[]{:S(2)}) collective-permute-start(bf16[192,768]{1,0:T(8,128)(2,1)} %wo0.1), channel_id=1, source_target_pairs={{0,1},{1,0},{2,3},{3,2},{4,5},{5,4},{6,7},{7,6},{8,9},{9,8},{10,11... | collective-permute-start | bytes 884744 | tf_op jit(solution)/shard_map/ppermute | solution.py:438
  5.0 24.5 %collective-permute-start.4 = (bf16[192,768]{1,0:T(8,128)(2,1)}, bf16[192,768]{1,0:T(8,128)(2,1)}, u32[]{:S(2)}, u32[]{:S(2)}) collective-permute-start(bf16[192,768]{1,0:T(8,128)(2,1)} %fc10.1), channel_id=1, source_target_pairs={{0,1},{1,0},{2,3},{3,2},{4,5},{5,4},{6,7},{7,6},{8,9},{9,8},{10,11... | collective-permute-start | bytes 884744 | tf_op jit(solution)/shard_map/ppermute | solution.py:438
  5.4 20.3 %collective-permute-start.1 = (bf16[256,768]{1,0:T(8,128)(2,1)}, bf16[256,768]{1,0:T(8,128)(2,1)}, u32[]{:S(2)}, u32[]{:S(2)}) collective-permute-start(bf16[256,768]{1,0:T(8,128)(2,1)} %x_ref.3), channel_id=1, source_target_pairs={{0,2},{1,3},{2,0},{3,1},{4,6},{5,7},{6,4},{7,5},{8,10},{9,11},{10,... | collective-permute-start | bytes 1179656 | tf_op jit(solution)/shard_map/ppermute | solution.py:441
  6.1 10.8 %copy-start.27 = (s32[8]{0:T(128)S(1)}, s32[8]{0:T(128)}, u32[]{:S(2)}) copy-start(s32[8]{0:T(128)} %refs_1_.3) | copy-start | bytes 100
  6.1 10.8 %copy-start.28 = (s32[8]{0:T(128)S(1)}, s32[8]{0:T(128)}, u32[]{:S(2)}) copy-start(s32[8]{0:T(128)} %refs_2_.3) | copy-start | bytes 100
  6.8 10.1 %copy-start.1 = (bf16[256,768]{1,0:T(8,128)(2,1)S(1)}, bf16[256,768]{1,0:T(8,128)(2,1)}, u32[]{:S(2)}) copy-start(bf16[256,768]{1,0:T(8,128)(2,1)} %x_ref.3) | copy-start | bytes 1179652
  12.8 10.8 %collective-permute-start.10 = (bf16[192]{0:T(256)(128)(2,1)}, bf16[192]{0:T(256)(128)(2,1)S(1)}, u32[]{:S(2)}, u32[]{:S(2)}) collective-permute-start(bf16[192]{0:T(256)(128)(2,1)} %param.23), channel_id=1, source_target_pairs={{0,1},{1,0},{2,3},{3,2},{4,5},{5,4},{6,7},{7,6},{8,9},{9,8},{10,11... | collective-permute-start | bytes 1160 | tf_op jit(solution)/shard_map/ppermute | solution.py:438
  13.7 12.4 %collective-permute-start.8 = (bf16[192,768]{1,0:T(8,128)(2,1)}, bf16[192,768]{1,0:T(8,128)(2,1)}, u32[]{:S(2)}, u32[]{:S(2)}) collective-permute-start(bf16[192,768]{1,0:T(8,128)(2,1)} %collective-permute-done.6.y0), channel_id=1, source_target_pairs={{0,4},{1,5},{2,6},{3,7},{4,0},{5,1},{6,2},{7,3},{8,12},{9,13},{10,... | collective-permute-start | bytes 884744 | tf_op jit(solution)/shard_map/ppermute | solution.py:449
  17.0 5.5 %copy-start = (bf16[256,768]{1,0:T(8,128)(2,1)S(1)}, bf16[256,768]{1,0:T(8,128)(2,1)}, u32[]{:S(2)}) copy-start(bf16[256,768]{1,0:T(8,128)(2,1)} %refs_4_.1) | copy-start | bytes 1179652
  24.1 22.7 %collective-permute-start.11 = (bf16[256,1152]{1,0:T(8,128)(2,1)}, bf16[256,1152]{1,0:T(8,128)(2,1)S(1)}, u32[]{:S(2)}, u32[]{:S(2)}) collective-permute-start(bf16[256,1152]{1,0:T(8,128)(2,1)} %pad_maximum_fusion.2), channel_id=1, source_target_pairs={{0,2},{1,3},{2,0},{3,1},{4,6},{5,7},{6,4},{7,5},{8,10},{9,11},{10,... | collective-permute-start | bytes 1769480 | tf_op jit(solution)/shard_map/ppermute | solution.py:441
  25.7 4.5 %collective-permute-start.5 = (bf16[192,768]{1,0:T(8,128)(2,1)}, bf16[192,768]{1,0:T(8,128)(2,1)}, u32[]{:S(2)}, u32[]{:S(2)}) collective-permute-start(bf16[192,768]{1,0:T(8,128)(2,1)} %fc20.1), channel_id=1, source_target_pairs={{0,1},{1,0},{2,3},{3,2},{4,5},{5,4},{6,7},{7,6},{8,9},{9,8},{10,11... | collective-permute-start | bytes 884744 | tf_op jit(solution)/shard_map/ppermute | solution.py:438
  25.7 4.5 %collective-permute-start.7 = (bf16[192,768]{1,0:T(8,128)(2,1)}, bf16[192,768]{1,0:T(8,128)(2,1)}, u32[]{:S(2)}, u32[]{:S(2)}) collective-permute-start(bf16[192,768]{1,0:T(8,128)(2,1)} %collective-permute-done.6.y0), channel_id=1, source_target_pairs={{0,1},{1,0},{2,3},{3,2},{4,5},{5,4},{6,7},{7,6},{8,9},{9,8},{10,11... | collective-permute-start | bytes 884744 | tf_op jit(solution)/shard_map/ppermute | solution.py:438
  26.2 4.0 %collective-permute-start.9 = (bf16[192,768]{1,0:T(8,128)(2,1)}, bf16[192,768]{1,0:T(8,128)(2,1)}, u32[]{:S(2)}, u32[]{:S(2)}) collective-permute-start(bf16[192,768]{1,0:T(8,128)(2,1)} %collective-permute-done.8.x0), channel_id=1, source_target_pairs={{0,1},{1,0},{2,3},{3,2},{4,5},{5,4},{6,7},{7,6},{8,9},{9,8},{10,11... | collective-permute-start | bytes 884744 | tf_op jit(solution)/shard_map/ppermute | solution.py:438
  26.2 3.8 %copy-start.33 = (bf16[192]{0:T(256)(128)(2,1)S(1)}, bf16[192]{0:T(256)(128)(2,1)}, u32[]{:S(2)}) copy-start(bf16[192]{0:T(256)(128)(2,1)} %param.23) | copy-start | bytes 1156
  26.2 3.8 %copy-start.31 = (f32[768]{0:T(1024)S(1)}, f32[768]{0:T(1024)}, u32[]{:S(2)}) copy-start(f32[768]{0:T(1024)} %param.20) | copy-start | bytes 9220
  26.3 3.8 %copy-start.32 = (f32[768]{0:T(1024)S(1)}, f32[768]{0:T(1024)}, u32[]{:S(2)}) copy-start(f32[768]{0:T(1024)} %param.21) | copy-start | bytes 9220
  26.3 3.9 %copy-start.35 = (bf16[192]{0:T(256)(128)(2,1)S(1)}, bf16[192]{0:T(256)(128)(2,1)}, u32[]{:S(2)}) copy-start(bf16[192]{0:T(256)(128)(2,1)} %copy-done.34) | copy-start | bytes 1156
  26.3 4.0 %copy-start.2 = (bf16[192,768]{1,0:T(8,128)(2,1)S(1)}, bf16[192,768]{1,0:T(8,128)(2,1)}, u32[]{:S(2)}) copy-start(bf16[192,768]{1,0:T(8,128)(2,1)} %wo0.1) | copy-start | bytes 884740
  26.3 4.0 %copy-start.3 = (bf16[192,768]{1,0:T(8,128)(2,1)S(1)}, bf16[192,768]{1,0:T(8,128)(2,1)}, u32[]{:S(2)}) copy-start(bf16[192,768]{1,0:T(8,128)(2,1)} %fc10.1) | copy-start | bytes 884740
  29.5 14.5 %collective-permute-start.2 = (bf16[256,384]{1,0:T(8,128)(2,1)S(1)}, bf16[256,384]{1,0:T(8,128)(2,1)S(1)}, u32[]{:S(2)}, u32[]{:S(2)}) collective-permute-start(bf16[256,384]{1,0:T(8,128)(2,1)S(1)} %get-tuple-element.64.oa_ref), channel_id=1, source_target_pairs={{0,2},{1,3},{2,0},{3,1},{4,6},{5,7},{6,4},{7,5},{8,10},{9,11},{10,... | collective-permute-start | bytes 589832 | tf_op jit(solution)/shard_map/ppermute | solution.py:441
  45.3 6.9 %collective-permute-start.14 = (bf16[256,384]{1,0:T(8,128)(2,1)S(1)}, bf16[256,384]{1,0:T(8,128)(2,1)S(1)}, u32[]{:S(2)}, u32[]{:S(2)}) collective-permute-start(bf16[256,384]{1,0:T(8,128)(2,1)S(1)} %get-tuple-element.70.du0.refs_0_), channel_id=1, source_target_pairs={{0,2},{1,3},{2,0},{3,1},{4,6},{5,7},{6,4},{7,5},{8,10},{9,11},{10,... | collective-permute-start | bytes 589832 | tf_op jit(solution)/shard_map/ppermute | solution.py:441
  49.1 9.3 %collective-permute-start.13 = (bf16[256,384]{1,0:T(8,128)(2,1)S(1)}, bf16[256,384]{1,0:T(8,128)(2,1)S(1)}, u32[]{:S(2)}, u32[]{:S(2)}) collective-permute-start(bf16[256,384]{1,0:T(8,128)(2,1)S(1)} %get-tuple-element.71.du1.refs_0_), channel_id=1, source_target_pairs={{0,2},{1,3},{2,0},{3,1},{4,6},{5,7},{6,4},{7,5},{8,10},{9,11},{10,... | collective-permute-start | bytes 589832 | tf_op jit(solution)/shard_map/ppermute | solution.py:441
  54.6 3.7 %copy-start.5 = (bf16[2,8,128,256]{3,2,1,0:T(8,128)(2,1)S(1)}, bf16[2,8,128,256]{3,2,1,0:T(8,128)(2,1)}, u32[]{:S(2)}) copy-start(bf16[2,8,128,256]{3,2,1,0:T(8,128)(2,1)} %copy-done.4) | copy-start | bytes 3145732
  54.6 3.7 %copy-start.18 = (bf16[384,256]{1,0:T(8,128)(2,1)S(1)}, bf16[384,256]{1,0:T(8,128)(2,1)}, u32[]{:S(2)}) copy-start(bf16[384,256]{1,0:T(8,128)(2,1)} %copy-done.17) | copy-start | bytes 589828
  54.7 3.7 %copy-start.20 = (bf16[256,384]{1,0:T(8,128)(2,1)S(1)}, bf16[256,384]{1,0:T(8,128)(2,1)}, u32[]{:S(2)}) copy-start(bf16[256,384]{1,0:T(8,128)(2,1)} %copy-done.19) | copy-start | bytes 589828
  58.4 2.5 %copy-start.22 = (bf16[384,256]{1,0:T(8,128)(2,1)S(1)}, bf16[384,256]{1,0:T(8,128)(2,1)}, u32[]{:S(2)}) copy-start(bf16[384,256]{1,0:T(8,128)(2,1)} %copy-done.21) | copy-start | bytes 589828
  62.4 22.7 %collective-permute-start.24 = (bf16[3,192,768]{2,1,0:T(8,128)(2,1)}, bf16[3,192,768]{2,1,0:T(8,128)(2,1)}, u32[]{:S(2)}, u32[]{:S(2)}) collective-permute-start(bf16[3,192,768]{2,1,0:T(8,128)(2,1)} %pad_maximum_fusion.1), channel_id=1, source_target_pairs={{0,1},{1,0},{2,3},{3,2},{4,5},{5,4},{6,7},{7,6},{8,9},{9,8},{10,11... | collective-permute-start | bytes 2654216 | tf_op jit(solution)/shard_map/ppermute | solution.py:438
  64.4 15.1 %copy-start.24 = (f32[8,768]{1,0:T(8,128)S(1)}, f32[8,768]{1,0:T(8,128)}, u32[]{:S(2)}) copy-start(f32[8,768]{1,0:T(8,128)} %copy-done.23) | copy-start | bytes 73732
  64.4 22.6 %collective-permute-start.16 = (bf16[3,192,768]{2,1,0:T(8,128)(2,1)}, bf16[3,192,768]{2,1,0:T(8,128)(2,1)}, u32[]{:S(2)}, u32[]{:S(2)}) collective-permute-start(bf16[3,192,768]{2,1,0:T(8,128)(2,1)} %get-tuple-element.97), channel_id=1, source_target_pairs={{0,1},{1,0},{2,3},{3,2},{4,5},{5,4},{6,7},{7,6},{8,9},{9,8},{10,11... | collective-permute-start | bytes 2654216 | tf_op jit(solution)/shard_map/ppermute | solution.py:438
  67.5 12.0 %collective-permute-start.15 = (bf16[256,768]{1,0:T(8,128)(2,1)}, bf16[256,768]{1,0:T(8,128)(2,1)S(1)}, u32[]{:S(2)}, u32[]{:S(2)}) collective-permute-start(bf16[256,768]{1,0:T(8,128)(2,1)} %get-tuple-element.89), channel_id=1, source_target_pairs={{0,2},{1,3},{2,0},{3,1},{4,6},{5,7},{6,4},{7,5},{8,10},{9,11},{10,... | collective-permute-start | bytes 1179656 | tf_op jit(solution)/shard_map/ppermute | solution.py:441
  81.8 3.2 %copy-start.16 = (bf16[2,192,768]{2,1,0:T(8,128)(2,1)S(1)}, bf16[2,192,768]{2,1,0:T(8,128)(2,1)}, u32[]{:S(2)}) copy-start(bf16[2,192,768]{2,1,0:T(8,128)(2,1)} %copy-done.15) | copy-start | bytes 1769476
  83.2 6.7 %collective-permute-start.19 = (bf16[16,768]{1,0:T(8,128)(2,1)S(1)}, bf16[16,768]{1,0:T(8,128)(2,1)S(1)}, u32[]{:S(2)}, u32[]{:S(2)}) collective-permute-start(bf16[16,768]{1,0:T(8,128)(2,1)S(1)} %get-tuple-element.102), channel_id=1, source_target_pairs={{0,2},{1,3},{2,0},{3,1},{4,6},{5,7},{6,4},{7,5},{8,10},{9,11},{10,... | collective-permute-start | bytes 73736 | tf_op jit(solution)/shard_map/ppermute | solution.py:441
  86.4 8.4 %collective-permute-start.25 = (bf16[288,768]{1,0:T(8,128)(2,1)S(1)}, bf16[288,768]{1,0:T(8,128)(2,1)S(1)}, u32[]{:S(2)}, u32[]{:S(2)}) collective-permute-start(bf16[288,768]{1,0:T(8,128)(2,1)S(1)} %get-tuple-element.112), channel_id=1, source_target_pairs={{0,4},{1,9},{2,6},{3,11},{4,0},{5,13},{6,2},{7,15},{8,12},{9,1},{1... | collective-permute-start | bytes 1327112 | tf_op jit(solution)/shard_map/ppermute | solution.py:449
  88.4 15.0 %collective-permute-start.17 = (bf16[288,768]{1,0:T(8,128)(2,1)S(1)}, bf16[288,768]{1,0:T(8,128)(2,1)S(1)}, u32[]{:S(2)}, u32[]{:S(2)}) collective-permute-start(bf16[288,768]{1,0:T(8,128)(2,1)S(1)} %get-tuple-element.99), channel_id=1, source_target_pairs={{0,4},{1,9},{2,6},{3,11},{4,0},{5,13},{6,2},{7,15},{8,12},{9,1},{1... | collective-permute-start | bytes 1327112 | tf_op jit(solution)/shard_map/ppermute | solution.py:449
  90.0 1.2 collective-permute-start.20
  94.9 23.4 %collective-permute-start.26 = (bf16[144,768]{1,0:T(8,128)(2,1)S(1)}, bf16[144,768]{1,0:T(8,128)(2,1)S(1)}, u32[]{:S(2)}, u32[]{:S(2)}) collective-permute-start(bf16[144,768]{1,0:T(8,128)(2,1)S(1)} %get-tuple-element.114), channel_id=1, source_target_pairs={{0,8},{1,5},{2,10},{3,7},{4,12},{5,1},{6,14},{7,3},{8,0},{9,13},{1... | collective-permute-start | bytes 663560 | tf_op jit(solution)/shard_map/ppermute | solution.py:449
  103.5 7.2 %collective-permute-start.18 = (bf16[144,768]{1,0:T(8,128)(2,1)S(1)}, bf16[144,768]{1,0:T(8,128)(2,1)S(1)}, u32[]{:S(2)}, u32[]{:S(2)}) collective-permute-start(bf16[144,768]{1,0:T(8,128)(2,1)S(1)} %get-tuple-element.101), channel_id=1, source_target_pairs={{0,8},{1,5},{2,10},{3,7},{4,12},{5,1},{6,14},{7,3},{8,0},{9,13},{1... | collective-permute-start | bytes 663560 | tf_op jit(solution)/shard_map/ppermute | solution.py:449
  110.8 17.8 %copy-start.26 = (bf16[256,768]{1,0:T(8,128)(2,1)S(1)}, bf16[256,768]{1,0:T(8,128)(2,1)}, u32[]{:S(2)}) copy-start(bf16[256,768]{1,0:T(8,128)(2,1)} %copy-done.25) | copy-start | bytes 1179652
  110.8 11.8 %collective-permute-start.21 = (bf16[160,768]{1,0:T(8,128)(2,1)S(1)}, bf16[160,768]{1,0:T(8,128)(2,1)S(1)}, u32[]{:S(2)}, u32[]{:S(2)}) collective-permute-start(bf16[160,768]{1,0:T(8,128)(2,1)S(1)} %pad_maximum_fusion.4.a_ref), channel_id=1, source_target_pairs={{0,24},{1,25},{2,26},{3,27},{4,28},{5,29},{6,30},{7,31},{8,16},{9,... | collective-permute-start | bytes 737288 | tf_op jit(solution)/shard_map/ppermute | solution.py:449
  118.3 7.9 %collective-permute-start.27 = (bf16[144,768]{1,0:T(8,128)(2,1)S(1)}, bf16[144,768]{1,0:T(8,128)(2,1)S(1)}, u32[]{:S(2)}, u32[]{:S(2)}) collective-permute-start(bf16[144,768]{1,0:T(8,128)(2,1)S(1)} %sum_two.6.a_ref), channel_id=1, source_target_pairs={{0,24},{1,25},{2,26},{3,27},{4,28},{5,29},{6,30},{7,31},{8,16},{9,... | collective-permute-start | bytes 663560 | tf_op jit(solution)/shard_map/ppermute | solution.py:449
  122.6 14.1 %collective-permute-start.22 = (bf16[160,768]{1,0:T(8,128)(2,1)S(1)}, bf16[160,768]{1,0:T(8,128)(2,1)S(1)}, u32[]{:S(2)}, u32[]{:S(2)}) collective-permute-start(bf16[160,768]{1,0:T(8,128)(2,1)S(1)} %sum_two.5), channel_id=1, source_target_pairs={{0,8},{1,5},{2,10},{3,7},{4,12},{5,1},{6,14},{7,3},{8,0},{9,13},{1... | collective-permute-start | bytes 737288 | tf_op jit(solution)/shard_map/ppermute | solution.py:449
  126.3 9.8 %collective-permute-start.28 = (bf16[144,768]{1,0:T(8,128)(2,1)S(1)}, bf16[144,768]{1,0:T(8,128)(2,1)S(1)}, u32[]{:S(2)}, u32[]{:S(2)}) collective-permute-start(bf16[144,768]{1,0:T(8,128)(2,1)S(1)} %sum_two.7.mine_ref), channel_id=1, source_target_pairs={{0,8},{1,5},{2,10},{3,7},{4,12},{5,1},{6,14},{7,3},{8,0},{9,13},{1... | collective-permute-start | bytes 663560 | tf_op jit(solution)/shard_map/ppermute | solution.py:449
  128.6 9.9 %collective-permute-start.12 = (bf16[256,768]{1,0:T(8,128)(2,1)S(1)}, bf16[256,768]{1,0:T(8,128)(2,1)S(1)}, u32[]{:S(2)}, u32[]{:S(2)}) collective-permute-start(bf16[256,768]{1,0:T(8,128)(2,1)S(1)} %copy-done.26), channel_id=1, source_target_pairs={{0,2},{1,3},{2,0},{3,1},{4,6},{5,7},{6,4},{7,5},{8,10},{9,11},{10,... | collective-permute-start | bytes 1179656 | tf_op jit(solution)/shard_map/ppermute | solution.py:441
  136.1 8.4 %collective-permute-start.29 = (bf16[288,768]{1,0:T(8,128)(2,1)S(1)}, bf16[288,768]{1,0:T(8,128)(2,1)S(1)}, u32[]{:S(2)}, u32[]{:S(2)}) collective-permute-start(bf16[288,768]{1,0:T(8,128)(2,1)S(1)} %bitcast.28), channel_id=1, source_target_pairs={{0,4},{1,9},{2,6},{3,11},{4,0},{5,13},{6,2},{7,15},{8,12},{9,1},{1... | collective-permute-start | bytes 1327112 | tf_op jit(solution)/shard_map/ppermute | solution.py:449
  136.9 12.7 %collective-permute-start.23 = (bf16[304,768]{1,0:T(8,128)(2,1)S(1)}, bf16[304,768]{1,0:T(8,128)(2,1)S(1)}, u32[]{:S(2)}, u32[]{:S(2)}) collective-permute-start(bf16[304,768]{1,0:T(8,128)(2,1)S(1)} %pad_maximum_fusion.3), channel_id=1, source_target_pairs={{0,4},{1,9},{2,6},{3,11},{4,0},{5,13},{6,2},{7,15},{8,12},{9,1},{1... | collective-permute-start | bytes 1400840 | tf_op jit(solution)/shard_map/ppermute | solution.py:449
  (18 other events, 18.6 us)

commit v3 on v2

v3 whole, which is shorter than its diff:
```python
import functools

import jax
import jax.numpy as jnp
from jax import lax
from jax.experimental import pallas as pl
from jax.experimental.pallas import tpu as pltpu
from jax.sharding import PartitionSpec as P

HEAD_DIM = 24
LEN = 128
PAIR = 2 * HEAD_DIM
EPSILON = 1e-05
SCALE = HEAD_DIM ** (-0.5)
LOG2E = 1.4426950408889634
F32 = jnp.float32
BF16 = jnp.bfloat16
MIB = 1024 * 1024


def dot_nn(a, b):
    return lax.dot_general(a, b, (((1,), (0,)), ((), ())), preferred_element_type=F32)


def dot_nt(a, b):
    return lax.dot_general(a, b, (((1,), (1,)), ((), ())), preferred_element_type=F32)


def dot_tn(a, b):
    return lax.dot_general(a, b, (((0,), (0,)), ((), ())), preferred_element_type=F32)


def normalise(v):
    centered = v - jnp.mean(v, axis=-1, keepdims=True)
    r = lax.rsqrt(jnp.mean(centered * centered, axis=-1, keepdims=True) + EPSILON)
    return centered * r, r


def norm_back(da, gain, xh, r):
    e = da * gain
    return r * (
        e - jnp.mean(e, axis=-1, keepdims=True) - xh * jnp.mean(e * xh, axis=-1, keepdims=True)
    )


def pair_blocks(rows):
    rows = rows.astype(F32)
    none = jnp.zeros((HEAD_DIM, LEN), F32)
    left = jnp.concatenate([rows[:HEAD_DIM], none], axis=0)
    right = jnp.concatenate([none, rows[HEAD_DIM:]], axis=0)
    return jnp.concatenate([left, right], axis=1).astype(BF16)


def pair_window(i, width):
    low = min(PAIR * i // LEN * LEN, width - 2 * LEN)
    return low, PAIR * i - low


def placed(block, before):
    parts = []
    if before:
        parts.append(jnp.zeros((before, 2 * LEN), BF16))
    parts.append(block)
    after = 2 * LEN - PAIR - before
    if after:
        parts.append(jnp.zeros((after, 2 * LEN), BF16))
    return jnp.concatenate(parts, axis=0)


def diagonal(both):
    return jnp.concatenate([both[:HEAD_DIM, :LEN], both[HEAD_DIM:, LEN:]], axis=0)


def call(kernel, name, args, outs, flops=0, scalars=0, far=(), direct=(), scratch=(), after=(), limit=16):
    size = lambda a: a.size * a.dtype.itemsize
    anywhere = pl.BlockSpec(memory_space=pl.ANY)
    vmem = pl.BlockSpec(memory_space=pltpu.VMEM)
    smem = pl.BlockSpec(memory_space=pltpu.SMEM)
    n = len(args)

    def body(*refs):
        kernel(*refs[:n], *refs[n + len(after) :])

    return pl.pallas_call(
        body,
        in_specs=[smem if j < scalars else anywhere if j in far else vmem for j in range(n)]
        + [anywhere] * len(after),
        out_specs=[anywhere if j in direct else vmem for j in range(len(outs))],
        out_shape=outs,
        scratch_shapes=list(scratch),
        compiler_params=pltpu.CompilerParams(vmem_limit_bytes=limit * MIB),
        cost_estimate=pl.CostEstimate(
            flops=flops,
            bytes_accessed=sum(map(size, args)) + sum(map(size, outs)),
            transcendentals=0,
        ),
        name=name,
    )(*args, *after)


def bf16(*shape):
    return jax.ShapeDtypeStruct(shape, BF16)


def f32(*shape):
    return jax.ShapeDtypeStruct(shape, F32)


def copies(sems, pairs):
    started = [pltpu.make_async_copy(a, b, sems.at[j]) for j, (a, b) in enumerate(pairs)]
    for copy in started:
        copy.start()
    return started


def finish(started):
    for copy in started:
        copy.wait()


def attention_body(place_ref, nodes_ref, edges_ref, x_ref, gain_ref, bias_ref, w_ref, a1_ref, qt_ref,
                   kt_ref, v_ref, p_ref, ot_ref, ready):
    width = w_ref.shape[1]
    mols = x_ref.shape[0] // LEN
    pairs = width // PAIR
    xh, _ = normalise(x_ref[...].astype(F32))
    a1 = (xh * gain_ref[...][None, :] + bias_ref[...][None, :]).astype(BF16)
    a1_ref[...] = a1
    ready()
    qt = dot_nt(w_ref[0], a1).astype(BF16)
    keys = dot_nt(a1, w_ref[1]).astype(BF16)
    vt = dot_nt(w_ref[2], a1).astype(BF16)
    qt_ref[...] = qt
    every = [(m, i) for m in range(mols) for i in range(pairs)]
    lanes = lambda m: slice(LEN * m, LEN * (m + 1))
    rows = lambda i: slice(PAIR * i, PAIR * (i + 1))
    scores, probs = {}, {}
    for m, i in every:
        low, before = pair_window(i, width)
        rhs = placed(pair_blocks(qt[rows(i), lanes(m)]), before)
        scores[m, i] = dot_nn(keys[lanes(m), low : low + 2 * LEN], rhs)
    for m in range(mols):
        mol = place_ref[0] + m
        count = 1 + nodes_ref[mol] + edges_ref[mol]
        valid = lax.broadcasted_iota(jnp.int32, (LEN, 2 * LEN), 0) < count
        for i in range(pairs):
            s = jnp.where(valid, scores[m, i], -1e30)
            e = jnp.exp2((s - jnp.max(s, axis=0, keepdims=True)) * (SCALE * LOG2E))
            p = (e * (1.0 / jnp.sum(e, axis=0, keepdims=True))).astype(BF16)
            p_ref[m, i] = p
            probs[m, i] = p
    for m, i in every:
        both = dot_nn(vt[rows(i), lanes(m)], probs[m, i])
        ot_ref[rows(i), lanes(m)] = diagonal(both).astype(BF16)
    kt_ref[...] = dot_nt(w_ref[1], a1).astype(BF16)
    v_ref[...] = dot_nt(a1, w_ref[2]).astype(BF16)


def attention_outs(rows, d, width):
    pairs = width // PAIR
    return [
        bf16(rows, d), bf16(width, rows), bf16(width, rows), bf16(rows, width),
        bf16(rows // LEN, pairs, LEN, 2 * LEN), bf16(width, rows),
    ]


def attention_first(place, nodes, edges, x, gain, bias, w_own, w_got, g):
    rows, d = x.shape
    shard = w_own.shape[1]
    width = 2 * shard

    def kernel(place_ref, nodes_ref, edges_ref, x_ref, gain_ref, bias_ref, own, got, g_ref, *refs):
        *kept, packet_ref, w_ref, sems = refs
        started = copies(
            sems,
            [(own, w_ref.at[:, :shard]), (got, w_ref.at[:, shard:]), (g_ref, packet_ref.at[:, :d])],
        )
        attention_body(
            place_ref, nodes_ref, edges_ref, x_ref, gain_ref, bias_ref, w_ref, *kept,
            lambda: finish(started[:2]),
        )
        packet_ref[:, d:] = kept[-1][...].T
        finish(started[2:])

    return call(
        kernel, "attention_first", (place, nodes, edges, x, gain, bias, w_own, w_got, g),
        [*attention_outs(rows, d, width), bf16(rows, d + width), bf16(3, width, d)],
        rows * width * (10 * d + 8 * LEN), scalars=3, far=(6, 7, 8),
        scratch=[pltpu.SemaphoreType.DMA((3,))],
    )


def attention_second(place, nodes, edges, x, gain, bias, w, after):
    rows, d = x.shape
    width = w.shape[1]

    def kernel(*refs):
        *refs, o_ref = refs
        attention_body(*refs, lambda: None)
        o_ref[...] = refs[-1][...].T

    return call(
        kernel, "attention_second", (place, nodes, edges, x, gain, bias, w),
        [*attention_outs(rows, d, width), bf16(rows, width)],
        rows * width * (10 * d + 8 * LEN), scalars=3, after=after,
    )


def hold(a, after):
    def kernel(a_ref, out_ref, sem):
        finish(copies(sem, [(a_ref, out_ref)]))

    return call(
        kernel, "hold", (a,), [jax.ShapeDtypeStruct(a.shape, a.dtype)], far=(0,), after=after,
        scratch=[pltpu.SemaphoreType.DMA((1,))], limit=4,
    )[0]


def pack_rest(bit, *parts):
    shard, d = parts[0].shape

    def kernel(bit_ref, wo0, wo1, fc10, fc11, fc20, fc21, y0, y1, x0, x1, wo_ref, fc1_ref, fc2_ref, sems):
        rows = lambda ref, at: ref.at[at * shard : (at + 1) * shard]
        started = copies(
            sems,
            [(wo0, rows(wo_ref, 0)), (wo1, rows(wo_ref, 1)), (fc10, rows(fc1_ref, 0)),
             (fc11, rows(fc1_ref, 1)), (fc20, rows(fc2_ref, 0)), (fc21, rows(fc2_ref, 1))],
        )

        def far(u, v):
            pairs = [(u[0], rows(wo_ref, 2)), (u[1], rows(wo_ref, 3)), (v[0], rows(fc1_ref, 2)),
                     (v[1], rows(fc1_ref, 3))]
            finish(copies(sems.at[6:], pairs))

        pl.when(bit_ref[0] == 0)(lambda: far((y0, y1), (x0, x1)))
        pl.when(bit_ref[0] != 0)(lambda: far((x0, x1), (y0, y1)))
        finish(started)

    return call(
        kernel, "pack_rest", (bit, *parts), [bf16(4 * shard, d), bf16(4 * shard, d), bf16(2 * shard, d)],
        scalars=1, far=range(1, 11), scratch=[pltpu.SemaphoreType.DMA((10,))], limit=4,
    )


def feed_body(x, oa, ob, g, wo_ref, gain_ref, bias_ref, fc1_ref, b1_ref, fc2_ref, h_ref, a2_ref, z_ref,
              du_ref):
    h = x.astype(F32) + dot_nn(jnp.concatenate([oa, ob], axis=1), wo_ref[...])
    h_ref[...] = h
    xh, _ = normalise(h)
    a2 = (xh * gain_ref[...][None, :] + bias_ref[...][None, :]).astype(BF16)
    a2_ref[...] = a2
    u = dot_nt(a2, fc1_ref[: fc2_ref.shape[0]]) + b1_ref[...]
    dz = dot_nt(g, fc2_ref[...])
    phi = 0.5 * (1.0 + lax.erf(u * (0.5**0.5)))
    slope = phi + u * (jnp.exp(-0.5 * u * u) * 0.3989422804014327)
    du_ref[...] = (dz * slope).astype(BF16)
    z_ref[...] = (u * phi).astype(BF16)


def feed(x, oa, got, wo, gain, bias, fc1, b1, fc2, after=()):
    rows, d = x.shape
    width = fc2.shape[0]
    got = got if isinstance(got, tuple) else (got,)

    def kernel(x_ref, oa_ref, *refs):
        if len(got) == 2:
            g, ob = refs[0][...], refs[1][...]
        else:
            g, ob = refs[0][:, :d], refs[0][:, d:]
        oa = oa_ref[:, oa_ref.shape[1] - width :]
        feed_body(x_ref[...], oa, ob, g, *refs[len(got) :])

    return call(
        kernel, "feed_forward", (x, oa, *got, wo, gain, bias, fc1, b1, fc2),
        [f32(rows, d), bf16(rows, d), bf16(rows, width), bf16(rows, width)],
        8 * rows * d * width, after=after,
    )


def feed_grads(zs, dus, a2s, gs, after):
    d = a2s[0].shape[1]
    width = zs[0].shape[1]
    shard = width // 2

    def kernel(z0, z1, du0, du1, a0, a1, g0, g1, keep_ref, send_ref, sums_ref):
        first = dot_tn(du0[...], a0[...]) + dot_tn(du1[...], a1[...])
        second = dot_tn(z0[...], g0[...]) + dot_tn(z1[...], g1[:, :d])
        for at, ref in enumerate((keep_ref, send_ref)):
            rows = slice(at * shard, (at + 1) * shard)
            ref[0] = first[rows].astype(BF16)
            ref[1] = second[rows].astype(BF16)
        sums_ref[...] = jnp.sum(du0[...].astype(F32), axis=0, keepdims=True) + jnp.sum(
            du1[...].astype(F32), axis=0, keepdims=True
        )

    return call(
        kernel, "feed_grads", (*zs, *dus, *a2s, *gs), [bf16(2, shard, d), bf16(2, shard, d), f32(1, width)],
        8 * zs[0].size * d, after=after,
    )


def feed_result(zs, fc2, h, after):
    rows, d = h.shape

    def kernel(z0, z1, fc2_ref, h_ref, mine_ref, theirs_ref):
        theirs_ref[...] = dot_nn(z1[...], fc2_ref[...]).astype(BF16)
        mine_ref[...] = h_ref[...] + dot_nn(z0[...], fc2_ref[...])

    return call(
        kernel, "feed_result", (*zs, fc2, h), [f32(rows, d), bf16(rows, d)], 4 * zs[0].size * d,
        after=after, limit=8,
    )


def backward_body(du_ref, dr_ref, fc1_ref, h_ref, g_ref, gain_ref, wo_ref, p_ref, qt_ref, kt_ref, v_ref,
                  gh_ref, dp_ref, dh_ref=None, sums_ref=None):
    width, d = kt_ref.shape[0], h_ref.shape[1]
    mols = h_ref.shape[0] // LEN
    pairs = width // PAIR
    du = jnp.concatenate([du_ref[...], dr_ref[...]], axis=1)
    da2 = dot_nn(du, fc1_ref[...])
    xh, r = normalise(h_ref[...])
    dh = g_ref[:, :d].astype(F32) + norm_back(da2, gain_ref[...][None, :], xh, r)
    if dh_ref is not None:
        dh_ref[...] = dh
        sums_ref[0:1] = jnp.sum(da2 * xh, axis=0, keepdims=True)
        sums_ref[1:2] = jnp.sum(da2, axis=0, keepdims=True)
    gh = dh.astype(BF16)
    gh_ref[...] = gh
    dot = dot_nt(wo_ref[:width], gh).astype(BF16)
    every = [(m, i) for m in range(mols) for i in range(pairs)]
    lanes = lambda m: slice(LEN * m, LEN * (m + 1))
    rows = lambda i: slice(PAIR * i, PAIR * (i + 1))
    dps, dss, dos = {}, {}, {}
    for m, i in every:
        low, before = pair_window(i, width)
        dos[m, i] = pair_blocks(dot[rows(i), lanes(m)])
        dps[m, i] = dot_nn(v_ref[lanes(m), low : low + 2 * LEN], placed(dos[m, i], before))
    for m, i in every:
        dp_ref[pl.ds(2 * width + PAIR * i, PAIR), lanes(m)] = dot_nt(dos[m, i], p_ref[m, i]).astype(BF16)
    for m, i in every:
        p = p_ref[m, i].astype(F32)
        t = dps[m, i] * p
        dss[m, i] = (t - p * jnp.sum(t, axis=0, keepdims=True)).astype(BF16)
    for m, i in every:
        dq = diagonal(dot_nn(kt_ref[rows(i), lanes(m)], dss[m, i])) * SCALE
        dp_ref[rows(i), lanes(m)] = dq.astype(BF16)
        dk = dot_nt(pair_blocks(qt_ref[rows(i), lanes(m)]), dss[m, i]) * SCALE
        dp_ref[pl.ds(width + PAIR * i, PAIR), lanes(m)] = dk.astype(BF16)


def backward(args, own, after=()):
    h, kt = args[3], args[9]
    rows, d = h.shape
    width = kt.shape[0]
    outs = [bf16(rows, d), bf16(3 * width, rows)]
    return call(
        backward_body, "attention_backward", args, outs + ([f32(rows, d), f32(8, d)] if own else []),
        rows * width * (6 * d + 16 * LEN), after=after,
    )


def out_grads(ots, ghs, keep, send):
    width, d = ots[0].shape[0], ghs[0].shape[1]
    shard = width // 2

    def kernel(ot0, ot1, gh0, gh1, keep2, send2, keep_ref, send_ref):
        total = dot_nn(ot0[...], gh0[...]) + dot_nn(ot1[...], gh1[...])
        for at, (two, ref) in enumerate(((keep2, keep_ref), (send2, send_ref))):
            ref[2] = total[at * shard : (at + 1) * shard].astype(BF16)
            ref[:2] = two[...]

    return call(
        kernel, "out_grads", (*ots, *ghs, keep, send), [bf16(3, shard, d), bf16(3, shard, d)],
        4 * ots[0].size * d, limit=8,
    )


def qkv_grads(dps, a1s, after):
    width, d = dps[0].shape[0] // 3, a1s[0].shape[1]
    shard = width // 2

    def kernel(dp0, dp1, a0, a1, keep_ref, send_ref):
        a = jnp.concatenate([a0[...], a1[...]], axis=0)
        for at, ref in ((1, send_ref), (0, keep_ref)):
            for c in range(3):
                rows = slice((2 * c + at) * shard, (2 * c + at + 1) * shard)
                ref[c] = dot_nn(jnp.concatenate([dp0[rows], dp1[rows]], axis=1), a).astype(BF16)

    return call(
        kernel, "qkv_grads", (*dps, *a1s), [bf16(3, shard, d), bf16(3, shard, d)],
        4 * dps[0].size * d, after=after,
    )


def input_grads(dps, w, xs, sums, bias, after):
    rows, d = xs[0].shape

    def kernel(dp0, dp1, w_ref, x0, x1, sums_ref, bias_ref, mine_ref, theirs_ref):
        w = w_ref[...].reshape(dp0.shape[0], d)
        theirs = dot_tn(dp1[...], w)
        mine = dot_tn(dp0[...], w)
        theirs_ref[:rows] = theirs.astype(BF16)
        mine_ref[...] = mine
        xh0, _ = normalise(x0[...].astype(F32))
        xh1, _ = normalise(x1[...].astype(F32))
        bias = bias_ref[...]
        vec = [
            jnp.sum(mine * xh0, axis=0, keepdims=True) + jnp.sum(theirs * xh1, axis=0, keepdims=True),
            jnp.sum(mine, axis=0, keepdims=True) + jnp.sum(theirs, axis=0, keepdims=True),
            sums_ref[0:2],
            jnp.concatenate([bias, jnp.zeros((1, d - bias.shape[1]), F32)], axis=1),
            jnp.zeros((11, d), F32),
        ]
        theirs_ref[rows:] = jnp.concatenate(vec, axis=0).astype(BF16)

    return call(
        kernel, "input_grads", (*dps, w, *xs, sums, bias), [f32(rows, d), bf16(rows + 16, d)],
        4 * dps[0].size * d, after=after,
    )


def input_norm(x, gain, mine, got, dh, after):
    rows, d = x.shape

    def kernel(x_ref, gain_ref, mine_ref, got_ref, dh_ref, out_ref):
        xh, r = normalise(x_ref[...].astype(F32))
        da1 = mine_ref[...] + got_ref[:rows].astype(F32)
        out_ref[...] = (dh_ref[...] + norm_back(da1, gain_ref[...][None, :], xh, r)).astype(BF16)

    return call(
        kernel, "input_norm", (x, gain, mine, got, dh), [bf16(rows, d)], rows * d * 20, after=after, limit=8
    )[0]


def add_result(mine, got, after):
    def kernel(mine_ref, got_ref, out_ref):
        out_ref[...] = (mine_ref[...] + got_ref[...].astype(F32)).astype(BF16)

    return call(kernel, "add_result", (mine, got), [bf16(*mine.shape)], mine.size, after=after, limit=8)[0]


def plus(*terms):
    total = terms[0].astype(F32)
    for term in terms[1:]:
        total = total + term.astype(F32)
    return total.astype(BF16)


def vector_rows(mine, got, after):
    rows, d = mine.shape

    def kernel(mine_ref, got_ref, out_ref):
        a, b = mine_ref[rows - 16 :], got_ref[rows - 16 :]
        same = lax.broadcasted_iota(jnp.int32, (16, d), 0) < 4
        out_ref[...] = plus(a, jnp.where(same, b.astype(F32), 0.0))

    return call(kernel, "vector_rows", (mine, got), [bf16(16, d)], after=after, limit=4)[0]


def sum_half(bits, mine, got, after):
    def kernel(bits_ref, mine_ref, got_ref, out_ref):
        at = 1 - bits_ref[0]
        out_ref[...] = mine_ref[at] + got_ref[at]

    return call(
        kernel, "sum_half", (bits, mine, got), [bf16(*mine.shape[1:])], mine.size, scalars=1, after=after,
        limit=8,
    )[0]


def sum_quarter(bits, mine, got, half, last, after, vec=()):
    rows, d = mine.shape[2:]

    def kernel(bits_ref, mine_ref, got_ref, half_ref, *refs):
        *refs, out_ref = refs
        first = bits_ref[0]
        at = bits_ref[1] if last else 1 - bits_ref[1]
        terms = [mine_ref[first, at], got_ref[first, at], half_ref[at]]
        out_ref[:rows] = plus(*terms, *(ref[...] for ref in refs[: len(last)]))
        if vec:
            a, b = refs[-2][...].astype(F32), refs[-1][...].astype(F32)
            shard = vec[2]
            turned = jnp.concatenate([b[:, shard : 2 * shard], b[:, :shard], b[:, 2 * shard :]], axis=1)
            same = lax.broadcasted_iota(jnp.int32, a.shape, 0) < 4
            out_ref[rows:] = plus(a, jnp.where(same, b, turned))

    args = (bits, mine, got, half, *last, *vec[:2])
    return call(
        kernel, "sum_quarter", args, [bf16(rows + (16 if vec else 0), d)], rows * d * 4, scalars=1,
        after=after, limit=8,
    )[0]


def sum_two(a, b, after):
    def kernel(a_ref, b_ref, out_ref):
        out_ref[...] = a_ref[...] + b_ref[...]

    return call(kernel, "sum_two", (a, b), [bf16(*a.shape)], a.size, after=after, limit=8)[0]


def side_by_side(mine, got, rows, after):
    extra = mine.shape[0] - rows

    def kernel(mine_ref, got_ref, out_ref):
        out_ref[:rows] = mine_ref[:rows]
        out_ref[rows : 2 * rows] = got_ref[:rows]
        if extra:
            out_ref[2 * rows :] = mine_ref[rows:] + got_ref[rows:]

    return call(
        kernel, "side_by_side", (mine, got), [bf16(2 * rows + extra, mine.shape[1])], after=after, limit=8
    )[0]


def place_sums(bits, mine, got, rows, outs, vec, after):
    d = mine.shape[1]

    def kernel(bits_ref, mine_ref, got_ref, *refs):
        out_refs, vec_refs = refs[: len(outs)], refs[len(outs) : -2]
        all_ref, sems = refs[-2:]
        for at, ref in enumerate((mine_ref, got_ref)):
            half = bits_ref[0] if at == 0 else 1 - bits_ref[0]
            for part in range(2):
                quarter = bits_ref[1] if part == 0 else 1 - bits_ref[1]
                start = pl.multiple_of((2 * half + quarter) * rows, 16)
                all_ref[pl.ds(start, rows), :] = ref[part * rows : (part + 1) * rows].astype(F32)
        pairs, start = [], 0
        for ref in out_refs:
            flat = ref if len(ref.shape) == 2 else None
            if flat is not None:
                pairs.append((all_ref.at[start : start + ref.shape[0]], ref))
                start += ref.shape[0]
            else:
                for c in range(ref.shape[0]):
                    pairs.append((all_ref.at[start : start + ref.shape[1]], ref.at[c]))
                    start += ref.shape[1]
        started = copies(sems, pairs)
        if vec:
            total = mine_ref[2 * rows :].astype(F32) + got_ref[2 * rows :].astype(F32)
            for at, (n, ref) in enumerate(zip(vec, vec_refs)):
                ref[...] = total[at, :n]
        finish(started)

    return call(
        kernel, "place_sums", (bits, mine, got), [*outs, *(f32(n) for n in vec)], 4 * rows * d, scalars=1,
        direct=range(len(outs)), after=after, limit=8,
        scratch=[pltpu.VMEM((4 * rows, d), F32), pltpu.SemaphoreType.DMA((3,))],
    )


def local(
    n_dp, n_tensor, tokens, node_counts, edge_counts, ln1_gain, ln1_bias, qkv_weight, out_weight,
    ln2_gain, ln2_bias, fc1_weight, fc1_bias, fc2_weight, out_grad,
):
    d = tokens.shape[1]
    shard = out_weight.shape[0]
    mols = tokens.shape[0] // LEN
    dp_at = lax.axis_index("dp")
    tensor_at = lax.axis_index("tensor")
    core = tensor_at % 2
    bit0 = dp_at % 2
    bit1 = (dp_at // 2 + dp_at // 4) % 2
    bits = jnp.stack([jnp.where(core == 0, bit0, bit1), jnp.where(core == 0, bit1, bit0)])
    bits = bits.astype(jnp.int32)
    scalar = lambda v: v.reshape(1).astype(jnp.int32)

    def swap_core(a):
        return lax.ppermute(a, "tensor", [(t, t ^ 1) for t in range(n_tensor)])

    def swap_y(a):
        return lax.ppermute(a, "tensor", [(t, t ^ 2) for t in range(n_tensor)])

    def swap_dp(a, mask0, mask1):
        pairs = [
            (p * n_tensor + t, (p ^ (mask1 if t % 2 else mask0)) * n_tensor + t)
            for p in range(n_dp)
            for t in range(n_tensor)
        ]
        return lax.ppermute(a, ("dp", "tensor"), pairs)

    swap_first = lambda a: swap_dp(a, 1, 2)
    swap_second = lambda a: swap_dp(a, 2, 1)
    far_masks = [6 if k == 2 else 1 << k for k in range(2, n_dp.bit_length() - 1)]

    x_got = swap_y(tokens)
    far_y = swap_y(jnp.where(bit0 == 0, out_weight, fc1_weight))
    bias = jnp.concatenate([fc1_bias, swap_core(fc1_bias)]).astype(F32).reshape(1, -1)

    place = lambda t: scalar(t * mols)
    counts = (node_counts, edge_counts)
    a1_0, qt_0, kt_0, v_0, p_0, ot_0, packet, w_qkv = attention_first(
        place(tensor_at), *counts, tokens, ln1_gain, ln1_bias, qkv_weight, swap_core(qkv_weight), out_grad
    )
    packet_got = swap_y(packet)
    far_y = hold(far_y, (a1_0,))
    far_x = swap_dp(far_y, 1, 1)
    a1_1, qt_1, kt_1, v_1, p_1, ot_1, o_1 = attention_second(
        place(tensor_at ^ 2), *counts, x_got, ln1_gain, ln1_bias, w_qkv, (a1_0,)
    )
    o_got = swap_y(o_1)
    wo, fc1, fc2 = pack_rest(
        scalar(bit0), out_weight, swap_core(out_weight), fc1_weight, swap_core(fc1_weight),
        fc2_weight, swap_core(fc2_weight), far_y, swap_core(far_y), far_x, swap_core(far_x),
    )

    ffn = (wo, ln2_gain, ln2_bias, fc1, bias, fc2)
    h_1, a2_1, z_1, du_1 = feed(x_got, o_1, packet_got, *ffn)
    dr_0 = swap_y(du_1)
    h_0, a2_0, z_0, du_0 = feed(tokens, packet, (out_grad, o_got), *ffn, after=(du_1,))
    dr_1 = swap_y(du_0)

    gh_0, dp_0, dh, sums = backward(
        (du_0, dr_0, fc1, h_0, out_grad, ln2_gain, wo, p_0, qt_0, kt_0, v_0), True
    )
    keep_fc, send_fc, bias_sums = feed_grads(
        (z_0, z_1), (du_0, du_1), (a2_0, a2_1), (out_grad, packet_got), (gh_0,)
    )
    gh_1, dp_1 = backward(
        (du_1, dr_1, fc1, h_1, packet_got, ln2_gain, wo, p_1, qt_1, kt_1, v_1), False, (keep_fc,)
    )

    keep_r, send_r = out_grads((ot_0, ot_1), (gh_0, gh_1), keep_fc, send_fc)
    got_r = swap_core(send_r)
    keep_q, send_q = qkv_grads((dp_0, dp_1), (a1_0, a1_1), (keep_r,))
    got_q = swap_core(send_q)
    half = lambda a: a.reshape(2, -1, d)
    size = 3 * shard // 4
    quarters = lambda a: a.reshape(2, 2, size, d)
    two = lambda a: a.reshape(2, size, d)

    send1_r = sum_half(bits, half(keep_r), half(got_r), (keep_q,))
    got1_r = swap_first(send1_r)
    send1_q = sum_half(bits, half(keep_q), half(got_q), (send1_r,))
    got1_q = swap_first(send1_q)
    da1_mine, da1_theirs = input_grads(
        (dp_0, dp_1), w_qkv, (tokens, x_got), sums, bias_sums, (send1_q,)
    )
    da1_got = swap_y(da1_theirs)
    view_r = (quarters(keep_r), quarters(got_r), two(got1_r))
    view_q = (quarters(keep_q), quarters(got_q), two(got1_q))
    send2_r = sum_quarter(bits, *view_r, (), (da1_theirs,))
    got2_r = swap_second(send2_r)
    res_mine, res_theirs = feed_result((z_0, z_1), fc2, h_0, (send2_r,))
    send2_q = sum_quarter(bits, *view_q, (), (send2_r,))
    got2_q = swap_second(send2_q)
    res_got = swap_y(res_theirs)
    s_r = sum_quarter(bits, *view_r, (got2_r,), (send2_q,))
    got3_r = swap_dp(s_r, far_masks[0], far_masks[0])
    vec = vector_rows(da1_theirs, da1_got, (s_r,))
    s_q = sum_quarter(bits, *view_q, (got2_q,), (s_r,), (vec, swap_core(vec), shard))
    got3_q = swap_dp(s_q, far_masks[0], far_masks[0])
    s_r = sum_two(s_r, got3_r, (s_q,))
    for mask in far_masks[1:]:
        s_r = sum_two(s_r, swap_dp(s_r, mask, mask), ())
    got4_r = swap_second(s_r)
    grad_tokens = input_norm(tokens, ln1_gain, da1_mine, da1_got, dh, (s_r,))
    s_q = sum_two(s_q, got3_q, (s_r,))
    for mask in far_masks[1:]:
        s_q = sum_two(s_q, swap_dp(s_q, mask, mask), ())
    got4_q = swap_second(s_q)
    both_r = side_by_side(s_r, got4_r, size, (s_q,))
    got5_r = swap_first(both_r)
    result = add_result(res_mine, res_got, (both_r,))
    both_q = side_by_side(s_q, got4_q, size, (both_r,))
    got5_q = swap_first(both_q)
    rows = f32(shard, d)
    grad_fc1, grad_fc2, grad_out = place_sums(bits, both_r, got5_r, size, [rows] * 3, (), (both_q,))
    grad_qkv, gain1, bias1, gain2, bias2, grad_b = place_sums(
        bits, both_q, got5_q, size, [f32(3, shard, d)], (d, d, d, d, shard), (grad_fc1,)
    )
    return (
        result, grad_tokens, gain1, bias1, grad_qkv, grad_out, gain2, bias2, grad_fc1, grad_b, grad_fc2,
    )


def solution(mesh):
    tokens = P(("dp", "tensor"), None)
    rows = P("tensor", None)
    qkv = P(None, "tensor", None)
    in_specs = (
        tokens, P("dp"), P("dp"), P(), P(), qkv, rows, P(), P(), rows, P("tensor"), rows, tokens,
    )
    out_specs = (tokens, tokens, P(), P(), qkv, rows, P(), P(), rows, P("tensor"), rows)
    step = functools.partial(local, mesh.shape["dp"], mesh.shape["tensor"])
    return jax.shard_map(step, mesh=mesh, in_specs=in_specs, out_specs=out_specs, check_vma=False)
```

time: 153 us -> 132 us (0.86)
  waiting for transfers between devices: 69.5 us -> 41.2 us
  Pallas kernels: 27.8 us -> 33.8 us
  starting transfers between devices: 34.2 us -> 37.4 us
  other arithmetic: 4.15 us -> 1.86 us
    ppermute x9 -> x8, waiting for transfers between devices: 29.8 us -> 9.22 us  [swap_y(): return lax.ppermute(a, 'tensor', [(t, t ^ 2) for t in range(n_tensor)])]
    ppermute x11, waiting for transfers between devices: 38.5 us -> 30.3 us  [swap_dp(): return lax.ppermute(a, ('dp', 'tensor'), pairs)]
    pallas_call x25 -> x28, Pallas kernels: 27.8 us -> 33.8 us  [call(): pl.pallas_call(body, in_specs=[smem if j < scalars else anywhere if j in...]
    ppermute x11, starting transfers between devices: 20.5 us -> 23.7 us  [swap_dp(): return lax.ppermute(a, ('dp', 'tensor'), pairs)]
    unnamed x72 -> x110, local copies, waits for them, and re-layouts: 11.3 us -> 13.9 us
    concatenate x5 -> x0, other arithmetic: 2.07 us -> none  [the longest x1 1.01 us: local(): jnp.concatenate([send_fc, send_out], axis=0)]
    concatenate x2, local copies, waits for them, and re-layouts: 0.01 us -> 1.84 us  [local(): jnp.concatenate([fc1_bias, swap_core(fc1_bias)]).astype(F32).reshape(1, -1)]
    ppermute x9 -> x8, starting transfers between devices: 11.5 us -> 11.6 us  [swap_y(): return lax.ppermute(a, 'tensor', [(t, t ^ 2) for t in range(n_tensor)])]
  transfers between devices with their start and end apart: 30 -> 29, of which waited for: 13 -> 13; matrix products, arithmetic and copies ran while one was open for 4% -> 3% of each run, Pallas kernels for 16% -> 20%
where the time goes in v3:
time: 132 us; the launch traced here: 131 us
  waiting for transfers between devices  41.2 us (31%)
  starting transfers between devices  37.4 us (28%)
  Pallas kernels  33.8 us (26%)
  local copies, waits for them, and re-layouts  15.7 us (12%)
  other arithmetic  1.86 us (1%)
  between operations  1.43 us (1%)
    pallas_call x28, Pallas kernels, call(): pl.pallas_call(body, in_specs=[smem if j < scalars else anywhere if j in...  33.8 us
    ppermute x11, waiting for transfers between devices, swap_dp(): return lax.ppermute(a, ('dp', 'tensor'), pairs)  30.3 us
    ppermute x11, starting transfers between devices, swap_dp(): return lax.ppermute(a, ('dp', 'tensor'), pairs)  23.7 us
    unnamed x110, local copies, waits for them, and re-layouts  13.9 us
    ppermute x8, starting transfers between devices, swap_y(): return lax.ppermute(a, 'tensor', [(t, t ^ 2) for t in range(n_tensor)])  11.6 us
    ppermute x8, waiting for transfers between devices, swap_y(): return lax.ppermute(a, 'tensor', [(t, t ^ 2) for t in range(n_tensor)])  9.22 us
  transfers between devices with their start and end apart: 29, of which 13 were waited for; matrix products, arithmetic and copies ran while one was open for 3% of the time, Pallas kernels for 20%

profile of v3, /device:TPU:0, one launch (start us, length us, event | category | flops | bytes accessed | tf_op | source)
XLA Modules:
  0.0 131.4 jit_solution(6202315039379344251)
XLA Ops:
  1.2 1.7 %broadcast_select_fusion = bf16[192,768]{1,0:T(8,128)(2,1)} fusion(bf16[192,768]{1,0:T(8,128)(2,1)} %refs_1_.6, bf16[192,768]{1,0:T(8,128)(2,1)} %refs_3_.4, pred[]{:T(512)S(6)} %eq.11), kind=kLoop, calls=%fused_computation | loop fusion | flops 147456 | bytes 884737 | tf_op jit(solution)/shard_map/jit(_where)/select_n | solution.py:587
  2.9 2.6 %collective-permute-start.6 = (bf16[192,768]{1,0:T(8,128)(2,1)}, bf16[192,768]{1,0:T(8,128)(2,1)S(1)}, u32[]{:S(2)}, u32[]{:S(2)}) collective-permute-start(bf16[192,768]{1,0:T(8,128)(2,1)} %broadcast_select_fusion), channel_id=1, source_target_pairs={{0,2},{1,3},{2,0},{3,1},{4,6},{5,7},{6,4},{7,5},{8,10},{9,11},{10,... | collective-permute-start | bytes 884744 | tf_op jit(solution)/shard_map/ppermute | solution.py:572
  5.7 0.9 copy-done.45
  6.6 1.0 copy-done.2
  7.6 1.0 copy-done.4
  9.2 1.2 copy-done.44
  10.4 1.2 copy-done.46
  13.6 3.8 %attention_first.1 = (bf16[256,768]{1,0:T(8,128)(2,1)S(1)}, bf16[384,256]{1,0:T(8,128)(2,1)S(1)}, bf16[384,256]{1,0:T(8,128)(2,1)S(1)}, bf16[256,384]{1,0:T(8,12...) custom-call(s32[1]{0:T(128)} %bitcast.refs_0_, ...), custom_call_target="tpu_custom_call" | custom-call | flops 855638016 | bytes 7149636 | tf_op jit(solution)/shard_map/attention_first/pallas_call | solution.py:84
  17.4 1.0 copy-done.15
  20.4 0.9 hold.1.refs_7_
  22.1 1.8 %collective-permute-start.8 = (bf16[192,768]{1,0:T(8,128)(2,1)}, bf16[192,768]{1,0:T(8,128)(2,1)}, u32[]{:S(2)}, u32[]{:S(2)}) collective-permute-start(bf16[192,768]{1,0:T(8,128)(2,1)} %hold.1.refs_7_), channel_id=1, source_target_pairs={{0,4},{1,5},{2,6},{3,7},{4,0},{5,1},{6,2},{7,3},{8,12},{9,13},{10,... | collective-permute-start | bytes 884744 | tf_op jit(solution)/shard_map/ppermute | solution.py:580
  23.8 1.5 %collective-permute-start.11 = (bf16[256,1152]{1,0:T(8,128)(2,1)}, bf16[256,1152]{1,0:T(8,128)(2,1)S(1)}, u32[]{:S(2)}, u32[]{:S(2)}) collective-permute-start(bf16[256,1152]{1,0:T(8,128)(2,1)} %get-tuple-element.63.refs_1_), channel_id=1, source_target_pairs={{0,2},{1,3},{2,0},{3,1},{4,6},{5,7},{6,4},{7,5},{8,10},{9,11},{10,... | collective-permute-start | bytes 1769480 | tf_op jit(solution)/shard_map/ppermute | solution.py:572
  25.4 1.2 collective-permute-done.10
  27.3 4.5 %collective-permute-done.8.refs_9_ = bf16[192,768]{1,0:T(8,128)(2,1)} collective-permute-done((bf16[192,768]{1,0:T(8,128)(2,1)}, bf16[192,768]{1,0:T(8,128)(2,1)}, u32[]{:S(2)}, u32[]{:S(2)}) %collective-permute-start.8) | collective-permute-done | bytes 294944 | tf_op jit(solution)/shard_map/ppermute | solution.py:580
  31.8 1.2 concatenate.14
  33.7 1.0 copy-done.29
  34.7 2.7 %attention_second.1 = (bf16[256,768]{1,0:T(8,128)(2,1)S(1)}, bf16[384,256]{1,0:T(8,128)(2,1)S(1)}, bf16[384,256]{1,0:T(8,128)(2,1)S(1)}, bf16[256,384]{1,0:T(8,1...) custom-call(s32[1]{0:T(128)} %bitcast.1.refs_0_, ...), custom_call_target="tpu_custom_call" | custom-call | flops 855638016 | bytes 4593732 | tf_op jit(solution)/shard_map/attention_second/pallas_call | solution.py:84
  37.4 1.8 %collective-permute-start.2 = (bf16[256,384]{1,0:T(8,128)(2,1)S(1)}, bf16[256,384]{1,0:T(8,128)(2,1)S(1)}, u32[]{:S(2)}, u32[]{:S(2)}) collective-permute-start(bf16[256,384]{1,0:T(8,128)(2,1)S(1)} %get-tuple-element.66.refs_1_), channel_id=1, source_target_pairs={{0,2},{1,3},{2,0},{3,1},{4,6},{5,7},{6,4},{7,5},{8,10},{9,11},{10,... | collective-permute-start | bytes 589832 | tf_op jit(solution)/shard_map/ppermute | solution.py:572
  39.3 1.8 %pack_rest.1 = (bf16[768,768]{1,0:T(8,128)(2,1)S(1)}, bf16[768,768]{1,0:T(8,128)(2,1)S(1)}, bf16[384,768]{1,0:T(8,128)(2,1)S(1)}) custom-call(s32[1]{0:T(128)} %bitcast.2.refs_0_, bf16[192,768]{1,0:T(8,128)(2,1)S(1)} %copy-done.13, bf16[192,768]{1,0:T(8,128)(2,1)} %collective-permute-done.3.refs_2_, bf16[192,768]{1,0:T(8,128)(2,1)S(1)} %copy-done.14, ...), custom_call_target="tpu_custom_call" | custom-call | bytes 5898244 | tf_op jit(solution)/shard_map/pack_rest/pallas_call | solution.py:84
  41.3 1.2 feed_forward.2
  42.9 2.0 %collective-permute-done.2.refs_3_ = bf16[256,384]{1,0:T(8,128)(2,1)S(1)} collective-permute-done((bf16[256,384]{1,0:T(8,128)(2,1)S(1)}, bf16[256,384]{1,0:T(8,128)(2,1)S(1)}, u32[]{:S(2)}, u32[]{:S(2)}) %collective-permute-start.2) | collective-permute-done | bytes 196640 | tf_op jit(solution)/shard_map/ppermute | solution.py:572
  44.8 2.3 %feed_forward.3 = (f32[256,768]{1,0:T(8,128)S(1)}, bf16[256,768]{1,0:T(8,128)(2,1)S(1)}, bf16[256,384]{1,0:T(8,128)(2,1)S(1)}, bf16[256,384]{1,0:T(8,128)(2,1)S(1)}) custom-call(bf16[256,768]{1,0:T(8,128)(2,1)S(1)} %copy-done.5, bf16[256,1152]{1,0:T(8,128)(2,1)} %get-tuple-element.63.refs_1_, bf16[256,768]{1,0:T(8,128)(2,1)S(1)} %copy-done.3, ...), custom_call_target="tpu_custom_call" | custom-call | flops 603979776 | bytes 6102528 | tf_op jit(solution)/shard_map/feed_forward/pallas_call | solution.py:84
  47.2 2.2 %collective-permute-start.13 = (bf16[256,384]{1,0:T(8,128)(2,1)S(1)}, bf16[256,384]{1,0:T(8,128)(2,1)S(1)}, u32[]{:S(2)}, u32[]{:S(2)}) collective-permute-start(bf16[256,384]{1,0:T(8,128)(2,1)S(1)} %get-tuple-element.76.refs_0_.refs_2_), channel_id=1, source_target_pairs={{0,2},{1,3},{2,0},{3,1},{4,6},{5,7},{6,4},{7,5},{8,10},{9,11},{10,... | collective-permute-start | bytes 589832 | tf_op jit(solution)/shard_map/ppermute | solution.py:572
  49.6 2.4 %attention_backward.2 = (bf16[256,768]{1,0:T(8,128)(2,1)S(1)}, bf16[1152,256]{1,0:T(8,128)(2,1)S(1)}, f32[256,768]{1,0:T(8,128)S(1)}, f32[8,768]{1,0:T(8,128)S(1)}) custom-call(bf16[256,384]{1,0:T(8,128)(2,1)S(1)} %get-tuple-element.76.refs_0_.refs_2_, bf16[256,384]{1,0:T(8,128)(2,1)S(1)} %collective-permute-done.12.refs_1_, ...), custom_call_target="tpu_custom_call" | custom-call | flops 654311424 | bytes 7367680 | tf_op jit(solution)/shard_map/attention_backward/pallas_call | solution.py:84
  53.0 0.9 collective-permute-done.13.refs_1_
  53.9 2.4 %attention_backward.3 = (bf16[256,768]{1,0:T(8,128)(2,1)S(1)}, bf16[1152,256]{1,0:T(8,128)(2,1)S(1)}) custom-call(bf16[256,384]{1,0:T(8,128)(2,1)S(1)} %get-tuple-element.70.refs_10_.refs_3_.refs_0_, bf16[256,384]{1,0:T(8,128)(2,1)S(1)} %collective-permute-done.13.refs_1_, bf16[768,768]{1,0:T(8,128)(2,1)S(1)} %get-tuple-element.68.refs_6_.refs_7_.refs_2_, ...), custom_call_target="tpu_custom_call" | custom-call | flops 654311424 | bytes 6753280 | tf_op jit(solution)/shard_map/attention_backward/pallas_call | solution.py:84
  56.3 1.4 %out_grads.1 = (bf16[3,192,768]{2,1,0:T(8,128)(2,1)S(1)}, bf16[3,192,768]{2,1,0:T(8,128)(2,1)}) custom-call(bf16[384,256]{1,0:T(8,128)(2,1)S(1)} %copy-done.37, bf16[384,256]{1,0:T(8,128)(2,1)S(1)} %get-tuple-element.75.refs_1_, bf16[256,768]{1,0:T(8,128)(2,1)S(1)} %get-tuple-element.81.refs_8_.refs_2_, bf16[256,768]{1,0:T(8,128)(2,1)S(1)} %get-tuple-element.90.refs_3_, ...), custom_call_target="tpu_custom_call" | custom-call | flops 301989888 | bytes 4128768 | tf_op jit(solution)/shard_map/out_grads/pallas_call | solution.py:84
  57.7 1.6 %qkv_grads.1 = (bf16[3,192,768]{2,1,0:T(8,128)(2,1)S(1)}, bf16[3,192,768]{2,1,0:T(8,128)(2,1)}) custom-call(bf16[1152,256]{1,0:T(8,128)(2,1)S(1)} %get-tuple-element.94.refs_0_, bf16[1152,256]{1,0:T(8,128)(2,1)S(1)} %get-tuple-element.95.refs_1_, bf16[256,768]{1,0:T(8,128)(2,1)S(1)} %copy-done.30, bf16[256,768]{1,0:T(8,128)(2,1)S(1)} %get-tuple-element.96.refs_3_, ...), custom_call_target="tpu_custom_call" | custom-call | flops 905969664 | bytes 3735552 | tf_op jit(solution)/shard_map/qkv_grads/pallas_call | solution.py:84
  61.0 1.7 %collective-permute-start.15 = (bf16[288,768]{1,0:T(8,128)(2,1)S(1)}, bf16[288,768]{1,0:T(8,128)(2,1)S(1)}, u32[]{:S(2)}, u32[]{:S(2)}) collective-permute-start(bf16[288,768]{1,0:T(8,128)(2,1)S(1)} %sum_half.2.refs_3_), channel_id=1, source_target_pairs={{0,4},{1,9},{2,6},{3,11},{4,0},{5,13},{6,2},{7,15},{8,12},{9,1},{1... | collective-permute-start | bytes 1327112 | tf_op jit(solution)/shard_map/ppermute | solution.py:580
  63.3 1.1 collective-permute-start.19
  64.4 1.3 %input_grads.1 = (f32[256,768]{1,0:T(8,128)S(1)}, bf16[272,768]{1,0:T(8,128)(2,1)S(1)}) custom-call(bf16[1152,256]{1,0:T(8,128)(2,1)S(1)} %copy-done.24, bf16[1152,256]{1,0:T(8,128)(2,1)S(1)} %copy-done.26, bf16[3,384,768]{2,1,0:T(8,128)(2,1)S(1)} %copy-done.10, bf16[256,768]{1,0:T(8,128)(2,1)S(1)} %copy-done.6, bf16[256,768]{1,0:T(8,128)(2,1)S(1)} %copy-done.12, ...), custom_call_target="tpu_custom_call" | custom-call | flops 905969664 | bytes 4965888 | tf_op jit(solution)/shard_map/input_grads/pallas_call | solution.py:84
  65.8 1.6 %collective-permute-start.22 = (bf16[272,768]{1,0:T(8,128)(2,1)S(1)}, bf16[272,768]{1,0:T(8,128)(2,1)S(1)}, u32[]{:S(2)}, u32[]{:S(2)}) collective-permute-start(bf16[272,768]{1,0:T(8,128)(2,1)S(1)} %get-tuple-element.101.refs_4_.refs_0_), channel_id=1, source_target_pairs={{0,2},{1,3},{2,0},{3,1},{4,6},{5,7},{6,4},{7,5},{8,10},{9,11},{10,... | collective-permute-start | bytes 1253384 | tf_op jit(solution)/shard_map/ppermute | solution.py:572
  67.4 2.0 %collective-permute-done.15 = bf16[288,768]{1,0:T(8,128)(2,1)S(1)} collective-permute-done((bf16[288,768]{1,0:T(8,128)(2,1)S(1)}, bf16[288,768]{1,0:T(8,128)(2,1)S(1)}, u32[]{:S(2)}, u32[]{:S(2)}) %collective-permute-start.15) | collective-permute-done | bytes 442400 | tf_op jit(solution)/shard_map/ppermute | solution.py:580
  70.0 1.8 %collective-permute-start.18 = (bf16[144,768]{1,0:T(8,128)(2,1)S(1)}, bf16[144,768]{1,0:T(8,128)(2,1)S(1)}, u32[]{:S(2)}, u32[]{:S(2)}) collective-permute-start(bf16[144,768]{1,0:T(8,128)(2,1)S(1)} %sum_quarter.4.refs_4_), channel_id=1, source_target_pairs={{0,8},{1,5},{2,10},{3,7},{4,12},{5,1},{6,14},{7,3},{8,0},{9,13},{1... | collective-permute-start | bytes 663560 | tf_op jit(solution)/shard_map/ppermute | solution.py:580
  71.8 4.4 %collective-permute-done.19 = bf16[288,768]{1,0:T(8,128)(2,1)S(1)} collective-permute-done((bf16[288,768]{1,0:T(8,128)(2,1)S(1)}, bf16[288,768]{1,0:T(8,128)(2,1)S(1)}, u32[]{:S(2)}, u32[]{:S(2)}) %collective-permute-start.19) | collective-permute-done | bytes 442400 | tf_op jit(solution)/shard_map/ppermute | solution.py:580
  76.9 1.8 %collective-permute-start.21 = (bf16[144,768]{1,0:T(8,128)(2,1)S(1)}, bf16[144,768]{1,0:T(8,128)(2,1)S(1)}, u32[]{:S(2)}, u32[]{:S(2)}) collective-permute-start(bf16[144,768]{1,0:T(8,128)(2,1)S(1)} %sum_quarter.5.refs_5_), channel_id=1, source_target_pairs={{0,8},{1,5},{2,10},{3,7},{4,12},{5,1},{6,14},{7,3},{8,0},{9,13},{1... | collective-permute-start | bytes 663560 | tf_op jit(solution)/shard_map/ppermute | solution.py:580
  79.4 3.4 %collective-permute-done.21.refs_4_ = bf16[144,768]{1,0:T(8,128)(2,1)S(1)} collective-permute-done((bf16[144,768]{1,0:T(8,128)(2,1)S(1)}, bf16[144,768]{1,0:T(8,128)(2,1)S(1)}, u32[]{:S(2)}, u32[]{:S(2)}) %collective-permute-start.21) | collective-permute-done | bytes 221216 | tf_op jit(solution)/shard_map/ppermute | solution.py:580
  83.6 3.8 %collective-permute-start.25 = (bf16[160,768]{1,0:T(8,128)(2,1)S(1)}, bf16[160,768]{1,0:T(8,128)(2,1)S(1)}, u32[]{:S(2)}, u32[]{:S(2)}) collective-permute-start(bf16[160,768]{1,0:T(8,128)(2,1)S(1)} %sum_quarter.7.refs_2_.refs_0_), channel_id=1, source_target_pairs={{0,24},{1,25},{2,26},{3,27},{4,28},{5,29},{6,30},{7,31},{8,16},{9,... | collective-permute-start | bytes 737288 | tf_op jit(solution)/shard_map/ppermute | solution.py:580
  87.5 8.6 %collective-permute-done.20.refs_1_ = bf16[144,768]{1,0:T(8,128)(2,1)S(1)} collective-permute-done((bf16[144,768]{1,0:T(8,128)(2,1)S(1)}, bf16[144,768]{1,0:T(8,128)(2,1)S(1)}, u32[]{:S(2)}, u32[]{:S(2)}) %collective-permute-start.20) | collective-permute-done | bytes 221216 | tf_op jit(solution)/shard_map/ppermute | solution.py:580
  96.2 9.6 %collective-permute-start.26 = (bf16[160,768]{1,0:T(8,128)(2,1)S(1)}, bf16[160,768]{1,0:T(8,128)(2,1)S(1)}, u32[]{:S(2)}, u32[]{:S(2)}) collective-permute-start(bf16[160,768]{1,0:T(8,128)(2,1)S(1)} %sum_two.3.refs_2_.refs_0_), channel_id=1, source_target_pairs={{0,8},{1,5},{2,10},{3,7},{4,12},{5,1},{6,14},{7,3},{8,0},{9,13},{1... | collective-permute-start | bytes 737288 | tf_op jit(solution)/shard_map/ppermute | solution.py:580
  105.8 6.5 %collective-permute-done.24.refs_1_ = bf16[144,768]{1,0:T(8,128)(2,1)S(1)} collective-permute-done((bf16[144,768]{1,0:T(8,128)(2,1)S(1)}, bf16[144,768]{1,0:T(8,128)(2,1)S(1)}, u32[]{:S(2)}, u32[]{:S(2)}) %collective-permute-start.24) | collective-permute-done | bytes 221216 | tf_op jit(solution)/shard_map/ppermute | solution.py:580
  112.4 1.6 %collective-permute-start.27 = (bf16[304,768]{1,0:T(8,128)(2,1)S(1)}, bf16[304,768]{1,0:T(8,128)(2,1)S(1)}, u32[]{:S(2)}, u32[]{:S(2)}) collective-permute-start(bf16[304,768]{1,0:T(8,128)(2,1)S(1)} %side_by_side.3.refs_3_.refs_1_), channel_id=1, source_target_pairs={{0,4},{1,9},{2,6},{3,11},{4,0},{5,13},{6,2},{7,15},{8,12},{9,1},{1... | collective-permute-start | bytes 1400840 | tf_op jit(solution)/shard_map/ppermute | solution.py:580
  115.1 1.6 %collective-permute-start.17 = (bf16[256,768]{1,0:T(8,128)(2,1)S(1)}, bf16[256,768]{1,0:T(8,128)(2,1)S(1)}, u32[]{:S(2)}, u32[]{:S(2)}) collective-permute-start(bf16[256,768]{1,0:T(8,128)(2,1)S(1)} %get-tuple-element.103), channel_id=1, source_target_pairs={{0,2},{1,3},{2,0},{3,1},{4,6},{5,7},{6,4},{7,5},{8,10},{9,11},{10,... | collective-permute-start | bytes 1179656 | tf_op jit(solution)/shard_map/ppermute | solution.py:572
  116.7 1.3 %input_norm.1 = bf16[256,768]{1,0:T(8,128)(2,1)} custom-call(bf16[256,768]{1,0:T(8,128)(2,1)S(1)} %copy-done.6, f32[768]{0:T(1024)S(1)} %copy-done.43, f32[256,768]{1,0:T(8,128)S(1)} %get-tuple-element.104.refs_2_, bf16[272,768]{1,0:T(8,128)(2,1)S(1)} %collective-permute-done.22.refs_1_.refs_3_, f32[256,768]{1,0:T(8,128)S(1)} %copy-done.18, ...), custom_call_target="tpu_custom_call" | custom-call | flops 3932160 | bytes 2780160 | tf_op jit(solution)/shard_map/input_norm/pallas_call | solution.py:84
  118.0 6.1 %collective-permute-done.17.refs_1_ = bf16[256,768]{1,0:T(8,128)(2,1)S(1)} collective-permute-done((bf16[256,768]{1,0:T(8,128)(2,1)S(1)}, bf16[256,768]{1,0:T(8,128)(2,1)S(1)}, u32[]{:S(2)}, u32[]{:S(2)}) %collective-permute-start.17) | collective-permute-done | bytes 393248 | tf_op jit(solution)/shard_map/ppermute | solution.py:572
  125.8 1.9 %place_sums.2 = (f32[192,768]{1,0:T(8,128)}, f32[192,768]{1,0:T(8,128)}, f32[192,768]{1,0:T(8,128)}) custom-call(s32[2]{0:T(128)S(1)} %pad_add_fusion.refs_0_, bf16[288,768]{1,0:T(8,128)(2,1)S(1)} %side_by_side.2.refs_2_.refs_1_, bf16[288,768]{1,0:T(8,128)(2,1)S(1)} %collective-permute-done.28.refs_2_, bf16[304,768]{1,0:T(8,128)(2,1)S(1)} %side_by_side.3.refs_3_.refs_1_), custom_call_target="tpu_custom_call" | custom-call | flops 442368 | bytes 2654216 | tf_op jit(solution)/shard_map/place_sums/pallas_call | solution.py:84
  127.7 1.1 copy-done.27
  128.7 2.5 %place_sums.3 = (f32[3,192,768]{2,1,0:T(8,128)}, f32[768]{0:T(1024)}, f32[768]{0:T(1024)}, f32[768]{0:T(1024)}, f32[768]{0:T(1024)}, /*index=5*/f32[192]{0:T(256)}) custom-call(s32[2]{0:T(128)S(1)} %pad_add_fusion.refs_0_, bf16[304,768]{1,0:T(8,128)(2,1)S(1)} %side_by_side.3.refs_3_.refs_1_, bf16[304,768]{1,0:T(8,128)(2,1)S(1)} %collective-permute-done.27.refs_2_, ...), custom_call_target="tpu_custom_call" | custom-call | flops 442368 | bytes 2716424 | tf_op jit(solution)/shard_map/place_sums/pallas_call | solution.py:84
  (153 shorter events, 17.3 us)
Async XLA Ops:
  0.6 5.0 %collective-permute-start = (bf16[3,192,768]{2,1,0:T(8,128)(2,1)}, bf16[3,192,768]{2,1,0:T(8,128)(2,1)S(1)}, u32[]{:S(2)}, u32[]{:S(2)}) collective-permute-start(bf16[3,192,768]{2,1,0:T(8,128)(2,1)} %refs_6_.3), channel_id=1, source_target_pairs={{0,1},{1,0},{2,3},{3,2},{4,5},{5,4},{6,7},{7,6},{8,9},{9,8},{10,11... | collective-permute-start | bytes 2654216 | tf_op jit(solution)/shard_map/ppermute | solution.py:569
  2.9 17.6 %collective-permute-start.6 = (bf16[192,768]{1,0:T(8,128)(2,1)}, bf16[192,768]{1,0:T(8,128)(2,1)S(1)}, u32[]{:S(2)}, u32[]{:S(2)}) collective-permute-start(bf16[192,768]{1,0:T(8,128)(2,1)} %broadcast_select_fusion), channel_id=1, source_target_pairs={{0,2},{1,3},{2,0},{3,1},{4,6},{5,7},{6,4},{7,5},{8,10},{9,11},{10,... | collective-permute-start | bytes 884744 | tf_op jit(solution)/shard_map/ppermute | solution.py:572
  5.4 21.7 %collective-permute-start.1 = (bf16[256,768]{1,0:T(8,128)(2,1)}, bf16[256,768]{1,0:T(8,128)(2,1)S(1)}, u32[]{:S(2)}, u32[]{:S(2)}) collective-permute-start(bf16[256,768]{1,0:T(8,128)(2,1)} %refs_0_.3), channel_id=1, source_target_pairs={{0,2},{1,3},{2,0},{3,1},{4,6},{5,7},{6,4},{7,5},{8,10},{9,11},{10,... | collective-permute-start | bytes 1179656 | tf_op jit(solution)/shard_map/ppermute | solution.py:572
  5.5 21.4 %collective-permute-start.5 = (bf16[192,768]{1,0:T(8,128)(2,1)}, bf16[192,768]{1,0:T(8,128)(2,1)}, u32[]{:S(2)}, u32[]{:S(2)}) collective-permute-start(bf16[192,768]{1,0:T(8,128)(2,1)} %refs_5_.9), channel_id=1, source_target_pairs={{0,1},{1,0},{2,3},{3,2},{4,5},{5,4},{6,7},{7,6},{8,9},{9,8},{10,11... | collective-permute-start | bytes 884744 | tf_op jit(solution)/shard_map/ppermute | solution.py:569
  13.6 11.8 %copy-start.54 = (bf16[192]{0:T(256)(128)(2,1)S(1)}, bf16[192]{0:T(256)(128)(2,1)}, u32[]{:S(2)}) copy-start(bf16[192]{0:T(256)(128)(2,1)} %param.23) | copy-start | bytes 1156
  13.6 13.0 %copy-start.13 = (bf16[192,768]{1,0:T(8,128)(2,1)S(1)}, bf16[192,768]{1,0:T(8,128)(2,1)}, u32[]{:S(2)}) copy-start(bf16[192,768]{1,0:T(8,128)(2,1)} %refs_1_.6) | copy-start | bytes 884740
  13.6 13.2 %copy-start.14 = (bf16[192,768]{1,0:T(8,128)(2,1)S(1)}, bf16[192,768]{1,0:T(8,128)(2,1)}, u32[]{:S(2)}) copy-start(bf16[192,768]{1,0:T(8,128)(2,1)} %refs_3_.4) | copy-start | bytes 884740
  13.6 20.1 %copy-start.43 = (f32[768]{0:T(1024)S(1)}, f32[768]{0:T(1024)}, u32[]{:S(2)}) copy-start(f32[768]{0:T(1024)} %refs_1_.7) | copy-start | bytes 9220
  13.6 20.1 %copy-start.48 = (f32[768]{0:T(1024)S(1)}, f32[768]{0:T(1024)}, u32[]{:S(2)}) copy-start(f32[768]{0:T(1024)} %refs_5_.8) | copy-start | bytes 9220
  13.6 20.1 %copy-start.50 = (s32[8]{0:T(128)S(1)}, s32[8]{0:T(128)}, u32[]{:S(2)}) copy-start(s32[8]{0:T(128)} %refs_1_.5) | copy-start | bytes 100
  13.6 20.1 %copy-start.52 = (s32[8]{0:T(128)S(1)}, s32[8]{0:T(128)}, u32[]{:S(2)}) copy-start(s32[8]{0:T(128)} %refs_2_.4) | copy-start | bytes 100
  20.4 17.0 %copy-start.9 = (bf16[3,384,768]{2,1,0:T(8,128)(2,1)}, bf16[3,384,768]{2,1,0:T(8,128)(2,1)S(1)}, u32[]{:S(2)}) copy-start(bf16[3,384,768]{2,1,0:T(8,128)(2,1)S(1)} %get-tuple-element.64.refs_6_.refs_2_) | copy-start | bytes 5308420
  22.1 9.8 %collective-permute-start.8 = (bf16[192,768]{1,0:T(8,128)(2,1)}, bf16[192,768]{1,0:T(8,128)(2,1)}, u32[]{:S(2)}, u32[]{:S(2)}) collective-permute-start(bf16[192,768]{1,0:T(8,128)(2,1)} %hold.1.refs_7_), channel_id=1, source_target_pairs={{0,4},{1,5},{2,6},{3,7},{4,0},{5,1},{6,2},{7,3},{8,12},{9,13},{10,... | collective-permute-start | bytes 884744 | tf_op jit(solution)/shard_map/ppermute | solution.py:580
  23.8 17.4 %collective-permute-start.11 = (bf16[256,1152]{1,0:T(8,128)(2,1)}, bf16[256,1152]{1,0:T(8,128)(2,1)S(1)}, u32[]{:S(2)}, u32[]{:S(2)}) collective-permute-start(bf16[256,1152]{1,0:T(8,128)(2,1)} %get-tuple-element.63.refs_1_), channel_id=1, source_target_pairs={{0,2},{1,3},{2,0},{3,1},{4,6},{5,7},{6,4},{7,5},{8,10},{9,11},{10,... | collective-permute-start | bytes 1769480 | tf_op jit(solution)/shard_map/ppermute | solution.py:572
  25.4 1.3 collective-permute-start.10
  26.6 10.8 %collective-permute-start.3 = (bf16[192,768]{1,0:T(8,128)(2,1)S(1)}, bf16[192,768]{1,0:T(8,128)(2,1)}, u32[]{:S(2)}, u32[]{:S(2)}) collective-permute-start(bf16[192,768]{1,0:T(8,128)(2,1)S(1)} %copy-done.13), channel_id=1, source_target_pairs={{0,1},{1,0},{2,3},{3,2},{4,5},{5,4},{6,7},{7,6},{8,9},{9,8},{10,11... | collective-permute-start | bytes 884744 | tf_op jit(solution)/shard_map/ppermute | solution.py:569
  26.8 12.5 %collective-permute-start.4 = (bf16[192,768]{1,0:T(8,128)(2,1)S(1)}, bf16[192,768]{1,0:T(8,128)(2,1)}, u32[]{:S(2)}, u32[]{:S(2)}) collective-permute-start(bf16[192,768]{1,0:T(8,128)(2,1)S(1)} %copy-done.14), channel_id=1, source_target_pairs={{0,1},{1,0},{2,3},{3,2},{4,5},{5,4},{6,7},{7,6},{8,9},{9,8},{10,11... | collective-permute-start | bytes 884744 | tf_op jit(solution)/shard_map/ppermute | solution.py:569
  27.1 14.1 %copy-start.11 = (bf16[256,768]{1,0:T(8,128)(2,1)}, bf16[256,768]{1,0:T(8,128)(2,1)S(1)}, u32[]{:S(2)}) copy-start(bf16[256,768]{1,0:T(8,128)(2,1)S(1)} %collective-permute-done.1.refs_3_.refs_0_.refs_4_) | copy-start | bytes 1179652
  27.1 12.2 %collective-permute-start.7 = (bf16[192,768]{1,0:T(8,128)(2,1)}, bf16[192,768]{1,0:T(8,128)(2,1)}, u32[]{:S(2)}, u32[]{:S(2)}) collective-permute-start(bf16[192,768]{1,0:T(8,128)(2,1)} %hold.1.refs_7_), channel_id=1, source_target_pairs={{0,1},{1,0},{2,3},{3,2},{4,5},{5,4},{6,7},{7,6},{8,9},{9,8},{10,11... | collective-permute-start | bytes 884744 | tf_op jit(solution)/shard_map/ppermute | solution.py:569
  31.8 7.5 %collective-permute-start.9 = (bf16[192,768]{1,0:T(8,128)(2,1)}, bf16[192,768]{1,0:T(8,128)(2,1)}, u32[]{:S(2)}, u32[]{:S(2)}) collective-permute-start(bf16[192,768]{1,0:T(8,128)(2,1)} %collective-permute-done.8.refs_9_), channel_id=1, source_target_pairs={{0,1},{1,0},{2,3},{3,2},{4,5},{5,4},{6,7},{7,6},{8,9},{9,8},{10,11... | collective-permute-start | bytes 884744 | tf_op jit(solution)/shard_map/ppermute | solution.py:569
  33.1 6.2 %copy-start.53 = (bf16[1,192]{1,0:T(2,128)(2,1)S(1)}, bf16[1,192]{1,0:T(2,128)(2,1)}, u32[]{:S(2)}) copy-start(bf16[1,192]{1,0:T(2,128)(2,1)} %concatenate.14) | copy-start | bytes 1156
  37.4 7.4 %collective-permute-start.2 = (bf16[256,384]{1,0:T(8,128)(2,1)S(1)}, bf16[256,384]{1,0:T(8,128)(2,1)S(1)}, u32[]{:S(2)}, u32[]{:S(2)}) collective-permute-start(bf16[256,384]{1,0:T(8,128)(2,1)S(1)} %get-tuple-element.66.refs_1_), channel_id=1, source_target_pairs={{0,2},{1,3},{2,0},{3,1},{4,6},{5,7},{6,4},{7,5},{8,10},{9,11},{10,... | collective-permute-start | bytes 589832 | tf_op jit(solution)/shard_map/ppermute | solution.py:572
  42.5 9.6 %copy-start.19 = (bf16[256,384]{1,0:T(8,128)(2,1)}, bf16[256,384]{1,0:T(8,128)(2,1)S(1)}, u32[]{:S(2)}) copy-start(bf16[256,384]{1,0:T(8,128)(2,1)S(1)} %get-tuple-element.72.refs_1_) | copy-start | bytes 589828
  42.5 7.1 %copy-start.16 = (bf16[2,8,128,256]{3,2,1,0:T(8,128)(2,1)S(1)}, bf16[2,8,128,256]{3,2,1,0:T(8,128)(2,1)}, u32[]{:S(2)}) copy-start(bf16[2,8,128,256]{3,2,1,0:T(8,128)(2,1)} %copy-done.15) | copy-start | bytes 3145732
  42.5 7.1 %copy-start.33 = (bf16[384,256]{1,0:T(8,128)(2,1)S(1)}, bf16[384,256]{1,0:T(8,128)(2,1)}, u32[]{:S(2)}) copy-start(bf16[384,256]{1,0:T(8,128)(2,1)} %copy-done.32) | copy-start | bytes 589828
  42.5 7.1 %copy-start.35 = (bf16[256,384]{1,0:T(8,128)(2,1)S(1)}, bf16[256,384]{1,0:T(8,128)(2,1)}, u32[]{:S(2)}) copy-start(bf16[256,384]{1,0:T(8,128)(2,1)} %copy-done.34) | copy-start | bytes 589828
  42.5 7.1 %collective-permute-start.12 = (bf16[256,384]{1,0:T(8,128)(2,1)S(1)}, bf16[256,384]{1,0:T(8,128)(2,1)S(1)}, u32[]{:S(2)}, u32[]{:S(2)}) collective-permute-start(bf16[256,384]{1,0:T(8,128)(2,1)S(1)} %get-tuple-element.70.refs_10_.refs_3_.refs_0_), channel_id=1, source_target_pairs={{0,2},{1,3},{2,0},{3,1},{4,6},{5,7},{6,4},{7,5},{8,10},{9,11},{10,... | collective-permute-start | bytes 589832 | tf_op jit(solution)/shard_map/ppermute | solution.py:572
  47.2 6.7 %collective-permute-start.13 = (bf16[256,384]{1,0:T(8,128)(2,1)S(1)}, bf16[256,384]{1,0:T(8,128)(2,1)S(1)}, u32[]{:S(2)}, u32[]{:S(2)}) collective-permute-start(bf16[256,384]{1,0:T(8,128)(2,1)S(1)} %get-tuple-element.76.refs_0_.refs_2_), channel_id=1, source_target_pairs={{0,2},{1,3},{2,0},{3,1},{4,6},{5,7},{6,4},{7,5},{8,10},{9,11},{10,... | collective-permute-start | bytes 589832 | tf_op jit(solution)/shard_map/ppermute | solution.py:572
  52.1 5.6 %copy-start.23 = (bf16[1152,256]{1,0:T(8,128)(2,1)}, bf16[1152,256]{1,0:T(8,128)(2,1)S(1)}, u32[]{:S(2)}) copy-start(bf16[1152,256]{1,0:T(8,128)(2,1)S(1)} %get-tuple-element.94.refs_0_) | copy-start | bytes 1769476
  57.7 2.6 %collective-permute-start.14 = (bf16[3,192,768]{2,1,0:T(8,128)(2,1)}, bf16[3,192,768]{2,1,0:T(8,128)(2,1)S(1)}, u32[]{:S(2)}, u32[]{:S(2)}) collective-permute-start(bf16[3,192,768]{2,1,0:T(8,128)(2,1)} %get-tuple-element.93), channel_id=1, source_target_pairs={{0,1},{1,0},{2,3},{3,2},{4,5},{5,4},{6,7},{7,6},{8,9},{9,8},{10,11... | collective-permute-start | bytes 2654216 | tf_op jit(solution)/shard_map/ppermute | solution.py:569
  59.4 3.4 %collective-permute-start.16 = (bf16[3,192,768]{2,1,0:T(8,128)(2,1)}, bf16[3,192,768]{2,1,0:T(8,128)(2,1)S(1)}, u32[]{:S(2)}, u32[]{:S(2)}) collective-permute-start(bf16[3,192,768]{2,1,0:T(8,128)(2,1)} %get-tuple-element.100), channel_id=1, source_target_pairs={{0,1},{1,0},{2,3},{3,2},{4,5},{5,4},{6,7},{7,6},{8,9},{9,8},{10,11... | collective-permute-start | bytes 2654216 | tf_op jit(solution)/shard_map/ppermute | solution.py:569
  61.0 8.4 %collective-permute-start.15 = (bf16[288,768]{1,0:T(8,128)(2,1)S(1)}, bf16[288,768]{1,0:T(8,128)(2,1)S(1)}, u32[]{:S(2)}, u32[]{:S(2)}) collective-permute-start(bf16[288,768]{1,0:T(8,128)(2,1)S(1)} %sum_half.2.refs_3_), channel_id=1, source_target_pairs={{0,4},{1,9},{2,6},{3,11},{4,0},{5,13},{6,2},{7,15},{8,12},{9,1},{1... | collective-permute-start | bytes 1327112 | tf_op jit(solution)/shard_map/ppermute | solution.py:580
  63.3 12.9 %collective-permute-start.19 = (bf16[288,768]{1,0:T(8,128)(2,1)S(1)}, bf16[288,768]{1,0:T(8,128)(2,1)S(1)}, u32[]{:S(2)}, u32[]{:S(2)}) collective-permute-start(bf16[288,768]{1,0:T(8,128)(2,1)S(1)} %sum_half.3.refs_7_), channel_id=1, source_target_pairs={{0,4},{1,9},{2,6},{3,11},{4,0},{5,13},{6,2},{7,15},{8,12},{9,1},{1... | collective-permute-start | bytes 1327112 | tf_op jit(solution)/shard_map/ppermute | solution.py:580
  65.8 13.5 %collective-permute-start.22 = (bf16[272,768]{1,0:T(8,128)(2,1)S(1)}, bf16[272,768]{1,0:T(8,128)(2,1)S(1)}, u32[]{:S(2)}, u32[]{:S(2)}) collective-permute-start(bf16[272,768]{1,0:T(8,128)(2,1)S(1)} %get-tuple-element.101.refs_4_.refs_0_), channel_id=1, source_target_pairs={{0,2},{1,3},{2,0},{3,1},{4,6},{5,7},{6,4},{7,5},{8,10},{9,11},{10,... | collective-permute-start | bytes 1253384 | tf_op jit(solution)/shard_map/ppermute | solution.py:572
  70.0 8.6 %collective-permute-start.18 = (bf16[144,768]{1,0:T(8,128)(2,1)S(1)}, bf16[144,768]{1,0:T(8,128)(2,1)S(1)}, u32[]{:S(2)}, u32[]{:S(2)}) collective-permute-start(bf16[144,768]{1,0:T(8,128)(2,1)S(1)} %sum_quarter.4.refs_4_), channel_id=1, source_target_pairs={{0,8},{1,5},{2,10},{3,7},{4,12},{5,1},{6,14},{7,3},{8,0},{9,13},{1... | collective-permute-start | bytes 663560 | tf_op jit(solution)/shard_map/ppermute | solution.py:580
  76.9 6.0 %collective-permute-start.21 = (bf16[144,768]{1,0:T(8,128)(2,1)S(1)}, bf16[144,768]{1,0:T(8,128)(2,1)S(1)}, u32[]{:S(2)}, u32[]{:S(2)}) collective-permute-start(bf16[144,768]{1,0:T(8,128)(2,1)S(1)} %sum_quarter.5.refs_5_), channel_id=1, source_target_pairs={{0,8},{1,5},{2,10},{3,7},{4,12},{5,1},{6,14},{7,3},{8,0},{9,13},{1... | collective-permute-start | bytes 663560 | tf_op jit(solution)/shard_map/ppermute | solution.py:580
  79.3 3.5 %collective-permute-start.23 = (bf16[16,768]{1,0:T(8,128)(2,1)S(1)}, bf16[16,768]{1,0:T(8,128)(2,1)S(1)}, u32[]{:S(2)}, u32[]{:S(2)}) collective-permute-start(bf16[16,768]{1,0:T(8,128)(2,1)S(1)} %vector_rows.1.refs_5_), channel_id=1, source_target_pairs={{0,1},{1,0},{2,3},{3,2},{4,5},{5,4},{6,7},{7,6},{8,9},{9,8},{10,11... | collective-permute-start | bytes 73736 | tf_op jit(solution)/shard_map/ppermute | solution.py:569
  83.6 12.5 %collective-permute-start.25 = (bf16[160,768]{1,0:T(8,128)(2,1)S(1)}, bf16[160,768]{1,0:T(8,128)(2,1)S(1)}, u32[]{:S(2)}, u32[]{:S(2)}) collective-permute-start(bf16[160,768]{1,0:T(8,128)(2,1)S(1)} %sum_quarter.7.refs_2_.refs_0_), channel_id=1, source_target_pairs={{0,24},{1,25},{2,26},{3,27},{4,28},{5,29},{6,30},{7,31},{8,16},{9,... | collective-permute-start | bytes 737288 | tf_op jit(solution)/shard_map/ppermute | solution.py:580
  87.4 8.7 %collective-permute-start.20 = (bf16[144,768]{1,0:T(8,128)(2,1)S(1)}, bf16[144,768]{1,0:T(8,128)(2,1)S(1)}, u32[]{:S(2)}, u32[]{:S(2)}) collective-permute-start(bf16[144,768]{1,0:T(8,128)(2,1)S(1)} %sum_quarter.6.refs_2_.refs_7_.refs_0_), channel_id=1, source_target_pairs={{0,24},{1,25},{2,26},{3,27},{4,28},{5,29},{6,30},{7,31},{8,16},{9,... | collective-permute-start | bytes 663560 | tf_op jit(solution)/shard_map/ppermute | solution.py:580
  96.1 18.4 %copy-start.1 = (bf16[384,768]{1,0:T(8,128)(2,1)S(1)}, bf16[384,768]{1,0:T(8,128)(2,1)}, u32[]{:S(2)}) copy-start(bf16[384,768]{1,0:T(8,128)(2,1)} %copy-done) | copy-start | bytes 1769476
  96.1 18.4 %copy-start.8 = (f32[256,768]{1,0:T(8,128)S(1)}, f32[256,768]{1,0:T(8,128)}, u32[]{:S(2)}) copy-start(f32[256,768]{1,0:T(8,128)} %copy-done.7) | copy-start | bytes 2359300
  96.1 18.4 %copy-start.20 = (bf16[256,384]{1,0:T(8,128)(2,1)S(1)}, bf16[256,384]{1,0:T(8,128)(2,1)}, u32[]{:S(2)}) copy-start(bf16[256,384]{1,0:T(8,128)(2,1)} %copy-done.19) | copy-start | bytes 589828
  96.1 18.4 %copy-start.22 = (bf16[256,384]{1,0:T(8,128)(2,1)S(1)}, bf16[256,384]{1,0:T(8,128)(2,1)}, u32[]{:S(2)}) copy-start(bf16[256,384]{1,0:T(8,128)(2,1)} %copy-done.21) | copy-start | bytes 589828
  96.2 16.2 %collective-permute-start.26 = (bf16[160,768]{1,0:T(8,128)(2,1)S(1)}, bf16[160,768]{1,0:T(8,128)(2,1)S(1)}, u32[]{:S(2)}, u32[]{:S(2)}) collective-permute-start(bf16[160,768]{1,0:T(8,128)(2,1)S(1)} %sum_two.3.refs_2_.refs_0_), channel_id=1, source_target_pairs={{0,8},{1,5},{2,10},{3,7},{4,12},{5,1},{6,14},{7,3},{8,0},{9,13},{1... | collective-permute-start | bytes 737288 | tf_op jit(solution)/shard_map/ppermute | solution.py:580
  105.8 6.5 %collective-permute-start.24 = (bf16[144,768]{1,0:T(8,128)(2,1)S(1)}, bf16[144,768]{1,0:T(8,128)(2,1)S(1)}, u32[]{:S(2)}, u32[]{:S(2)}) collective-permute-start(bf16[144,768]{1,0:T(8,128)(2,1)S(1)} %sum_two.2.refs_2_.refs_0_.refs_5_), channel_id=1, source_target_pairs={{0,8},{1,5},{2,10},{3,7},{4,12},{5,1},{6,14},{7,3},{8,0},{9,13},{1... | collective-permute-start | bytes 663560 | tf_op jit(solution)/shard_map/ppermute | solution.py:580
  112.4 15.3 %collective-permute-start.27 = (bf16[304,768]{1,0:T(8,128)(2,1)S(1)}, bf16[304,768]{1,0:T(8,128)(2,1)S(1)}, u32[]{:S(2)}, u32[]{:S(2)}) collective-permute-start(bf16[304,768]{1,0:T(8,128)(2,1)S(1)} %side_by_side.3.refs_3_.refs_1_), channel_id=1, source_target_pairs={{0,4},{1,9},{2,6},{3,11},{4,0},{5,13},{6,2},{7,15},{8,12},{9,1},{1... | collective-permute-start | bytes 1400840 | tf_op jit(solution)/shard_map/ppermute | solution.py:580
  114.0 11.8 %collective-permute-start.28 = (bf16[288,768]{1,0:T(8,128)(2,1)S(1)}, bf16[288,768]{1,0:T(8,128)(2,1)S(1)}, u32[]{:S(2)}, u32[]{:S(2)}) collective-permute-start(bf16[288,768]{1,0:T(8,128)(2,1)S(1)} %side_by_side.2.refs_2_.refs_1_), channel_id=1, source_target_pairs={{0,4},{1,9},{2,6},{3,11},{4,0},{5,13},{6,2},{7,15},{8,12},{9,1},{1... | collective-permute-start | bytes 1327112 | tf_op jit(solution)/shard_map/ppermute | solution.py:580
  115.1 9.0 %collective-permute-start.17 = (bf16[256,768]{1,0:T(8,128)(2,1)S(1)}, bf16[256,768]{1,0:T(8,128)(2,1)S(1)}, u32[]{:S(2)}, u32[]{:S(2)}) collective-permute-start(bf16[256,768]{1,0:T(8,128)(2,1)S(1)} %get-tuple-element.103), channel_id=1, source_target_pairs={{0,2},{1,3},{2,0},{3,1},{4,6},{5,7},{6,4},{7,5},{8,10},{9,11},{10,... | collective-permute-start | bytes 1179656 | tf_op jit(solution)/shard_map/ppermute | solution.py:572
  (36 other events, 85.9 us)

commit v4 on v3

v4 whole, which is shorter than its diff:
```python
import functools

import jax
import jax.numpy as jnp
from jax import lax
from jax.experimental import pallas as pl
from jax.experimental.pallas import tpu as pltpu
from jax.sharding import PartitionSpec as P

HEAD_DIM = 24
LEN = 128
PAIR = 2 * HEAD_DIM
EPSILON = 1e-05
SCALE = HEAD_DIM ** (-0.5)
LOG2E = 1.4426950408889634
F32 = jnp.float32
BF16 = jnp.bfloat16
MIB = 1024 * 1024


def dot_nn(a, b):
    return lax.dot_general(a, b, (((1,), (0,)), ((), ())), preferred_element_type=F32)


def dot_nt(a, b):
    return lax.dot_general(a, b, (((1,), (1,)), ((), ())), preferred_element_type=F32)


def dot_tn(a, b):
    return lax.dot_general(a, b, (((0,), (0,)), ((), ())), preferred_element_type=F32)


def normalise(v):
    centered = v - jnp.mean(v, axis=-1, keepdims=True)
    r = lax.rsqrt(jnp.mean(centered * centered, axis=-1, keepdims=True) + EPSILON)
    return centered * r, r


def norm_back(da, gain, xh, r):
    e = da * gain
    return r * (
        e - jnp.mean(e, axis=-1, keepdims=True) - xh * jnp.mean(e * xh, axis=-1, keepdims=True)
    )


def pair_blocks(rows):
    rows = rows.astype(F32)
    none = jnp.zeros((HEAD_DIM, LEN), F32)
    left = jnp.concatenate([rows[:HEAD_DIM], none], axis=0)
    right = jnp.concatenate([none, rows[HEAD_DIM:]], axis=0)
    return jnp.concatenate([left, right], axis=1).astype(BF16)


def pair_window(i, width):
    low = min(PAIR * i // LEN * LEN, width - 2 * LEN)
    return low, PAIR * i - low


def placed(block, before):
    parts = []
    if before:
        parts.append(jnp.zeros((before, 2 * LEN), BF16))
    parts.append(block)
    after = 2 * LEN - PAIR - before
    if after:
        parts.append(jnp.zeros((after, 2 * LEN), BF16))
    return jnp.concatenate(parts, axis=0)


def diagonal(both):
    return jnp.concatenate([both[:HEAD_DIM, :LEN], both[HEAD_DIM:, LEN:]], axis=0)


class IO:
    def __init__(self, reads, writes):
        self.reads, self.writes = reads, writes
        self.started = set()

    def wait(self, *args):
        for j in args:
            if j in self.reads:
                self.reads[j].wait()

    def flush(self, *outs):
        for j in outs:
            if j in self.writes:
                self.started.add(j)
                self.writes[j].start()

    def finish(self):
        self.flush(*(j for j in self.writes if j not in self.started))
        for copy in self.writes.values():
            copy.wait()


def pinned(a):
    return pltpu.with_memory_space_constraint(a, pltpu.HBM)


class Chain:
    def __init__(self):
        self.token = None

    def call(self, kernel, name, args, outs, kinds, scratch=(), limit=16, weight=1):
        ins, out_kinds = kinds.split("-")
        assert len(ins) == len(args) and len(out_kinds) == len(outs)
        hbm = pl.BlockSpec(memory_space=pltpu.HBM)
        vmem = pl.BlockSpec(memory_space=pltpu.VMEM)
        smem = pl.BlockSpec(memory_space=pltpu.SMEM)
        spec = lambda kind: {"s": smem, "v": vmem}.get(kind, hbm)
        tokens = () if self.token is None else (self.token,)
        staged = [j for j, kind in enumerate(ins) if kind in "hcl"]
        written = [j for j, kind in enumerate(out_kinds) if kind == "w"]
        memory = lambda kind: pltpu.SMEM if kind == "c" else pltpu.VMEM
        buffers = [memory(ins[j])(args[j].shape, args[j].dtype) for j in staged]
        buffers += [pltpu.VMEM(outs[j].shape, outs[j].dtype) for j in written]
        n_in, n_out, n_buf = len(args) + len(tokens), len(outs), len(buffers)

        def body(*refs):
            arg_refs = list(refs[: len(args)])
            out_refs = list(refs[n_in : n_in + n_out])
            token_ref = refs[n_in + n_out]
            own = refs[n_in + n_out + 1 :]
            bufs, sems, extra = own[:n_buf], own[n_buf], own[n_buf + 1 :]
            reads, writes = {}, {}
            for at, j in enumerate(staged):
                reads[j] = pltpu.make_async_copy(arg_refs[j], bufs[at], sems.at[at])
                reads[j].start()
                arg_refs[j] = bufs[at]
            for at, j in enumerate(written, len(staged)):
                writes[j] = pltpu.make_async_copy(bufs[at], out_refs[j], sems.at[at])
                out_refs[j] = bufs[at]
            io = IO(reads, writes)
            io.wait(*(j for j in staged if ins[j] == "h"))
            token_ref[...] = jnp.zeros_like(token_ref)
            kernel(io, *arg_refs, *out_refs, *extra)
            io.finish()

        *results, self.token = pl.pallas_call(
            body,
            in_specs=[spec(kind) for kind in ins] + [vmem] * len(tokens),
            out_specs=[spec(kind) for kind in out_kinds] + [vmem],
            out_shape=[*outs, f32(8, 128)],
            scratch_shapes=[*buffers, pltpu.SemaphoreType.DMA((max(n_buf, 1),)), *scratch],
            compiler_params=pltpu.CompilerParams(vmem_limit_bytes=limit * MIB),
            cost_estimate=pl.CostEstimate(flops=weight * 10**10, bytes_accessed=10**8, transcendentals=0),
            name=name,
        )(*(pinned(a) if kind in "hclp" else a for a, kind in zip(args, ins)), *tokens)
        return results


def bf16(*shape):
    return jax.ShapeDtypeStruct(shape, BF16)


def f32(*shape):
    return jax.ShapeDtypeStruct(shape, F32)


def copies(sems, pairs):
    started = [pltpu.make_async_copy(a, b, sems.at[j]) for j, (a, b) in enumerate(pairs)]
    for copy in started:
        copy.start()
    return started


def finish(started):
    for copy in started:
        copy.wait()


def attention(chain, bits, place, nodes, edges, x, gain, bias, w, g=None):
    rows, d = x.shape
    width = w.shape[1] if g is None else 2 * w[0].shape[1]
    shard = width // 2
    pairs = width // PAIR
    mols = rows // LEN

    def kernel(io, bits_ref, nodes_ref, edges_ref, x_ref, gain_ref, bias_ref, *refs):
        started = []
        if g is None:
            w_ref, *refs = refs
            a1_ref, qt_ref, kt_ref, v_ref, p_ref, ot_ref, o_ref = refs
        else:
            own, got, g_ref, *refs, w_ref, sems = refs
            a1_ref, qt_ref, kt_ref, v_ref, p_ref, ot_ref, o_ref = refs
            pairs_w = [(own, w_ref.at[:, :shard]), (got, w_ref.at[:, shard:]), (g_ref, o_ref.at[:, :d])]
            started = copies(sems, pairs_w)
        xh, _ = normalise(x_ref[...].astype(F32))
        a1 = (xh * gain_ref[...][None, :] + bias_ref[...][None, :]).astype(BF16)
        a1_ref[...] = a1
        finish(started[:2])
        qt = dot_nt(w_ref[0], a1).astype(BF16)
        keys = dot_nt(a1, w_ref[1]).astype(BF16)
        vt = dot_nt(w_ref[2], a1).astype(BF16)
        qt_ref[...] = qt
        every = [(m, i) for m in range(mols) for i in range(pairs)]
        lanes = lambda m: slice(LEN * m, LEN * (m + 1))
        rows_of = lambda i: slice(PAIR * i, PAIR * (i + 1))
        scores, probs = {}, {}
        for m, i in every:
            low, before = pair_window(i, width)
            rhs = placed(pair_blocks(qt[rows_of(i), lanes(m)]), before)
            scores[m, i] = dot_nn(keys[lanes(m), low : low + 2 * LEN], rhs)
        io.wait(1, 2)
        for m in range(mols):
            mol = bits_ref[place] + m
            count = 1 + nodes_ref[mol] + edges_ref[mol]
            valid = lax.broadcasted_iota(jnp.int32, (LEN, 2 * LEN), 0) < count
            for i in range(pairs):
                s = jnp.where(valid, scores[m, i], -1e30)
                e = jnp.exp2((s - jnp.max(s, axis=0, keepdims=True)) * (SCALE * LOG2E))
                p = (e * (1.0 / jnp.sum(e, axis=0, keepdims=True))).astype(BF16)
                p_ref[m, i] = p
                probs[m, i] = p
        for m, i in every:
            both = dot_nn(vt[rows_of(i), lanes(m)], probs[m, i])
            ot_ref[rows_of(i), lanes(m)] = diagonal(both).astype(BF16)
        o_ref[:, o_ref.shape[1] - width :] = ot_ref[...].T
        kt_ref[...] = dot_nt(w_ref[1], a1).astype(BF16)
        v_ref[...] = dot_nt(a1, w_ref[2]).astype(BF16)
        finish(started[2:])

    outs = [
        bf16(rows, d), bf16(width, rows), bf16(width, rows), bf16(rows, width),
        bf16(mols, pairs, LEN, 2 * LEN), bf16(width, rows),
    ]
    args = (bits, nodes, edges, x, gain, bias)
    if g is None:
        return chain.call(
            kernel, "attention_forward", (*args, w), [*outs, bf16(rows, width)], "sccvvvv-vvvvvvv"
        )
    return chain.call(
        kernel, "attention_forward", (*args, *w, g), [*outs, bf16(rows, d + width), bf16(3, width, d)],
        "sccvvvprv-vvvvvvvv", scratch=[pltpu.SemaphoreType.DMA((3,))],
    )


def send_parts(chain, bits, out_weight, fc1_weight, fc2_weight, bias, others):
    shard, d = out_weight.shape
    n = len(others)

    def kernel(io, bits_ref, wo, fc1, fc2, bias_ref, *refs):
        others_in, (far_ref, near_ref, *others_out, sems) = refs[:n], refs[n:]
        rows = lambda at: near_ref.at[at * shard : (at + 1) * shard]
        pl.when(bits_ref[2] == 0)(lambda: finish(copies(sems, [(wo, far_ref)])))
        pl.when(bits_ref[2] != 0)(lambda: finish(copies(sems, [(fc1, far_ref)])))
        near = [(wo, rows(0)), (fc1, rows(1)), (fc2, rows(2)), (bias_ref, near_ref.at[3 * shard :])]
        finish(copies(sems, near + list(zip(others_in, others_out))))

    far, near, *others = chain.call(
        kernel, "send_parts", (bits, out_weight, fc1_weight, fc2_weight, bias, *others),
        [bf16(shard, d), bf16(3 * shard + 16, d)] + [jax.ShapeDtypeStruct(a.shape, a.dtype) for a in others],
        "spppr" + "p" * n + "-vv" + "v" * n, limit=4, scratch=[pltpu.SemaphoreType.DMA((4 + n,))],
    )
    return far, near, others


def join_arrays(chain, *parts):
    def kernel(io, *refs):
        *ins, out_ref, sems = refs
        finish(copies(sems, [(ref, out_ref.at[j]) for j, ref in enumerate(ins)]))

    return chain.call(
        kernel, "join_arrays", parts, [bf16(len(parts), *parts[0].shape)], "v" * len(parts) + "-v", limit=4,
        scratch=[pltpu.SemaphoreType.DMA((len(parts),))],
    )[0]


def pack_near(chain, near, near_got):
    d = near.shape[1]
    shard = (near.shape[0] - 16) // 3

    def kernel(io, near0, near1, fc2_ref, sems):
        rows = lambda ref, at: ref.at[at * shard : (at + 1) * shard]
        finish(copies(sems, [(rows(near0, 2), rows(fc2_ref, 0)), (rows(near1, 2), rows(fc2_ref, 1))]))

    return chain.call(
        kernel, "pack_near", (near, near_got), [bf16(2 * shard, d)], "vv-v", limit=4,
        scratch=[pltpu.SemaphoreType.DMA((2,))],
    )[0]


def pack_rest(chain, bits, near, near_got, far, far_got):
    shard, d = far.shape[1:]

    def kernel(io, bits_ref, near0, near1, far0, far1, wo_ref, fc1_ref, sems):
        rows = lambda ref, at: ref.at[at * shard : (at + 1) * shard]
        wo_at = bits_ref[2]
        pairs = []
        for at, (near_ref, far_ref) in enumerate(((near0, far0), (near1, far1))):
            pairs += [(rows(near_ref, c), rows(ref, at)) for c, ref in enumerate((wo_ref, fc1_ref))]
            pairs += [(far_ref.at[wo_at], rows(wo_ref, 2 + at)), (far_ref.at[1 - wo_at], rows(fc1_ref, 2 + at))]
        finish(copies(sems, pairs))

    return chain.call(
        kernel, "pack_rest", (bits, near, near_got, far, far_got), [bf16(4 * shard, d), bf16(4 * shard, d)],
        "svvvv-vv", limit=4, scratch=[pltpu.SemaphoreType.DMA((8,))],
    )


def feed(chain, x, oa, got, wo, gain, bias, fc1, b1, fc2, kinds):
    rows, d = x.shape
    width = fc2.shape[0]
    shard = width // 2

    def kernel(io, x_ref, oa_ref, *refs):
        if len(got) == 2:
            g, ob = refs[0][...], refs[1][...]
        else:
            g, ob = refs[0][:, :d], refs[0][:, d:]
        wo_ref, gain_ref, bias_ref, fc1_ref, b10, b11, fc2_ref, h_ref, a2_ref, z_ref, du_ref = refs[len(got) :]
        oa = oa_ref[:, oa_ref.shape[1] - width :]
        h = x_ref[...].astype(F32) + dot_nn(jnp.concatenate([oa, ob], axis=1), wo_ref[...])
        h_ref[...] = h
        xh, _ = normalise(h)
        a2 = (xh * gain_ref[...][None, :] + bias_ref[...][None, :]).astype(BF16)
        a2_ref[...] = a2
        b1 = jnp.concatenate([b[3 * shard : 3 * shard + 1, :shard] for b in (b10, b11)], axis=1).astype(F32)
        u = dot_nt(a2, fc1_ref[:width]) + b1
        dz = dot_nt(g, fc2_ref[...])
        phi = 0.5 * (1.0 + lax.erf(u * (0.5**0.5)))
        slope = phi + u * (jnp.exp(-0.5 * u * u) * 0.3989422804014327)
        du_ref[...] = (dz * slope).astype(BF16)
        z_ref[...] = (u * phi).astype(BF16)

    return chain.call(
        kernel, "feed_forward", (x, oa, *got, wo, gain, bias, fc1, *b1, fc2),
        [f32(rows, d), bf16(rows, d), bf16(rows, width), bf16(rows, width)],
        kinds + "vvvvvvv-vvvv",
    )


def feed_grads(chain, zs, dus, a2s, gs):
    d = a2s[0].shape[1]
    width = zs[0].shape[1]
    shard = width // 2

    def kernel(io, z0, z1, du0, du1, a0, a1, g0, g1, keep_ref, send_ref, sums_ref):
        first = dot_tn(du0[...], a0[...]) + dot_tn(du1[...], a1[...])
        second = dot_tn(z0[...], g0[...]) + dot_tn(z1[...], g1[:, :d])
        for at, ref in enumerate((keep_ref, send_ref)):
            rows = slice(at * shard, (at + 1) * shard)
            ref[0] = first[rows].astype(BF16)
            ref[1] = second[rows].astype(BF16)
        sums_ref[...] = jnp.sum(du0[...].astype(F32), axis=0, keepdims=True) + jnp.sum(
            du1[...].astype(F32), axis=0, keepdims=True
        )

    return chain.call(
        kernel, "feed_grads", (*zs, *dus, *a2s, *gs), [bf16(2, shard, d), bf16(2, shard, d), f32(1, width)],
        "vvvvvvvv-vvv", weight=10,
    )


def feed_result(chain, zs, fc2, h):
    rows, d = h.shape

    def kernel(io, z0, z1, fc2_ref, h_ref, mine_ref, theirs_ref):
        theirs_ref[...] = dot_nn(z1[...], fc2_ref[...]).astype(BF16)
        mine_ref[...] = h_ref[...] + dot_nn(z0[...], fc2_ref[...])

    return chain.call(
        kernel, "feed_result", (*zs, fc2, h), [f32(rows, d), bf16(rows, d)], "vvvv-vv", limit=8,
    )


def backward(chain, args, own):
    h, kt = args[3], args[9]
    rows, d = h.shape
    width = kt.shape[0]
    mols, pairs = rows // LEN, width // PAIR

    def kernel(io, du_ref, dr_ref, fc1_ref, h_ref, g_ref, gain_ref, wo_ref, p_ref, qt_ref, kt_ref, v_ref,
               gh_ref, dp_ref, dh_ref=None, sums_ref=None):
        du = jnp.concatenate([du_ref[...], dr_ref[...]], axis=1)
        da2 = dot_nn(du, fc1_ref[...])
        xh, r = normalise(h_ref[...])
        dh = g_ref[:, :d].astype(F32) + norm_back(da2, gain_ref[...][None, :], xh, r)
        if own:
            dh_ref[...] = dh
            sums_ref[0:1] = jnp.sum(da2 * xh, axis=0, keepdims=True)
            sums_ref[1:2] = jnp.sum(da2, axis=0, keepdims=True)
            io.flush(2)
        gh = dh.astype(BF16)
        gh_ref[...] = gh
        dot = dot_nt(wo_ref[:width], gh).astype(BF16)
        every = [(m, i) for m in range(mols) for i in range(pairs)]
        lanes = lambda m: slice(LEN * m, LEN * (m + 1))
        rows_of = lambda i: slice(PAIR * i, PAIR * (i + 1))
        dps, dss, dos = {}, {}, {}
        io.wait(7, 8, 9, 10)
        for m, i in every:
            low, before = pair_window(i, width)
            dos[m, i] = pair_blocks(dot[rows_of(i), lanes(m)])
            dps[m, i] = dot_nn(v_ref[lanes(m), low : low + 2 * LEN], placed(dos[m, i], before))
        for m, i in every:
            dv = dot_nt(dos[m, i], p_ref[m, i])
            dp_ref[pl.ds(2 * width + PAIR * i, PAIR), lanes(m)] = dv.astype(BF16)
        for m, i in every:
            p = p_ref[m, i].astype(F32)
            t = dps[m, i] * p
            dss[m, i] = (t - p * jnp.sum(t, axis=0, keepdims=True)).astype(BF16)
        for m, i in every:
            dq = diagonal(dot_nn(kt_ref[rows_of(i), lanes(m)], dss[m, i])) * SCALE
            dp_ref[rows_of(i), lanes(m)] = dq.astype(BF16)
            dk = dot_nt(pair_blocks(qt_ref[rows_of(i), lanes(m)]), dss[m, i]) * SCALE
            dp_ref[pl.ds(width + PAIR * i, PAIR), lanes(m)] = dk.astype(BF16)

    outs = [bf16(rows, d), bf16(3 * width, rows)] + ([f32(rows, d), f32(8, d)] if own else [])
    return chain.call(
        kernel, "attention_backward", args, outs, "v" * 11 + ("-vvvv" if own else "-vv"),
    )


def weight_grads(chain, name, shard, lefts, rights):
    d = rights[0][0].shape[1]
    args, count = [], len(lefts)
    for (u0, u1, _), (v0, v1) in zip(lefts, rights):
        args += [u0, u1, v0, v1]

    def kernel(io, *refs):
        keep_ref, send_ref = refs[-2:]
        for at, ref in ((1, send_ref), (0, keep_ref)):
            for c in range(count):
                u0, u1, v0, v1 = refs[4 * c : 4 * c + 4]
                rows = slice(lefts[c][2] + at * shard, lefts[c][2] + (at + 1) * shard)
                left = jnp.concatenate([u0[rows], u1[rows]], axis=1)
                right = jnp.concatenate([v0[...], v1[...]], axis=0)
                ref[c] = dot_nn(left, right).astype(BF16)

    return chain.call(
        kernel, name, args, [bf16(count, shard, d), bf16(count, shard, d)], "v" * len(args) + "-vv",
    )


def input_grads(chain, dps, w, xs, sums, bias):
    rows, d = xs[0].shape

    def kernel(io, dp0, dp1, w_ref, x0, x1, sums_ref, bias_ref, mine_ref, theirs_ref):
        w = w_ref[...].reshape(dp0.shape[0], d)
        theirs = dot_tn(dp1[...], w)
        theirs_ref[:rows] = theirs.astype(BF16)
        mine = dot_tn(dp0[...], w)
        mine_ref[...] = mine
        xh0, _ = normalise(x0[...].astype(F32))
        xh1, _ = normalise(x1[...].astype(F32))
        bias = bias_ref[...]
        vec = [
            jnp.sum(mine * xh0, axis=0, keepdims=True) + jnp.sum(theirs * xh1, axis=0, keepdims=True),
            jnp.sum(mine, axis=0, keepdims=True) + jnp.sum(theirs, axis=0, keepdims=True),
            sums_ref[0:2],
            jnp.concatenate([bias, jnp.zeros((1, d - bias.shape[1]), F32)], axis=1),
            jnp.zeros((11, d), F32),
        ]
        theirs_ref[rows:] = jnp.concatenate(vec, axis=0).astype(BF16)

    return chain.call(
        kernel, "input_grads", (*dps, w, *xs, sums, bias), [f32(rows, d), bf16(rows + 16, d)], "vvvvvvv-vv"
    )


def input_norm(chain, x, gain, mine, got, dh):
    rows, d = x.shape

    def kernel(io, x_ref, gain_ref, mine_ref, got_ref, dh_ref, out_ref):
        xh, r = normalise(x_ref[...].astype(F32))
        da1 = mine_ref[...] + got_ref[:rows].astype(F32)
        out_ref[...] = (dh_ref[...] + norm_back(da1, gain_ref[...][None, :], xh, r)).astype(BF16)

    return chain.call(
        kernel, "input_norm", (x, gain, mine, got, dh), [bf16(rows, d)], "vvvvv-w", limit=8
    )[0]


def add_result(chain, mine, got):
    def kernel(io, mine_ref, got_ref, out_ref):
        out_ref[...] = (mine_ref[...] + got_ref[...].astype(F32)).astype(BF16)

    return chain.call(kernel, "add_result", (mine, got), [bf16(*mine.shape)], "vv-w", limit=8)[0]


def plus(*terms):
    total = terms[0].astype(F32)
    for term in terms[1:]:
        total = total + term.astype(F32)
    return total.astype(BF16)


def vector_rows(chain, mine, got):
    rows, d = mine.shape

    def kernel(io, mine_ref, got_ref, out_ref):
        a, b = mine_ref[rows - 16 :], got_ref[rows - 16 :]
        same = lax.broadcasted_iota(jnp.int32, (16, d), 0) < 4
        out_ref[...] = plus(a, jnp.where(same, b.astype(F32), 0.0))

    return chain.call(kernel, "vector_rows", (mine, got), [bf16(16, d)], "vv-v", limit=4)[0]


def sum_half(chain, bits, mine, got):
    def kernel(io, bits_ref, mine_ref, got_ref, out_ref):
        at = 1 - bits_ref[0]
        out_ref[...] = mine_ref[at] + got_ref[at]

    return chain.call(
        kernel, "sum_half", (bits, mine, got), [bf16(*mine.shape[1:])], "svv-v", limit=8
    )[0]


def sum_quarter(chain, bits, mine, got, half, last=(), vec=()):
    rows, d = mine.shape[2:]

    def kernel(io, bits_ref, mine_ref, got_ref, half_ref, *refs):
        *refs, out_ref = refs
        first = bits_ref[0]
        at = bits_ref[1] if last else 1 - bits_ref[1]
        terms = [mine_ref[first, at], got_ref[first, at], half_ref[at]]
        out_ref[:rows] = plus(*terms, *(ref[...] for ref in refs[: len(last)]))
        if vec:
            a, b = refs[-2][...].astype(F32), refs[-1][...].astype(F32)
            shard = vec[2]
            turned = jnp.concatenate([b[:, shard : 2 * shard], b[:, :shard], b[:, 2 * shard :]], axis=1)
            same = lax.broadcasted_iota(jnp.int32, a.shape, 0) < 4
            out_ref[rows:] = plus(a, jnp.where(same, b, turned))

    args = (bits, mine, got, half, *last, *vec[:2])
    return chain.call(
        kernel, "sum_quarter", args, [bf16(rows + (16 if vec else 0), d)], "s" + "v" * (len(args) - 1) + "-v",
        limit=8,
    )[0]


def sum_two(chain, a, b):
    def kernel(io, a_ref, b_ref, out_ref):
        out_ref[...] = a_ref[...] + b_ref[...]

    return chain.call(kernel, "sum_two", (a, b), [bf16(*a.shape)], "vv-v", limit=8)[0]


def side_by_side(chain, mine, got, rows):
    extra = mine.shape[0] - rows

    def kernel(io, mine_ref, got_ref, out_ref):
        out_ref[:rows] = mine_ref[:rows]
        out_ref[rows : 2 * rows] = got_ref[:rows]
        if extra:
            out_ref[2 * rows :] = mine_ref[rows:] + got_ref[rows:]

    return chain.call(
        kernel, "side_by_side", (mine, got), [bf16(2 * rows + extra, mine.shape[1])], "vv-v", limit=8
    )[0]


def place_sums(chain, bits, mine, got, rows, outs, vec=()):
    d = mine.shape[1]

    def kernel(io, bits_ref, mine_ref, got_ref, *refs):
        out_refs, vec_refs = refs[: len(outs)], refs[len(outs) : -2]
        all_ref, sems = refs[-2:]
        for at, ref in enumerate((mine_ref, got_ref)):
            half = bits_ref[0] if at == 0 else 1 - bits_ref[0]
            for part in range(2):
                quarter = bits_ref[1] if part == 0 else 1 - bits_ref[1]
                start = pl.multiple_of((2 * half + quarter) * rows, 16)
                all_ref[pl.ds(start, rows), :] = ref[part * rows : (part + 1) * rows].astype(F32)
        pairs, start = [], 0
        for ref in out_refs:
            for piece in [ref] if len(ref.shape) == 2 else [ref.at[c] for c in range(ref.shape[0])]:
                pairs.append((all_ref.at[start : start + piece.shape[0]], piece))
                start += piece.shape[0]
        started = copies(sems, pairs)
        if vec:
            total = mine_ref[2 * rows :].astype(F32) + got_ref[2 * rows :].astype(F32)
            for at, (n, ref) in enumerate(zip(vec, vec_refs)):
                ref[...] = total[at, :n]
        finish(started)

    return chain.call(
        kernel, "place_sums", (bits, mine, got), [*outs, *(f32(n) for n in vec)],
        "svv-" + "r" * len(outs) + "v" * len(vec), limit=8,
        scratch=[pltpu.VMEM((4 * rows, d), F32), pltpu.SemaphoreType.DMA((4,))],
    )


def local(
    n_dp, n_tensor, tokens, node_counts, edge_counts, ln1_gain, ln1_bias, qkv_weight, out_weight,
    ln2_gain, ln2_bias, fc1_weight, fc1_bias, fc2_weight, out_grad,
):
    d = tokens.shape[1]
    shard = out_weight.shape[0]
    width = 2 * shard
    mols = tokens.shape[0] // LEN
    dp_at = lax.axis_index("dp")
    tensor_at = lax.axis_index("tensor")
    core = tensor_at % 2
    bit0 = dp_at % 2
    bit1 = (dp_at // 2 + dp_at // 4) % 2
    bits = jnp.stack(
        [jnp.where(core == 0, bit0, bit1), jnp.where(core == 0, bit1, bit0), bit0, tensor_at * mols,
         (tensor_at ^ 2) * mols]
    ).astype(jnp.int32)
    chain = Chain()

    def swap_core(a):
        return lax.ppermute(a, "tensor", [(t, t ^ 1) for t in range(n_tensor)])

    def swap_y(a):
        return lax.ppermute(a, "tensor", [(t, t ^ 2) for t in range(n_tensor)])

    def swap_dp(a, mask0, mask1):
        pairs = [
            (p * n_tensor + t, (p ^ (mask1 if t % 2 else mask0)) * n_tensor + t)
            for p in range(n_dp)
            for t in range(n_tensor)
        ]
        return lax.ppermute(a, ("dp", "tensor"), pairs)

    swap_first = lambda a: swap_dp(a, 1, 2)
    swap_second = lambda a: swap_dp(a, 2, 1)
    far_masks = [6 if k == 2 else 1 << k for k in range(2, n_dp.bit_length() - 1)]

    w_got = swap_core(qkv_weight)
    bias = jnp.pad(fc1_bias.reshape(1, -1), ((0, 15), (0, d - shard)))
    far_y, near, others = send_parts(
        chain, bits, out_weight, fc1_weight, fc2_weight, bias,
        (tokens, out_grad, ln1_gain, ln1_bias, ln2_gain, ln2_bias),
    )
    far_y = swap_y(far_y)
    near_got = swap_core(near)
    x_got = swap_y(others[0])
    tokens, out_grad, ln1_gain, ln1_bias, ln2_gain, ln2_bias = others

    counts = (node_counts, edge_counts)
    norm1 = (ln1_gain, ln1_bias)
    a1_0, qt_0, kt_0, v_0, p_0, ot_0, packet, w_qkv = attention(
        chain, bits, 3, *counts, tokens, *norm1, (qkv_weight, w_got), out_grad
    )
    packet_got = swap_y(packet)
    far_x = swap_dp(join_arrays(chain, far_y)[0], 1, 1)
    a1_1, qt_1, kt_1, v_1, p_1, ot_1, o_1 = attention(chain, bits, 4, *counts, x_got, *norm1, w_qkv)
    o_got = swap_y(o_1)
    far = join_arrays(chain, far_y, far_x)
    far_got = swap_core(far)
    fc2 = pack_near(chain, near, near_got)
    wo, fc1 = pack_rest(chain, bits, near, near_got, far, far_got)

    ffn = (wo, ln2_gain, ln2_bias, fc1, (near, near_got), fc2)
    h_1, a2_1, z_1, du_1 = feed(chain, x_got, o_1, (packet_got,), *ffn, "vvv")
    dr_0 = swap_y(du_1)
    h_0, a2_0, z_0, du_0 = feed(chain, tokens, packet, (out_grad, o_got), *ffn, "vvvv")
    dr_1 = swap_y(du_0)
    keep_r, send_r, bias_sums = feed_grads(
        chain, (z_0, z_1), (du_0, du_1), (a2_0, a2_1), (out_grad, packet_got)
    )
    got_r = swap_core(send_r)
    gh_0, dp_0, dh, sums = backward(
        chain, (du_0, dr_0, fc1, h_0, out_grad, ln2_gain, wo, p_0, qt_0, kt_0, v_0), True
    )

    class Sum:
        def __init__(self, count, keep, got):
            self.size = count * shard // 4
            self.keep, self.got = keep, got

        def first(self):
            half = lambda a: a.reshape(2, 2 * self.size, d)
            got = swap_first(sum_half(chain, bits, half(self.keep), half(self.got)))
            quarters = lambda a: a.reshape(2, 2, self.size, d)
            self.view = (quarters(self.keep), quarters(self.got), got.reshape(2, self.size, d))

        def second(self):
            self.last = swap_second(sum_quarter(chain, bits, *self.view))

        def third(self, vec=()):
            self.sum = sum_quarter(chain, bits, *self.view, (self.last,), vec)
            self.last = swap_dp(self.sum, far_masks[0], far_masks[0])

        def fourth(self):
            self.sum = sum_two(chain, self.sum, self.last)
            for mask in far_masks[1:]:
                self.sum = sum_two(chain, self.sum, swap_dp(self.sum, mask, mask))
            self.last = swap_second(self.sum)

        def fifth(self):
            self.both = side_by_side(chain, self.sum, self.last, self.size)
            self.last = swap_first(self.both)

        def place(self, outs, vec=()):
            return place_sums(chain, bits, self.both, self.last, self.size, outs, vec)

    r = Sum(2, keep_r, got_r)
    r.first()
    gh_1, dp_1 = backward(
        chain, (du_1, dr_1, fc1, h_1, packet_got, ln2_gain, wo, p_1, qt_1, kt_1, v_1), False
    )
    a1s = (a1_0, a1_1)
    keep_q, send_q = weight_grads(
        chain, "weight_grads", shard, [(dp_0, dp_1, c * width) for c in range(3)] + [(ot_0, ot_1, 0)],
        [a1s] * 3 + [(gh_0, gh_1)],
    )
    q = Sum(4, keep_q, swap_core(send_q))
    r.second()
    q.first()
    da1_mine, da1_theirs = input_grads(chain, (dp_0, dp_1), w_qkv, (tokens, x_got), sums, bias_sums)
    da1_got = swap_y(da1_theirs)
    r.third()
    q.second()
    r.fourth()
    vec = vector_rows(chain, da1_theirs, da1_got)
    q.third((vec, swap_core(vec), shard))
    res_mine, res_theirs = feed_result(chain, (z_0, z_1), fc2, h_0)
    res_got = swap_y(res_theirs)
    grad_tokens = input_norm(chain, tokens, ln1_gain, da1_mine, da1_got, dh)
    r.fifth()
    q.fourth()
    rows = f32(shard, d)
    grad_fc1, grad_fc2 = r.place([rows, rows])
    result = add_result(chain, res_mine, res_got)
    q.fifth()
    grad_qkv, grad_out, gain1, bias1, gain2, bias2, grad_b = q.place(
        [f32(3, shard, d), rows], (d, d, d, d, shard)
    )
    return (
        result, grad_tokens, gain1, bias1, grad_qkv, grad_out, gain2, bias2, grad_fc1, grad_b, grad_fc2,
    )


def solution(mesh):
    tokens = P(("dp", "tensor"), None)
    rows = P("tensor", None)
    qkv = P(None, "tensor", None)
    in_specs = (
        tokens, P("dp"), P("dp"), P(), P(), qkv, rows, P(), P(), rows, P("tensor"), rows, tokens,
    )
    out_specs = (tokens, tokens, P(), P(), qkv, rows, P(), P(), rows, P("tensor"), rows)
    step = functools.partial(local, mesh.shape["dp"], mesh.shape["tensor"])
    return jax.shard_map(step, mesh=mesh, in_specs=in_specs, out_specs=out_specs, check_vma=False)
```

time: 132 us -> 121 us (0.917)
  local copies, waits for them, and re-layouts: 15.7 us -> 1.02 us
  waiting for transfers between devices: 41.2 us -> 51.8 us
  starting transfers between devices: 37.4 us -> 32 us
  other arithmetic: 1.86 us -> 0 us
    ppermute x8, waiting for transfers between devices: 9.22 us -> 26.8 us  [swap_y(): return lax.ppermute(a, 'tensor', [(t, t ^ 2) for t in range(n_tensor)])]
    unnamed x110 -> x16, local copies, waits for them, and re-layouts: 13.9 us -> 0.26 us
    ppermute x11, waiting for transfers between devices: 30.3 us -> 22.1 us  [swap_dp(): return lax.ppermute(a, ('dp', 'tensor'), pairs)]
    ppermute x11, starting transfers between devices: 23.7 us -> 19.6 us  [swap_dp(): return lax.ppermute(a, ('dp', 'tensor'), pairs)]
    concatenate x2 -> x0, local copies, waits for them, and re-layouts: 1.84 us -> none  [local(): jnp.concatenate([fc1_bias, swap_core(fc1_bias)]).astype(F32).reshape(1, -1)]
    select_n x1 -> x0, other arithmetic: 1.71 us -> none  [local(): far_y = swap_y(jnp.where(bit0 == 0, out_weight, fc1_weight))]
    ppermute x10 -> x6, waiting for transfers between devices: 1.71 us -> 2.92 us  [swap_core(): return lax.ppermute(a, 'tensor', [(t, t ^ 1) for t in range(n_tensor)])]
    pallas_call x28 -> x30, Pallas kernels: 33.8 us -> 34.4 us  [call(): pl.pallas_call(body, in_specs=[spec(kind) for kind in ins] + [vmem] * len...]
  transfers between devices with their start and end apart: 29 -> 25, of which waited for: 13 -> 15; matrix products, arithmetic and copies ran while one was open for 3% -> 1% of each run, Pallas kernels for 20% -> 25%
where the time goes in v4:
time: 121 us; the launch traced here: 120 us
  waiting for transfers between devices  51.8 us (43%)
  Pallas kernels  34.4 us (28%)
  starting transfers between devices  32 us (26%)
    pallas_call x30, Pallas kernels, call(): pl.pallas_call(body, in_specs=[spec(kind) for kind in ins] + [vmem] * len...  34.4 us
    ppermute x8, waiting for transfers between devices, swap_y(): return lax.ppermute(a, 'tensor', [(t, t ^ 2) for t in range(n_tensor)])  26.8 us
    ppermute x11, waiting for transfers between devices, swap_dp(): return lax.ppermute(a, ('dp', 'tensor'), pairs)  22.1 us
    ppermute x11, starting transfers between devices, swap_dp(): return lax.ppermute(a, ('dp', 'tensor'), pairs)  19.6 us
    ppermute x8, starting transfers between devices, swap_y(): return lax.ppermute(a, 'tensor', [(t, t ^ 2) for t in range(n_tensor)])  11.4 us
    ppermute x6, waiting for transfers between devices, swap_core(): return lax.ppermute(a, 'tensor', [(t, t ^ 1) for t in range(n_tensor)])  2.92 us
  transfers between devices with their start and end apart: 25, of which 15 were waited for; matrix products, arithmetic and copies ran while one was open for 1% of the time, Pallas kernels for 25%

profile of v4, /device:TPU:0, one launch (start us, length us, event | category | flops | bytes accessed | tf_op | source)
XLA Modules:
  0.0 120.4 jit_solution(11510347396313764651)
XLA Ops:
  1.2 0.7 reshape.49
  1.9 3.0 %send_parts.1 = (bf16[192,768]{1,0:T(8,128)(2,1)S(1)}, bf16[592,768]{1,0:T(8,128)(2,1)S(1)}, bf16[256,768]{1,0:T(8,128)(2,1)S(1)}, bf16[256,768]{1,0:T(8,128)(2,...) custom-call(s32[5]{0:T(128)S(1)} %stack.23.refs_0_, ...), custom_call_target="tpu_custom_call" | custom-call | flops 10000000000 | bytes 100000000 | tf_op jit(solution)/shard_map/send_parts/pallas_call | solution.py:139
  4.9 2.7 %collective-permute-start.2 = (bf16[192,768]{1,0:T(8,128)(2,1)S(1)}, bf16[192,768]{1,0:T(8,128)(2,1)S(1)}, u32[]{:S(2)}, u32[]{:S(2)}) collective-permute-start(bf16[192,768]{1,0:T(8,128)(2,1)S(1)} %get-tuple-element.120), channel_id=1, source_target_pairs={{0,2},{1,3},{2,0},{3,1},{4,6},{5,7},{6,4},{7,5},{8,10},{9,11},{10,... | collective-permute-start | bytes 884744 | tf_op jit(solution)/shard_map/ppermute | solution.py:609
  7.8 4.0 %attention_forward.2 = (bf16[256,768]{1,0:T(8,128)(2,1)S(1)}, bf16[384,256]{1,0:T(8,128)(2,1)S(1)}, bf16[384,256]{1,0:T(8,128)(2,1)S(1)}, bf16[256,384]{1,0:T(8,...) custom-call(s32[5]{0:T(128)S(1)} %stack.23.refs_0_, ...), custom_call_target="tpu_custom_call" | custom-call | flops 10000000000 | bytes 100000000 | tf_op jit(solution)/shard_map/attention_forward/pallas_call | solution.py:139
  11.9 3.6 %collective-permute-done.2.refs_0_ = bf16[192,768]{1,0:T(8,128)(2,1)S(1)} collective-permute-done((bf16[192,768]{1,0:T(8,128)(2,1)S(1)}, bf16[192,768]{1,0:T(8,128)(2,1)S(1)}, u32[]{:S(2)}, u32[]{:S(2)}) %collective-permute-start.2) | collective-permute-done | bytes 294944 | tf_op jit(solution)/shard_map/ppermute | solution.py:609
  15.5 2.0 %collective-permute-start.5 = (bf16[192,768]{1,0:T(8,128)(2,1)S(1)}, bf16[192,768]{1,0:T(8,128)(2,1)S(1)}, u32[]{:S(2)}, u32[]{:S(2)}) collective-permute-start(bf16[192,768]{1,0:T(8,128)(2,1)S(1)} %bitcast.23), channel_id=1, source_target_pairs={{0,4},{1,5},{2,6},{3,7},{4,0},{5,1},{6,2},{7,3},{8,12},{9,13},{10,... | collective-permute-start | bytes 884744 | tf_op jit(solution)/shard_map/ppermute | solution.py:617
  17.5 1.5 %collective-permute-start.7 = (bf16[256,1152]{1,0:T(8,128)(2,1)S(1)}, bf16[256,1152]{1,0:T(8,128)(2,1)S(1)}, u32[]{:S(2)}, u32[]{:S(2)}) collective-permute-start(bf16[256,1152]{1,0:T(8,128)(2,1)S(1)} %get-tuple-element.118.refs_1_), channel_id=1, source_target_pairs={{0,2},{1,3},{2,0},{3,1},{4,6},{5,7},{6,4},{7,5},{8,10},{9,11},{10,... | collective-permute-start | bytes 1769480 | tf_op jit(solution)/shard_map/ppermute | solution.py:609
  19.0 4.8 %collective-permute-done.1.refs_3_.refs_0_.refs_4_ = bf16[256,768]{1,0:T(8,128)(2,1)S(1)} collective-permute-done((bf16[256,768]{1,0:T(8,128)(2,1)S(1)}, bf16[256,768]{1,0:T(8,128)(2,1)S(1)}, u32[]{:S(2)}, u32[]{:S(2)}) %collective-permute-start.1) | collective-permute-done | bytes 393248 | tf_op jit(solution)/shard_map/ppermute | solution.py:609
  23.9 3.6 %attention_forward.3 = (bf16[256,768]{1,0:T(8,128)(2,1)S(1)}, bf16[384,256]{1,0:T(8,128)(2,1)S(1)}, bf16[384,256]{1,0:T(8,128)(2,1)S(1)}, bf16[256,384]{1,0:T(8,...) custom-call(s32[5]{0:T(128)S(1)} %stack.23.refs_0_, ...), custom_call_target="tpu_custom_call" | custom-call | flops 10000000000 | bytes 100000000 | tf_op jit(solution)/shard_map/attention_forward/pallas_call | solution.py:139
  27.4 2.0 %collective-permute-start.3 = (bf16[256,384]{1,0:T(8,128)(2,1)S(1)}, bf16[256,384]{1,0:T(8,128)(2,1)S(1)}, u32[]{:S(2)}, u32[]{:S(2)}) collective-permute-start(bf16[256,384]{1,0:T(8,128)(2,1)S(1)} %get-tuple-element.123.refs_1_), channel_id=1, source_target_pairs={{0,2},{1,3},{2,0},{3,1},{4,6},{5,7},{6,4},{7,5},{8,10},{9,11},{10,... | collective-permute-start | bytes 589832 | tf_op jit(solution)/shard_map/ppermute | solution.py:609
  29.9 1.8 %collective-permute-done.6.refs_4_ = bf16[2,192,768]{2,1,0:T(8,128)(2,1)S(1)} collective-permute-done((bf16[2,192,768]{2,1,0:T(8,128)(2,1)S(1)}, bf16[2,192,768]{2,1,0:T(8,128)(2,1)S(1)}, u32[]{:S(2)}, u32[]{:S(2)}) %collective-permute-start.6) | collective-permute-done | bytes 589856 | tf_op jit(solution)/shard_map/ppermute | solution.py:606
  31.7 1.3 %pack_rest.1 = (bf16[768,768]{1,0:T(8,128)(2,1)S(1)}, bf16[768,768]{1,0:T(8,128)(2,1)S(1)}, f32[8,128]{1,0:T(8,128)S(1)}) custom-call(s32[5]{0:T(128)S(1)} %stack.23.refs_0_, bf16[592,768]{1,0:T(8,128)(2,1)S(1)} %get-tuple-element.124.refs_0_.refs_1_.refs_7_.refs_8_, bf16[592,768]{1,0:T(8,128)(2,1)S(1)} %collective-permute-done.4.refs_1_.refs_2_.refs_8_.refs_9_, ...), custom_call_target="tpu_custom_call" | custom-call | flops 10000000000 | bytes 100000000 | tf_op jit(solution)/shard_map/pack_rest/pallas_call | solution.py:139
  33.0 3.5 %collective-permute-done.7.refs_2_.refs_7_.refs_4_ = bf16[256,1152]{1,0:T(8,128)(2,1)S(1)} collective-permute-done((bf16[256,1152]{1,0:T(8,128)(2,1)S(1)}, bf16[256,1152]{1,0:T(8,128)(2,1)S(1)}, u32[]{:S(2)}, u32[]{:S(2)}) %collective-permute-start.7) | collective-permute-done | bytes 589856 | tf_op jit(solution)/shard_map/ppermute | solution.py:609
  36.5 1.2 %feed_forward.2 = (f32[256,768]{1,0:T(8,128)S(1)}, bf16[256,768]{1,0:T(8,128)(2,1)S(1)}, bf16[256,384]{1,0:T(8,128)(2,1)S(1)}, bf16[256,384]{1,0:T(8,128)(2,1)S(1)}, f32[8,128]{1,0:T(8,128)S(1)}) custom-call(bf16[256,768]{1,0:T(8,128)(2,1)S(1)} %collective-permute-done.1.refs_3_.refs_0_.refs_4_, bf16[256,384]{1,0:T(8,128)(2,1)S(1)} %get-tuple-element.123.refs_1_, ...), custom_call_target="tpu_custom_call" | custom-call | flops 10000000000 | bytes 100000000 | tf_op jit(solution)/shard_map/feed_forward/pallas_call | solution.py:139
  37.8 2.7 %collective-permute-done.3.refs_3_ = bf16[256,384]{1,0:T(8,128)(2,1)S(1)} collective-permute-done((bf16[256,384]{1,0:T(8,128)(2,1)S(1)}, bf16[256,384]{1,0:T(8,128)(2,1)S(1)}, u32[]{:S(2)}, u32[]{:S(2)}) %collective-permute-start.3) | collective-permute-done | bytes 196640 | tf_op jit(solution)/shard_map/ppermute | solution.py:609
  40.5 1.2 %feed_forward.3 = (f32[256,768]{1,0:T(8,128)S(1)}, bf16[256,768]{1,0:T(8,128)(2,1)S(1)}, bf16[256,384]{1,0:T(8,128)(2,1)S(1)}, bf16[256,384]{1,0:T(8,128)(2,1)S(1)}, f32[8,128]{1,0:T(8,128)S(1)}) custom-call(bf16[256,768]{1,0:T(8,128)(2,1)S(1)} %get-tuple-element.113.refs_3_.refs_0_, bf16[256,1152]{1,0:T(8,128)(2,1)S(1)} %get-tuple-element.118.refs_1_, ...), custom_call_target="tpu_custom_call" | custom-call | flops 10000000000 | bytes 100000000 | tf_op jit(solution)/shard_map/feed_forward/pallas_call | solution.py:139
  41.7 1.8 %collective-permute-start.9 = (bf16[256,384]{1,0:T(8,128)(2,1)S(1)}, bf16[256,384]{1,0:T(8,128)(2,1)S(1)}, u32[]{:S(2)}, u32[]{:S(2)}) collective-permute-start(bf16[256,384]{1,0:T(8,128)(2,1)S(1)} %get-tuple-element.140.refs_2_.refs_0_), channel_id=1, source_target_pairs={{0,2},{1,3},{2,0},{3,1},{4,6},{5,7},{6,4},{7,5},{8,10},{9,11},{10,... | collective-permute-start | bytes 589832 | tf_op jit(solution)/shard_map/ppermute | solution.py:609
  43.8 0.8 feed_grads.1
  44.7 7.9 %collective-permute-done.8.refs_1_ = bf16[256,384]{1,0:T(8,128)(2,1)S(1)} collective-permute-done((bf16[256,384]{1,0:T(8,128)(2,1)S(1)}, bf16[256,384]{1,0:T(8,128)(2,1)S(1)}, u32[]{:S(2)}, u32[]{:S(2)}) %collective-permute-start.8) | collective-permute-done | bytes 196640 | tf_op jit(solution)/shard_map/ppermute | solution.py:609
  52.7 2.4 %attention_backward.2 = (bf16[256,768]{1,0:T(8,128)(2,1)S(1)}, bf16[1152,256]{1,0:T(8,128)(2,1)S(1)}, f32[256,768]{1,0:T(8,128)S(1)}, f32[8,768]{1,0:T(8,128)S(1)}, f32[8,128]{1,0:T(8,128)S(1)}) custom-call(bf16[256,384]{1,0:T(8,128)(2,1)S(1)} %get-tuple-element.140.refs_2_.refs_0_, bf16[256,384]{1,0:T(8,128)(2,1)S(1)} %collective-permute-done.8.refs_1_, ...), custom_call_target="tpu_custom_call" | custom-call | flops 10000000000 | bytes 100000000 | tf_op jit(solution)/shard_map/attention_backward/pallas_call | solution.py:139
  55.7 1.6 %collective-permute-start.12 = (bf16[192,768]{1,0:T(8,128)(2,1)S(1)}, bf16[192,768]{1,0:T(8,128)(2,1)S(1)}, u32[]{:S(2)}, u32[]{:S(2)}) collective-permute-start(bf16[192,768]{1,0:T(8,128)(2,1)S(1)} %get-tuple-element.170), channel_id=1, source_target_pairs={{0,4},{1,9},{2,6},{3,11},{4,0},{5,13},{6,2},{7,15},{8,12},{9,1},{1... | collective-permute-start | bytes 884744 | tf_op jit(solution)/shard_map/ppermute | solution.py:617
  57.3 2.4 %attention_backward.3 = (bf16[256,768]{1,0:T(8,128)(2,1)S(1)}, bf16[1152,256]{1,0:T(8,128)(2,1)S(1)}, f32[8,128]{1,0:T(8,128)S(1)}) custom-call(bf16[256,384]{1,0:T(8,128)(2,1)S(1)} %get-tuple-element.141.refs_3_.refs_0_, bf16[256,384]{1,0:T(8,128)(2,1)S(1)} %collective-permute-done.9.refs_1_, ...), custom_call_target="tpu_custom_call" | custom-call | flops 10000000000 | bytes 100000000 | tf_op jit(solution)/shard_map/attention_backward/pallas_call | solution.py:139
  59.7 1.4 %weight_grads.1 = (bf16[4,192,768]{2,1,0:T(8,128)(2,1)S(1)}, bf16[4,192,768]{2,1,0:T(8,128)(2,1)S(1)}, f32[8,128]{1,0:T(8,128)S(1)}) custom-call(bf16[1152,256]{1,0:T(8,128)(2,1)S(1)} %get-tuple-element.150.refs_0_.refs_4_.refs_8_, bf16[1152,256]{1,0:T(8,128)(2,1)S(1)} %get-tuple-element.160.refs_1_.refs_5_.refs_9_, ...), custom_call_target="tpu_custom_call" | custom-call | flops 10000000000 | bytes 100000000 | tf_op jit(solution)/shard_map/weight_grads/pallas_call | solution.py:139
  61.2 1.3 %collective-permute-done.12 = bf16[192,768]{1,0:T(8,128)(2,1)S(1)} collective-permute-done((bf16[192,768]{1,0:T(8,128)(2,1)S(1)}, bf16[192,768]{1,0:T(8,128)(2,1)S(1)}, u32[]{:S(2)}, u32[]{:S(2)}) %collective-permute-start.12) | collective-permute-done | bytes 294944 | tf_op jit(solution)/shard_map/ppermute | solution.py:617
  63.1 1.7 %collective-permute-start.14 = (bf16[96,768]{1,0:T(8,128)(2,1)S(1)}, bf16[96,768]{1,0:T(8,128)(2,1)S(1)}, u32[]{:S(2)}, u32[]{:S(2)}) collective-permute-start(bf16[96,768]{1,0:T(8,128)(2,1)S(1)} %get-tuple-element.174), channel_id=1, source_target_pairs={{0,8},{1,5},{2,10},{3,7},{4,12},{5,1},{6,14},{7,3},{8,0},{9,13},{1... | collective-permute-start | bytes 442376 | tf_op jit(solution)/shard_map/ppermute | solution.py:617
  65.4 1.6 %collective-permute-start.13 = (bf16[384,768]{1,0:T(8,128)(2,1)S(1)}, bf16[384,768]{1,0:T(8,128)(2,1)S(1)}, u32[]{:S(2)}, u32[]{:S(2)}) collective-permute-start(bf16[384,768]{1,0:T(8,128)(2,1)S(1)} %get-tuple-element.173), channel_id=1, source_target_pairs={{0,4},{1,9},{2,6},{3,11},{4,0},{5,13},{6,2},{7,15},{8,12},{9,1},{1... | collective-permute-start | bytes 1769480 | tf_op jit(solution)/shard_map/ppermute | solution.py:617
  67.0 1.3 %input_grads.1 = (f32[256,768]{1,0:T(8,128)S(1)}, bf16[272,768]{1,0:T(8,128)(2,1)S(1)}, f32[8,128]{1,0:T(8,128)S(1)}) custom-call(bf16[1152,256]{1,0:T(8,128)(2,1)S(1)} %get-tuple-element.150.refs_0_.refs_4_.refs_8_, bf16[1152,256]{1,0:T(8,128)(2,1)S(1)} %get-tuple-element.160.refs_1_.refs_5_.refs_9_, bf16[3,384,768]{2,1,0:T(8,128)(2,1)S(1)} %copy-done.3, ...), custom_call_target="tpu_custom_call" | custom-call | flops 10000000000 | bytes 100000000 | tf_op jit(solution)/shard_map/input_grads/pallas_call | solution.py:139
  68.3 0.8 collective-permute-done.14.refs_4_
  69.8 3.7 %collective-permute-start.17 = (bf16[96,768]{1,0:T(8,128)(2,1)S(1)}, bf16[96,768]{1,0:T(8,128)(2,1)S(1)}, u32[]{:S(2)}, u32[]{:S(2)}) collective-permute-start(bf16[96,768]{1,0:T(8,128)(2,1)S(1)} %get-tuple-element.182.refs_0_), channel_id=1, source_target_pairs={{0,24},{1,25},{2,26},{3,27},{4,28},{5,29},{6,30},{7,31},{8,16},{9,... | collective-permute-start | bytes 442376 | tf_op jit(solution)/shard_map/ppermute | solution.py:617
  73.5 1.5 %collective-permute-start.16 = (bf16[272,768]{1,0:T(8,128)(2,1)S(1)}, bf16[272,768]{1,0:T(8,128)(2,1)S(1)}, u32[]{:S(2)}, u32[]{:S(2)}) collective-permute-start(bf16[272,768]{1,0:T(8,128)(2,1)S(1)} %get-tuple-element.181.refs_0_), channel_id=1, source_target_pairs={{0,2},{1,3},{2,0},{3,1},{4,6},{5,7},{6,4},{7,5},{8,10},{9,11},{10,... | collective-permute-start | bytes 1253384 | tf_op jit(solution)/shard_map/ppermute | solution.py:609
  75.3 0.7 sum_quarter.6
  76.0 0.9 collective-permute-start.15
  76.9 1.5 %collective-permute-done.17.refs_1_ = bf16[96,768]{1,0:T(8,128)(2,1)S(1)} collective-permute-done((bf16[96,768]{1,0:T(8,128)(2,1)S(1)}, bf16[96,768]{1,0:T(8,128)(2,1)S(1)}, u32[]{:S(2)}, u32[]{:S(2)}) %collective-permute-start.17) | collective-permute-done | bytes 147488 | tf_op jit(solution)/shard_map/ppermute | solution.py:617
  78.5 4.2 %collective-permute-done.16.refs_1_.refs_3_ = bf16[272,768]{1,0:T(8,128)(2,1)S(1)} collective-permute-done((bf16[272,768]{1,0:T(8,128)(2,1)S(1)}, bf16[272,768]{1,0:T(8,128)(2,1)S(1)}, u32[]{:S(2)}, u32[]{:S(2)}) %collective-permute-start.16) | collective-permute-done | bytes 417824 | tf_op jit(solution)/shard_map/ppermute | solution.py:609
  82.9 1.1 collective-permute-done.18.refs_6_
  84.0 0.8 sum_quarter.7
  85.7 1.7 %collective-permute-start.22 = (bf16[208,768]{1,0:T(8,128)(2,1)S(1)}, bf16[208,768]{1,0:T(8,128)(2,1)S(1)}, u32[]{:S(2)}, u32[]{:S(2)}) collective-permute-start(bf16[208,768]{1,0:T(8,128)(2,1)S(1)} %get-tuple-element.196.refs_0_), channel_id=1, source_target_pairs={{0,24},{1,25},{2,26},{3,27},{4,28},{5,29},{6,30},{7,31},{8,16},{9,... | collective-permute-start | bytes 958472 | tf_op jit(solution)/shard_map/ppermute | solution.py:617
  87.4 1.3 %input_norm.1 = (bf16[256,768]{1,0:T(8,128)(2,1)}, f32[8,128]{1,0:T(8,128)S(1)}) custom-call(bf16[256,768]{1,0:T(8,128)(2,1)S(1)} %get-tuple-element.113.refs_3_.refs_0_, f32[768]{0:T(1024)S(1)} %copy-done.7, f32[256,768]{1,0:T(8,128)S(1)} %get-tuple-element.191.refs_2_, bf16[272,768]{1,0:T(8,128)(2,1)S(1)} %collective-permute-done.16.refs_1_.refs_3_, ...), custom_call_target="tpu_custom_call" | custom-call | flops 10000000000 | bytes 100000000 | tf_op jit(solution)/shard_map/input_norm/pallas_call | solution.py:139
  88.8 1.1 collective-permute-start.21
  89.9 1.5 %collective-permute-start.19 = (bf16[256,768]{1,0:T(8,128)(2,1)S(1)}, bf16[256,768]{1,0:T(8,128)(2,1)S(1)}, u32[]{:S(2)}, u32[]{:S(2)}) collective-permute-start(bf16[256,768]{1,0:T(8,128)(2,1)S(1)} %get-tuple-element.189), channel_id=1, source_target_pairs={{0,2},{1,3},{2,0},{3,1},{4,6},{5,7},{6,4},{7,5},{8,10},{9,11},{10,... | collective-permute-start | bytes 1179656 | tf_op jit(solution)/shard_map/ppermute | solution.py:609
  91.4 6.5 %collective-permute-done.22.refs_1_ = bf16[208,768]{1,0:T(8,128)(2,1)S(1)} collective-permute-done((bf16[208,768]{1,0:T(8,128)(2,1)S(1)}, bf16[208,768]{1,0:T(8,128)(2,1)S(1)}, u32[]{:S(2)}, u32[]{:S(2)}) %collective-permute-start.22) | collective-permute-done | bytes 319520 | tf_op jit(solution)/shard_map/ppermute | solution.py:617
  98.0 4.3 %collective-permute-start.23 = (bf16[208,768]{1,0:T(8,128)(2,1)S(1)}, bf16[208,768]{1,0:T(8,128)(2,1)S(1)}, u32[]{:S(2)}, u32[]{:S(2)}) collective-permute-start(bf16[208,768]{1,0:T(8,128)(2,1)S(1)} %get-tuple-element.202.refs_0_), channel_id=1, source_target_pairs={{0,8},{1,5},{2,10},{3,7},{4,12},{5,1},{6,14},{7,3},{8,0},{9,13},{1... | collective-permute-start | bytes 958472 | tf_op jit(solution)/shard_map/ppermute | solution.py:617
  102.3 1.7 %place_sums.2 = (f32[192,768]{1,0:T(8,128)}, f32[192,768]{1,0:T(8,128)}, f32[8,128]{1,0:T(8,128)S(1)}) custom-call(s32[5]{0:T(128)S(1)} %stack.23.refs_0_, bf16[192,768]{1,0:T(8,128)(2,1)S(1)} %get-tuple-element.195.refs_1_, bf16[192,768]{1,0:T(8,128)(2,1)S(1)} %collective-permute-done.21.refs_2_, f32[8,128]{1,0:T(8,128)S(1)} %get-tuple-element.198.refs_3_), custom_call_target="tpu_custom_call" | custom-call | flops 10000000000 | bytes 100000000 | tf_op jit(solution)/shard_map/place_sums/pallas_call | solution.py:139
  104.0 0.8 add_result.1
  104.8 2.4 %collective-permute-done.23.refs_1_ = bf16[208,768]{1,0:T(8,128)(2,1)S(1)} collective-permute-done((bf16[208,768]{1,0:T(8,128)(2,1)S(1)}, bf16[208,768]{1,0:T(8,128)(2,1)S(1)}, u32[]{:S(2)}, u32[]{:S(2)}) %collective-permute-start.23) | collective-permute-done | bytes 319520 | tf_op jit(solution)/shard_map/ppermute | solution.py:617
  107.3 0.9 collective-permute-start.24
  108.2 9.3 %collective-permute-done.24.refs_2_ = bf16[400,768]{1,0:T(8,128)(2,1)S(1)} collective-permute-done((bf16[400,768]{1,0:T(8,128)(2,1)S(1)}, bf16[400,768]{1,0:T(8,128)(2,1)S(1)}, u32[]{:S(2)}, u32[]{:S(2)}) %collective-permute-start.24) | collective-permute-done | bytes 614432 | tf_op jit(solution)/shard_map/ppermute | solution.py:617
  117.5 2.7 %place_sums.3 = (f32[3,192,768]{2,1,0:T(8,128)}, f32[192,768]{1,0:T(8,128)}, f32[768]{0:T(1024)}, f32[768]{0:T(1024)}, f32[768]{0:T(1024)}, /*index=5*/f32[768]{0:T(1024)}, f32[192]{0:T(256)}, f32[8,128]{1,0:T(8,128)}) custom-call(s32[5]{0:T(128)S(1)} %stack.23.refs_0_, bf16[400,768]{1,0:T(8,128)(2,1)S(1)} %get-tuple-element.204.refs_1_, ...), custom_call_target="tpu_custom_call" | custom-call | flops 10000000000 | bytes 100000000 | tf_op jit(solution)/shard_map/place_sums/pallas_call | solution.py:139
  (51 shorter events, 5.7 us)
Async XLA Ops:
  0.6 7.2 %collective-permute-start = (bf16[3,192,768]{2,1,0:T(8,128)(2,1)}, bf16[3,192,768]{2,1,0:T(8,128)(2,1)S(1)}, u32[]{:S(2)}, u32[]{:S(2)}) collective-permute-start(bf16[3,192,768]{2,1,0:T(8,128)(2,1)} %refs_6_.3), channel_id=1, source_target_pairs={{0,1},{1,0},{2,3},{3,2},{4,5},{5,4},{6,7},{7,6},{8,9},{9,8},{10,11... | collective-permute-start | bytes 2654216 | tf_op jit(solution)/shard_map/ppermute | solution.py:606
  4.9 19.0 %copy-start.6 = (f32[768]{0:T(1024)}, f32[768]{0:T(1024)S(1)}, u32[]{:S(2)}) copy-start(f32[768]{0:T(1024)S(1)} %get-tuple-element.114.refs_4_.refs_1_) | copy-start | bytes 9220
  4.9 10.5 %collective-permute-start.2 = (bf16[192,768]{1,0:T(8,128)(2,1)S(1)}, bf16[192,768]{1,0:T(8,128)(2,1)S(1)}, u32[]{:S(2)}, u32[]{:S(2)}) collective-permute-start(bf16[192,768]{1,0:T(8,128)(2,1)S(1)} %get-tuple-element.120), channel_id=1, source_target_pairs={{0,2},{1,3},{2,0},{3,1},{4,6},{5,7},{6,4},{7,5},{8,10},{9,11},{10,... | collective-permute-start | bytes 884744 | tf_op jit(solution)/shard_map/ppermute | solution.py:609
  7.6 16.3 %collective-permute-start.1 = (bf16[256,768]{1,0:T(8,128)(2,1)S(1)}, bf16[256,768]{1,0:T(8,128)(2,1)S(1)}, u32[]{:S(2)}, u32[]{:S(2)}) collective-permute-start(bf16[256,768]{1,0:T(8,128)(2,1)S(1)} %get-tuple-element.113.refs_3_.refs_0_), channel_id=1, source_target_pairs={{0,2},{1,3},{2,0},{3,1},{4,6},{5,7},{6,4},{7,5},{8,10},{9,11},{10,... | collective-permute-start | bytes 1179656 | tf_op jit(solution)/shard_map/ppermute | solution.py:609
  7.7 22.0 %collective-permute-start.4 = (bf16[592,768]{1,0:T(8,128)(2,1)S(1)}, bf16[592,768]{1,0:T(8,128)(2,1)S(1)}, u32[]{:S(2)}, u32[]{:S(2)}) collective-permute-start(bf16[592,768]{1,0:T(8,128)(2,1)S(1)} %get-tuple-element.124.refs_0_.refs_1_.refs_7_.refs_8_), channel_id=1, source_target_pairs={{0,1},{1,0},{2,3},{3,2},{4,5},{5,4},{6,7},{7,6},{8,9},{9,8},{10,11... | collective-permute-start | bytes 2727944 | tf_op jit(solution)/shard_map/ppermute | solution.py:606
  11.8 12.0 %copy-start.2 = (bf16[3,384,768]{2,1,0:T(8,128)(2,1)}, bf16[3,384,768]{2,1,0:T(8,128)(2,1)S(1)}, u32[]{:S(2)}) copy-start(bf16[3,384,768]{2,1,0:T(8,128)(2,1)S(1)} %get-tuple-element.119.refs_6_.refs_2_) | copy-start | bytes 5308420
  15.5 13.9 %collective-permute-start.5 = (bf16[192,768]{1,0:T(8,128)(2,1)S(1)}, bf16[192,768]{1,0:T(8,128)(2,1)S(1)}, u32[]{:S(2)}, u32[]{:S(2)}) collective-permute-start(bf16[192,768]{1,0:T(8,128)(2,1)S(1)} %bitcast.23), channel_id=1, source_target_pairs={{0,4},{1,5},{2,6},{3,7},{4,0},{5,1},{6,2},{7,3},{8,12},{9,13},{10,... | collective-permute-start | bytes 884744 | tf_op jit(solution)/shard_map/ppermute | solution.py:617
  17.5 19.0 %collective-permute-start.7 = (bf16[256,1152]{1,0:T(8,128)(2,1)S(1)}, bf16[256,1152]{1,0:T(8,128)(2,1)S(1)}, u32[]{:S(2)}, u32[]{:S(2)}) collective-permute-start(bf16[256,1152]{1,0:T(8,128)(2,1)S(1)} %get-tuple-element.118.refs_1_), channel_id=1, source_target_pairs={{0,2},{1,3},{2,0},{3,1},{4,6},{5,7},{6,4},{7,5},{8,10},{9,11},{10,... | collective-permute-start | bytes 1769480 | tf_op jit(solution)/shard_map/ppermute | solution.py:609
  23.9 12.6 %copy-start = (bf16[256,768]{1,0:T(8,128)(2,1)}, bf16[256,768]{1,0:T(8,128)(2,1)S(1)}, u32[]{:S(2)}) copy-start(bf16[256,768]{1,0:T(8,128)(2,1)S(1)} %collective-permute-done.1.refs_3_.refs_0_.refs_4_) | copy-start | bytes 1179652
  27.4 13.0 %collective-permute-start.3 = (bf16[256,384]{1,0:T(8,128)(2,1)S(1)}, bf16[256,384]{1,0:T(8,128)(2,1)S(1)}, u32[]{:S(2)}, u32[]{:S(2)}) collective-permute-start(bf16[256,384]{1,0:T(8,128)(2,1)S(1)} %get-tuple-element.123.refs_1_), channel_id=1, source_target_pairs={{0,2},{1,3},{2,0},{3,1},{4,6},{5,7},{6,4},{7,5},{8,10},{9,11},{10,... | collective-permute-start | bytes 589832 | tf_op jit(solution)/shard_map/ppermute | solution.py:609
  29.6 2.1 %collective-permute-start.6 = (bf16[2,192,768]{2,1,0:T(8,128)(2,1)S(1)}, bf16[2,192,768]{2,1,0:T(8,128)(2,1)S(1)}, u32[]{:S(2)}, u32[]{:S(2)}) collective-permute-start(bf16[2,192,768]{2,1,0:T(8,128)(2,1)S(1)} %get-tuple-element.127.refs_3_), channel_id=1, source_target_pairs={{0,1},{1,0},{2,3},{3,2},{4,5},{5,4},{6,7},{7,6},{8,9},{9,8},{10,11... | collective-permute-start | bytes 1769480 | tf_op jit(solution)/shard_map/ppermute | solution.py:606
  29.9 10.6 %copy-start.4 = (bf16[384,768]{1,0:T(8,128)(2,1)}, bf16[384,768]{1,0:T(8,128)(2,1)S(1)}, u32[]{:S(2)}) copy-start(bf16[384,768]{1,0:T(8,128)(2,1)S(1)} %get-tuple-element.134.refs_9_.refs_10_.refs_2_) | copy-start | bytes 1769476
  41.7 15.5 %collective-permute-start.9 = (bf16[256,384]{1,0:T(8,128)(2,1)S(1)}, bf16[256,384]{1,0:T(8,128)(2,1)S(1)}, u32[]{:S(2)}, u32[]{:S(2)}) collective-permute-start(bf16[256,384]{1,0:T(8,128)(2,1)S(1)} %get-tuple-element.140.refs_2_.refs_0_), channel_id=1, source_target_pairs={{0,2},{1,3},{2,0},{3,1},{4,6},{5,7},{6,4},{7,5},{8,10},{9,11},{10,... | collective-permute-start | bytes 589832 | tf_op jit(solution)/shard_map/ppermute | solution.py:609
  43.5 9.1 %collective-permute-start.8 = (bf16[256,384]{1,0:T(8,128)(2,1)S(1)}, bf16[256,384]{1,0:T(8,128)(2,1)S(1)}, u32[]{:S(2)}, u32[]{:S(2)}) collective-permute-start(bf16[256,384]{1,0:T(8,128)(2,1)S(1)} %get-tuple-element.141.refs_3_.refs_0_), channel_id=1, source_target_pairs={{0,2},{1,3},{2,0},{3,1},{4,6},{5,7},{6,4},{7,5},{8,10},{9,11},{10,... | collective-permute-start | bytes 589832 | tf_op jit(solution)/shard_map/ppermute | solution.py:609
  44.7 10.4 %collective-permute-start.10 = (bf16[2,192,768]{2,1,0:T(8,128)(2,1)S(1)}, bf16[2,192,768]{2,1,0:T(8,128)(2,1)S(1)}, u32[]{:S(2)}, u32[]{:S(2)}) collective-permute-start(bf16[2,192,768]{2,1,0:T(8,128)(2,1)S(1)} %get-tuple-element.157), channel_id=1, source_target_pairs={{0,1},{1,0},{2,3},{3,2},{4,5},{5,4},{6,7},{7,6},{8,9},{9,8},{10,11... | collective-permute-start | bytes 1769480 | tf_op jit(solution)/shard_map/ppermute | solution.py:606
  55.7 6.8 %collective-permute-start.12 = (bf16[192,768]{1,0:T(8,128)(2,1)S(1)}, bf16[192,768]{1,0:T(8,128)(2,1)S(1)}, u32[]{:S(2)}, u32[]{:S(2)}) collective-permute-start(bf16[192,768]{1,0:T(8,128)(2,1)S(1)} %get-tuple-element.170), channel_id=1, source_target_pairs={{0,4},{1,9},{2,6},{3,11},{4,0},{5,13},{6,2},{7,15},{8,12},{9,1},{1... | collective-permute-start | bytes 884744 | tf_op jit(solution)/shard_map/ppermute | solution.py:617
  61.1 3.6 %collective-permute-start.11 = (bf16[4,192,768]{2,1,0:T(8,128)(2,1)S(1)}, bf16[4,192,768]{2,1,0:T(8,128)(2,1)S(1)}, u32[]{:S(2)}, u32[]{:S(2)}) collective-permute-start(bf16[4,192,768]{2,1,0:T(8,128)(2,1)S(1)} %get-tuple-element.169), channel_id=1, source_target_pairs={{0,1},{1,0},{2,3},{3,2},{4,5},{5,4},{6,7},{7,6},{8,9},{9,8},{10,11... | collective-permute-start | bytes 3538952 | tf_op jit(solution)/shard_map/ppermute | solution.py:606
  63.1 6.1 %collective-permute-start.14 = (bf16[96,768]{1,0:T(8,128)(2,1)S(1)}, bf16[96,768]{1,0:T(8,128)(2,1)S(1)}, u32[]{:S(2)}, u32[]{:S(2)}) collective-permute-start(bf16[96,768]{1,0:T(8,128)(2,1)S(1)} %get-tuple-element.174), channel_id=1, source_target_pairs={{0,8},{1,5},{2,10},{3,7},{4,12},{5,1},{6,14},{7,3},{8,0},{9,13},{1... | collective-permute-start | bytes 442376 | tf_op jit(solution)/shard_map/ppermute | solution.py:617
  64.8 2.2 %copy-start.1 = (bf16[256,768]{1,0:T(8,128)(2,1)S(1)}, bf16[256,768]{1,0:T(8,128)(2,1)}, u32[]{:S(2)}) copy-start(bf16[256,768]{1,0:T(8,128)(2,1)} %copy-done) | copy-start | bytes 1179652
  64.8 2.2 %copy-start.3 = (bf16[3,384,768]{2,1,0:T(8,128)(2,1)S(1)}, bf16[3,384,768]{2,1,0:T(8,128)(2,1)}, u32[]{:S(2)}) copy-start(bf16[3,384,768]{2,1,0:T(8,128)(2,1)} %copy-done.2) | copy-start | bytes 5308420
  65.4 9.9 %collective-permute-start.13 = (bf16[384,768]{1,0:T(8,128)(2,1)S(1)}, bf16[384,768]{1,0:T(8,128)(2,1)S(1)}, u32[]{:S(2)}, u32[]{:S(2)}) collective-permute-start(bf16[384,768]{1,0:T(8,128)(2,1)S(1)} %get-tuple-element.173), channel_id=1, source_target_pairs={{0,4},{1,9},{2,6},{3,11},{4,0},{5,13},{6,2},{7,15},{8,12},{9,1},{1... | collective-permute-start | bytes 1769480 | tf_op jit(solution)/shard_map/ppermute | solution.py:617
  69.8 8.7 %collective-permute-start.17 = (bf16[96,768]{1,0:T(8,128)(2,1)S(1)}, bf16[96,768]{1,0:T(8,128)(2,1)S(1)}, u32[]{:S(2)}, u32[]{:S(2)}) collective-permute-start(bf16[96,768]{1,0:T(8,128)(2,1)S(1)} %get-tuple-element.182.refs_0_), channel_id=1, source_target_pairs={{0,24},{1,25},{2,26},{3,27},{4,28},{5,29},{6,30},{7,31},{8,16},{9,... | collective-permute-start | bytes 442376 | tf_op jit(solution)/shard_map/ppermute | solution.py:617
  73.5 9.2 %collective-permute-start.16 = (bf16[272,768]{1,0:T(8,128)(2,1)S(1)}, bf16[272,768]{1,0:T(8,128)(2,1)S(1)}, u32[]{:S(2)}, u32[]{:S(2)}) collective-permute-start(bf16[272,768]{1,0:T(8,128)(2,1)S(1)} %get-tuple-element.181.refs_0_), channel_id=1, source_target_pairs={{0,2},{1,3},{2,0},{3,1},{4,6},{5,7},{6,4},{7,5},{8,10},{9,11},{10,... | collective-permute-start | bytes 1253384 | tf_op jit(solution)/shard_map/ppermute | solution.py:609
  76.0 8.0 %collective-permute-start.15 = (bf16[192,768]{1,0:T(8,128)(2,1)S(1)}, bf16[192,768]{1,0:T(8,128)(2,1)S(1)}, u32[]{:S(2)}, u32[]{:S(2)}) collective-permute-start(bf16[192,768]{1,0:T(8,128)(2,1)S(1)} %get-tuple-element.180), channel_id=1, source_target_pairs={{0,8},{1,5},{2,10},{3,7},{4,12},{5,1},{6,14},{7,3},{8,0},{9,13},{1... | collective-permute-start | bytes 884744 | tf_op jit(solution)/shard_map/ppermute | solution.py:617
  82.7 1.3 %collective-permute-start.18 = (bf16[16,768]{1,0:T(8,128)(2,1)S(1)}, bf16[16,768]{1,0:T(8,128)(2,1)S(1)}, u32[]{:S(2)}, u32[]{:S(2)}) collective-permute-start(bf16[16,768]{1,0:T(8,128)(2,1)S(1)} %get-tuple-element.185.refs_5_), channel_id=1, source_target_pairs={{0,1},{1,0},{2,3},{3,2},{4,5},{5,4},{6,7},{7,6},{8,9},{9,8},{10,11... | collective-permute-start | bytes 73736 | tf_op jit(solution)/shard_map/ppermute | solution.py:606
  82.8 5.9 %collective-permute-start.20 = (bf16[96,768]{1,0:T(8,128)(2,1)S(1)}, bf16[96,768]{1,0:T(8,128)(2,1)S(1)}, u32[]{:S(2)}, u32[]{:S(2)}) collective-permute-start(bf16[96,768]{1,0:T(8,128)(2,1)S(1)} %get-tuple-element.190.refs_0_), channel_id=1, source_target_pairs={{0,8},{1,5},{2,10},{3,7},{4,12},{5,1},{6,14},{7,3},{8,0},{9,13},{1... | collective-permute-start | bytes 442376 | tf_op jit(solution)/shard_map/ppermute | solution.py:617
  84.0 1.1 copy-start.5
  85.1 2.3 %copy-start.7 = (f32[768]{0:T(1024)S(1)}, f32[768]{0:T(1024)}, u32[]{:S(2)}) copy-start(f32[768]{0:T(1024)} %copy-done.6) | copy-start | bytes 9220
  85.7 12.3 %collective-permute-start.22 = (bf16[208,768]{1,0:T(8,128)(2,1)S(1)}, bf16[208,768]{1,0:T(8,128)(2,1)S(1)}, u32[]{:S(2)}, u32[]{:S(2)}) collective-permute-start(bf16[208,768]{1,0:T(8,128)(2,1)S(1)} %get-tuple-element.196.refs_0_), channel_id=1, source_target_pairs={{0,24},{1,25},{2,26},{3,27},{4,28},{5,29},{6,30},{7,31},{8,16},{9,... | collective-permute-start | bytes 958472 | tf_op jit(solution)/shard_map/ppermute | solution.py:617
  88.8 13.5 %collective-permute-start.21 = (bf16[192,768]{1,0:T(8,128)(2,1)S(1)}, bf16[192,768]{1,0:T(8,128)(2,1)S(1)}, u32[]{:S(2)}, u32[]{:S(2)}) collective-permute-start(bf16[192,768]{1,0:T(8,128)(2,1)S(1)} %get-tuple-element.195.refs_1_), channel_id=1, source_target_pairs={{0,4},{1,9},{2,6},{3,11},{4,0},{5,13},{6,2},{7,15},{8,12},{9,1},{1... | collective-permute-start | bytes 884744 | tf_op jit(solution)/shard_map/ppermute | solution.py:617
  89.9 14.0 %collective-permute-start.19 = (bf16[256,768]{1,0:T(8,128)(2,1)S(1)}, bf16[256,768]{1,0:T(8,128)(2,1)S(1)}, u32[]{:S(2)}, u32[]{:S(2)}) collective-permute-start(bf16[256,768]{1,0:T(8,128)(2,1)S(1)} %get-tuple-element.189), channel_id=1, source_target_pairs={{0,2},{1,3},{2,0},{3,1},{4,6},{5,7},{6,4},{7,5},{8,10},{9,11},{10,... | collective-permute-start | bytes 1179656 | tf_op jit(solution)/shard_map/ppermute | solution.py:609
  98.0 9.2 %collective-permute-start.23 = (bf16[208,768]{1,0:T(8,128)(2,1)S(1)}, bf16[208,768]{1,0:T(8,128)(2,1)S(1)}, u32[]{:S(2)}, u32[]{:S(2)}) collective-permute-start(bf16[208,768]{1,0:T(8,128)(2,1)S(1)} %get-tuple-element.202.refs_0_), channel_id=1, source_target_pairs={{0,8},{1,5},{2,10},{3,7},{4,12},{5,1},{6,14},{7,3},{8,0},{9,13},{1... | collective-permute-start | bytes 958472 | tf_op jit(solution)/shard_map/ppermute | solution.py:617
  107.3 10.2 %collective-permute-start.24 = (bf16[400,768]{1,0:T(8,128)(2,1)S(1)}, bf16[400,768]{1,0:T(8,128)(2,1)S(1)}, u32[]{:S(2)}, u32[]{:S(2)}) collective-permute-start(bf16[400,768]{1,0:T(8,128)(2,1)S(1)} %get-tuple-element.204.refs_1_), channel_id=1, source_target_pairs={{0,4},{1,9},{2,6},{3,11},{4,0},{5,13},{6,2},{7,15},{8,12},{9,1},{1... | collective-permute-start | bytes 1843208 | tf_op jit(solution)/shard_map/ppermute | solution.py:617

commit v5 on v4

--- a/solution.py
+++ b/solution.py
@@ -169,7 +169,7 @@
         copy.wait()
 
 
-def attention(chain, bits, place, nodes, edges, x, gain, bias, w, g=None):
+def attention(chain, bits, place, nodes, edges, x, gain, bias, w, g=None, near=()):
     rows, d = x.shape
     width = w.shape[1] if g is None else 2 * w[0].shape[1]
     shard = width // 2
@@ -179,8 +179,14 @@
     def kernel(io, bits_ref, nodes_ref, edges_ref, x_ref, gain_ref, bias_ref, *refs):
         started = []
         if g is None:
-            w_ref, *refs = refs
+            w_ref, near0, near1, *refs, wo_ref, fc1_ref, fc2_ref, sems = refs
             a1_ref, qt_ref, kt_ref, v_ref, p_ref, ot_ref, o_ref = refs
+            pairs_w = []
+            for at, ref in enumerate((near0, near1)):
+                for c, out in enumerate((wo_ref, fc1_ref, fc2_ref)):
+                    part = ref.at[c * shard : (c + 1) * shard]
+                    pairs_w.append((part, out.at[at * shard : (at + 1) * shard]))
+            started = copies(sems, pairs_w)
         else:
             own, got, g_ref, *refs, w_ref, sems = refs
             a1_ref, qt_ref, kt_ref, v_ref, p_ref, ot_ref, o_ref = refs
@@ -189,7 +195,8 @@
         xh, _ = normalise(x_ref[...].astype(F32))
         a1 = (xh * gain_ref[...][None, :] + bias_ref[...][None, :]).astype(BF16)
         a1_ref[...] = a1
-        finish(started[:2])
+        if g is not None:
+            finish(started[:2])
         qt = dot_nt(w_ref[0], a1).astype(BF16)
         keys = dot_nt(a1, w_ref[1]).astype(BF16)
         vt = dot_nt(w_ref[2], a1).astype(BF16)
@@ -219,7 +226,7 @@
         o_ref[:, o_ref.shape[1] - width :] = ot_ref[...].T
         kt_ref[...] = dot_nt(w_ref[1], a1).astype(BF16)
         v_ref[...] = dot_nt(a1, w_ref[2]).astype(BF16)
-        finish(started[2:])
+        finish(started if g is None else started[2:])
 
     outs = [
         bf16(rows, d), bf16(width, rows), bf16(width, rows), bf16(rows, width),
@@ -228,7 +235,8 @@
     args = (bits, nodes, edges, x, gain, bias)
     if g is None:
         return chain.call(
-            kernel, "attention_forward", (*args, w), [*outs, bf16(rows, width)], "sccvvvv-vvvvvvv"
+            kernel, "attention_forward", (*args, w, *near), [*outs, bf16(rows, width)] + [bf16(width, d)] * 3,
+            "sccvvvvvv-vvvvvvvvvv", scratch=[pltpu.SemaphoreType.DMA((6,))],
         )
     return chain.call(
         kernel, "attention_forward", (*args, *w, g), [*outs, bf16(rows, d + width), bf16(3, width, d)],
@@ -236,120 +244,116 @@
     )
 
 
-def send_parts(chain, bits, out_weight, fc1_weight, fc2_weight, bias, others):
+def pick(chain, bits, a, b):
+    def kernel(io, bits_ref, a_ref, b_ref, out_ref, sems):
+        pl.when(bits_ref[2] == 0)(lambda: finish(copies(sems, [(a_ref, out_ref)])))
+        pl.when(bits_ref[2] != 0)(lambda: finish(copies(sems, [(b_ref, out_ref)])))
+
+    return chain.call(
+        kernel, "pick", (bits, a, b), [bf16(*a.shape)], "spp-v", limit=4,
+        scratch=[pltpu.SemaphoreType.DMA((1,))],
+    )[0]
+
+
+def hold(chain, a):
+    def kernel(io, a_ref, out_ref, sems):
+        finish(copies(sems, [(a_ref, out_ref)]))
+
+    return chain.call(
+        kernel, "hold", (a,), [bf16(*a.shape)], "v-v", limit=4, scratch=[pltpu.SemaphoreType.DMA((1,))]
+    )[0]
+
+
+def load(chain, out_weight, fc1_weight, fc2_weight, bias, others):
     shard, d = out_weight.shape
     n = len(others)
 
-    def kernel(io, bits_ref, wo, fc1, fc2, bias_ref, *refs):
-        others_in, (far_ref, near_ref, *others_out, sems) = refs[:n], refs[n:]
+    def kernel(io, wo, fc1, fc2, bias_ref, *refs):
+        others_in, (near_ref, *others_out, sems) = refs[:n], refs[n:]
         rows = lambda at: near_ref.at[at * shard : (at + 1) * shard]
-        pl.when(bits_ref[2] == 0)(lambda: finish(copies(sems, [(wo, far_ref)])))
-        pl.when(bits_ref[2] != 0)(lambda: finish(copies(sems, [(fc1, far_ref)])))
         near = [(wo, rows(0)), (fc1, rows(1)), (fc2, rows(2)), (bias_ref, near_ref.at[3 * shard :])]
         finish(copies(sems, near + list(zip(others_in, others_out))))
 
-    far, near, *others = chain.call(
-        kernel, "send_parts", (bits, out_weight, fc1_weight, fc2_weight, bias, *others),
-        [bf16(shard, d), bf16(3 * shard + 16, d)] + [jax.ShapeDtypeStruct(a.shape, a.dtype) for a in others],
-        "spppr" + "p" * n + "-vv" + "v" * n, limit=4, scratch=[pltpu.SemaphoreType.DMA((4 + n,))],
-    )
-    return far, near, others
-
-
-def join_arrays(chain, *parts):
-    def kernel(io, *refs):
-        *ins, out_ref, sems = refs
-        finish(copies(sems, [(ref, out_ref.at[j]) for j, ref in enumerate(ins)]))
-
-    return chain.call(
-        kernel, "join_arrays", parts, [bf16(len(parts), *parts[0].shape)], "v" * len(parts) + "-v", limit=4,
-        scratch=[pltpu.SemaphoreType.DMA((len(parts),))],
-    )[0]
-
-
-def pack_near(chain, near, near_got):
-    d = near.shape[1]
-    shard = (near.shape[0] - 16) // 3
-
-    def kernel(io, near0, near1, fc2_ref, sems):
-        rows = lambda ref, at: ref.at[at * shard : (at + 1) * shard]
-        finish(copies(sems, [(rows(near0, 2), rows(fc2_ref, 0)), (rows(near1, 2), rows(fc2_ref, 1))]))
-
-    return chain.call(
-        kernel, "pack_near", (near, near_got), [bf16(2 * shard, d)], "vv-v", limit=4,
-        scratch=[pltpu.SemaphoreType.DMA((2,))],
-    )[0]
-
-
-def pack_rest(chain, bits, near, near_got, far, far_got):
-    shard, d = far.shape[1:]
-
-    def kernel(io, bits_ref, near0, near1, far0, far1, wo_ref, fc1_ref, sems):
-        rows = lambda ref, at: ref.at[at * shard : (at + 1) * shard]
-        wo_at = bits_ref[2]
-        pairs = []
-        for at, (near_ref, far_ref) in enumerate(((near0, far0), (near1, far1))):
-            pairs += [(rows(near_ref, c), rows(ref, at)) for c, ref in enumerate((wo_ref, fc1_ref))]
-            pairs += [(far_ref.at[wo_at], rows(wo_ref, 2 + at)), (far_ref.at[1 - wo_at], rows(fc1_ref, 2 + at))]
-        finish(copies(sems, pairs))
-
-    return chain.call(
-        kernel, "pack_rest", (bits, near, near_got, far, far_got), [bf16(4 * shard, d), bf16(4 * shard, d)],
-        "svvvv-vv", limit=4, scratch=[pltpu.SemaphoreType.DMA((8,))],
-    )
-
-
-def feed(chain, x, oa, got, wo, gain, bias, fc1, b1, fc2, kinds):
+    near, *others = chain.call(
+        kernel, "load", (out_weight, fc1_weight, fc2_weight, bias, *others),
+        [bf16(3 * shard + 16, d)] + [jax.ShapeDtypeStruct(a.shape, a.dtype) for a in others],
+        "pppr" + "p" * n + "-v" + "v" * n, limit=4, scratch=[pltpu.SemaphoreType.DMA((4 + n,))],
+    )
+    return near, others
+
+
+def feed_body(x, oa, ob, g, wo, gain_ref, bias_ref, fc1_ref, b1, fc2_ref, h_ref, a2_ref, z_ref, du_ref):
+    h = x.astype(F32) + dot_nn(oa, wo[0][...]) + dot_nn(ob, wo[1][...])
+    h_ref[...] = h
+    xh, _ = normalise(h)
+    a2 = (xh * gain_ref[...][None, :] + bias_ref[...][None, :]).astype(BF16)
+    a2_ref[...] = a2
+    shard = fc2_ref.shape[0] // 2
+    b1 = jnp.concatenate([b[3 * shard : 3 * shard + 1, :shard] for b in b1], axis=1).astype(F32)
+    u = dot_nt(a2, fc1_ref[...]) + b1
+    dz = dot_nt(g, fc2_ref[...])
+    phi = 0.5 * (1.0 + lax.erf(u * (0.5**0.5)))
+    slope = phi + u * (jnp.exp(-0.5 * u * u) * 0.3989422804014327)
+    du = (dz * slope).astype(BF16)
+    z = (u * phi).astype(BF16)
+    du_ref[...] = du
+    z_ref[...] = z
+    return a2, z, du
+
+
+def feed_far(chain, bits, x, oa, packet, gain, bias, fc1, fc2, wo, near, fars):
     rows, d = x.shape
     width = fc2.shape[0]
     shard = width // 2
 
-    def kernel(io, x_ref, oa_ref, *refs):
-        if len(got) == 2:
-            g, ob = refs[0][...], refs[1][...]
-        else:
-            g, ob = refs[0][:, :d], refs[0][:, d:]
-        wo_ref, gain_ref, bias_ref, fc1_ref, b10, b11, fc2_ref, h_ref, a2_ref, z_ref, du_ref = refs[len(got) :]
-        oa = oa_ref[:, oa_ref.shape[1] - width :]
-        h = x_ref[...].astype(F32) + dot_nn(jnp.concatenate([oa, ob], axis=1), wo_ref[...])
-        h_ref[...] = h
-        xh, _ = normalise(h)
-        a2 = (xh * gain_ref[...][None, :] + bias_ref[...][None, :]).astype(BF16)
-        a2_ref[...] = a2
-        b1 = jnp.concatenate([b[3 * shard : 3 * shard + 1, :shard] for b in (b10, b11)], axis=1).astype(F32)
-        u = dot_nt(a2, fc1_ref[:width]) + b1
-        dz = dot_nt(g, fc2_ref[...])
-        phi = 0.5 * (1.0 + lax.erf(u * (0.5**0.5)))
-        slope = phi + u * (jnp.exp(-0.5 * u * u) * 0.3989422804014327)
-        du_ref[...] = (dz * slope).astype(BF16)
-        z_ref[...] = (u * phi).astype(BF16)
-
-    return chain.call(
-        kernel, "feed_forward", (x, oa, *got, wo, gain, bias, fc1, *b1, fc2),
-        [f32(rows, d), bf16(rows, d), bf16(rows, width), bf16(rows, width)],
-        kinds + "vvvvvvv-vvvv",
-    )
-
-
-def feed_grads(chain, zs, dus, a2s, gs):
-    d = a2s[0].shape[1]
-    width = zs[0].shape[1]
+    def kernel(io, bits_ref, x_ref, oa_ref, packet_ref, gain_ref, bias_ref, fc1_ref, fc2_ref, wo_ref, b10, b11,
+               y0, x0, y1, x1, h_ref, a2_ref, z_ref, du_ref, wo_far, fc1_far, sems):
+        def both(first, second):
+            pairs = []
+            for at in range(2):
+                here = slice(at * shard, (at + 1) * shard)
+                pairs += [(first[at], wo_far.at[here]), (second[at], fc1_far.at[here])]
+            finish(copies(sems, pairs))
+
+        pl.when(bits_ref[2] == 0)(lambda: both((y0, y1), (x0, x1)))
+        pl.when(bits_ref[2] != 0)(lambda: both((x0, x1), (y0, y1)))
+        feed_body(
+            x_ref[...], oa_ref[...], packet_ref[:, d:], packet_ref[:, :d], (wo_ref, wo_far), gain_ref, bias_ref,
+            fc1_ref, (b10, b11), fc2_ref, h_ref, a2_ref, z_ref, du_ref,
+        )
+
+    return chain.call(
+        kernel, "feed_far", (bits, x, oa, packet, gain, bias, fc1, fc2, wo, *near, *fars),
+        [f32(rows, d), bf16(rows, d), bf16(rows, width), bf16(rows, width), bf16(width, d), bf16(width, d)],
+        "s" + "v" * 14 + "-vvvvvv", scratch=[pltpu.SemaphoreType.DMA((4,))],
+    )
+
+
+def feed_own(chain, x, packet, g, ob, gain, bias, fc1, fc2, wos, near, far):
+    rows, d = x.shape
+    width = fc2.shape[0]
     shard = width // 2
 
-    def kernel(io, z0, z1, du0, du1, a0, a1, g0, g1, keep_ref, send_ref, sums_ref):
-        first = dot_tn(du0[...], a0[...]) + dot_tn(du1[...], a1[...])
-        second = dot_tn(z0[...], g0[...]) + dot_tn(z1[...], g1[:, :d])
+    def kernel(io, x_ref, oa_ref, g_ref, ob_ref, gain_ref, bias_ref, fc1_ref, fc2_ref, wo0, wo1, b10, b11,
+               z1, du1, a1, g1, h_ref, a2_ref, z_ref, du_ref, keep_ref, send_ref, sums_ref):
+        a2, z, du = feed_body(
+            x_ref[...], oa_ref[:, d:], ob_ref[...], g_ref[...], (wo0, wo1), gain_ref, bias_ref, fc1_ref,
+            (b10, b11), fc2_ref, h_ref, a2_ref, z_ref, du_ref,
+        )
+        first = dot_tn(du, a2) + dot_tn(du1[...], a1[...])
+        second = dot_tn(z, g_ref[...]) + dot_tn(z1[...], g1[:, :d])
         for at, ref in enumerate((keep_ref, send_ref)):
-            rows = slice(at * shard, (at + 1) * shard)
-            ref[0] = first[rows].astype(BF16)
-            ref[1] = second[rows].astype(BF16)
-        sums_ref[...] = jnp.sum(du0[...].astype(F32), axis=0, keepdims=True) + jnp.sum(
+            here = slice(at * shard, (at + 1) * shard)
+            ref[0] = first[here].astype(BF16)
+            ref[1] = second[here].astype(BF16)
+        sums_ref[...] = jnp.sum(du.astype(F32), axis=0, keepdims=True) + jnp.sum(
             du1[...].astype(F32), axis=0, keepdims=True
         )
 
     return chain.call(
-        kernel, "feed_grads", (*zs, *dus, *a2s, *gs), [bf16(2, shard, d), bf16(2, shard, d), f32(1, width)],
-        "vvvvvvvv-vvv", weight=10,
+        kernel, "feed_own", (x, packet, g, ob, gain, bias, fc1, fc2, *wos, *near, *far),
+        [f32(rows, d), bf16(rows, d), bf16(rows, width), bf16(rows, width), bf16(2, shard, d),
+         bf16(2, shard, d), f32(1, width)], "v" * 16 + "-vvvvvvv",
     )
 
 
@@ -366,15 +370,14 @@
 
 
 def backward(chain, args, own):
-    h, kt = args[3], args[9]
+    h, kt = args[4], args[10]
     rows, d = h.shape
     width = kt.shape[0]
     mols, pairs = rows // LEN, width // PAIR
 
-    def kernel(io, du_ref, dr_ref, fc1_ref, h_ref, g_ref, gain_ref, wo_ref, p_ref, qt_ref, kt_ref, v_ref,
+    def kernel(io, du_ref, dr_ref, fc1_ref, fc1_far, h_ref, g_ref, gain_ref, wo_ref, p_ref, qt_ref, kt_ref, v_ref,
                gh_ref, dp_ref, dh_ref=None, sums_ref=None):
-        du = jnp.concatenate([du_ref[...], dr_ref[...]], axis=1)
-        da2 = dot_nn(du, fc1_ref[...])
+        da2 = dot_nn(du_ref[...], fc1_ref[...]) + dot_nn(dr_ref[...], fc1_far[...])
         xh, r = normalise(h_ref[...])
         dh = g_ref[:, :d].astype(F32) + norm_back(da2, gain_ref[...][None, :], xh, r)
         if own:
@@ -384,12 +387,11 @@
             io.flush(2)
         gh = dh.astype(BF16)
         gh_ref[...] = gh
-        dot = dot_nt(wo_ref[:width], gh).astype(BF16)
+        dot = dot_nt(wo_ref[...], gh).astype(BF16)
         every = [(m, i) for m in range(mols) for i in range(pairs)]
         lanes = lambda m: slice(LEN * m, LEN * (m + 1))
         rows_of = lambda i: slice(PAIR * i, PAIR * (i + 1))
         dps, dss, dos = {}, {}, {}
-        io.wait(7, 8, 9, 10)
         for m, i in every:
             low, before = pair_window(i, width)
             dos[m, i] = pair_blocks(dot[rows_of(i), lanes(m)])
@@ -409,7 +411,7 @@
 
     outs = [bf16(rows, d), bf16(3 * width, rows)] + ([f32(rows, d), f32(8, d)] if own else [])
     return chain.call(
-        kernel, "attention_backward", args, outs, "v" * 11 + ("-vvvv" if own else "-vv"),
+        kernel, "attention_backward", args, outs, "v" * 12 + ("-vvvv" if own else "-vv"),
     )
 
 
@@ -621,14 +623,14 @@
     far_masks = [6 if k == 2 else 1 << k for k in range(2, n_dp.bit_length() - 1)]
 
     w_got = swap_core(qkv_weight)
+    x_got = swap_y(tokens)
+    far_y = swap_y(pick(chain, bits, out_weight, fc1_weight))
     bias = jnp.pad(fc1_bias.reshape(1, -1), ((0, 15), (0, d - shard)))
-    far_y, near, others = send_parts(
-        chain, bits, out_weight, fc1_weight, fc2_weight, bias,
+    near, others = load(
+        chain, out_weight, fc1_weight, fc2_weight, bias,
         (tokens, out_grad, ln1_gain, ln1_bias, ln2_gain, ln2_bias),
     )
-    far_y = swap_y(far_y)
-    near_got = swap_core(near)
-    x_got = swap_y(others[0])
+    near = (near, swap_core(near))
     tokens, out_grad, ln1_gain, ln1_bias, ln2_gain, ln2_bias = others
 
     counts = (node_counts, edge_counts)
@@ -637,25 +639,26 @@
         chain, bits, 3, *counts, tokens, *norm1, (qkv_weight, w_got), out_grad
     )
     packet_got = swap_y(packet)
-    far_x = swap_dp(join_arrays(chain, far_y)[0], 1, 1)
-    a1_1, qt_1, kt_1, v_1, p_1, ot_1, o_1 = attention(chain, bits, 4, *counts, x_got, *norm1, w_qkv)
+    far_y = hold(chain, far_y)
+    far_x = swap_dp(far_y, 1, 1)
+    a1_1, qt_1, kt_1, v_1, p_1, ot_1, o_1, wo, fc1, fc2 = attention(
+        chain, bits, 4, *counts, x_got, *norm1, w_qkv, near=near
+    )
     o_got = swap_y(o_1)
-    far = join_arrays(chain, far_y, far_x)
-    far_got = swap_core(far)
-    fc2 = pack_near(chain, near, near_got)
-    wo, fc1 = pack_rest(chain, bits, near, near_got, far, far_got)
-
-    ffn = (wo, ln2_gain, ln2_bias, fc1, (near, near_got), fc2)
-    h_1, a2_1, z_1, du_1 = feed(chain, x_got, o_1, (packet_got,), *ffn, "vvv")
+    fars = (far_y, far_x, swap_core(far_y), swap_core(far_x))
+    norm2 = (ln2_gain, ln2_bias)
+    h_1, a2_1, z_1, du_1, wo_far, fc1_far = feed_far(
+        chain, bits, x_got, o_1, packet_got, *norm2, fc1, fc2, wo, near, fars
+    )
     dr_0 = swap_y(du_1)
-    h_0, a2_0, z_0, du_0 = feed(chain, tokens, packet, (out_grad, o_got), *ffn, "vvvv")
+    h_0, a2_0, z_0, du_0, keep_r, send_r, bias_sums = feed_own(
+        chain, tokens, packet, out_grad, o_got, *norm2, fc1, fc2, (wo, wo_far), near,
+        (z_1, du_1, a2_1, packet_got),
+    )
     dr_1 = swap_y(du_0)
-    keep_r, send_r, bias_sums = feed_grads(
-        chain, (z_0, z_1), (du_0, du_1), (a2_0, a2_1), (out_grad, packet_got)
-    )
     got_r = swap_core(send_r)
     gh_0, dp_0, dh, sums = backward(
-        chain, (du_0, dr_0, fc1, h_0, out_grad, ln2_gain, wo, p_0, qt_0, kt_0, v_0), True
+        chain, (du_0, dr_0, fc1, fc1_far, h_0, out_grad, ln2_gain, wo, p_0, qt_0, kt_0, v_0), True
     )
 
     class Sum:
@@ -692,7 +695,7 @@
     r = Sum(2, keep_r, got_r)
     r.first()
     gh_1, dp_1 = backward(
-        chain, (du_1, dr_1, fc1, h_1, packet_got, ln2_gain, wo, p_1, qt_1, kt_1, v_1), False
+        chain, (du_1, dr_1, fc1, fc1_far, h_1, packet_got, ln2_gain, wo, p_1, qt_1, kt_1, v_1), False
     )
     a1s = (a1_0, a1_1)
     keep_q, send_q = weight_grads(

time: 121 us -> 112 us (0.926)
  waiting for transfers between devices: 51.8 us -> 38.6 us
  starting transfers between devices: 32 us -> 36.1 us
    ppermute x8, waiting for transfers between devices: 26.8 us -> 13.9 us  [swap_y(): return lax.ppermute(a, 'tensor', [(t, t ^ 2) for t in range(n_tensor)])]
    ppermute x11, starting transfers between devices: 19.6 us -> 23.1 us  [swap_dp(): return lax.ppermute(a, ('dp', 'tensor'), pairs)]
    ppermute x6 -> x7, waiting for transfers between devices: 2.92 us -> 0.96 us  [swap_core(): return lax.ppermute(a, 'tensor', [(t, t ^ 1) for t in range(n_tensor)])]
    ppermute x11, waiting for transfers between devices: 22.1 us -> 23.7 us  [swap_dp(): return lax.ppermute(a, ('dp', 'tensor'), pairs)]
    pallas_call x30 -> x27, Pallas kernels: 34.4 us -> 35.5 us  [call(): pl.pallas_call(body, in_specs=[spec(kind) for kind in ins] + [vmem] * len...]
  transfers between devices with their start and end apart: 25 -> 26, of which waited for: 15 -> 14; matrix products, arithmetic and copies ran while one was open for 1% -> 0% of each run, Pallas kernels for 25% -> 28%
where the time goes in v5:
time: 112 us
  waiting for transfers between devices  38.6 us (34%)
  starting transfers between devices  36.1 us (32%)
  Pallas kernels  35.5 us (32%)
  between operations  1.16 us (1%)
    pallas_call x27, Pallas kernels, call(): pl.pallas_call(body, in_specs=[spec(kind) for kind in ins] + [vmem] * len...  35.5 us
    ppermute x11, waiting for transfers between devices, swap_dp(): return lax.ppermute(a, ('dp', 'tensor'), pairs)  23.7 us
    ppermute x11, starting transfers between devices, swap_dp(): return lax.ppermute(a, ('dp', 'tensor'), pairs)  23.1 us
    ppermute x8, waiting for transfers between devices, swap_y(): return lax.ppermute(a, 'tensor', [(t, t ^ 2) for t in range(n_tensor)])  13.9 us
    ppermute x8, starting transfers between devices, swap_y(): return lax.ppermute(a, 'tensor', [(t, t ^ 2) for t in range(n_tensor)])  12.2 us
  transfers between devices with their start and end apart: 26, of which 14 were waited for; matrix products, arithmetic and copies ran while one was open for 0% of the time, Pallas kernels for 28%

profile of v5, /device:TPU:0, one launch (start us, length us, event | category | flops | bytes accessed | tf_op | source)
XLA Modules:
  0.0 111.5 jit_solution(244967337244757431)
XLA Ops:
  0.8 1.5 %pick.1 = (bf16[192,768]{1,0:T(8,128)(2,1)S(1)}, f32[8,128]{1,0:T(8,128)S(1)}) custom-call(s32[5]{0:T(128)S(1)} %stack.23.refs_0_, bf16[192,768]{1,0:T(8,128)(2,1)} %refs_0_.1, bf16[192,768]{1,0:T(8,128)(2,1)} %refs_1_.5), custom_call_target="tpu_custom_call" | custom-call | flops 10000000000 | bytes 100000000 | tf_op jit(solution)/shard_map/pick/pallas_call | solution.py:139
  2.3 3.0 %collective-permute-start.3 = (bf16[192,768]{1,0:T(8,128)(2,1)S(1)}, bf16[192,768]{1,0:T(8,128)(2,1)S(1)}, u32[]{:S(2)}, u32[]{:S(2)}) collective-permute-start(bf16[192,768]{1,0:T(8,128)(2,1)S(1)} %get-tuple-element.119), channel_id=1, source_target_pairs={{0,2},{1,3},{2,0},{3,1},{4,6},{5,7},{6,4},{7,5},{8,10},{9,11},{10,... | collective-permute-start | bytes 884744 | tf_op jit(solution)/shard_map/ppermute | solution.py:611
  5.5 1.5 %load.1 = (bf16[592,768]{1,0:T(8,128)(2,1)S(1)}, bf16[256,768]{1,0:T(8,128)(2,1)S(1)}, bf16[256,768]{1,0:T(8,128)(2,1)S(1)}, f32[768]{0:T(1024)S(1)}, f32[768]{0...) custom-call(bf16[192,768]{1,0:T(8,128)(2,1)} %refs_0_.1, bf16[192,768]{1,0:T(8,128)(2,1)} %refs_1_.5, ...), custom_call_target="tpu_custom_call" | custom-call | flops 10000000000 | bytes 100000000 | tf_op jit(solution)/shard_map/load/pallas_call | solution.py:139
  7.9 4.0 %attention_forward.2 = (bf16[256,768]{1,0:T(8,128)(2,1)S(1)}, bf16[384,256]{1,0:T(8,128)(2,1)S(1)}, bf16[384,256]{1,0:T(8,128)(2,1)S(1)}, bf16[256,384]{1,0:T(8,...) custom-call(s32[5]{0:T(128)S(1)} %stack.23.refs_0_, ...), custom_call_target="tpu_custom_call" | custom-call | flops 10000000000 | bytes 100000000 | tf_op jit(solution)/shard_map/attention_forward/pallas_call | solution.py:139
  11.9 1.3 %collective-permute-done.3.refs_0_ = bf16[192,768]{1,0:T(8,128)(2,1)S(1)} collective-permute-done((bf16[192,768]{1,0:T(8,128)(2,1)S(1)}, bf16[192,768]{1,0:T(8,128)(2,1)S(1)}, u32[]{:S(2)}, u32[]{:S(2)}) %collective-permute-start.3) | collective-permute-done | bytes 294944 | tf_op jit(solution)/shard_map/ppermute | solution.py:611
  13.3 2.1 %collective-permute-start.6 = (bf16[192,768]{1,0:T(8,128)(2,1)S(1)}, bf16[192,768]{1,0:T(8,128)(2,1)S(1)}, u32[]{:S(2)}, u32[]{:S(2)}) collective-permute-start(bf16[192,768]{1,0:T(8,128)(2,1)S(1)} %get-tuple-element.128.refs_11_), channel_id=1, source_target_pairs={{0,4},{1,5},{2,6},{3,7},{4,0},{5,1},{6,2},{7,3},{8,12},{9,13},{10,... | collective-permute-start | bytes 884744 | tf_op jit(solution)/shard_map/ppermute | solution.py:619
  15.4 1.5 %collective-permute-start.5 = (bf16[256,1152]{1,0:T(8,128)(2,1)S(1)}, bf16[256,1152]{1,0:T(8,128)(2,1)S(1)}, u32[]{:S(2)}, u32[]{:S(2)}) collective-permute-start(bf16[256,1152]{1,0:T(8,128)(2,1)S(1)} %get-tuple-element.116.refs_1_), channel_id=1, source_target_pairs={{0,2},{1,3},{2,0},{3,1},{4,6},{5,7},{6,4},{7,5},{8,10},{9,11},{10,... | collective-permute-start | bytes 1769480 | tf_op jit(solution)/shard_map/ppermute | solution.py:611
  16.9 4.4 %collective-permute-done.6.refs_12_ = bf16[192,768]{1,0:T(8,128)(2,1)S(1)} collective-permute-done((bf16[192,768]{1,0:T(8,128)(2,1)S(1)}, bf16[192,768]{1,0:T(8,128)(2,1)S(1)}, u32[]{:S(2)}, u32[]{:S(2)}) %collective-permute-start.6) | collective-permute-done | bytes 294944 | tf_op jit(solution)/shard_map/ppermute | solution.py:619
  21.6 3.5 %attention_forward.3 = (bf16[256,768]{1,0:T(8,128)(2,1)S(1)}, bf16[384,256]{1,0:T(8,128)(2,1)S(1)}, bf16[384,256]{1,0:T(8,128)(2,1)S(1)}, bf16[256,384]{1,0:T(8,...) custom-call(s32[5]{0:T(128)S(1)} %stack.23.refs_0_, ...), custom_call_target="tpu_custom_call" | custom-call | flops 10000000000 | bytes 100000000 | tf_op jit(solution)/shard_map/attention_forward/pallas_call | solution.py:139
  25.1 2.1 %collective-permute-start.4 = (bf16[256,384]{1,0:T(8,128)(2,1)S(1)}, bf16[256,384]{1,0:T(8,128)(2,1)S(1)}, u32[]{:S(2)}, u32[]{:S(2)}) collective-permute-start(bf16[256,384]{1,0:T(8,128)(2,1)S(1)} %get-tuple-element.122.refs_2_), channel_id=1, source_target_pairs={{0,2},{1,3},{2,0},{3,1},{4,6},{5,7},{6,4},{7,5},{8,10},{9,11},{10,... | collective-permute-start | bytes 589832 | tf_op jit(solution)/shard_map/ppermute | solution.py:611
  27.3 7.0 %collective-permute-done.5.refs_3_.refs_15_.refs_5_ = bf16[256,1152]{1,0:T(8,128)(2,1)S(1)} collective-permute-done((bf16[256,1152]{1,0:T(8,128)(2,1)S(1)}, bf16[256,1152]{1,0:T(8,128)(2,1)S(1)}, u32[]{:S(2)}, u32[]{:S(2)}) %collective-permute-start.5) | collective-permute-done | bytes 589856 | tf_op jit(solution)/shard_map/ppermute | solution.py:611
  34.3 2.7 %feed_far.1 = (f32[256,768]{1,0:T(8,128)S(1)}, bf16[256,768]{1,0:T(8,128)(2,1)S(1)}, bf16[256,384]{1,0:T(8,128)(2,1)S(1)}, bf16[256,384]{1,0:T(8,128)(2,1)S(1)},...) custom-call(s32[5]{0:T(128)S(1)} %stack.23.refs_0_, ...), custom_call_target="tpu_custom_call" | custom-call | flops 10000000000 | bytes 100000000 | tf_op jit(solution)/shard_map/feed_far/pallas_call | solution.py:139
  37.0 2.1 %collective-permute-start.9 = (bf16[256,384]{1,0:T(8,128)(2,1)S(1)}, bf16[256,384]{1,0:T(8,128)(2,1)S(1)}, u32[]{:S(2)}, u32[]{:S(2)}) collective-permute-start(bf16[256,384]{1,0:T(8,128)(2,1)S(1)} %get-tuple-element.132.refs_13_.refs_0_), channel_id=1, source_target_pairs={{0,2},{1,3},{2,0},{3,1},{4,6},{5,7},{6,4},{7,5},{8,10},{9,11},{10,... | collective-permute-start | bytes 589832 | tf_op jit(solution)/shard_map/ppermute | solution.py:611
  39.1 2.8 %feed_own.1 = (f32[256,768]{1,0:T(8,128)S(1)}, bf16[256,768]{1,0:T(8,128)(2,1)}, bf16[256,384]{1,0:T(8,128)(2,1)S(1)}, bf16[256,384]{1,0:T(8,128)(2,1)S(1)}, bf1...) custom-call(bf16[256,768]{1,0:T(8,128)(2,1)S(1)} %get-tuple-element., ...), custom_call_target="tpu_custom_call" | custom-call | flops 10000000000 | bytes 100000000 | tf_op jit(solution)/shard_map/feed_own/pallas_call | solution.py:139
  42.3 1.0 collective-permute-done.9.refs_1_
  43.3 2.6 %attention_backward.2 = (bf16[256,768]{1,0:T(8,128)(2,1)S(1)}, bf16[1152,256]{1,0:T(8,128)(2,1)S(1)}, f32[256,768]{1,0:T(8,128)S(1)}, f32[8,768]{1,0:T(8,128)S(1)}, f32[8,128]{1,0:T(8,128)S(1)}) custom-call(bf16[256,384]{1,0:T(8,128)(2,1)S(1)} %get-tuple-element.137.refs_0_, bf16[256,384]{1,0:T(8,128)(2,1)S(1)} %collective-permute-done.9.refs_1_, ...), custom_call_target="tpu_custom_call" | custom-call | flops 10000000000 | bytes 100000000 | tf_op jit(solution)/shard_map/attention_backward/pallas_call | solution.py:139
  45.9 0.6 sum_half.2
  46.5 2.5 %collective-permute-start.13 = (bf16[192,768]{1,0:T(8,128)(2,1)S(1)}, bf16[192,768]{1,0:T(8,128)(2,1)S(1)}, u32[]{:S(2)}, u32[]{:S(2)}) collective-permute-start(bf16[192,768]{1,0:T(8,128)(2,1)S(1)} %get-tuple-element.164), channel_id=1, source_target_pairs={{0,4},{1,9},{2,6},{3,11},{4,0},{5,13},{6,2},{7,15},{8,12},{9,1},{1... | collective-permute-start | bytes 884744 | tf_op jit(solution)/shard_map/ppermute | solution.py:619
  49.0 2.6 %attention_backward.3 = (bf16[256,768]{1,0:T(8,128)(2,1)S(1)}, bf16[1152,256]{1,0:T(8,128)(2,1)S(1)}, f32[8,128]{1,0:T(8,128)S(1)}) custom-call(bf16[256,384]{1,0:T(8,128)(2,1)S(1)} %get-tuple-element.132.refs_13_.refs_0_, bf16[256,384]{1,0:T(8,128)(2,1)S(1)} %collective-permute-done.10.refs_1_, bf16[384,768]{1,0:T(8,128)(2,1)S(1)} %get-tuple-element.125.refs_6_.refs_2_, ...), custom_call_target="tpu_custom_call" | custom-call | flops 10000000000 | bytes 100000000 | tf_op jit(solution)/shard_map/attention_backward/pallas_call | solution.py:139
  51.6 1.4 %weight_grads.1 = (bf16[4,192,768]{2,1,0:T(8,128)(2,1)S(1)}, bf16[4,192,768]{2,1,0:T(8,128)(2,1)S(1)}, f32[8,128]{1,0:T(8,128)S(1)}) custom-call(bf16[1152,256]{1,0:T(8,128)(2,1)S(1)} %get-tuple-element.144.refs_0_.refs_4_.refs_8_, bf16[1152,256]{1,0:T(8,128)(2,1)S(1)} %get-tuple-element.154.refs_1_.refs_5_.refs_9_, ...), custom_call_target="tpu_custom_call" | custom-call | flops 10000000000 | bytes 100000000 | tf_op jit(solution)/shard_map/weight_grads/pallas_call | solution.py:139
  53.1 0.6 collective-permute-done.13
  53.7 0.6 sum_quarter.4
  54.3 2.2 %collective-permute-start.15 = (bf16[96,768]{1,0:T(8,128)(2,1)S(1)}, bf16[96,768]{1,0:T(8,128)(2,1)S(1)}, u32[]{:S(2)}, u32[]{:S(2)}) collective-permute-start(bf16[96,768]{1,0:T(8,128)(2,1)S(1)} %get-tuple-element.168), channel_id=1, source_target_pairs={{0,8},{1,5},{2,10},{3,7},{4,12},{5,1},{6,14},{7,3},{8,0},{9,13},{1... | collective-permute-start | bytes 442376 | tf_op jit(solution)/shard_map/ppermute | solution.py:619
  56.5 0.6 sum_half.3
  57.1 1.6 %collective-permute-start.14 = (bf16[384,768]{1,0:T(8,128)(2,1)S(1)}, bf16[384,768]{1,0:T(8,128)(2,1)S(1)}, u32[]{:S(2)}, u32[]{:S(2)}) collective-permute-start(bf16[384,768]{1,0:T(8,128)(2,1)S(1)} %get-tuple-element.167), channel_id=1, source_target_pairs={{0,4},{1,9},{2,6},{3,11},{4,0},{5,13},{6,2},{7,15},{8,12},{9,1},{1... | collective-permute-start | bytes 1769480 | tf_op jit(solution)/shard_map/ppermute | solution.py:619
  58.7 1.4 %input_grads.1 = (f32[256,768]{1,0:T(8,128)S(1)}, bf16[272,768]{1,0:T(8,128)(2,1)S(1)}, f32[8,128]{1,0:T(8,128)S(1)}) custom-call(bf16[1152,256]{1,0:T(8,128)(2,1)S(1)} %get-tuple-element.144.refs_0_.refs_4_.refs_8_, bf16[1152,256]{1,0:T(8,128)(2,1)S(1)} %get-tuple-element.154.refs_1_.refs_5_.refs_9_, ...), custom_call_target="tpu_custom_call" | custom-call | flops 10000000000 | bytes 100000000 | tf_op jit(solution)/shard_map/input_grads/pallas_call | solution.py:139
  60.1 0.6 sum_quarter.5
  60.7 4.3 %collective-permute-start.18 = (bf16[96,768]{1,0:T(8,128)(2,1)S(1)}, bf16[96,768]{1,0:T(8,128)(2,1)S(1)}, u32[]{:S(2)}, u32[]{:S(2)}) collective-permute-start(bf16[96,768]{1,0:T(8,128)(2,1)S(1)} %get-tuple-element.176.refs_0_), channel_id=1, source_target_pairs={{0,24},{1,25},{2,26},{3,27},{4,28},{5,29},{6,30},{7,31},{8,16},{9,... | collective-permute-start | bytes 442376 | tf_op jit(solution)/shard_map/ppermute | solution.py:619
  65.0 1.5 %collective-permute-start.17 = (bf16[272,768]{1,0:T(8,128)(2,1)S(1)}, bf16[272,768]{1,0:T(8,128)(2,1)S(1)}, u32[]{:S(2)}, u32[]{:S(2)}) collective-permute-start(bf16[272,768]{1,0:T(8,128)(2,1)S(1)} %get-tuple-element.175.refs_0_), channel_id=1, source_target_pairs={{0,2},{1,3},{2,0},{3,1},{4,6},{5,7},{6,4},{7,5},{8,10},{9,11},{10,... | collective-permute-start | bytes 1253384 | tf_op jit(solution)/shard_map/ppermute | solution.py:611
  67.0 0.7 sum_quarter.6
  67.7 1.1 collective-permute-start.16
  68.8 1.0 collective-permute-done.18.refs_1_
  69.8 4.3 %collective-permute-done.17.refs_1_.refs_3_ = bf16[272,768]{1,0:T(8,128)(2,1)S(1)} collective-permute-done((bf16[272,768]{1,0:T(8,128)(2,1)S(1)}, bf16[272,768]{1,0:T(8,128)(2,1)S(1)}, u32[]{:S(2)}, u32[]{:S(2)}) %collective-permute-start.17) | collective-permute-done | bytes 417824 | tf_op jit(solution)/shard_map/ppermute | solution.py:611
  74.8 0.6 collective-permute-done.19.refs_6_
  75.4 0.8 sum_quarter.7
  76.3 2.2 %collective-permute-start.23 = (bf16[208,768]{1,0:T(8,128)(2,1)S(1)}, bf16[208,768]{1,0:T(8,128)(2,1)S(1)}, u32[]{:S(2)}, u32[]{:S(2)}) collective-permute-start(bf16[208,768]{1,0:T(8,128)(2,1)S(1)} %get-tuple-element.190.refs_0_), channel_id=1, source_target_pairs={{0,24},{1,25},{2,26},{3,27},{4,28},{5,29},{6,30},{7,31},{8,16},{9,... | collective-permute-start | bytes 958472 | tf_op jit(solution)/shard_map/ppermute | solution.py:619
  78.5 0.6 feed_result.1
  79.2 1.3 %input_norm.1 = (bf16[256,768]{1,0:T(8,128)(2,1)}, f32[8,128]{1,0:T(8,128)S(1)}) custom-call(bf16[256,768]{1,0:T(8,128)(2,1)S(1)} %get-tuple-element.111.refs_3_.refs_0_, f32[768]{0:T(1024)S(1)} %copy-done.1, f32[256,768]{1,0:T(8,128)S(1)} %get-tuple-element.185.refs_2_, bf16[272,768]{1,0:T(8,128)(2,1)S(1)} %collective-permute-done.17.refs_1_.refs_3_, ...), custom_call_target="tpu_custom_call" | custom-call | flops 10000000000 | bytes 100000000 | tf_op jit(solution)/shard_map/input_norm/pallas_call | solution.py:139
  80.6 1.0 collective-permute-start.22
  81.5 1.5 %collective-permute-start.20 = (bf16[256,768]{1,0:T(8,128)(2,1)S(1)}, bf16[256,768]{1,0:T(8,128)(2,1)S(1)}, u32[]{:S(2)}, u32[]{:S(2)}) collective-permute-start(bf16[256,768]{1,0:T(8,128)(2,1)S(1)} %get-tuple-element.183), channel_id=1, source_target_pairs={{0,2},{1,3},{2,0},{3,1},{4,6},{5,7},{6,4},{7,5},{8,10},{9,11},{10,... | collective-permute-start | bytes 1179656 | tf_op jit(solution)/shard_map/ppermute | solution.py:611
  83.0 5.6 %collective-permute-done.23.refs_1_ = bf16[208,768]{1,0:T(8,128)(2,1)S(1)} collective-permute-done((bf16[208,768]{1,0:T(8,128)(2,1)S(1)}, bf16[208,768]{1,0:T(8,128)(2,1)S(1)}, u32[]{:S(2)}, u32[]{:S(2)}) %collective-permute-start.23) | collective-permute-done | bytes 319520 | tf_op jit(solution)/shard_map/ppermute | solution.py:619
  88.7 4.7 %collective-permute-start.24 = (bf16[208,768]{1,0:T(8,128)(2,1)S(1)}, bf16[208,768]{1,0:T(8,128)(2,1)S(1)}, u32[]{:S(2)}, u32[]{:S(2)}) collective-permute-start(bf16[208,768]{1,0:T(8,128)(2,1)S(1)} %get-tuple-element.196.refs_0_), channel_id=1, source_target_pairs={{0,8},{1,5},{2,10},{3,7},{4,12},{5,1},{6,14},{7,3},{8,0},{9,13},{1... | collective-permute-start | bytes 958472 | tf_op jit(solution)/shard_map/ppermute | solution.py:619
  93.4 1.7 %place_sums.2 = (f32[192,768]{1,0:T(8,128)}, f32[192,768]{1,0:T(8,128)}, f32[8,128]{1,0:T(8,128)S(1)}) custom-call(s32[5]{0:T(128)S(1)} %stack.23.refs_0_, bf16[192,768]{1,0:T(8,128)(2,1)S(1)} %get-tuple-element.189.refs_1_, bf16[192,768]{1,0:T(8,128)(2,1)S(1)} %collective-permute-done.22.refs_2_, f32[8,128]{1,0:T(8,128)S(1)} %get-tuple-element.192.refs_3_), custom_call_target="tpu_custom_call" | custom-call | flops 10000000000 | bytes 100000000 | tf_op jit(solution)/shard_map/place_sums/pallas_call | solution.py:139
  95.1 0.9 add_result.1
  95.9 2.4 %collective-permute-done.24.refs_1_ = bf16[208,768]{1,0:T(8,128)(2,1)S(1)} collective-permute-done((bf16[208,768]{1,0:T(8,128)(2,1)S(1)}, bf16[208,768]{1,0:T(8,128)(2,1)S(1)}, u32[]{:S(2)}, u32[]{:S(2)}) %collective-permute-start.24) | collective-permute-done | bytes 319520 | tf_op jit(solution)/shard_map/ppermute | solution.py:619
  98.4 1.0 collective-permute-start.25
  99.4 9.2 %collective-permute-done.25.refs_2_ = bf16[400,768]{1,0:T(8,128)(2,1)S(1)} collective-permute-done((bf16[400,768]{1,0:T(8,128)(2,1)S(1)}, bf16[400,768]{1,0:T(8,128)(2,1)S(1)}, u32[]{:S(2)}, u32[]{:S(2)}) %collective-permute-start.25) | collective-permute-done | bytes 614432 | tf_op jit(solution)/shard_map/ppermute | solution.py:619
  108.6 2.7 %place_sums.3 = (f32[3,192,768]{2,1,0:T(8,128)}, f32[192,768]{1,0:T(8,128)}, f32[768]{0:T(1024)}, f32[768]{0:T(1024)}, f32[768]{0:T(1024)}, /*index=5*/f32[768]{0:T(1024)}, f32[192]{0:T(256)}, f32[8,128]{1,0:T(8,128)}) custom-call(s32[5]{0:T(128)S(1)} %stack.23.refs_0_, bf16[400,768]{1,0:T(8,128)(2,1)S(1)} %get-tuple-element.198.refs_1_, ...), custom_call_target="tpu_custom_call" | custom-call | flops 10000000000 | bytes 100000000 | tf_op jit(solution)/shard_map/place_sums/pallas_call | solution.py:139
  (44 shorter events, 3.2 us)
Async XLA Ops:
  0.8 4.6 %copy-start.3 = (bf16[256,768]{1,0:T(8,128)(2,1)S(1)}, bf16[256,768]{1,0:T(8,128)(2,1)}, u32[]{:S(2)}) copy-start(bf16[256,768]{1,0:T(8,128)(2,1)} %refs_4_.1) | copy-start | bytes 1179652
  0.8 4.7 %copy-start.2 = (bf16[3,192,768]{2,1,0:T(8,128)(2,1)S(1)}, bf16[3,192,768]{2,1,0:T(8,128)(2,1)}, u32[]{:S(2)}) copy-start(bf16[3,192,768]{2,1,0:T(8,128)(2,1)} %refs_6_.3) | copy-start | bytes 2654212
  0.8 4.7 %copy-start.4 = (bf16[192]{0:T(256)(128)(2,1)S(1)}, bf16[192]{0:T(256)(128)(2,1)}, u32[]{:S(2)}) copy-start(bf16[192]{0:T(256)(128)(2,1)} %param.23) | copy-start | bytes 1156
  2.3 10.9 %collective-permute-start.3 = (bf16[192,768]{1,0:T(8,128)(2,1)S(1)}, bf16[192,768]{1,0:T(8,128)(2,1)S(1)}, u32[]{:S(2)}, u32[]{:S(2)}) collective-permute-start(bf16[192,768]{1,0:T(8,128)(2,1)S(1)} %get-tuple-element.119), channel_id=1, source_target_pairs={{0,2},{1,3},{2,0},{3,1},{4,6},{5,7},{6,4},{7,5},{8,10},{9,11},{10,... | collective-permute-start | bytes 884744 | tf_op jit(solution)/shard_map/ppermute | solution.py:611
  5.4 16.3 %collective-permute-start.1 = (bf16[256,768]{1,0:T(8,128)(2,1)S(1)}, bf16[256,768]{1,0:T(8,128)(2,1)S(1)}, u32[]{:S(2)}, u32[]{:S(2)}) collective-permute-start(bf16[256,768]{1,0:T(8,128)(2,1)S(1)} %copy-done.3), channel_id=1, source_target_pairs={{0,2},{1,3},{2,0},{3,1},{4,6},{5,7},{6,4},{7,5},{8,10},{9,11},{10,... | collective-permute-start | bytes 1179656 | tf_op jit(solution)/shard_map/ppermute | solution.py:611
  5.4 2.4 %collective-permute-start = (bf16[3,192,768]{2,1,0:T(8,128)(2,1)S(1)}, bf16[3,192,768]{2,1,0:T(8,128)(2,1)S(1)}, u32[]{:S(2)}, u32[]{:S(2)}) collective-permute-start(bf16[3,192,768]{2,1,0:T(8,128)(2,1)S(1)} %copy-done.2), channel_id=1, source_target_pairs={{0,1},{1,0},{2,3},{3,2},{4,5},{5,4},{6,7},{7,6},{8,9},{9,8},{10,11... | collective-permute-start | bytes 2654216 | tf_op jit(solution)/shard_map/ppermute | solution.py:608
  7.0 14.6 %copy-start = (f32[768]{0:T(1024)}, f32[768]{0:T(1024)S(1)}, u32[]{:S(2)}) copy-start(f32[768]{0:T(1024)S(1)} %get-tuple-element.112.refs_4_.refs_1_) | copy-start | bytes 9220
  7.0 14.6 %collective-permute-start.2 = (bf16[592,768]{1,0:T(8,128)(2,1)S(1)}, bf16[592,768]{1,0:T(8,128)(2,1)S(1)}, u32[]{:S(2)}, u32[]{:S(2)}) collective-permute-start(bf16[592,768]{1,0:T(8,128)(2,1)S(1)} %get-tuple-element.118.refs_7_.refs_9_.refs_10_), channel_id=1, source_target_pairs={{0,1},{1,0},{2,3},{3,2},{4,5},{5,4},{6,7},{7,6},{8,9},{9,8},{10,11... | collective-permute-start | bytes 2727944 | tf_op jit(solution)/shard_map/ppermute | solution.py:608
  13.3 8.0 %collective-permute-start.6 = (bf16[192,768]{1,0:T(8,128)(2,1)S(1)}, bf16[192,768]{1,0:T(8,128)(2,1)S(1)}, u32[]{:S(2)}, u32[]{:S(2)}) collective-permute-start(bf16[192,768]{1,0:T(8,128)(2,1)S(1)} %get-tuple-element.128.refs_11_), channel_id=1, source_target_pairs={{0,4},{1,5},{2,6},{3,7},{4,0},{5,1},{6,2},{7,3},{8,12},{9,13},{10,... | collective-permute-start | bytes 884744 | tf_op jit(solution)/shard_map/ppermute | solution.py:619
  15.4 11.9 %collective-permute-start.7 = (bf16[192,768]{1,0:T(8,128)(2,1)S(1)}, bf16[192,768]{1,0:T(8,128)(2,1)S(1)}, u32[]{:S(2)}, u32[]{:S(2)}) collective-permute-start(bf16[192,768]{1,0:T(8,128)(2,1)S(1)} %get-tuple-element.128.refs_11_), channel_id=1, source_target_pairs={{0,1},{1,0},{2,3},{3,2},{4,5},{5,4},{6,7},{7,6},{8,9},{9,8},{10,11... | collective-permute-start | bytes 884744 | tf_op jit(solution)/shard_map/ppermute | solution.py:608
  15.4 18.9 %collective-permute-start.5 = (bf16[256,1152]{1,0:T(8,128)(2,1)S(1)}, bf16[256,1152]{1,0:T(8,128)(2,1)S(1)}, u32[]{:S(2)}, u32[]{:S(2)}) collective-permute-start(bf16[256,1152]{1,0:T(8,128)(2,1)S(1)} %get-tuple-element.116.refs_1_), channel_id=1, source_target_pairs={{0,2},{1,3},{2,0},{3,1},{4,6},{5,7},{6,4},{7,5},{8,10},{9,11},{10,... | collective-permute-start | bytes 1769480 | tf_op jit(solution)/shard_map/ppermute | solution.py:611
  21.3 6.0 %collective-permute-start.8 = (bf16[192,768]{1,0:T(8,128)(2,1)S(1)}, bf16[192,768]{1,0:T(8,128)(2,1)S(1)}, u32[]{:S(2)}, u32[]{:S(2)}) collective-permute-start(bf16[192,768]{1,0:T(8,128)(2,1)S(1)} %collective-permute-done.6.refs_12_), channel_id=1, source_target_pairs={{0,1},{1,0},{2,3},{3,2},{4,5},{5,4},{6,7},{7,6},{8,9},{9,8},{10,11... | collective-permute-start | bytes 884744 | tf_op jit(solution)/shard_map/ppermute | solution.py:608
  25.1 14.0 %collective-permute-start.4 = (bf16[256,384]{1,0:T(8,128)(2,1)S(1)}, bf16[256,384]{1,0:T(8,128)(2,1)S(1)}, u32[]{:S(2)}, u32[]{:S(2)}) collective-permute-start(bf16[256,384]{1,0:T(8,128)(2,1)S(1)} %get-tuple-element.122.refs_2_), channel_id=1, source_target_pairs={{0,2},{1,3},{2,0},{3,1},{4,6},{5,7},{6,4},{7,5},{8,10},{9,11},{10,... | collective-permute-start | bytes 589832 | tf_op jit(solution)/shard_map/ppermute | solution.py:611
  37.0 6.3 %collective-permute-start.9 = (bf16[256,384]{1,0:T(8,128)(2,1)S(1)}, bf16[256,384]{1,0:T(8,128)(2,1)S(1)}, u32[]{:S(2)}, u32[]{:S(2)}) collective-permute-start(bf16[256,384]{1,0:T(8,128)(2,1)S(1)} %get-tuple-element.132.refs_13_.refs_0_), channel_id=1, source_target_pairs={{0,2},{1,3},{2,0},{3,1},{4,6},{5,7},{6,4},{7,5},{8,10},{9,11},{10,... | collective-permute-start | bytes 589832 | tf_op jit(solution)/shard_map/ppermute | solution.py:611
  41.9 7.1 %collective-permute-start.10 = (bf16[256,384]{1,0:T(8,128)(2,1)S(1)}, bf16[256,384]{1,0:T(8,128)(2,1)S(1)}, u32[]{:S(2)}, u32[]{:S(2)}) collective-permute-start(bf16[256,384]{1,0:T(8,128)(2,1)S(1)} %get-tuple-element.137.refs_0_), channel_id=1, source_target_pairs={{0,2},{1,3},{2,0},{3,1},{4,6},{5,7},{6,4},{7,5},{8,10},{9,11},{10,... | collective-permute-start | bytes 589832 | tf_op jit(solution)/shard_map/ppermute | solution.py:611
  42.3 3.6 %collective-permute-start.11 = (bf16[2,192,768]{2,1,0:T(8,128)(2,1)S(1)}, bf16[2,192,768]{2,1,0:T(8,128)(2,1)S(1)}, u32[]{:S(2)}, u32[]{:S(2)}) collective-permute-start(bf16[2,192,768]{2,1,0:T(8,128)(2,1)S(1)} %get-tuple-element.151), channel_id=1, source_target_pairs={{0,1},{1,0},{2,3},{3,2},{4,5},{5,4},{6,7},{7,6},{8,9},{9,8},{10,11... | collective-permute-start | bytes 1769480 | tf_op jit(solution)/shard_map/ppermute | solution.py:608
  46.5 7.2 %collective-permute-start.13 = (bf16[192,768]{1,0:T(8,128)(2,1)S(1)}, bf16[192,768]{1,0:T(8,128)(2,1)S(1)}, u32[]{:S(2)}, u32[]{:S(2)}) collective-permute-start(bf16[192,768]{1,0:T(8,128)(2,1)S(1)} %get-tuple-element.164), channel_id=1, source_target_pairs={{0,4},{1,9},{2,6},{3,11},{4,0},{5,13},{6,2},{7,15},{8,12},{9,1},{1... | collective-permute-start | bytes 884744 | tf_op jit(solution)/shard_map/ppermute | solution.py:619
  53.0 3.4 %collective-permute-start.12 = (bf16[4,192,768]{2,1,0:T(8,128)(2,1)S(1)}, bf16[4,192,768]{2,1,0:T(8,128)(2,1)S(1)}, u32[]{:S(2)}, u32[]{:S(2)}) collective-permute-start(bf16[4,192,768]{2,1,0:T(8,128)(2,1)S(1)} %get-tuple-element.163), channel_id=1, source_target_pairs={{0,1},{1,0},{2,3},{3,2},{4,5},{5,4},{6,7},{7,6},{8,9},{9,8},{10,11... | collective-permute-start | bytes 3538952 | tf_op jit(solution)/shard_map/ppermute | solution.py:608
  54.3 5.8 %collective-permute-start.15 = (bf16[96,768]{1,0:T(8,128)(2,1)S(1)}, bf16[96,768]{1,0:T(8,128)(2,1)S(1)}, u32[]{:S(2)}, u32[]{:S(2)}) collective-permute-start(bf16[96,768]{1,0:T(8,128)(2,1)S(1)} %get-tuple-element.168), channel_id=1, source_target_pairs={{0,8},{1,5},{2,10},{3,7},{4,12},{5,1},{6,14},{7,3},{8,0},{9,13},{1... | collective-permute-start | bytes 442376 | tf_op jit(solution)/shard_map/ppermute | solution.py:619
  57.1 9.9 %collective-permute-start.14 = (bf16[384,768]{1,0:T(8,128)(2,1)S(1)}, bf16[384,768]{1,0:T(8,128)(2,1)S(1)}, u32[]{:S(2)}, u32[]{:S(2)}) collective-permute-start(bf16[384,768]{1,0:T(8,128)(2,1)S(1)} %get-tuple-element.167), channel_id=1, source_target_pairs={{0,4},{1,9},{2,6},{3,11},{4,0},{5,13},{6,2},{7,15},{8,12},{9,1},{1... | collective-permute-start | bytes 1769480 | tf_op jit(solution)/shard_map/ppermute | solution.py:619
  60.7 9.1 %collective-permute-start.18 = (bf16[96,768]{1,0:T(8,128)(2,1)S(1)}, bf16[96,768]{1,0:T(8,128)(2,1)S(1)}, u32[]{:S(2)}, u32[]{:S(2)}) collective-permute-start(bf16[96,768]{1,0:T(8,128)(2,1)S(1)} %get-tuple-element.176.refs_0_), channel_id=1, source_target_pairs={{0,24},{1,25},{2,26},{3,27},{4,28},{5,29},{6,30},{7,31},{8,16},{9,... | collective-permute-start | bytes 442376 | tf_op jit(solution)/shard_map/ppermute | solution.py:619
  65.0 9.1 %collective-permute-start.17 = (bf16[272,768]{1,0:T(8,128)(2,1)S(1)}, bf16[272,768]{1,0:T(8,128)(2,1)S(1)}, u32[]{:S(2)}, u32[]{:S(2)}) collective-permute-start(bf16[272,768]{1,0:T(8,128)(2,1)S(1)} %get-tuple-element.175.refs_0_), channel_id=1, source_target_pairs={{0,2},{1,3},{2,0},{3,1},{4,6},{5,7},{6,4},{7,5},{8,10},{9,11},{10,... | collective-permute-start | bytes 1253384 | tf_op jit(solution)/shard_map/ppermute | solution.py:611
  67.7 7.7 %collective-permute-start.16 = (bf16[192,768]{1,0:T(8,128)(2,1)S(1)}, bf16[192,768]{1,0:T(8,128)(2,1)S(1)}, u32[]{:S(2)}, u32[]{:S(2)}) collective-permute-start(bf16[192,768]{1,0:T(8,128)(2,1)S(1)} %get-tuple-element.174), channel_id=1, source_target_pairs={{0,8},{1,5},{2,10},{3,7},{4,12},{5,1},{6,14},{7,3},{8,0},{9,13},{1... | collective-permute-start | bytes 884744 | tf_op jit(solution)/shard_map/ppermute | solution.py:619
  74.2 1.3 %collective-permute-start.19 = (bf16[16,768]{1,0:T(8,128)(2,1)S(1)}, bf16[16,768]{1,0:T(8,128)(2,1)S(1)}, u32[]{:S(2)}, u32[]{:S(2)}) collective-permute-start(bf16[16,768]{1,0:T(8,128)(2,1)S(1)} %get-tuple-element.179.refs_5_), channel_id=1, source_target_pairs={{0,1},{1,0},{2,3},{3,2},{4,5},{5,4},{6,7},{7,6},{8,9},{9,8},{10,11... | collective-permute-start | bytes 73736 | tf_op jit(solution)/shard_map/ppermute | solution.py:608
  74.3 6.2 %collective-permute-start.21 = (bf16[96,768]{1,0:T(8,128)(2,1)S(1)}, bf16[96,768]{1,0:T(8,128)(2,1)S(1)}, u32[]{:S(2)}, u32[]{:S(2)}) collective-permute-start(bf16[96,768]{1,0:T(8,128)(2,1)S(1)} %get-tuple-element.184.refs_0_), channel_id=1, source_target_pairs={{0,8},{1,5},{2,10},{3,7},{4,12},{5,1},{6,14},{7,3},{8,0},{9,13},{1... | collective-permute-start | bytes 442376 | tf_op jit(solution)/shard_map/ppermute | solution.py:619
  76.3 12.4 %collective-permute-start.23 = (bf16[208,768]{1,0:T(8,128)(2,1)S(1)}, bf16[208,768]{1,0:T(8,128)(2,1)S(1)}, u32[]{:S(2)}, u32[]{:S(2)}) collective-permute-start(bf16[208,768]{1,0:T(8,128)(2,1)S(1)} %get-tuple-element.190.refs_0_), channel_id=1, source_target_pairs={{0,24},{1,25},{2,26},{3,27},{4,28},{5,29},{6,30},{7,31},{8,16},{9,... | collective-permute-start | bytes 958472 | tf_op jit(solution)/shard_map/ppermute | solution.py:619
  78.5 0.7 copy-start.1
  80.6 12.8 %collective-permute-start.22 = (bf16[192,768]{1,0:T(8,128)(2,1)S(1)}, bf16[192,768]{1,0:T(8,128)(2,1)S(1)}, u32[]{:S(2)}, u32[]{:S(2)}) collective-permute-start(bf16[192,768]{1,0:T(8,128)(2,1)S(1)} %get-tuple-element.189.refs_1_), channel_id=1, source_target_pairs={{0,4},{1,9},{2,6},{3,11},{4,0},{5,13},{6,2},{7,15},{8,12},{9,1},{1... | collective-permute-start | bytes 884744 | tf_op jit(solution)/shard_map/ppermute | solution.py:619
  81.5 13.5 %collective-permute-start.20 = (bf16[256,768]{1,0:T(8,128)(2,1)S(1)}, bf16[256,768]{1,0:T(8,128)(2,1)S(1)}, u32[]{:S(2)}, u32[]{:S(2)}) collective-permute-start(bf16[256,768]{1,0:T(8,128)(2,1)S(1)} %get-tuple-element.183), channel_id=1, source_target_pairs={{0,2},{1,3},{2,0},{3,1},{4,6},{5,7},{6,4},{7,5},{8,10},{9,11},{10,... | collective-permute-start | bytes 1179656 | tf_op jit(solution)/shard_map/ppermute | solution.py:611
  88.7 9.6 %collective-permute-start.24 = (bf16[208,768]{1,0:T(8,128)(2,1)S(1)}, bf16[208,768]{1,0:T(8,128)(2,1)S(1)}, u32[]{:S(2)}, u32[]{:S(2)}) collective-permute-start(bf16[208,768]{1,0:T(8,128)(2,1)S(1)} %get-tuple-element.196.refs_0_), channel_id=1, source_target_pairs={{0,8},{1,5},{2,10},{3,7},{4,12},{5,1},{6,14},{7,3},{8,0},{9,13},{1... | collective-permute-start | bytes 958472 | tf_op jit(solution)/shard_map/ppermute | solution.py:619
  98.4 10.2 %collective-permute-start.25 = (bf16[400,768]{1,0:T(8,128)(2,1)S(1)}, bf16[400,768]{1,0:T(8,128)(2,1)S(1)}, u32[]{:S(2)}, u32[]{:S(2)}) collective-permute-start(bf16[400,768]{1,0:T(8,128)(2,1)S(1)} %get-tuple-element.198.refs_1_), channel_id=1, source_target_pairs={{0,4},{1,9},{2,6},{3,11},{4,0},{5,13},{6,2},{7,15},{8,12},{9,1},{1... | collective-permute-start | bytes 1843208 | tf_op jit(solution)/shard_map/ppermute | solution.py:619

commit v6 on v5

--- a/solution.py
+++ b/solution.py
@@ -71,6 +71,9 @@
     return jnp.concatenate([both[:HEAD_DIM, :LEN], both[HEAD_DIM:, LEN:]], axis=0)
 
 
+COSTS = (100, 100, 100, 100, 100, 100, 100, 100, 100, 0, 0, 0, 0, 150, 0, 60, 0, 0, 30, 0, 0, 0, 0, 0, 0, 0, 0, 0, 0, 0, 0)
+
+
 class IO:
     def __init__(self, reads, writes):
         self.reads, self.writes = reads, writes
@@ -99,10 +102,12 @@
 
 class Chain:
     def __init__(self):
-        self.token = None
-
-    def call(self, kernel, name, args, outs, kinds, scratch=(), limit=16, weight=1):
+        self.token, self.calls = None, 0
+
+    def call(self, kernel, name, args, outs, kinds, scratch=(), limit=16, aliases={}):
         ins, out_kinds = kinds.split("-")
+        cost = COSTS[min(self.calls, len(COSTS) - 1)]
+        self.calls += 1
         assert len(ins) == len(args) and len(out_kinds) == len(outs)
         hbm = pl.BlockSpec(memory_space=pltpu.HBM)
         vmem = pl.BlockSpec(memory_space=pltpu.VMEM)
@@ -141,9 +146,10 @@
             in_specs=[spec(kind) for kind in ins] + [vmem] * len(tokens),
             out_specs=[spec(kind) for kind in out_kinds] + [vmem],
             out_shape=[*outs, f32(8, 128)],
+            input_output_aliases=aliases,
             scratch_shapes=[*buffers, pltpu.SemaphoreType.DMA((max(n_buf, 1),)), *scratch],
             compiler_params=pltpu.CompilerParams(vmem_limit_bytes=limit * MIB),
-            cost_estimate=pl.CostEstimate(flops=weight * 10**10, bytes_accessed=10**8, transcendentals=0),
+            cost_estimate=pl.CostEstimate(flops=cost * 10**8, bytes_accessed=10**8, transcendentals=0),
             name=name,
         )(*(pinned(a) if kind in "hclp" else a for a, kind in zip(args, ins)), *tokens)
         return results
@@ -282,15 +288,15 @@
     return near, others
 
 
-def feed_body(x, oa, ob, g, wo, gain_ref, bias_ref, fc1_ref, b1, fc2_ref, h_ref, a2_ref, z_ref, du_ref):
-    h = x.astype(F32) + dot_nn(oa, wo[0][...]) + dot_nn(ob, wo[1][...])
+def feed_body(x, oa, ob, g, wo_ref, gain_ref, bias_ref, fc1_ref, b1, fc2_ref, h_ref, a2_ref, z_ref, du_ref):
+    h = x.astype(F32) + dot_nn(jnp.concatenate([oa, ob], axis=1), wo_ref[...])
     h_ref[...] = h
     xh, _ = normalise(h)
     a2 = (xh * gain_ref[...][None, :] + bias_ref[...][None, :]).astype(BF16)
     a2_ref[...] = a2
     shard = fc2_ref.shape[0] // 2
     b1 = jnp.concatenate([b[3 * shard : 3 * shard + 1, :shard] for b in b1], axis=1).astype(F32)
-    u = dot_nt(a2, fc1_ref[...]) + b1
+    u = dot_nt(a2, fc1_ref[: 2 * shard]) + b1
     dz = dot_nt(g, fc2_ref[...])
     phi = 0.5 * (1.0 + lax.erf(u * (0.5**0.5)))
     slope = phi + u * (jnp.exp(-0.5 * u * u) * 0.3989422804014327)
@@ -301,44 +307,56 @@
     return a2, z, du
 
 
-def feed_far(chain, bits, x, oa, packet, gain, bias, fc1, fc2, wo, near, fars):
+def pack_far(chain, bits, wo, fc1, fars):
+    shard, d = fars[0].shape
+    width = 2 * shard
+
+    def kernel(io, bits_ref, wo_near, fc1_near, y0, x0, y1, x1, wo_ref, fc1_ref, sems):
+        near = copies(sems.at[4:], [(wo_near, wo_ref.at[:width]), (fc1_near, fc1_ref.at[:width])])
+
+        def both(first, second):
+            pairs = []
+            for at in range(2):
+                here = slice(width + at * shard, width + (at + 1) * shard)
+                pairs += [(first[at], wo_ref.at[here]), (second[at], fc1_ref.at[here])]
+            finish(copies(sems, pairs))
+
+        pl.when(bits_ref[2] == 0)(lambda: both((y0, y1), (x0, x1)))
+        pl.when(bits_ref[2] != 0)(lambda: both((x0, x1), (y0, y1)))
+        finish(near)
+
+    return chain.call(
+        kernel, "pack_far", (bits, wo, fc1, *fars), [bf16(2 * width, d), bf16(2 * width, d)], "svvvvvv-vv", limit=4,
+        scratch=[pltpu.SemaphoreType.DMA((6,))],
+    )
+
+
+def feed_far(chain, x, oa, packet, gain, bias, fc1, fc2, wo, near):
+    rows, d = x.shape
+    width = fc2.shape[0]
+
+    def kernel(io, x_ref, oa_ref, packet_ref, gain_ref, bias_ref, fc1_ref, fc2_ref, wo_ref, b10, b11, *outs):
+        feed_body(
+            x_ref[...], oa_ref[...], packet_ref[:, d:], packet_ref[:, :d], wo_ref, gain_ref, bias_ref, fc1_ref,
+            (b10, b11), fc2_ref, *outs,
+        )
+
+    return chain.call(
+        kernel, "feed_far", (x, oa, packet, gain, bias, fc1, fc2, wo, *near),
+        [f32(rows, d), bf16(rows, d), bf16(rows, width), bf16(rows, width)], "v" * 10 + "-vvvv",
+    )
+
+
+def feed_own(chain, x, packet, g, ob, gain, bias, fc1, fc2, wo, near, far):
     rows, d = x.shape
     width = fc2.shape[0]
     shard = width // 2
 
-    def kernel(io, bits_ref, x_ref, oa_ref, packet_ref, gain_ref, bias_ref, fc1_ref, fc2_ref, wo_ref, b10, b11,
-               y0, x0, y1, x1, h_ref, a2_ref, z_ref, du_ref, wo_far, fc1_far, sems):
-        def both(first, second):
-            pairs = []
-            for at in range(2):
-                here = slice(at * shard, (at + 1) * shard)
-                pairs += [(first[at], wo_far.at[here]), (second[at], fc1_far.at[here])]
-            finish(copies(sems, pairs))
-
-        pl.when(bits_ref[2] == 0)(lambda: both((y0, y1), (x0, x1)))
-        pl.when(bits_ref[2] != 0)(lambda: both((x0, x1), (y0, y1)))
-        feed_body(
-            x_ref[...], oa_ref[...], packet_ref[:, d:], packet_ref[:, :d], (wo_ref, wo_far), gain_ref, bias_ref,
-            fc1_ref, (b10, b11), fc2_ref, h_ref, a2_ref, z_ref, du_ref,
-        )
-
-    return chain.call(
-        kernel, "feed_far", (bits, x, oa, packet, gain, bias, fc1, fc2, wo, *near, *fars),
-        [f32(rows, d), bf16(rows, d), bf16(rows, width), bf16(rows, width), bf16(width, d), bf16(width, d)],
-        "s" + "v" * 14 + "-vvvvvv", scratch=[pltpu.SemaphoreType.DMA((4,))],
-    )
-
-
-def feed_own(chain, x, packet, g, ob, gain, bias, fc1, fc2, wos, near, far):
-    rows, d = x.shape
-    width = fc2.shape[0]
-    shard = width // 2
-
-    def kernel(io, x_ref, oa_ref, g_ref, ob_ref, gain_ref, bias_ref, fc1_ref, fc2_ref, wo0, wo1, b10, b11,
+    def kernel(io, x_ref, oa_ref, g_ref, ob_ref, gain_ref, bias_ref, fc1_ref, fc2_ref, wo_ref, b10, b11,
                z1, du1, a1, g1, h_ref, a2_ref, z_ref, du_ref, keep_ref, send_ref, sums_ref):
         a2, z, du = feed_body(
-            x_ref[...], oa_ref[:, d:], ob_ref[...], g_ref[...], (wo0, wo1), gain_ref, bias_ref, fc1_ref,
-            (b10, b11), fc2_ref, h_ref, a2_ref, z_ref, du_ref,
+            x_ref[...], oa_ref[:, d:], ob_ref[...], g_ref[...], wo_ref, gain_ref, bias_ref, fc1_ref, (b10, b11),
+            fc2_ref, h_ref, a2_ref, z_ref, du_ref,
         )
         first = dot_tn(du, a2) + dot_tn(du1[...], a1[...])
         second = dot_tn(z, g_ref[...]) + dot_tn(z1[...], g1[:, :d])
@@ -351,9 +369,9 @@
         )
 
     return chain.call(
-        kernel, "feed_own", (x, packet, g, ob, gain, bias, fc1, fc2, *wos, *near, *far),
-        [f32(rows, d), bf16(rows, d), bf16(rows, width), bf16(rows, width), bf16(2, shard, d),
-         bf16(2, shard, d), f32(1, width)], "v" * 16 + "-vvvvvvv",
+        kernel, "feed_own", (x, packet, g, ob, gain, bias, fc1, fc2, wo, *near, *far),
+        [f32(rows, d), bf16(rows, d), bf16(rows, width), bf16(rows, width), bf16(2, shard, d), bf16(2, shard, d),
+         f32(1, width)], "v" * 15 + "-vvvvvvv",
     )
 
 
@@ -370,14 +388,14 @@
 
 
 def backward(chain, args, own):
-    h, kt = args[4], args[10]
+    h, kt = args[3], args[9]
     rows, d = h.shape
     width = kt.shape[0]
     mols, pairs = rows // LEN, width // PAIR
 
-    def kernel(io, du_ref, dr_ref, fc1_ref, fc1_far, h_ref, g_ref, gain_ref, wo_ref, p_ref, qt_ref, kt_ref, v_ref,
+    def kernel(io, du_ref, dr_ref, fc1_ref, h_ref, g_ref, gain_ref, wo_ref, p_ref, qt_ref, kt_ref, v_ref,
                gh_ref, dp_ref, dh_ref=None, sums_ref=None):
-        da2 = dot_nn(du_ref[...], fc1_ref[...]) + dot_nn(dr_ref[...], fc1_far[...])
+        da2 = dot_nn(jnp.concatenate([du_ref[...], dr_ref[...]], axis=1), fc1_ref[...])
         xh, r = normalise(h_ref[...])
         dh = g_ref[:, :d].astype(F32) + norm_back(da2, gain_ref[...][None, :], xh, r)
         if own:
@@ -387,7 +405,7 @@
             io.flush(2)
         gh = dh.astype(BF16)
         gh_ref[...] = gh
-        dot = dot_nt(wo_ref[...], gh).astype(BF16)
+        dot = dot_nt(wo_ref[:width], gh).astype(BF16)
         every = [(m, i) for m in range(mols) for i in range(pairs)]
         lanes = lambda m: slice(LEN * m, LEN * (m + 1))
         rows_of = lambda i: slice(PAIR * i, PAIR * (i + 1))
@@ -411,29 +429,26 @@
 
     outs = [bf16(rows, d), bf16(3 * width, rows)] + ([f32(rows, d), f32(8, d)] if own else [])
     return chain.call(
-        kernel, "attention_backward", args, outs, "v" * 12 + ("-vvvv" if own else "-vv"),
-    )
-
-
-def weight_grads(chain, name, shard, lefts, rights):
+        kernel, "attention_backward", args, outs, "v" * 11 + ("-vvvv" if own else "-vv"),
+    )
+
+
+def weight_grads(chain, name, shard, at, lefts, rights):
     d = rights[0][0].shape[1]
     args, count = [], len(lefts)
     for (u0, u1, _), (v0, v1) in zip(lefts, rights):
         args += [u0, u1, v0, v1]
 
     def kernel(io, *refs):
-        keep_ref, send_ref = refs[-2:]
-        for at, ref in ((1, send_ref), (0, keep_ref)):
-            for c in range(count):
-                u0, u1, v0, v1 = refs[4 * c : 4 * c + 4]
-                rows = slice(lefts[c][2] + at * shard, lefts[c][2] + (at + 1) * shard)
-                left = jnp.concatenate([u0[rows], u1[rows]], axis=1)
-                right = jnp.concatenate([v0[...], v1[...]], axis=0)
-                ref[c] = dot_nn(left, right).astype(BF16)
-
-    return chain.call(
-        kernel, name, args, [bf16(count, shard, d), bf16(count, shard, d)], "v" * len(args) + "-vv",
-    )
+        out_ref = refs[-1]
+        for c in range(count):
+            u0, u1, v0, v1 = refs[4 * c : 4 * c + 4]
+            rows = slice(lefts[c][2] + at * shard, lefts[c][2] + (at + 1) * shard)
+            left = jnp.concatenate([u0[rows], u1[rows]], axis=1)
+            right = jnp.concatenate([v0[...], v1[...]], axis=0)
+            out_ref[c] = dot_nn(left, right).astype(BF16)
+
+    return chain.call(kernel, name, args, [bf16(count, shard, d)], "v" * len(args) + "-v")[0]
 
 
 def input_grads(chain, dps, w, xs, sums, bias):
@@ -500,88 +515,139 @@
     return chain.call(kernel, "vector_rows", (mine, got), [bf16(16, d)], "vv-v", limit=4)[0]
 
 
-def sum_half(chain, bits, mine, got):
-    def kernel(io, bits_ref, mine_ref, got_ref, out_ref):
-        at = 1 - bits_ref[0]
-        out_ref[...] = mine_ref[at] + got_ref[at]
-
-    return chain.call(
-        kernel, "sum_half", (bits, mine, got), [bf16(*mine.shape[1:])], "svv-v", limit=8
-    )[0]
-
-
-def sum_quarter(chain, bits, mine, got, half, last=(), vec=()):
+def vector_cores(chain, mine, got, shard):
+    def kernel(io, mine_ref, got_ref, out_ref):
+        a, b = mine_ref[...].astype(F32), got_ref[...].astype(F32)
+        turned = jnp.concatenate([b[:, shard : 2 * shard], b[:, :shard], b[:, 2 * shard :]], axis=1)
+        same = lax.broadcasted_iota(jnp.int32, a.shape, 0) < 4
+        out_ref[...] = plus(a, jnp.where(same, b, turned))
+
+    return chain.call(kernel, "vector_cores", (mine, got), [bf16(*mine.shape)], "vv-v", limit=4)[0]
+
+
+def sum_half(chain, bits, mine, got, apart):
+    def kernel(io, bits_ref, mine_ref, got_ref, *outs):
+        half, quarter = 1 - bits_ref[0], bits_ref[1]
+        on_ref, kept_ref = outs if apart else (outs[0].at[0], outs[0].at[1])
+        on_ref[...] = mine_ref[half, 1 - quarter] + got_ref[half, 1 - quarter]
+        kept_ref[...] = mine_ref[half, quarter] + got_ref[half, quarter]
+
     rows, d = mine.shape[2:]
-
-    def kernel(io, bits_ref, mine_ref, got_ref, half_ref, *refs):
+    outs = [bf16(rows, d)] * 2 if apart else [bf16(2, rows, d)]
+    return chain.call(kernel, "sum_half", (bits, mine, got), outs, "svv-" + "v" * len(outs), limit=8)
+
+
+def sum_quarter(chain, bits, mine, got, kept, *more, vec=()):
+    rows, d = mine.shape[2:]
+    arrays = [a[0] if isinstance(a, tuple) else a for a in more]
+
+    def kernel(io, bits_ref, mine_ref, got_ref, *refs):
         *refs, out_ref = refs
-        first = bits_ref[0]
-        at = bits_ref[1] if last else 1 - bits_ref[1]
-        terms = [mine_ref[first, at], got_ref[first, at], half_ref[at]]
-        out_ref[:rows] = plus(*terms, *(ref[...] for ref in refs[: len(last)]))
+        half = bits_ref[0]
+        quarter = bits_ref[1] if kept else 1 - bits_ref[1]
+        terms = [ref[a[1]] if isinstance(a, tuple) else ref[...] for a, ref in zip(more, refs)]
+        out_ref[:rows] = plus(mine_ref[half, quarter], got_ref[half, quarter], *terms)
         if vec:
-            a, b = refs[-2][...].astype(F32), refs[-1][...].astype(F32)
-            shard = vec[2]
-            turned = jnp.concatenate([b[:, shard : 2 * shard], b[:, :shard], b[:, 2 * shard :]], axis=1)
-            same = lax.broadcasted_iota(jnp.int32, a.shape, 0) < 4
-            out_ref[rows:] = plus(a, jnp.where(same, b, turned))
-
-    args = (bits, mine, got, half, *last, *vec[:2])
+            out_ref[rows:] = refs[-1][...]
+
+    args = (bits, mine, got, *arrays, *vec)
     return chain.call(
         kernel, "sum_quarter", args, [bf16(rows + (16 if vec else 0), d)], "s" + "v" * (len(args) - 1) + "-v",
         limit=8,
     )[0]
 
 
-def sum_two(chain, a, b):
-    def kernel(io, a_ref, b_ref, out_ref):
-        out_ref[...] = a_ref[...] + b_ref[...]
-
-    return chain.call(kernel, "sum_two", (a, b), [bf16(*a.shape)], "vv-v", limit=8)[0]
-
-
-def side_by_side(chain, mine, got, rows):
-    extra = mine.shape[0] - rows
-
-    def kernel(io, mine_ref, got_ref, out_ref):
-        out_ref[:rows] = mine_ref[:rows]
-        out_ref[rows : 2 * rows] = got_ref[:rows]
-        if extra:
-            out_ref[2 * rows :] = mine_ref[rows:] + got_ref[rows:]
-
-    return chain.call(
-        kernel, "side_by_side", (mine, got), [bf16(2 * rows + extra, mine.shape[1])], "vv-v", limit=8
+def sum_quarter_apart(chain, bits, mine, got, *more):
+    rows, d = mine.shape[2:]
+    arrays = [a[0] if isinstance(a, tuple) else a for a in more]
+
+    def kernel(io, bits_ref, mine_ref, got_ref, *refs):
+        *refs, upper_ref, lower_ref = refs
+        half, quarter = bits_ref[0], bits_ref[1]
+        terms = [ref[a[1]] if isinstance(a, tuple) else ref[...] for a, ref in zip(more, refs)]
+        total = plus(mine_ref[half, quarter], got_ref[half, quarter], *terms)
+        upper_ref[...] = total[: rows // 2]
+        lower_ref[...] = total[rows // 2 :]
+
+    args = (bits, mine, got, *arrays)
+    return chain.call(
+        kernel, "sum_quarter", args, [bf16(rows // 2, d)] * 2, "s" + "v" * (len(args) - 1) + "-vv", limit=8
+    )
+
+
+def side_by_side(chain, a, b, apart):
+    rows, d = a.shape
+
+    def kernel(io, a_ref, b_ref, *outs):
+        first, second = outs if apart else (outs[0].at[:rows], outs[0].at[rows:])
+        first[...] = a_ref[...]
+        second[...] = b_ref[...]
+
+    outs = [bf16(rows, d)] * 2 if apart else [bf16(2 * rows, d)]
+    return chain.call(kernel, "side_by_side", (a, b), outs, "vv-" + "v" * len(outs), limit=8)
+
+
+def sum_pairs(chain, *pairs):
+    rows = [a.shape[0] for a, _ in pairs]
+
+    def kernel(io, *refs):
+        *refs, out_ref = refs
+        start = 0
+        for a_ref, b_ref in zip(refs[::2], refs[1::2]):
+            out_ref[start : start + a_ref.shape[0]] = a_ref[...] + b_ref[...]
+            start += a_ref.shape[0]
+
+    args = [a for pair in pairs for a in pair]
+    return chain.call(
+        kernel, "sum_pairs", args, [bf16(sum(rows), args[0].shape[1])], "v" * len(args) + "-v", limit=8
     )[0]
 
 
-def place_sums(chain, bits, mine, got, rows, outs, vec=()):
-    d = mine.shape[1]
-
-    def kernel(io, bits_ref, mine_ref, got_ref, *refs):
-        out_refs, vec_refs = refs[: len(outs)], refs[len(outs) : -2]
-        all_ref, sems = refs[-2:]
-        for at, ref in enumerate((mine_ref, got_ref)):
-            half = bits_ref[0] if at == 0 else 1 - bits_ref[0]
-            for part in range(2):
-                quarter = bits_ref[1] if part == 0 else 1 - bits_ref[1]
-                start = pl.multiple_of((2 * half + quarter) * rows, 16)
-                all_ref[pl.ds(start, rows), :] = ref[part * rows : (part + 1) * rows].astype(F32)
-        pairs, start = [], 0
-        for ref in out_refs:
-            for piece in [ref] if len(ref.shape) == 2 else [ref.at[c] for c in range(ref.shape[0])]:
-                pairs.append((all_ref.at[start : start + piece.shape[0]], piece))
-                start += piece.shape[0]
-        started = copies(sems, pairs)
+def place_sums(chain, bits, quarters, rows, targets, outs, whole=(), vec=(), skip=0):
+    d = quarters[0][0].shape[1]
+    n = len(outs)
+    arrays = []
+    for a, *_ in quarters:
+        if not any(a is b for b in arrays):
+            arrays.append(a)
+    which = [next(k for k, b in enumerate(arrays) if b is a) for a, *_ in quarters]
+
+    def kernel(io, bits_ref, *refs):
+        refs, (buf, sems) = refs[:-2], refs[-2:]
+        ins = [refs[k] for k in which]
+        refs = refs[len(arrays) + len(whole) :]
+        out_refs, vec_refs = refs[:n], refs[n:]
+
+        def each(step):
+            for j, (_, _, half, quarter) in enumerate(quarters):
+                if j < skip:
+                    continue
+                half = 1 - bits_ref[0] if half else bits_ref[0]
+                quarter = 1 - bits_ref[1] if quarter else bits_ref[1]
+                for at, (out, index, first) in enumerate(targets):
+                    ref = out_refs[out]
+                    ref = ref if index is None else ref.at[index]
+                    ref = ref.at[first : first + rows]
+                    copy = pltpu.make_async_copy(buf.at[j], ref, sems.at[j])
+                    pl.when(2 * half + quarter == at)(functools.partial(step, copy))
+
+        starts = [start for _, start, _, _ in quarters]
+        for j, ref in enumerate(ins):
+            if j >= skip:
+                buf[j] = ref[starts[j] : starts[j] + rows].astype(F32)
+        each(lambda copy: copy.start())
         if vec:
-            total = mine_ref[2 * rows :].astype(F32) + got_ref[2 * rows :].astype(F32)
-            for at, (n, ref) in enumerate(zip(vec, vec_refs)):
-                ref[...] = total[at, :n]
-        finish(started)
-
-    return chain.call(
-        kernel, "place_sums", (bits, mine, got), [*outs, *(f32(n) for n in vec)],
-        "svv-" + "r" * len(outs) + "v" * len(vec), limit=8,
-        scratch=[pltpu.VMEM((4 * rows, d), F32), pltpu.SemaphoreType.DMA((4,))],
+            a, b, c, e = (ref[x + rows : x + rows + 16].astype(F32) for ref, x in zip(ins, starts))
+            total = jnp.where(bits_ref[5] == 0, (a + b) + (c + e), (a + c) + (b + e))
+            for at, (length, ref) in enumerate(zip(vec, vec_refs)):
+                ref[...] = total[at, :length]
+        each(lambda copy: copy.wait())
+
+    return chain.call(
+        kernel, "place_sums", (bits, *arrays, *whole), [*outs, *(f32(length) for length in vec)],
+        "s" + "v" * len(arrays) + "p" * len(whole) + "-" + "r" * n + "v" * len(vec), limit=8,
+        aliases={1 + len(arrays) + j: j for j in range(len(whole))},
+        scratch=[pltpu.VMEM((len(quarters), rows, d), F32), pltpu.SemaphoreType.DMA((len(quarters),))],
     )
 
 
@@ -597,10 +663,10 @@
     tensor_at = lax.axis_index("tensor")
     core = tensor_at % 2
     bit0 = dp_at % 2
-    bit1 = (dp_at // 2 + dp_at // 4) % 2
+    bit1 = (dp_at // 2) % 2
     bits = jnp.stack(
         [jnp.where(core == 0, bit0, bit1), jnp.where(core == 0, bit1, bit0), bit0, tensor_at * mols,
-         (tensor_at ^ 2) * mols]
+         (tensor_at ^ 2) * mols, core]
     ).astype(jnp.int32)
     chain = Chain()
 
@@ -620,7 +686,7 @@
 
     swap_first = lambda a: swap_dp(a, 1, 2)
     swap_second = lambda a: swap_dp(a, 2, 1)
-    far_masks = [6 if k == 2 else 1 << k for k in range(2, n_dp.bit_length() - 1)]
+    far_masks = [1 << k for k in range(2, n_dp.bit_length() - 1)]
 
     w_got = swap_core(qkv_weight)
     x_got = swap_y(tokens)
@@ -647,82 +713,102 @@
     o_got = swap_y(o_1)
     fars = (far_y, far_x, swap_core(far_y), swap_core(far_x))
     norm2 = (ln2_gain, ln2_bias)
-    h_1, a2_1, z_1, du_1, wo_far, fc1_far = feed_far(
-        chain, bits, x_got, o_1, packet_got, *norm2, fc1, fc2, wo, near, fars
-    )
+    wo, fc1 = pack_far(chain, bits, wo, fc1, fars)
+    h_1, a2_1, z_1, du_1 = feed_far(chain, x_got, o_1, packet_got, *norm2, fc1, fc2, wo, near)
     dr_0 = swap_y(du_1)
     h_0, a2_0, z_0, du_0, keep_r, send_r, bias_sums = feed_own(
-        chain, tokens, packet, out_grad, o_got, *norm2, fc1, fc2, (wo, wo_far), near,
-        (z_1, du_1, a2_1, packet_got),
+        chain, tokens, packet, out_grad, o_got, *norm2, fc1, fc2, wo, near, (z_1, du_1, a2_1, packet_got)
     )
     dr_1 = swap_y(du_0)
-    got_r = swap_core(send_r)
+
+    class Sum:
+        def __init__(self, count, keep, got, apart, early):
+            self.size = count * shard // 4
+            self.apart, self.early = apart, early
+            view = lambda a: a.reshape(2, 2, self.size, d)
+            self.parts = (view(keep), view(got))
+
+        def first(self):
+            sent = sum_half(chain, bits, *self.parts, self.apart)
+            got = [swap_first(a) for a in sent]
+            self.on, self.kept = got if self.apart else ((got[0], 0), (got[0], 1))
+
+        def second(self):
+            self.got = swap_second(sum_quarter(chain, bits, *self.parts, False, self.on))
+
+        def third(self, *vec):
+            self.sum = sum_quarter(chain, bits, *self.parts, True, self.kept, self.got, vec=vec)
+            self.got = swap_dp(self.sum, far_masks[0], far_masks[0])
+
+        def third_apart(self):
+            self.sums = sum_quarter_apart(chain, bits, *self.parts, self.kept, self.got)
+            self.gots = [swap_dp(a, far_masks[0], far_masks[0]) for a in self.sums]
+            self.halves = [None, None]
+
+        def fourth_apart(self, at, *vec):
+            self.sum, self.got = self.sums[at], self.gots[at]
+            self.fourth(*vec)
+            self.halves[at] = self.quarters
+
+        def fourth(self, *vec):
+            a = sum_pairs(chain, (self.sum, self.got), *vec)
+            for mask in far_masks[1:]:
+                a = sum_pairs(chain, (a, swap_dp(a, mask, mask)))
+            b = swap_second(a)
+            if self.early == 1:
+                self.quarters = [(a, 0, 0, 0), (b, 0, 0, 1), (swap_first(a), 0, 1, 0), (swap_first(b), 0, 1, 1)]
+            self.last = (a, b)
+
+        def fifth(self):
+            if self.early == 0:
+                (a,) = side_by_side(chain, *self.last, False)
+                b = swap_first(a)
+                rows = a.shape[0] // 2
+                self.quarters = [(a, 0, 0, 0), (a, rows, 0, 1), (b, 0, 1, 0), (b, rows, 1, 1)]
+            if self.early == 2:
+                a, b = side_by_side(chain, *self.last, True)
+                self.quarters = [(a, 0, 0, 0), (b, 0, 0, 1), (swap_first(a), 0, 1, 0), (swap_first(b), 0, 1, 1)]
+
     gh_0, dp_0, dh, sums = backward(
-        chain, (du_0, dr_0, fc1, fc1_far, h_0, out_grad, ln2_gain, wo, p_0, qt_0, kt_0, v_0), True
-    )
-
-    class Sum:
-        def __init__(self, count, keep, got):
-            self.size = count * shard // 4
-            self.keep, self.got = keep, got
-
-        def first(self):
-            half = lambda a: a.reshape(2, 2 * self.size, d)
-            got = swap_first(sum_half(chain, bits, half(self.keep), half(self.got)))
-            quarters = lambda a: a.reshape(2, 2, self.size, d)
-            self.view = (quarters(self.keep), quarters(self.got), got.reshape(2, self.size, d))
-
-        def second(self):
-            self.last = swap_second(sum_quarter(chain, bits, *self.view))
-
-        def third(self, vec=()):
-            self.sum = sum_quarter(chain, bits, *self.view, (self.last,), vec)
-            self.last = swap_dp(self.sum, far_masks[0], far_masks[0])
-
-        def fourth(self):
-            self.sum = sum_two(chain, self.sum, self.last)
-            for mask in far_masks[1:]:
-                self.sum = sum_two(chain, self.sum, swap_dp(self.sum, mask, mask))
-            self.last = swap_second(self.sum)
-
-        def fifth(self):
-            self.both = side_by_side(chain, self.sum, self.last, self.size)
-            self.last = swap_first(self.both)
-
-        def place(self, outs, vec=()):
-            return place_sums(chain, bits, self.both, self.last, self.size, outs, vec)
-
-    r = Sum(2, keep_r, got_r)
+        chain, (du_0, dr_0, fc1, h_0, out_grad, ln2_gain, wo, p_0, qt_0, kt_0, v_0), True
+    )
+    r = Sum(2, keep_r, swap_core(send_r), True, 1)
     r.first()
     gh_1, dp_1 = backward(
-        chain, (du_1, dr_1, fc1, fc1_far, h_1, packet_got, ln2_gain, wo, p_1, qt_1, kt_1, v_1), False
+        chain, (du_1, dr_1, fc1, h_1, packet_got, ln2_gain, wo, p_1, qt_1, kt_1, v_1), False
     )
     a1s = (a1_0, a1_1)
-    keep_q, send_q = weight_grads(
-        chain, "weight_grads", shard, [(dp_0, dp_1, c * width) for c in range(3)] + [(ot_0, ot_1, 0)],
-        [a1s] * 3 + [(gh_0, gh_1)],
-    )
-    q = Sum(4, keep_q, swap_core(send_q))
+    lefts = [(dp_0, dp_1, c * width) for c in range(3)] + [(ot_0, ot_1, 0)]
+    rights = [a1s] * 3 + [(gh_0, gh_1)]
+    got_q = swap_core(weight_grads(chain, "weight_grads", shard, 1, lefts, rights))
+    q = Sum(4, weight_grads(chain, "weight_grads", shard, 0, lefts, rights), got_q, True, 2)
     r.second()
     q.first()
+    r.third()
     da1_mine, da1_theirs = input_grads(chain, (dp_0, dp_1), w_qkv, (tokens, x_got), sums, bias_sums)
     da1_got = swap_y(da1_theirs)
-    r.third()
     q.second()
     r.fourth()
-    vec = vector_rows(chain, da1_theirs, da1_got)
-    q.third((vec, swap_core(vec), shard))
     res_mine, res_theirs = feed_result(chain, (z_0, z_1), fc2, h_0)
     res_got = swap_y(res_theirs)
+    q.third()
+    vec = vector_rows(chain, da1_theirs, da1_got)
+    vec_got = swap_core(vec)
+    r.fifth()
+    halves = [(c, None, half * shard // 2) for c in range(2) for half in range(2)]
+    grad_fc1, grad_fc2 = place_sums(chain, bits, r.quarters, r.size, halves, [f32(shard, d)] * 2)
+    vec = vector_cores(chain, vec, vec_got, shard)
+    vec_got = swap_dp(vec, far_masks[0], far_masks[0])
+    result = add_result(chain, res_mine, res_got)
+    q.fourth((vec, vec_got))
     grad_tokens = input_norm(chain, tokens, ln1_gain, da1_mine, da1_got, dh)
-    r.fifth()
-    q.fourth()
-    rows = f32(shard, d)
-    grad_fc1, grad_fc2 = r.place([rows, rows])
-    result = add_result(chain, res_mine, res_got)
     q.fifth()
-    grad_qkv, grad_out, gain1, bias1, gain2, bias2, grad_b = q.place(
-        [f32(3, shard, d), rows], (d, d, d, d, shard)
+    each = [(0, 0, 0), (0, 1, 0), (0, 2, 0), (1, None, 0)]
+    outs = [f32(3, shard, d), f32(shard, d)]
+    grads = place_sums(chain, bits, q.quarters[:2], q.size, each, outs)
+    grads = place_sums(chain, bits, q.quarters[:3], q.size, each, outs, grads, skip=2)
+    grad_qkv, grad_out, gain1, bias1, gain2, bias2, grad_b = place_sums(
+        chain, bits, q.quarters, q.size, each, outs, grads, (d, d, d, d, shard), 3
     )
     return (
         result, grad_tokens, gain1, bias1, grad_qkv, grad_out, gain2, bias2, grad_fc1, grad_b, grad_fc2,

time: 112 us -> 109 us (0.973)
  waiting for transfers between devices: 38.6 us -> 35.2 us
  Pallas kernels: 35.5 us -> 37.4 us
  starting transfers between devices: 36.1 us -> 34.9 us
    ppermute x8, waiting for transfers between devices: 13.9 us -> 8.48 us  [swap_y(): return lax.ppermute(a, 'tensor', [(t, t ^ 2) for t in range(n_tensor)])]
    ppermute x11 -> x16, waiting for transfers between devices: 23.7 us -> 25.8 us  [swap_dp(): return lax.ppermute(a, ('dp', 'tensor'), pairs)]
    pallas_call x27 -> x31, Pallas kernels: 35.5 us -> 37.4 us  [call(): pl.pallas_call(body, in_specs=[spec(kind) for kind in ins] + [vmem] * len...]
    ppermute x11 -> x16, starting transfers between devices: 23.1 us -> 22.1 us  [swap_dp(): return lax.ppermute(a, ('dp', 'tensor'), pairs)]
  transfers between devices with their start and end apart: 26 -> 31, of which waited for: 14 -> 17; matrix products, arithmetic and copies ran while one was open for 0% -> 0% of each run, Pallas kernels for 28% -> 31%
where the time goes in v6:
time: 109 us
  Pallas kernels  37.4 us (34%)
  waiting for transfers between devices  35.2 us (32%)
  starting transfers between devices  34.9 us (32%)
  between operations  1.18 us (1%)
    pallas_call x31, Pallas kernels, call(): pl.pallas_call(body, in_specs=[spec(kind) for kind in ins] + [vmem] * len...  37.4 us
    ppermute x16, waiting for transfers between devices, swap_dp(): return lax.ppermute(a, ('dp', 'tensor'), pairs)  25.8 us
    ppermute x16, starting transfers between devices, swap_dp(): return lax.ppermute(a, ('dp', 'tensor'), pairs)  22.1 us
    ppermute x8, starting transfers between devices, swap_y(): return lax.ppermute(a, 'tensor', [(t, t ^ 2) for t in range(n_tensor)])  12.1 us
    ppermute x8, waiting for transfers between devices, swap_y(): return lax.ppermute(a, 'tensor', [(t, t ^ 2) for t in range(n_tensor)])  8.48 us
  transfers between devices with their start and end apart: 31, of which 17 were waited for; matrix products, arithmetic and copies ran while one was open for 0% of the time, Pallas kernels for 31%

profile of v6, /device:TPU:0, one launch (start us, length us, event | category | flops | bytes accessed | tf_op | source)
XLA Modules:
  0.0 108.8 jit_solution(18370202193275200953)
XLA Ops:
  0.8 1.5 %pick.1 = (bf16[192,768]{1,0:T(8,128)(2,1)S(1)}, f32[8,128]{1,0:T(8,128)S(1)}) custom-call(s32[6]{0:T(128)S(1)} %stack.27.refs_0_, bf16[192,768]{1,0:T(8,128)(2,1)} %refs_0_.1, bf16[192,768]{1,0:T(8,128)(2,1)} %refs_1_.5), custom_call_target="tpu_custom_call" | custom-call | flops 10000000000 | bytes 100000000 | tf_op jit(solution)/shard_map/pick/pallas_call | solution.py:144
  2.3 3.0 %collective-permute-start.3 = (bf16[192,768]{1,0:T(8,128)(2,1)S(1)}, bf16[192,768]{1,0:T(8,128)(2,1)S(1)}, u32[]{:S(2)}, u32[]{:S(2)}) collective-permute-start(bf16[192,768]{1,0:T(8,128)(2,1)S(1)} %get-tuple-element.130), channel_id=1, source_target_pairs={{0,2},{1,3},{2,0},{3,1},{4,6},{5,7},{6,4},{7,5},{8,10},{9,11},{10,... | collective-permute-start | bytes 884744 | tf_op jit(solution)/shard_map/ppermute | solution.py:677
  5.5 1.5 %load.1 = (bf16[592,768]{1,0:T(8,128)(2,1)S(1)}, bf16[256,768]{1,0:T(8,128)(2,1)S(1)}, bf16[256,768]{1,0:T(8,128)(2,1)S(1)}, f32[768]{0:T(1024)S(1)}, f32[768]{0...) custom-call(bf16[192,768]{1,0:T(8,128)(2,1)} %refs_0_.1, bf16[192,768]{1,0:T(8,128)(2,1)} %refs_1_.5, ...), custom_call_target="tpu_custom_call" | custom-call | flops 10000000000 | bytes 100000000 | tf_op jit(solution)/shard_map/load/pallas_call | solution.py:144
  7.9 4.0 %attention_forward.2 = (bf16[256,768]{1,0:T(8,128)(2,1)S(1)}, bf16[384,256]{1,0:T(8,128)(2,1)S(1)}, bf16[384,256]{1,0:T(8,128)(2,1)S(1)}, bf16[256,384]{1,0:T(8,...) custom-call(s32[6]{0:T(128)S(1)} %stack.27.refs_0_, ...), custom_call_target="tpu_custom_call" | custom-call | flops 10000000000 | bytes 100000000 | tf_op jit(solution)/shard_map/attention_forward/pallas_call | solution.py:144
  11.9 1.3 %collective-permute-done.3.refs_0_ = bf16[192,768]{1,0:T(8,128)(2,1)S(1)} collective-permute-done((bf16[192,768]{1,0:T(8,128)(2,1)S(1)}, bf16[192,768]{1,0:T(8,128)(2,1)S(1)}, u32[]{:S(2)}, u32[]{:S(2)}) %collective-permute-start.3) | collective-permute-done | bytes 294944 | tf_op jit(solution)/shard_map/ppermute | solution.py:677
  13.3 2.1 %collective-permute-start.5 = (bf16[192,768]{1,0:T(8,128)(2,1)S(1)}, bf16[192,768]{1,0:T(8,128)(2,1)S(1)}, u32[]{:S(2)}, u32[]{:S(2)}) collective-permute-start(bf16[192,768]{1,0:T(8,128)(2,1)S(1)} %get-tuple-element.138.refs_3_), channel_id=1, source_target_pairs={{0,4},{1,5},{2,6},{3,7},{4,0},{5,1},{6,2},{7,3},{8,12},{9,13},{10,... | collective-permute-start | bytes 884744 | tf_op jit(solution)/shard_map/ppermute | solution.py:685
  15.4 1.5 %collective-permute-start.8 = (bf16[256,1152]{1,0:T(8,128)(2,1)S(1)}, bf16[256,1152]{1,0:T(8,128)(2,1)S(1)}, u32[]{:S(2)}, u32[]{:S(2)}) collective-permute-start(bf16[256,1152]{1,0:T(8,128)(2,1)S(1)} %get-tuple-element.127.refs_1_), channel_id=1, source_target_pairs={{0,2},{1,3},{2,0},{3,1},{4,6},{5,7},{6,4},{7,5},{8,10},{9,11},{10,... | collective-permute-start | bytes 1769480 | tf_op jit(solution)/shard_map/ppermute | solution.py:677
  16.9 4.4 %collective-permute-done.5.refs_4_ = bf16[192,768]{1,0:T(8,128)(2,1)S(1)} collective-permute-done((bf16[192,768]{1,0:T(8,128)(2,1)S(1)}, bf16[192,768]{1,0:T(8,128)(2,1)S(1)}, u32[]{:S(2)}, u32[]{:S(2)}) %collective-permute-start.5) | collective-permute-done | bytes 294944 | tf_op jit(solution)/shard_map/ppermute | solution.py:685
  21.6 3.5 %attention_forward.3 = (bf16[256,768]{1,0:T(8,128)(2,1)S(1)}, bf16[384,256]{1,0:T(8,128)(2,1)S(1)}, bf16[384,256]{1,0:T(8,128)(2,1)S(1)}, bf16[256,384]{1,0:T(8,...) custom-call(s32[6]{0:T(128)S(1)} %stack.27.refs_0_, ...), custom_call_target="tpu_custom_call" | custom-call | flops 10000000000 | bytes 100000000 | tf_op jit(solution)/shard_map/attention_forward/pallas_call | solution.py:144
  25.1 2.1 %collective-permute-start.4 = (bf16[256,384]{1,0:T(8,128)(2,1)S(1)}, bf16[256,384]{1,0:T(8,128)(2,1)S(1)}, u32[]{:S(2)}, u32[]{:S(2)}) collective-permute-start(bf16[256,384]{1,0:T(8,128)(2,1)S(1)} %get-tuple-element.133.refs_1_), channel_id=1, source_target_pairs={{0,2},{1,3},{2,0},{3,1},{4,6},{5,7},{6,4},{7,5},{8,10},{9,11},{10,... | collective-permute-start | bytes 589832 | tf_op jit(solution)/shard_map/ppermute | solution.py:677
  27.3 1.3 %pack_far.1 = (bf16[768,768]{1,0:T(8,128)(2,1)S(1)}, bf16[768,768]{1,0:T(8,128)(2,1)S(1)}, f32[8,128]{1,0:T(8,128)S(1)}) custom-call(s32[6]{0:T(128)S(1)} %stack.27.refs_0_, bf16[384,768]{1,0:T(8,128)(2,1)S(1)} %get-tuple-element.136.refs_1_, bf16[384,768]{1,0:T(8,128)(2,1)S(1)} %get-tuple-element.137.refs_2_, ...), custom_call_target="tpu_custom_call" | custom-call | flops 10000000000 | bytes 100000000 | tf_op jit(solution)/shard_map/pack_far/pallas_call | solution.py:144
  28.6 5.7 %collective-permute-done.8.refs_2_.refs_14_.refs_4_ = bf16[256,1152]{1,0:T(8,128)(2,1)S(1)} collective-permute-done((bf16[256,1152]{1,0:T(8,128)(2,1)S(1)}, bf16[256,1152]{1,0:T(8,128)(2,1)S(1)}, u32[]{:S(2)}, u32[]{:S(2)}) %collective-permute-start.8) | collective-permute-done | bytes 589856 | tf_op jit(solution)/shard_map/ppermute | solution.py:677
  34.2 1.2 %feed_far.1 = (f32[256,768]{1,0:T(8,128)S(1)}, bf16[256,768]{1,0:T(8,128)(2,1)S(1)}, bf16[256,384]{1,0:T(8,128)(2,1)S(1)}, bf16[256,384]{1,0:T(8,128)(2,1)S(1)}, f32[8,128]{1,0:T(8,128)S(1)}) custom-call(bf16[256,768]{1,0:T(8,128)(2,1)S(1)} %collective-permute-done.1.refs_3_.refs_0_.refs_4_, bf16[256,384]{1,0:T(8,128)(2,1)S(1)} %get-tuple-element.133.refs_1_, ...), custom_call_target="tpu_custom_call" | custom-call | flops 10000000000 | bytes 100000000 | tf_op jit(solution)/shard_map/feed_far/pallas_call | solution.py:144
  35.5 2.1 %collective-permute-start.10 = (bf16[256,384]{1,0:T(8,128)(2,1)S(1)}, bf16[256,384]{1,0:T(8,128)(2,1)S(1)}, u32[]{:S(2)}, u32[]{:S(2)}) collective-permute-start(bf16[256,384]{1,0:T(8,128)(2,1)S(1)} %get-tuple-element.145.refs_12_.refs_0_), channel_id=1, source_target_pairs={{0,2},{1,3},{2,0},{3,1},{4,6},{5,7},{6,4},{7,5},{8,10},{9,11},{10,... | collective-permute-start | bytes 589832 | tf_op jit(solution)/shard_map/ppermute | solution.py:677
  37.6 0.8 collective-permute-done.4.refs_3_
  38.5 2.6 %feed_own.1 = (f32[256,768]{1,0:T(8,128)S(1)}, bf16[256,768]{1,0:T(8,128)(2,1)}, bf16[256,384]{1,0:T(8,128)(2,1)S(1)}, bf16[256,384]{1,0:T(8,128)(2,1)S(1)}, bf1...) custom-call(bf16[256,768]{1,0:T(8,128)(2,1)S(1)} %get-tuple-element., ...), custom_call_target="tpu_custom_call" | custom-call | flops 10000000000 | bytes 100000000 | tf_op jit(solution)/shard_map/feed_own/pallas_call | solution.py:144
  41.1 2.1 %collective-permute-start.13 = (bf16[256,384]{1,0:T(8,128)(2,1)S(1)}, bf16[256,384]{1,0:T(8,128)(2,1)S(1)}, u32[]{:S(2)}, u32[]{:S(2)}) collective-permute-start(bf16[256,384]{1,0:T(8,128)(2,1)S(1)} %get-tuple-element.152.refs_0_), channel_id=1, source_target_pairs={{0,2},{1,3},{2,0},{3,1},{4,6},{5,7},{6,4},{7,5},{8,10},{9,11},{10,... | collective-permute-start | bytes 589832 | tf_op jit(solution)/shard_map/ppermute | solution.py:677
  43.2 2.5 %attention_backward.2 = (bf16[256,768]{1,0:T(8,128)(2,1)S(1)}, bf16[1152,256]{1,0:T(8,128)(2,1)S(1)}, f32[256,768]{1,0:T(8,128)S(1)}, f32[8,768]{1,0:T(8,128)S(1)}, f32[8,128]{1,0:T(8,128)S(1)}) custom-call(bf16[256,384]{1,0:T(8,128)(2,1)S(1)} %get-tuple-element.152.refs_0_, bf16[256,384]{1,0:T(8,128)(2,1)S(1)} %collective-permute-done.10.refs_1_, ...), custom_call_target="tpu_custom_call" | custom-call | flops 10000000000 | bytes 100000000 | tf_op jit(solution)/shard_map/attention_backward/pallas_call | solution.py:144
  46.3 1.6 %collective-permute-start.12 = (bf16[96,768]{1,0:T(8,128)(2,1)S(1)}, bf16[96,768]{1,0:T(8,128)(2,1)S(1)}, u32[]{:S(2)}, u32[]{:S(2)}) collective-permute-start(bf16[96,768]{1,0:T(8,128)(2,1)S(1)} %get-tuple-element.160), channel_id=1, source_target_pairs={{0,4},{1,9},{2,6},{3,11},{4,0},{5,13},{6,2},{7,15},{8,12},{9,1},{1... | collective-permute-start | bytes 442376 | tf_op jit(solution)/shard_map/ppermute | solution.py:685
  48.4 2.5 %attention_backward.3 = (bf16[256,768]{1,0:T(8,128)(2,1)S(1)}, bf16[1152,256]{1,0:T(8,128)(2,1)S(1)}, f32[8,128]{1,0:T(8,128)S(1)}) custom-call(bf16[256,384]{1,0:T(8,128)(2,1)S(1)} %get-tuple-element.145.refs_12_.refs_0_, bf16[256,384]{1,0:T(8,128)(2,1)S(1)} %collective-permute-done.13.refs_1_, ...), custom_call_target="tpu_custom_call" | custom-call | bytes 100000000 | tf_op jit(solution)/shard_map/attention_backward/pallas_call | solution.py:144
  50.9 0.8 weight_grads.2
  51.7 0.8 weight_grads.3
  53.2 1.6 %collective-permute-start.14 = (bf16[96,768]{1,0:T(8,128)(2,1)S(1)}, bf16[96,768]{1,0:T(8,128)(2,1)S(1)}, u32[]{:S(2)}, u32[]{:S(2)}) collective-permute-start(bf16[96,768]{1,0:T(8,128)(2,1)S(1)} %get-tuple-element.178), channel_id=1, source_target_pairs={{0,8},{1,5},{2,10},{3,7},{4,12},{5,1},{6,14},{7,3},{8,0},{9,13},{1... | collective-permute-start | bytes 442376 | tf_op jit(solution)/shard_map/ppermute | solution.py:685
  56.1 1.6 %collective-permute-start.17 = (bf16[192,768]{1,0:T(8,128)(2,1)S(1)}, bf16[192,768]{1,0:T(8,128)(2,1)S(1)}, u32[]{:S(2)}, u32[]{:S(2)}) collective-permute-start(bf16[192,768]{1,0:T(8,128)(2,1)S(1)} %get-tuple-element.184), channel_id=1, source_target_pairs={{0,4},{1,9},{2,6},{3,11},{4,0},{5,13},{6,2},{7,15},{8,12},{9,1},{1... | collective-permute-start | bytes 884744 | tf_op jit(solution)/shard_map/ppermute | solution.py:685
  57.6 0.8 collective-permute-done.14.refs_4_
  59.1 2.7 %collective-permute-start.16 = (bf16[96,768]{1,0:T(8,128)(2,1)S(1)}, bf16[96,768]{1,0:T(8,128)(2,1)S(1)}, u32[]{:S(2)}, u32[]{:S(2)}) collective-permute-start(bf16[96,768]{1,0:T(8,128)(2,1)S(1)} %get-tuple-element.183.refs_0_), channel_id=1, source_target_pairs={{0,16},{1,17},{2,18},{3,19},{4,20},{5,21},{6,22},{7,23},{8,24},{9,... | collective-permute-start | bytes 442376 | tf_op jit(solution)/shard_map/ppermute | solution.py:685
  61.7 1.5 %collective-permute-start.20 = (bf16[192,768]{1,0:T(8,128)(2,1)S(1)}, bf16[192,768]{1,0:T(8,128)(2,1)S(1)}, u32[]{:S(2)}, u32[]{:S(2)}) collective-permute-start(bf16[192,768]{1,0:T(8,128)(2,1)S(1)} %get-tuple-element.194), channel_id=1, source_target_pairs={{0,4},{1,9},{2,6},{3,11},{4,0},{5,13},{6,2},{7,15},{8,12},{9,1},{1... | collective-permute-start | bytes 884744 | tf_op jit(solution)/shard_map/ppermute | solution.py:685
  63.2 1.4 %input_grads.1 = (f32[256,768]{1,0:T(8,128)S(1)}, bf16[272,768]{1,0:T(8,128)(2,1)S(1)}, f32[8,128]{1,0:T(8,128)S(1)}) custom-call(bf16[1152,256]{1,0:T(8,128)(2,1)S(1)} %get-tuple-element.161.refs_0_.refs_4_.refs_8_, bf16[1152,256]{1,0:T(8,128)(2,1)S(1)} %get-tuple-element.168.refs_1_.refs_5_.refs_9_, ...), custom_call_target="tpu_custom_call" | custom-call | bytes 100000000 | tf_op jit(solution)/shard_map/input_grads/pallas_call | solution.py:144
  65.9 1.6 %collective-permute-start.21 = (bf16[192,768]{1,0:T(8,128)(2,1)S(1)}, bf16[192,768]{1,0:T(8,128)(2,1)S(1)}, u32[]{:S(2)}, u32[]{:S(2)}) collective-permute-start(bf16[192,768]{1,0:T(8,128)(2,1)S(1)} %get-tuple-element.195), channel_id=1, source_target_pairs={{0,8},{1,5},{2,10},{3,7},{4,12},{5,1},{6,14},{7,3},{8,0},{9,13},{1... | collective-permute-start | bytes 884744 | tf_op jit(solution)/shard_map/ppermute | solution.py:685
  67.5 1.1 collective-permute-done.16.refs_1_
  70.5 2.2 %collective-permute-done.21.refs_4_ = bf16[192,768]{1,0:T(8,128)(2,1)S(1)} collective-permute-done((bf16[192,768]{1,0:T(8,128)(2,1)S(1)}, bf16[192,768]{1,0:T(8,128)(2,1)S(1)}, u32[]{:S(2)}, u32[]{:S(2)}) %collective-permute-start.21) | collective-permute-done | bytes 294944 | tf_op jit(solution)/shard_map/ppermute | solution.py:685
  73.4 1.5 %collective-permute-start.26 = (bf16[192,768]{1,0:T(8,128)(2,1)S(1)}, bf16[192,768]{1,0:T(8,128)(2,1)S(1)}, u32[]{:S(2)}, u32[]{:S(2)}) collective-permute-start(bf16[192,768]{1,0:T(8,128)(2,1)S(1)} %get-tuple-element.206.refs_0_), channel_id=1, source_target_pairs={{0,16},{1,17},{2,18},{3,19},{4,20},{5,21},{6,22},{7,23},{8,24},{9,... | collective-permute-start | bytes 884744 | tf_op jit(solution)/shard_map/ppermute | solution.py:685
  74.9 1.5 %collective-permute-start.24 = (bf16[96,768]{1,0:T(8,128)(2,1)S(1)}, bf16[96,768]{1,0:T(8,128)(2,1)S(1)}, u32[]{:S(2)}, u32[]{:S(2)}) collective-permute-start(bf16[96,768]{1,0:T(8,128)(2,1)S(1)} %get-tuple-element.199.refs_1_), channel_id=1, source_target_pairs={{0,4},{1,9},{2,6},{3,11},{4,0},{5,13},{6,2},{7,15},{8,12},{9,1},{1... | collective-permute-start | bytes 442376 | tf_op jit(solution)/shard_map/ppermute | solution.py:685
  77.4 2.7 %collective-permute-done.24.refs_3_ = bf16[96,768]{1,0:T(8,128)(2,1)S(1)} collective-permute-done((bf16[96,768]{1,0:T(8,128)(2,1)S(1)}, bf16[96,768]{1,0:T(8,128)(2,1)S(1)}, u32[]{:S(2)}, u32[]{:S(2)}) %collective-permute-start.24) | collective-permute-done | bytes 147488 | tf_op jit(solution)/shard_map/ppermute | solution.py:685
  80.1 1.6 %collective-permute-done.25.refs_4_ = bf16[96,768]{1,0:T(8,128)(2,1)S(1)} collective-permute-done((bf16[96,768]{1,0:T(8,128)(2,1)S(1)}, bf16[96,768]{1,0:T(8,128)(2,1)S(1)}, u32[]{:S(2)}, u32[]{:S(2)}) %collective-permute-start.25) | collective-permute-done | bytes 147488 | tf_op jit(solution)/shard_map/ppermute | solution.py:685
  81.6 1.7 %place_sums.4 = (f32[192,768]{1,0:T(8,128)}, f32[192,768]{1,0:T(8,128)}, f32[8,128]{1,0:T(8,128)S(1)}) custom-call(s32[6]{0:T(128)S(1)} %stack.27.refs_0_, bf16[96,768]{1,0:T(8,128)(2,1)S(1)} %get-tuple-element.199.refs_1_, bf16[96,768]{1,0:T(8,128)(2,1)S(1)} %collective-permute-done.23.refs_2_, bf16[96,768]{1,0:T(8,128)(2,1)S(1)} %collective-permute-done.24.refs_3_, ...), custom_call_target="tpu_custom_call" | custom-call | bytes 100000000 | tf_op jit(solution)/shard_map/place_sums/pallas_call | solution.py:144
  83.4 1.5 %collective-permute-start.27 = (bf16[16,768]{1,0:T(8,128)(2,1)S(1)}, bf16[16,768]{1,0:T(8,128)(2,1)S(1)}, u32[]{:S(2)}, u32[]{:S(2)}) collective-permute-start(bf16[16,768]{1,0:T(8,128)(2,1)S(1)} %get-tuple-element.207.refs_2_), channel_id=1, source_target_pairs={{0,16},{1,17},{2,18},{3,19},{4,20},{5,21},{6,22},{7,23},{8,24},{9,... | collective-permute-start | bytes 73736 | tf_op jit(solution)/shard_map/ppermute | solution.py:685
  85.0 0.8 add_result.1
  85.8 3.1 %collective-permute-done.27.refs_3_ = bf16[16,768]{1,0:T(8,128)(2,1)S(1)} collective-permute-done((bf16[16,768]{1,0:T(8,128)(2,1)S(1)}, bf16[16,768]{1,0:T(8,128)(2,1)S(1)}, u32[]{:S(2)}, u32[]{:S(2)}) %collective-permute-start.27) | collective-permute-done | bytes 24608 | tf_op jit(solution)/shard_map/ppermute | solution.py:685
  89.0 1.0 collective-permute-start.28
  90.0 1.3 %input_norm.1 = (bf16[256,768]{1,0:T(8,128)(2,1)}, f32[8,128]{1,0:T(8,128)S(1)}) custom-call(bf16[256,768]{1,0:T(8,128)(2,1)S(1)} %get-tuple-element.122.refs_3_.refs_0_, f32[768]{0:T(1024)S(1)} %get-tuple-element.123.refs_4_.refs_1_, f32[256,768]{1,0:T(8,128)S(1)} %get-tuple-element.204.refs_2_, ...), custom_call_target="tpu_custom_call" | custom-call | bytes 100000000 | tf_op jit(solution)/shard_map/input_norm/pallas_call | solution.py:144
  91.4 4.7 %collective-permute-done.28.refs_1_ = bf16[208,768]{1,0:T(8,128)(2,1)S(1)} collective-permute-done((bf16[208,768]{1,0:T(8,128)(2,1)S(1)}, bf16[208,768]{1,0:T(8,128)(2,1)S(1)}, u32[]{:S(2)}, u32[]{:S(2)}) %collective-permute-start.28) | collective-permute-done | bytes 319520 | tf_op jit(solution)/shard_map/ppermute | solution.py:685
  96.1 1.6 %collective-permute-start.29 = (bf16[208,768]{1,0:T(8,128)(2,1)S(1)}, bf16[208,768]{1,0:T(8,128)(2,1)S(1)}, u32[]{:S(2)}, u32[]{:S(2)}) collective-permute-start(bf16[208,768]{1,0:T(8,128)(2,1)S(1)} %get-tuple-element.213.refs_1_), channel_id=1, source_target_pairs={{0,4},{1,9},{2,6},{3,11},{4,0},{5,13},{6,2},{7,15},{8,12},{9,1},{1... | collective-permute-start | bytes 958472 | tf_op jit(solution)/shard_map/ppermute | solution.py:685
  98.2 1.6 %place_sums.5 = (f32[3,192,768]{2,1,0:T(8,128)}, f32[192,768]{1,0:T(8,128)}, f32[8,128]{1,0:T(8,128)S(1)}) custom-call(s32[6]{0:T(128)S(1)} %stack.27.refs_0_, bf16[208,768]{1,0:T(8,128)(2,1)S(1)} %get-tuple-element.213.refs_1_, bf16[208,768]{1,0:T(8,128)(2,1)S(1)} %get-tuple-element.214.refs_2_, f32[8,128]{1,0:T(8,128)S(1)} %get-tuple-element.215.refs_3_), custom_call_target="tpu_custom_call" | custom-call | bytes 100000000 | tf_op jit(solution)/shard_map/place_sums/pallas_call | solution.py:144
  99.8 3.3 %collective-permute-done.29.refs_3_ = bf16[208,768]{1,0:T(8,128)(2,1)S(1)} collective-permute-done((bf16[208,768]{1,0:T(8,128)(2,1)S(1)}, bf16[208,768]{1,0:T(8,128)(2,1)S(1)}, u32[]{:S(2)}, u32[]{:S(2)}) %collective-permute-start.29) | collective-permute-done | bytes 319520 | tf_op jit(solution)/shard_map/ppermute | solution.py:685
  103.1 1.4 %place_sums.6 = (f32[3,192,768]{2,1,0:T(8,128)}, f32[192,768]{1,0:T(8,128)}, f32[8,128]{1,0:T(8,128)S(1)}) custom-call(s32[6]{0:T(128)S(1)} %stack.27.refs_0_, bf16[208,768]{1,0:T(8,128)(2,1)S(1)} %get-tuple-element.213.refs_1_, bf16[208,768]{1,0:T(8,128)(2,1)S(1)} %get-tuple-element.214.refs_2_, ...), custom_call_target="tpu_custom_call", output_to_operand_aliasing={{0}: (4, {}), {1}: (5, {})} | custom-call | bytes 100000000 | tf_op jit(solution)/shard_map/place_sums/pallas_call | solution.py:144
  104.6 2.0 %collective-permute-done.30.refs_4_ = bf16[208,768]{1,0:T(8,128)(2,1)S(1)} collective-permute-done((bf16[208,768]{1,0:T(8,128)(2,1)S(1)}, bf16[208,768]{1,0:T(8,128)(2,1)S(1)}, u32[]{:S(2)}, u32[]{:S(2)}) %collective-permute-start.30) | collective-permute-done | bytes 319520 | tf_op jit(solution)/shard_map/ppermute | solution.py:685
  106.6 2.0 %place_sums.7 = (f32[3,192,768]{2,1,0:T(8,128)}, f32[192,768]{1,0:T(8,128)}, f32[768]{0:T(1024)}, f32[768]{0:T(1024)}, f32[768]{0:T(1024)}, /*index=5*/f32[768]{0:T(1024)}, f32[192]{0:T(256)}, f32[8,128]{1,0:T(8,128)}) custom-call(s32[6]{0:T(128)S(1)} %stack.27.refs_0_, ...), custom_call_target="tpu_custom_call", output_to_operand_aliasing={{0}: (5, {}), {1}: (6, {})} | custom-call | bytes 100000000 | tf_op jit(solution)/shard_map/place_sums/pallas_call | solution.py:144
  (54 shorter events, 10.6 us)
Async XLA Ops:
  0.8 4.6 %copy-start.1 = (bf16[256,768]{1,0:T(8,128)(2,1)S(1)}, bf16[256,768]{1,0:T(8,128)(2,1)}, u32[]{:S(2)}) copy-start(bf16[256,768]{1,0:T(8,128)(2,1)} %refs_4_.1) | copy-start | bytes 1179652
  0.8 4.7 %copy-start = (bf16[3,192,768]{2,1,0:T(8,128)(2,1)S(1)}, bf16[3,192,768]{2,1,0:T(8,128)(2,1)}, u32[]{:S(2)}) copy-start(bf16[3,192,768]{2,1,0:T(8,128)(2,1)} %refs_6_.3) | copy-start | bytes 2654212
  0.8 4.7 %copy-start.2 = (bf16[192]{0:T(256)(128)(2,1)S(1)}, bf16[192]{0:T(256)(128)(2,1)}, u32[]{:S(2)}) copy-start(bf16[192]{0:T(256)(128)(2,1)} %param.23) | copy-start | bytes 1156
  2.3 10.9 %collective-permute-start.3 = (bf16[192,768]{1,0:T(8,128)(2,1)S(1)}, bf16[192,768]{1,0:T(8,128)(2,1)S(1)}, u32[]{:S(2)}, u32[]{:S(2)}) collective-permute-start(bf16[192,768]{1,0:T(8,128)(2,1)S(1)} %get-tuple-element.130), channel_id=1, source_target_pairs={{0,2},{1,3},{2,0},{3,1},{4,6},{5,7},{6,4},{7,5},{8,10},{9,11},{10,... | collective-permute-start | bytes 884744 | tf_op jit(solution)/shard_map/ppermute | solution.py:677
  5.3 16.3 %collective-permute-start.1 = (bf16[256,768]{1,0:T(8,128)(2,1)S(1)}, bf16[256,768]{1,0:T(8,128)(2,1)S(1)}, u32[]{:S(2)}, u32[]{:S(2)}) collective-permute-start(bf16[256,768]{1,0:T(8,128)(2,1)S(1)} %copy-done.1), channel_id=1, source_target_pairs={{0,2},{1,3},{2,0},{3,1},{4,6},{5,7},{6,4},{7,5},{8,10},{9,11},{10,... | collective-permute-start | bytes 1179656 | tf_op jit(solution)/shard_map/ppermute | solution.py:677
  5.4 2.4 %collective-permute-start = (bf16[3,192,768]{2,1,0:T(8,128)(2,1)S(1)}, bf16[3,192,768]{2,1,0:T(8,128)(2,1)S(1)}, u32[]{:S(2)}, u32[]{:S(2)}) collective-permute-start(bf16[3,192,768]{2,1,0:T(8,128)(2,1)S(1)} %copy-done), channel_id=1, source_target_pairs={{0,1},{1,0},{2,3},{3,2},{4,5},{5,4},{6,7},{7,6},{8,9},{9,8},{10,11... | collective-permute-start | bytes 2654216 | tf_op jit(solution)/shard_map/ppermute | solution.py:674
  7.0 14.6 %collective-permute-start.2 = (bf16[592,768]{1,0:T(8,128)(2,1)S(1)}, bf16[592,768]{1,0:T(8,128)(2,1)S(1)}, u32[]{:S(2)}, u32[]{:S(2)}) collective-permute-start(bf16[592,768]{1,0:T(8,128)(2,1)S(1)} %get-tuple-element.129.refs_7_.refs_8_.refs_9_), channel_id=1, source_target_pairs={{0,1},{1,0},{2,3},{3,2},{4,5},{5,4},{6,7},{7,6},{8,9},{9,8},{10,11... | collective-permute-start | bytes 2727944 | tf_op jit(solution)/shard_map/ppermute | solution.py:674
  13.3 8.0 %collective-permute-start.5 = (bf16[192,768]{1,0:T(8,128)(2,1)S(1)}, bf16[192,768]{1,0:T(8,128)(2,1)S(1)}, u32[]{:S(2)}, u32[]{:S(2)}) collective-permute-start(bf16[192,768]{1,0:T(8,128)(2,1)S(1)} %get-tuple-element.138.refs_3_), channel_id=1, source_target_pairs={{0,4},{1,5},{2,6},{3,7},{4,0},{5,1},{6,2},{7,3},{8,12},{9,13},{10,... | collective-permute-start | bytes 884744 | tf_op jit(solution)/shard_map/ppermute | solution.py:685
  15.4 11.9 %collective-permute-start.6 = (bf16[192,768]{1,0:T(8,128)(2,1)S(1)}, bf16[192,768]{1,0:T(8,128)(2,1)S(1)}, u32[]{:S(2)}, u32[]{:S(2)}) collective-permute-start(bf16[192,768]{1,0:T(8,128)(2,1)S(1)} %get-tuple-element.138.refs_3_), channel_id=1, source_target_pairs={{0,1},{1,0},{2,3},{3,2},{4,5},{5,4},{6,7},{7,6},{8,9},{9,8},{10,11... | collective-permute-start | bytes 884744 | tf_op jit(solution)/shard_map/ppermute | solution.py:674
  15.4 18.9 %collective-permute-start.8 = (bf16[256,1152]{1,0:T(8,128)(2,1)S(1)}, bf16[256,1152]{1,0:T(8,128)(2,1)S(1)}, u32[]{:S(2)}, u32[]{:S(2)}) collective-permute-start(bf16[256,1152]{1,0:T(8,128)(2,1)S(1)} %get-tuple-element.127.refs_1_), channel_id=1, source_target_pairs={{0,2},{1,3},{2,0},{3,1},{4,6},{5,7},{6,4},{7,5},{8,10},{9,11},{10,... | collective-permute-start | bytes 1769480 | tf_op jit(solution)/shard_map/ppermute | solution.py:677
  21.3 6.0 %collective-permute-start.7 = (bf16[192,768]{1,0:T(8,128)(2,1)S(1)}, bf16[192,768]{1,0:T(8,128)(2,1)S(1)}, u32[]{:S(2)}, u32[]{:S(2)}) collective-permute-start(bf16[192,768]{1,0:T(8,128)(2,1)S(1)} %collective-permute-done.5.refs_4_), channel_id=1, source_target_pairs={{0,1},{1,0},{2,3},{3,2},{4,5},{5,4},{6,7},{7,6},{8,9},{9,8},{10,11... | collective-permute-start | bytes 884744 | tf_op jit(solution)/shard_map/ppermute | solution.py:674
  25.1 13.3 %collective-permute-start.4 = (bf16[256,384]{1,0:T(8,128)(2,1)S(1)}, bf16[256,384]{1,0:T(8,128)(2,1)S(1)}, u32[]{:S(2)}, u32[]{:S(2)}) collective-permute-start(bf16[256,384]{1,0:T(8,128)(2,1)S(1)} %get-tuple-element.133.refs_1_), channel_id=1, source_target_pairs={{0,2},{1,3},{2,0},{3,1},{4,6},{5,7},{6,4},{7,5},{8,10},{9,11},{10,... | collective-permute-start | bytes 589832 | tf_op jit(solution)/shard_map/ppermute | solution.py:677
  35.5 7.7 %collective-permute-start.10 = (bf16[256,384]{1,0:T(8,128)(2,1)S(1)}, bf16[256,384]{1,0:T(8,128)(2,1)S(1)}, u32[]{:S(2)}, u32[]{:S(2)}) collective-permute-start(bf16[256,384]{1,0:T(8,128)(2,1)S(1)} %get-tuple-element.145.refs_12_.refs_0_), channel_id=1, source_target_pairs={{0,2},{1,3},{2,0},{3,1},{4,6},{5,7},{6,4},{7,5},{8,10},{9,11},{10,... | collective-permute-start | bytes 589832 | tf_op jit(solution)/shard_map/ppermute | solution.py:677
  41.1 7.3 %collective-permute-start.13 = (bf16[256,384]{1,0:T(8,128)(2,1)S(1)}, bf16[256,384]{1,0:T(8,128)(2,1)S(1)}, u32[]{:S(2)}, u32[]{:S(2)}) collective-permute-start(bf16[256,384]{1,0:T(8,128)(2,1)S(1)} %get-tuple-element.152.refs_0_), channel_id=1, source_target_pairs={{0,2},{1,3},{2,0},{3,1},{4,6},{5,7},{6,4},{7,5},{8,10},{9,11},{10,... | collective-permute-start | bytes 589832 | tf_op jit(solution)/shard_map/ppermute | solution.py:677
  43.2 2.5 %collective-permute-start.9 = (bf16[2,192,768]{2,1,0:T(8,128)(2,1)S(1)}, bf16[2,192,768]{2,1,0:T(8,128)(2,1)S(1)}, u32[]{:S(2)}, u32[]{:S(2)}) collective-permute-start(bf16[2,192,768]{2,1,0:T(8,128)(2,1)S(1)} %get-tuple-element.151), channel_id=1, source_target_pairs={{0,1},{1,0},{2,3},{3,2},{4,5},{5,4},{6,7},{7,6},{8,9},{9,8},{10,11... | collective-permute-start | bytes 1769480 | tf_op jit(solution)/shard_map/ppermute | solution.py:674
  46.3 6.3 %collective-permute-start.12 = (bf16[96,768]{1,0:T(8,128)(2,1)S(1)}, bf16[96,768]{1,0:T(8,128)(2,1)S(1)}, u32[]{:S(2)}, u32[]{:S(2)}) collective-permute-start(bf16[96,768]{1,0:T(8,128)(2,1)S(1)} %get-tuple-element.160), channel_id=1, source_target_pairs={{0,4},{1,9},{2,6},{3,11},{4,0},{5,13},{6,2},{7,15},{8,12},{9,1},{1... | collective-permute-start | bytes 442376 | tf_op jit(solution)/shard_map/ppermute | solution.py:685
  47.9 9.8 %collective-permute-start.11 = (bf16[96,768]{1,0:T(8,128)(2,1)S(1)}, bf16[96,768]{1,0:T(8,128)(2,1)S(1)}, u32[]{:S(2)}, u32[]{:S(2)}) collective-permute-start(bf16[96,768]{1,0:T(8,128)(2,1)S(1)} %get-tuple-element.159), channel_id=1, source_target_pairs={{0,4},{1,9},{2,6},{3,11},{4,0},{5,13},{6,2},{7,15},{8,12},{9,1},{1... | collective-permute-start | bytes 442376 | tf_op jit(solution)/shard_map/ppermute | solution.py:685
  52.5 2.9 %collective-permute-start.15 = (bf16[4,192,768]{2,1,0:T(8,128)(2,1)S(1)}, bf16[4,192,768]{2,1,0:T(8,128)(2,1)S(1)}, u32[]{:S(2)}, u32[]{:S(2)}) collective-permute-start(bf16[4,192,768]{2,1,0:T(8,128)(2,1)S(1)} %get-tuple-element.180), channel_id=1, source_target_pairs={{0,1},{1,0},{2,3},{3,2},{4,5},{5,4},{6,7},{7,6},{8,9},{9,8},{10,11... | collective-permute-start | bytes 3538952 | tf_op jit(solution)/shard_map/ppermute | solution.py:674
  53.2 5.2 %collective-permute-start.14 = (bf16[96,768]{1,0:T(8,128)(2,1)S(1)}, bf16[96,768]{1,0:T(8,128)(2,1)S(1)}, u32[]{:S(2)}, u32[]{:S(2)}) collective-permute-start(bf16[96,768]{1,0:T(8,128)(2,1)S(1)} %get-tuple-element.178), channel_id=1, source_target_pairs={{0,8},{1,5},{2,10},{3,7},{4,12},{5,1},{6,14},{7,3},{8,0},{9,13},{1... | collective-permute-start | bytes 442376 | tf_op jit(solution)/shard_map/ppermute | solution.py:685
  56.1 9.1 %collective-permute-start.17 = (bf16[192,768]{1,0:T(8,128)(2,1)S(1)}, bf16[192,768]{1,0:T(8,128)(2,1)S(1)}, u32[]{:S(2)}, u32[]{:S(2)}) collective-permute-start(bf16[192,768]{1,0:T(8,128)(2,1)S(1)} %get-tuple-element.184), channel_id=1, source_target_pairs={{0,4},{1,9},{2,6},{3,11},{4,0},{5,13},{6,2},{7,15},{8,12},{9,1},{1... | collective-permute-start | bytes 884744 | tf_op jit(solution)/shard_map/ppermute | solution.py:685
  59.1 9.5 %collective-permute-start.16 = (bf16[96,768]{1,0:T(8,128)(2,1)S(1)}, bf16[96,768]{1,0:T(8,128)(2,1)S(1)}, u32[]{:S(2)}, u32[]{:S(2)}) collective-permute-start(bf16[96,768]{1,0:T(8,128)(2,1)S(1)} %get-tuple-element.183.refs_0_), channel_id=1, source_target_pairs={{0,16},{1,17},{2,18},{3,19},{4,20},{5,21},{6,22},{7,23},{8,24},{9,... | collective-permute-start | bytes 442376 | tf_op jit(solution)/shard_map/ppermute | solution.py:685
  61.7 8.7 %collective-permute-start.20 = (bf16[192,768]{1,0:T(8,128)(2,1)S(1)}, bf16[192,768]{1,0:T(8,128)(2,1)S(1)}, u32[]{:S(2)}, u32[]{:S(2)}) collective-permute-start(bf16[192,768]{1,0:T(8,128)(2,1)S(1)} %get-tuple-element.194), channel_id=1, source_target_pairs={{0,4},{1,9},{2,6},{3,11},{4,0},{5,13},{6,2},{7,15},{8,12},{9,1},{1... | collective-permute-start | bytes 884744 | tf_op jit(solution)/shard_map/ppermute | solution.py:685
  64.7 12.6 %collective-permute-start.19 = (bf16[272,768]{1,0:T(8,128)(2,1)S(1)}, bf16[272,768]{1,0:T(8,128)(2,1)S(1)}, u32[]{:S(2)}, u32[]{:S(2)}) collective-permute-start(bf16[272,768]{1,0:T(8,128)(2,1)S(1)} %get-tuple-element.193.refs_0_), channel_id=1, source_target_pairs={{0,2},{1,3},{2,0},{3,1},{4,6},{5,7},{6,4},{7,5},{8,10},{9,11},{10,... | collective-permute-start | bytes 1253384 | tf_op jit(solution)/shard_map/ppermute | solution.py:677
  65.9 6.8 %collective-permute-start.21 = (bf16[192,768]{1,0:T(8,128)(2,1)S(1)}, bf16[192,768]{1,0:T(8,128)(2,1)S(1)}, u32[]{:S(2)}, u32[]{:S(2)}) collective-permute-start(bf16[192,768]{1,0:T(8,128)(2,1)S(1)} %get-tuple-element.195), channel_id=1, source_target_pairs={{0,8},{1,5},{2,10},{3,7},{4,12},{5,1},{6,14},{7,3},{8,0},{9,13},{1... | collective-permute-start | bytes 884744 | tf_op jit(solution)/shard_map/ppermute | solution.py:685
  69.2 15.7 %collective-permute-start.18 = (bf16[256,768]{1,0:T(8,128)(2,1)S(1)}, bf16[256,768]{1,0:T(8,128)(2,1)S(1)}, u32[]{:S(2)}, u32[]{:S(2)}) collective-permute-start(bf16[256,768]{1,0:T(8,128)(2,1)S(1)} %get-tuple-element.192), channel_id=1, source_target_pairs={{0,2},{1,3},{2,0},{3,1},{4,6},{5,7},{6,4},{7,5},{8,10},{9,11},{10,... | collective-permute-start | bytes 1179656 | tf_op jit(solution)/shard_map/ppermute | solution.py:677
  69.8 6.7 %collective-permute-start.23 = (bf16[96,768]{1,0:T(8,128)(2,1)S(1)}, bf16[96,768]{1,0:T(8,128)(2,1)S(1)}, u32[]{:S(2)}, u32[]{:S(2)}) collective-permute-start(bf16[96,768]{1,0:T(8,128)(2,1)S(1)} %get-tuple-element.199.refs_1_), channel_id=1, source_target_pairs={{0,8},{1,5},{2,10},{3,7},{4,12},{5,1},{6,14},{7,3},{8,0},{9,13},{1... | collective-permute-start | bytes 442376 | tf_op jit(solution)/shard_map/ppermute | solution.py:685
  73.4 15.5 %collective-permute-start.26 = (bf16[192,768]{1,0:T(8,128)(2,1)S(1)}, bf16[192,768]{1,0:T(8,128)(2,1)S(1)}, u32[]{:S(2)}, u32[]{:S(2)}) collective-permute-start(bf16[192,768]{1,0:T(8,128)(2,1)S(1)} %get-tuple-element.206.refs_0_), channel_id=1, source_target_pairs={{0,16},{1,17},{2,18},{3,19},{4,20},{5,21},{6,22},{7,23},{8,24},{9,... | collective-permute-start | bytes 884744 | tf_op jit(solution)/shard_map/ppermute | solution.py:685
  74.9 5.1 %collective-permute-start.24 = (bf16[96,768]{1,0:T(8,128)(2,1)S(1)}, bf16[96,768]{1,0:T(8,128)(2,1)S(1)}, u32[]{:S(2)}, u32[]{:S(2)}) collective-permute-start(bf16[96,768]{1,0:T(8,128)(2,1)S(1)} %get-tuple-element.199.refs_1_), channel_id=1, source_target_pairs={{0,4},{1,9},{2,6},{3,11},{4,0},{5,13},{6,2},{7,15},{8,12},{9,1},{1... | collective-permute-start | bytes 442376 | tf_op jit(solution)/shard_map/ppermute | solution.py:685
  76.4 5.2 %collective-permute-start.25 = (bf16[96,768]{1,0:T(8,128)(2,1)S(1)}, bf16[96,768]{1,0:T(8,128)(2,1)S(1)}, u32[]{:S(2)}, u32[]{:S(2)}) collective-permute-start(bf16[96,768]{1,0:T(8,128)(2,1)S(1)} %collective-permute-done.23.refs_2_), channel_id=1, source_target_pairs={{0,4},{1,9},{2,6},{3,11},{4,0},{5,13},{6,2},{7,15},{8,12},{9,1},{1... | collective-permute-start | bytes 442376 | tf_op jit(solution)/shard_map/ppermute | solution.py:685
  77.3 6.0 %collective-permute-start.22 = (bf16[16,768]{1,0:T(8,128)(2,1)S(1)}, bf16[16,768]{1,0:T(8,128)(2,1)S(1)}, u32[]{:S(2)}, u32[]{:S(2)}) collective-permute-start(bf16[16,768]{1,0:T(8,128)(2,1)S(1)} %get-tuple-element.198.refs_0_), channel_id=1, source_target_pairs={{0,1},{1,0},{2,3},{3,2},{4,5},{5,4},{6,7},{7,6},{8,9},{9,8},{10,11... | collective-permute-start | bytes 73736 | tf_op jit(solution)/shard_map/ppermute | solution.py:674
  83.4 5.5 %collective-permute-start.27 = (bf16[16,768]{1,0:T(8,128)(2,1)S(1)}, bf16[16,768]{1,0:T(8,128)(2,1)S(1)}, u32[]{:S(2)}, u32[]{:S(2)}) collective-permute-start(bf16[16,768]{1,0:T(8,128)(2,1)S(1)} %get-tuple-element.207.refs_2_), channel_id=1, source_target_pairs={{0,16},{1,17},{2,18},{3,19},{4,20},{5,21},{6,22},{7,23},{8,24},{9,... | collective-permute-start | bytes 73736 | tf_op jit(solution)/shard_map/ppermute | solution.py:685
  89.0 7.1 %collective-permute-start.28 = (bf16[208,768]{1,0:T(8,128)(2,1)S(1)}, bf16[208,768]{1,0:T(8,128)(2,1)S(1)}, u32[]{:S(2)}, u32[]{:S(2)}) collective-permute-start(bf16[208,768]{1,0:T(8,128)(2,1)S(1)} %get-tuple-element.211.refs_0_), channel_id=1, source_target_pairs={{0,8},{1,5},{2,10},{3,7},{4,12},{5,1},{6,14},{7,3},{8,0},{9,13},{1... | collective-permute-start | bytes 958472 | tf_op jit(solution)/shard_map/ppermute | solution.py:685
  96.1 7.1 %collective-permute-start.29 = (bf16[208,768]{1,0:T(8,128)(2,1)S(1)}, bf16[208,768]{1,0:T(8,128)(2,1)S(1)}, u32[]{:S(2)}, u32[]{:S(2)}) collective-permute-start(bf16[208,768]{1,0:T(8,128)(2,1)S(1)} %get-tuple-element.213.refs_1_), channel_id=1, source_target_pairs={{0,4},{1,9},{2,6},{3,11},{4,0},{5,13},{6,2},{7,15},{8,12},{9,1},{1... | collective-permute-start | bytes 958472 | tf_op jit(solution)/shard_map/ppermute | solution.py:685
  97.7 8.9 %collective-permute-start.30 = (bf16[208,768]{1,0:T(8,128)(2,1)S(1)}, bf16[208,768]{1,0:T(8,128)(2,1)S(1)}, u32[]{:S(2)}, u32[]{:S(2)}) collective-permute-start(bf16[208,768]{1,0:T(8,128)(2,1)S(1)} %get-tuple-element.214.refs_2_), channel_id=1, source_target_pairs={{0,4},{1,9},{2,6},{3,11},{4,0},{5,13},{6,2},{7,15},{8,12},{9,1},{1... | collective-permute-start | bytes 958472 | tf_op jit(solution)/shard_map/ppermute | solution.py:685

commit v7 on v6

--- a/solution.py
+++ b/solution.py
@@ -71,7 +71,7 @@
     return jnp.concatenate([both[:HEAD_DIM, :LEN], both[HEAD_DIM:, LEN:]], axis=0)
 
 
-COSTS = (100, 100, 100, 100, 100, 100, 100, 100, 100, 0, 0, 0, 0, 150, 0, 60, 0, 0, 30, 0, 0, 0, 0, 0, 0, 0, 0, 0, 0, 0, 0)
+COSTS = (0, 0, 100, 0, 0, 0, 0, 0, 0, 100, 0, 0, 0, 0, 150, 0, 60, 0, 0, 30, 0, 0, 0, 0, 0, 0, 0, 0, 0, 0, 0, 0)
 
 
 class IO:
@@ -241,7 +241,7 @@
     args = (bits, nodes, edges, x, gain, bias)
     if g is None:
         return chain.call(
-            kernel, "attention_forward", (*args, w, *near), [*outs, bf16(rows, width)] + [bf16(width, d)] * 3,
+            kernel, "attention_forward", (*args, w, *near), [*outs, bf16(rows, width), bf16(2 * width, d), bf16(2 * width, d), bf16(width, d)],
             "sccvvvvvv-vvvvvvvvvv", scratch=[pltpu.SemaphoreType.DMA((6,))],
         )
     return chain.call(
@@ -251,23 +251,33 @@
 
 
 def pick(chain, bits, a, b):
+    half = a.shape[0] // 2
+
     def kernel(io, bits_ref, a_ref, b_ref, out_ref, sems):
-        pl.when(bits_ref[2] == 0)(lambda: finish(copies(sems, [(a_ref, out_ref)])))
-        pl.when(bits_ref[2] != 0)(lambda: finish(copies(sems, [(b_ref, out_ref)])))
-
-    return chain.call(
-        kernel, "pick", (bits, a, b), [bf16(*a.shape)], "spp-v", limit=4,
+        which = 2 * bits_ref[2] + bits_ref[6]
+        for at, ref in enumerate((a_ref.at[:half], a_ref.at[half:], b_ref.at[:half], b_ref.at[half:])):
+            pl.when(which == at)(lambda ref=ref: finish(copies(sems, [(ref, out_ref)])))
+
+    return chain.call(
+        kernel, "pick", (bits, a, b), [bf16(half, a.shape[1])], "spp-v", limit=4,
         scratch=[pltpu.SemaphoreType.DMA((1,))],
     )[0]
 
 
 def hold(chain, a):
-    def kernel(io, a_ref, out_ref, sems):
-        finish(copies(sems, [(a_ref, out_ref)]))
-
-    return chain.call(
-        kernel, "hold", (a,), [bf16(*a.shape)], "v-v", limit=4, scratch=[pltpu.SemaphoreType.DMA((1,))]
-    )[0]
+    def kernel(io, a_ref, out_ref):
+        out_ref[...] = a_ref[...]
+
+    return chain.call(kernel, "hold", (a,), [bf16(*a.shape)], "v-v", limit=4)[0]
+
+
+def pair_up(chain, a, b):
+    def kernel(io, a_ref, b_ref, out_ref, both_ref):
+        out_ref[...] = b_ref[...]
+        both_ref[0] = a_ref[...]
+        both_ref[1] = b_ref[...]
+
+    return chain.call(kernel, "pair_up", (a, b), [bf16(*b.shape), bf16(2, *a.shape)], "vv-vv", limit=4)
 
 
 def load(chain, out_weight, fc1_weight, fc2_weight, bias, others):
@@ -308,26 +318,25 @@
 
 
 def pack_far(chain, bits, wo, fc1, fars):
-    shard, d = fars[0].shape
+    half, d = fars[0].shape
+    shard = 2 * half
     width = 2 * shard
 
-    def kernel(io, bits_ref, wo_near, fc1_near, y0, x0, y1, x1, wo_ref, fc1_ref, sems):
-        near = copies(sems.at[4:], [(wo_near, wo_ref.at[:width]), (fc1_near, fc1_ref.at[:width])])
-
-        def both(first, second):
-            pairs = []
-            for at in range(2):
-                here = slice(width + at * shard, width + (at + 1) * shard)
-                pairs += [(first[at], wo_ref.at[here]), (second[at], fc1_ref.at[here])]
-            finish(copies(sems, pairs))
-
-        pl.when(bits_ref[2] == 0)(lambda: both((y0, y1), (x0, x1)))
-        pl.when(bits_ref[2] != 0)(lambda: both((x0, x1), (y0, y1)))
-        finish(near)
-
-    return chain.call(
-        kernel, "pack_far", (bits, wo, fc1, *fars), [bf16(2 * width, d), bf16(2 * width, d)], "svvvvvv-vv", limit=4,
-        scratch=[pltpu.SemaphoreType.DMA((6,))],
+    def kernel(io, bits_ref, wo_in, fc1_in, y0, pair0, xz0, y1, pair1, xz1, wo_ref, fc1_ref):
+        def placed_at(which):
+            for at, (y, pair, xz) in enumerate(((y0, pair0, xz0), (y1, pair1, xz1))):
+                for turn, part in enumerate((y[...], pair[1], pair[0], xz[...])):
+                    quarter = which ^ turn
+                    row = width + at * shard + quarter % 2 * half
+                    (wo_ref, fc1_ref)[quarter // 2][row : row + half] = part
+
+        which = 2 * bits_ref[2] + bits_ref[6]
+        for at in range(4):
+            pl.when(which == at)(functools.partial(placed_at, at))
+
+    return chain.call(
+        kernel, "pack_far", (bits, wo, fc1, *fars), [bf16(2 * width, d), bf16(2 * width, d)], "svvvvvvvv-vv", limit=4,
+        aliases={1: 0, 2: 1},
     )
 
 
@@ -666,7 +675,7 @@
     bit1 = (dp_at // 2) % 2
     bits = jnp.stack(
         [jnp.where(core == 0, bit0, bit1), jnp.where(core == 0, bit1, bit0), bit0, tensor_at * mols,
-         (tensor_at ^ 2) * mols, core]
+         (tensor_at ^ 2) * mols, core, bit1]
     ).astype(jnp.int32)
     chain = Chain()
 
@@ -706,12 +715,15 @@
     )
     packet_got = swap_y(packet)
     far_y = hold(chain, far_y)
-    far_x = swap_dp(far_y, 1, 1)
+    far_x, far_z = swap_dp(far_y, 1, 1), swap_dp(far_y, 2, 2)
     a1_1, qt_1, kt_1, v_1, p_1, ot_1, o_1, wo, fc1, fc2 = attention(
         chain, bits, 4, *counts, x_got, *norm1, w_qkv, near=near
     )
     o_got = swap_y(o_1)
-    fars = (far_y, far_x, swap_core(far_y), swap_core(far_x))
+    far_z, pair = pair_up(chain, far_x, far_z)
+    far_xz = swap_dp(far_z, 1, 1)
+    fars = (far_y, pair, far_xz)
+    fars += tuple(swap_core(a) for a in fars)
     norm2 = (ln2_gain, ln2_bias)
     wo, fc1 = pack_far(chain, bits, wo, fc1, fars)
     h_1, a2_1, z_1, du_1 = feed_far(chain, x_got, o_1, packet_got, *norm2, fc1, fc2, wo, near)
@@ -785,9 +797,9 @@
     r.second()
     q.first()
     r.third()
+    q.second()
     da1_mine, da1_theirs = input_grads(chain, (dp_0, dp_1), w_qkv, (tokens, x_got), sums, bias_sums)
     da1_got = swap_y(da1_theirs)
-    q.second()
     r.fourth()
     res_mine, res_theirs = feed_result(chain, (z_0, z_1), fc2, h_0)
     res_got = swap_y(res_theirs)

time: 109 us -> 105 us (0.963)
  waiting for transfers between devices: 35.2 us -> 26.4 us
  starting transfers between devices: 34.9 us -> 40.1 us
    ppermute x16 -> x18, waiting for transfers between devices: 25.8 us -> 19.4 us  [swap_dp(): return lax.ppermute(a, ('dp', 'tensor'), pairs)]
    ppermute x16 -> x18, starting transfers between devices: 22.1 us -> 26.1 us  [swap_dp(): return lax.ppermute(a, ('dp', 'tensor'), pairs)]
    ppermute x8, waiting for transfers between devices: 8.48 us -> 6.44 us  [swap_y(): return lax.ppermute(a, 'tensor', [(t, t ^ 2) for t in range(n_tensor)])]
    pallas_call x31 -> x32, Pallas kernels: 37.4 us -> 36.8 us  [call(): pl.pallas_call(body, in_specs=[spec(kind) for kind in ins] + [vmem] * len...]
  transfers between devices with their start and end apart: 31 -> 34, of which waited for: 17 -> 16; matrix products, arithmetic and copies ran while one was open for 0% -> 1% of each run, Pallas kernels for 31% -> 33%
where the time goes in v7:
time: 105 us
  starting transfers between devices  40.1 us (38%)
  Pallas kernels  36.8 us (35%)
  waiting for transfers between devices  26.4 us (25%)
  between operations  1.14 us (1%)
    pallas_call x32, Pallas kernels, call(): pl.pallas_call(body, in_specs=[spec(kind) for kind in ins] + [vmem] * len...  36.8 us
    ppermute x18, starting transfers between devices, swap_dp(): return lax.ppermute(a, ('dp', 'tensor'), pairs)  26.1 us
    ppermute x18, waiting for transfers between devices, swap_dp(): return lax.ppermute(a, ('dp', 'tensor'), pairs)  19.4 us
    ppermute x8, starting transfers between devices, swap_y(): return lax.ppermute(a, 'tensor', [(t, t ^ 2) for t in range(n_tensor)])  12.7 us
    ppermute x8, waiting for transfers between devices, swap_y(): return lax.ppermute(a, 'tensor', [(t, t ^ 2) for t in range(n_tensor)])  6.44 us
  transfers between devices with their start and end apart: 34, of which 16 were waited for; matrix products, arithmetic and copies ran while one was open for 1% of the time, Pallas kernels for 33%

profile of v7, /device:TPU:0, one launch (start us, length us, event | category | flops | bytes accessed | tf_op | source)
XLA Modules:
  0.0 105.3 jit_solution(13235917440908328623)
XLA Ops:
  1.2 1.5 %pick.1 = (bf16[96,768]{1,0:T(8,128)(2,1)S(1)}, f32[8,128]{1,0:T(8,128)S(1)}) custom-call(s32[7]{0:T(128)S(1)} %stack.31.refs_0_, bf16[192,768]{1,0:T(8,128)(2,1)} %refs_0_.1, bf16[192,768]{1,0:T(8,128)(2,1)} %refs_1_.5), custom_call_target="tpu_custom_call" | custom-call | bytes 100000000 | tf_op jit(solution)/shard_map/pick/pallas_call | solution.py:144
  2.7 2.6 %collective-permute-start.3 = (bf16[96,768]{1,0:T(8,128)(2,1)S(1)}, bf16[96,768]{1,0:T(8,128)(2,1)S(1)}, u32[]{:S(2)}, u32[]{:S(2)}) collective-permute-start(bf16[96,768]{1,0:T(8,128)(2,1)S(1)} %get-tuple-element.133), channel_id=1, source_target_pairs={{0,2},{1,3},{2,0},{3,1},{4,6},{5,7},{6,4},{7,5},{8,10},{9,11},{10,... | collective-permute-start | bytes 442376 | tf_op jit(solution)/shard_map/ppermute | solution.py:686
  6.1 1.5 %load.1 = (bf16[592,768]{1,0:T(8,128)(2,1)S(1)}, bf16[256,768]{1,0:T(8,128)(2,1)S(1)}, bf16[256,768]{1,0:T(8,128)(2,1)S(1)}, f32[768]{0:T(1024)S(1)}, f32[768]{0...) custom-call(bf16[192,768]{1,0:T(8,128)(2,1)} %refs_0_.1, bf16[192,768]{1,0:T(8,128)(2,1)} %refs_1_.5, ...), custom_call_target="tpu_custom_call" | custom-call | bytes 100000000 | tf_op jit(solution)/shard_map/load/pallas_call | solution.py:144
  7.9 4.0 %attention_forward.2 = (bf16[256,768]{1,0:T(8,128)(2,1)S(1)}, bf16[384,256]{1,0:T(8,128)(2,1)S(1)}, bf16[384,256]{1,0:T(8,128)(2,1)S(1)}, bf16[256,384]{1,0:T(8,...) custom-call(s32[7]{0:T(128)S(1)} %stack.31.refs_0_, ...), custom_call_target="tpu_custom_call" | custom-call | flops 10000000000 | bytes 100000000 | tf_op jit(solution)/shard_map/attention_forward/pallas_call | solution.py:144
  11.9 1.9 %collective-permute-start.11 = (bf16[256,1152]{1,0:T(8,128)(2,1)S(1)}, bf16[256,1152]{1,0:T(8,128)(2,1)S(1)}, u32[]{:S(2)}, u32[]{:S(2)}) collective-permute-start(bf16[256,1152]{1,0:T(8,128)(2,1)S(1)} %get-tuple-element.130.refs_1_), channel_id=1, source_target_pairs={{0,2},{1,3},{2,0},{3,1},{4,6},{5,7},{6,4},{7,5},{8,10},{9,11},{10,... | collective-permute-start | bytes 1769480 | tf_op jit(solution)/shard_map/ppermute | solution.py:686
  13.8 1.6 %collective-permute-start.6 = (bf16[96,768]{1,0:T(8,128)(2,1)S(1)}, bf16[96,768]{1,0:T(8,128)(2,1)S(1)}, u32[]{:S(2)}, u32[]{:S(2)}) collective-permute-start(bf16[96,768]{1,0:T(8,128)(2,1)S(1)} %get-tuple-element.141.refs_3_), channel_id=1, source_target_pairs={{0,8},{1,9},{2,10},{3,11},{4,12},{5,13},{6,14},{7,15},{8,0},{9,1},... | collective-permute-start | bytes 442376 | tf_op jit(solution)/shard_map/ppermute | solution.py:694
  15.5 1.5 %collective-permute-start.5 = (bf16[96,768]{1,0:T(8,128)(2,1)S(1)}, bf16[96,768]{1,0:T(8,128)(2,1)S(1)}, u32[]{:S(2)}, u32[]{:S(2)}) collective-permute-start(bf16[96,768]{1,0:T(8,128)(2,1)S(1)} %get-tuple-element.141.refs_3_), channel_id=1, source_target_pairs={{0,4},{1,5},{2,6},{3,7},{4,0},{5,1},{6,2},{7,3},{8,12},{9,13},{10,... | collective-permute-start | bytes 442376 | tf_op jit(solution)/shard_map/ppermute | solution.py:694
  17.0 1.5 %collective-permute-done.1.refs_3_.refs_0_.refs_4_ = bf16[256,768]{1,0:T(8,128)(2,1)S(1)} collective-permute-done((bf16[256,768]{1,0:T(8,128)(2,1)}, bf16[256,768]{1,0:T(8,128)(2,1)S(1)}, u32[]{:S(2)}, u32[]{:S(2)}) %collective-permute-start.1) | collective-permute-done | bytes 393248 | tf_op jit(solution)/shard_map/ppermute | solution.py:686
  18.5 3.5 %attention_forward.3 = (bf16[256,768]{1,0:T(8,128)(2,1)S(1)}, bf16[384,256]{1,0:T(8,128)(2,1)S(1)}, bf16[384,256]{1,0:T(8,128)(2,1)S(1)}, bf16[256,384]{1,0:T(8,...) custom-call(s32[7]{0:T(128)S(1)} %stack.31.refs_0_, ...), custom_call_target="tpu_custom_call" | custom-call | bytes 100000000 | tf_op jit(solution)/shard_map/attention_forward/pallas_call | solution.py:144
  22.1 2.0 %collective-permute-start.7 = (bf16[96,768]{1,0:T(8,128)(2,1)S(1)}, bf16[96,768]{1,0:T(8,128)(2,1)S(1)}, u32[]{:S(2)}, u32[]{:S(2)}) collective-permute-start(bf16[96,768]{1,0:T(8,128)(2,1)S(1)} %get-tuple-element.144), channel_id=1, source_target_pairs={{0,4},{1,5},{2,6},{3,7},{4,0},{5,1},{6,2},{7,3},{8,12},{9,13},{10,... | collective-permute-start | bytes 442376 | tf_op jit(solution)/shard_map/ppermute | solution.py:694
  24.6 2.9 %collective-permute-done.7.refs_5_ = bf16[96,768]{1,0:T(8,128)(2,1)S(1)} collective-permute-done((bf16[96,768]{1,0:T(8,128)(2,1)S(1)}, bf16[96,768]{1,0:T(8,128)(2,1)S(1)}, u32[]{:S(2)}, u32[]{:S(2)}) %collective-permute-start.7) | collective-permute-done | bytes 147488 | tf_op jit(solution)/shard_map/ppermute | solution.py:694
  27.5 1.7 %collective-permute-start.4 = (bf16[256,384]{1,0:T(8,128)(2,1)S(1)}, bf16[256,384]{1,0:T(8,128)(2,1)S(1)}, u32[]{:S(2)}, u32[]{:S(2)}) collective-permute-start(bf16[256,384]{1,0:T(8,128)(2,1)S(1)} %get-tuple-element.136.refs_1_), channel_id=1, source_target_pairs={{0,2},{1,3},{2,0},{3,1},{4,6},{5,7},{6,4},{7,5},{8,10},{9,11},{10,... | collective-permute-start | bytes 589832 | tf_op jit(solution)/shard_map/ppermute | solution.py:686
  29.3 0.8 pack_far.1
  30.1 1.0 collective-permute-done.11.refs_2_.refs_14_.refs_4_
  31.1 1.2 %feed_far.1 = (f32[256,768]{1,0:T(8,128)S(1)}, bf16[256,768]{1,0:T(8,128)(2,1)S(1)}, bf16[256,384]{1,0:T(8,128)(2,1)S(1)}, bf16[256,384]{1,0:T(8,128)(2,1)S(1)}, f32[8,128]{1,0:T(8,128)S(1)}) custom-call(bf16[256,768]{1,0:T(8,128)(2,1)S(1)} %collective-permute-done.1.refs_3_.refs_0_.refs_4_, bf16[256,384]{1,0:T(8,128)(2,1)S(1)} %get-tuple-element.136.refs_1_, ...), custom_call_target="tpu_custom_call" | custom-call | bytes 100000000 | tf_op jit(solution)/shard_map/feed_far/pallas_call | solution.py:144
  32.4 1.8 %collective-permute-start.13 = (bf16[256,384]{1,0:T(8,128)(2,1)S(1)}, bf16[256,384]{1,0:T(8,128)(2,1)S(1)}, u32[]{:S(2)}, u32[]{:S(2)}) collective-permute-start(bf16[256,384]{1,0:T(8,128)(2,1)S(1)} %get-tuple-element.151.refs_12_.refs_0_), channel_id=1, source_target_pairs={{0,2},{1,3},{2,0},{3,1},{4,6},{5,7},{6,4},{7,5},{8,10},{9,11},{10,... | collective-permute-start | bytes 589832 | tf_op jit(solution)/shard_map/ppermute | solution.py:686
  34.2 1.2 %collective-permute-done.4.refs_3_ = bf16[256,384]{1,0:T(8,128)(2,1)S(1)} collective-permute-done((bf16[256,384]{1,0:T(8,128)(2,1)S(1)}, bf16[256,384]{1,0:T(8,128)(2,1)S(1)}, u32[]{:S(2)}, u32[]{:S(2)}) %collective-permute-start.4) | collective-permute-done | bytes 196640 | tf_op jit(solution)/shard_map/ppermute | solution.py:686
  35.3 2.6 %feed_own.1 = (f32[256,768]{1,0:T(8,128)S(1)}, bf16[256,768]{1,0:T(8,128)(2,1)}, bf16[256,384]{1,0:T(8,128)(2,1)S(1)}, bf16[256,384]{1,0:T(8,128)(2,1)S(1)}, bf1...) custom-call(bf16[256,768]{1,0:T(8,128)(2,1)S(1)} %get-tuple-element., ...), custom_call_target="tpu_custom_call" | custom-call | bytes 100000000 | tf_op jit(solution)/shard_map/feed_own/pallas_call | solution.py:144
  38.0 1.8 %collective-permute-start.16 = (bf16[256,384]{1,0:T(8,128)(2,1)S(1)}, bf16[256,384]{1,0:T(8,128)(2,1)S(1)}, u32[]{:S(2)}, u32[]{:S(2)}) collective-permute-start(bf16[256,384]{1,0:T(8,128)(2,1)S(1)} %get-tuple-element.158.refs_0_), channel_id=1, source_target_pairs={{0,2},{1,3},{2,0},{3,1},{4,6},{5,7},{6,4},{7,5},{8,10},{9,11},{10,... | collective-permute-start | bytes 589832 | tf_op jit(solution)/shard_map/ppermute | solution.py:686
  39.8 2.5 %attention_backward.2 = (bf16[256,768]{1,0:T(8,128)(2,1)S(1)}, bf16[1152,256]{1,0:T(8,128)(2,1)S(1)}, f32[256,768]{1,0:T(8,128)S(1)}, f32[8,768]{1,0:T(8,128)S(1)}, f32[8,128]{1,0:T(8,128)S(1)}) custom-call(bf16[256,384]{1,0:T(8,128)(2,1)S(1)} %get-tuple-element.158.refs_0_, bf16[256,384]{1,0:T(8,128)(2,1)S(1)} %collective-permute-done.13.refs_1_, ...), custom_call_target="tpu_custom_call" | custom-call | flops 10000000000 | bytes 100000000 | tf_op jit(solution)/shard_map/attention_backward/pallas_call | solution.py:144
  42.8 1.6 %collective-permute-start.15 = (bf16[96,768]{1,0:T(8,128)(2,1)S(1)}, bf16[96,768]{1,0:T(8,128)(2,1)S(1)}, u32[]{:S(2)}, u32[]{:S(2)}) collective-permute-start(bf16[96,768]{1,0:T(8,128)(2,1)S(1)} %get-tuple-element.166), channel_id=1, source_target_pairs={{0,4},{1,9},{2,6},{3,11},{4,0},{5,13},{6,2},{7,15},{8,12},{9,1},{1... | collective-permute-start | bytes 442376 | tf_op jit(solution)/shard_map/ppermute | solution.py:694
  44.9 2.5 %attention_backward.3 = (bf16[256,768]{1,0:T(8,128)(2,1)S(1)}, bf16[1152,256]{1,0:T(8,128)(2,1)S(1)}, f32[8,128]{1,0:T(8,128)S(1)}) custom-call(bf16[256,384]{1,0:T(8,128)(2,1)S(1)} %get-tuple-element.151.refs_12_.refs_0_, bf16[256,384]{1,0:T(8,128)(2,1)S(1)} %collective-permute-done.16.refs_1_, ...), custom_call_target="tpu_custom_call" | custom-call | bytes 100000000 | tf_op jit(solution)/shard_map/attention_backward/pallas_call | solution.py:144
  49.7 1.6 %collective-permute-start.17 = (bf16[96,768]{1,0:T(8,128)(2,1)S(1)}, bf16[96,768]{1,0:T(8,128)(2,1)S(1)}, u32[]{:S(2)}, u32[]{:S(2)}) collective-permute-start(bf16[96,768]{1,0:T(8,128)(2,1)S(1)} %get-tuple-element.184), channel_id=1, source_target_pairs={{0,8},{1,5},{2,10},{3,7},{4,12},{5,1},{6,14},{7,3},{8,0},{9,13},{1... | collective-permute-start | bytes 442376 | tf_op jit(solution)/shard_map/ppermute | solution.py:694
  52.6 1.6 %collective-permute-start.20 = (bf16[192,768]{1,0:T(8,128)(2,1)S(1)}, bf16[192,768]{1,0:T(8,128)(2,1)S(1)}, u32[]{:S(2)}, u32[]{:S(2)}) collective-permute-start(bf16[192,768]{1,0:T(8,128)(2,1)S(1)} %get-tuple-element.192), channel_id=1, source_target_pairs={{0,4},{1,9},{2,6},{3,11},{4,0},{5,13},{6,2},{7,15},{8,12},{9,1},{1... | collective-permute-start | bytes 884744 | tf_op jit(solution)/shard_map/ppermute | solution.py:694
  55.6 2.6 %collective-permute-start.19 = (bf16[96,768]{1,0:T(8,128)(2,1)S(1)}, bf16[96,768]{1,0:T(8,128)(2,1)S(1)}, u32[]{:S(2)}, u32[]{:S(2)}) collective-permute-start(bf16[96,768]{1,0:T(8,128)(2,1)S(1)} %get-tuple-element.189.refs_0_), channel_id=1, source_target_pairs={{0,16},{1,17},{2,18},{3,19},{4,20},{5,21},{6,22},{7,23},{8,24},{9,... | collective-permute-start | bytes 442376 | tf_op jit(solution)/shard_map/ppermute | solution.py:694
  58.2 1.5 %collective-permute-start.23 = (bf16[192,768]{1,0:T(8,128)(2,1)S(1)}, bf16[192,768]{1,0:T(8,128)(2,1)S(1)}, u32[]{:S(2)}, u32[]{:S(2)}) collective-permute-start(bf16[192,768]{1,0:T(8,128)(2,1)S(1)} %get-tuple-element.200), channel_id=1, source_target_pairs={{0,4},{1,9},{2,6},{3,11},{4,0},{5,13},{6,2},{7,15},{8,12},{9,1},{1... | collective-permute-start | bytes 884744 | tf_op jit(solution)/shard_map/ppermute | solution.py:694
  60.4 1.6 %collective-permute-start.24 = (bf16[192,768]{1,0:T(8,128)(2,1)S(1)}, bf16[192,768]{1,0:T(8,128)(2,1)S(1)}, u32[]{:S(2)}, u32[]{:S(2)}) collective-permute-start(bf16[192,768]{1,0:T(8,128)(2,1)S(1)} %get-tuple-element.201), channel_id=1, source_target_pairs={{0,8},{1,5},{2,10},{3,7},{4,12},{5,1},{6,14},{7,3},{8,0},{9,13},{1... | collective-permute-start | bytes 884744 | tf_op jit(solution)/shard_map/ppermute | solution.py:694
  62.1 1.4 %input_grads.1 = (f32[256,768]{1,0:T(8,128)S(1)}, bf16[272,768]{1,0:T(8,128)(2,1)S(1)}, f32[8,128]{1,0:T(8,128)S(1)}) custom-call(bf16[1152,256]{1,0:T(8,128)(2,1)S(1)} %get-tuple-element.167.refs_0_.refs_4_.refs_8_, bf16[1152,256]{1,0:T(8,128)(2,1)S(1)} %get-tuple-element.174.refs_1_.refs_5_.refs_9_, ...), custom_call_target="tpu_custom_call" | custom-call | bytes 100000000 | tf_op jit(solution)/shard_map/input_grads/pallas_call | solution.py:144
  63.5 1.4 %collective-permute-start.22 = (bf16[272,768]{1,0:T(8,128)(2,1)S(1)}, bf16[272,768]{1,0:T(8,128)(2,1)S(1)}, u32[]{:S(2)}, u32[]{:S(2)}) collective-permute-start(bf16[272,768]{1,0:T(8,128)(2,1)S(1)} %get-tuple-element.199.refs_0_), channel_id=1, source_target_pairs={{0,2},{1,3},{2,0},{3,1},{4,6},{5,7},{6,4},{7,5},{8,10},{9,11},{10,... | collective-permute-start | bytes 1253384 | tf_op jit(solution)/shard_map/ppermute | solution.py:686
  65.8 1.4 %collective-permute-start.21 = (bf16[256,768]{1,0:T(8,128)(2,1)S(1)}, bf16[256,768]{1,0:T(8,128)(2,1)S(1)}, u32[]{:S(2)}, u32[]{:S(2)}) collective-permute-start(bf16[256,768]{1,0:T(8,128)(2,1)S(1)} %get-tuple-element.198), channel_id=1, source_target_pairs={{0,2},{1,3},{2,0},{3,1},{4,6},{5,7},{6,4},{7,5},{8,10},{9,11},{10,... | collective-permute-start | bytes 1179656 | tf_op jit(solution)/shard_map/ppermute | solution.py:686
  69.0 3.1 %collective-permute-start.29 = (bf16[192,768]{1,0:T(8,128)(2,1)S(1)}, bf16[192,768]{1,0:T(8,128)(2,1)S(1)}, u32[]{:S(2)}, u32[]{:S(2)}) collective-permute-start(bf16[192,768]{1,0:T(8,128)(2,1)S(1)} %get-tuple-element.212.refs_0_), channel_id=1, source_target_pairs={{0,16},{1,17},{2,18},{3,19},{4,20},{5,21},{6,22},{7,23},{8,24},{9,... | collective-permute-start | bytes 884744 | tf_op jit(solution)/shard_map/ppermute | solution.py:694
  72.1 1.5 %collective-permute-start.27 = (bf16[96,768]{1,0:T(8,128)(2,1)S(1)}, bf16[96,768]{1,0:T(8,128)(2,1)S(1)}, u32[]{:S(2)}, u32[]{:S(2)}) collective-permute-start(bf16[96,768]{1,0:T(8,128)(2,1)S(1)} %get-tuple-element.205.refs_1_), channel_id=1, source_target_pairs={{0,4},{1,9},{2,6},{3,11},{4,0},{5,13},{6,2},{7,15},{8,12},{9,1},{1... | collective-permute-start | bytes 442376 | tf_op jit(solution)/shard_map/ppermute | solution.py:694
  74.1 2.0 %collective-permute-done.22.refs_1_.refs_3_ = bf16[272,768]{1,0:T(8,128)(2,1)S(1)} collective-permute-done((bf16[272,768]{1,0:T(8,128)(2,1)S(1)}, bf16[272,768]{1,0:T(8,128)(2,1)S(1)}, u32[]{:S(2)}, u32[]{:S(2)}) %collective-permute-start.22) | collective-permute-done | bytes 417824 | tf_op jit(solution)/shard_map/ppermute | solution.py:686
  76.2 1.0 collective-permute-done.27.refs_3_
  77.2 1.6 %collective-permute-done.28.refs_4_ = bf16[96,768]{1,0:T(8,128)(2,1)S(1)} collective-permute-done((bf16[96,768]{1,0:T(8,128)(2,1)S(1)}, bf16[96,768]{1,0:T(8,128)(2,1)S(1)}, u32[]{:S(2)}, u32[]{:S(2)}) %collective-permute-start.28) | collective-permute-done | bytes 147488 | tf_op jit(solution)/shard_map/ppermute | solution.py:694
  78.8 1.7 %place_sums.4 = (f32[192,768]{1,0:T(8,128)}, f32[192,768]{1,0:T(8,128)}, f32[8,128]{1,0:T(8,128)S(1)}) custom-call(s32[7]{0:T(128)S(1)} %stack.31.refs_0_, bf16[96,768]{1,0:T(8,128)(2,1)S(1)} %get-tuple-element.205.refs_1_, bf16[96,768]{1,0:T(8,128)(2,1)S(1)} %collective-permute-done.26.refs_2_, bf16[96,768]{1,0:T(8,128)(2,1)S(1)} %collective-permute-done.27.refs_3_, ...), custom_call_target="tpu_custom_call" | custom-call | bytes 100000000 | tf_op jit(solution)/shard_map/place_sums/pallas_call | solution.py:144
  80.6 1.1 %collective-permute-start.30 = (bf16[16,768]{1,0:T(8,128)(2,1)S(1)}, bf16[16,768]{1,0:T(8,128)(2,1)S(1)}, u32[]{:S(2)}, u32[]{:S(2)}) collective-permute-start(bf16[16,768]{1,0:T(8,128)(2,1)S(1)} %get-tuple-element.213.refs_2_), channel_id=1, source_target_pairs={{0,16},{1,17},{2,18},{3,19},{4,20},{5,21},{6,22},{7,23},{8,24},{9,... | collective-permute-start | bytes 73736 | tf_op jit(solution)/shard_map/ppermute | solution.py:694
  82.3 0.8 add_result.1
  83.1 2.3 %collective-permute-done.30.refs_3_ = bf16[16,768]{1,0:T(8,128)(2,1)S(1)} collective-permute-done((bf16[16,768]{1,0:T(8,128)(2,1)S(1)}, bf16[16,768]{1,0:T(8,128)(2,1)S(1)}, u32[]{:S(2)}, u32[]{:S(2)}) %collective-permute-start.30) | collective-permute-done | bytes 24608 | tf_op jit(solution)/shard_map/ppermute | solution.py:694
  85.5 1.0 collective-permute-start.31
  86.5 1.3 %input_norm.1 = (bf16[256,768]{1,0:T(8,128)(2,1)}, f32[8,128]{1,0:T(8,128)S(1)}) custom-call(bf16[256,768]{1,0:T(8,128)(2,1)S(1)} %get-tuple-element.125.refs_3_.refs_0_, f32[768]{0:T(1024)S(1)} %get-tuple-element.126.refs_4_.refs_1_, f32[256,768]{1,0:T(8,128)S(1)} %get-tuple-element.210.refs_2_, ...), custom_call_target="tpu_custom_call" | custom-call | bytes 100000000 | tf_op jit(solution)/shard_map/input_norm/pallas_call | solution.py:144
  87.9 4.7 %collective-permute-done.31.refs_1_ = bf16[208,768]{1,0:T(8,128)(2,1)S(1)} collective-permute-done((bf16[208,768]{1,0:T(8,128)(2,1)S(1)}, bf16[208,768]{1,0:T(8,128)(2,1)S(1)}, u32[]{:S(2)}, u32[]{:S(2)}) %collective-permute-start.31) | collective-permute-done | bytes 319520 | tf_op jit(solution)/shard_map/ppermute | solution.py:694
  92.6 1.6 %collective-permute-start.32 = (bf16[208,768]{1,0:T(8,128)(2,1)S(1)}, bf16[208,768]{1,0:T(8,128)(2,1)S(1)}, u32[]{:S(2)}, u32[]{:S(2)}) collective-permute-start(bf16[208,768]{1,0:T(8,128)(2,1)S(1)} %get-tuple-element.219.refs_1_), channel_id=1, source_target_pairs={{0,4},{1,9},{2,6},{3,11},{4,0},{5,13},{6,2},{7,15},{8,12},{9,1},{1... | collective-permute-start | bytes 958472 | tf_op jit(solution)/shard_map/ppermute | solution.py:694
  94.7 1.6 %place_sums.5 = (f32[3,192,768]{2,1,0:T(8,128)}, f32[192,768]{1,0:T(8,128)}, f32[8,128]{1,0:T(8,128)S(1)}) custom-call(s32[7]{0:T(128)S(1)} %stack.31.refs_0_, bf16[208,768]{1,0:T(8,128)(2,1)S(1)} %get-tuple-element.219.refs_1_, bf16[208,768]{1,0:T(8,128)(2,1)S(1)} %get-tuple-element.220.refs_2_, f32[8,128]{1,0:T(8,128)S(1)} %get-tuple-element.221.refs_3_), custom_call_target="tpu_custom_call" | custom-call | bytes 100000000 | tf_op jit(solution)/shard_map/place_sums/pallas_call | solution.py:144
  96.3 3.3 %collective-permute-done.32.refs_3_ = bf16[208,768]{1,0:T(8,128)(2,1)S(1)} collective-permute-done((bf16[208,768]{1,0:T(8,128)(2,1)S(1)}, bf16[208,768]{1,0:T(8,128)(2,1)S(1)}, u32[]{:S(2)}, u32[]{:S(2)}) %collective-permute-start.32) | collective-permute-done | bytes 319520 | tf_op jit(solution)/shard_map/ppermute | solution.py:694
  99.6 1.4 %place_sums.6 = (f32[3,192,768]{2,1,0:T(8,128)}, f32[192,768]{1,0:T(8,128)}, f32[8,128]{1,0:T(8,128)S(1)}) custom-call(s32[7]{0:T(128)S(1)} %stack.31.refs_0_, bf16[208,768]{1,0:T(8,128)(2,1)S(1)} %get-tuple-element.219.refs_1_, bf16[208,768]{1,0:T(8,128)(2,1)S(1)} %get-tuple-element.220.refs_2_, ...), custom_call_target="tpu_custom_call", output_to_operand_aliasing={{0}: (4, {}), {1}: (5, {})} | custom-call | bytes 100000000 | tf_op jit(solution)/shard_map/place_sums/pallas_call | solution.py:144
  101.1 2.0 %collective-permute-done.33.refs_4_ = bf16[208,768]{1,0:T(8,128)(2,1)S(1)} collective-permute-done((bf16[208,768]{1,0:T(8,128)(2,1)S(1)}, bf16[208,768]{1,0:T(8,128)(2,1)S(1)}, u32[]{:S(2)}, u32[]{:S(2)}) %collective-permute-start.33) | collective-permute-done | bytes 319520 | tf_op jit(solution)/shard_map/ppermute | solution.py:694
  103.1 2.0 %place_sums.7 = (f32[3,192,768]{2,1,0:T(8,128)}, f32[192,768]{1,0:T(8,128)}, f32[768]{0:T(1024)}, f32[768]{0:T(1024)}, f32[768]{0:T(1024)}, /*index=5*/f32[768]{0:T(1024)}, f32[192]{0:T(256)}, f32[8,128]{1,0:T(8,128)}) custom-call(s32[7]{0:T(128)S(1)} %stack.31.refs_0_, ...), custom_call_target="tpu_custom_call", output_to_operand_aliasing={{0}: (5, {}), {1}: (6, {})} | custom-call | bytes 100000000 | tf_op jit(solution)/shard_map/place_sums/pallas_call | solution.py:144
  (55 shorter events, 13.5 us)
Async XLA Ops:
  0.6 7.2 %collective-permute-start = (bf16[3,192,768]{2,1,0:T(8,128)(2,1)}, bf16[3,192,768]{2,1,0:T(8,128)(2,1)S(1)}, u32[]{:S(2)}, u32[]{:S(2)}) collective-permute-start(bf16[3,192,768]{2,1,0:T(8,128)(2,1)} %refs_6_.3), channel_id=1, source_target_pairs={{0,1},{1,0},{2,3},{3,2},{4,5},{5,4},{6,7},{7,6},{8,9},{9,8},{10,11... | collective-permute-start | bytes 2654216 | tf_op jit(solution)/shard_map/ppermute | solution.py:683
  2.7 11.1 %collective-permute-start.3 = (bf16[96,768]{1,0:T(8,128)(2,1)S(1)}, bf16[96,768]{1,0:T(8,128)(2,1)S(1)}, u32[]{:S(2)}, u32[]{:S(2)}) collective-permute-start(bf16[96,768]{1,0:T(8,128)(2,1)S(1)} %get-tuple-element.133), channel_id=1, source_target_pairs={{0,2},{1,3},{2,0},{3,1},{4,6},{5,7},{6,4},{7,5},{8,10},{9,11},{10,... | collective-permute-start | bytes 442376 | tf_op jit(solution)/shard_map/ppermute | solution.py:686
  5.4 13.1 %collective-permute-start.1 = (bf16[256,768]{1,0:T(8,128)(2,1)}, bf16[256,768]{1,0:T(8,128)(2,1)S(1)}, u32[]{:S(2)}, u32[]{:S(2)}) collective-permute-start(bf16[256,768]{1,0:T(8,128)(2,1)} %refs_4_.1), channel_id=1, source_target_pairs={{0,2},{1,3},{2,0},{3,1},{4,6},{5,7},{6,4},{7,5},{8,10},{9,11},{10,... | collective-permute-start | bytes 1179656 | tf_op jit(solution)/shard_map/ppermute | solution.py:686
  7.6 10.9 %collective-permute-start.2 = (bf16[592,768]{1,0:T(8,128)(2,1)S(1)}, bf16[592,768]{1,0:T(8,128)(2,1)S(1)}, u32[]{:S(2)}, u32[]{:S(2)}) collective-permute-start(bf16[592,768]{1,0:T(8,128)(2,1)S(1)} %get-tuple-element.132.refs_7_.refs_8_.refs_9_), channel_id=1, source_target_pairs={{0,1},{1,0},{2,3},{3,2},{4,5},{5,4},{6,7},{7,6},{8,9},{9,8},{10,11... | collective-permute-start | bytes 2727944 | tf_op jit(solution)/shard_map/ppermute | solution.py:683
  11.9 19.2 %collective-permute-start.11 = (bf16[256,1152]{1,0:T(8,128)(2,1)S(1)}, bf16[256,1152]{1,0:T(8,128)(2,1)S(1)}, u32[]{:S(2)}, u32[]{:S(2)}) collective-permute-start(bf16[256,1152]{1,0:T(8,128)(2,1)S(1)} %get-tuple-element.130.refs_1_), channel_id=1, source_target_pairs={{0,2},{1,3},{2,0},{3,1},{4,6},{5,7},{6,4},{7,5},{8,10},{9,11},{10,... | collective-permute-start | bytes 1769480 | tf_op jit(solution)/shard_map/ppermute | solution.py:686
  13.8 8.2 %collective-permute-start.6 = (bf16[96,768]{1,0:T(8,128)(2,1)S(1)}, bf16[96,768]{1,0:T(8,128)(2,1)S(1)}, u32[]{:S(2)}, u32[]{:S(2)}) collective-permute-start(bf16[96,768]{1,0:T(8,128)(2,1)S(1)} %get-tuple-element.141.refs_3_), channel_id=1, source_target_pairs={{0,8},{1,9},{2,10},{3,11},{4,12},{5,13},{6,14},{7,15},{8,0},{9,1},... | collective-permute-start | bytes 442376 | tf_op jit(solution)/shard_map/ppermute | solution.py:694
  15.5 6.6 %collective-permute-start.5 = (bf16[96,768]{1,0:T(8,128)(2,1)S(1)}, bf16[96,768]{1,0:T(8,128)(2,1)S(1)}, u32[]{:S(2)}, u32[]{:S(2)}) collective-permute-start(bf16[96,768]{1,0:T(8,128)(2,1)S(1)} %get-tuple-element.141.refs_3_), channel_id=1, source_target_pairs={{0,4},{1,5},{2,6},{3,7},{4,0},{5,1},{6,2},{7,3},{8,12},{9,13},{10,... | collective-permute-start | bytes 442376 | tf_op jit(solution)/shard_map/ppermute | solution.py:694
  22.1 5.4 %collective-permute-start.7 = (bf16[96,768]{1,0:T(8,128)(2,1)S(1)}, bf16[96,768]{1,0:T(8,128)(2,1)S(1)}, u32[]{:S(2)}, u32[]{:S(2)}) collective-permute-start(bf16[96,768]{1,0:T(8,128)(2,1)S(1)} %get-tuple-element.144), channel_id=1, source_target_pairs={{0,4},{1,5},{2,6},{3,7},{4,0},{5,1},{6,2},{7,3},{8,12},{9,13},{10,... | collective-permute-start | bytes 442376 | tf_op jit(solution)/shard_map/ppermute | solution.py:694
  24.1 5.2 %collective-permute-start.9 = (bf16[2,96,768]{2,1,0:T(8,128)(2,1)S(1)}, bf16[2,96,768]{2,1,0:T(8,128)(2,1)S(1)}, u32[]{:S(2)}, u32[]{:S(2)}) collective-permute-start(bf16[2,96,768]{2,1,0:T(8,128)(2,1)S(1)} %get-tuple-element.143.refs_4_), channel_id=1, source_target_pairs={{0,1},{1,0},{2,3},{3,2},{4,5},{5,4},{6,7},{7,6},{8,9},{9,8},{10,11... | collective-permute-start | bytes 884744 | tf_op jit(solution)/shard_map/ppermute | solution.py:683
  24.1 5.2 %collective-permute-start.8 = (bf16[96,768]{1,0:T(8,128)(2,1)S(1)}, bf16[96,768]{1,0:T(8,128)(2,1)S(1)}, u32[]{:S(2)}, u32[]{:S(2)}) collective-permute-start(bf16[96,768]{1,0:T(8,128)(2,1)S(1)} %get-tuple-element.141.refs_3_), channel_id=1, source_target_pairs={{0,1},{1,0},{2,3},{3,2},{4,5},{5,4},{6,7},{7,6},{8,9},{9,8},{10,11... | collective-permute-start | bytes 442376 | tf_op jit(solution)/shard_map/ppermute | solution.py:683
  27.5 1.7 %collective-permute-start.10 = (bf16[96,768]{1,0:T(8,128)(2,1)S(1)}, bf16[96,768]{1,0:T(8,128)(2,1)S(1)}, u32[]{:S(2)}, u32[]{:S(2)}) collective-permute-start(bf16[96,768]{1,0:T(8,128)(2,1)S(1)} %collective-permute-done.7.refs_5_), channel_id=1, source_target_pairs={{0,1},{1,0},{2,3},{3,2},{4,5},{5,4},{6,7},{7,6},{8,9},{9,8},{10,11... | collective-permute-start | bytes 442376 | tf_op jit(solution)/shard_map/ppermute | solution.py:683
  27.5 7.8 %collective-permute-start.4 = (bf16[256,384]{1,0:T(8,128)(2,1)S(1)}, bf16[256,384]{1,0:T(8,128)(2,1)S(1)}, u32[]{:S(2)}, u32[]{:S(2)}) collective-permute-start(bf16[256,384]{1,0:T(8,128)(2,1)S(1)} %get-tuple-element.136.refs_1_), channel_id=1, source_target_pairs={{0,2},{1,3},{2,0},{3,1},{4,6},{5,7},{6,4},{7,5},{8,10},{9,11},{10,... | collective-permute-start | bytes 589832 | tf_op jit(solution)/shard_map/ppermute | solution.py:686
  32.4 7.4 %collective-permute-start.13 = (bf16[256,384]{1,0:T(8,128)(2,1)S(1)}, bf16[256,384]{1,0:T(8,128)(2,1)S(1)}, u32[]{:S(2)}, u32[]{:S(2)}) collective-permute-start(bf16[256,384]{1,0:T(8,128)(2,1)S(1)} %get-tuple-element.151.refs_12_.refs_0_), channel_id=1, source_target_pairs={{0,2},{1,3},{2,0},{3,1},{4,6},{5,7},{6,4},{7,5},{8,10},{9,11},{10,... | collective-permute-start | bytes 589832 | tf_op jit(solution)/shard_map/ppermute | solution.py:686
  38.0 6.9 %collective-permute-start.16 = (bf16[256,384]{1,0:T(8,128)(2,1)S(1)}, bf16[256,384]{1,0:T(8,128)(2,1)S(1)}, u32[]{:S(2)}, u32[]{:S(2)}) collective-permute-start(bf16[256,384]{1,0:T(8,128)(2,1)S(1)} %get-tuple-element.158.refs_0_), channel_id=1, source_target_pairs={{0,2},{1,3},{2,0},{3,1},{4,6},{5,7},{6,4},{7,5},{8,10},{9,11},{10,... | collective-permute-start | bytes 589832 | tf_op jit(solution)/shard_map/ppermute | solution.py:686
  39.8 2.5 %collective-permute-start.12 = (bf16[2,192,768]{2,1,0:T(8,128)(2,1)S(1)}, bf16[2,192,768]{2,1,0:T(8,128)(2,1)S(1)}, u32[]{:S(2)}, u32[]{:S(2)}) collective-permute-start(bf16[2,192,768]{2,1,0:T(8,128)(2,1)S(1)} %get-tuple-element.157), channel_id=1, source_target_pairs={{0,1},{1,0},{2,3},{3,2},{4,5},{5,4},{6,7},{7,6},{8,9},{9,8},{10,11... | collective-permute-start | bytes 1769480 | tf_op jit(solution)/shard_map/ppermute | solution.py:683
  42.8 6.3 %collective-permute-start.15 = (bf16[96,768]{1,0:T(8,128)(2,1)S(1)}, bf16[96,768]{1,0:T(8,128)(2,1)S(1)}, u32[]{:S(2)}, u32[]{:S(2)}) collective-permute-start(bf16[96,768]{1,0:T(8,128)(2,1)S(1)} %get-tuple-element.166), channel_id=1, source_target_pairs={{0,4},{1,9},{2,6},{3,11},{4,0},{5,13},{6,2},{7,15},{8,12},{9,1},{1... | collective-permute-start | bytes 442376 | tf_op jit(solution)/shard_map/ppermute | solution.py:694
  44.4 9.8 %collective-permute-start.14 = (bf16[96,768]{1,0:T(8,128)(2,1)S(1)}, bf16[96,768]{1,0:T(8,128)(2,1)S(1)}, u32[]{:S(2)}, u32[]{:S(2)}) collective-permute-start(bf16[96,768]{1,0:T(8,128)(2,1)S(1)} %get-tuple-element.165), channel_id=1, source_target_pairs={{0,4},{1,9},{2,6},{3,11},{4,0},{5,13},{6,2},{7,15},{8,12},{9,1},{1... | collective-permute-start | bytes 442376 | tf_op jit(solution)/shard_map/ppermute | solution.py:694
  49.0 2.9 %collective-permute-start.18 = (bf16[4,192,768]{2,1,0:T(8,128)(2,1)S(1)}, bf16[4,192,768]{2,1,0:T(8,128)(2,1)S(1)}, u32[]{:S(2)}, u32[]{:S(2)}) collective-permute-start(bf16[4,192,768]{2,1,0:T(8,128)(2,1)S(1)} %get-tuple-element.186), channel_id=1, source_target_pairs={{0,1},{1,0},{2,3},{3,2},{4,5},{5,4},{6,7},{7,6},{8,9},{9,8},{10,11... | collective-permute-start | bytes 3538952 | tf_op jit(solution)/shard_map/ppermute | solution.py:683
  49.7 5.2 %collective-permute-start.17 = (bf16[96,768]{1,0:T(8,128)(2,1)S(1)}, bf16[96,768]{1,0:T(8,128)(2,1)S(1)}, u32[]{:S(2)}, u32[]{:S(2)}) collective-permute-start(bf16[96,768]{1,0:T(8,128)(2,1)S(1)} %get-tuple-element.184), channel_id=1, source_target_pairs={{0,8},{1,5},{2,10},{3,7},{4,12},{5,1},{6,14},{7,3},{8,0},{9,13},{1... | collective-permute-start | bytes 442376 | tf_op jit(solution)/shard_map/ppermute | solution.py:694
  52.6 7.2 %collective-permute-start.20 = (bf16[192,768]{1,0:T(8,128)(2,1)S(1)}, bf16[192,768]{1,0:T(8,128)(2,1)S(1)}, u32[]{:S(2)}, u32[]{:S(2)}) collective-permute-start(bf16[192,768]{1,0:T(8,128)(2,1)S(1)} %get-tuple-element.192), channel_id=1, source_target_pairs={{0,4},{1,9},{2,6},{3,11},{4,0},{5,13},{6,2},{7,15},{8,12},{9,1},{1... | collective-permute-start | bytes 884744 | tf_op jit(solution)/shard_map/ppermute | solution.py:694
  55.6 9.6 %collective-permute-start.19 = (bf16[96,768]{1,0:T(8,128)(2,1)S(1)}, bf16[96,768]{1,0:T(8,128)(2,1)S(1)}, u32[]{:S(2)}, u32[]{:S(2)}) collective-permute-start(bf16[96,768]{1,0:T(8,128)(2,1)S(1)} %get-tuple-element.189.refs_0_), channel_id=1, source_target_pairs={{0,16},{1,17},{2,18},{3,19},{4,20},{5,21},{6,22},{7,23},{8,24},{9,... | collective-permute-start | bytes 442376 | tf_op jit(solution)/shard_map/ppermute | solution.py:694
  58.2 9.6 %collective-permute-start.23 = (bf16[192,768]{1,0:T(8,128)(2,1)S(1)}, bf16[192,768]{1,0:T(8,128)(2,1)S(1)}, u32[]{:S(2)}, u32[]{:S(2)}) collective-permute-start(bf16[192,768]{1,0:T(8,128)(2,1)S(1)} %get-tuple-element.200), channel_id=1, source_target_pairs={{0,4},{1,9},{2,6},{3,11},{4,0},{5,13},{6,2},{7,15},{8,12},{9,1},{1... | collective-permute-start | bytes 884744 | tf_op jit(solution)/shard_map/ppermute | solution.py:694
  60.4 7.8 %collective-permute-start.24 = (bf16[192,768]{1,0:T(8,128)(2,1)S(1)}, bf16[192,768]{1,0:T(8,128)(2,1)S(1)}, u32[]{:S(2)}, u32[]{:S(2)}) collective-permute-start(bf16[192,768]{1,0:T(8,128)(2,1)S(1)} %get-tuple-element.201), channel_id=1, source_target_pairs={{0,8},{1,5},{2,10},{3,7},{4,12},{5,1},{6,14},{7,3},{8,0},{9,13},{1... | collective-permute-start | bytes 884744 | tf_op jit(solution)/shard_map/ppermute | solution.py:694
  63.5 12.6 %collective-permute-start.22 = (bf16[272,768]{1,0:T(8,128)(2,1)S(1)}, bf16[272,768]{1,0:T(8,128)(2,1)S(1)}, u32[]{:S(2)}, u32[]{:S(2)}) collective-permute-start(bf16[272,768]{1,0:T(8,128)(2,1)S(1)} %get-tuple-element.199.refs_0_), channel_id=1, source_target_pairs={{0,2},{1,3},{2,0},{3,1},{4,6},{5,7},{6,4},{7,5},{8,10},{9,11},{10,... | collective-permute-start | bytes 1253384 | tf_op jit(solution)/shard_map/ppermute | solution.py:686
  65.8 16.5 %collective-permute-start.21 = (bf16[256,768]{1,0:T(8,128)(2,1)S(1)}, bf16[256,768]{1,0:T(8,128)(2,1)S(1)}, u32[]{:S(2)}, u32[]{:S(2)}) collective-permute-start(bf16[256,768]{1,0:T(8,128)(2,1)S(1)} %get-tuple-element.198), channel_id=1, source_target_pairs={{0,2},{1,3},{2,0},{3,1},{4,6},{5,7},{6,4},{7,5},{8,10},{9,11},{10,... | collective-permute-start | bytes 1179656 | tf_op jit(solution)/shard_map/ppermute | solution.py:686
  67.2 6.3 %collective-permute-start.26 = (bf16[96,768]{1,0:T(8,128)(2,1)S(1)}, bf16[96,768]{1,0:T(8,128)(2,1)S(1)}, u32[]{:S(2)}, u32[]{:S(2)}) collective-permute-start(bf16[96,768]{1,0:T(8,128)(2,1)S(1)} %get-tuple-element.205.refs_1_), channel_id=1, source_target_pairs={{0,8},{1,5},{2,10},{3,7},{4,12},{5,1},{6,14},{7,3},{8,0},{9,13},{1... | collective-permute-start | bytes 442376 | tf_op jit(solution)/shard_map/ppermute | solution.py:694
  69.0 16.4 %collective-permute-start.29 = (bf16[192,768]{1,0:T(8,128)(2,1)S(1)}, bf16[192,768]{1,0:T(8,128)(2,1)S(1)}, u32[]{:S(2)}, u32[]{:S(2)}) collective-permute-start(bf16[192,768]{1,0:T(8,128)(2,1)S(1)} %get-tuple-element.212.refs_0_), channel_id=1, source_target_pairs={{0,16},{1,17},{2,18},{3,19},{4,20},{5,21},{6,22},{7,23},{8,24},{9,... | collective-permute-start | bytes 884744 | tf_op jit(solution)/shard_map/ppermute | solution.py:694
  72.1 5.1 %collective-permute-start.27 = (bf16[96,768]{1,0:T(8,128)(2,1)S(1)}, bf16[96,768]{1,0:T(8,128)(2,1)S(1)}, u32[]{:S(2)}, u32[]{:S(2)}) collective-permute-start(bf16[96,768]{1,0:T(8,128)(2,1)S(1)} %get-tuple-element.205.refs_1_), channel_id=1, source_target_pairs={{0,4},{1,9},{2,6},{3,11},{4,0},{5,13},{6,2},{7,15},{8,12},{9,1},{1... | collective-permute-start | bytes 442376 | tf_op jit(solution)/shard_map/ppermute | solution.py:694
  73.6 5.2 %collective-permute-start.28 = (bf16[96,768]{1,0:T(8,128)(2,1)S(1)}, bf16[96,768]{1,0:T(8,128)(2,1)S(1)}, u32[]{:S(2)}, u32[]{:S(2)}) collective-permute-start(bf16[96,768]{1,0:T(8,128)(2,1)S(1)} %collective-permute-done.26.refs_2_), channel_id=1, source_target_pairs={{0,4},{1,9},{2,6},{3,11},{4,0},{5,13},{6,2},{7,15},{8,12},{9,1},{1... | collective-permute-start | bytes 442376 | tf_op jit(solution)/shard_map/ppermute | solution.py:694
  76.1 4.3 %collective-permute-start.25 = (bf16[16,768]{1,0:T(8,128)(2,1)S(1)}, bf16[16,768]{1,0:T(8,128)(2,1)S(1)}, u32[]{:S(2)}, u32[]{:S(2)}) collective-permute-start(bf16[16,768]{1,0:T(8,128)(2,1)S(1)} %get-tuple-element.204.refs_0_), channel_id=1, source_target_pairs={{0,1},{1,0},{2,3},{3,2},{4,5},{5,4},{6,7},{7,6},{8,9},{9,8},{10,11... | collective-permute-start | bytes 73736 | tf_op jit(solution)/shard_map/ppermute | solution.py:683
  80.6 4.8 %collective-permute-start.30 = (bf16[16,768]{1,0:T(8,128)(2,1)S(1)}, bf16[16,768]{1,0:T(8,128)(2,1)S(1)}, u32[]{:S(2)}, u32[]{:S(2)}) collective-permute-start(bf16[16,768]{1,0:T(8,128)(2,1)S(1)} %get-tuple-element.213.refs_2_), channel_id=1, source_target_pairs={{0,16},{1,17},{2,18},{3,19},{4,20},{5,21},{6,22},{7,23},{8,24},{9,... | collective-permute-start | bytes 73736 | tf_op jit(solution)/shard_map/ppermute | solution.py:694
  85.5 7.1 %collective-permute-start.31 = (bf16[208,768]{1,0:T(8,128)(2,1)S(1)}, bf16[208,768]{1,0:T(8,128)(2,1)S(1)}, u32[]{:S(2)}, u32[]{:S(2)}) collective-permute-start(bf16[208,768]{1,0:T(8,128)(2,1)S(1)} %get-tuple-element.217.refs_0_), channel_id=1, source_target_pairs={{0,8},{1,5},{2,10},{3,7},{4,12},{5,1},{6,14},{7,3},{8,0},{9,13},{1... | collective-permute-start | bytes 958472 | tf_op jit(solution)/shard_map/ppermute | solution.py:694
  92.6 7.1 %collective-permute-start.32 = (bf16[208,768]{1,0:T(8,128)(2,1)S(1)}, bf16[208,768]{1,0:T(8,128)(2,1)S(1)}, u32[]{:S(2)}, u32[]{:S(2)}) collective-permute-start(bf16[208,768]{1,0:T(8,128)(2,1)S(1)} %get-tuple-element.219.refs_1_), channel_id=1, source_target_pairs={{0,4},{1,9},{2,6},{3,11},{4,0},{5,13},{6,2},{7,15},{8,12},{9,1},{1... | collective-permute-start | bytes 958472 | tf_op jit(solution)/shard_map/ppermute | solution.py:694
  94.2 8.9 %collective-permute-start.33 = (bf16[208,768]{1,0:T(8,128)(2,1)S(1)}, bf16[208,768]{1,0:T(8,128)(2,1)S(1)}, u32[]{:S(2)}, u32[]{:S(2)}) collective-permute-start(bf16[208,768]{1,0:T(8,128)(2,1)S(1)} %get-tuple-element.220.refs_2_), channel_id=1, source_target_pairs={{0,4},{1,9},{2,6},{3,11},{4,0},{5,13},{6,2},{7,15},{8,12},{9,1},{1... | collective-permute-start | bytes 958472 | tf_op jit(solution)/shard_map/ppermute | solution.py:694

commit v8 on v7

--- a/solution.py
+++ b/solution.py
@@ -71,7 +71,7 @@
     return jnp.concatenate([both[:HEAD_DIM, :LEN], both[HEAD_DIM:, LEN:]], axis=0)
 
 
-COSTS = (0, 0, 100, 0, 0, 0, 0, 0, 0, 100, 0, 0, 0, 0, 150, 0, 60, 0, 0, 30, 0, 0, 0, 0, 0, 0, 0, 0, 0, 0, 0, 0)
+COSTS = (0, 0, 100, 0, 0, 30, 30, 0, 0, 0, 0, 100, 0, 0, 0, 200, 0, 60, 0, 0, 30, 0, 0, 0, 0, 0, 0, 0, 0, 0, 0, 0)
 
 
 class IO:
@@ -241,7 +241,7 @@
     args = (bits, nodes, edges, x, gain, bias)
     if g is None:
         return chain.call(
-            kernel, "attention_forward", (*args, w, *near), [*outs, bf16(rows, width), bf16(2 * width, d), bf16(2 * width, d), bf16(width, d)],
+            kernel, "attention_forward", (*args, w, *near), [*outs, bf16(rows, width), bf16(2 * width, d), bf16(2 * width, d), bf16(2 * width, d)],
             "sccvvvvvv-vvvvvvvvvv", scratch=[pltpu.SemaphoreType.DMA((6,))],
         )
     return chain.call(
@@ -250,25 +250,51 @@
     )
 
 
-def pick(chain, bits, a, b):
-    half = a.shape[0] // 2
-
-    def kernel(io, bits_ref, a_ref, b_ref, out_ref, sems):
+def pick(chain, bits, wo, fc1, fc2, bias):
+    shard, d = wo.shape
+    rows = 3 * shard // 4
+
+    def kernel(io, bits_ref, wo_ref, fc1_ref, fc2_ref, bias_ref, out_ref, sems):
+        refs = (wo_ref, fc1_ref, fc2_ref)
+        out_ref[rows:] = jnp.concatenate(
+            [jnp.broadcast_to(bias_ref[...].astype(F32)[None, :], (16, shard)), jnp.zeros((16, d - shard), F32)], axis=1
+        ).astype(BF16)
+
+        def part(quarter):
+            pairs = []
+            for c, first, at, n in quarter_rows(quarter, shard):
+                pairs.append((refs[c].at[first : first + n], out_ref.at[at : at + n]))
+            finish(copies(sems, pairs))
+
         which = 2 * bits_ref[2] + bits_ref[6]
-        for at, ref in enumerate((a_ref.at[:half], a_ref.at[half:], b_ref.at[:half], b_ref.at[half:])):
-            pl.when(which == at)(lambda ref=ref: finish(copies(sems, [(ref, out_ref)])))
-
-    return chain.call(
-        kernel, "pick", (bits, a, b), [bf16(half, a.shape[1])], "spp-v", limit=4,
-        scratch=[pltpu.SemaphoreType.DMA((1,))],
+        for at in range(4):
+            pl.when(which == at)(functools.partial(part, at))
+
+    return chain.call(
+        kernel, "pick", (bits, wo, fc1, fc2, bias), [bf16(rows + 16, d)], "spppv-v", limit=4,
+        scratch=[pltpu.SemaphoreType.DMA((2,))],
     )[0]
 
 
+def quarter_rows(quarter, shard):
+    size = 3 * shard // 4
+    found, at = [], 0
+    while at < size:
+        which, first = divmod(quarter * size + at, shard)
+        n = min(size - at, shard - first)
+        found.append((which, first, at, n))
+        at += n
+    return found
+
+
 def hold(chain, a):
-    def kernel(io, a_ref, out_ref):
+    rows, d = a.shape
+
+    def kernel(io, a_ref, out_ref, short_ref):
         out_ref[...] = a_ref[...]
-
-    return chain.call(kernel, "hold", (a,), [bf16(*a.shape)], "v-v", limit=4)[0]
+        short_ref[...] = a_ref[: rows - 16]
+
+    return chain.call(kernel, "hold", (a,), [bf16(rows, d), bf16(rows - 16, d)], "v-vv", limit=4)
 
 
 def pair_up(chain, a, b):
@@ -280,6 +306,13 @@
     return chain.call(kernel, "pair_up", (a, b), [bf16(*b.shape), bf16(2, *a.shape)], "vv-vv", limit=4)
 
 
+def spacer(chain):
+    def kernel(io):
+        pass
+
+    chain.call(kernel, "spacer", (), [], "-", limit=2)
+
+
 def load(chain, out_weight, fc1_weight, fc2_weight, bias, others):
     shard, d = out_weight.shape
     n = len(others)
@@ -298,15 +331,13 @@
     return near, others
 
 
-def feed_body(x, oa, ob, g, wo_ref, gain_ref, bias_ref, fc1_ref, b1, fc2_ref, h_ref, a2_ref, z_ref, du_ref):
+def feed_body(x, oa, ob, g, wo_ref, gain_ref, bias_ref, fc1_ref, b1_ref, fc2_ref, h_ref, a2_ref, z_ref, du_ref):
     h = x.astype(F32) + dot_nn(jnp.concatenate([oa, ob], axis=1), wo_ref[...])
     h_ref[...] = h
     xh, _ = normalise(h)
     a2 = (xh * gain_ref[...][None, :] + bias_ref[...][None, :]).astype(BF16)
     a2_ref[...] = a2
-    shard = fc2_ref.shape[0] // 2
-    b1 = jnp.concatenate([b[3 * shard : 3 * shard + 1, :shard] for b in b1], axis=1).astype(F32)
-    u = dot_nt(a2, fc1_ref[: 2 * shard]) + b1
+    u = dot_nt(a2, fc1_ref[...]) + b1_ref[...]
     dz = dot_nt(g, fc2_ref[...])
     phi = 0.5 * (1.0 + lax.erf(u * (0.5**0.5)))
     slope = phi + u * (jnp.exp(-0.5 * u * u) * 0.3989422804014327)
@@ -317,94 +348,94 @@
     return a2, z, du
 
 
-def pack_far(chain, bits, wo, fc1, fars):
-    half, d = fars[0].shape
-    shard = 2 * half
-    width = 2 * shard
-
-    def kernel(io, bits_ref, wo_in, fc1_in, y0, pair0, xz0, y1, pair1, xz1, wo_ref, fc1_ref):
+def pack_far(chain, bits, weights, fars):
+    rows, d = weights[0].shape
+    shard = rows // 4
+
+    def kernel(io, bits_ref, wo_in, fc1_in, fc2_in, y0, pair0, xz0, y1, pair1, xz1, *outs):
         def placed_at(which):
             for at, (y, pair, xz) in enumerate(((y0, pair0, xz0), (y1, pair1, xz1))):
-                for turn, part in enumerate((y[...], pair[1], pair[0], xz[...])):
-                    quarter = which ^ turn
-                    row = width + at * shard + quarter % 2 * half
-                    (wo_ref, fc1_ref)[quarter // 2][row : row + half] = part
+                for turn, ref in enumerate((y, pair.at[1], pair.at[0], xz)):
+                    for c, first, start, n in quarter_rows(which ^ turn, shard):
+                        row = (2 + at) * shard + first
+                        outs[c][row : row + n] = ref[start : start + n]
 
         which = 2 * bits_ref[2] + bits_ref[6]
         for at in range(4):
             pl.when(which == at)(functools.partial(placed_at, at))
 
     return chain.call(
-        kernel, "pack_far", (bits, wo, fc1, *fars), [bf16(2 * width, d), bf16(2 * width, d)], "svvvvvvvv-vv", limit=4,
-        aliases={1: 0, 2: 1},
-    )
-
-
-def feed_far(chain, x, oa, packet, gain, bias, fc1, fc2, wo, near):
+        kernel, "pack_far", (bits, *weights, *fars), [bf16(rows, d)] * 3, "s" + "v" * 9 + "-vvv", limit=4,
+        aliases={1: 0, 2: 1, 3: 2},
+    )
+
+
+def feed_far(chain, x, oa, packet, gain, bias, wo, fc1, fc2, biases):
     rows, d = x.shape
-    width = fc2.shape[0]
-
-    def kernel(io, x_ref, oa_ref, packet_ref, gain_ref, bias_ref, fc1_ref, fc2_ref, wo_ref, b10, b11, *outs):
+    columns = fc1.shape[0]
+    shard = columns // 4
+
+    def kernel(io, x_ref, oa_ref, packet_ref, gain_ref, bias_ref, wo_ref, fc1_ref, fc2_ref, *refs):
+        b_refs, (h_ref, a2_ref, z_ref, du_ref, b1_ref) = refs[:4], refs[4:]
+        parts = [ref[row : row + 1, :shard].astype(F32) for ref, (_, row) in zip(b_refs, biases)]
+        b1_ref[...] = jnp.concatenate(parts, axis=1)
         feed_body(
-            x_ref[...], oa_ref[...], packet_ref[:, d:], packet_ref[:, :d], wo_ref, gain_ref, bias_ref, fc1_ref,
-            (b10, b11), fc2_ref, *outs,
-        )
-
-    return chain.call(
-        kernel, "feed_far", (x, oa, packet, gain, bias, fc1, fc2, wo, *near),
-        [f32(rows, d), bf16(rows, d), bf16(rows, width), bf16(rows, width)], "v" * 10 + "-vvvv",
-    )
-
-
-def feed_own(chain, x, packet, g, ob, gain, bias, fc1, fc2, wo, near, far):
-    rows, d = x.shape
-    width = fc2.shape[0]
-    shard = width // 2
-
-    def kernel(io, x_ref, oa_ref, g_ref, ob_ref, gain_ref, bias_ref, fc1_ref, fc2_ref, wo_ref, b10, b11,
-               z1, du1, a1, g1, h_ref, a2_ref, z_ref, du_ref, keep_ref, send_ref, sums_ref):
-        a2, z, du = feed_body(
-            x_ref[...], oa_ref[:, d:], ob_ref[...], g_ref[...], wo_ref, gain_ref, bias_ref, fc1_ref, (b10, b11),
+            x_ref[...], oa_ref[...], packet_ref[:, d:], packet_ref[:, :d], wo_ref, gain_ref, bias_ref, fc1_ref, b1_ref,
             fc2_ref, h_ref, a2_ref, z_ref, du_ref,
         )
-        first = dot_tn(du, a2) + dot_tn(du1[...], a1[...])
-        second = dot_tn(z, g_ref[...]) + dot_tn(z1[...], g1[:, :d])
+
+    return chain.call(
+        kernel, "feed_far", (x, oa, packet, gain, bias, wo, fc1, fc2, *(a for a, _ in biases)),
+        [f32(rows, d), bf16(rows, d), bf16(rows, columns), bf16(rows, columns), f32(1, columns)], "v" * 12 + "-vvvvv",
+    )
+
+
+def feed_own(chain, x, packet, g, ob, gain, bias, wo, fc1, b1, fc2, far):
+    rows, d = x.shape
+    columns = fc1.shape[0]
+    width = columns // 2
+    shard = width // 2
+
+    def kernel(io, x_ref, oa_ref, g_ref, ob_ref, gain_ref, bias_ref, wo_ref, fc1_ref, b1_ref, fc2_ref, z1, du1, a1, g1,
+               h_ref, a2_ref, z_ref, du_ref, keep_ref, send_ref, sums_ref):
+        a2, z, du = feed_body(
+            x_ref[...], oa_ref[:, d:], ob_ref[...], g_ref[...], wo_ref, gain_ref, bias_ref, fc1_ref, b1_ref, fc2_ref,
+            h_ref, a2_ref, z_ref, du_ref,
+        )
+        z, du = z[:, :width], du[:, :width]
+        first = dot_tn(du, a2) + dot_tn(du1[:, :width], a1[...])
+        second = dot_tn(z, g_ref[...]) + dot_tn(z1[:, :width], g1[:, :d])
         for at, ref in enumerate((keep_ref, send_ref)):
             here = slice(at * shard, (at + 1) * shard)
             ref[0] = first[here].astype(BF16)
             ref[1] = second[here].astype(BF16)
         sums_ref[...] = jnp.sum(du.astype(F32), axis=0, keepdims=True) + jnp.sum(
-            du1[...].astype(F32), axis=0, keepdims=True
+            du1[:, :width].astype(F32), axis=0, keepdims=True
         )
 
     return chain.call(
-        kernel, "feed_own", (x, packet, g, ob, gain, bias, fc1, fc2, wo, *near, *far),
-        [f32(rows, d), bf16(rows, d), bf16(rows, width), bf16(rows, width), bf16(2, shard, d), bf16(2, shard, d),
-         f32(1, width)], "v" * 15 + "-vvvvvvv",
-    )
-
-
-def feed_result(chain, zs, fc2, h):
-    rows, d = h.shape
-
-    def kernel(io, z0, z1, fc2_ref, h_ref, mine_ref, theirs_ref):
-        theirs_ref[...] = dot_nn(z1[...], fc2_ref[...]).astype(BF16)
-        mine_ref[...] = h_ref[...] + dot_nn(z0[...], fc2_ref[...])
-
-    return chain.call(
-        kernel, "feed_result", (*zs, fc2, h), [f32(rows, d), bf16(rows, d)], "vvvv-vv", limit=8,
-    )
+        kernel, "feed_own", (x, packet, g, ob, gain, bias, wo, fc1, b1, fc2, *far),
+        [f32(rows, d), bf16(rows, d), bf16(rows, columns), bf16(rows, columns), bf16(2, shard, d), bf16(2, shard, d),
+         f32(1, width)], "v" * 14 + "-vvvvvvv",
+    )
+
+
+def feed_result(chain, z, fc2, h):
+    def kernel(io, z_ref, fc2_ref, h_ref, out_ref):
+        out_ref[...] = (h_ref[...] + dot_nn(z_ref[...], fc2_ref[...])).astype(BF16)
+
+    return chain.call(kernel, "feed_result", (z, fc2, h), [bf16(*h.shape)], "vvv-w", limit=8)[0]
 
 
 def backward(chain, args, own):
-    h, kt = args[3], args[9]
+    h, kt = args[2], args[8]
     rows, d = h.shape
     width = kt.shape[0]
     mols, pairs = rows // LEN, width // PAIR
 
-    def kernel(io, du_ref, dr_ref, fc1_ref, h_ref, g_ref, gain_ref, wo_ref, p_ref, qt_ref, kt_ref, v_ref,
+    def kernel(io, du_ref, fc1_ref, h_ref, g_ref, gain_ref, wo_ref, p_ref, qt_ref, kt_ref, v_ref,
                gh_ref, dp_ref, dh_ref=None, sums_ref=None):
-        da2 = dot_nn(jnp.concatenate([du_ref[...], dr_ref[...]], axis=1), fc1_ref[...])
+        da2 = dot_nn(du_ref[...], fc1_ref[...])
         xh, r = normalise(h_ref[...])
         dh = g_ref[:, :d].astype(F32) + norm_back(da2, gain_ref[...][None, :], xh, r)
         if own:
@@ -438,7 +469,7 @@
 
     outs = [bf16(rows, d), bf16(3 * width, rows)] + ([f32(rows, d), f32(8, d)] if own else [])
     return chain.call(
-        kernel, "attention_backward", args, outs, "v" * 11 + ("-vvvv" if own else "-vv"),
+        kernel, "attention_backward", args, outs, "v" * 10 + ("-vvvv" if own else "-vv"),
     )
 
 
@@ -497,13 +528,6 @@
     return chain.call(
         kernel, "input_norm", (x, gain, mine, got, dh), [bf16(rows, d)], "vvvvv-w", limit=8
     )[0]
-
-
-def add_result(chain, mine, got):
-    def kernel(io, mine_ref, got_ref, out_ref):
-        out_ref[...] = (mine_ref[...] + got_ref[...].astype(F32)).astype(BF16)
-
-    return chain.call(kernel, "add_result", (mine, got), [bf16(*mine.shape)], "vv-w", limit=8)[0]
 
 
 def plus(*terms):
@@ -699,7 +723,7 @@
 
     w_got = swap_core(qkv_weight)
     x_got = swap_y(tokens)
-    far_y = swap_y(pick(chain, bits, out_weight, fc1_weight))
+    far_y = swap_y(pick(chain, bits, out_weight, fc1_weight, fc2_weight, fc1_bias))
     bias = jnp.pad(fc1_bias.reshape(1, -1), ((0, 15), (0, d - shard)))
     near, others = load(
         chain, out_weight, fc1_weight, fc2_weight, bias,
@@ -714,24 +738,21 @@
         chain, bits, 3, *counts, tokens, *norm1, (qkv_weight, w_got), out_grad
     )
     packet_got = swap_y(packet)
-    far_y = hold(chain, far_y)
-    far_x, far_z = swap_dp(far_y, 1, 1), swap_dp(far_y, 2, 2)
+    far_y, short = hold(chain, far_y)
+    far_x, far_z = swap_dp(short, 1, 1), swap_dp(short, 2, 2)
+    far_z, pair = pair_up(chain, far_x, far_z)
+    far_xz = swap_dp(far_z, 1, 1)
     a1_1, qt_1, kt_1, v_1, p_1, ot_1, o_1, wo, fc1, fc2 = attention(
         chain, bits, 4, *counts, x_got, *norm1, w_qkv, near=near
     )
     o_got = swap_y(o_1)
-    far_z, pair = pair_up(chain, far_x, far_z)
-    far_xz = swap_dp(far_z, 1, 1)
+    spacer(chain)
     fars = (far_y, pair, far_xz)
     fars += tuple(swap_core(a) for a in fars)
     norm2 = (ln2_gain, ln2_bias)
-    wo, fc1 = pack_far(chain, bits, wo, fc1, fars)
-    h_1, a2_1, z_1, du_1 = feed_far(chain, x_got, o_1, packet_got, *norm2, fc1, fc2, wo, near)
-    dr_0 = swap_y(du_1)
-    h_0, a2_0, z_0, du_0, keep_r, send_r, bias_sums = feed_own(
-        chain, tokens, packet, out_grad, o_got, *norm2, fc1, fc2, wo, near, (z_1, du_1, a2_1, packet_got)
-    )
-    dr_1 = swap_y(du_0)
+    wo, fc1, fc2 = pack_far(chain, bits, (wo, fc1, fc2), fars)
+    low, far_low = 3 * shard, 3 * shard // 4
+    biases = ((near[0], low), (near[1], low), (fars[0], far_low), (fars[3], far_low))
 
     class Sum:
         def __init__(self, count, keep, got, apart, early):
@@ -781,14 +802,14 @@
                 a, b = side_by_side(chain, *self.last, True)
                 self.quarters = [(a, 0, 0, 0), (b, 0, 0, 1), (swap_first(a), 0, 1, 0), (swap_first(b), 0, 1, 1)]
 
-    gh_0, dp_0, dh, sums = backward(
-        chain, (du_0, dr_0, fc1, h_0, out_grad, ln2_gain, wo, p_0, qt_0, kt_0, v_0), True
-    )
+    h_1, a2_1, z_1, du_1, b1 = feed_far(chain, x_got, o_1, packet_got, *norm2, wo, fc1, fc2, biases)
+    gh_1, dp_1 = backward(chain, (du_1, fc1, h_1, packet_got, ln2_gain, wo, p_1, qt_1, kt_1, v_1), False)
+    h_0, a2_0, z_0, du_0, keep_r, send_r, bias_sums = feed_own(
+        chain, tokens, packet, out_grad, o_got, *norm2, wo, fc1, b1, fc2, (z_1, du_1, a2_1, packet_got)
+    )
+    gh_0, dp_0, dh, sums = backward(chain, (du_0, fc1, h_0, out_grad, ln2_gain, wo, p_0, qt_0, kt_0, v_0), True)
     r = Sum(2, keep_r, swap_core(send_r), True, 1)
     r.first()
-    gh_1, dp_1 = backward(
-        chain, (du_1, dr_1, fc1, h_1, packet_got, ln2_gain, wo, p_1, qt_1, kt_1, v_1), False
-    )
     a1s = (a1_0, a1_1)
     lefts = [(dp_0, dp_1, c * width) for c in range(3)] + [(ot_0, ot_1, 0)]
     rights = [a1s] * 3 + [(gh_0, gh_1)]
@@ -801,8 +822,7 @@
     da1_mine, da1_theirs = input_grads(chain, (dp_0, dp_1), w_qkv, (tokens, x_got), sums, bias_sums)
     da1_got = swap_y(da1_theirs)
     r.fourth()
-    res_mine, res_theirs = feed_result(chain, (z_0, z_1), fc2, h_0)
-    res_got = swap_y(res_theirs)
+    result = feed_result(chain, z_0, fc2, h_0)
     q.third()
     vec = vector_rows(chain, da1_theirs, da1_got)
     vec_got = swap_core(vec)
@@ -811,7 +831,6 @@
     grad_fc1, grad_fc2 = place_sums(chain, bits, r.quarters, r.size, halves, [f32(shard, d)] * 2)
     vec = vector_cores(chain, vec, vec_got, shard)
     vec_got = swap_dp(vec, far_masks[0], far_masks[0])
-    result = add_result(chain, res_mine, res_got)
     q.fourth((vec, vec_got))
     grad_tokens = input_norm(chain, tokens, ln1_gain, da1_mine, da1_got, dh)
     q.fifth()

time: 105 us -> 105 us (level)
  starting transfers between devices: 40.1 us -> 34.2 us
  waiting for transfers between devices: 26.4 us -> 31.1 us
    ppermute x18, waiting for transfers between devices: 19.4 us -> 26.2 us  [swap_dp(): return lax.ppermute(a, ('dp', 'tensor'), pairs)]
    ppermute x8 -> x5, starting transfers between devices: 12.7 us -> 7.43 us  [swap_y(): return lax.ppermute(a, 'tensor', [(t, t ^ 2) for t in range(n_tensor)])]
    ppermute x8 -> x5, waiting for transfers between devices: 6.44 us -> 3.47 us  [swap_y(): return lax.ppermute(a, 'tensor', [(t, t ^ 2) for t in range(n_tensor)])]
  transfers between devices with their start and end apart: 34 -> 31, of which waited for: 16 -> 16; matrix products, arithmetic and copies ran while one was open for 1% -> 1% of each run, Pallas kernels for 33% -> 30%
where the time goes in v8:
time: 105 us
  Pallas kernels  36.8 us (35%)
  starting transfers between devices  34.2 us (33%)
  waiting for transfers between devices  31.1 us (30%)
  local copies, waits for them, and re-layouts  1.41 us (1%)
  between operations  1.12 us (1%)
    pallas_call x32, Pallas kernels, call(): pl.pallas_call(body, in_specs=[spec(kind) for kind in ins] + [vmem] * len...  36.8 us
    ppermute x18, waiting for transfers between devices, swap_dp(): return lax.ppermute(a, ('dp', 'tensor'), pairs)  26.2 us
    ppermute x18, starting transfers between devices, swap_dp(): return lax.ppermute(a, ('dp', 'tensor'), pairs)  25.3 us
    ppermute x5, starting transfers between devices, swap_y(): return lax.ppermute(a, 'tensor', [(t, t ^ 2) for t in range(n_tensor)])  7.43 us
    ppermute x5, waiting for transfers between devices, swap_y(): return lax.ppermute(a, 'tensor', [(t, t ^ 2) for t in range(n_tensor)])  3.47 us
  transfers between devices with their start and end apart: 31, of which 16 were waited for; matrix products, arithmetic and copies ran while one was open for 1% of the time, Pallas kernels for 30%

profile of v8, /device:TPU:0, one launch (start us, length us, event | category | flops | bytes accessed | tf_op | source)
XLA Modules:
  0.0 104.7 jit_solution(2817386549315309990)
XLA Ops:
  1.9 1.5 %pick.1 = (bf16[160,768]{1,0:T(8,128)(2,1)S(1)}, f32[8,128]{1,0:T(8,128)S(1)}) custom-call(s32[7]{0:T(128)S(1)} %stack.31.refs_0_, bf16[192,768]{1,0:T(8,128)(2,1)} %refs_0_.1, bf16[192,768]{1,0:T(8,128)(2,1)} %refs_1_.5, bf16[192,768]{1,0:T(8,128)(2,1)} %refs_2_.5, bf16[192]{0:T(256)(128)(2,1)S(1)} %copy-done), custom_call_target="tpu_custom_call" | custom-call | bytes 100000000 | tf_op jit(solution)/shard_map/pick/pallas_call | solution.py:144
  3.4 2.6 %collective-permute-start.3 = (bf16[160,768]{1,0:T(8,128)(2,1)S(1)}, bf16[160,768]{1,0:T(8,128)(2,1)S(1)}, u32[]{:S(2)}, u32[]{:S(2)}) collective-permute-start(bf16[160,768]{1,0:T(8,128)(2,1)S(1)} %get-tuple-element.133), channel_id=1, source_target_pairs={{0,2},{1,3},{2,0},{3,1},{4,6},{5,7},{6,4},{7,5},{8,10},{9,11},{10,... | collective-permute-start | bytes 737288 | tf_op jit(solution)/shard_map/ppermute | solution.py:710
  6.8 1.5 %load.1 = (bf16[592,768]{1,0:T(8,128)(2,1)S(1)}, bf16[256,768]{1,0:T(8,128)(2,1)S(1)}, bf16[256,768]{1,0:T(8,128)(2,1)S(1)}, f32[768]{0:T(1024)S(1)}, f32[768]{0...) custom-call(bf16[192,768]{1,0:T(8,128)(2,1)} %refs_0_.1, bf16[192,768]{1,0:T(8,128)(2,1)} %refs_1_.5, ...), custom_call_target="tpu_custom_call" | custom-call | bytes 100000000 | tf_op jit(solution)/shard_map/load/pallas_call | solution.py:144
  8.6 4.0 %attention_forward.2 = (bf16[256,768]{1,0:T(8,128)(2,1)S(1)}, bf16[384,256]{1,0:T(8,128)(2,1)S(1)}, bf16[384,256]{1,0:T(8,128)(2,1)S(1)}, bf16[256,384]{1,0:T(8,...) custom-call(s32[7]{0:T(128)S(1)} %stack.31.refs_0_, ...), custom_call_target="tpu_custom_call" | custom-call | flops 10000000000 | bytes 100000000 | tf_op jit(solution)/shard_map/attention_forward/pallas_call | solution.py:144
  12.9 2.0 %collective-permute-start.4 = (bf16[144,768]{1,0:T(8,128)(2,1)S(1)}, bf16[144,768]{1,0:T(8,128)(2,1)S(1)}, u32[]{:S(2)}, u32[]{:S(2)}) collective-permute-start(bf16[144,768]{1,0:T(8,128)(2,1)S(1)} %get-tuple-element.135), channel_id=1, source_target_pairs={{0,4},{1,5},{2,6},{3,7},{4,0},{5,1},{6,2},{7,3},{8,12},{9,13},{10,... | collective-permute-start | bytes 663560 | tf_op jit(solution)/shard_map/ppermute | solution.py:718
  14.9 1.6 %collective-permute-start.5 = (bf16[144,768]{1,0:T(8,128)(2,1)S(1)}, bf16[144,768]{1,0:T(8,128)(2,1)S(1)}, u32[]{:S(2)}, u32[]{:S(2)}) collective-permute-start(bf16[144,768]{1,0:T(8,128)(2,1)S(1)} %get-tuple-element.135), channel_id=1, source_target_pairs={{0,8},{1,9},{2,10},{3,11},{4,12},{5,13},{6,14},{7,15},{8,0},{9,1},... | collective-permute-start | bytes 663560 | tf_op jit(solution)/shard_map/ppermute | solution.py:718
  16.5 1.5 %collective-permute-start.11 = (bf16[256,1152]{1,0:T(8,128)(2,1)S(1)}, bf16[256,1152]{1,0:T(8,128)(2,1)S(1)}, u32[]{:S(2)}, u32[]{:S(2)}) collective-permute-start(bf16[256,1152]{1,0:T(8,128)(2,1)S(1)} %get-tuple-element.130.refs_1_), channel_id=1, source_target_pairs={{0,2},{1,3},{2,0},{3,1},{4,6},{5,7},{6,4},{7,5},{8,10},{9,11},{10,... | collective-permute-start | bytes 1769480 | tf_op jit(solution)/shard_map/ppermute | solution.py:710
  18.0 2.6 %collective-permute-done.4.refs_0_ = bf16[144,768]{1,0:T(8,128)(2,1)S(1)} collective-permute-done((bf16[144,768]{1,0:T(8,128)(2,1)S(1)}, bf16[144,768]{1,0:T(8,128)(2,1)S(1)}, u32[]{:S(2)}, u32[]{:S(2)}) %collective-permute-start.4) | collective-permute-done | bytes 221216 | tf_op jit(solution)/shard_map/ppermute | solution.py:718
  20.6 1.5 %collective-permute-done.5.refs_1_ = bf16[144,768]{1,0:T(8,128)(2,1)S(1)} collective-permute-done((bf16[144,768]{1,0:T(8,128)(2,1)S(1)}, bf16[144,768]{1,0:T(8,128)(2,1)S(1)}, u32[]{:S(2)}, u32[]{:S(2)}) %collective-permute-start.5) | collective-permute-done | bytes 221216 | tf_op jit(solution)/shard_map/ppermute | solution.py:718
  22.7 3.5 %attention_forward.3 = (bf16[256,768]{1,0:T(8,128)(2,1)S(1)}, bf16[384,256]{1,0:T(8,128)(2,1)S(1)}, bf16[384,256]{1,0:T(8,128)(2,1)S(1)}, bf16[256,384]{1,0:T(8,...) custom-call(s32[7]{0:T(128)S(1)} %stack.31.refs_0_, ...), custom_call_target="tpu_custom_call" | custom-call | flops 3000000000 | bytes 100000000 | tf_op jit(solution)/shard_map/attention_forward/pallas_call | solution.py:144
  26.2 1.6 %collective-permute-start.6 = (bf16[256,384]{1,0:T(8,128)(2,1)S(1)}, bf16[256,384]{1,0:T(8,128)(2,1)S(1)}, u32[]{:S(2)}, u32[]{:S(2)}) collective-permute-start(bf16[256,384]{1,0:T(8,128)(2,1)S(1)} %get-tuple-element.138.refs_1_), channel_id=1, source_target_pairs={{0,2},{1,3},{2,0},{3,1},{4,6},{5,7},{6,4},{7,5},{8,10},{9,11},{10,... | collective-permute-start | bytes 589832 | tf_op jit(solution)/shard_map/ppermute | solution.py:710
  28.6 1.4 %collective-permute-done.10.refs_9_ = bf16[144,768]{1,0:T(8,128)(2,1)S(1)} collective-permute-done((bf16[144,768]{1,0:T(8,128)(2,1)S(1)}, bf16[144,768]{1,0:T(8,128)(2,1)S(1)}, u32[]{:S(2)}, u32[]{:S(2)}) %collective-permute-start.10) | collective-permute-done | bytes 221216 | tf_op jit(solution)/shard_map/ppermute | solution.py:707
  30.1 0.9 pack_far.1
  30.9 3.0 %collective-permute-done.11.refs_2_.refs_3_.refs_13_ = bf16[256,1152]{1,0:T(8,128)(2,1)S(1)} collective-permute-done((bf16[256,1152]{1,0:T(8,128)(2,1)S(1)}, bf16[256,1152]{1,0:T(8,128)(2,1)S(1)}, u32[]{:S(2)}, u32[]{:S(2)}) %collective-permute-start.11) | collective-permute-done | bytes 589856 | tf_op jit(solution)/shard_map/ppermute | solution.py:710
  33.9 1.5 %feed_far.1 = (f32[256,768]{1,0:T(8,128)S(1)}, bf16[256,768]{1,0:T(8,128)(2,1)S(1)}, bf16[256,768]{1,0:T(8,128)(2,1)S(1)}, bf16[256,768]{1,0:T(8,128)(2,1)S(1)},...) custom-call(bf16[256,768]{1,0:T(8,128)(2,1)S(1)} %collective-permute-done.1.refs_3_.refs_0_.refs_4_, ...), custom_call_target="tpu_custom_call" | custom-call | bytes 100000000 | tf_op jit(solution)/shard_map/feed_far/pallas_call | solution.py:144
  35.4 2.4 %attention_backward.2 = (bf16[256,768]{1,0:T(8,128)(2,1)S(1)}, bf16[1152,256]{1,0:T(8,128)(2,1)S(1)}, f32[8,128]{1,0:T(8,128)S(1)}) custom-call(bf16[256,768]{1,0:T(8,128)(2,1)S(1)} %get-tuple-element.154.refs_0_.refs_11_, bf16[768,768]{1,0:T(8,128)(2,1)S(1)} %get-tuple-element.149.refs_6_.refs_1_.refs_7_, f32[256,768]{1,0:T(8,128)S(1)} %get-tuple-element.156.refs_2_, ...), custom_call_target="tpu_custom_call" | custom-call | bytes 100000000 | tf_op jit(solution)/shard_map/attention_backward/pallas_call | solution.py:144
  37.9 2.5 %feed_own.1 = (f32[256,768]{1,0:T(8,128)S(1)}, bf16[256,768]{1,0:T(8,128)(2,1)}, bf16[256,768]{1,0:T(8,128)(2,1)S(1)}, bf16[256,768]{1,0:T(8,128)(2,1)S(1)}, bf1...) custom-call(bf16[256,768]{1,0:T(8,128)(2,1)S(1)} %get-tuple-element., ...), custom_call_target="tpu_custom_call" | custom-call | bytes 100000000 | tf_op jit(solution)/shard_map/feed_own/pallas_call | solution.py:144
  40.5 2.5 %attention_backward.3 = (bf16[256,768]{1,0:T(8,128)(2,1)S(1)}, bf16[1152,256]{1,0:T(8,128)(2,1)S(1)}, f32[256,768]{1,0:T(8,128)S(1)}, f32[8,768]{1,0:T(8,128)S(1)}, f32[8,128]{1,0:T(8,128)S(1)}) custom-call(bf16[256,768]{1,0:T(8,128)(2,1)S(1)} %get-tuple-element.167.refs_0_, bf16[768,768]{1,0:T(8,128)(2,1)S(1)} %get-tuple-element.149.refs_6_.refs_1_.refs_7_, ...), custom_call_target="tpu_custom_call" | custom-call | flops 10000000000 | bytes 100000000 | tf_op jit(solution)/shard_map/attention_backward/pallas_call | solution.py:144
  43.5 2.0 %collective-permute-start.14 = (bf16[96,768]{1,0:T(8,128)(2,1)S(1)}, bf16[96,768]{1,0:T(8,128)(2,1)S(1)}, u32[]{:S(2)}, u32[]{:S(2)}) collective-permute-start(bf16[96,768]{1,0:T(8,128)(2,1)S(1)} %get-tuple-element.175), channel_id=1, source_target_pairs={{0,4},{1,9},{2,6},{3,11},{4,0},{5,13},{6,2},{7,15},{8,12},{9,1},{1... | collective-permute-start | bytes 442376 | tf_op jit(solution)/shard_map/ppermute | solution.py:718
  45.5 0.8 weight_grads.2
  46.3 0.8 weight_grads.3
  47.5 1.5 %collective-permute-start.13 = (bf16[96,768]{1,0:T(8,128)(2,1)S(1)}, bf16[96,768]{1,0:T(8,128)(2,1)S(1)}, u32[]{:S(2)}, u32[]{:S(2)}) collective-permute-start(bf16[96,768]{1,0:T(8,128)(2,1)S(1)} %get-tuple-element.174), channel_id=1, source_target_pairs={{0,4},{1,9},{2,6},{3,11},{4,0},{5,13},{6,2},{7,15},{8,12},{9,1},{1... | collective-permute-start | bytes 442376 | tf_op jit(solution)/shard_map/ppermute | solution.py:718
  49.6 1.8 %collective-permute-start.15 = (bf16[96,768]{1,0:T(8,128)(2,1)S(1)}, bf16[96,768]{1,0:T(8,128)(2,1)S(1)}, u32[]{:S(2)}, u32[]{:S(2)}) collective-permute-start(bf16[96,768]{1,0:T(8,128)(2,1)S(1)} %get-tuple-element.187), channel_id=1, source_target_pairs={{0,8},{1,5},{2,10},{3,7},{4,12},{5,1},{6,14},{7,3},{8,0},{9,13},{1... | collective-permute-start | bytes 442376 | tf_op jit(solution)/shard_map/ppermute | solution.py:718
  52.0 1.6 %collective-permute-start.18 = (bf16[192,768]{1,0:T(8,128)(2,1)S(1)}, bf16[192,768]{1,0:T(8,128)(2,1)S(1)}, u32[]{:S(2)}, u32[]{:S(2)}) collective-permute-start(bf16[192,768]{1,0:T(8,128)(2,1)S(1)} %get-tuple-element.195), channel_id=1, source_target_pairs={{0,4},{1,9},{2,6},{3,11},{4,0},{5,13},{6,2},{7,15},{8,12},{9,1},{1... | collective-permute-start | bytes 884744 | tf_op jit(solution)/shard_map/ppermute | solution.py:718
  53.6 2.1 %collective-permute-done.15.refs_4_ = bf16[96,768]{1,0:T(8,128)(2,1)S(1)} collective-permute-done((bf16[96,768]{1,0:T(8,128)(2,1)S(1)}, bf16[96,768]{1,0:T(8,128)(2,1)S(1)}, u32[]{:S(2)}, u32[]{:S(2)}) %collective-permute-start.15) | collective-permute-done | bytes 147488 | tf_op jit(solution)/shard_map/ppermute | solution.py:718
  56.4 3.0 %collective-permute-start.17 = (bf16[96,768]{1,0:T(8,128)(2,1)S(1)}, bf16[96,768]{1,0:T(8,128)(2,1)S(1)}, u32[]{:S(2)}, u32[]{:S(2)}) collective-permute-start(bf16[96,768]{1,0:T(8,128)(2,1)S(1)} %get-tuple-element.192.refs_0_), channel_id=1, source_target_pairs={{0,16},{1,17},{2,18},{3,19},{4,20},{5,21},{6,22},{7,23},{8,24},{9,... | collective-permute-start | bytes 442376 | tf_op jit(solution)/shard_map/ppermute | solution.py:718
  59.3 1.8 %collective-permute-start.20 = (bf16[192,768]{1,0:T(8,128)(2,1)S(1)}, bf16[192,768]{1,0:T(8,128)(2,1)S(1)}, u32[]{:S(2)}, u32[]{:S(2)}) collective-permute-start(bf16[192,768]{1,0:T(8,128)(2,1)S(1)} %get-tuple-element.204), channel_id=1, source_target_pairs={{0,4},{1,9},{2,6},{3,11},{4,0},{5,13},{6,2},{7,15},{8,12},{9,1},{1... | collective-permute-start | bytes 884744 | tf_op jit(solution)/shard_map/ppermute | solution.py:718
  61.8 1.8 %collective-permute-start.21 = (bf16[192,768]{1,0:T(8,128)(2,1)S(1)}, bf16[192,768]{1,0:T(8,128)(2,1)S(1)}, u32[]{:S(2)}, u32[]{:S(2)}) collective-permute-start(bf16[192,768]{1,0:T(8,128)(2,1)S(1)} %get-tuple-element.205), channel_id=1, source_target_pairs={{0,8},{1,5},{2,10},{3,7},{4,12},{5,1},{6,14},{7,3},{8,0},{9,13},{1... | collective-permute-start | bytes 884744 | tf_op jit(solution)/shard_map/ppermute | solution.py:718
  63.6 1.4 %input_grads.1 = (f32[256,768]{1,0:T(8,128)S(1)}, bf16[272,768]{1,0:T(8,128)(2,1)S(1)}, f32[8,128]{1,0:T(8,128)S(1)}) custom-call(bf16[1152,256]{1,0:T(8,128)(2,1)S(1)} %get-tuple-element.176.refs_0_.refs_4_.refs_8_, bf16[1152,256]{1,0:T(8,128)(2,1)S(1)} %get-tuple-element.177.refs_1_.refs_5_.refs_9_, ...), custom_call_target="tpu_custom_call" | custom-call | bytes 100000000 | tf_op jit(solution)/shard_map/input_grads/pallas_call | solution.py:144
  65.0 1.6 %collective-permute-start.19 = (bf16[272,768]{1,0:T(8,128)(2,1)S(1)}, bf16[272,768]{1,0:T(8,128)(2,1)S(1)}, u32[]{:S(2)}, u32[]{:S(2)}) collective-permute-start(bf16[272,768]{1,0:T(8,128)(2,1)S(1)} %get-tuple-element.202.refs_0_), channel_id=1, source_target_pairs={{0,2},{1,3},{2,0},{3,1},{4,6},{5,7},{6,4},{7,5},{8,10},{9,11},{10,... | collective-permute-start | bytes 1253384 | tf_op jit(solution)/shard_map/ppermute | solution.py:710
  67.0 1.2 %feed_result.1 = (bf16[256,768]{1,0:T(8,128)(2,1)}, f32[8,128]{1,0:T(8,128)S(1)}) custom-call(bf16[256,768]{1,0:T(8,128)(2,1)S(1)} %get-tuple-element.163.refs_0_, bf16[768,768]{1,0:T(8,128)(2,1)S(1)} %get-tuple-element.150.refs_7_.refs_9_.refs_1_, f32[256,768]{1,0:T(8,128)S(1)} %get-tuple-element.164.refs_2_, f32[8,128]{1,0:T(8,128)S(1)} %get-tuple-element.199.refs_3_), custom_call_target="tpu_custom_call" | custom-call | bytes 100000000 | tf_op jit(solution)/shard_map/feed_result/pallas_call | solution.py:144
  68.3 0.9 collective-permute-done.20.refs_3_
  69.9 1.1 %collective-permute-start.22 = (bf16[192,768]{1,0:T(8,128)(2,1)S(1)}, bf16[192,768]{1,0:T(8,128)(2,1)S(1)}, u32[]{:S(2)}, u32[]{:S(2)}) collective-permute-start(bf16[192,768]{1,0:T(8,128)(2,1)S(1)} %get-tuple-element.207.refs_0_), channel_id=1, source_target_pairs={{0,16},{1,17},{2,18},{3,19},{4,20},{5,21},{6,22},{7,23},{8,24},{9,... | collective-permute-start | bytes 884744 | tf_op jit(solution)/shard_map/ppermute | solution.py:718
  71.1 1.5 %collective-permute-start.25 = (bf16[96,768]{1,0:T(8,128)(2,1)S(1)}, bf16[96,768]{1,0:T(8,128)(2,1)S(1)}, u32[]{:S(2)}, u32[]{:S(2)}) collective-permute-start(bf16[96,768]{1,0:T(8,128)(2,1)S(1)} %get-tuple-element.210.refs_1_), channel_id=1, source_target_pairs={{0,4},{1,9},{2,6},{3,11},{4,0},{5,13},{6,2},{7,15},{8,12},{9,1},{1... | collective-permute-start | bytes 442376 | tf_op jit(solution)/shard_map/ppermute | solution.py:718
  73.4 2.9 %collective-permute-done.25.refs_3_ = bf16[96,768]{1,0:T(8,128)(2,1)S(1)} collective-permute-done((bf16[96,768]{1,0:T(8,128)(2,1)S(1)}, bf16[96,768]{1,0:T(8,128)(2,1)S(1)}, u32[]{:S(2)}, u32[]{:S(2)}) %collective-permute-start.25) | collective-permute-done | bytes 147488 | tf_op jit(solution)/shard_map/ppermute | solution.py:718
  76.2 2.0 %collective-permute-done.26.refs_4_ = bf16[96,768]{1,0:T(8,128)(2,1)S(1)} collective-permute-done((bf16[96,768]{1,0:T(8,128)(2,1)S(1)}, bf16[96,768]{1,0:T(8,128)(2,1)S(1)}, u32[]{:S(2)}, u32[]{:S(2)}) %collective-permute-start.26) | collective-permute-done | bytes 147488 | tf_op jit(solution)/shard_map/ppermute | solution.py:718
  78.2 1.7 %place_sums.4 = (f32[192,768]{1,0:T(8,128)}, f32[192,768]{1,0:T(8,128)}, f32[8,128]{1,0:T(8,128)S(1)}) custom-call(s32[7]{0:T(128)S(1)} %stack.31.refs_0_, bf16[96,768]{1,0:T(8,128)(2,1)S(1)} %get-tuple-element.210.refs_1_, bf16[96,768]{1,0:T(8,128)(2,1)S(1)} %collective-permute-done.24.refs_2_, bf16[96,768]{1,0:T(8,128)(2,1)S(1)} %collective-permute-done.25.refs_3_, ...), custom_call_target="tpu_custom_call" | custom-call | bytes 100000000 | tf_op jit(solution)/shard_map/place_sums/pallas_call | solution.py:144
  80.0 1.7 %collective-permute-start.27 = (bf16[16,768]{1,0:T(8,128)(2,1)S(1)}, bf16[16,768]{1,0:T(8,128)(2,1)S(1)}, u32[]{:S(2)}, u32[]{:S(2)}) collective-permute-start(bf16[16,768]{1,0:T(8,128)(2,1)S(1)} %get-tuple-element.213.refs_2_), channel_id=1, source_target_pairs={{0,16},{1,17},{2,18},{3,19},{4,20},{5,21},{6,22},{7,23},{8,24},{9,... | collective-permute-start | bytes 73736 | tf_op jit(solution)/shard_map/ppermute | solution.py:718
  81.7 3.1 %collective-permute-done.27.refs_3_ = bf16[16,768]{1,0:T(8,128)(2,1)S(1)} collective-permute-done((bf16[16,768]{1,0:T(8,128)(2,1)S(1)}, bf16[16,768]{1,0:T(8,128)(2,1)S(1)}, u32[]{:S(2)}, u32[]{:S(2)}) %collective-permute-start.27) | collective-permute-done | bytes 24608 | tf_op jit(solution)/shard_map/ppermute | solution.py:718
  84.9 1.1 %collective-permute-start.28 = (bf16[208,768]{1,0:T(8,128)(2,1)S(1)}, bf16[208,768]{1,0:T(8,128)(2,1)S(1)}, u32[]{:S(2)}, u32[]{:S(2)}) collective-permute-start(bf16[208,768]{1,0:T(8,128)(2,1)S(1)} %get-tuple-element.217.refs_0_), channel_id=1, source_target_pairs={{0,8},{1,5},{2,10},{3,7},{4,12},{5,1},{6,14},{7,3},{8,0},{9,13},{1... | collective-permute-start | bytes 958472 | tf_op jit(solution)/shard_map/ppermute | solution.py:718
  86.0 1.3 %input_norm.1 = (bf16[256,768]{1,0:T(8,128)(2,1)}, f32[8,128]{1,0:T(8,128)S(1)}) custom-call(bf16[256,768]{1,0:T(8,128)(2,1)S(1)} %get-tuple-element.125.refs_3_.refs_0_, f32[768]{0:T(1024)S(1)} %get-tuple-element.126.refs_4_.refs_1_, f32[256,768]{1,0:T(8,128)S(1)} %get-tuple-element.201.refs_2_, ...), custom_call_target="tpu_custom_call" | custom-call | bytes 100000000 | tf_op jit(solution)/shard_map/input_norm/pallas_call | solution.py:144
  87.3 4.6 %collective-permute-done.28.refs_1_ = bf16[208,768]{1,0:T(8,128)(2,1)S(1)} collective-permute-done((bf16[208,768]{1,0:T(8,128)(2,1)S(1)}, bf16[208,768]{1,0:T(8,128)(2,1)S(1)}, u32[]{:S(2)}, u32[]{:S(2)}) %collective-permute-start.28) | collective-permute-done | bytes 319520 | tf_op jit(solution)/shard_map/ppermute | solution.py:718
  92.0 1.3 %collective-permute-start.29 = (bf16[208,768]{1,0:T(8,128)(2,1)S(1)}, bf16[208,768]{1,0:T(8,128)(2,1)S(1)}, u32[]{:S(2)}, u32[]{:S(2)}) collective-permute-start(bf16[208,768]{1,0:T(8,128)(2,1)S(1)} %get-tuple-element.219.refs_1_), channel_id=1, source_target_pairs={{0,4},{1,9},{2,6},{3,11},{4,0},{5,13},{6,2},{7,15},{8,12},{9,1},{1... | collective-permute-start | bytes 958472 | tf_op jit(solution)/shard_map/ppermute | solution.py:718
  94.1 1.6 %place_sums.5 = (f32[3,192,768]{2,1,0:T(8,128)}, f32[192,768]{1,0:T(8,128)}, f32[8,128]{1,0:T(8,128)S(1)}) custom-call(s32[7]{0:T(128)S(1)} %stack.31.refs_0_, bf16[208,768]{1,0:T(8,128)(2,1)S(1)} %get-tuple-element.219.refs_1_, bf16[208,768]{1,0:T(8,128)(2,1)S(1)} %get-tuple-element.220.refs_2_, f32[8,128]{1,0:T(8,128)S(1)} %get-tuple-element.221.refs_3_), custom_call_target="tpu_custom_call" | custom-call | bytes 100000000 | tf_op jit(solution)/shard_map/place_sums/pallas_call | solution.py:144
  95.7 3.3 %collective-permute-done.29.refs_3_ = bf16[208,768]{1,0:T(8,128)(2,1)S(1)} collective-permute-done((bf16[208,768]{1,0:T(8,128)(2,1)S(1)}, bf16[208,768]{1,0:T(8,128)(2,1)S(1)}, u32[]{:S(2)}, u32[]{:S(2)}) %collective-permute-start.29) | collective-permute-done | bytes 319520 | tf_op jit(solution)/shard_map/ppermute | solution.py:718
  99.0 1.4 %place_sums.6 = (f32[3,192,768]{2,1,0:T(8,128)}, f32[192,768]{1,0:T(8,128)}, f32[8,128]{1,0:T(8,128)S(1)}) custom-call(s32[7]{0:T(128)S(1)} %stack.31.refs_0_, bf16[208,768]{1,0:T(8,128)(2,1)S(1)} %get-tuple-element.219.refs_1_, bf16[208,768]{1,0:T(8,128)(2,1)S(1)} %get-tuple-element.220.refs_2_, ...), custom_call_target="tpu_custom_call", output_to_operand_aliasing={{0}: (4, {}), {1}: (5, {})} | custom-call | bytes 100000000 | tf_op jit(solution)/shard_map/place_sums/pallas_call | solution.py:144
  100.5 2.0 %collective-permute-done.30.refs_4_ = bf16[208,768]{1,0:T(8,128)(2,1)S(1)} collective-permute-done((bf16[208,768]{1,0:T(8,128)(2,1)S(1)}, bf16[208,768]{1,0:T(8,128)(2,1)S(1)}, u32[]{:S(2)}, u32[]{:S(2)}) %collective-permute-start.30) | collective-permute-done | bytes 319520 | tf_op jit(solution)/shard_map/ppermute | solution.py:718
  102.4 2.0 %place_sums.7 = (f32[3,192,768]{2,1,0:T(8,128)}, f32[192,768]{1,0:T(8,128)}, f32[768]{0:T(1024)}, f32[768]{0:T(1024)}, f32[768]{0:T(1024)}, /*index=5*/f32[768]{0:T(1024)}, f32[192]{0:T(256)}, f32[8,128]{1,0:T(8,128)}) custom-call(s32[7]{0:T(128)S(1)} %stack.31.refs_0_, ...), custom_call_target="tpu_custom_call", output_to_operand_aliasing={{0}: (5, {}), {1}: (6, {})} | custom-call | bytes 100000000 | tf_op jit(solution)/shard_map/place_sums/pallas_call | solution.py:144
  (51 shorter events, 10.5 us)
Async XLA Ops:
  0.6 7.9 %collective-permute-start = (bf16[3,192,768]{2,1,0:T(8,128)(2,1)}, bf16[3,192,768]{2,1,0:T(8,128)(2,1)S(1)}, u32[]{:S(2)}, u32[]{:S(2)}) collective-permute-start(bf16[3,192,768]{2,1,0:T(8,128)(2,1)} %refs_6_.3), channel_id=1, source_target_pairs={{0,1},{1,0},{2,3},{3,2},{4,5},{5,4},{6,7},{7,6},{8,9},{9,8},{10,11... | collective-permute-start | bytes 2654216 | tf_op jit(solution)/shard_map/ppermute | solution.py:707
  1.2 0.7 copy-start
  3.4 9.5 %collective-permute-start.3 = (bf16[160,768]{1,0:T(8,128)(2,1)S(1)}, bf16[160,768]{1,0:T(8,128)(2,1)S(1)}, u32[]{:S(2)}, u32[]{:S(2)}) collective-permute-start(bf16[160,768]{1,0:T(8,128)(2,1)S(1)} %get-tuple-element.133), channel_id=1, source_target_pairs={{0,2},{1,3},{2,0},{3,1},{4,6},{5,7},{6,4},{7,5},{8,10},{9,11},{10,... | collective-permute-start | bytes 737288 | tf_op jit(solution)/shard_map/ppermute | solution.py:710
  6.1 16.5 %collective-permute-start.1 = (bf16[256,768]{1,0:T(8,128)(2,1)}, bf16[256,768]{1,0:T(8,128)(2,1)S(1)}, u32[]{:S(2)}, u32[]{:S(2)}) collective-permute-start(bf16[256,768]{1,0:T(8,128)(2,1)} %refs_4_.3), channel_id=1, source_target_pairs={{0,2},{1,3},{2,0},{3,1},{4,6},{5,7},{6,4},{7,5},{8,10},{9,11},{10,... | collective-permute-start | bytes 1179656 | tf_op jit(solution)/shard_map/ppermute | solution.py:710
  8.3 14.4 %collective-permute-start.2 = (bf16[592,768]{1,0:T(8,128)(2,1)S(1)}, bf16[592,768]{1,0:T(8,128)(2,1)S(1)}, u32[]{:S(2)}, u32[]{:S(2)}) collective-permute-start(bf16[592,768]{1,0:T(8,128)(2,1)S(1)} %get-tuple-element.132.refs_7_.refs_8_), channel_id=1, source_target_pairs={{0,1},{1,0},{2,3},{3,2},{4,5},{5,4},{6,7},{7,6},{8,9},{9,8},{10,11... | collective-permute-start | bytes 2727944 | tf_op jit(solution)/shard_map/ppermute | solution.py:707
  12.9 7.7 %collective-permute-start.4 = (bf16[144,768]{1,0:T(8,128)(2,1)S(1)}, bf16[144,768]{1,0:T(8,128)(2,1)S(1)}, u32[]{:S(2)}, u32[]{:S(2)}) collective-permute-start(bf16[144,768]{1,0:T(8,128)(2,1)S(1)} %get-tuple-element.135), channel_id=1, source_target_pairs={{0,4},{1,5},{2,6},{3,7},{4,0},{5,1},{6,2},{7,3},{8,12},{9,13},{10,... | collective-permute-start | bytes 663560 | tf_op jit(solution)/shard_map/ppermute | solution.py:718
  14.9 7.1 %collective-permute-start.5 = (bf16[144,768]{1,0:T(8,128)(2,1)S(1)}, bf16[144,768]{1,0:T(8,128)(2,1)S(1)}, u32[]{:S(2)}, u32[]{:S(2)}) collective-permute-start(bf16[144,768]{1,0:T(8,128)(2,1)S(1)} %get-tuple-element.135), channel_id=1, source_target_pairs={{0,8},{1,9},{2,10},{3,11},{4,12},{5,13},{6,14},{7,15},{8,0},{9,1},... | collective-permute-start | bytes 663560 | tf_op jit(solution)/shard_map/ppermute | solution.py:718
  16.5 17.4 %collective-permute-start.11 = (bf16[256,1152]{1,0:T(8,128)(2,1)S(1)}, bf16[256,1152]{1,0:T(8,128)(2,1)S(1)}, u32[]{:S(2)}, u32[]{:S(2)}) collective-permute-start(bf16[256,1152]{1,0:T(8,128)(2,1)S(1)} %get-tuple-element.130.refs_1_), channel_id=1, source_target_pairs={{0,2},{1,3},{2,0},{3,1},{4,6},{5,7},{6,4},{7,5},{8,10},{9,11},{10,... | collective-permute-start | bytes 1769480 | tf_op jit(solution)/shard_map/ppermute | solution.py:710
  20.6 8.0 %collective-permute-start.8 = (bf16[160,768]{1,0:T(8,128)(2,1)S(1)}, bf16[160,768]{1,0:T(8,128)(2,1)S(1)}, u32[]{:S(2)}, u32[]{:S(2)}) collective-permute-start(bf16[160,768]{1,0:T(8,128)(2,1)S(1)} %get-tuple-element.144.refs_4_.refs_10_), channel_id=1, source_target_pairs={{0,1},{1,0},{2,3},{3,2},{4,5},{5,4},{6,7},{7,6},{8,9},{9,8},{10,11... | collective-permute-start | bytes 737288 | tf_op jit(solution)/shard_map/ppermute | solution.py:707
  22.1 6.5 %collective-permute-start.7 = (bf16[144,768]{1,0:T(8,128)(2,1)S(1)}, bf16[144,768]{1,0:T(8,128)(2,1)S(1)}, u32[]{:S(2)}, u32[]{:S(2)}) collective-permute-start(bf16[144,768]{1,0:T(8,128)(2,1)S(1)} %get-tuple-element.146), channel_id=1, source_target_pairs={{0,4},{1,5},{2,6},{3,7},{4,0},{5,1},{6,2},{7,3},{8,12},{9,13},{10,... | collective-permute-start | bytes 663560 | tf_op jit(solution)/shard_map/ppermute | solution.py:718
  22.6 7.5 %collective-permute-start.9 = (bf16[2,144,768]{2,1,0:T(8,128)(2,1)S(1)}, bf16[2,144,768]{2,1,0:T(8,128)(2,1)S(1)}, u32[]{:S(2)}, u32[]{:S(2)}) collective-permute-start(bf16[2,144,768]{2,1,0:T(8,128)(2,1)S(1)} %get-tuple-element.145.refs_5_), channel_id=1, source_target_pairs={{0,1},{1,0},{2,3},{3,2},{4,5},{5,4},{6,7},{7,6},{8,9},{9,8},{10,11... | collective-permute-start | bytes 1327112 | tf_op jit(solution)/shard_map/ppermute | solution.py:707
  26.2 11.7 %collective-permute-start.6 = (bf16[256,384]{1,0:T(8,128)(2,1)S(1)}, bf16[256,384]{1,0:T(8,128)(2,1)S(1)}, u32[]{:S(2)}, u32[]{:S(2)}) collective-permute-start(bf16[256,384]{1,0:T(8,128)(2,1)S(1)} %get-tuple-element.138.refs_1_), channel_id=1, source_target_pairs={{0,2},{1,3},{2,0},{3,1},{4,6},{5,7},{6,4},{7,5},{8,10},{9,11},{10,... | collective-permute-start | bytes 589832 | tf_op jit(solution)/shard_map/ppermute | solution.py:710
  28.6 1.5 %collective-permute-start.10 = (bf16[144,768]{1,0:T(8,128)(2,1)S(1)}, bf16[144,768]{1,0:T(8,128)(2,1)S(1)}, u32[]{:S(2)}, u32[]{:S(2)}) collective-permute-start(bf16[144,768]{1,0:T(8,128)(2,1)S(1)} %collective-permute-done.7.refs_6_), channel_id=1, source_target_pairs={{0,1},{1,0},{2,3},{3,2},{4,5},{5,4},{6,7},{7,6},{8,9},{9,8},{10,11... | collective-permute-start | bytes 663560 | tf_op jit(solution)/shard_map/ppermute | solution.py:707
  40.4 2.6 %collective-permute-start.12 = (bf16[2,192,768]{2,1,0:T(8,128)(2,1)S(1)}, bf16[2,192,768]{2,1,0:T(8,128)(2,1)S(1)}, u32[]{:S(2)}, u32[]{:S(2)}) collective-permute-start(bf16[2,192,768]{2,1,0:T(8,128)(2,1)S(1)} %get-tuple-element.166), channel_id=1, source_target_pairs={{0,1},{1,0},{2,3},{3,2},{4,5},{5,4},{6,7},{7,6},{8,9},{9,8},{10,11... | collective-permute-start | bytes 1769480 | tf_op jit(solution)/shard_map/ppermute | solution.py:707
  43.5 5.5 %collective-permute-start.14 = (bf16[96,768]{1,0:T(8,128)(2,1)S(1)}, bf16[96,768]{1,0:T(8,128)(2,1)S(1)}, u32[]{:S(2)}, u32[]{:S(2)}) collective-permute-start(bf16[96,768]{1,0:T(8,128)(2,1)S(1)} %get-tuple-element.175), channel_id=1, source_target_pairs={{0,4},{1,9},{2,6},{3,11},{4,0},{5,13},{6,2},{7,15},{8,12},{9,1},{1... | collective-permute-start | bytes 442376 | tf_op jit(solution)/shard_map/ppermute | solution.py:718
  47.2 4.3 %collective-permute-start.16 = (bf16[4,192,768]{2,1,0:T(8,128)(2,1)S(1)}, bf16[4,192,768]{2,1,0:T(8,128)(2,1)S(1)}, u32[]{:S(2)}, u32[]{:S(2)}) collective-permute-start(bf16[4,192,768]{2,1,0:T(8,128)(2,1)S(1)} %get-tuple-element.189), channel_id=1, source_target_pairs={{0,1},{1,0},{2,3},{3,2},{4,5},{5,4},{6,7},{7,6},{8,9},{9,8},{10,11... | collective-permute-start | bytes 3538952 | tf_op jit(solution)/shard_map/ppermute | solution.py:707
  47.5 6.1 %collective-permute-start.13 = (bf16[96,768]{1,0:T(8,128)(2,1)S(1)}, bf16[96,768]{1,0:T(8,128)(2,1)S(1)}, u32[]{:S(2)}, u32[]{:S(2)}) collective-permute-start(bf16[96,768]{1,0:T(8,128)(2,1)S(1)} %get-tuple-element.174), channel_id=1, source_target_pairs={{0,4},{1,9},{2,6},{3,11},{4,0},{5,13},{6,2},{7,15},{8,12},{9,1},{1... | collective-permute-start | bytes 442376 | tf_op jit(solution)/shard_map/ppermute | solution.py:718
  49.6 6.1 %collective-permute-start.15 = (bf16[96,768]{1,0:T(8,128)(2,1)S(1)}, bf16[96,768]{1,0:T(8,128)(2,1)S(1)}, u32[]{:S(2)}, u32[]{:S(2)}) collective-permute-start(bf16[96,768]{1,0:T(8,128)(2,1)S(1)} %get-tuple-element.187), channel_id=1, source_target_pairs={{0,8},{1,5},{2,10},{3,7},{4,12},{5,1},{6,14},{7,3},{8,0},{9,13},{1... | collective-permute-start | bytes 442376 | tf_op jit(solution)/shard_map/ppermute | solution.py:718
  52.0 9.1 %collective-permute-start.18 = (bf16[192,768]{1,0:T(8,128)(2,1)S(1)}, bf16[192,768]{1,0:T(8,128)(2,1)S(1)}, u32[]{:S(2)}, u32[]{:S(2)}) collective-permute-start(bf16[192,768]{1,0:T(8,128)(2,1)S(1)} %get-tuple-element.195), channel_id=1, source_target_pairs={{0,4},{1,9},{2,6},{3,11},{4,0},{5,13},{6,2},{7,15},{8,12},{9,1},{1... | collective-permute-start | bytes 884744 | tf_op jit(solution)/shard_map/ppermute | solution.py:718
  56.4 10.2 %collective-permute-start.17 = (bf16[96,768]{1,0:T(8,128)(2,1)S(1)}, bf16[96,768]{1,0:T(8,128)(2,1)S(1)}, u32[]{:S(2)}, u32[]{:S(2)}) collective-permute-start(bf16[96,768]{1,0:T(8,128)(2,1)S(1)} %get-tuple-element.192.refs_0_), channel_id=1, source_target_pairs={{0,16},{1,17},{2,18},{3,19},{4,20},{5,21},{6,22},{7,23},{8,24},{9,... | collective-permute-start | bytes 442376 | tf_op jit(solution)/shard_map/ppermute | solution.py:718
  59.3 9.9 %collective-permute-start.20 = (bf16[192,768]{1,0:T(8,128)(2,1)S(1)}, bf16[192,768]{1,0:T(8,128)(2,1)S(1)}, u32[]{:S(2)}, u32[]{:S(2)}) collective-permute-start(bf16[192,768]{1,0:T(8,128)(2,1)S(1)} %get-tuple-element.204), channel_id=1, source_target_pairs={{0,4},{1,9},{2,6},{3,11},{4,0},{5,13},{6,2},{7,15},{8,12},{9,1},{1... | collective-permute-start | bytes 884744 | tf_op jit(solution)/shard_map/ppermute | solution.py:718
  61.8 7.4 %collective-permute-start.21 = (bf16[192,768]{1,0:T(8,128)(2,1)S(1)}, bf16[192,768]{1,0:T(8,128)(2,1)S(1)}, u32[]{:S(2)}, u32[]{:S(2)}) collective-permute-start(bf16[192,768]{1,0:T(8,128)(2,1)S(1)} %get-tuple-element.205), channel_id=1, source_target_pairs={{0,8},{1,5},{2,10},{3,7},{4,12},{5,1},{6,14},{7,3},{8,0},{9,13},{1... | collective-permute-start | bytes 884744 | tf_op jit(solution)/shard_map/ppermute | solution.py:718
  65.0 8.3 %collective-permute-start.19 = (bf16[272,768]{1,0:T(8,128)(2,1)S(1)}, bf16[272,768]{1,0:T(8,128)(2,1)S(1)}, u32[]{:S(2)}, u32[]{:S(2)}) collective-permute-start(bf16[272,768]{1,0:T(8,128)(2,1)S(1)} %get-tuple-element.202.refs_0_), channel_id=1, source_target_pairs={{0,2},{1,3},{2,0},{3,1},{4,6},{5,7},{6,4},{7,5},{8,10},{9,11},{10,... | collective-permute-start | bytes 1253384 | tf_op jit(solution)/shard_map/ppermute | solution.py:710
  66.6 6.5 %collective-permute-start.24 = (bf16[96,768]{1,0:T(8,128)(2,1)S(1)}, bf16[96,768]{1,0:T(8,128)(2,1)S(1)}, u32[]{:S(2)}, u32[]{:S(2)}) collective-permute-start(bf16[96,768]{1,0:T(8,128)(2,1)S(1)} %get-tuple-element.210.refs_1_), channel_id=1, source_target_pairs={{0,8},{1,5},{2,10},{3,7},{4,12},{5,1},{6,14},{7,3},{8,0},{9,13},{1... | collective-permute-start | bytes 442376 | tf_op jit(solution)/shard_map/ppermute | solution.py:718
  69.9 14.9 %collective-permute-start.22 = (bf16[192,768]{1,0:T(8,128)(2,1)S(1)}, bf16[192,768]{1,0:T(8,128)(2,1)S(1)}, u32[]{:S(2)}, u32[]{:S(2)}) collective-permute-start(bf16[192,768]{1,0:T(8,128)(2,1)S(1)} %get-tuple-element.207.refs_0_), channel_id=1, source_target_pairs={{0,16},{1,17},{2,18},{3,19},{4,20},{5,21},{6,22},{7,23},{8,24},{9,... | collective-permute-start | bytes 884744 | tf_op jit(solution)/shard_map/ppermute | solution.py:718
  71.1 5.1 %collective-permute-start.25 = (bf16[96,768]{1,0:T(8,128)(2,1)S(1)}, bf16[96,768]{1,0:T(8,128)(2,1)S(1)}, u32[]{:S(2)}, u32[]{:S(2)}) collective-permute-start(bf16[96,768]{1,0:T(8,128)(2,1)S(1)} %get-tuple-element.210.refs_1_), channel_id=1, source_target_pairs={{0,4},{1,9},{2,6},{3,11},{4,0},{5,13},{6,2},{7,15},{8,12},{9,1},{1... | collective-permute-start | bytes 442376 | tf_op jit(solution)/shard_map/ppermute | solution.py:718
  73.1 5.1 %collective-permute-start.26 = (bf16[96,768]{1,0:T(8,128)(2,1)S(1)}, bf16[96,768]{1,0:T(8,128)(2,1)S(1)}, u32[]{:S(2)}, u32[]{:S(2)}) collective-permute-start(bf16[96,768]{1,0:T(8,128)(2,1)S(1)} %collective-permute-done.24.refs_2_), channel_id=1, source_target_pairs={{0,4},{1,9},{2,6},{3,11},{4,0},{5,13},{6,2},{7,15},{8,12},{9,1},{1... | collective-permute-start | bytes 442376 | tf_op jit(solution)/shard_map/ppermute | solution.py:718
  73.3 6.6 %collective-permute-start.23 = (bf16[16,768]{1,0:T(8,128)(2,1)S(1)}, bf16[16,768]{1,0:T(8,128)(2,1)S(1)}, u32[]{:S(2)}, u32[]{:S(2)}) collective-permute-start(bf16[16,768]{1,0:T(8,128)(2,1)S(1)} %get-tuple-element.209.refs_0_), channel_id=1, source_target_pairs={{0,1},{1,0},{2,3},{3,2},{4,5},{5,4},{6,7},{7,6},{8,9},{9,8},{10,11... | collective-permute-start | bytes 73736 | tf_op jit(solution)/shard_map/ppermute | solution.py:707
  80.0 4.8 %collective-permute-start.27 = (bf16[16,768]{1,0:T(8,128)(2,1)S(1)}, bf16[16,768]{1,0:T(8,128)(2,1)S(1)}, u32[]{:S(2)}, u32[]{:S(2)}) collective-permute-start(bf16[16,768]{1,0:T(8,128)(2,1)S(1)} %get-tuple-element.213.refs_2_), channel_id=1, source_target_pairs={{0,16},{1,17},{2,18},{3,19},{4,20},{5,21},{6,22},{7,23},{8,24},{9,... | collective-permute-start | bytes 73736 | tf_op jit(solution)/shard_map/ppermute | solution.py:718
  84.9 7.1 %collective-permute-start.28 = (bf16[208,768]{1,0:T(8,128)(2,1)S(1)}, bf16[208,768]{1,0:T(8,128)(2,1)S(1)}, u32[]{:S(2)}, u32[]{:S(2)}) collective-permute-start(bf16[208,768]{1,0:T(8,128)(2,1)S(1)} %get-tuple-element.217.refs_0_), channel_id=1, source_target_pairs={{0,8},{1,5},{2,10},{3,7},{4,12},{5,1},{6,14},{7,3},{8,0},{9,13},{1... | collective-permute-start | bytes 958472 | tf_op jit(solution)/shard_map/ppermute | solution.py:718
  92.0 7.1 %collective-permute-start.29 = (bf16[208,768]{1,0:T(8,128)(2,1)S(1)}, bf16[208,768]{1,0:T(8,128)(2,1)S(1)}, u32[]{:S(2)}, u32[]{:S(2)}) collective-permute-start(bf16[208,768]{1,0:T(8,128)(2,1)S(1)} %get-tuple-element.219.refs_1_), channel_id=1, source_target_pairs={{0,4},{1,9},{2,6},{3,11},{4,0},{5,13},{6,2},{7,15},{8,12},{9,1},{1... | collective-permute-start | bytes 958472 | tf_op jit(solution)/shard_map/ppermute | solution.py:718
  93.2 9.2 %collective-permute-start.30 = (bf16[208,768]{1,0:T(8,128)(2,1)S(1)}, bf16[208,768]{1,0:T(8,128)(2,1)S(1)}, u32[]{:S(2)}, u32[]{:S(2)}) collective-permute-start(bf16[208,768]{1,0:T(8,128)(2,1)S(1)} %get-tuple-element.220.refs_2_), channel_id=1, source_target_pairs={{0,4},{1,9},{2,6},{3,11},{4,0},{5,13},{6,2},{7,15},{8,12},{9,1},{1... | collective-permute-start | bytes 958472 | tf_op jit(solution)/shard_map/ppermute | solution.py:718

commit v9 on v8

--- a/solution.py
+++ b/solution.py
@@ -71,7 +71,8 @@
     return jnp.concatenate([both[:HEAD_DIM, :LEN], both[HEAD_DIM:, LEN:]], axis=0)
 
 
-COSTS = (0, 0, 100, 0, 0, 30, 30, 0, 0, 0, 0, 100, 0, 0, 0, 200, 0, 60, 0, 0, 30, 0, 0, 0, 0, 0, 0, 0, 0, 0, 0, 0)
+STRIP = 256
+COSTS = (0, 0, 100, 0, 0, 30, 30, 0, 0, 0, 0, 0, 100, 0, 0, 0, 200, 0, 60, 0, 0, 30, 0, 0, 0, 0, 0, 0, 0, 0, 0, 0, 0)
 
 
 class IO:
@@ -175,16 +176,17 @@
         copy.wait()
 
 
-def attention(chain, bits, place, nodes, edges, x, gain, bias, w, g=None, near=()):
+def attention(chain, bits, place, nodes, edges, x, gain, bias, w, near=()):
     rows, d = x.shape
-    width = w.shape[1] if g is None else 2 * w[0].shape[1]
+    apart = isinstance(w, tuple)
+    width = 2 * w[0].shape[1] if apart else w.shape[1]
     shard = width // 2
     pairs = width // PAIR
     mols = rows // LEN
 
     def kernel(io, bits_ref, nodes_ref, edges_ref, x_ref, gain_ref, bias_ref, *refs):
         started = []
-        if g is None:
+        if not apart:
             w_ref, near0, near1, *refs, wo_ref, fc1_ref, fc2_ref, sems = refs
             a1_ref, qt_ref, kt_ref, v_ref, p_ref, ot_ref, o_ref = refs
             pairs_w = []
@@ -194,15 +196,15 @@
                     pairs_w.append((part, out.at[at * shard : (at + 1) * shard]))
             started = copies(sems, pairs_w)
         else:
-            own, got, g_ref, *refs, w_ref, sems = refs
+            own, got, *refs, w_ref, sems = refs
             a1_ref, qt_ref, kt_ref, v_ref, p_ref, ot_ref, o_ref = refs
-            pairs_w = [(own, w_ref.at[:, :shard]), (got, w_ref.at[:, shard:]), (g_ref, o_ref.at[:, :d])]
-            started = copies(sems, pairs_w)
+            pairs_w = [(own, w_ref.at[:, :shard]), (got, w_ref.at[:, shard:])]
+            near_w = copies(sems, pairs_w)
         xh, _ = normalise(x_ref[...].astype(F32))
         a1 = (xh * gain_ref[...][None, :] + bias_ref[...][None, :]).astype(BF16)
         a1_ref[...] = a1
-        if g is not None:
-            finish(started[:2])
+        if apart:
+            finish(near_w)
         qt = dot_nt(w_ref[0], a1).astype(BF16)
         keys = dot_nt(a1, w_ref[1]).astype(BF16)
         vt = dot_nt(w_ref[2], a1).astype(BF16)
@@ -229,50 +231,56 @@
         for m, i in every:
             both = dot_nn(vt[rows_of(i), lanes(m)], probs[m, i])
             ot_ref[rows_of(i), lanes(m)] = diagonal(both).astype(BF16)
-        o_ref[:, o_ref.shape[1] - width :] = ot_ref[...].T
+        o_ref[...] = ot_ref[...].T
         kt_ref[...] = dot_nt(w_ref[1], a1).astype(BF16)
         v_ref[...] = dot_nt(a1, w_ref[2]).astype(BF16)
-        finish(started if g is None else started[2:])
+        finish(started)
 
     outs = [
         bf16(rows, d), bf16(width, rows), bf16(width, rows), bf16(rows, width),
         bf16(mols, pairs, LEN, 2 * LEN), bf16(width, rows),
     ]
     args = (bits, nodes, edges, x, gain, bias)
-    if g is None:
+    if not apart:
         return chain.call(
             kernel, "attention_forward", (*args, w, *near), [*outs, bf16(rows, width), bf16(2 * width, d), bf16(2 * width, d), bf16(2 * width, d)],
             "sccvvvvvv-vvvvvvvvvv", scratch=[pltpu.SemaphoreType.DMA((6,))],
         )
     return chain.call(
-        kernel, "attention_forward", (*args, *w, g), [*outs, bf16(rows, d + width), bf16(3, width, d)],
-        "sccvvvprv-vvvvvvvv", scratch=[pltpu.SemaphoreType.DMA((3,))],
+        kernel, "attention_forward", (*args, *w), [*outs, bf16(rows, width), bf16(3, width, d)],
+        "sccvvvpr-vvvvvvvv", scratch=[pltpu.SemaphoreType.DMA((2,))],
     )
 
 
 def pick(chain, bits, wo, fc1, fc2, bias):
     shard, d = wo.shape
     rows = 3 * shard // 4
+    strips = d // STRIP
 
     def kernel(io, bits_ref, wo_ref, fc1_ref, fc2_ref, bias_ref, out_ref, sems):
         refs = (wo_ref, fc1_ref, fc2_ref)
-        out_ref[rows:] = jnp.concatenate(
-            [jnp.broadcast_to(bias_ref[...].astype(F32)[None, :], (16, shard)), jnp.zeros((16, d - shard), F32)], axis=1
-        ).astype(BF16)
 
         def part(quarter):
             pairs = []
             for c, first, at, n in quarter_rows(quarter, shard):
-                pairs.append((refs[c].at[first : first + n], out_ref.at[at : at + n]))
-            finish(copies(sems, pairs))
+                for k in range(strips):
+                    source = refs[c].at[first : first + n, k * STRIP : (k + 1) * STRIP]
+                    pairs.append((source, out_ref.at[k * rows + at : k * rows + at + n]))
+            started = copies(sems, pairs)
+            io.wait(4)
+            out_ref[strips * rows :] = jnp.concatenate(
+                [jnp.broadcast_to(bias_ref[...].astype(F32)[None, :], (16, shard)), jnp.zeros((16, STRIP - shard), F32)],
+                axis=1,
+            ).astype(BF16)
+            finish(started)
 
         which = 2 * bits_ref[2] + bits_ref[6]
         for at in range(4):
             pl.when(which == at)(functools.partial(part, at))
 
     return chain.call(
-        kernel, "pick", (bits, wo, fc1, fc2, bias), [bf16(rows + 16, d)], "spppv-v", limit=4,
-        scratch=[pltpu.SemaphoreType.DMA((2,))],
+        kernel, "pick", (bits, wo, fc1, fc2, bias), [bf16(strips * rows + 16, STRIP)], "spppl-v", limit=4,
+        scratch=[pltpu.SemaphoreType.DMA((2 * strips,))],
     )[0]
 
 
@@ -287,14 +295,22 @@
     return found
 
 
-def hold(chain, a):
-    rows, d = a.shape
+def hold(chain, a, d):
+    strips = d // STRIP
+    rows = (a.shape[0] - 16) // strips
 
     def kernel(io, a_ref, out_ref, short_ref):
-        out_ref[...] = a_ref[...]
-        short_ref[...] = a_ref[: rows - 16]
-
-    return chain.call(kernel, "hold", (a,), [bf16(rows, d), bf16(rows - 16, d)], "v-vv", limit=4)
+        for k in range(strips):
+            strip = a_ref[k * rows : (k + 1) * rows]
+            out_ref[:rows, k * STRIP : (k + 1) * STRIP] = strip
+            short_ref[:, k * STRIP : (k + 1) * STRIP] = strip
+        out_ref[rows:] = widened(a_ref[strips * rows :], d)
+
+    return chain.call(kernel, "hold", (a,), [bf16(rows + 16, d), bf16(rows, d)], "v-vv", limit=4)
+
+
+def widened(a, d):
+    return jnp.concatenate([a, jnp.zeros((a.shape[0], d - a.shape[1]), a.dtype)], axis=1)
 
 
 def pair_up(chain, a, b):
@@ -313,39 +329,36 @@
     chain.call(kernel, "spacer", (), [], "-", limit=2)
 
 
-def load(chain, out_weight, fc1_weight, fc2_weight, bias, others):
+def load(chain, out_weight, fc1_weight, fc2_weight, picked, others):
     shard, d = out_weight.shape
     n = len(others)
 
-    def kernel(io, wo, fc1, fc2, bias_ref, *refs):
+    def kernel(io, wo, fc1, fc2, picked_ref, *refs):
         others_in, (near_ref, *others_out, sems) = refs[:n], refs[n:]
+        near_ref[3 * shard :] = widened(picked_ref[picked.shape[0] - 16 :], d)
         rows = lambda at: near_ref.at[at * shard : (at + 1) * shard]
-        near = [(wo, rows(0)), (fc1, rows(1)), (fc2, rows(2)), (bias_ref, near_ref.at[3 * shard :])]
+        near = [(wo, rows(0)), (fc1, rows(1)), (fc2, rows(2))]
         finish(copies(sems, near + list(zip(others_in, others_out))))
 
     near, *others = chain.call(
-        kernel, "load", (out_weight, fc1_weight, fc2_weight, bias, *others),
+        kernel, "load", (out_weight, fc1_weight, fc2_weight, picked, *others),
         [bf16(3 * shard + 16, d)] + [jax.ShapeDtypeStruct(a.shape, a.dtype) for a in others],
-        "pppr" + "p" * n + "-v" + "v" * n, limit=4, scratch=[pltpu.SemaphoreType.DMA((4 + n,))],
+        "pppv" + "p" * n + "-v" + "v" * n, limit=4, scratch=[pltpu.SemaphoreType.DMA((3 + n,))],
     )
     return near, others
 
 
-def feed_body(x, oa, ob, g, wo_ref, gain_ref, bias_ref, fc1_ref, b1_ref, fc2_ref, h_ref, a2_ref, z_ref, du_ref):
-    h = x.astype(F32) + dot_nn(jnp.concatenate([oa, ob], axis=1), wo_ref[...])
+def feed_body(part, ob, dz, wo_ref, gain_ref, bias_ref, fc1_ref, b1, h_ref, a2_ref, z_ref, du_ref):
+    h = part + dot_nn(ob, wo_ref[wo_ref.shape[0] // 2 :])
     h_ref[...] = h
     xh, _ = normalise(h)
     a2 = (xh * gain_ref[...][None, :] + bias_ref[...][None, :]).astype(BF16)
     a2_ref[...] = a2
-    u = dot_nt(a2, fc1_ref[...]) + b1_ref[...]
-    dz = dot_nt(g, fc2_ref[...])
+    u = dot_nt(a2, fc1_ref[...]) + b1
     phi = 0.5 * (1.0 + lax.erf(u * (0.5**0.5)))
     slope = phi + u * (jnp.exp(-0.5 * u * u) * 0.3989422804014327)
-    du = (dz * slope).astype(BF16)
-    z = (u * phi).astype(BF16)
-    du_ref[...] = du
-    z_ref[...] = z
-    return a2, z, du
+    du_ref[...] = (dz * slope).astype(BF16)
+    z_ref[...] = (u * phi).astype(BF16)
 
 
 def pack_far(chain, bits, weights, fars):
@@ -370,41 +383,62 @@
     )
 
 
-def feed_far(chain, x, oa, packet, gain, bias, wo, fc1, fc2, biases):
-    rows, d = x.shape
-    columns = fc1.shape[0]
+def feed_in(chain, xs, os, gs, wo, fc2, biases):
+    rows, d = xs[0].shape
+    columns = fc2.shape[0]
     shard = columns // 4
 
-    def kernel(io, x_ref, oa_ref, packet_ref, gain_ref, bias_ref, wo_ref, fc1_ref, fc2_ref, *refs):
-        b_refs, (h_ref, a2_ref, z_ref, du_ref, b1_ref) = refs[:4], refs[4:]
+    def kernel(io, x0, x1, o0, o1, g0, g1, wo_ref, fc2_ref, *refs):
+        b_refs, (h0, h1, dz0, dz1, b1_ref) = refs[:4], refs[4:]
+        for x_ref, o_ref, h_ref in ((x0, o0, h0), (x1, o1, h1)):
+            h_ref[...] = x_ref[...].astype(F32) + dot_nn(o_ref[...], wo_ref[: o_ref.shape[1]])
+        for g_ref, dz_ref in ((g0, dz0), (g1, dz1)):
+            dz_ref[...] = dot_nt(g_ref[...], fc2_ref[...])
         parts = [ref[row : row + 1, :shard].astype(F32) for ref, (_, row) in zip(b_refs, biases)]
         b1_ref[...] = jnp.concatenate(parts, axis=1)
+
+    return chain.call(
+        kernel, "feed_in", (*xs, *os, *gs, wo, fc2, *(a for a, _ in biases)),
+        [f32(rows, d)] * 2 + [f32(rows, columns)] * 2 + [f32(1, columns)], "v" * 12 + "-vvvvv",
+    )
+
+
+def feed_far(chain, h, ob, dz, g, gain, bias, wo, fc1, b1):
+    rows, d = h.shape
+    columns = fc1.shape[0]
+    width = columns // 2
+
+    def kernel(io, part_ref, ob_ref, dz_ref, g_ref, gain_ref, bias_ref, wo_ref, fc1_ref, b1_ref,
+               h_ref, du_ref, first_ref, second_ref, a2_ref, z_ref):
         feed_body(
-            x_ref[...], oa_ref[...], packet_ref[:, d:], packet_ref[:, :d], wo_ref, gain_ref, bias_ref, fc1_ref, b1_ref,
-            fc2_ref, h_ref, a2_ref, z_ref, du_ref,
+            part_ref[...], ob_ref[...], dz_ref[...], wo_ref, gain_ref, bias_ref, fc1_ref, b1_ref[...], h_ref, a2_ref,
+            z_ref, du_ref,
         )
-
-    return chain.call(
-        kernel, "feed_far", (x, oa, packet, gain, bias, wo, fc1, fc2, *(a for a, _ in biases)),
-        [f32(rows, d), bf16(rows, d), bf16(rows, columns), bf16(rows, columns), f32(1, columns)], "v" * 12 + "-vvvvv",
-    )
-
-
-def feed_own(chain, x, packet, g, ob, gain, bias, wo, fc1, b1, fc2, far):
-    rows, d = x.shape
+        first_ref[...] = dot_tn(du_ref[:, :width], a2_ref[...])
+        second_ref[...] = dot_tn(z_ref[:, :width], g_ref[...])
+
+    return chain.call(
+        kernel, "feed_far", (h, ob, dz, g, gain, bias, wo, fc1, b1),
+        [f32(rows, d), bf16(rows, columns), f32(width, d), f32(width, d)], "v" * 9 + "-vvvv",
+        scratch=[pltpu.VMEM((rows, d), BF16), pltpu.VMEM((rows, columns), BF16)],
+    )
+
+
+def feed_own(chain, h, ob, dz, g, gain, bias, wo, fc1, b1, far):
+    rows, d = h.shape
     columns = fc1.shape[0]
     width = columns // 2
     shard = width // 2
 
-    def kernel(io, x_ref, oa_ref, g_ref, ob_ref, gain_ref, bias_ref, wo_ref, fc1_ref, b1_ref, fc2_ref, z1, du1, a1, g1,
-               h_ref, a2_ref, z_ref, du_ref, keep_ref, send_ref, sums_ref):
-        a2, z, du = feed_body(
-            x_ref[...], oa_ref[:, d:], ob_ref[...], g_ref[...], wo_ref, gain_ref, bias_ref, fc1_ref, b1_ref, fc2_ref,
-            h_ref, a2_ref, z_ref, du_ref,
+    def kernel(io, part_ref, ob_ref, dz_ref, g_ref, gain_ref, bias_ref, wo_ref, fc1_ref, b1_ref, du1, first1, second1,
+               h_ref, z_ref, du_ref, keep_ref, send_ref, sums_ref, a2_ref):
+        feed_body(
+            part_ref[...], ob_ref[...], dz_ref[...], wo_ref, gain_ref, bias_ref, fc1_ref, b1_ref[...], h_ref, a2_ref,
+            z_ref, du_ref,
         )
-        z, du = z[:, :width], du[:, :width]
-        first = dot_tn(du, a2) + dot_tn(du1[:, :width], a1[...])
-        second = dot_tn(z, g_ref[...]) + dot_tn(z1[:, :width], g1[:, :d])
+        du = du_ref[:, :width]
+        first = dot_tn(du, a2_ref[...]) + first1[...]
+        second = dot_tn(z_ref[:, :width], g_ref[...]) + second1[...]
         for at, ref in enumerate((keep_ref, send_ref)):
             here = slice(at * shard, (at + 1) * shard)
             ref[0] = first[here].astype(BF16)
@@ -414,9 +448,9 @@
         )
 
     return chain.call(
-        kernel, "feed_own", (x, packet, g, ob, gain, bias, wo, fc1, b1, fc2, *far),
-        [f32(rows, d), bf16(rows, d), bf16(rows, columns), bf16(rows, columns), bf16(2, shard, d), bf16(2, shard, d),
-         f32(1, width)], "v" * 14 + "-vvvvvvv",
+        kernel, "feed_own", (h, ob, dz, g, gain, bias, wo, fc1, b1, *far),
+        [f32(rows, d), bf16(rows, columns), bf16(rows, columns), bf16(2, shard, d), bf16(2, shard, d), f32(1, width)],
+        "v" * 12 + "-vvvvvv", scratch=[pltpu.VMEM((rows, d), BF16)],
     )
 
 
@@ -722,11 +756,11 @@
     far_masks = [1 << k for k in range(2, n_dp.bit_length() - 1)]
 
     w_got = swap_core(qkv_weight)
-    x_got = swap_y(tokens)
-    far_y = swap_y(pick(chain, bits, out_weight, fc1_weight, fc2_weight, fc1_bias))
-    bias = jnp.pad(fc1_bias.reshape(1, -1), ((0, 15), (0, d - shard)))
+    x_got, far_g = swap_y(tokens), swap_y(out_grad)
+    picked = pick(chain, bits, out_weight, fc1_weight, fc2_weight, fc1_bias)
+    far_y = swap_y(picked)
     near, others = load(
-        chain, out_weight, fc1_weight, fc2_weight, bias,
+        chain, out_weight, fc1_weight, fc2_weight, picked,
         (tokens, out_grad, ln1_gain, ln1_bias, ln2_gain, ln2_bias),
     )
     near = (near, swap_core(near))
@@ -734,11 +768,11 @@
 
     counts = (node_counts, edge_counts)
     norm1 = (ln1_gain, ln1_bias)
-    a1_0, qt_0, kt_0, v_0, p_0, ot_0, packet, w_qkv = attention(
-        chain, bits, 3, *counts, tokens, *norm1, (qkv_weight, w_got), out_grad
-    )
-    packet_got = swap_y(packet)
-    far_y, short = hold(chain, far_y)
+    a1_0, qt_0, kt_0, v_0, p_0, ot_0, o_0, w_qkv = attention(
+        chain, bits, 3, *counts, tokens, *norm1, (qkv_weight, w_got)
+    )
+    far_o = swap_y(o_0)
+    far_y, short = hold(chain, far_y, d)
     far_x, far_z = swap_dp(short, 1, 1), swap_dp(short, 2, 2)
     far_z, pair = pair_up(chain, far_x, far_z)
     far_xz = swap_dp(far_z, 1, 1)
@@ -753,6 +787,10 @@
     wo, fc1, fc2 = pack_far(chain, bits, (wo, fc1, fc2), fars)
     low, far_low = 3 * shard, 3 * shard // 4
     biases = ((near[0], low), (near[1], low), (fars[0], far_low), (fars[3], far_low))
+
+    part_0, part_1, dz_0, dz_1, b1 = feed_in(
+        chain, (tokens, x_got), (o_0, o_1), (out_grad, far_g), wo, fc2, biases
+    )
 
     class Sum:
         def __init__(self, count, keep, got, apart, early):
@@ -802,10 +840,10 @@
                 a, b = side_by_side(chain, *self.last, True)
                 self.quarters = [(a, 0, 0, 0), (b, 0, 0, 1), (swap_first(a), 0, 1, 0), (swap_first(b), 0, 1, 1)]
 
-    h_1, a2_1, z_1, du_1, b1 = feed_far(chain, x_got, o_1, packet_got, *norm2, wo, fc1, fc2, biases)
-    gh_1, dp_1 = backward(chain, (du_1, fc1, h_1, packet_got, ln2_gain, wo, p_1, qt_1, kt_1, v_1), False)
-    h_0, a2_0, z_0, du_0, keep_r, send_r, bias_sums = feed_own(
-        chain, tokens, packet, out_grad, o_got, *norm2, wo, fc1, b1, fc2, (z_1, du_1, a2_1, packet_got)
+    h_1, du_1, *far_r = feed_far(chain, part_1, far_o, dz_1, far_g, *norm2, wo, fc1, b1)
+    gh_1, dp_1 = backward(chain, (du_1, fc1, h_1, far_g, ln2_gain, wo, p_1, qt_1, kt_1, v_1), False)
+    h_0, z_0, du_0, keep_r, send_r, bias_sums = feed_own(
+        chain, part_0, o_got, dz_0, out_grad, *norm2, wo, fc1, b1, (du_1, *far_r)
     )
     gh_0, dp_0, dh, sums = backward(chain, (du_0, fc1, h_0, out_grad, ln2_gain, wo, p_0, qt_0, kt_0, v_0), True)
     r = Sum(2, keep_r, swap_core(send_r), True, 1)

time: 105 us -> 104 us (level)
  local copies, waits for them, and re-layouts: 1.41 us -> 0.09 us
    ppermute x5 -> x6, waiting for transfers between devices: 3.47 us -> 1.29 us  [swap_y(): return lax.ppermute(a, 'tensor', [(t, t ^ 2) for t in range(n_tensor)])]
    ppermute x18, waiting for transfers between devices: 26.2 us -> 27.9 us  [swap_dp(): return lax.ppermute(a, ('dp', 'tensor'), pairs)]
    pallas_call x32 -> x33, Pallas kernels: 36.8 us -> 37.8 us  [call(): pl.pallas_call(body, in_specs=[spec(kind) for kind in ins] + [vmem] * len...]
    ppermute x5 -> x6, starting transfers between devices: 7.43 us -> 8.19 us  [swap_y(): return lax.ppermute(a, 'tensor', [(t, t ^ 2) for t in range(n_tensor)])]
  transfers between devices with their start and end apart: 31 -> 32, of which waited for: 16 -> 15; matrix products, arithmetic and copies ran while one was open for 1% -> 0% of each run, Pallas kernels for 30% -> 32%
where the time goes in v9:
time: 104 us
  Pallas kernels  37.8 us (36%)
  starting transfers between devices  33.9 us (33%)
  waiting for transfers between devices  30.7 us (30%)
  between operations  1.15 us (1%)
    pallas_call x33, Pallas kernels, call(): pl.pallas_call(body, in_specs=[spec(kind) for kind in ins] + [vmem] * len...  37.8 us
    ppermute x18, waiting for transfers between devices, swap_dp(): return lax.ppermute(a, ('dp', 'tensor'), pairs)  27.9 us
    ppermute x18, starting transfers between devices, swap_dp(): return lax.ppermute(a, ('dp', 'tensor'), pairs)  24.4 us
    ppermute x6, starting transfers between devices, swap_y(): return lax.ppermute(a, 'tensor', [(t, t ^ 2) for t in range(n_tensor)])  8.19 us
  transfers between devices with their start and end apart: 32, of which 15 were waited for; matrix products, arithmetic and copies ran while one was open for 0% of the time, Pallas kernels for 32%

profile of v9, /device:TPU:0, one launch (start us, length us, event | category | flops | bytes accessed | tf_op | source)
XLA Modules:
  0.0 103.6 jit_solution(2969885725535126691)
XLA Ops:
  1.2 1.6 %pick.1 = (bf16[448,256]{1,0:T(8,128)(2,1)S(1)}, f32[8,128]{1,0:T(8,128)S(1)}) custom-call(s32[7]{0:T(128)S(1)} %stack.31.refs_0_, bf16[192,768]{1,0:T(8,128)(2,1)} %refs_0_.1, bf16[192,768]{1,0:T(8,128)(2,1)} %refs_1_.5, bf16[192,768]{1,0:T(8,128)(2,1)} %refs_2_.5, bf16[192]{0:T(256)(128)(2,1)} %refs_4_.2), custom_call_target="tpu_custom_call" | custom-call | bytes 100000000 | tf_op jit(solution)/shard_map/pick/pallas_call | solution.py:145
  2.8 2.6 %collective-permute-start.3 = (bf16[448,256]{1,0:T(8,128)(2,1)S(1)}, bf16[448,256]{1,0:T(8,128)(2,1)S(1)}, u32[]{:S(2)}, u32[]{:S(2)}) collective-permute-start(bf16[448,256]{1,0:T(8,128)(2,1)S(1)} %get-tuple-element.129.refs_3_), channel_id=1, source_target_pairs={{0,2},{1,3},{2,0},{3,1},{4,6},{5,7},{6,4},{7,5},{8,10},{9,11},{10,... | collective-permute-start | bytes 688136 | tf_op jit(solution)/shard_map/ppermute | solution.py:744
  5.6 1.5 %load.1 = (bf16[592,768]{1,0:T(8,128)(2,1)S(1)}, bf16[256,768]{1,0:T(8,128)(2,1)S(1)}, bf16[256,768]{1,0:T(8,128)(2,1)S(1)}, f32[768]{0:T(1024)S(1)}, f32[768]{0...) custom-call(bf16[192,768]{1,0:T(8,128)(2,1)} %refs_0_.1, bf16[192,768]{1,0:T(8,128)(2,1)} %refs_1_.5, ...), custom_call_target="tpu_custom_call" | custom-call | bytes 100000000 | tf_op jit(solution)/shard_map/load/pallas_call | solution.py:145
  7.3 4.0 %attention_forward.2 = (bf16[256,768]{1,0:T(8,128)(2,1)S(1)}, bf16[384,256]{1,0:T(8,128)(2,1)S(1)}, bf16[384,256]{1,0:T(8,128)(2,1)S(1)}, bf16[256,384]{1,0:T(8,...) custom-call(s32[7]{0:T(128)S(1)} %stack.31.refs_0_, ...), custom_call_target="tpu_custom_call" | custom-call | flops 10000000000 | bytes 100000000 | tf_op jit(solution)/shard_map/attention_forward/pallas_call | solution.py:145
  12.0 1.9 %collective-permute-start.4 = (bf16[144,768]{1,0:T(8,128)(2,1)S(1)}, bf16[144,768]{1,0:T(8,128)(2,1)S(1)}, u32[]{:S(2)}, u32[]{:S(2)}) collective-permute-start(bf16[144,768]{1,0:T(8,128)(2,1)S(1)} %get-tuple-element.139), channel_id=1, source_target_pairs={{0,4},{1,5},{2,6},{3,7},{4,0},{5,1},{6,2},{7,3},{8,12},{9,13},{10,... | collective-permute-start | bytes 663560 | tf_op jit(solution)/shard_map/ppermute | solution.py:752
  13.9 1.7 %collective-permute-start.5 = (bf16[144,768]{1,0:T(8,128)(2,1)S(1)}, bf16[144,768]{1,0:T(8,128)(2,1)S(1)}, u32[]{:S(2)}, u32[]{:S(2)}) collective-permute-start(bf16[144,768]{1,0:T(8,128)(2,1)S(1)} %get-tuple-element.139), channel_id=1, source_target_pairs={{0,8},{1,9},{2,10},{3,11},{4,12},{5,13},{6,14},{7,15},{8,0},{9,1},... | collective-permute-start | bytes 663560 | tf_op jit(solution)/shard_map/ppermute | solution.py:752
  15.5 1.5 %collective-permute-start.6 = (bf16[256,768]{1,0:T(8,128)(2,1)S(1)}, bf16[256,768]{1,0:T(8,128)(2,1)S(1)}, u32[]{:S(2)}, u32[]{:S(2)}) collective-permute-start(bf16[256,768]{1,0:T(8,128)(2,1)S(1)} %copy-done), channel_id=1, source_target_pairs={{0,2},{1,3},{2,0},{3,1},{4,6},{5,7},{6,4},{7,5},{8,10},{9,11},{10,... | collective-permute-start | bytes 1179656 | tf_op jit(solution)/shard_map/ppermute | solution.py:744
  17.1 2.1 %collective-permute-done.4.refs_0_ = bf16[144,768]{1,0:T(8,128)(2,1)S(1)} collective-permute-done((bf16[144,768]{1,0:T(8,128)(2,1)S(1)}, bf16[144,768]{1,0:T(8,128)(2,1)S(1)}, u32[]{:S(2)}, u32[]{:S(2)}) %collective-permute-start.4) | collective-permute-done | bytes 221216 | tf_op jit(solution)/shard_map/ppermute | solution.py:752
  19.2 1.5 %collective-permute-done.5.refs_1_ = bf16[144,768]{1,0:T(8,128)(2,1)S(1)} collective-permute-done((bf16[144,768]{1,0:T(8,128)(2,1)S(1)}, bf16[144,768]{1,0:T(8,128)(2,1)S(1)}, u32[]{:S(2)}, u32[]{:S(2)}) %collective-permute-start.5) | collective-permute-done | bytes 221216 | tf_op jit(solution)/shard_map/ppermute | solution.py:752
  20.6 1.5 %collective-permute-start.12 = (bf16[256,384]{1,0:T(8,128)(2,1)S(1)}, bf16[256,384]{1,0:T(8,128)(2,1)S(1)}, u32[]{:S(2)}, u32[]{:S(2)}) collective-permute-start(bf16[256,384]{1,0:T(8,128)(2,1)S(1)} %get-tuple-element.135.refs_2_), channel_id=1, source_target_pairs={{0,2},{1,3},{2,0},{3,1},{4,6},{5,7},{6,4},{7,5},{8,10},{9,11},{10,... | collective-permute-start | bytes 589832 | tf_op jit(solution)/shard_map/ppermute | solution.py:744
  22.9 3.5 %attention_forward.3 = (bf16[256,768]{1,0:T(8,128)(2,1)S(1)}, bf16[384,256]{1,0:T(8,128)(2,1)S(1)}, bf16[384,256]{1,0:T(8,128)(2,1)S(1)}, bf16[256,384]{1,0:T(8,...) custom-call(s32[7]{0:T(128)S(1)} %stack.31.refs_0_, ...), custom_call_target="tpu_custom_call" | custom-call | flops 3000000000 | bytes 100000000 | tf_op jit(solution)/shard_map/attention_forward/pallas_call | solution.py:145
  27.3 1.5 %collective-permute-done.7.refs_6_ = bf16[144,768]{1,0:T(8,128)(2,1)S(1)} collective-permute-done((bf16[144,768]{1,0:T(8,128)(2,1)S(1)}, bf16[144,768]{1,0:T(8,128)(2,1)S(1)}, u32[]{:S(2)}, u32[]{:S(2)}) %collective-permute-start.7) | collective-permute-done | bytes 221216 | tf_op jit(solution)/shard_map/ppermute | solution.py:752
  28.8 1.5 %collective-permute-done.10.refs_9_ = bf16[144,768]{1,0:T(8,128)(2,1)S(1)} collective-permute-done((bf16[144,768]{1,0:T(8,128)(2,1)S(1)}, bf16[144,768]{1,0:T(8,128)(2,1)S(1)}, u32[]{:S(2)}, u32[]{:S(2)}) %collective-permute-start.10) | collective-permute-done | bytes 221216 | tf_op jit(solution)/shard_map/ppermute | solution.py:741
  30.2 0.9 pack_far.1
  31.1 1.2 %feed_in.1 = (f32[256,768]{1,0:T(8,128)S(1)}, f32[256,768]{1,0:T(8,128)S(1)}, f32[256,768]{1,0:T(8,128)S(1)}, f32[256,768]{1,0:T(8,128)S(1)}, f32[1,768]{1,0:T(1,128)S(1)}, /*index=5*/f32[8,128]{1,0:T(8,128)S(1)}) custom-call(bf16[256,768]{1,0:T(8,128)(2,1)S(1)} %get-tuple-element.131.refs_3_.refs_0_, ...), custom_call_target="tpu_custom_call" | custom-call | bytes 100000000 | tf_op jit(solution)/shard_map/feed_in/pallas_call | solution.py:145
  33.0 1.7 %feed_far.1 = (f32[256,768]{1,0:T(8,128)S(1)}, bf16[256,768]{1,0:T(8,128)(2,1)S(1)}, f32[384,768]{1,0:T(8,128)S(1)}, f32[384,768]{1,0:T(8,128)S(1)}, f32[8,128]{1,0:T(8,128)S(1)}) custom-call(f32[256,768]{1,0:T(8,128)S(1)} %get-tuple-element.160.refs_0_, bf16[256,384]{1,0:T(8,128)(2,1)S(1)} %collective-permute-done.12.refs_1_, ...), custom_call_target="tpu_custom_call" | custom-call | bytes 100000000 | tf_op jit(solution)/shard_map/feed_far/pallas_call | solution.py:145
  34.7 2.5 %attention_backward.2 = (bf16[256,768]{1,0:T(8,128)(2,1)S(1)}, bf16[1152,256]{1,0:T(8,128)(2,1)S(1)}, f32[8,128]{1,0:T(8,128)S(1)}) custom-call(bf16[256,768]{1,0:T(8,128)(2,1)S(1)} %get-tuple-element.163.refs_0_.refs_9_, bf16[768,768]{1,0:T(8,128)(2,1)S(1)} %get-tuple-element.158.refs_7_.refs_1_, f32[256,768]{1,0:T(8,128)S(1)} %get-tuple-element.166.refs_2_, ...), custom_call_target="tpu_custom_call" | custom-call | bytes 100000000 | tf_op jit(solution)/shard_map/attention_backward/pallas_call | solution.py:145
  37.3 1.8 %feed_own.1 = (f32[256,768]{1,0:T(8,128)S(1)}, bf16[256,768]{1,0:T(8,128)(2,1)S(1)}, bf16[256,768]{1,0:T(8,128)(2,1)S(1)}, bf16[2,192,768]{2,1,0:T(8,128)(2,1)S(...) custom-call(f32[256,768]{1,0:T(8,128)S(1)} %get-tuple-element.154.refs_0_, ...), custom_call_target="tpu_custom_call" | custom-call | bytes 100000000 | tf_op jit(solution)/shard_map/feed_own/pallas_call | solution.py:145
  39.2 2.5 %attention_backward.3 = (bf16[256,768]{1,0:T(8,128)(2,1)S(1)}, bf16[1152,256]{1,0:T(8,128)(2,1)S(1)}, f32[256,768]{1,0:T(8,128)S(1)}, f32[8,768]{1,0:T(8,128)S(1)}, f32[8,128]{1,0:T(8,128)S(1)}) custom-call(bf16[256,768]{1,0:T(8,128)(2,1)S(1)} %get-tuple-element.177.refs_0_, bf16[768,768]{1,0:T(8,128)(2,1)S(1)} %get-tuple-element.158.refs_7_.refs_1_, ...), custom_call_target="tpu_custom_call" | custom-call | flops 10000000000 | bytes 100000000 | tf_op jit(solution)/shard_map/attention_backward/pallas_call | solution.py:145
  42.2 1.9 %collective-permute-start.15 = (bf16[96,768]{1,0:T(8,128)(2,1)S(1)}, bf16[96,768]{1,0:T(8,128)(2,1)S(1)}, u32[]{:S(2)}, u32[]{:S(2)}) collective-permute-start(bf16[96,768]{1,0:T(8,128)(2,1)S(1)} %get-tuple-element.185), channel_id=1, source_target_pairs={{0,4},{1,9},{2,6},{3,11},{4,0},{5,13},{6,2},{7,15},{8,12},{9,1},{1... | collective-permute-start | bytes 442376 | tf_op jit(solution)/shard_map/ppermute | solution.py:752
  46.2 1.6 %collective-permute-start.14 = (bf16[96,768]{1,0:T(8,128)(2,1)S(1)}, bf16[96,768]{1,0:T(8,128)(2,1)S(1)}, u32[]{:S(2)}, u32[]{:S(2)}) collective-permute-start(bf16[96,768]{1,0:T(8,128)(2,1)S(1)} %get-tuple-element.184), channel_id=1, source_target_pairs={{0,4},{1,9},{2,6},{3,11},{4,0},{5,13},{6,2},{7,15},{8,12},{9,1},{1... | collective-permute-start | bytes 442376 | tf_op jit(solution)/shard_map/ppermute | solution.py:752
  48.3 1.7 %collective-permute-start.16 = (bf16[96,768]{1,0:T(8,128)(2,1)S(1)}, bf16[96,768]{1,0:T(8,128)(2,1)S(1)}, u32[]{:S(2)}, u32[]{:S(2)}) collective-permute-start(bf16[96,768]{1,0:T(8,128)(2,1)S(1)} %get-tuple-element.197), channel_id=1, source_target_pairs={{0,8},{1,5},{2,10},{3,7},{4,12},{5,1},{6,14},{7,3},{8,0},{9,13},{1... | collective-permute-start | bytes 442376 | tf_op jit(solution)/shard_map/ppermute | solution.py:752
  50.7 1.6 %collective-permute-start.19 = (bf16[192,768]{1,0:T(8,128)(2,1)S(1)}, bf16[192,768]{1,0:T(8,128)(2,1)S(1)}, u32[]{:S(2)}, u32[]{:S(2)}) collective-permute-start(bf16[192,768]{1,0:T(8,128)(2,1)S(1)} %get-tuple-element.205), channel_id=1, source_target_pairs={{0,4},{1,9},{2,6},{3,11},{4,0},{5,13},{6,2},{7,15},{8,12},{9,1},{1... | collective-permute-start | bytes 884744 | tf_op jit(solution)/shard_map/ppermute | solution.py:752
  52.3 2.2 %collective-permute-done.16.refs_4_ = bf16[96,768]{1,0:T(8,128)(2,1)S(1)} collective-permute-done((bf16[96,768]{1,0:T(8,128)(2,1)S(1)}, bf16[96,768]{1,0:T(8,128)(2,1)S(1)}, u32[]{:S(2)}, u32[]{:S(2)}) %collective-permute-start.16) | collective-permute-done | bytes 147488 | tf_op jit(solution)/shard_map/ppermute | solution.py:752
  55.2 3.0 %collective-permute-start.18 = (bf16[96,768]{1,0:T(8,128)(2,1)S(1)}, bf16[96,768]{1,0:T(8,128)(2,1)S(1)}, u32[]{:S(2)}, u32[]{:S(2)}) collective-permute-start(bf16[96,768]{1,0:T(8,128)(2,1)S(1)} %get-tuple-element.202.refs_0_), channel_id=1, source_target_pairs={{0,16},{1,17},{2,18},{3,19},{4,20},{5,21},{6,22},{7,23},{8,24},{9,... | collective-permute-start | bytes 442376 | tf_op jit(solution)/shard_map/ppermute | solution.py:752
  58.2 1.4 %collective-permute-start.21 = (bf16[192,768]{1,0:T(8,128)(2,1)S(1)}, bf16[192,768]{1,0:T(8,128)(2,1)S(1)}, u32[]{:S(2)}, u32[]{:S(2)}) collective-permute-start(bf16[192,768]{1,0:T(8,128)(2,1)S(1)} %get-tuple-element.214), channel_id=1, source_target_pairs={{0,4},{1,9},{2,6},{3,11},{4,0},{5,13},{6,2},{7,15},{8,12},{9,1},{1... | collective-permute-start | bytes 884744 | tf_op jit(solution)/shard_map/ppermute | solution.py:752
  60.3 2.0 %collective-permute-start.22 = (bf16[192,768]{1,0:T(8,128)(2,1)S(1)}, bf16[192,768]{1,0:T(8,128)(2,1)S(1)}, u32[]{:S(2)}, u32[]{:S(2)}) collective-permute-start(bf16[192,768]{1,0:T(8,128)(2,1)S(1)} %get-tuple-element.215), channel_id=1, source_target_pairs={{0,8},{1,5},{2,10},{3,7},{4,12},{5,1},{6,14},{7,3},{8,0},{9,13},{1... | collective-permute-start | bytes 884744 | tf_op jit(solution)/shard_map/ppermute | solution.py:752
  62.3 1.4 %input_grads.1 = (f32[256,768]{1,0:T(8,128)S(1)}, bf16[272,768]{1,0:T(8,128)(2,1)S(1)}, f32[8,128]{1,0:T(8,128)S(1)}) custom-call(bf16[1152,256]{1,0:T(8,128)(2,1)S(1)} %get-tuple-element.186.refs_0_.refs_4_.refs_8_, bf16[1152,256]{1,0:T(8,128)(2,1)S(1)} %get-tuple-element.187.refs_1_.refs_5_.refs_9_, ...), custom_call_target="tpu_custom_call" | custom-call | bytes 100000000 | tf_op jit(solution)/shard_map/input_grads/pallas_call | solution.py:145
  63.7 1.6 %collective-permute-start.20 = (bf16[272,768]{1,0:T(8,128)(2,1)S(1)}, bf16[272,768]{1,0:T(8,128)(2,1)S(1)}, u32[]{:S(2)}, u32[]{:S(2)}) collective-permute-start(bf16[272,768]{1,0:T(8,128)(2,1)S(1)} %get-tuple-element.212.refs_0_), channel_id=1, source_target_pairs={{0,2},{1,3},{2,0},{3,1},{4,6},{5,7},{6,4},{7,5},{8,10},{9,11},{10,... | collective-permute-start | bytes 1253384 | tf_op jit(solution)/shard_map/ppermute | solution.py:744
  65.5 1.2 %feed_result.1 = (bf16[256,768]{1,0:T(8,128)(2,1)}, f32[8,128]{1,0:T(8,128)S(1)}) custom-call(bf16[256,768]{1,0:T(8,128)(2,1)S(1)} %get-tuple-element.173.refs_0_, bf16[768,768]{1,0:T(8,128)(2,1)S(1)} %get-tuple-element.152.refs_7_.refs_1_, f32[256,768]{1,0:T(8,128)S(1)} %get-tuple-element.174.refs_2_, f32[8,128]{1,0:T(8,128)S(1)} %get-tuple-element.209.refs_3_), custom_call_target="tpu_custom_call" | custom-call | bytes 100000000 | tf_op jit(solution)/shard_map/feed_result/pallas_call | solution.py:145
  66.8 1.3 %collective-permute-done.21.refs_3_ = bf16[192,768]{1,0:T(8,128)(2,1)S(1)} collective-permute-done((bf16[192,768]{1,0:T(8,128)(2,1)S(1)}, bf16[192,768]{1,0:T(8,128)(2,1)S(1)}, u32[]{:S(2)}, u32[]{:S(2)}) %collective-permute-start.21) | collective-permute-done | bytes 294944 | tf_op jit(solution)/shard_map/ppermute | solution.py:752
  68.8 0.9 collective-permute-start.23
  69.7 1.4 %collective-permute-start.26 = (bf16[96,768]{1,0:T(8,128)(2,1)S(1)}, bf16[96,768]{1,0:T(8,128)(2,1)S(1)}, u32[]{:S(2)}, u32[]{:S(2)}) collective-permute-start(bf16[96,768]{1,0:T(8,128)(2,1)S(1)} %get-tuple-element.220.refs_1_), channel_id=1, source_target_pairs={{0,4},{1,9},{2,6},{3,11},{4,0},{5,13},{6,2},{7,15},{8,12},{9,1},{1... | collective-permute-start | bytes 442376 | tf_op jit(solution)/shard_map/ppermute | solution.py:752
  71.1 0.9 collective-permute-done.25.refs_2_
  72.1 2.8 %collective-permute-done.26.refs_3_ = bf16[96,768]{1,0:T(8,128)(2,1)S(1)} collective-permute-done((bf16[96,768]{1,0:T(8,128)(2,1)S(1)}, bf16[96,768]{1,0:T(8,128)(2,1)S(1)}, u32[]{:S(2)}, u32[]{:S(2)}) %collective-permute-start.26) | collective-permute-done | bytes 147488 | tf_op jit(solution)/shard_map/ppermute | solution.py:752
  74.9 2.3 %collective-permute-done.27.refs_4_ = bf16[96,768]{1,0:T(8,128)(2,1)S(1)} collective-permute-done((bf16[96,768]{1,0:T(8,128)(2,1)S(1)}, bf16[96,768]{1,0:T(8,128)(2,1)S(1)}, u32[]{:S(2)}, u32[]{:S(2)}) %collective-permute-start.27) | collective-permute-done | bytes 147488 | tf_op jit(solution)/shard_map/ppermute | solution.py:752
  77.1 1.7 %place_sums.4 = (f32[192,768]{1,0:T(8,128)}, f32[192,768]{1,0:T(8,128)}, f32[8,128]{1,0:T(8,128)S(1)}) custom-call(s32[7]{0:T(128)S(1)} %stack.31.refs_0_, bf16[96,768]{1,0:T(8,128)(2,1)S(1)} %get-tuple-element.220.refs_1_, bf16[96,768]{1,0:T(8,128)(2,1)S(1)} %collective-permute-done.25.refs_2_, bf16[96,768]{1,0:T(8,128)(2,1)S(1)} %collective-permute-done.26.refs_3_, ...), custom_call_target="tpu_custom_call" | custom-call | bytes 100000000 | tf_op jit(solution)/shard_map/place_sums/pallas_call | solution.py:145
  78.9 1.5 %collective-permute-start.28 = (bf16[16,768]{1,0:T(8,128)(2,1)S(1)}, bf16[16,768]{1,0:T(8,128)(2,1)S(1)}, u32[]{:S(2)}, u32[]{:S(2)}) collective-permute-start(bf16[16,768]{1,0:T(8,128)(2,1)S(1)} %get-tuple-element.223.refs_2_), channel_id=1, source_target_pairs={{0,16},{1,17},{2,18},{3,19},{4,20},{5,21},{6,22},{7,23},{8,24},{9,... | collective-permute-start | bytes 73736 | tf_op jit(solution)/shard_map/ppermute | solution.py:752
  80.4 3.3 %collective-permute-done.28.refs_3_ = bf16[16,768]{1,0:T(8,128)(2,1)S(1)} collective-permute-done((bf16[16,768]{1,0:T(8,128)(2,1)S(1)}, bf16[16,768]{1,0:T(8,128)(2,1)S(1)}, u32[]{:S(2)}, u32[]{:S(2)}) %collective-permute-start.28) | collective-permute-done | bytes 24608 | tf_op jit(solution)/shard_map/ppermute | solution.py:752
  83.8 0.9 collective-permute-start.29
  84.7 1.3 %input_norm.1 = (bf16[256,768]{1,0:T(8,128)(2,1)}, f32[8,128]{1,0:T(8,128)S(1)}) custom-call(bf16[256,768]{1,0:T(8,128)(2,1)S(1)} %get-tuple-element.131.refs_3_.refs_0_, f32[768]{0:T(1024)S(1)} %get-tuple-element.132.refs_4_.refs_1_, f32[256,768]{1,0:T(8,128)S(1)} %get-tuple-element.211.refs_2_, ...), custom_call_target="tpu_custom_call" | custom-call | bytes 100000000 | tf_op jit(solution)/shard_map/input_norm/pallas_call | solution.py:145
  86.0 4.8 %collective-permute-done.29.refs_1_ = bf16[208,768]{1,0:T(8,128)(2,1)S(1)} collective-permute-done((bf16[208,768]{1,0:T(8,128)(2,1)S(1)}, bf16[208,768]{1,0:T(8,128)(2,1)S(1)}, u32[]{:S(2)}, u32[]{:S(2)}) %collective-permute-start.29) | collective-permute-done | bytes 319520 | tf_op jit(solution)/shard_map/ppermute | solution.py:752
  91.7 1.3 %collective-permute-start.31 = (bf16[208,768]{1,0:T(8,128)(2,1)S(1)}, bf16[208,768]{1,0:T(8,128)(2,1)S(1)}, u32[]{:S(2)}, u32[]{:S(2)}) collective-permute-start(bf16[208,768]{1,0:T(8,128)(2,1)S(1)} %get-tuple-element.230.refs_2_), channel_id=1, source_target_pairs={{0,4},{1,9},{2,6},{3,11},{4,0},{5,13},{6,2},{7,15},{8,12},{9,1},{1... | collective-permute-start | bytes 958472 | tf_op jit(solution)/shard_map/ppermute | solution.py:752
  93.0 1.6 %place_sums.5 = (f32[3,192,768]{2,1,0:T(8,128)}, f32[192,768]{1,0:T(8,128)}, f32[8,128]{1,0:T(8,128)S(1)}) custom-call(s32[7]{0:T(128)S(1)} %stack.31.refs_0_, bf16[208,768]{1,0:T(8,128)(2,1)S(1)} %get-tuple-element.229.refs_1_, bf16[208,768]{1,0:T(8,128)(2,1)S(1)} %get-tuple-element.230.refs_2_, f32[8,128]{1,0:T(8,128)S(1)} %get-tuple-element.231.refs_3_), custom_call_target="tpu_custom_call" | custom-call | bytes 100000000 | tf_op jit(solution)/shard_map/place_sums/pallas_call | solution.py:145
  94.6 3.3 %collective-permute-done.30.refs_3_ = bf16[208,768]{1,0:T(8,128)(2,1)S(1)} collective-permute-done((bf16[208,768]{1,0:T(8,128)(2,1)S(1)}, bf16[208,768]{1,0:T(8,128)(2,1)S(1)}, u32[]{:S(2)}, u32[]{:S(2)}) %collective-permute-start.30) | collective-permute-done | bytes 319520 | tf_op jit(solution)/shard_map/ppermute | solution.py:752
  97.9 1.4 %place_sums.6 = (f32[3,192,768]{2,1,0:T(8,128)}, f32[192,768]{1,0:T(8,128)}, f32[8,128]{1,0:T(8,128)S(1)}) custom-call(s32[7]{0:T(128)S(1)} %stack.31.refs_0_, bf16[208,768]{1,0:T(8,128)(2,1)S(1)} %get-tuple-element.229.refs_1_, bf16[208,768]{1,0:T(8,128)(2,1)S(1)} %get-tuple-element.230.refs_2_, ...), custom_call_target="tpu_custom_call", output_to_operand_aliasing={{0}: (4, {}), {1}: (5, {})} | custom-call | bytes 100000000 | tf_op jit(solution)/shard_map/place_sums/pallas_call | solution.py:145
  99.4 2.0 %collective-permute-done.31.refs_4_ = bf16[208,768]{1,0:T(8,128)(2,1)S(1)} collective-permute-done((bf16[208,768]{1,0:T(8,128)(2,1)S(1)}, bf16[208,768]{1,0:T(8,128)(2,1)S(1)}, u32[]{:S(2)}, u32[]{:S(2)}) %collective-permute-start.31) | collective-permute-done | bytes 319520 | tf_op jit(solution)/shard_map/ppermute | solution.py:752
  101.4 2.0 %place_sums.7 = (f32[3,192,768]{2,1,0:T(8,128)}, f32[192,768]{1,0:T(8,128)}, f32[768]{0:T(1024)}, f32[768]{0:T(1024)}, f32[768]{0:T(1024)}, /*index=5*/f32[768]{0:T(1024)}, f32[192]{0:T(256)}, f32[8,128]{1,0:T(8,128)}) custom-call(s32[7]{0:T(128)S(1)} %stack.31.refs_0_, ...), custom_call_target="tpu_custom_call", output_to_operand_aliasing={{0}: (5, {}), {1}: (6, {})} | custom-call | bytes 100000000 | tf_op jit(solution)/shard_map/place_sums/pallas_call | solution.py:145
  (52 shorter events, 11.1 us)
Async XLA Ops:
  0.6 6.6 %collective-permute-start.1 = (bf16[3,192,768]{2,1,0:T(8,128)(2,1)}, bf16[3,192,768]{2,1,0:T(8,128)(2,1)S(1)}, u32[]{:S(2)}, u32[]{:S(2)}) collective-permute-start(bf16[3,192,768]{2,1,0:T(8,128)(2,1)} %refs_6_.3), channel_id=1, source_target_pairs={{0,1},{1,0},{2,3},{3,2},{4,5},{5,4},{6,7},{7,6},{8,9},{9,8},{10,11... | collective-permute-start | bytes 2654216 | tf_op jit(solution)/shard_map/ppermute | solution.py:741
  2.8 9.1 %collective-permute-start.3 = (bf16[448,256]{1,0:T(8,128)(2,1)S(1)}, bf16[448,256]{1,0:T(8,128)(2,1)S(1)}, u32[]{:S(2)}, u32[]{:S(2)}) collective-permute-start(bf16[448,256]{1,0:T(8,128)(2,1)S(1)} %get-tuple-element.129.refs_3_), channel_id=1, source_target_pairs={{0,2},{1,3},{2,0},{3,1},{4,6},{5,7},{6,4},{7,5},{8,10},{9,11},{10,... | collective-permute-start | bytes 688136 | tf_op jit(solution)/shard_map/ppermute | solution.py:744
  5.5 16.7 %collective-permute-start = (bf16[256,768]{1,0:T(8,128)(2,1)}, bf16[256,768]{1,0:T(8,128)(2,1)S(1)}, u32[]{:S(2)}, u32[]{:S(2)}) collective-permute-start(bf16[256,768]{1,0:T(8,128)(2,1)} %refs_4_.3), channel_id=1, source_target_pairs={{0,2},{1,3},{2,0},{3,1},{4,6},{5,7},{6,4},{7,5},{8,10},{9,11},{10,... | collective-permute-start | bytes 1179656 | tf_op jit(solution)/shard_map/ppermute | solution.py:744
  7.1 15.9 %collective-permute-start.2 = (bf16[592,768]{1,0:T(8,128)(2,1)S(1)}, bf16[592,768]{1,0:T(8,128)(2,1)S(1)}, u32[]{:S(2)}, u32[]{:S(2)}) collective-permute-start(bf16[592,768]{1,0:T(8,128)(2,1)S(1)} %get-tuple-element.137.refs_7_.refs_8_), channel_id=1, source_target_pairs={{0,1},{1,0},{2,3},{3,2},{4,5},{5,4},{6,7},{7,6},{8,9},{9,8},{10,11... | collective-permute-start | bytes 2727944 | tf_op jit(solution)/shard_map/ppermute | solution.py:741
  7.3 8.3 %copy-start = (bf16[256,768]{1,0:T(8,128)(2,1)S(1)}, bf16[256,768]{1,0:T(8,128)(2,1)}, u32[]{:S(2)}) copy-start(bf16[256,768]{1,0:T(8,128)(2,1)} %refs_5_.1) | copy-start | bytes 1179652
  12.0 7.2 %collective-permute-start.4 = (bf16[144,768]{1,0:T(8,128)(2,1)S(1)}, bf16[144,768]{1,0:T(8,128)(2,1)S(1)}, u32[]{:S(2)}, u32[]{:S(2)}) collective-permute-start(bf16[144,768]{1,0:T(8,128)(2,1)S(1)} %get-tuple-element.139), channel_id=1, source_target_pairs={{0,4},{1,5},{2,6},{3,7},{4,0},{5,1},{6,2},{7,3},{8,12},{9,13},{10,... | collective-permute-start | bytes 663560 | tf_op jit(solution)/shard_map/ppermute | solution.py:752
  13.9 6.8 %collective-permute-start.5 = (bf16[144,768]{1,0:T(8,128)(2,1)S(1)}, bf16[144,768]{1,0:T(8,128)(2,1)S(1)}, u32[]{:S(2)}, u32[]{:S(2)}) collective-permute-start(bf16[144,768]{1,0:T(8,128)(2,1)S(1)} %get-tuple-element.139), channel_id=1, source_target_pairs={{0,8},{1,9},{2,10},{3,11},{4,12},{5,13},{6,14},{7,15},{8,0},{9,1},... | collective-permute-start | bytes 663560 | tf_op jit(solution)/shard_map/ppermute | solution.py:752
  15.5 15.6 %collective-permute-start.6 = (bf16[256,768]{1,0:T(8,128)(2,1)S(1)}, bf16[256,768]{1,0:T(8,128)(2,1)S(1)}, u32[]{:S(2)}, u32[]{:S(2)}) collective-permute-start(bf16[256,768]{1,0:T(8,128)(2,1)S(1)} %copy-done), channel_id=1, source_target_pairs={{0,2},{1,3},{2,0},{3,1},{4,6},{5,7},{6,4},{7,5},{8,10},{9,11},{10,... | collective-permute-start | bytes 1179656 | tf_op jit(solution)/shard_map/ppermute | solution.py:744
  19.2 7.3 %collective-permute-start.8 = (bf16[160,768]{1,0:T(8,128)(2,1)S(1)}, bf16[160,768]{1,0:T(8,128)(2,1)S(1)}, u32[]{:S(2)}, u32[]{:S(2)}) collective-permute-start(bf16[160,768]{1,0:T(8,128)(2,1)S(1)} %get-tuple-element.147.refs_4_.refs_10_), channel_id=1, source_target_pairs={{0,1},{1,0},{2,3},{3,2},{4,5},{5,4},{6,7},{7,6},{8,9},{9,8},{10,11... | collective-permute-start | bytes 737288 | tf_op jit(solution)/shard_map/ppermute | solution.py:741
  20.6 12.4 %collective-permute-start.12 = (bf16[256,384]{1,0:T(8,128)(2,1)S(1)}, bf16[256,384]{1,0:T(8,128)(2,1)S(1)}, u32[]{:S(2)}, u32[]{:S(2)}) collective-permute-start(bf16[256,384]{1,0:T(8,128)(2,1)S(1)} %get-tuple-element.135.refs_2_), channel_id=1, source_target_pairs={{0,2},{1,3},{2,0},{3,1},{4,6},{5,7},{6,4},{7,5},{8,10},{9,11},{10,... | collective-permute-start | bytes 589832 | tf_op jit(solution)/shard_map/ppermute | solution.py:744
  22.2 6.5 %collective-permute-start.7 = (bf16[144,768]{1,0:T(8,128)(2,1)S(1)}, bf16[144,768]{1,0:T(8,128)(2,1)S(1)}, u32[]{:S(2)}, u32[]{:S(2)}) collective-permute-start(bf16[144,768]{1,0:T(8,128)(2,1)S(1)} %get-tuple-element.149), channel_id=1, source_target_pairs={{0,4},{1,5},{2,6},{3,7},{4,0},{5,1},{6,2},{7,3},{8,12},{9,13},{10,... | collective-permute-start | bytes 663560 | tf_op jit(solution)/shard_map/ppermute | solution.py:752
  22.9 7.3 %collective-permute-start.9 = (bf16[2,144,768]{2,1,0:T(8,128)(2,1)S(1)}, bf16[2,144,768]{2,1,0:T(8,128)(2,1)S(1)}, u32[]{:S(2)}, u32[]{:S(2)}) collective-permute-start(bf16[2,144,768]{2,1,0:T(8,128)(2,1)S(1)} %get-tuple-element.148.refs_5_), channel_id=1, source_target_pairs={{0,1},{1,0},{2,3},{3,2},{4,5},{5,4},{6,7},{7,6},{8,9},{9,8},{10,11... | collective-permute-start | bytes 1327112 | tf_op jit(solution)/shard_map/ppermute | solution.py:741
  26.5 10.8 %collective-permute-start.11 = (bf16[256,384]{1,0:T(8,128)(2,1)S(1)}, bf16[256,384]{1,0:T(8,128)(2,1)S(1)}, u32[]{:S(2)}, u32[]{:S(2)}) collective-permute-start(bf16[256,384]{1,0:T(8,128)(2,1)S(1)} %get-tuple-element.142.refs_3_), channel_id=1, source_target_pairs={{0,2},{1,3},{2,0},{3,1},{4,6},{5,7},{6,4},{7,5},{8,10},{9,11},{10,... | collective-permute-start | bytes 589832 | tf_op jit(solution)/shard_map/ppermute | solution.py:744
  28.8 1.5 %collective-permute-start.10 = (bf16[144,768]{1,0:T(8,128)(2,1)S(1)}, bf16[144,768]{1,0:T(8,128)(2,1)S(1)}, u32[]{:S(2)}, u32[]{:S(2)}) collective-permute-start(bf16[144,768]{1,0:T(8,128)(2,1)S(1)} %collective-permute-done.7.refs_6_), channel_id=1, source_target_pairs={{0,1},{1,0},{2,3},{3,2},{4,5},{5,4},{6,7},{7,6},{8,9},{9,8},{10,11... | collective-permute-start | bytes 663560 | tf_op jit(solution)/shard_map/ppermute | solution.py:741
  39.1 2.6 %collective-permute-start.13 = (bf16[2,192,768]{2,1,0:T(8,128)(2,1)S(1)}, bf16[2,192,768]{2,1,0:T(8,128)(2,1)S(1)}, u32[]{:S(2)}, u32[]{:S(2)}) collective-permute-start(bf16[2,192,768]{2,1,0:T(8,128)(2,1)S(1)} %get-tuple-element.176), channel_id=1, source_target_pairs={{0,1},{1,0},{2,3},{3,2},{4,5},{5,4},{6,7},{7,6},{8,9},{9,8},{10,11... | collective-permute-start | bytes 1769480 | tf_op jit(solution)/shard_map/ppermute | solution.py:741
  42.2 5.5 %collective-permute-start.15 = (bf16[96,768]{1,0:T(8,128)(2,1)S(1)}, bf16[96,768]{1,0:T(8,128)(2,1)S(1)}, u32[]{:S(2)}, u32[]{:S(2)}) collective-permute-start(bf16[96,768]{1,0:T(8,128)(2,1)S(1)} %get-tuple-element.185), channel_id=1, source_target_pairs={{0,4},{1,9},{2,6},{3,11},{4,0},{5,13},{6,2},{7,15},{8,12},{9,1},{1... | collective-permute-start | bytes 442376 | tf_op jit(solution)/shard_map/ppermute | solution.py:752
  45.8 4.3 %collective-permute-start.17 = (bf16[4,192,768]{2,1,0:T(8,128)(2,1)S(1)}, bf16[4,192,768]{2,1,0:T(8,128)(2,1)S(1)}, u32[]{:S(2)}, u32[]{:S(2)}) collective-permute-start(bf16[4,192,768]{2,1,0:T(8,128)(2,1)S(1)} %get-tuple-element.199), channel_id=1, source_target_pairs={{0,1},{1,0},{2,3},{3,2},{4,5},{5,4},{6,7},{7,6},{8,9},{9,8},{10,11... | collective-permute-start | bytes 3538952 | tf_op jit(solution)/shard_map/ppermute | solution.py:741
  46.2 6.2 %collective-permute-start.14 = (bf16[96,768]{1,0:T(8,128)(2,1)S(1)}, bf16[96,768]{1,0:T(8,128)(2,1)S(1)}, u32[]{:S(2)}, u32[]{:S(2)}) collective-permute-start(bf16[96,768]{1,0:T(8,128)(2,1)S(1)} %get-tuple-element.184), channel_id=1, source_target_pairs={{0,4},{1,9},{2,6},{3,11},{4,0},{5,13},{6,2},{7,15},{8,12},{9,1},{1... | collective-permute-start | bytes 442376 | tf_op jit(solution)/shard_map/ppermute | solution.py:752
  48.3 6.2 %collective-permute-start.16 = (bf16[96,768]{1,0:T(8,128)(2,1)S(1)}, bf16[96,768]{1,0:T(8,128)(2,1)S(1)}, u32[]{:S(2)}, u32[]{:S(2)}) collective-permute-start(bf16[96,768]{1,0:T(8,128)(2,1)S(1)} %get-tuple-element.197), channel_id=1, source_target_pairs={{0,8},{1,5},{2,10},{3,7},{4,12},{5,1},{6,14},{7,3},{8,0},{9,13},{1... | collective-permute-start | bytes 442376 | tf_op jit(solution)/shard_map/ppermute | solution.py:752
  50.7 8.9 %collective-permute-start.19 = (bf16[192,768]{1,0:T(8,128)(2,1)S(1)}, bf16[192,768]{1,0:T(8,128)(2,1)S(1)}, u32[]{:S(2)}, u32[]{:S(2)}) collective-permute-start(bf16[192,768]{1,0:T(8,128)(2,1)S(1)} %get-tuple-element.205), channel_id=1, source_target_pairs={{0,4},{1,9},{2,6},{3,11},{4,0},{5,13},{6,2},{7,15},{8,12},{9,1},{1... | collective-permute-start | bytes 884744 | tf_op jit(solution)/shard_map/ppermute | solution.py:752
  55.2 10.1 %collective-permute-start.18 = (bf16[96,768]{1,0:T(8,128)(2,1)S(1)}, bf16[96,768]{1,0:T(8,128)(2,1)S(1)}, u32[]{:S(2)}, u32[]{:S(2)}) collective-permute-start(bf16[96,768]{1,0:T(8,128)(2,1)S(1)} %get-tuple-element.202.refs_0_), channel_id=1, source_target_pairs={{0,16},{1,17},{2,18},{3,19},{4,20},{5,21},{6,22},{7,23},{8,24},{9,... | collective-permute-start | bytes 442376 | tf_op jit(solution)/shard_map/ppermute | solution.py:752
  58.2 9.9 %collective-permute-start.21 = (bf16[192,768]{1,0:T(8,128)(2,1)S(1)}, bf16[192,768]{1,0:T(8,128)(2,1)S(1)}, u32[]{:S(2)}, u32[]{:S(2)}) collective-permute-start(bf16[192,768]{1,0:T(8,128)(2,1)S(1)} %get-tuple-element.214), channel_id=1, source_target_pairs={{0,4},{1,9},{2,6},{3,11},{4,0},{5,13},{6,2},{7,15},{8,12},{9,1},{1... | collective-permute-start | bytes 884744 | tf_op jit(solution)/shard_map/ppermute | solution.py:752
  60.3 7.8 %collective-permute-start.22 = (bf16[192,768]{1,0:T(8,128)(2,1)S(1)}, bf16[192,768]{1,0:T(8,128)(2,1)S(1)}, u32[]{:S(2)}, u32[]{:S(2)}) collective-permute-start(bf16[192,768]{1,0:T(8,128)(2,1)S(1)} %get-tuple-element.215), channel_id=1, source_target_pairs={{0,8},{1,5},{2,10},{3,7},{4,12},{5,1},{6,14},{7,3},{8,0},{9,13},{1... | collective-permute-start | bytes 884744 | tf_op jit(solution)/shard_map/ppermute | solution.py:752
  63.7 8.3 %collective-permute-start.20 = (bf16[272,768]{1,0:T(8,128)(2,1)S(1)}, bf16[272,768]{1,0:T(8,128)(2,1)S(1)}, u32[]{:S(2)}, u32[]{:S(2)}) collective-permute-start(bf16[272,768]{1,0:T(8,128)(2,1)S(1)} %get-tuple-element.212.refs_0_), channel_id=1, source_target_pairs={{0,2},{1,3},{2,0},{3,1},{4,6},{5,7},{6,4},{7,5},{8,10},{9,11},{10,... | collective-permute-start | bytes 1253384 | tf_op jit(solution)/shard_map/ppermute | solution.py:744
  65.4 6.6 %collective-permute-start.25 = (bf16[96,768]{1,0:T(8,128)(2,1)S(1)}, bf16[96,768]{1,0:T(8,128)(2,1)S(1)}, u32[]{:S(2)}, u32[]{:S(2)}) collective-permute-start(bf16[96,768]{1,0:T(8,128)(2,1)S(1)} %get-tuple-element.220.refs_1_), channel_id=1, source_target_pairs={{0,8},{1,5},{2,10},{3,7},{4,12},{5,1},{6,14},{7,3},{8,0},{9,13},{1... | collective-permute-start | bytes 442376 | tf_op jit(solution)/shard_map/ppermute | solution.py:752
  68.8 14.9 %collective-permute-start.23 = (bf16[192,768]{1,0:T(8,128)(2,1)S(1)}, bf16[192,768]{1,0:T(8,128)(2,1)S(1)}, u32[]{:S(2)}, u32[]{:S(2)}) collective-permute-start(bf16[192,768]{1,0:T(8,128)(2,1)S(1)} %get-tuple-element.217.refs_0_), channel_id=1, source_target_pairs={{0,16},{1,17},{2,18},{3,19},{4,20},{5,21},{6,22},{7,23},{8,24},{9,... | collective-permute-start | bytes 884744 | tf_op jit(solution)/shard_map/ppermute | solution.py:752
  69.7 5.1 %collective-permute-start.26 = (bf16[96,768]{1,0:T(8,128)(2,1)S(1)}, bf16[96,768]{1,0:T(8,128)(2,1)S(1)}, u32[]{:S(2)}, u32[]{:S(2)}) collective-permute-start(bf16[96,768]{1,0:T(8,128)(2,1)S(1)} %get-tuple-element.220.refs_1_), channel_id=1, source_target_pairs={{0,4},{1,9},{2,6},{3,11},{4,0},{5,13},{6,2},{7,15},{8,12},{9,1},{1... | collective-permute-start | bytes 442376 | tf_op jit(solution)/shard_map/ppermute | solution.py:752
  72.0 5.1 %collective-permute-start.27 = (bf16[96,768]{1,0:T(8,128)(2,1)S(1)}, bf16[96,768]{1,0:T(8,128)(2,1)S(1)}, u32[]{:S(2)}, u32[]{:S(2)}) collective-permute-start(bf16[96,768]{1,0:T(8,128)(2,1)S(1)} %collective-permute-done.25.refs_2_), channel_id=1, source_target_pairs={{0,4},{1,9},{2,6},{3,11},{4,0},{5,13},{6,2},{7,15},{8,12},{9,1},{1... | collective-permute-start | bytes 442376 | tf_op jit(solution)/shard_map/ppermute | solution.py:752
  72.0 6.8 %collective-permute-start.24 = (bf16[16,768]{1,0:T(8,128)(2,1)S(1)}, bf16[16,768]{1,0:T(8,128)(2,1)S(1)}, u32[]{:S(2)}, u32[]{:S(2)}) collective-permute-start(bf16[16,768]{1,0:T(8,128)(2,1)S(1)} %get-tuple-element.219.refs_0_), channel_id=1, source_target_pairs={{0,1},{1,0},{2,3},{3,2},{4,5},{5,4},{6,7},{7,6},{8,9},{9,8},{10,11... | collective-permute-start | bytes 73736 | tf_op jit(solution)/shard_map/ppermute | solution.py:741
  78.9 4.8 %collective-permute-start.28 = (bf16[16,768]{1,0:T(8,128)(2,1)S(1)}, bf16[16,768]{1,0:T(8,128)(2,1)S(1)}, u32[]{:S(2)}, u32[]{:S(2)}) collective-permute-start(bf16[16,768]{1,0:T(8,128)(2,1)S(1)} %get-tuple-element.223.refs_2_), channel_id=1, source_target_pairs={{0,16},{1,17},{2,18},{3,19},{4,20},{5,21},{6,22},{7,23},{8,24},{9,... | collective-permute-start | bytes 73736 | tf_op jit(solution)/shard_map/ppermute | solution.py:752
  83.8 7.1 %collective-permute-start.29 = (bf16[208,768]{1,0:T(8,128)(2,1)S(1)}, bf16[208,768]{1,0:T(8,128)(2,1)S(1)}, u32[]{:S(2)}, u32[]{:S(2)}) collective-permute-start(bf16[208,768]{1,0:T(8,128)(2,1)S(1)} %get-tuple-element.227.refs_0_), channel_id=1, source_target_pairs={{0,8},{1,5},{2,10},{3,7},{4,12},{5,1},{6,14},{7,3},{8,0},{9,13},{1... | collective-permute-start | bytes 958472 | tf_op jit(solution)/shard_map/ppermute | solution.py:752
  90.9 7.1 %collective-permute-start.30 = (bf16[208,768]{1,0:T(8,128)(2,1)S(1)}, bf16[208,768]{1,0:T(8,128)(2,1)S(1)}, u32[]{:S(2)}, u32[]{:S(2)}) collective-permute-start(bf16[208,768]{1,0:T(8,128)(2,1)S(1)} %get-tuple-element.229.refs_1_), channel_id=1, source_target_pairs={{0,4},{1,9},{2,6},{3,11},{4,0},{5,13},{6,2},{7,15},{8,12},{9,1},{1... | collective-permute-start | bytes 958472 | tf_op jit(solution)/shard_map/ppermute | solution.py:752
  91.7 9.6 %collective-permute-start.31 = (bf16[208,768]{1,0:T(8,128)(2,1)S(1)}, bf16[208,768]{1,0:T(8,128)(2,1)S(1)}, u32[]{:S(2)}, u32[]{:S(2)}) collective-permute-start(bf16[208,768]{1,0:T(8,128)(2,1)S(1)} %get-tuple-element.230.refs_2_), channel_id=1, source_target_pairs={{0,4},{1,9},{2,6},{3,11},{4,0},{5,13},{6,2},{7,15},{8,12},{9,1},{1... | collective-permute-start | bytes 958472 | tf_op jit(solution)/shard_map/ppermute | solution.py:752

commit v10 on v9

--- a/solution.py
+++ b/solution.py
@@ -72,7 +72,7 @@
 
 
 STRIP = 256
-COSTS = (0, 0, 100, 0, 0, 30, 30, 0, 0, 0, 0, 0, 100, 0, 0, 0, 200, 0, 60, 0, 0, 30, 0, 0, 0, 0, 0, 0, 0, 0, 0, 0, 0)
+COSTS = (0, 0, 100, 0, 0, 30, 30, 0, 0, 0, 0, 0, 100, 0, 0, 0, 200, 0, 60, 0, 0, 30, 0, 0, 0, 0, 0, 0, 0, 0, 0, 0)
 
 
 class IO:
@@ -322,11 +322,11 @@
     return chain.call(kernel, "pair_up", (a, b), [bf16(*b.shape), bf16(2, *a.shape)], "vv-vv", limit=4)
 
 
-def spacer(chain):
-    def kernel(io):
+def spacer(chain, *after):
+    def kernel(io, *refs):
         pass
 
-    chain.call(kernel, "spacer", (), [], "-", limit=2)
+    chain.call(kernel, "spacer", after, [], "r" * len(after) + "-", limit=2)
 
 
 def load(chain, out_weight, fc1_weight, fc2_weight, picked, others):
@@ -836,6 +836,10 @@
                 b = swap_first(a)
                 rows = a.shape[0] // 2
                 self.quarters = [(a, 0, 0, 0), (a, rows, 0, 1), (b, 0, 1, 0), (b, rows, 1, 1)]
+            if self.early == 3:
+                a, b = self.last
+                sent = lax.optimization_barrier((a, chain.token))[0]
+                self.quarters = [(a, 0, 0, 0), (b, 0, 0, 1), (swap_first(sent), 0, 1, 0), (swap_first(b), 0, 1, 1)]
             if self.early == 2:
                 a, b = side_by_side(chain, *self.last, True)
                 self.quarters = [(a, 0, 0, 0), (b, 0, 0, 1), (swap_first(a), 0, 1, 0), (swap_first(b), 0, 1, 1)]
@@ -852,7 +856,7 @@
     lefts = [(dp_0, dp_1, c * width) for c in range(3)] + [(ot_0, ot_1, 0)]
     rights = [a1s] * 3 + [(gh_0, gh_1)]
     got_q = swap_core(weight_grads(chain, "weight_grads", shard, 1, lefts, rights))
-    q = Sum(4, weight_grads(chain, "weight_grads", shard, 0, lefts, rights), got_q, True, 2)
+    q = Sum(4, weight_grads(chain, "weight_grads", shard, 0, lefts, rights), got_q, True, 3)
     r.second()
     q.first()
     r.third()
@@ -860,7 +864,6 @@
     da1_mine, da1_theirs = input_grads(chain, (dp_0, dp_1), w_qkv, (tokens, x_got), sums, bias_sums)
     da1_got = swap_y(da1_theirs)
     r.fourth()
-    result = feed_result(chain, z_0, fc2, h_0)
     q.third()
     vec = vector_rows(chain, da1_theirs, da1_got)
     vec_got = swap_core(vec)
@@ -870,12 +873,12 @@
     vec = vector_cores(chain, vec, vec_got, shard)
     vec_got = swap_dp(vec, far_masks[0], far_masks[0])
     q.fourth((vec, vec_got))
+    result = feed_result(chain, z_0, fc2, h_0)
     grad_tokens = input_norm(chain, tokens, ln1_gain, da1_mine, da1_got, dh)
     q.fifth()
     each = [(0, 0, 0), (0, 1, 0), (0, 2, 0), (1, None, 0)]
     outs = [f32(3, shard, d), f32(shard, d)]
-    grads = place_sums(chain, bits, q.quarters[:2], q.size, each, outs)
-    grads = place_sums(chain, bits, q.quarters[:3], q.size, each, outs, grads, skip=2)
+    grads = place_sums(chain, bits, q.quarters[:3], q.size, each, outs)
     grad_qkv, grad_out, gain1, bias1, gain2, bias2, grad_b = place_sums(
         chain, bits, q.quarters, q.size, each, outs, grads, (d, d, d, d, shard), 3
     )

time: 104 us -> 100 us (0.962)
  waiting for transfers between devices: 30.7 us -> 28.4 us
  Pallas kernels: 37.8 us -> 36.5 us
    ppermute x18, waiting for transfers between devices: 27.9 us -> 25.6 us  [swap_dp(): return lax.ppermute(a, ('dp', 'tensor'), pairs)]
    pallas_call x33 -> x31, Pallas kernels: 37.8 us -> 36.5 us  [call(): pl.pallas_call(body, in_specs=[spec(kind) for kind in ins] + [vmem] * len...]
where the time goes in v10:
time: 100 us
  Pallas kernels  36.5 us (36%)
  starting transfers between devices  33.9 us (34%)
  waiting for transfers between devices  28.4 us (28%)
  between operations  1.13 us (1%)
    pallas_call x31, Pallas kernels, call(): pl.pallas_call(body, in_specs=[spec(kind) for kind in ins] + [vmem] * len...  36.5 us
    ppermute x18, waiting for transfers between devices, swap_dp(): return lax.ppermute(a, ('dp', 'tensor'), pairs)  25.6 us
    ppermute x18, starting transfers between devices, swap_dp(): return lax.ppermute(a, ('dp', 'tensor'), pairs)  24.4 us
    ppermute x6, starting transfers between devices, swap_y(): return lax.ppermute(a, 'tensor', [(t, t ^ 2) for t in range(n_tensor)])  8.19 us
  transfers between devices with their start and end apart: 32, of which 15 were waited for; matrix products, arithmetic and copies ran while one was open for 0% of the time, Pallas kernels for 32%

profile of v10, /device:TPU:0, one launch (start us, length us, event | category | flops | bytes accessed | tf_op | source)
XLA Modules:
  0.0 100.0 jit_solution(14127430076455059554)
XLA Ops:
  1.2 1.6 %pick.1 = (bf16[448,256]{1,0:T(8,128)(2,1)S(1)}, f32[8,128]{1,0:T(8,128)S(1)}) custom-call(s32[7]{0:T(128)S(1)} %stack.31.refs_0_, bf16[192,768]{1,0:T(8,128)(2,1)} %refs_0_.1, bf16[192,768]{1,0:T(8,128)(2,1)} %refs_1_.5, bf16[192,768]{1,0:T(8,128)(2,1)} %refs_2_.5, bf16[192]{0:T(256)(128)(2,1)} %refs_4_.2), custom_call_target="tpu_custom_call" | custom-call | bytes 100000000 | tf_op jit(solution)/shard_map/pick/pallas_call | solution.py:145
  2.8 2.6 %collective-permute-start.3 = (bf16[448,256]{1,0:T(8,128)(2,1)S(1)}, bf16[448,256]{1,0:T(8,128)(2,1)S(1)}, u32[]{:S(2)}, u32[]{:S(2)}) collective-permute-start(bf16[448,256]{1,0:T(8,128)(2,1)S(1)} %get-tuple-element.124.refs_3_), channel_id=1, source_target_pairs={{0,2},{1,3},{2,0},{3,1},{4,6},{5,7},{6,4},{7,5},{8,10},{9,11},{10,... | collective-permute-start | bytes 688136 | tf_op jit(solution)/shard_map/ppermute | solution.py:744
  5.6 1.5 %load.1 = (bf16[592,768]{1,0:T(8,128)(2,1)S(1)}, bf16[256,768]{1,0:T(8,128)(2,1)S(1)}, bf16[256,768]{1,0:T(8,128)(2,1)S(1)}, f32[768]{0:T(1024)S(1)}, f32[768]{0...) custom-call(bf16[192,768]{1,0:T(8,128)(2,1)} %refs_0_.1, bf16[192,768]{1,0:T(8,128)(2,1)} %refs_1_.5, ...), custom_call_target="tpu_custom_call" | custom-call | bytes 100000000 | tf_op jit(solution)/shard_map/load/pallas_call | solution.py:145
  7.3 4.0 %attention_forward.2 = (bf16[256,768]{1,0:T(8,128)(2,1)S(1)}, bf16[384,256]{1,0:T(8,128)(2,1)S(1)}, bf16[384,256]{1,0:T(8,128)(2,1)S(1)}, bf16[256,384]{1,0:T(8,...) custom-call(s32[7]{0:T(128)S(1)} %stack.31.refs_0_, ...), custom_call_target="tpu_custom_call" | custom-call | flops 10000000000 | bytes 100000000 | tf_op jit(solution)/shard_map/attention_forward/pallas_call | solution.py:145
  12.0 1.9 %collective-permute-start.4 = (bf16[144,768]{1,0:T(8,128)(2,1)S(1)}, bf16[144,768]{1,0:T(8,128)(2,1)S(1)}, u32[]{:S(2)}, u32[]{:S(2)}) collective-permute-start(bf16[144,768]{1,0:T(8,128)(2,1)S(1)} %get-tuple-element.134), channel_id=1, source_target_pairs={{0,4},{1,5},{2,6},{3,7},{4,0},{5,1},{6,2},{7,3},{8,12},{9,13},{10,... | collective-permute-start | bytes 663560 | tf_op jit(solution)/shard_map/ppermute | solution.py:752
  13.9 1.7 %collective-permute-start.5 = (bf16[144,768]{1,0:T(8,128)(2,1)S(1)}, bf16[144,768]{1,0:T(8,128)(2,1)S(1)}, u32[]{:S(2)}, u32[]{:S(2)}) collective-permute-start(bf16[144,768]{1,0:T(8,128)(2,1)S(1)} %get-tuple-element.134), channel_id=1, source_target_pairs={{0,8},{1,9},{2,10},{3,11},{4,12},{5,13},{6,14},{7,15},{8,0},{9,1},... | collective-permute-start | bytes 663560 | tf_op jit(solution)/shard_map/ppermute | solution.py:752
  15.5 1.5 %collective-permute-start.6 = (bf16[256,768]{1,0:T(8,128)(2,1)S(1)}, bf16[256,768]{1,0:T(8,128)(2,1)S(1)}, u32[]{:S(2)}, u32[]{:S(2)}) collective-permute-start(bf16[256,768]{1,0:T(8,128)(2,1)S(1)} %copy-done), channel_id=1, source_target_pairs={{0,2},{1,3},{2,0},{3,1},{4,6},{5,7},{6,4},{7,5},{8,10},{9,11},{10,... | collective-permute-start | bytes 1179656 | tf_op jit(solution)/shard_map/ppermute | solution.py:744
  17.1 2.1 %collective-permute-done.4.refs_0_ = bf16[144,768]{1,0:T(8,128)(2,1)S(1)} collective-permute-done((bf16[144,768]{1,0:T(8,128)(2,1)S(1)}, bf16[144,768]{1,0:T(8,128)(2,1)S(1)}, u32[]{:S(2)}, u32[]{:S(2)}) %collective-permute-start.4) | collective-permute-done | bytes 221216 | tf_op jit(solution)/shard_map/ppermute | solution.py:752
  19.2 1.5 %collective-permute-done.5.refs_1_ = bf16[144,768]{1,0:T(8,128)(2,1)S(1)} collective-permute-done((bf16[144,768]{1,0:T(8,128)(2,1)S(1)}, bf16[144,768]{1,0:T(8,128)(2,1)S(1)}, u32[]{:S(2)}, u32[]{:S(2)}) %collective-permute-start.5) | collective-permute-done | bytes 221216 | tf_op jit(solution)/shard_map/ppermute | solution.py:752
  20.6 1.5 %collective-permute-start.12 = (bf16[256,384]{1,0:T(8,128)(2,1)S(1)}, bf16[256,384]{1,0:T(8,128)(2,1)S(1)}, u32[]{:S(2)}, u32[]{:S(2)}) collective-permute-start(bf16[256,384]{1,0:T(8,128)(2,1)S(1)} %get-tuple-element.130.refs_2_), channel_id=1, source_target_pairs={{0,2},{1,3},{2,0},{3,1},{4,6},{5,7},{6,4},{7,5},{8,10},{9,11},{10,... | collective-permute-start | bytes 589832 | tf_op jit(solution)/shard_map/ppermute | solution.py:744
  22.9 3.5 %attention_forward.3 = (bf16[256,768]{1,0:T(8,128)(2,1)S(1)}, bf16[384,256]{1,0:T(8,128)(2,1)S(1)}, bf16[384,256]{1,0:T(8,128)(2,1)S(1)}, bf16[256,384]{1,0:T(8,...) custom-call(s32[7]{0:T(128)S(1)} %stack.31.refs_0_, ...), custom_call_target="tpu_custom_call" | custom-call | flops 3000000000 | bytes 100000000 | tf_op jit(solution)/shard_map/attention_forward/pallas_call | solution.py:145
  26.5 0.8 collective-permute-start.11
  27.3 1.5 %collective-permute-done.7.refs_6_ = bf16[144,768]{1,0:T(8,128)(2,1)S(1)} collective-permute-done((bf16[144,768]{1,0:T(8,128)(2,1)S(1)}, bf16[144,768]{1,0:T(8,128)(2,1)S(1)}, u32[]{:S(2)}, u32[]{:S(2)}) %collective-permute-start.7) | collective-permute-done | bytes 221216 | tf_op jit(solution)/shard_map/ppermute | solution.py:752
  28.8 1.5 %collective-permute-done.10.refs_9_ = bf16[144,768]{1,0:T(8,128)(2,1)S(1)} collective-permute-done((bf16[144,768]{1,0:T(8,128)(2,1)S(1)}, bf16[144,768]{1,0:T(8,128)(2,1)S(1)}, u32[]{:S(2)}, u32[]{:S(2)}) %collective-permute-start.10) | collective-permute-done | bytes 221216 | tf_op jit(solution)/shard_map/ppermute | solution.py:741
  30.2 0.9 pack_far.1
  31.1 1.2 %feed_in.1 = (f32[256,768]{1,0:T(8,128)S(1)}, f32[256,768]{1,0:T(8,128)S(1)}, f32[256,768]{1,0:T(8,128)S(1)}, f32[256,768]{1,0:T(8,128)S(1)}, f32[1,768]{1,0:T(1,128)S(1)}, /*index=5*/f32[8,128]{1,0:T(8,128)S(1)}) custom-call(bf16[256,768]{1,0:T(8,128)(2,1)S(1)} %get-tuple-element.126.refs_3_.refs_0_, ...), custom_call_target="tpu_custom_call" | custom-call | bytes 100000000 | tf_op jit(solution)/shard_map/feed_in/pallas_call | solution.py:145
  33.0 1.7 %feed_far.1 = (f32[256,768]{1,0:T(8,128)S(1)}, bf16[256,768]{1,0:T(8,128)(2,1)S(1)}, f32[384,768]{1,0:T(8,128)S(1)}, f32[384,768]{1,0:T(8,128)S(1)}, f32[8,128]{1,0:T(8,128)S(1)}) custom-call(f32[256,768]{1,0:T(8,128)S(1)} %get-tuple-element.155.refs_0_, bf16[256,384]{1,0:T(8,128)(2,1)S(1)} %collective-permute-done.12.refs_1_, ...), custom_call_target="tpu_custom_call" | custom-call | bytes 100000000 | tf_op jit(solution)/shard_map/feed_far/pallas_call | solution.py:145
  34.7 2.5 %attention_backward.2 = (bf16[256,768]{1,0:T(8,128)(2,1)S(1)}, bf16[1152,256]{1,0:T(8,128)(2,1)S(1)}, f32[8,128]{1,0:T(8,128)S(1)}) custom-call(bf16[256,768]{1,0:T(8,128)(2,1)S(1)} %get-tuple-element.158.refs_0_.refs_9_, bf16[768,768]{1,0:T(8,128)(2,1)S(1)} %get-tuple-element.153.refs_7_.refs_1_, f32[256,768]{1,0:T(8,128)S(1)} %get-tuple-element.161.refs_2_, ...), custom_call_target="tpu_custom_call" | custom-call | bytes 100000000 | tf_op jit(solution)/shard_map/attention_backward/pallas_call | solution.py:145
  37.3 1.8 %feed_own.1 = (f32[256,768]{1,0:T(8,128)S(1)}, bf16[256,768]{1,0:T(8,128)(2,1)S(1)}, bf16[256,768]{1,0:T(8,128)(2,1)S(1)}, bf16[2,192,768]{2,1,0:T(8,128)(2,1)S(...) custom-call(f32[256,768]{1,0:T(8,128)S(1)} %get-tuple-element.149.refs_0_, ...), custom_call_target="tpu_custom_call" | custom-call | bytes 100000000 | tf_op jit(solution)/shard_map/feed_own/pallas_call | solution.py:145
  39.2 2.5 %attention_backward.3 = (bf16[256,768]{1,0:T(8,128)(2,1)S(1)}, bf16[1152,256]{1,0:T(8,128)(2,1)S(1)}, f32[256,768]{1,0:T(8,128)S(1)}, f32[8,768]{1,0:T(8,128)S(1)}, f32[8,128]{1,0:T(8,128)S(1)}) custom-call(bf16[256,768]{1,0:T(8,128)(2,1)S(1)} %get-tuple-element.170.refs_0_, bf16[768,768]{1,0:T(8,128)(2,1)S(1)} %get-tuple-element.153.refs_7_.refs_1_, ...), custom_call_target="tpu_custom_call" | custom-call | flops 10000000000 | bytes 100000000 | tf_op jit(solution)/shard_map/attention_backward/pallas_call | solution.py:145
  42.2 1.9 %collective-permute-start.15 = (bf16[96,768]{1,0:T(8,128)(2,1)S(1)}, bf16[96,768]{1,0:T(8,128)(2,1)S(1)}, u32[]{:S(2)}, u32[]{:S(2)}) collective-permute-start(bf16[96,768]{1,0:T(8,128)(2,1)S(1)} %get-tuple-element.191), channel_id=1, source_target_pairs={{0,4},{1,9},{2,6},{3,11},{4,0},{5,13},{6,2},{7,15},{8,12},{9,1},{1... | collective-permute-start | bytes 442376 | tf_op jit(solution)/shard_map/ppermute | solution.py:752
  46.2 1.6 %collective-permute-start.18 = (bf16[96,768]{1,0:T(8,128)(2,1)S(1)}, bf16[96,768]{1,0:T(8,128)(2,1)S(1)}, u32[]{:S(2)}, u32[]{:S(2)}) collective-permute-start(bf16[96,768]{1,0:T(8,128)(2,1)S(1)} %get-tuple-element.196), channel_id=1, source_target_pairs={{0,4},{1,9},{2,6},{3,11},{4,0},{5,13},{6,2},{7,15},{8,12},{9,1},{1... | collective-permute-start | bytes 442376 | tf_op jit(solution)/shard_map/ppermute | solution.py:752
  48.3 1.7 %collective-permute-start.19 = (bf16[96,768]{1,0:T(8,128)(2,1)S(1)}, bf16[96,768]{1,0:T(8,128)(2,1)S(1)}, u32[]{:S(2)}, u32[]{:S(2)}) collective-permute-start(bf16[96,768]{1,0:T(8,128)(2,1)S(1)} %get-tuple-element.197), channel_id=1, source_target_pairs={{0,8},{1,5},{2,10},{3,7},{4,12},{5,1},{6,14},{7,3},{8,0},{9,13},{1... | collective-permute-start | bytes 442376 | tf_op jit(solution)/shard_map/ppermute | solution.py:752
  50.7 1.6 %collective-permute-start.17 = (bf16[192,768]{1,0:T(8,128)(2,1)S(1)}, bf16[192,768]{1,0:T(8,128)(2,1)S(1)}, u32[]{:S(2)}, u32[]{:S(2)}) collective-permute-start(bf16[192,768]{1,0:T(8,128)(2,1)S(1)} %get-tuple-element.195), channel_id=1, source_target_pairs={{0,4},{1,9},{2,6},{3,11},{4,0},{5,13},{6,2},{7,15},{8,12},{9,1},{1... | collective-permute-start | bytes 884744 | tf_op jit(solution)/shard_map/ppermute | solution.py:752
  52.3 2.2 %collective-permute-done.19.refs_4_ = bf16[96,768]{1,0:T(8,128)(2,1)S(1)} collective-permute-done((bf16[96,768]{1,0:T(8,128)(2,1)S(1)}, bf16[96,768]{1,0:T(8,128)(2,1)S(1)}, u32[]{:S(2)}, u32[]{:S(2)}) %collective-permute-start.19) | collective-permute-done | bytes 147488 | tf_op jit(solution)/shard_map/ppermute | solution.py:752
  55.2 3.0 %collective-permute-start.21 = (bf16[96,768]{1,0:T(8,128)(2,1)S(1)}, bf16[96,768]{1,0:T(8,128)(2,1)S(1)}, u32[]{:S(2)}, u32[]{:S(2)}) collective-permute-start(bf16[96,768]{1,0:T(8,128)(2,1)S(1)} %get-tuple-element.201.refs_0_), channel_id=1, source_target_pairs={{0,16},{1,17},{2,18},{3,19},{4,20},{5,21},{6,22},{7,23},{8,24},{9,... | collective-permute-start | bytes 442376 | tf_op jit(solution)/shard_map/ppermute | solution.py:752
  58.2 1.4 %collective-permute-start.16 = (bf16[192,768]{1,0:T(8,128)(2,1)S(1)}, bf16[192,768]{1,0:T(8,128)(2,1)S(1)}, u32[]{:S(2)}, u32[]{:S(2)}) collective-permute-start(bf16[192,768]{1,0:T(8,128)(2,1)S(1)} %get-tuple-element.194), channel_id=1, source_target_pairs={{0,4},{1,9},{2,6},{3,11},{4,0},{5,13},{6,2},{7,15},{8,12},{9,1},{1... | collective-permute-start | bytes 884744 | tf_op jit(solution)/shard_map/ppermute | solution.py:752
  60.3 2.0 %collective-permute-start.20 = (bf16[192,768]{1,0:T(8,128)(2,1)S(1)}, bf16[192,768]{1,0:T(8,128)(2,1)S(1)}, u32[]{:S(2)}, u32[]{:S(2)}) collective-permute-start(bf16[192,768]{1,0:T(8,128)(2,1)S(1)} %get-tuple-element.200), channel_id=1, source_target_pairs={{0,8},{1,5},{2,10},{3,7},{4,12},{5,1},{6,14},{7,3},{8,0},{9,13},{1... | collective-permute-start | bytes 884744 | tf_op jit(solution)/shard_map/ppermute | solution.py:752
  62.3 1.4 %input_grads.1 = (f32[256,768]{1,0:T(8,128)S(1)}, bf16[272,768]{1,0:T(8,128)(2,1)S(1)}, f32[8,128]{1,0:T(8,128)S(1)}) custom-call(bf16[1152,256]{1,0:T(8,128)(2,1)S(1)} %get-tuple-element.176.refs_0_.refs_4_.refs_8_, bf16[1152,256]{1,0:T(8,128)(2,1)S(1)} %get-tuple-element.177.refs_1_.refs_5_.refs_9_, ...), custom_call_target="tpu_custom_call" | custom-call | bytes 100000000 | tf_op jit(solution)/shard_map/input_grads/pallas_call | solution.py:145
  63.7 1.6 %collective-permute-start.23 = (bf16[272,768]{1,0:T(8,128)(2,1)S(1)}, bf16[272,768]{1,0:T(8,128)(2,1)S(1)}, u32[]{:S(2)}, u32[]{:S(2)}) collective-permute-start(bf16[272,768]{1,0:T(8,128)(2,1)S(1)} %get-tuple-element.208.refs_0_), channel_id=1, source_target_pairs={{0,2},{1,3},{2,0},{3,1},{4,6},{5,7},{6,4},{7,5},{8,10},{9,11},{10,... | collective-permute-start | bytes 1253384 | tf_op jit(solution)/shard_map/ppermute | solution.py:744
  65.5 2.6 %collective-permute-done.16.refs_3_ = bf16[192,768]{1,0:T(8,128)(2,1)S(1)} collective-permute-done((bf16[192,768]{1,0:T(8,128)(2,1)S(1)}, bf16[192,768]{1,0:T(8,128)(2,1)S(1)}, u32[]{:S(2)}, u32[]{:S(2)}) %collective-permute-start.16) | collective-permute-done | bytes 294944 | tf_op jit(solution)/shard_map/ppermute | solution.py:752
  68.8 0.9 collective-permute-start.22
  69.7 1.4 %collective-permute-start.26 = (bf16[96,768]{1,0:T(8,128)(2,1)S(1)}, bf16[96,768]{1,0:T(8,128)(2,1)S(1)}, u32[]{:S(2)}, u32[]{:S(2)}) collective-permute-start(bf16[96,768]{1,0:T(8,128)(2,1)S(1)} %get-tuple-element.211.refs_1_), channel_id=1, source_target_pairs={{0,4},{1,9},{2,6},{3,11},{4,0},{5,13},{6,2},{7,15},{8,12},{9,1},{1... | collective-permute-start | bytes 442376 | tf_op jit(solution)/shard_map/ppermute | solution.py:752
  71.1 0.9 collective-permute-done.25.refs_2_
  72.1 2.7 %collective-permute-done.26.refs_3_ = bf16[96,768]{1,0:T(8,128)(2,1)S(1)} collective-permute-done((bf16[96,768]{1,0:T(8,128)(2,1)S(1)}, bf16[96,768]{1,0:T(8,128)(2,1)S(1)}, u32[]{:S(2)}, u32[]{:S(2)}) %collective-permute-start.26) | collective-permute-done | bytes 147488 | tf_op jit(solution)/shard_map/ppermute | solution.py:752
  74.9 2.3 %collective-permute-done.27.refs_4_ = bf16[96,768]{1,0:T(8,128)(2,1)S(1)} collective-permute-done((bf16[96,768]{1,0:T(8,128)(2,1)S(1)}, bf16[96,768]{1,0:T(8,128)(2,1)S(1)}, u32[]{:S(2)}, u32[]{:S(2)}) %collective-permute-start.27) | collective-permute-done | bytes 147488 | tf_op jit(solution)/shard_map/ppermute | solution.py:752
  77.1 1.7 %place_sums.3 = (f32[192,768]{1,0:T(8,128)}, f32[192,768]{1,0:T(8,128)}, f32[8,128]{1,0:T(8,128)S(1)}) custom-call(s32[7]{0:T(128)S(1)} %stack.31.refs_0_, bf16[96,768]{1,0:T(8,128)(2,1)S(1)} %get-tuple-element.211.refs_1_, bf16[96,768]{1,0:T(8,128)(2,1)S(1)} %collective-permute-done.25.refs_2_, bf16[96,768]{1,0:T(8,128)(2,1)S(1)} %collective-permute-done.26.refs_3_, ...), custom_call_target="tpu_custom_call" | custom-call | bytes 100000000 | tf_op jit(solution)/shard_map/place_sums/pallas_call | solution.py:145
  78.9 1.4 %collective-permute-start.28 = (bf16[16,768]{1,0:T(8,128)(2,1)S(1)}, bf16[16,768]{1,0:T(8,128)(2,1)S(1)}, u32[]{:S(2)}, u32[]{:S(2)}) collective-permute-start(bf16[16,768]{1,0:T(8,128)(2,1)S(1)} %get-tuple-element.214.refs_2_), channel_id=1, source_target_pairs={{0,16},{1,17},{2,18},{3,19},{4,20},{5,21},{6,22},{7,23},{8,24},{9,... | collective-permute-start | bytes 73736 | tf_op jit(solution)/shard_map/ppermute | solution.py:752
  80.4 3.4 %collective-permute-done.28.refs_3_ = bf16[16,768]{1,0:T(8,128)(2,1)S(1)} collective-permute-done((bf16[16,768]{1,0:T(8,128)(2,1)S(1)}, bf16[16,768]{1,0:T(8,128)(2,1)S(1)}, u32[]{:S(2)}, u32[]{:S(2)}) %collective-permute-start.28) | collective-permute-done | bytes 24608 | tf_op jit(solution)/shard_map/ppermute | solution.py:752
  83.8 0.9 collective-permute-start.29
  84.7 1.2 %feed_result.1 = (bf16[256,768]{1,0:T(8,128)(2,1)}, f32[8,128]{1,0:T(8,128)S(1)}) custom-call(bf16[256,768]{1,0:T(8,128)(2,1)S(1)} %get-tuple-element.168.refs_0_, bf16[768,768]{1,0:T(8,128)(2,1)S(1)} %get-tuple-element.147.refs_7_.refs_1_, f32[256,768]{1,0:T(8,128)S(1)} %get-tuple-element.169.refs_2_, f32[8,128]{1,0:T(8,128)S(1)} %get-tuple-element.216.refs_3_), custom_call_target="tpu_custom_call" | custom-call | bytes 100000000 | tf_op jit(solution)/shard_map/feed_result/pallas_call | solution.py:145
  85.9 1.3 %input_norm.1 = (bf16[256,768]{1,0:T(8,128)(2,1)}, f32[8,128]{1,0:T(8,128)S(1)}) custom-call(bf16[256,768]{1,0:T(8,128)(2,1)S(1)} %get-tuple-element.126.refs_3_.refs_0_, f32[768]{0:T(1024)S(1)} %get-tuple-element.127.refs_4_.refs_1_, f32[256,768]{1,0:T(8,128)S(1)} %get-tuple-element.218.refs_2_, ...), custom_call_target="tpu_custom_call" | custom-call | bytes 100000000 | tf_op jit(solution)/shard_map/input_norm/pallas_call | solution.py:145
  87.3 1.4 %collective-permute-start.30 = (bf16[208,768]{1,0:T(8,128)(2,1)S(1)}, bf16[208,768]{1,0:T(8,128)(2,1)S(1)}, u32[]{:S(2)}, u32[]{:S(2)}) collective-permute-start(bf16[208,768]{1,0:T(8,128)(2,1)S(1)} %get-tuple-element.224.refs_1_), channel_id=1, source_target_pairs={{0,4},{1,9},{2,6},{3,11},{4,0},{5,13},{6,2},{7,15},{8,12},{9,1},{1... | collective-permute-start | bytes 958472 | tf_op jit(solution)/shard_map/ppermute | solution.py:752
  88.7 2.2 %collective-permute-done.29.refs_2_ = bf16[208,768]{1,0:T(8,128)(2,1)S(1)} collective-permute-done((bf16[208,768]{1,0:T(8,128)(2,1)S(1)}, bf16[208,768]{1,0:T(8,128)(2,1)S(1)}, u32[]{:S(2)}, u32[]{:S(2)}) %collective-permute-start.29) | collective-permute-done | bytes 319520 | tf_op jit(solution)/shard_map/ppermute | solution.py:752
  91.6 2.7 %collective-permute-done.30.refs_3_ = bf16[208,768]{1,0:T(8,128)(2,1)S(1)} collective-permute-done((bf16[208,768]{1,0:T(8,128)(2,1)S(1)}, bf16[208,768]{1,0:T(8,128)(2,1)S(1)}, u32[]{:S(2)}, u32[]{:S(2)}) %collective-permute-start.30) | collective-permute-done | bytes 319520 | tf_op jit(solution)/shard_map/ppermute | solution.py:752
  94.3 1.9 %place_sums.4 = (f32[3,192,768]{2,1,0:T(8,128)}, f32[192,768]{1,0:T(8,128)}, f32[8,128]{1,0:T(8,128)S(1)}) custom-call(s32[7]{0:T(128)S(1)} %stack.31.refs_0_, bf16[208,768]{1,0:T(8,128)(2,1)S(1)} %get-tuple-element.224.refs_1_, bf16[208,768]{1,0:T(8,128)(2,1)S(1)} %collective-permute-done.29.refs_2_, bf16[208,768]{1,0:T(8,128)(2,1)S(1)} %collective-permute-done.30.refs_3_, ...), custom_call_target="tpu_custom_call" | custom-call | bytes 100000000 | tf_op jit(solution)/shard_map/place_sums/pallas_call | solution.py:145
  96.2 1.6 %collective-permute-done.31.refs_4_ = bf16[208,768]{1,0:T(8,128)(2,1)S(1)} collective-permute-done((bf16[208,768]{1,0:T(8,128)(2,1)S(1)}, bf16[208,768]{1,0:T(8,128)(2,1)S(1)}, u32[]{:S(2)}, u32[]{:S(2)}) %collective-permute-start.31) | collective-permute-done | bytes 319520 | tf_op jit(solution)/shard_map/ppermute | solution.py:752
  97.8 2.0 %place_sums.5 = (f32[3,192,768]{2,1,0:T(8,128)}, f32[192,768]{1,0:T(8,128)}, f32[768]{0:T(1024)}, f32[768]{0:T(1024)}, f32[768]{0:T(1024)}, /*index=5*/f32[768]{0:T(1024)}, f32[192]{0:T(256)}, f32[8,128]{1,0:T(8,128)}) custom-call(s32[7]{0:T(128)S(1)} %stack.31.refs_0_, ...), custom_call_target="tpu_custom_call", output_to_operand_aliasing={{0}: (5, {}), {1}: (6, {})} | custom-call | bytes 100000000 | tf_op jit(solution)/shard_map/place_sums/pallas_call | solution.py:145
  (50 shorter events, 10.1 us)
Async XLA Ops:
  0.6 6.6 %collective-permute-start.1 = (bf16[3,192,768]{2,1,0:T(8,128)(2,1)}, bf16[3,192,768]{2,1,0:T(8,128)(2,1)S(1)}, u32[]{:S(2)}, u32[]{:S(2)}) collective-permute-start(bf16[3,192,768]{2,1,0:T(8,128)(2,1)} %refs_6_.3), channel_id=1, source_target_pairs={{0,1},{1,0},{2,3},{3,2},{4,5},{5,4},{6,7},{7,6},{8,9},{9,8},{10,11... | collective-permute-start | bytes 2654216 | tf_op jit(solution)/shard_map/ppermute | solution.py:741
  2.8 9.1 %collective-permute-start.3 = (bf16[448,256]{1,0:T(8,128)(2,1)S(1)}, bf16[448,256]{1,0:T(8,128)(2,1)S(1)}, u32[]{:S(2)}, u32[]{:S(2)}) collective-permute-start(bf16[448,256]{1,0:T(8,128)(2,1)S(1)} %get-tuple-element.124.refs_3_), channel_id=1, source_target_pairs={{0,2},{1,3},{2,0},{3,1},{4,6},{5,7},{6,4},{7,5},{8,10},{9,11},{10,... | collective-permute-start | bytes 688136 | tf_op jit(solution)/shard_map/ppermute | solution.py:744
  5.5 16.7 %collective-permute-start = (bf16[256,768]{1,0:T(8,128)(2,1)}, bf16[256,768]{1,0:T(8,128)(2,1)S(1)}, u32[]{:S(2)}, u32[]{:S(2)}) collective-permute-start(bf16[256,768]{1,0:T(8,128)(2,1)} %refs_4_.3), channel_id=1, source_target_pairs={{0,2},{1,3},{2,0},{3,1},{4,6},{5,7},{6,4},{7,5},{8,10},{9,11},{10,... | collective-permute-start | bytes 1179656 | tf_op jit(solution)/shard_map/ppermute | solution.py:744
  7.1 15.9 %collective-permute-start.2 = (bf16[592,768]{1,0:T(8,128)(2,1)S(1)}, bf16[592,768]{1,0:T(8,128)(2,1)S(1)}, u32[]{:S(2)}, u32[]{:S(2)}) collective-permute-start(bf16[592,768]{1,0:T(8,128)(2,1)S(1)} %get-tuple-element.132.refs_7_.refs_8_), channel_id=1, source_target_pairs={{0,1},{1,0},{2,3},{3,2},{4,5},{5,4},{6,7},{7,6},{8,9},{9,8},{10,11... | collective-permute-start | bytes 2727944 | tf_op jit(solution)/shard_map/ppermute | solution.py:741
  7.3 8.3 %copy-start = (bf16[256,768]{1,0:T(8,128)(2,1)S(1)}, bf16[256,768]{1,0:T(8,128)(2,1)}, u32[]{:S(2)}) copy-start(bf16[256,768]{1,0:T(8,128)(2,1)} %refs_5_.1) | copy-start | bytes 1179652
  12.0 7.2 %collective-permute-start.4 = (bf16[144,768]{1,0:T(8,128)(2,1)S(1)}, bf16[144,768]{1,0:T(8,128)(2,1)S(1)}, u32[]{:S(2)}, u32[]{:S(2)}) collective-permute-start(bf16[144,768]{1,0:T(8,128)(2,1)S(1)} %get-tuple-element.134), channel_id=1, source_target_pairs={{0,4},{1,5},{2,6},{3,7},{4,0},{5,1},{6,2},{7,3},{8,12},{9,13},{10,... | collective-permute-start | bytes 663560 | tf_op jit(solution)/shard_map/ppermute | solution.py:752
  13.9 6.8 %collective-permute-start.5 = (bf16[144,768]{1,0:T(8,128)(2,1)S(1)}, bf16[144,768]{1,0:T(8,128)(2,1)S(1)}, u32[]{:S(2)}, u32[]{:S(2)}) collective-permute-start(bf16[144,768]{1,0:T(8,128)(2,1)S(1)} %get-tuple-element.134), channel_id=1, source_target_pairs={{0,8},{1,9},{2,10},{3,11},{4,12},{5,13},{6,14},{7,15},{8,0},{9,1},... | collective-permute-start | bytes 663560 | tf_op jit(solution)/shard_map/ppermute | solution.py:752
  15.5 15.6 %collective-permute-start.6 = (bf16[256,768]{1,0:T(8,128)(2,1)S(1)}, bf16[256,768]{1,0:T(8,128)(2,1)S(1)}, u32[]{:S(2)}, u32[]{:S(2)}) collective-permute-start(bf16[256,768]{1,0:T(8,128)(2,1)S(1)} %copy-done), channel_id=1, source_target_pairs={{0,2},{1,3},{2,0},{3,1},{4,6},{5,7},{6,4},{7,5},{8,10},{9,11},{10,... | collective-permute-start | bytes 1179656 | tf_op jit(solution)/shard_map/ppermute | solution.py:744
  19.2 7.3 %collective-permute-start.8 = (bf16[160,768]{1,0:T(8,128)(2,1)S(1)}, bf16[160,768]{1,0:T(8,128)(2,1)S(1)}, u32[]{:S(2)}, u32[]{:S(2)}) collective-permute-start(bf16[160,768]{1,0:T(8,128)(2,1)S(1)} %get-tuple-element.142.refs_4_.refs_10_), channel_id=1, source_target_pairs={{0,1},{1,0},{2,3},{3,2},{4,5},{5,4},{6,7},{7,6},{8,9},{9,8},{10,11... | collective-permute-start | bytes 737288 | tf_op jit(solution)/shard_map/ppermute | solution.py:741
  20.6 12.4 %collective-permute-start.12 = (bf16[256,384]{1,0:T(8,128)(2,1)S(1)}, bf16[256,384]{1,0:T(8,128)(2,1)S(1)}, u32[]{:S(2)}, u32[]{:S(2)}) collective-permute-start(bf16[256,384]{1,0:T(8,128)(2,1)S(1)} %get-tuple-element.130.refs_2_), channel_id=1, source_target_pairs={{0,2},{1,3},{2,0},{3,1},{4,6},{5,7},{6,4},{7,5},{8,10},{9,11},{10,... | collective-permute-start | bytes 589832 | tf_op jit(solution)/shard_map/ppermute | solution.py:744
  22.2 6.5 %collective-permute-start.7 = (bf16[144,768]{1,0:T(8,128)(2,1)S(1)}, bf16[144,768]{1,0:T(8,128)(2,1)S(1)}, u32[]{:S(2)}, u32[]{:S(2)}) collective-permute-start(bf16[144,768]{1,0:T(8,128)(2,1)S(1)} %get-tuple-element.144), channel_id=1, source_target_pairs={{0,4},{1,5},{2,6},{3,7},{4,0},{5,1},{6,2},{7,3},{8,12},{9,13},{10,... | collective-permute-start | bytes 663560 | tf_op jit(solution)/shard_map/ppermute | solution.py:752
  22.9 7.3 %collective-permute-start.9 = (bf16[2,144,768]{2,1,0:T(8,128)(2,1)S(1)}, bf16[2,144,768]{2,1,0:T(8,128)(2,1)S(1)}, u32[]{:S(2)}, u32[]{:S(2)}) collective-permute-start(bf16[2,144,768]{2,1,0:T(8,128)(2,1)S(1)} %get-tuple-element.143.refs_5_), channel_id=1, source_target_pairs={{0,1},{1,0},{2,3},{3,2},{4,5},{5,4},{6,7},{7,6},{8,9},{9,8},{10,11... | collective-permute-start | bytes 1327112 | tf_op jit(solution)/shard_map/ppermute | solution.py:741
  26.5 10.8 %collective-permute-start.11 = (bf16[256,384]{1,0:T(8,128)(2,1)S(1)}, bf16[256,384]{1,0:T(8,128)(2,1)S(1)}, u32[]{:S(2)}, u32[]{:S(2)}) collective-permute-start(bf16[256,384]{1,0:T(8,128)(2,1)S(1)} %get-tuple-element.137.refs_3_), channel_id=1, source_target_pairs={{0,2},{1,3},{2,0},{3,1},{4,6},{5,7},{6,4},{7,5},{8,10},{9,11},{10,... | collective-permute-start | bytes 589832 | tf_op jit(solution)/shard_map/ppermute | solution.py:744
  28.8 1.5 %collective-permute-start.10 = (bf16[144,768]{1,0:T(8,128)(2,1)S(1)}, bf16[144,768]{1,0:T(8,128)(2,1)S(1)}, u32[]{:S(2)}, u32[]{:S(2)}) collective-permute-start(bf16[144,768]{1,0:T(8,128)(2,1)S(1)} %collective-permute-done.7.refs_6_), channel_id=1, source_target_pairs={{0,1},{1,0},{2,3},{3,2},{4,5},{5,4},{6,7},{7,6},{8,9},{9,8},{10,11... | collective-permute-start | bytes 663560 | tf_op jit(solution)/shard_map/ppermute | solution.py:741
  39.1 2.6 %collective-permute-start.13 = (bf16[2,192,768]{2,1,0:T(8,128)(2,1)S(1)}, bf16[2,192,768]{2,1,0:T(8,128)(2,1)S(1)}, u32[]{:S(2)}, u32[]{:S(2)}) collective-permute-start(bf16[2,192,768]{2,1,0:T(8,128)(2,1)S(1)} %get-tuple-element.185), channel_id=1, source_target_pairs={{0,1},{1,0},{2,3},{3,2},{4,5},{5,4},{6,7},{7,6},{8,9},{9,8},{10,11... | collective-permute-start | bytes 1769480 | tf_op jit(solution)/shard_map/ppermute | solution.py:741
  42.2 5.5 %collective-permute-start.15 = (bf16[96,768]{1,0:T(8,128)(2,1)S(1)}, bf16[96,768]{1,0:T(8,128)(2,1)S(1)}, u32[]{:S(2)}, u32[]{:S(2)}) collective-permute-start(bf16[96,768]{1,0:T(8,128)(2,1)S(1)} %get-tuple-element.191), channel_id=1, source_target_pairs={{0,4},{1,9},{2,6},{3,11},{4,0},{5,13},{6,2},{7,15},{8,12},{9,1},{1... | collective-permute-start | bytes 442376 | tf_op jit(solution)/shard_map/ppermute | solution.py:752
  45.8 4.3 %collective-permute-start.14 = (bf16[4,192,768]{2,1,0:T(8,128)(2,1)S(1)}, bf16[4,192,768]{2,1,0:T(8,128)(2,1)S(1)}, u32[]{:S(2)}, u32[]{:S(2)}) collective-permute-start(bf16[4,192,768]{2,1,0:T(8,128)(2,1)S(1)} %get-tuple-element.190), channel_id=1, source_target_pairs={{0,1},{1,0},{2,3},{3,2},{4,5},{5,4},{6,7},{7,6},{8,9},{9,8},{10,11... | collective-permute-start | bytes 3538952 | tf_op jit(solution)/shard_map/ppermute | solution.py:741
  46.2 6.2 %collective-permute-start.18 = (bf16[96,768]{1,0:T(8,128)(2,1)S(1)}, bf16[96,768]{1,0:T(8,128)(2,1)S(1)}, u32[]{:S(2)}, u32[]{:S(2)}) collective-permute-start(bf16[96,768]{1,0:T(8,128)(2,1)S(1)} %get-tuple-element.196), channel_id=1, source_target_pairs={{0,4},{1,9},{2,6},{3,11},{4,0},{5,13},{6,2},{7,15},{8,12},{9,1},{1... | collective-permute-start | bytes 442376 | tf_op jit(solution)/shard_map/ppermute | solution.py:752
  48.3 6.2 %collective-permute-start.19 = (bf16[96,768]{1,0:T(8,128)(2,1)S(1)}, bf16[96,768]{1,0:T(8,128)(2,1)S(1)}, u32[]{:S(2)}, u32[]{:S(2)}) collective-permute-start(bf16[96,768]{1,0:T(8,128)(2,1)S(1)} %get-tuple-element.197), channel_id=1, source_target_pairs={{0,8},{1,5},{2,10},{3,7},{4,12},{5,1},{6,14},{7,3},{8,0},{9,13},{1... | collective-permute-start | bytes 442376 | tf_op jit(solution)/shard_map/ppermute | solution.py:752
  50.7 8.9 %collective-permute-start.17 = (bf16[192,768]{1,0:T(8,128)(2,1)S(1)}, bf16[192,768]{1,0:T(8,128)(2,1)S(1)}, u32[]{:S(2)}, u32[]{:S(2)}) collective-permute-start(bf16[192,768]{1,0:T(8,128)(2,1)S(1)} %get-tuple-element.195), channel_id=1, source_target_pairs={{0,4},{1,9},{2,6},{3,11},{4,0},{5,13},{6,2},{7,15},{8,12},{9,1},{1... | collective-permute-start | bytes 884744 | tf_op jit(solution)/shard_map/ppermute | solution.py:752
  55.2 10.1 %collective-permute-start.21 = (bf16[96,768]{1,0:T(8,128)(2,1)S(1)}, bf16[96,768]{1,0:T(8,128)(2,1)S(1)}, u32[]{:S(2)}, u32[]{:S(2)}) collective-permute-start(bf16[96,768]{1,0:T(8,128)(2,1)S(1)} %get-tuple-element.201.refs_0_), channel_id=1, source_target_pairs={{0,16},{1,17},{2,18},{3,19},{4,20},{5,21},{6,22},{7,23},{8,24},{9,... | collective-permute-start | bytes 442376 | tf_op jit(solution)/shard_map/ppermute | solution.py:752
  58.2 9.9 %collective-permute-start.16 = (bf16[192,768]{1,0:T(8,128)(2,1)S(1)}, bf16[192,768]{1,0:T(8,128)(2,1)S(1)}, u32[]{:S(2)}, u32[]{:S(2)}) collective-permute-start(bf16[192,768]{1,0:T(8,128)(2,1)S(1)} %get-tuple-element.194), channel_id=1, source_target_pairs={{0,4},{1,9},{2,6},{3,11},{4,0},{5,13},{6,2},{7,15},{8,12},{9,1},{1... | collective-permute-start | bytes 884744 | tf_op jit(solution)/shard_map/ppermute | solution.py:752
  60.3 7.8 %collective-permute-start.20 = (bf16[192,768]{1,0:T(8,128)(2,1)S(1)}, bf16[192,768]{1,0:T(8,128)(2,1)S(1)}, u32[]{:S(2)}, u32[]{:S(2)}) collective-permute-start(bf16[192,768]{1,0:T(8,128)(2,1)S(1)} %get-tuple-element.200), channel_id=1, source_target_pairs={{0,8},{1,5},{2,10},{3,7},{4,12},{5,1},{6,14},{7,3},{8,0},{9,13},{1... | collective-permute-start | bytes 884744 | tf_op jit(solution)/shard_map/ppermute | solution.py:752
  63.7 8.3 %collective-permute-start.23 = (bf16[272,768]{1,0:T(8,128)(2,1)S(1)}, bf16[272,768]{1,0:T(8,128)(2,1)S(1)}, u32[]{:S(2)}, u32[]{:S(2)}) collective-permute-start(bf16[272,768]{1,0:T(8,128)(2,1)S(1)} %get-tuple-element.208.refs_0_), channel_id=1, source_target_pairs={{0,2},{1,3},{2,0},{3,1},{4,6},{5,7},{6,4},{7,5},{8,10},{9,11},{10,... | collective-permute-start | bytes 1253384 | tf_op jit(solution)/shard_map/ppermute | solution.py:744
  65.4 6.6 %collective-permute-start.25 = (bf16[96,768]{1,0:T(8,128)(2,1)S(1)}, bf16[96,768]{1,0:T(8,128)(2,1)S(1)}, u32[]{:S(2)}, u32[]{:S(2)}) collective-permute-start(bf16[96,768]{1,0:T(8,128)(2,1)S(1)} %get-tuple-element.211.refs_1_), channel_id=1, source_target_pairs={{0,8},{1,5},{2,10},{3,7},{4,12},{5,1},{6,14},{7,3},{8,0},{9,13},{1... | collective-permute-start | bytes 442376 | tf_op jit(solution)/shard_map/ppermute | solution.py:752
  68.8 14.9 %collective-permute-start.22 = (bf16[192,768]{1,0:T(8,128)(2,1)S(1)}, bf16[192,768]{1,0:T(8,128)(2,1)S(1)}, u32[]{:S(2)}, u32[]{:S(2)}) collective-permute-start(bf16[192,768]{1,0:T(8,128)(2,1)S(1)} %get-tuple-element.207.refs_0_), channel_id=1, source_target_pairs={{0,16},{1,17},{2,18},{3,19},{4,20},{5,21},{6,22},{7,23},{8,24},{9,... | collective-permute-start | bytes 884744 | tf_op jit(solution)/shard_map/ppermute | solution.py:752
  69.7 5.1 %collective-permute-start.26 = (bf16[96,768]{1,0:T(8,128)(2,1)S(1)}, bf16[96,768]{1,0:T(8,128)(2,1)S(1)}, u32[]{:S(2)}, u32[]{:S(2)}) collective-permute-start(bf16[96,768]{1,0:T(8,128)(2,1)S(1)} %get-tuple-element.211.refs_1_), channel_id=1, source_target_pairs={{0,4},{1,9},{2,6},{3,11},{4,0},{5,13},{6,2},{7,15},{8,12},{9,1},{1... | collective-permute-start | bytes 442376 | tf_op jit(solution)/shard_map/ppermute | solution.py:752
  72.0 5.1 %collective-permute-start.27 = (bf16[96,768]{1,0:T(8,128)(2,1)S(1)}, bf16[96,768]{1,0:T(8,128)(2,1)S(1)}, u32[]{:S(2)}, u32[]{:S(2)}) collective-permute-start(bf16[96,768]{1,0:T(8,128)(2,1)S(1)} %collective-permute-done.25.refs_2_), channel_id=1, source_target_pairs={{0,4},{1,9},{2,6},{3,11},{4,0},{5,13},{6,2},{7,15},{8,12},{9,1},{1... | collective-permute-start | bytes 442376 | tf_op jit(solution)/shard_map/ppermute | solution.py:752
  72.0 6.8 %collective-permute-start.24 = (bf16[16,768]{1,0:T(8,128)(2,1)S(1)}, bf16[16,768]{1,0:T(8,128)(2,1)S(1)}, u32[]{:S(2)}, u32[]{:S(2)}) collective-permute-start(bf16[16,768]{1,0:T(8,128)(2,1)S(1)} %get-tuple-element.210.refs_0_), channel_id=1, source_target_pairs={{0,1},{1,0},{2,3},{3,2},{4,5},{5,4},{6,7},{7,6},{8,9},{9,8},{10,11... | collective-permute-start | bytes 73736 | tf_op jit(solution)/shard_map/ppermute | solution.py:741
  78.9 4.8 %collective-permute-start.28 = (bf16[16,768]{1,0:T(8,128)(2,1)S(1)}, bf16[16,768]{1,0:T(8,128)(2,1)S(1)}, u32[]{:S(2)}, u32[]{:S(2)}) collective-permute-start(bf16[16,768]{1,0:T(8,128)(2,1)S(1)} %get-tuple-element.214.refs_2_), channel_id=1, source_target_pairs={{0,16},{1,17},{2,18},{3,19},{4,20},{5,21},{6,22},{7,23},{8,24},{9,... | collective-permute-start | bytes 73736 | tf_op jit(solution)/shard_map/ppermute | solution.py:752
  83.8 7.1 %collective-permute-start.29 = (bf16[208,768]{1,0:T(8,128)(2,1)S(1)}, bf16[208,768]{1,0:T(8,128)(2,1)S(1)}, u32[]{:S(2)}, u32[]{:S(2)}) collective-permute-start(bf16[208,768]{1,0:T(8,128)(2,1)S(1)} %get-tuple-element.224.refs_1_), channel_id=1, source_target_pairs={{0,8},{1,5},{2,10},{3,7},{4,12},{5,1},{6,14},{7,3},{8,0},{9,13},{1... | collective-permute-start | bytes 958472 | tf_op jit(solution)/shard_map/ppermute | solution.py:752
  87.3 7.1 %collective-permute-start.30 = (bf16[208,768]{1,0:T(8,128)(2,1)S(1)}, bf16[208,768]{1,0:T(8,128)(2,1)S(1)}, u32[]{:S(2)}, u32[]{:S(2)}) collective-permute-start(bf16[208,768]{1,0:T(8,128)(2,1)S(1)} %get-tuple-element.224.refs_1_), channel_id=1, source_target_pairs={{0,4},{1,9},{2,6},{3,11},{4,0},{5,13},{6,2},{7,15},{8,12},{9,1},{1... | collective-permute-start | bytes 958472 | tf_op jit(solution)/shard_map/ppermute | solution.py:752
  90.8 7.0 %collective-permute-start.31 = (bf16[208,768]{1,0:T(8,128)(2,1)S(1)}, bf16[208,768]{1,0:T(8,128)(2,1)S(1)}, u32[]{:S(2)}, u32[]{:S(2)}) collective-permute-start(bf16[208,768]{1,0:T(8,128)(2,1)S(1)} %collective-permute-done.29.refs_2_), channel_id=1, source_target_pairs={{0,4},{1,9},{2,6},{3,11},{4,0},{5,13},{6,2},{7,15},{8,12},{9,1},{1... | collective-permute-start | bytes 958472 | tf_op jit(solution)/shard_map/ppermute | solution.py:752

commit v11 on v10

--- a/solution.py
+++ b/solution.py
@@ -105,7 +105,7 @@
     def __init__(self):
         self.token, self.calls = None, 0
 
-    def call(self, kernel, name, args, outs, kinds, scratch=(), limit=16, aliases={}):
+    def call(self, kernel, name, args, outs, kinds, scratch=(), limit=16, aliases={}, last=False):
         ins, out_kinds = kinds.split("-")
         cost = COSTS[min(self.calls, len(COSTS) - 1)]
         self.calls += 1
@@ -120,13 +120,12 @@
         memory = lambda kind: pltpu.SMEM if kind == "c" else pltpu.VMEM
         buffers = [memory(ins[j])(args[j].shape, args[j].dtype) for j in staged]
         buffers += [pltpu.VMEM(outs[j].shape, outs[j].dtype) for j in written]
-        n_in, n_out, n_buf = len(args) + len(tokens), len(outs), len(buffers)
+        n_in, n_out, n_buf, n_tokens = len(args) + len(tokens), len(outs), len(buffers), 0 if last else 1
 
         def body(*refs):
             arg_refs = list(refs[: len(args)])
             out_refs = list(refs[n_in : n_in + n_out])
-            token_ref = refs[n_in + n_out]
-            own = refs[n_in + n_out + 1 :]
+            tokens_out, own = refs[n_in + n_out :][:n_tokens], refs[n_in + n_out + n_tokens :]
             bufs, sems, extra = own[:n_buf], own[n_buf], own[n_buf + 1 :]
             reads, writes = {}, {}
             for at, j in enumerate(staged):
@@ -138,22 +137,24 @@
                 out_refs[j] = bufs[at]
             io = IO(reads, writes)
             io.wait(*(j for j in staged if ins[j] == "h"))
-            token_ref[...] = jnp.zeros_like(token_ref)
+            for token_ref in tokens_out:
+                token_ref[...] = jnp.zeros_like(token_ref)
             kernel(io, *arg_refs, *out_refs, *extra)
             io.finish()
 
-        *results, self.token = pl.pallas_call(
+        results = pl.pallas_call(
             body,
             in_specs=[spec(kind) for kind in ins] + [vmem] * len(tokens),
-            out_specs=[spec(kind) for kind in out_kinds] + [vmem],
-            out_shape=[*outs, f32(8, 128)],
+            out_specs=[spec(kind) for kind in out_kinds] + [vmem] * n_tokens,
+            out_shape=[*outs, *[f32(8, 128)] * n_tokens],
             input_output_aliases=aliases,
             scratch_shapes=[*buffers, pltpu.SemaphoreType.DMA((max(n_buf, 1),)), *scratch],
             compiler_params=pltpu.CompilerParams(vmem_limit_bytes=limit * MIB),
             cost_estimate=pl.CostEstimate(flops=cost * 10**8, bytes_accessed=10**8, transcendentals=0),
             name=name,
         )(*(pinned(a) if kind in "hclp" else a for a, kind in zip(args, ins)), *tokens)
-        return results
+        self.token = None if last else results[-1]
+        return results[: len(outs)]
 
 
 def bf16(*shape):
@@ -708,11 +709,12 @@
             total = jnp.where(bits_ref[5] == 0, (a + b) + (c + e), (a + c) + (b + e))
             for at, (length, ref) in enumerate(zip(vec, vec_refs)):
                 ref[...] = total[at, :length]
+            io.flush(*range(n, n + len(vec)))
         each(lambda copy: copy.wait())
 
     return chain.call(
         kernel, "place_sums", (bits, *arrays, *whole), [*outs, *(f32(length) for length in vec)],
-        "s" + "v" * len(arrays) + "p" * len(whole) + "-" + "r" * n + "v" * len(vec), limit=8,
+        "s" + "v" * len(arrays) + "p" * len(whole) + "-" + "r" * n + "w" * len(vec), limit=8, last=bool(vec),
         aliases={1 + len(arrays) + j: j for j in range(len(whole))},
         scratch=[pltpu.VMEM((len(quarters), rows, d), F32), pltpu.SemaphoreType.DMA((len(quarters),))],
     )

time: 100 us -> 99.7 us (level)
  no operation moved by 1% of the time
where the time goes in v11:
time: 99.7 us; the launch traced here: 99.5 us
  Pallas kernels  36 us (36%)
  starting transfers between devices  33.9 us (34%)
  waiting for transfers between devices  28.4 us (28%)
  between operations  1.13 us (1%)
    pallas_call x31, Pallas kernels, call(): pl.pallas_call(body, in_specs=[spec(kind) for kind in ins] + [vmem] * len...  36 us
    ppermute x18, waiting for transfers between devices, swap_dp(): return lax.ppermute(a, ('dp', 'tensor'), pairs)  25.6 us
    ppermute x18, starting transfers between devices, swap_dp(): return lax.ppermute(a, ('dp', 'tensor'), pairs)  24.4 us
    ppermute x6, starting transfers between devices, swap_y(): return lax.ppermute(a, 'tensor', [(t, t ^ 2) for t in range(n_tensor)])  8.19 us
  transfers between devices with their start and end apart: 32, of which 15 were waited for; matrix products, arithmetic and copies ran while one was open for 0% of the time, Pallas kernels for 32%

profile of v11, /device:TPU:0, one launch (start us, length us, event | category | flops | bytes accessed | tf_op | source)
XLA Modules:
  0.0 99.5 jit_solution(1650026222860592933)
XLA Ops:
  1.2 1.6 %pick.1 = (bf16[448,256]{1,0:T(8,128)(2,1)S(1)}, f32[8,128]{1,0:T(8,128)S(1)}) custom-call(s32[7]{0:T(128)S(1)} %stack.31.refs_0_, bf16[192,768]{1,0:T(8,128)(2,1)} %refs_0_.1, bf16[192,768]{1,0:T(8,128)(2,1)} %refs_1_.5, bf16[192,768]{1,0:T(8,128)(2,1)} %refs_2_.5, bf16[192]{0:T(256)(128)(2,1)} %refs_4_.2), custom_call_target="tpu_custom_call" | custom-call | bytes 100000000 | tf_op jit(solution)/shard_map/pick/pallas_call | solution.py:145
  2.8 2.6 %collective-permute-start.3 = (bf16[448,256]{1,0:T(8,128)(2,1)S(1)}, bf16[448,256]{1,0:T(8,128)(2,1)S(1)}, u32[]{:S(2)}, u32[]{:S(2)}) collective-permute-start(bf16[448,256]{1,0:T(8,128)(2,1)S(1)} %get-tuple-element.124.refs_3_), channel_id=1, source_target_pairs={{0,2},{1,3},{2,0},{3,1},{4,6},{5,7},{6,4},{7,5},{8,10},{9,11},{10,... | collective-permute-start | bytes 688136 | tf_op jit(solution)/shard_map/ppermute | solution.py:746
  5.6 1.5 %load.1 = (bf16[592,768]{1,0:T(8,128)(2,1)S(1)}, bf16[256,768]{1,0:T(8,128)(2,1)S(1)}, bf16[256,768]{1,0:T(8,128)(2,1)S(1)}, f32[768]{0:T(1024)S(1)}, f32[768]{0...) custom-call(bf16[192,768]{1,0:T(8,128)(2,1)} %refs_0_.1, bf16[192,768]{1,0:T(8,128)(2,1)} %refs_1_.5, ...), custom_call_target="tpu_custom_call" | custom-call | bytes 100000000 | tf_op jit(solution)/shard_map/load/pallas_call | solution.py:145
  7.3 4.0 %attention_forward.2 = (bf16[256,768]{1,0:T(8,128)(2,1)S(1)}, bf16[384,256]{1,0:T(8,128)(2,1)S(1)}, bf16[384,256]{1,0:T(8,128)(2,1)S(1)}, bf16[256,384]{1,0:T(8,...) custom-call(s32[7]{0:T(128)S(1)} %stack.31.refs_0_, ...), custom_call_target="tpu_custom_call" | custom-call | flops 10000000000 | bytes 100000000 | tf_op jit(solution)/shard_map/attention_forward/pallas_call | solution.py:145
  12.0 1.9 %collective-permute-start.4 = (bf16[144,768]{1,0:T(8,128)(2,1)S(1)}, bf16[144,768]{1,0:T(8,128)(2,1)S(1)}, u32[]{:S(2)}, u32[]{:S(2)}) collective-permute-start(bf16[144,768]{1,0:T(8,128)(2,1)S(1)} %get-tuple-element.134), channel_id=1, source_target_pairs={{0,4},{1,5},{2,6},{3,7},{4,0},{5,1},{6,2},{7,3},{8,12},{9,13},{10,... | collective-permute-start | bytes 663560 | tf_op jit(solution)/shard_map/ppermute | solution.py:754
  13.9 1.7 %collective-permute-start.5 = (bf16[144,768]{1,0:T(8,128)(2,1)S(1)}, bf16[144,768]{1,0:T(8,128)(2,1)S(1)}, u32[]{:S(2)}, u32[]{:S(2)}) collective-permute-start(bf16[144,768]{1,0:T(8,128)(2,1)S(1)} %get-tuple-element.134), channel_id=1, source_target_pairs={{0,8},{1,9},{2,10},{3,11},{4,12},{5,13},{6,14},{7,15},{8,0},{9,1},... | collective-permute-start | bytes 663560 | tf_op jit(solution)/shard_map/ppermute | solution.py:754
  15.5 1.5 %collective-permute-start.6 = (bf16[256,768]{1,0:T(8,128)(2,1)S(1)}, bf16[256,768]{1,0:T(8,128)(2,1)S(1)}, u32[]{:S(2)}, u32[]{:S(2)}) collective-permute-start(bf16[256,768]{1,0:T(8,128)(2,1)S(1)} %copy-done), channel_id=1, source_target_pairs={{0,2},{1,3},{2,0},{3,1},{4,6},{5,7},{6,4},{7,5},{8,10},{9,11},{10,... | collective-permute-start | bytes 1179656 | tf_op jit(solution)/shard_map/ppermute | solution.py:746
  17.1 2.1 %collective-permute-done.4.refs_0_ = bf16[144,768]{1,0:T(8,128)(2,1)S(1)} collective-permute-done((bf16[144,768]{1,0:T(8,128)(2,1)S(1)}, bf16[144,768]{1,0:T(8,128)(2,1)S(1)}, u32[]{:S(2)}, u32[]{:S(2)}) %collective-permute-start.4) | collective-permute-done | bytes 221216 | tf_op jit(solution)/shard_map/ppermute | solution.py:754
  19.2 1.5 %collective-permute-done.5.refs_1_ = bf16[144,768]{1,0:T(8,128)(2,1)S(1)} collective-permute-done((bf16[144,768]{1,0:T(8,128)(2,1)S(1)}, bf16[144,768]{1,0:T(8,128)(2,1)S(1)}, u32[]{:S(2)}, u32[]{:S(2)}) %collective-permute-start.5) | collective-permute-done | bytes 221216 | tf_op jit(solution)/shard_map/ppermute | solution.py:754
  20.6 1.5 %collective-permute-start.12 = (bf16[256,384]{1,0:T(8,128)(2,1)S(1)}, bf16[256,384]{1,0:T(8,128)(2,1)S(1)}, u32[]{:S(2)}, u32[]{:S(2)}) collective-permute-start(bf16[256,384]{1,0:T(8,128)(2,1)S(1)} %get-tuple-element.130.refs_2_), channel_id=1, source_target_pairs={{0,2},{1,3},{2,0},{3,1},{4,6},{5,7},{6,4},{7,5},{8,10},{9,11},{10,... | collective-permute-start | bytes 589832 | tf_op jit(solution)/shard_map/ppermute | solution.py:746
  22.9 3.5 %attention_forward.3 = (bf16[256,768]{1,0:T(8,128)(2,1)S(1)}, bf16[384,256]{1,0:T(8,128)(2,1)S(1)}, bf16[384,256]{1,0:T(8,128)(2,1)S(1)}, bf16[256,384]{1,0:T(8,...) custom-call(s32[7]{0:T(128)S(1)} %stack.31.refs_0_, ...), custom_call_target="tpu_custom_call" | custom-call | flops 3000000000 | bytes 100000000 | tf_op jit(solution)/shard_map/attention_forward/pallas_call | solution.py:145
  26.5 0.8 collective-permute-start.11
  27.3 1.5 %collective-permute-done.7.refs_6_ = bf16[144,768]{1,0:T(8,128)(2,1)S(1)} collective-permute-done((bf16[144,768]{1,0:T(8,128)(2,1)S(1)}, bf16[144,768]{1,0:T(8,128)(2,1)S(1)}, u32[]{:S(2)}, u32[]{:S(2)}) %collective-permute-start.7) | collective-permute-done | bytes 221216 | tf_op jit(solution)/shard_map/ppermute | solution.py:754
  28.8 1.5 %collective-permute-done.10.refs_9_ = bf16[144,768]{1,0:T(8,128)(2,1)S(1)} collective-permute-done((bf16[144,768]{1,0:T(8,128)(2,1)S(1)}, bf16[144,768]{1,0:T(8,128)(2,1)S(1)}, u32[]{:S(2)}, u32[]{:S(2)}) %collective-permute-start.10) | collective-permute-done | bytes 221216 | tf_op jit(solution)/shard_map/ppermute | solution.py:743
  30.2 0.9 pack_far.1
  31.1 1.2 %feed_in.1 = (f32[256,768]{1,0:T(8,128)S(1)}, f32[256,768]{1,0:T(8,128)S(1)}, f32[256,768]{1,0:T(8,128)S(1)}, f32[256,768]{1,0:T(8,128)S(1)}, f32[1,768]{1,0:T(1,128)S(1)}, /*index=5*/f32[8,128]{1,0:T(8,128)S(1)}) custom-call(bf16[256,768]{1,0:T(8,128)(2,1)S(1)} %get-tuple-element.126.refs_3_.refs_0_, ...), custom_call_target="tpu_custom_call" | custom-call | bytes 100000000 | tf_op jit(solution)/shard_map/feed_in/pallas_call | solution.py:145
  33.0 1.7 %feed_far.1 = (f32[256,768]{1,0:T(8,128)S(1)}, bf16[256,768]{1,0:T(8,128)(2,1)S(1)}, f32[384,768]{1,0:T(8,128)S(1)}, f32[384,768]{1,0:T(8,128)S(1)}, f32[8,128]{1,0:T(8,128)S(1)}) custom-call(f32[256,768]{1,0:T(8,128)S(1)} %get-tuple-element.155.refs_0_, bf16[256,384]{1,0:T(8,128)(2,1)S(1)} %collective-permute-done.12.refs_1_, ...), custom_call_target="tpu_custom_call" | custom-call | bytes 100000000 | tf_op jit(solution)/shard_map/feed_far/pallas_call | solution.py:145
  34.7 2.5 %attention_backward.2 = (bf16[256,768]{1,0:T(8,128)(2,1)S(1)}, bf16[1152,256]{1,0:T(8,128)(2,1)S(1)}, f32[8,128]{1,0:T(8,128)S(1)}) custom-call(bf16[256,768]{1,0:T(8,128)(2,1)S(1)} %get-tuple-element.158.refs_0_.refs_9_, bf16[768,768]{1,0:T(8,128)(2,1)S(1)} %get-tuple-element.153.refs_7_.refs_1_, f32[256,768]{1,0:T(8,128)S(1)} %get-tuple-element.161.refs_2_, ...), custom_call_target="tpu_custom_call" | custom-call | bytes 100000000 | tf_op jit(solution)/shard_map/attention_backward/pallas_call | solution.py:145
  37.3 1.8 %feed_own.1 = (f32[256,768]{1,0:T(8,128)S(1)}, bf16[256,768]{1,0:T(8,128)(2,1)S(1)}, bf16[256,768]{1,0:T(8,128)(2,1)S(1)}, bf16[2,192,768]{2,1,0:T(8,128)(2,1)S(...) custom-call(f32[256,768]{1,0:T(8,128)S(1)} %get-tuple-element.149.refs_0_, ...), custom_call_target="tpu_custom_call" | custom-call | bytes 100000000 | tf_op jit(solution)/shard_map/feed_own/pallas_call | solution.py:145
  39.2 2.5 %attention_backward.3 = (bf16[256,768]{1,0:T(8,128)(2,1)S(1)}, bf16[1152,256]{1,0:T(8,128)(2,1)S(1)}, f32[256,768]{1,0:T(8,128)S(1)}, f32[8,768]{1,0:T(8,128)S(1)}, f32[8,128]{1,0:T(8,128)S(1)}) custom-call(bf16[256,768]{1,0:T(8,128)(2,1)S(1)} %get-tuple-element.170.refs_0_, bf16[768,768]{1,0:T(8,128)(2,1)S(1)} %get-tuple-element.153.refs_7_.refs_1_, ...), custom_call_target="tpu_custom_call" | custom-call | flops 10000000000 | bytes 100000000 | tf_op jit(solution)/shard_map/attention_backward/pallas_call | solution.py:145
  42.2 1.9 %collective-permute-start.15 = (bf16[96,768]{1,0:T(8,128)(2,1)S(1)}, bf16[96,768]{1,0:T(8,128)(2,1)S(1)}, u32[]{:S(2)}, u32[]{:S(2)}) collective-permute-start(bf16[96,768]{1,0:T(8,128)(2,1)S(1)} %get-tuple-element.191), channel_id=1, source_target_pairs={{0,4},{1,9},{2,6},{3,11},{4,0},{5,13},{6,2},{7,15},{8,12},{9,1},{1... | collective-permute-start | bytes 442376 | tf_op jit(solution)/shard_map/ppermute | solution.py:754
  46.2 1.6 %collective-permute-start.18 = (bf16[96,768]{1,0:T(8,128)(2,1)S(1)}, bf16[96,768]{1,0:T(8,128)(2,1)S(1)}, u32[]{:S(2)}, u32[]{:S(2)}) collective-permute-start(bf16[96,768]{1,0:T(8,128)(2,1)S(1)} %get-tuple-element.196), channel_id=1, source_target_pairs={{0,4},{1,9},{2,6},{3,11},{4,0},{5,13},{6,2},{7,15},{8,12},{9,1},{1... | collective-permute-start | bytes 442376 | tf_op jit(solution)/shard_map/ppermute | solution.py:754
  48.3 1.7 %collective-permute-start.19 = (bf16[96,768]{1,0:T(8,128)(2,1)S(1)}, bf16[96,768]{1,0:T(8,128)(2,1)S(1)}, u32[]{:S(2)}, u32[]{:S(2)}) collective-permute-start(bf16[96,768]{1,0:T(8,128)(2,1)S(1)} %get-tuple-element.197), channel_id=1, source_target_pairs={{0,8},{1,5},{2,10},{3,7},{4,12},{5,1},{6,14},{7,3},{8,0},{9,13},{1... | collective-permute-start | bytes 442376 | tf_op jit(solution)/shard_map/ppermute | solution.py:754
  50.7 1.6 %collective-permute-start.17 = (bf16[192,768]{1,0:T(8,128)(2,1)S(1)}, bf16[192,768]{1,0:T(8,128)(2,1)S(1)}, u32[]{:S(2)}, u32[]{:S(2)}) collective-permute-start(bf16[192,768]{1,0:T(8,128)(2,1)S(1)} %get-tuple-element.195), channel_id=1, source_target_pairs={{0,4},{1,9},{2,6},{3,11},{4,0},{5,13},{6,2},{7,15},{8,12},{9,1},{1... | collective-permute-start | bytes 884744 | tf_op jit(solution)/shard_map/ppermute | solution.py:754
  52.3 2.2 %collective-permute-done.19.refs_4_ = bf16[96,768]{1,0:T(8,128)(2,1)S(1)} collective-permute-done((bf16[96,768]{1,0:T(8,128)(2,1)S(1)}, bf16[96,768]{1,0:T(8,128)(2,1)S(1)}, u32[]{:S(2)}, u32[]{:S(2)}) %collective-permute-start.19) | collective-permute-done | bytes 147488 | tf_op jit(solution)/shard_map/ppermute | solution.py:754
  55.2 3.0 %collective-permute-start.21 = (bf16[96,768]{1,0:T(8,128)(2,1)S(1)}, bf16[96,768]{1,0:T(8,128)(2,1)S(1)}, u32[]{:S(2)}, u32[]{:S(2)}) collective-permute-start(bf16[96,768]{1,0:T(8,128)(2,1)S(1)} %get-tuple-element.201.refs_0_), channel_id=1, source_target_pairs={{0,16},{1,17},{2,18},{3,19},{4,20},{5,21},{6,22},{7,23},{8,24},{9,... | collective-permute-start | bytes 442376 | tf_op jit(solution)/shard_map/ppermute | solution.py:754
  58.2 1.4 %collective-permute-start.16 = (bf16[192,768]{1,0:T(8,128)(2,1)S(1)}, bf16[192,768]{1,0:T(8,128)(2,1)S(1)}, u32[]{:S(2)}, u32[]{:S(2)}) collective-permute-start(bf16[192,768]{1,0:T(8,128)(2,1)S(1)} %get-tuple-element.194), channel_id=1, source_target_pairs={{0,4},{1,9},{2,6},{3,11},{4,0},{5,13},{6,2},{7,15},{8,12},{9,1},{1... | collective-permute-start | bytes 884744 | tf_op jit(solution)/shard_map/ppermute | solution.py:754
  60.3 2.0 %collective-permute-start.20 = (bf16[192,768]{1,0:T(8,128)(2,1)S(1)}, bf16[192,768]{1,0:T(8,128)(2,1)S(1)}, u32[]{:S(2)}, u32[]{:S(2)}) collective-permute-start(bf16[192,768]{1,0:T(8,128)(2,1)S(1)} %get-tuple-element.200), channel_id=1, source_target_pairs={{0,8},{1,5},{2,10},{3,7},{4,12},{5,1},{6,14},{7,3},{8,0},{9,13},{1... | collective-permute-start | bytes 884744 | tf_op jit(solution)/shard_map/ppermute | solution.py:754
  62.3 1.4 %input_grads.1 = (f32[256,768]{1,0:T(8,128)S(1)}, bf16[272,768]{1,0:T(8,128)(2,1)S(1)}, f32[8,128]{1,0:T(8,128)S(1)}) custom-call(bf16[1152,256]{1,0:T(8,128)(2,1)S(1)} %get-tuple-element.176.refs_0_.refs_4_.refs_8_, bf16[1152,256]{1,0:T(8,128)(2,1)S(1)} %get-tuple-element.177.refs_1_.refs_5_.refs_9_, ...), custom_call_target="tpu_custom_call" | custom-call | bytes 100000000 | tf_op jit(solution)/shard_map/input_grads/pallas_call | solution.py:145
  63.7 1.6 %collective-permute-start.23 = (bf16[272,768]{1,0:T(8,128)(2,1)S(1)}, bf16[272,768]{1,0:T(8,128)(2,1)S(1)}, u32[]{:S(2)}, u32[]{:S(2)}) collective-permute-start(bf16[272,768]{1,0:T(8,128)(2,1)S(1)} %get-tuple-element.208.refs_0_), channel_id=1, source_target_pairs={{0,2},{1,3},{2,0},{3,1},{4,6},{5,7},{6,4},{7,5},{8,10},{9,11},{10,... | collective-permute-start | bytes 1253384 | tf_op jit(solution)/shard_map/ppermute | solution.py:746
  65.5 2.6 %collective-permute-done.16.refs_3_ = bf16[192,768]{1,0:T(8,128)(2,1)S(1)} collective-permute-done((bf16[192,768]{1,0:T(8,128)(2,1)S(1)}, bf16[192,768]{1,0:T(8,128)(2,1)S(1)}, u32[]{:S(2)}, u32[]{:S(2)}) %collective-permute-start.16) | collective-permute-done | bytes 294944 | tf_op jit(solution)/shard_map/ppermute | solution.py:754
  68.8 0.9 collective-permute-start.22
  69.7 1.4 %collective-permute-start.26 = (bf16[96,768]{1,0:T(8,128)(2,1)S(1)}, bf16[96,768]{1,0:T(8,128)(2,1)S(1)}, u32[]{:S(2)}, u32[]{:S(2)}) collective-permute-start(bf16[96,768]{1,0:T(8,128)(2,1)S(1)} %get-tuple-element.211.refs_1_), channel_id=1, source_target_pairs={{0,4},{1,9},{2,6},{3,11},{4,0},{5,13},{6,2},{7,15},{8,12},{9,1},{1... | collective-permute-start | bytes 442376 | tf_op jit(solution)/shard_map/ppermute | solution.py:754
  71.1 0.9 collective-permute-done.25.refs_2_
  72.1 2.7 %collective-permute-done.26.refs_3_ = bf16[96,768]{1,0:T(8,128)(2,1)S(1)} collective-permute-done((bf16[96,768]{1,0:T(8,128)(2,1)S(1)}, bf16[96,768]{1,0:T(8,128)(2,1)S(1)}, u32[]{:S(2)}, u32[]{:S(2)}) %collective-permute-start.26) | collective-permute-done | bytes 147488 | tf_op jit(solution)/shard_map/ppermute | solution.py:754
  74.9 2.3 %collective-permute-done.27.refs_4_ = bf16[96,768]{1,0:T(8,128)(2,1)S(1)} collective-permute-done((bf16[96,768]{1,0:T(8,128)(2,1)S(1)}, bf16[96,768]{1,0:T(8,128)(2,1)S(1)}, u32[]{:S(2)}, u32[]{:S(2)}) %collective-permute-start.27) | collective-permute-done | bytes 147488 | tf_op jit(solution)/shard_map/ppermute | solution.py:754
  77.1 1.7 %place_sums.3 = (f32[192,768]{1,0:T(8,128)}, f32[192,768]{1,0:T(8,128)}, f32[8,128]{1,0:T(8,128)S(1)}) custom-call(s32[7]{0:T(128)S(1)} %stack.31.refs_0_, bf16[96,768]{1,0:T(8,128)(2,1)S(1)} %get-tuple-element.211.refs_1_, bf16[96,768]{1,0:T(8,128)(2,1)S(1)} %collective-permute-done.25.refs_2_, bf16[96,768]{1,0:T(8,128)(2,1)S(1)} %collective-permute-done.26.refs_3_, ...), custom_call_target="tpu_custom_call" | custom-call | bytes 100000000 | tf_op jit(solution)/shard_map/place_sums/pallas_call | solution.py:145
  78.9 1.4 %collective-permute-start.28 = (bf16[16,768]{1,0:T(8,128)(2,1)S(1)}, bf16[16,768]{1,0:T(8,128)(2,1)S(1)}, u32[]{:S(2)}, u32[]{:S(2)}) collective-permute-start(bf16[16,768]{1,0:T(8,128)(2,1)S(1)} %get-tuple-element.214.refs_2_), channel_id=1, source_target_pairs={{0,16},{1,17},{2,18},{3,19},{4,20},{5,21},{6,22},{7,23},{8,24},{9,... | collective-permute-start | bytes 73736 | tf_op jit(solution)/shard_map/ppermute | solution.py:754
  80.4 3.4 %collective-permute-done.28.refs_3_ = bf16[16,768]{1,0:T(8,128)(2,1)S(1)} collective-permute-done((bf16[16,768]{1,0:T(8,128)(2,1)S(1)}, bf16[16,768]{1,0:T(8,128)(2,1)S(1)}, u32[]{:S(2)}, u32[]{:S(2)}) %collective-permute-start.28) | collective-permute-done | bytes 24608 | tf_op jit(solution)/shard_map/ppermute | solution.py:754
  83.8 0.9 collective-permute-start.29
  84.7 1.2 %feed_result.1 = (bf16[256,768]{1,0:T(8,128)(2,1)}, f32[8,128]{1,0:T(8,128)S(1)}) custom-call(bf16[256,768]{1,0:T(8,128)(2,1)S(1)} %get-tuple-element.168.refs_0_, bf16[768,768]{1,0:T(8,128)(2,1)S(1)} %get-tuple-element.147.refs_7_.refs_1_, f32[256,768]{1,0:T(8,128)S(1)} %get-tuple-element.169.refs_2_, f32[8,128]{1,0:T(8,128)S(1)} %get-tuple-element.216.refs_3_), custom_call_target="tpu_custom_call" | custom-call | bytes 100000000 | tf_op jit(solution)/shard_map/feed_result/pallas_call | solution.py:145
  85.9 1.3 %input_norm.1 = (bf16[256,768]{1,0:T(8,128)(2,1)}, f32[8,128]{1,0:T(8,128)S(1)}) custom-call(bf16[256,768]{1,0:T(8,128)(2,1)S(1)} %get-tuple-element.126.refs_3_.refs_0_, f32[768]{0:T(1024)S(1)} %get-tuple-element.127.refs_4_.refs_1_, f32[256,768]{1,0:T(8,128)S(1)} %get-tuple-element.218.refs_2_, ...), custom_call_target="tpu_custom_call" | custom-call | bytes 100000000 | tf_op jit(solution)/shard_map/input_norm/pallas_call | solution.py:145
  87.3 1.4 %collective-permute-start.30 = (bf16[208,768]{1,0:T(8,128)(2,1)S(1)}, bf16[208,768]{1,0:T(8,128)(2,1)S(1)}, u32[]{:S(2)}, u32[]{:S(2)}) collective-permute-start(bf16[208,768]{1,0:T(8,128)(2,1)S(1)} %get-tuple-element.224.refs_1_), channel_id=1, source_target_pairs={{0,4},{1,9},{2,6},{3,11},{4,0},{5,13},{6,2},{7,15},{8,12},{9,1},{1... | collective-permute-start | bytes 958472 | tf_op jit(solution)/shard_map/ppermute | solution.py:754
  88.7 2.2 %collective-permute-done.29.refs_2_ = bf16[208,768]{1,0:T(8,128)(2,1)S(1)} collective-permute-done((bf16[208,768]{1,0:T(8,128)(2,1)S(1)}, bf16[208,768]{1,0:T(8,128)(2,1)S(1)}, u32[]{:S(2)}, u32[]{:S(2)}) %collective-permute-start.29) | collective-permute-done | bytes 319520 | tf_op jit(solution)/shard_map/ppermute | solution.py:754
  91.6 2.7 %collective-permute-done.30.refs_3_ = bf16[208,768]{1,0:T(8,128)(2,1)S(1)} collective-permute-done((bf16[208,768]{1,0:T(8,128)(2,1)S(1)}, bf16[208,768]{1,0:T(8,128)(2,1)S(1)}, u32[]{:S(2)}, u32[]{:S(2)}) %collective-permute-start.30) | collective-permute-done | bytes 319520 | tf_op jit(solution)/shard_map/ppermute | solution.py:754
  94.3 1.9 %place_sums.4 = (f32[3,192,768]{2,1,0:T(8,128)}, f32[192,768]{1,0:T(8,128)}, f32[8,128]{1,0:T(8,128)S(1)}) custom-call(s32[7]{0:T(128)S(1)} %stack.31.refs_0_, bf16[208,768]{1,0:T(8,128)(2,1)S(1)} %get-tuple-element.224.refs_1_, bf16[208,768]{1,0:T(8,128)(2,1)S(1)} %collective-permute-done.29.refs_2_, bf16[208,768]{1,0:T(8,128)(2,1)S(1)} %collective-permute-done.30.refs_3_, ...), custom_call_target="tpu_custom_call" | custom-call | bytes 100000000 | tf_op jit(solution)/shard_map/place_sums/pallas_call | solution.py:145
  96.2 1.6 %collective-permute-done.31.refs_4_ = bf16[208,768]{1,0:T(8,128)(2,1)S(1)} collective-permute-done((bf16[208,768]{1,0:T(8,128)(2,1)S(1)}, bf16[208,768]{1,0:T(8,128)(2,1)S(1)}, u32[]{:S(2)}, u32[]{:S(2)}) %collective-permute-start.31) | collective-permute-done | bytes 319520 | tf_op jit(solution)/shard_map/ppermute | solution.py:754
  97.8 1.5 %place_sums.5 = (f32[3,192,768]{2,1,0:T(8,128)}, f32[192,768]{1,0:T(8,128)}, f32[768]{0:T(1024)}, f32[768]{0:T(1024)}, f32[768]{0:T(1024)}, /*index=5*/f32[768]{0:T(1024)}, f32[192]{0:T(256)}) custom-call(s32[7]{0:T(128)S(1)} %stack.31.refs_0_, bf16[208,768]{1,0:T(8,128)(2,1)S(1)} %get-tuple-element.224.refs_1_, ...), custom_call_target="tpu_custom_call", output_to_operand_aliasing={{0}: (5, {}), {1}: (6, {})} | custom-call | bytes 100000000 | tf_op jit(solution)/shard_map/place_sums/pallas_call | solution.py:145
  (50 shorter events, 10.1 us)
Async XLA Ops:
  0.6 6.6 %collective-permute-start.1 = (bf16[3,192,768]{2,1,0:T(8,128)(2,1)}, bf16[3,192,768]{2,1,0:T(8,128)(2,1)S(1)}, u32[]{:S(2)}, u32[]{:S(2)}) collective-permute-start(bf16[3,192,768]{2,1,0:T(8,128)(2,1)} %refs_6_.3), channel_id=1, source_target_pairs={{0,1},{1,0},{2,3},{3,2},{4,5},{5,4},{6,7},{7,6},{8,9},{9,8},{10,11... | collective-permute-start | bytes 2654216 | tf_op jit(solution)/shard_map/ppermute | solution.py:743
  2.8 9.1 %collective-permute-start.3 = (bf16[448,256]{1,0:T(8,128)(2,1)S(1)}, bf16[448,256]{1,0:T(8,128)(2,1)S(1)}, u32[]{:S(2)}, u32[]{:S(2)}) collective-permute-start(bf16[448,256]{1,0:T(8,128)(2,1)S(1)} %get-tuple-element.124.refs_3_), channel_id=1, source_target_pairs={{0,2},{1,3},{2,0},{3,1},{4,6},{5,7},{6,4},{7,5},{8,10},{9,11},{10,... | collective-permute-start | bytes 688136 | tf_op jit(solution)/shard_map/ppermute | solution.py:746
  5.5 16.7 %collective-permute-start = (bf16[256,768]{1,0:T(8,128)(2,1)}, bf16[256,768]{1,0:T(8,128)(2,1)S(1)}, u32[]{:S(2)}, u32[]{:S(2)}) collective-permute-start(bf16[256,768]{1,0:T(8,128)(2,1)} %refs_4_.3), channel_id=1, source_target_pairs={{0,2},{1,3},{2,0},{3,1},{4,6},{5,7},{6,4},{7,5},{8,10},{9,11},{10,... | collective-permute-start | bytes 1179656 | tf_op jit(solution)/shard_map/ppermute | solution.py:746
  7.1 15.9 %collective-permute-start.2 = (bf16[592,768]{1,0:T(8,128)(2,1)S(1)}, bf16[592,768]{1,0:T(8,128)(2,1)S(1)}, u32[]{:S(2)}, u32[]{:S(2)}) collective-permute-start(bf16[592,768]{1,0:T(8,128)(2,1)S(1)} %get-tuple-element.132.refs_7_.refs_8_), channel_id=1, source_target_pairs={{0,1},{1,0},{2,3},{3,2},{4,5},{5,4},{6,7},{7,6},{8,9},{9,8},{10,11... | collective-permute-start | bytes 2727944 | tf_op jit(solution)/shard_map/ppermute | solution.py:743
  7.3 8.3 %copy-start = (bf16[256,768]{1,0:T(8,128)(2,1)S(1)}, bf16[256,768]{1,0:T(8,128)(2,1)}, u32[]{:S(2)}) copy-start(bf16[256,768]{1,0:T(8,128)(2,1)} %refs_5_.1) | copy-start | bytes 1179652
  12.0 7.2 %collective-permute-start.4 = (bf16[144,768]{1,0:T(8,128)(2,1)S(1)}, bf16[144,768]{1,0:T(8,128)(2,1)S(1)}, u32[]{:S(2)}, u32[]{:S(2)}) collective-permute-start(bf16[144,768]{1,0:T(8,128)(2,1)S(1)} %get-tuple-element.134), channel_id=1, source_target_pairs={{0,4},{1,5},{2,6},{3,7},{4,0},{5,1},{6,2},{7,3},{8,12},{9,13},{10,... | collective-permute-start | bytes 663560 | tf_op jit(solution)/shard_map/ppermute | solution.py:754
  13.9 6.8 %collective-permute-start.5 = (bf16[144,768]{1,0:T(8,128)(2,1)S(1)}, bf16[144,768]{1,0:T(8,128)(2,1)S(1)}, u32[]{:S(2)}, u32[]{:S(2)}) collective-permute-start(bf16[144,768]{1,0:T(8,128)(2,1)S(1)} %get-tuple-element.134), channel_id=1, source_target_pairs={{0,8},{1,9},{2,10},{3,11},{4,12},{5,13},{6,14},{7,15},{8,0},{9,1},... | collective-permute-start | bytes 663560 | tf_op jit(solution)/shard_map/ppermute | solution.py:754
  15.5 15.6 %collective-permute-start.6 = (bf16[256,768]{1,0:T(8,128)(2,1)S(1)}, bf16[256,768]{1,0:T(8,128)(2,1)S(1)}, u32[]{:S(2)}, u32[]{:S(2)}) collective-permute-start(bf16[256,768]{1,0:T(8,128)(2,1)S(1)} %copy-done), channel_id=1, source_target_pairs={{0,2},{1,3},{2,0},{3,1},{4,6},{5,7},{6,4},{7,5},{8,10},{9,11},{10,... | collective-permute-start | bytes 1179656 | tf_op jit(solution)/shard_map/ppermute | solution.py:746
  19.2 7.3 %collective-permute-start.8 = (bf16[160,768]{1,0:T(8,128)(2,1)S(1)}, bf16[160,768]{1,0:T(8,128)(2,1)S(1)}, u32[]{:S(2)}, u32[]{:S(2)}) collective-permute-start(bf16[160,768]{1,0:T(8,128)(2,1)S(1)} %get-tuple-element.142.refs_4_.refs_10_), channel_id=1, source_target_pairs={{0,1},{1,0},{2,3},{3,2},{4,5},{5,4},{6,7},{7,6},{8,9},{9,8},{10,11... | collective-permute-start | bytes 737288 | tf_op jit(solution)/shard_map/ppermute | solution.py:743
  20.6 12.4 %collective-permute-start.12 = (bf16[256,384]{1,0:T(8,128)(2,1)S(1)}, bf16[256,384]{1,0:T(8,128)(2,1)S(1)}, u32[]{:S(2)}, u32[]{:S(2)}) collective-permute-start(bf16[256,384]{1,0:T(8,128)(2,1)S(1)} %get-tuple-element.130.refs_2_), channel_id=1, source_target_pairs={{0,2},{1,3},{2,0},{3,1},{4,6},{5,7},{6,4},{7,5},{8,10},{9,11},{10,... | collective-permute-start | bytes 589832 | tf_op jit(solution)/shard_map/ppermute | solution.py:746
  22.2 6.5 %collective-permute-start.7 = (bf16[144,768]{1,0:T(8,128)(2,1)S(1)}, bf16[144,768]{1,0:T(8,128)(2,1)S(1)}, u32[]{:S(2)}, u32[]{:S(2)}) collective-permute-start(bf16[144,768]{1,0:T(8,128)(2,1)S(1)} %get-tuple-element.144), channel_id=1, source_target_pairs={{0,4},{1,5},{2,6},{3,7},{4,0},{5,1},{6,2},{7,3},{8,12},{9,13},{10,... | collective-permute-start | bytes 663560 | tf_op jit(solution)/shard_map/ppermute | solution.py:754
  22.9 7.3 %collective-permute-start.9 = (bf16[2,144,768]{2,1,0:T(8,128)(2,1)S(1)}, bf16[2,144,768]{2,1,0:T(8,128)(2,1)S(1)}, u32[]{:S(2)}, u32[]{:S(2)}) collective-permute-start(bf16[2,144,768]{2,1,0:T(8,128)(2,1)S(1)} %get-tuple-element.143.refs_5_), channel_id=1, source_target_pairs={{0,1},{1,0},{2,3},{3,2},{4,5},{5,4},{6,7},{7,6},{8,9},{9,8},{10,11... | collective-permute-start | bytes 1327112 | tf_op jit(solution)/shard_map/ppermute | solution.py:743
  26.5 10.8 %collective-permute-start.11 = (bf16[256,384]{1,0:T(8,128)(2,1)S(1)}, bf16[256,384]{1,0:T(8,128)(2,1)S(1)}, u32[]{:S(2)}, u32[]{:S(2)}) collective-permute-start(bf16[256,384]{1,0:T(8,128)(2,1)S(1)} %get-tuple-element.137.refs_3_), channel_id=1, source_target_pairs={{0,2},{1,3},{2,0},{3,1},{4,6},{5,7},{6,4},{7,5},{8,10},{9,11},{10,... | collective-permute-start | bytes 589832 | tf_op jit(solution)/shard_map/ppermute | solution.py:746
  28.8 1.5 %collective-permute-start.10 = (bf16[144,768]{1,0:T(8,128)(2,1)S(1)}, bf16[144,768]{1,0:T(8,128)(2,1)S(1)}, u32[]{:S(2)}, u32[]{:S(2)}) collective-permute-start(bf16[144,768]{1,0:T(8,128)(2,1)S(1)} %collective-permute-done.7.refs_6_), channel_id=1, source_target_pairs={{0,1},{1,0},{2,3},{3,2},{4,5},{5,4},{6,7},{7,6},{8,9},{9,8},{10,11... | collective-permute-start | bytes 663560 | tf_op jit(solution)/shard_map/ppermute | solution.py:743
  39.1 2.6 %collective-permute-start.13 = (bf16[2,192,768]{2,1,0:T(8,128)(2,1)S(1)}, bf16[2,192,768]{2,1,0:T(8,128)(2,1)S(1)}, u32[]{:S(2)}, u32[]{:S(2)}) collective-permute-start(bf16[2,192,768]{2,1,0:T(8,128)(2,1)S(1)} %get-tuple-element.185), channel_id=1, source_target_pairs={{0,1},{1,0},{2,3},{3,2},{4,5},{5,4},{6,7},{7,6},{8,9},{9,8},{10,11... | collective-permute-start | bytes 1769480 | tf_op jit(solution)/shard_map/ppermute | solution.py:743
  42.2 5.5 %collective-permute-start.15 = (bf16[96,768]{1,0:T(8,128)(2,1)S(1)}, bf16[96,768]{1,0:T(8,128)(2,1)S(1)}, u32[]{:S(2)}, u32[]{:S(2)}) collective-permute-start(bf16[96,768]{1,0:T(8,128)(2,1)S(1)} %get-tuple-element.191), channel_id=1, source_target_pairs={{0,4},{1,9},{2,6},{3,11},{4,0},{5,13},{6,2},{7,15},{8,12},{9,1},{1... | collective-permute-start | bytes 442376 | tf_op jit(solution)/shard_map/ppermute | solution.py:754
  45.8 4.3 %collective-permute-start.14 = (bf16[4,192,768]{2,1,0:T(8,128)(2,1)S(1)}, bf16[4,192,768]{2,1,0:T(8,128)(2,1)S(1)}, u32[]{:S(2)}, u32[]{:S(2)}) collective-permute-start(bf16[4,192,768]{2,1,0:T(8,128)(2,1)S(1)} %get-tuple-element.190), channel_id=1, source_target_pairs={{0,1},{1,0},{2,3},{3,2},{4,5},{5,4},{6,7},{7,6},{8,9},{9,8},{10,11... | collective-permute-start | bytes 3538952 | tf_op jit(solution)/shard_map/ppermute | solution.py:743
  46.2 6.2 %collective-permute-start.18 = (bf16[96,768]{1,0:T(8,128)(2,1)S(1)}, bf16[96,768]{1,0:T(8,128)(2,1)S(1)}, u32[]{:S(2)}, u32[]{:S(2)}) collective-permute-start(bf16[96,768]{1,0:T(8,128)(2,1)S(1)} %get-tuple-element.196), channel_id=1, source_target_pairs={{0,4},{1,9},{2,6},{3,11},{4,0},{5,13},{6,2},{7,15},{8,12},{9,1},{1... | collective-permute-start | bytes 442376 | tf_op jit(solution)/shard_map/ppermute | solution.py:754
  48.3 6.2 %collective-permute-start.19 = (bf16[96,768]{1,0:T(8,128)(2,1)S(1)}, bf16[96,768]{1,0:T(8,128)(2,1)S(1)}, u32[]{:S(2)}, u32[]{:S(2)}) collective-permute-start(bf16[96,768]{1,0:T(8,128)(2,1)S(1)} %get-tuple-element.197), channel_id=1, source_target_pairs={{0,8},{1,5},{2,10},{3,7},{4,12},{5,1},{6,14},{7,3},{8,0},{9,13},{1... | collective-permute-start | bytes 442376 | tf_op jit(solution)/shard_map/ppermute | solution.py:754
  50.7 8.9 %collective-permute-start.17 = (bf16[192,768]{1,0:T(8,128)(2,1)S(1)}, bf16[192,768]{1,0:T(8,128)(2,1)S(1)}, u32[]{:S(2)}, u32[]{:S(2)}) collective-permute-start(bf16[192,768]{1,0:T(8,128)(2,1)S(1)} %get-tuple-element.195), channel_id=1, source_target_pairs={{0,4},{1,9},{2,6},{3,11},{4,0},{5,13},{6,2},{7,15},{8,12},{9,1},{1... | collective-permute-start | bytes 884744 | tf_op jit(solution)/shard_map/ppermute | solution.py:754
  55.2 10.1 %collective-permute-start.21 = (bf16[96,768]{1,0:T(8,128)(2,1)S(1)}, bf16[96,768]{1,0:T(8,128)(2,1)S(1)}, u32[]{:S(2)}, u32[]{:S(2)}) collective-permute-start(bf16[96,768]{1,0:T(8,128)(2,1)S(1)} %get-tuple-element.201.refs_0_), channel_id=1, source_target_pairs={{0,16},{1,17},{2,18},{3,19},{4,20},{5,21},{6,22},{7,23},{8,24},{9,... | collective-permute-start | bytes 442376 | tf_op jit(solution)/shard_map/ppermute | solution.py:754
  58.2 9.9 %collective-permute-start.16 = (bf16[192,768]{1,0:T(8,128)(2,1)S(1)}, bf16[192,768]{1,0:T(8,128)(2,1)S(1)}, u32[]{:S(2)}, u32[]{:S(2)}) collective-permute-start(bf16[192,768]{1,0:T(8,128)(2,1)S(1)} %get-tuple-element.194), channel_id=1, source_target_pairs={{0,4},{1,9},{2,6},{3,11},{4,0},{5,13},{6,2},{7,15},{8,12},{9,1},{1... | collective-permute-start | bytes 884744 | tf_op jit(solution)/shard_map/ppermute | solution.py:754
  60.3 7.8 %collective-permute-start.20 = (bf16[192,768]{1,0:T(8,128)(2,1)S(1)}, bf16[192,768]{1,0:T(8,128)(2,1)S(1)}, u32[]{:S(2)}, u32[]{:S(2)}) collective-permute-start(bf16[192,768]{1,0:T(8,128)(2,1)S(1)} %get-tuple-element.200), channel_id=1, source_target_pairs={{0,8},{1,5},{2,10},{3,7},{4,12},{5,1},{6,14},{7,3},{8,0},{9,13},{1... | collective-permute-start | bytes 884744 | tf_op jit(solution)/shard_map/ppermute | solution.py:754
  63.7 8.3 %collective-permute-start.23 = (bf16[272,768]{1,0:T(8,128)(2,1)S(1)}, bf16[272,768]{1,0:T(8,128)(2,1)S(1)}, u32[]{:S(2)}, u32[]{:S(2)}) collective-permute-start(bf16[272,768]{1,0:T(8,128)(2,1)S(1)} %get-tuple-element.208.refs_0_), channel_id=1, source_target_pairs={{0,2},{1,3},{2,0},{3,1},{4,6},{5,7},{6,4},{7,5},{8,10},{9,11},{10,... | collective-permute-start | bytes 1253384 | tf_op jit(solution)/shard_map/ppermute | solution.py:746
  65.4 6.6 %collective-permute-start.25 = (bf16[96,768]{1,0:T(8,128)(2,1)S(1)}, bf16[96,768]{1,0:T(8,128)(2,1)S(1)}, u32[]{:S(2)}, u32[]{:S(2)}) collective-permute-start(bf16[96,768]{1,0:T(8,128)(2,1)S(1)} %get-tuple-element.211.refs_1_), channel_id=1, source_target_pairs={{0,8},{1,5},{2,10},{3,7},{4,12},{5,1},{6,14},{7,3},{8,0},{9,13},{1... | collective-permute-start | bytes 442376 | tf_op jit(solution)/shard_map/ppermute | solution.py:754
  68.8 14.9 %collective-permute-start.22 = (bf16[192,768]{1,0:T(8,128)(2,1)S(1)}, bf16[192,768]{1,0:T(8,128)(2,1)S(1)}, u32[]{:S(2)}, u32[]{:S(2)}) collective-permute-start(bf16[192,768]{1,0:T(8,128)(2,1)S(1)} %get-tuple-element.207.refs_0_), channel_id=1, source_target_pairs={{0,16},{1,17},{2,18},{3,19},{4,20},{5,21},{6,22},{7,23},{8,24},{9,... | collective-permute-start | bytes 884744 | tf_op jit(solution)/shard_map/ppermute | solution.py:754
  69.7 5.1 %collective-permute-start.26 = (bf16[96,768]{1,0:T(8,128)(2,1)S(1)}, bf16[96,768]{1,0:T(8,128)(2,1)S(1)}, u32[]{:S(2)}, u32[]{:S(2)}) collective-permute-start(bf16[96,768]{1,0:T(8,128)(2,1)S(1)} %get-tuple-element.211.refs_1_), channel_id=1, source_target_pairs={{0,4},{1,9},{2,6},{3,11},{4,0},{5,13},{6,2},{7,15},{8,12},{9,1},{1... | collective-permute-start | bytes 442376 | tf_op jit(solution)/shard_map/ppermute | solution.py:754
  72.0 5.1 %collective-permute-start.27 = (bf16[96,768]{1,0:T(8,128)(2,1)S(1)}, bf16[96,768]{1,0:T(8,128)(2,1)S(1)}, u32[]{:S(2)}, u32[]{:S(2)}) collective-permute-start(bf16[96,768]{1,0:T(8,128)(2,1)S(1)} %collective-permute-done.25.refs_2_), channel_id=1, source_target_pairs={{0,4},{1,9},{2,6},{3,11},{4,0},{5,13},{6,2},{7,15},{8,12},{9,1},{1... | collective-permute-start | bytes 442376 | tf_op jit(solution)/shard_map/ppermute | solution.py:754
  72.0 6.8 %collective-permute-start.24 = (bf16[16,768]{1,0:T(8,128)(2,1)S(1)}, bf16[16,768]{1,0:T(8,128)(2,1)S(1)}, u32[]{:S(2)}, u32[]{:S(2)}) collective-permute-start(bf16[16,768]{1,0:T(8,128)(2,1)S(1)} %get-tuple-element.210.refs_0_), channel_id=1, source_target_pairs={{0,1},{1,0},{2,3},{3,2},{4,5},{5,4},{6,7},{7,6},{8,9},{9,8},{10,11... | collective-permute-start | bytes 73736 | tf_op jit(solution)/shard_map/ppermute | solution.py:743
  78.9 4.8 %collective-permute-start.28 = (bf16[16,768]{1,0:T(8,128)(2,1)S(1)}, bf16[16,768]{1,0:T(8,128)(2,1)S(1)}, u32[]{:S(2)}, u32[]{:S(2)}) collective-permute-start(bf16[16,768]{1,0:T(8,128)(2,1)S(1)} %get-tuple-element.214.refs_2_), channel_id=1, source_target_pairs={{0,16},{1,17},{2,18},{3,19},{4,20},{5,21},{6,22},{7,23},{8,24},{9,... | collective-permute-start | bytes 73736 | tf_op jit(solution)/shard_map/ppermute | solution.py:754
  83.8 7.1 %collective-permute-start.29 = (bf16[208,768]{1,0:T(8,128)(2,1)S(1)}, bf16[208,768]{1,0:T(8,128)(2,1)S(1)}, u32[]{:S(2)}, u32[]{:S(2)}) collective-permute-start(bf16[208,768]{1,0:T(8,128)(2,1)S(1)} %get-tuple-element.224.refs_1_), channel_id=1, source_target_pairs={{0,8},{1,5},{2,10},{3,7},{4,12},{5,1},{6,14},{7,3},{8,0},{9,13},{1... | collective-permute-start | bytes 958472 | tf_op jit(solution)/shard_map/ppermute | solution.py:754
  87.3 7.1 %collective-permute-start.30 = (bf16[208,768]{1,0:T(8,128)(2,1)S(1)}, bf16[208,768]{1,0:T(8,128)(2,1)S(1)}, u32[]{:S(2)}, u32[]{:S(2)}) collective-permute-start(bf16[208,768]{1,0:T(8,128)(2,1)S(1)} %get-tuple-element.224.refs_1_), channel_id=1, source_target_pairs={{0,4},{1,9},{2,6},{3,11},{4,0},{5,13},{6,2},{7,15},{8,12},{9,1},{1... | collective-permute-start | bytes 958472 | tf_op jit(solution)/shard_map/ppermute | solution.py:754
  90.8 7.0 %collective-permute-start.31 = (bf16[208,768]{1,0:T(8,128)(2,1)S(1)}, bf16[208,768]{1,0:T(8,128)(2,1)S(1)}, u32[]{:S(2)}, u32[]{:S(2)}) collective-permute-start(bf16[208,768]{1,0:T(8,128)(2,1)S(1)} %collective-permute-done.29.refs_2_), channel_id=1, source_target_pairs={{0,4},{1,9},{2,6},{3,11},{4,0},{5,13},{6,2},{7,15},{8,12},{9,1},{1... | collective-permute-start | bytes 958472 | tf_op jit(solution)/shard_map/ppermute | solution.py:754

commit v12 on v11

--- a/solution.py
+++ b/solution.py
@@ -72,7 +72,7 @@
 
 
 STRIP = 256
-COSTS = (0, 0, 100, 0, 0, 30, 30, 0, 0, 0, 0, 0, 100, 0, 0, 0, 200, 0, 60, 0, 0, 30, 0, 0, 0, 0, 0, 0, 0, 0, 0, 0)
+COSTS = (0, 0, 100, 0, 0, 30, 30, 0, 0, 0, 0, 0, 100, 0, 0, 0, 200, 0, 30, 0, 0, 30, 0, 0, 0, 0, 0, 0, 0, 0, 0, 0)
 
 
 class IO:
@@ -875,8 +875,8 @@
     vec = vector_cores(chain, vec, vec_got, shard)
     vec_got = swap_dp(vec, far_masks[0], far_masks[0])
     q.fourth((vec, vec_got))
+    grad_tokens = input_norm(chain, tokens, ln1_gain, da1_mine, da1_got, dh)
     result = feed_result(chain, z_0, fc2, h_0)
-    grad_tokens = input_norm(chain, tokens, ln1_gain, da1_mine, da1_got, dh)
     q.fifth()
     each = [(0, 0, 0), (0, 1, 0), (0, 2, 0), (1, None, 0)]
     outs = [f32(3, shard, d), f32(shard, d)]

time: 99.7 us -> 99.7 us (level)
  no operation moved by 1% of the time
where the time goes in v12:
time: 99.7 us; the launch traced here: 99.5 us
  Pallas kernels  36 us (36%)
  starting transfers between devices  33.9 us (34%)
  waiting for transfers between devices  28.4 us (28%)
  between operations  1.13 us (1%)
    pallas_call x31, Pallas kernels, call(): pl.pallas_call(body, in_specs=[spec(kind) for kind in ins] + [vmem] * len...  36 us
    ppermute x18, waiting for transfers between devices, swap_dp(): return lax.ppermute(a, ('dp', 'tensor'), pairs)  25.6 us
    ppermute x18, starting transfers between devices, swap_dp(): return lax.ppermute(a, ('dp', 'tensor'), pairs)  24.4 us
    ppermute x6, starting transfers between devices, swap_y(): return lax.ppermute(a, 'tensor', [(t, t ^ 2) for t in range(n_tensor)])  8.19 us
  transfers between devices with their start and end apart: 32, of which 15 were waited for; matrix products, arithmetic and copies ran while one was open for 0% of the time, Pallas kernels for 32%

profile of v12, /device:TPU:0, one launch (start us, length us, event | category | flops | bytes accessed | tf_op | source)
XLA Modules:
  0.0 99.5 jit_solution(15720855189362967342)
XLA Ops:
  1.2 1.6 %pick.1 = (bf16[448,256]{1,0:T(8,128)(2,1)S(1)}, f32[8,128]{1,0:T(8,128)S(1)}) custom-call(s32[7]{0:T(128)S(1)} %stack.31.refs_0_, bf16[192,768]{1,0:T(8,128)(2,1)} %refs_0_.1, bf16[192,768]{1,0:T(8,128)(2,1)} %refs_1_.5, bf16[192,768]{1,0:T(8,128)(2,1)} %refs_2_.5, bf16[192]{0:T(256)(128)(2,1)} %refs_4_.2), custom_call_target="tpu_custom_call" | custom-call | bytes 100000000 | tf_op jit(solution)/shard_map/pick/pallas_call | solution.py:145
  2.8 2.6 %collective-permute-start.3 = (bf16[448,256]{1,0:T(8,128)(2,1)S(1)}, bf16[448,256]{1,0:T(8,128)(2,1)S(1)}, u32[]{:S(2)}, u32[]{:S(2)}) collective-permute-start(bf16[448,256]{1,0:T(8,128)(2,1)S(1)} %get-tuple-element.124.refs_3_), channel_id=1, source_target_pairs={{0,2},{1,3},{2,0},{3,1},{4,6},{5,7},{6,4},{7,5},{8,10},{9,11},{10,... | collective-permute-start | bytes 688136 | tf_op jit(solution)/shard_map/ppermute | solution.py:746
  5.6 1.5 %load.1 = (bf16[592,768]{1,0:T(8,128)(2,1)S(1)}, bf16[256,768]{1,0:T(8,128)(2,1)S(1)}, bf16[256,768]{1,0:T(8,128)(2,1)S(1)}, f32[768]{0:T(1024)S(1)}, f32[768]{0...) custom-call(bf16[192,768]{1,0:T(8,128)(2,1)} %refs_0_.1, bf16[192,768]{1,0:T(8,128)(2,1)} %refs_1_.5, ...), custom_call_target="tpu_custom_call" | custom-call | bytes 100000000 | tf_op jit(solution)/shard_map/load/pallas_call | solution.py:145
  7.3 4.0 %attention_forward.2 = (bf16[256,768]{1,0:T(8,128)(2,1)S(1)}, bf16[384,256]{1,0:T(8,128)(2,1)S(1)}, bf16[384,256]{1,0:T(8,128)(2,1)S(1)}, bf16[256,384]{1,0:T(8,...) custom-call(s32[7]{0:T(128)S(1)} %stack.31.refs_0_, ...), custom_call_target="tpu_custom_call" | custom-call | flops 10000000000 | bytes 100000000 | tf_op jit(solution)/shard_map/attention_forward/pallas_call | solution.py:145
  12.0 1.9 %collective-permute-start.4 = (bf16[144,768]{1,0:T(8,128)(2,1)S(1)}, bf16[144,768]{1,0:T(8,128)(2,1)S(1)}, u32[]{:S(2)}, u32[]{:S(2)}) collective-permute-start(bf16[144,768]{1,0:T(8,128)(2,1)S(1)} %get-tuple-element.134), channel_id=1, source_target_pairs={{0,4},{1,5},{2,6},{3,7},{4,0},{5,1},{6,2},{7,3},{8,12},{9,13},{10,... | collective-permute-start | bytes 663560 | tf_op jit(solution)/shard_map/ppermute | solution.py:754
  13.9 1.7 %collective-permute-start.5 = (bf16[144,768]{1,0:T(8,128)(2,1)S(1)}, bf16[144,768]{1,0:T(8,128)(2,1)S(1)}, u32[]{:S(2)}, u32[]{:S(2)}) collective-permute-start(bf16[144,768]{1,0:T(8,128)(2,1)S(1)} %get-tuple-element.134), channel_id=1, source_target_pairs={{0,8},{1,9},{2,10},{3,11},{4,12},{5,13},{6,14},{7,15},{8,0},{9,1},... | collective-permute-start | bytes 663560 | tf_op jit(solution)/shard_map/ppermute | solution.py:754
  15.5 1.5 %collective-permute-start.6 = (bf16[256,768]{1,0:T(8,128)(2,1)S(1)}, bf16[256,768]{1,0:T(8,128)(2,1)S(1)}, u32[]{:S(2)}, u32[]{:S(2)}) collective-permute-start(bf16[256,768]{1,0:T(8,128)(2,1)S(1)} %copy-done), channel_id=1, source_target_pairs={{0,2},{1,3},{2,0},{3,1},{4,6},{5,7},{6,4},{7,5},{8,10},{9,11},{10,... | collective-permute-start | bytes 1179656 | tf_op jit(solution)/shard_map/ppermute | solution.py:746
  17.1 2.1 %collective-permute-done.4.refs_0_ = bf16[144,768]{1,0:T(8,128)(2,1)S(1)} collective-permute-done((bf16[144,768]{1,0:T(8,128)(2,1)S(1)}, bf16[144,768]{1,0:T(8,128)(2,1)S(1)}, u32[]{:S(2)}, u32[]{:S(2)}) %collective-permute-start.4) | collective-permute-done | bytes 221216 | tf_op jit(solution)/shard_map/ppermute | solution.py:754
  19.2 1.5 %collective-permute-done.5.refs_1_ = bf16[144,768]{1,0:T(8,128)(2,1)S(1)} collective-permute-done((bf16[144,768]{1,0:T(8,128)(2,1)S(1)}, bf16[144,768]{1,0:T(8,128)(2,1)S(1)}, u32[]{:S(2)}, u32[]{:S(2)}) %collective-permute-start.5) | collective-permute-done | bytes 221216 | tf_op jit(solution)/shard_map/ppermute | solution.py:754
  20.6 1.5 %collective-permute-start.12 = (bf16[256,384]{1,0:T(8,128)(2,1)S(1)}, bf16[256,384]{1,0:T(8,128)(2,1)S(1)}, u32[]{:S(2)}, u32[]{:S(2)}) collective-permute-start(bf16[256,384]{1,0:T(8,128)(2,1)S(1)} %get-tuple-element.130.refs_2_), channel_id=1, source_target_pairs={{0,2},{1,3},{2,0},{3,1},{4,6},{5,7},{6,4},{7,5},{8,10},{9,11},{10,... | collective-permute-start | bytes 589832 | tf_op jit(solution)/shard_map/ppermute | solution.py:746
  22.9 3.5 %attention_forward.3 = (bf16[256,768]{1,0:T(8,128)(2,1)S(1)}, bf16[384,256]{1,0:T(8,128)(2,1)S(1)}, bf16[384,256]{1,0:T(8,128)(2,1)S(1)}, bf16[256,384]{1,0:T(8,...) custom-call(s32[7]{0:T(128)S(1)} %stack.31.refs_0_, ...), custom_call_target="tpu_custom_call" | custom-call | flops 3000000000 | bytes 100000000 | tf_op jit(solution)/shard_map/attention_forward/pallas_call | solution.py:145
  26.5 0.8 collective-permute-start.11
  27.3 1.5 %collective-permute-done.7.refs_6_ = bf16[144,768]{1,0:T(8,128)(2,1)S(1)} collective-permute-done((bf16[144,768]{1,0:T(8,128)(2,1)S(1)}, bf16[144,768]{1,0:T(8,128)(2,1)S(1)}, u32[]{:S(2)}, u32[]{:S(2)}) %collective-permute-start.7) | collective-permute-done | bytes 221216 | tf_op jit(solution)/shard_map/ppermute | solution.py:754
  28.8 1.5 %collective-permute-done.10.refs_9_ = bf16[144,768]{1,0:T(8,128)(2,1)S(1)} collective-permute-done((bf16[144,768]{1,0:T(8,128)(2,1)S(1)}, bf16[144,768]{1,0:T(8,128)(2,1)S(1)}, u32[]{:S(2)}, u32[]{:S(2)}) %collective-permute-start.10) | collective-permute-done | bytes 221216 | tf_op jit(solution)/shard_map/ppermute | solution.py:743
  30.2 0.9 pack_far.1
  31.1 1.2 %feed_in.1 = (f32[256,768]{1,0:T(8,128)S(1)}, f32[256,768]{1,0:T(8,128)S(1)}, f32[256,768]{1,0:T(8,128)S(1)}, f32[256,768]{1,0:T(8,128)S(1)}, f32[1,768]{1,0:T(1,128)S(1)}, /*index=5*/f32[8,128]{1,0:T(8,128)S(1)}) custom-call(bf16[256,768]{1,0:T(8,128)(2,1)S(1)} %get-tuple-element.126.refs_3_.refs_0_, ...), custom_call_target="tpu_custom_call" | custom-call | bytes 100000000 | tf_op jit(solution)/shard_map/feed_in/pallas_call | solution.py:145
  33.0 1.7 %feed_far.1 = (f32[256,768]{1,0:T(8,128)S(1)}, bf16[256,768]{1,0:T(8,128)(2,1)S(1)}, f32[384,768]{1,0:T(8,128)S(1)}, f32[384,768]{1,0:T(8,128)S(1)}, f32[8,128]{1,0:T(8,128)S(1)}) custom-call(f32[256,768]{1,0:T(8,128)S(1)} %get-tuple-element.155.refs_0_, bf16[256,384]{1,0:T(8,128)(2,1)S(1)} %collective-permute-done.12.refs_1_, ...), custom_call_target="tpu_custom_call" | custom-call | bytes 100000000 | tf_op jit(solution)/shard_map/feed_far/pallas_call | solution.py:145
  34.7 2.5 %attention_backward.2 = (bf16[256,768]{1,0:T(8,128)(2,1)S(1)}, bf16[1152,256]{1,0:T(8,128)(2,1)S(1)}, f32[8,128]{1,0:T(8,128)S(1)}) custom-call(bf16[256,768]{1,0:T(8,128)(2,1)S(1)} %get-tuple-element.158.refs_0_.refs_9_, bf16[768,768]{1,0:T(8,128)(2,1)S(1)} %get-tuple-element.153.refs_7_.refs_1_, f32[256,768]{1,0:T(8,128)S(1)} %get-tuple-element.161.refs_2_, ...), custom_call_target="tpu_custom_call" | custom-call | bytes 100000000 | tf_op jit(solution)/shard_map/attention_backward/pallas_call | solution.py:145
  37.3 1.8 %feed_own.1 = (f32[256,768]{1,0:T(8,128)S(1)}, bf16[256,768]{1,0:T(8,128)(2,1)S(1)}, bf16[256,768]{1,0:T(8,128)(2,1)S(1)}, bf16[2,192,768]{2,1,0:T(8,128)(2,1)S(...) custom-call(f32[256,768]{1,0:T(8,128)S(1)} %get-tuple-element.149.refs_0_, ...), custom_call_target="tpu_custom_call" | custom-call | bytes 100000000 | tf_op jit(solution)/shard_map/feed_own/pallas_call | solution.py:145
  39.2 2.5 %attention_backward.3 = (bf16[256,768]{1,0:T(8,128)(2,1)S(1)}, bf16[1152,256]{1,0:T(8,128)(2,1)S(1)}, f32[256,768]{1,0:T(8,128)S(1)}, f32[8,768]{1,0:T(8,128)S(1)}, f32[8,128]{1,0:T(8,128)S(1)}) custom-call(bf16[256,768]{1,0:T(8,128)(2,1)S(1)} %get-tuple-element.170.refs_0_, bf16[768,768]{1,0:T(8,128)(2,1)S(1)} %get-tuple-element.153.refs_7_.refs_1_, ...), custom_call_target="tpu_custom_call" | custom-call | flops 10000000000 | bytes 100000000 | tf_op jit(solution)/shard_map/attention_backward/pallas_call | solution.py:145
  42.2 1.9 %collective-permute-start.15 = (bf16[96,768]{1,0:T(8,128)(2,1)S(1)}, bf16[96,768]{1,0:T(8,128)(2,1)S(1)}, u32[]{:S(2)}, u32[]{:S(2)}) collective-permute-start(bf16[96,768]{1,0:T(8,128)(2,1)S(1)} %get-tuple-element.193), channel_id=1, source_target_pairs={{0,4},{1,9},{2,6},{3,11},{4,0},{5,13},{6,2},{7,15},{8,12},{9,1},{1... | collective-permute-start | bytes 442376 | tf_op jit(solution)/shard_map/ppermute | solution.py:754
  46.2 1.6 %collective-permute-start.17 = (bf16[96,768]{1,0:T(8,128)(2,1)S(1)}, bf16[96,768]{1,0:T(8,128)(2,1)S(1)}, u32[]{:S(2)}, u32[]{:S(2)}) collective-permute-start(bf16[96,768]{1,0:T(8,128)(2,1)S(1)} %get-tuple-element.197), channel_id=1, source_target_pairs={{0,4},{1,9},{2,6},{3,11},{4,0},{5,13},{6,2},{7,15},{8,12},{9,1},{1... | collective-permute-start | bytes 442376 | tf_op jit(solution)/shard_map/ppermute | solution.py:754
  48.3 1.7 %collective-permute-start.18 = (bf16[96,768]{1,0:T(8,128)(2,1)S(1)}, bf16[96,768]{1,0:T(8,128)(2,1)S(1)}, u32[]{:S(2)}, u32[]{:S(2)}) collective-permute-start(bf16[96,768]{1,0:T(8,128)(2,1)S(1)} %get-tuple-element.198), channel_id=1, source_target_pairs={{0,8},{1,5},{2,10},{3,7},{4,12},{5,1},{6,14},{7,3},{8,0},{9,13},{1... | collective-permute-start | bytes 442376 | tf_op jit(solution)/shard_map/ppermute | solution.py:754
  50.7 1.6 %collective-permute-start.16 = (bf16[192,768]{1,0:T(8,128)(2,1)S(1)}, bf16[192,768]{1,0:T(8,128)(2,1)S(1)}, u32[]{:S(2)}, u32[]{:S(2)}) collective-permute-start(bf16[192,768]{1,0:T(8,128)(2,1)S(1)} %get-tuple-element.196), channel_id=1, source_target_pairs={{0,4},{1,9},{2,6},{3,11},{4,0},{5,13},{6,2},{7,15},{8,12},{9,1},{1... | collective-permute-start | bytes 884744 | tf_op jit(solution)/shard_map/ppermute | solution.py:754
  52.3 2.2 %collective-permute-done.18.refs_4_ = bf16[96,768]{1,0:T(8,128)(2,1)S(1)} collective-permute-done((bf16[96,768]{1,0:T(8,128)(2,1)S(1)}, bf16[96,768]{1,0:T(8,128)(2,1)S(1)}, u32[]{:S(2)}, u32[]{:S(2)}) %collective-permute-start.18) | collective-permute-done | bytes 147488 | tf_op jit(solution)/shard_map/ppermute | solution.py:754
  55.2 3.0 %collective-permute-start.22 = (bf16[96,768]{1,0:T(8,128)(2,1)S(1)}, bf16[96,768]{1,0:T(8,128)(2,1)S(1)}, u32[]{:S(2)}, u32[]{:S(2)}) collective-permute-start(bf16[96,768]{1,0:T(8,128)(2,1)S(1)} %get-tuple-element.207.refs_0_), channel_id=1, source_target_pairs={{0,16},{1,17},{2,18},{3,19},{4,20},{5,21},{6,22},{7,23},{8,24},{9,... | collective-permute-start | bytes 442376 | tf_op jit(solution)/shard_map/ppermute | solution.py:754
  58.2 1.4 %collective-permute-start.20 = (bf16[192,768]{1,0:T(8,128)(2,1)S(1)}, bf16[192,768]{1,0:T(8,128)(2,1)S(1)}, u32[]{:S(2)}, u32[]{:S(2)}) collective-permute-start(bf16[192,768]{1,0:T(8,128)(2,1)S(1)} %get-tuple-element.205), channel_id=1, source_target_pairs={{0,4},{1,9},{2,6},{3,11},{4,0},{5,13},{6,2},{7,15},{8,12},{9,1},{1... | collective-permute-start | bytes 884744 | tf_op jit(solution)/shard_map/ppermute | solution.py:754
  60.3 2.0 %collective-permute-start.21 = (bf16[192,768]{1,0:T(8,128)(2,1)S(1)}, bf16[192,768]{1,0:T(8,128)(2,1)S(1)}, u32[]{:S(2)}, u32[]{:S(2)}) collective-permute-start(bf16[192,768]{1,0:T(8,128)(2,1)S(1)} %get-tuple-element.206), channel_id=1, source_target_pairs={{0,8},{1,5},{2,10},{3,7},{4,12},{5,1},{6,14},{7,3},{8,0},{9,13},{1... | collective-permute-start | bytes 884744 | tf_op jit(solution)/shard_map/ppermute | solution.py:754
  62.3 1.4 %input_grads.1 = (f32[256,768]{1,0:T(8,128)S(1)}, bf16[272,768]{1,0:T(8,128)(2,1)S(1)}, f32[8,128]{1,0:T(8,128)S(1)}) custom-call(bf16[1152,256]{1,0:T(8,128)(2,1)S(1)} %get-tuple-element.176.refs_0_.refs_4_.refs_8_, bf16[1152,256]{1,0:T(8,128)(2,1)S(1)} %get-tuple-element.177.refs_1_.refs_5_.refs_9_, ...), custom_call_target="tpu_custom_call" | custom-call | bytes 100000000 | tf_op jit(solution)/shard_map/input_grads/pallas_call | solution.py:145
  63.7 1.6 %collective-permute-start.19 = (bf16[272,768]{1,0:T(8,128)(2,1)S(1)}, bf16[272,768]{1,0:T(8,128)(2,1)S(1)}, u32[]{:S(2)}, u32[]{:S(2)}) collective-permute-start(bf16[272,768]{1,0:T(8,128)(2,1)S(1)} %get-tuple-element.203.refs_0_), channel_id=1, source_target_pairs={{0,2},{1,3},{2,0},{3,1},{4,6},{5,7},{6,4},{7,5},{8,10},{9,11},{10,... | collective-permute-start | bytes 1253384 | tf_op jit(solution)/shard_map/ppermute | solution.py:746
  65.5 2.6 %collective-permute-done.20.refs_3_ = bf16[192,768]{1,0:T(8,128)(2,1)S(1)} collective-permute-done((bf16[192,768]{1,0:T(8,128)(2,1)S(1)}, bf16[192,768]{1,0:T(8,128)(2,1)S(1)}, u32[]{:S(2)}, u32[]{:S(2)}) %collective-permute-start.20) | collective-permute-done | bytes 294944 | tf_op jit(solution)/shard_map/ppermute | solution.py:754
  68.8 0.9 collective-permute-start.23
  69.7 1.4 %collective-permute-start.26 = (bf16[96,768]{1,0:T(8,128)(2,1)S(1)}, bf16[96,768]{1,0:T(8,128)(2,1)S(1)}, u32[]{:S(2)}, u32[]{:S(2)}) collective-permute-start(bf16[96,768]{1,0:T(8,128)(2,1)S(1)} %get-tuple-element.213.refs_1_), channel_id=1, source_target_pairs={{0,4},{1,9},{2,6},{3,11},{4,0},{5,13},{6,2},{7,15},{8,12},{9,1},{1... | collective-permute-start | bytes 442376 | tf_op jit(solution)/shard_map/ppermute | solution.py:754
  71.1 0.9 collective-permute-done.25.refs_2_
  72.1 2.7 %collective-permute-done.26.refs_3_ = bf16[96,768]{1,0:T(8,128)(2,1)S(1)} collective-permute-done((bf16[96,768]{1,0:T(8,128)(2,1)S(1)}, bf16[96,768]{1,0:T(8,128)(2,1)S(1)}, u32[]{:S(2)}, u32[]{:S(2)}) %collective-permute-start.26) | collective-permute-done | bytes 147488 | tf_op jit(solution)/shard_map/ppermute | solution.py:754
  74.9 2.3 %collective-permute-done.27.refs_4_ = bf16[96,768]{1,0:T(8,128)(2,1)S(1)} collective-permute-done((bf16[96,768]{1,0:T(8,128)(2,1)S(1)}, bf16[96,768]{1,0:T(8,128)(2,1)S(1)}, u32[]{:S(2)}, u32[]{:S(2)}) %collective-permute-start.27) | collective-permute-done | bytes 147488 | tf_op jit(solution)/shard_map/ppermute | solution.py:754
  77.1 1.7 %place_sums.3 = (f32[192,768]{1,0:T(8,128)}, f32[192,768]{1,0:T(8,128)}, f32[8,128]{1,0:T(8,128)S(1)}) custom-call(s32[7]{0:T(128)S(1)} %stack.31.refs_0_, bf16[96,768]{1,0:T(8,128)(2,1)S(1)} %get-tuple-element.213.refs_1_, bf16[96,768]{1,0:T(8,128)(2,1)S(1)} %collective-permute-done.25.refs_2_, bf16[96,768]{1,0:T(8,128)(2,1)S(1)} %collective-permute-done.26.refs_3_, ...), custom_call_target="tpu_custom_call" | custom-call | bytes 100000000 | tf_op jit(solution)/shard_map/place_sums/pallas_call | solution.py:145
  78.9 1.4 %collective-permute-start.28 = (bf16[16,768]{1,0:T(8,128)(2,1)S(1)}, bf16[16,768]{1,0:T(8,128)(2,1)S(1)}, u32[]{:S(2)}, u32[]{:S(2)}) collective-permute-start(bf16[16,768]{1,0:T(8,128)(2,1)S(1)} %get-tuple-element.216.refs_2_), channel_id=1, source_target_pairs={{0,16},{1,17},{2,18},{3,19},{4,20},{5,21},{6,22},{7,23},{8,24},{9,... | collective-permute-start | bytes 73736 | tf_op jit(solution)/shard_map/ppermute | solution.py:754
  80.4 3.4 %collective-permute-done.28.refs_3_ = bf16[16,768]{1,0:T(8,128)(2,1)S(1)} collective-permute-done((bf16[16,768]{1,0:T(8,128)(2,1)S(1)}, bf16[16,768]{1,0:T(8,128)(2,1)S(1)}, u32[]{:S(2)}, u32[]{:S(2)}) %collective-permute-start.28) | collective-permute-done | bytes 24608 | tf_op jit(solution)/shard_map/ppermute | solution.py:754
  83.8 0.9 collective-permute-start.29
  84.7 1.3 %input_norm.1 = (bf16[256,768]{1,0:T(8,128)(2,1)}, f32[8,128]{1,0:T(8,128)S(1)}) custom-call(bf16[256,768]{1,0:T(8,128)(2,1)S(1)} %get-tuple-element.126.refs_3_.refs_0_, f32[768]{0:T(1024)S(1)} %get-tuple-element.127.refs_4_.refs_1_, f32[256,768]{1,0:T(8,128)S(1)} %get-tuple-element.202.refs_2_, ...), custom_call_target="tpu_custom_call" | custom-call | bytes 100000000 | tf_op jit(solution)/shard_map/input_norm/pallas_call | solution.py:145
  86.0 1.2 %feed_result.1 = (bf16[256,768]{1,0:T(8,128)(2,1)}, f32[8,128]{1,0:T(8,128)S(1)}) custom-call(bf16[256,768]{1,0:T(8,128)(2,1)S(1)} %get-tuple-element.168.refs_0_, bf16[768,768]{1,0:T(8,128)(2,1)S(1)} %get-tuple-element.147.refs_7_.refs_1_, f32[256,768]{1,0:T(8,128)S(1)} %get-tuple-element.169.refs_2_, f32[8,128]{1,0:T(8,128)S(1)} %get-tuple-element.219.refs_3_), custom_call_target="tpu_custom_call" | custom-call | bytes 100000000 | tf_op jit(solution)/shard_map/feed_result/pallas_call | solution.py:145
  87.3 1.4 %collective-permute-start.30 = (bf16[208,768]{1,0:T(8,128)(2,1)S(1)}, bf16[208,768]{1,0:T(8,128)(2,1)S(1)}, u32[]{:S(2)}, u32[]{:S(2)}) collective-permute-start(bf16[208,768]{1,0:T(8,128)(2,1)S(1)} %get-tuple-element.224.refs_1_), channel_id=1, source_target_pairs={{0,4},{1,9},{2,6},{3,11},{4,0},{5,13},{6,2},{7,15},{8,12},{9,1},{1... | collective-permute-start | bytes 958472 | tf_op jit(solution)/shard_map/ppermute | solution.py:754
  88.7 2.2 %collective-permute-done.29.refs_2_ = bf16[208,768]{1,0:T(8,128)(2,1)S(1)} collective-permute-done((bf16[208,768]{1,0:T(8,128)(2,1)S(1)}, bf16[208,768]{1,0:T(8,128)(2,1)S(1)}, u32[]{:S(2)}, u32[]{:S(2)}) %collective-permute-start.29) | collective-permute-done | bytes 319520 | tf_op jit(solution)/shard_map/ppermute | solution.py:754
  91.6 2.7 %collective-permute-done.30.refs_3_ = bf16[208,768]{1,0:T(8,128)(2,1)S(1)} collective-permute-done((bf16[208,768]{1,0:T(8,128)(2,1)S(1)}, bf16[208,768]{1,0:T(8,128)(2,1)S(1)}, u32[]{:S(2)}, u32[]{:S(2)}) %collective-permute-start.30) | collective-permute-done | bytes 319520 | tf_op jit(solution)/shard_map/ppermute | solution.py:754
  94.3 1.9 %place_sums.4 = (f32[3,192,768]{2,1,0:T(8,128)}, f32[192,768]{1,0:T(8,128)}, f32[8,128]{1,0:T(8,128)S(1)}) custom-call(s32[7]{0:T(128)S(1)} %stack.31.refs_0_, bf16[208,768]{1,0:T(8,128)(2,1)S(1)} %get-tuple-element.224.refs_1_, bf16[208,768]{1,0:T(8,128)(2,1)S(1)} %collective-permute-done.29.refs_2_, bf16[208,768]{1,0:T(8,128)(2,1)S(1)} %collective-permute-done.30.refs_3_, ...), custom_call_target="tpu_custom_call" | custom-call | bytes 100000000 | tf_op jit(solution)/shard_map/place_sums/pallas_call | solution.py:145
  96.2 1.6 %collective-permute-done.31.refs_4_ = bf16[208,768]{1,0:T(8,128)(2,1)S(1)} collective-permute-done((bf16[208,768]{1,0:T(8,128)(2,1)S(1)}, bf16[208,768]{1,0:T(8,128)(2,1)S(1)}, u32[]{:S(2)}, u32[]{:S(2)}) %collective-permute-start.31) | collective-permute-done | bytes 319520 | tf_op jit(solution)/shard_map/ppermute | solution.py:754
  97.8 1.5 %place_sums.5 = (f32[3,192,768]{2,1,0:T(8,128)}, f32[192,768]{1,0:T(8,128)}, f32[768]{0:T(1024)}, f32[768]{0:T(1024)}, f32[768]{0:T(1024)}, /*index=5*/f32[768]{0:T(1024)}, f32[192]{0:T(256)}) custom-call(s32[7]{0:T(128)S(1)} %stack.31.refs_0_, bf16[208,768]{1,0:T(8,128)(2,1)S(1)} %get-tuple-element.224.refs_1_, ...), custom_call_target="tpu_custom_call", output_to_operand_aliasing={{0}: (5, {}), {1}: (6, {})} | custom-call | bytes 100000000 | tf_op jit(solution)/shard_map/place_sums/pallas_call | solution.py:145
  (50 shorter events, 10.1 us)
Async XLA Ops:
  0.6 6.6 %collective-permute-start.1 = (bf16[3,192,768]{2,1,0:T(8,128)(2,1)}, bf16[3,192,768]{2,1,0:T(8,128)(2,1)S(1)}, u32[]{:S(2)}, u32[]{:S(2)}) collective-permute-start(bf16[3,192,768]{2,1,0:T(8,128)(2,1)} %refs_6_.3), channel_id=1, source_target_pairs={{0,1},{1,0},{2,3},{3,2},{4,5},{5,4},{6,7},{7,6},{8,9},{9,8},{10,11... | collective-permute-start | bytes 2654216 | tf_op jit(solution)/shard_map/ppermute | solution.py:743
  2.8 9.1 %collective-permute-start.3 = (bf16[448,256]{1,0:T(8,128)(2,1)S(1)}, bf16[448,256]{1,0:T(8,128)(2,1)S(1)}, u32[]{:S(2)}, u32[]{:S(2)}) collective-permute-start(bf16[448,256]{1,0:T(8,128)(2,1)S(1)} %get-tuple-element.124.refs_3_), channel_id=1, source_target_pairs={{0,2},{1,3},{2,0},{3,1},{4,6},{5,7},{6,4},{7,5},{8,10},{9,11},{10,... | collective-permute-start | bytes 688136 | tf_op jit(solution)/shard_map/ppermute | solution.py:746
  5.5 16.7 %collective-permute-start = (bf16[256,768]{1,0:T(8,128)(2,1)}, bf16[256,768]{1,0:T(8,128)(2,1)S(1)}, u32[]{:S(2)}, u32[]{:S(2)}) collective-permute-start(bf16[256,768]{1,0:T(8,128)(2,1)} %refs_4_.3), channel_id=1, source_target_pairs={{0,2},{1,3},{2,0},{3,1},{4,6},{5,7},{6,4},{7,5},{8,10},{9,11},{10,... | collective-permute-start | bytes 1179656 | tf_op jit(solution)/shard_map/ppermute | solution.py:746
  7.1 15.9 %collective-permute-start.2 = (bf16[592,768]{1,0:T(8,128)(2,1)S(1)}, bf16[592,768]{1,0:T(8,128)(2,1)S(1)}, u32[]{:S(2)}, u32[]{:S(2)}) collective-permute-start(bf16[592,768]{1,0:T(8,128)(2,1)S(1)} %get-tuple-element.132.refs_7_.refs_8_), channel_id=1, source_target_pairs={{0,1},{1,0},{2,3},{3,2},{4,5},{5,4},{6,7},{7,6},{8,9},{9,8},{10,11... | collective-permute-start | bytes 2727944 | tf_op jit(solution)/shard_map/ppermute | solution.py:743
  7.3 8.3 %copy-start = (bf16[256,768]{1,0:T(8,128)(2,1)S(1)}, bf16[256,768]{1,0:T(8,128)(2,1)}, u32[]{:S(2)}) copy-start(bf16[256,768]{1,0:T(8,128)(2,1)} %refs_5_.1) | copy-start | bytes 1179652
  12.0 7.2 %collective-permute-start.4 = (bf16[144,768]{1,0:T(8,128)(2,1)S(1)}, bf16[144,768]{1,0:T(8,128)(2,1)S(1)}, u32[]{:S(2)}, u32[]{:S(2)}) collective-permute-start(bf16[144,768]{1,0:T(8,128)(2,1)S(1)} %get-tuple-element.134), channel_id=1, source_target_pairs={{0,4},{1,5},{2,6},{3,7},{4,0},{5,1},{6,2},{7,3},{8,12},{9,13},{10,... | collective-permute-start | bytes 663560 | tf_op jit(solution)/shard_map/ppermute | solution.py:754
  13.9 6.8 %collective-permute-start.5 = (bf16[144,768]{1,0:T(8,128)(2,1)S(1)}, bf16[144,768]{1,0:T(8,128)(2,1)S(1)}, u32[]{:S(2)}, u32[]{:S(2)}) collective-permute-start(bf16[144,768]{1,0:T(8,128)(2,1)S(1)} %get-tuple-element.134), channel_id=1, source_target_pairs={{0,8},{1,9},{2,10},{3,11},{4,12},{5,13},{6,14},{7,15},{8,0},{9,1},... | collective-permute-start | bytes 663560 | tf_op jit(solution)/shard_map/ppermute | solution.py:754
  15.5 15.6 %collective-permute-start.6 = (bf16[256,768]{1,0:T(8,128)(2,1)S(1)}, bf16[256,768]{1,0:T(8,128)(2,1)S(1)}, u32[]{:S(2)}, u32[]{:S(2)}) collective-permute-start(bf16[256,768]{1,0:T(8,128)(2,1)S(1)} %copy-done), channel_id=1, source_target_pairs={{0,2},{1,3},{2,0},{3,1},{4,6},{5,7},{6,4},{7,5},{8,10},{9,11},{10,... | collective-permute-start | bytes 1179656 | tf_op jit(solution)/shard_map/ppermute | solution.py:746
  19.2 7.3 %collective-permute-start.8 = (bf16[160,768]{1,0:T(8,128)(2,1)S(1)}, bf16[160,768]{1,0:T(8,128)(2,1)S(1)}, u32[]{:S(2)}, u32[]{:S(2)}) collective-permute-start(bf16[160,768]{1,0:T(8,128)(2,1)S(1)} %get-tuple-element.142.refs_4_.refs_10_), channel_id=1, source_target_pairs={{0,1},{1,0},{2,3},{3,2},{4,5},{5,4},{6,7},{7,6},{8,9},{9,8},{10,11... | collective-permute-start | bytes 737288 | tf_op jit(solution)/shard_map/ppermute | solution.py:743
  20.6 12.4 %collective-permute-start.12 = (bf16[256,384]{1,0:T(8,128)(2,1)S(1)}, bf16[256,384]{1,0:T(8,128)(2,1)S(1)}, u32[]{:S(2)}, u32[]{:S(2)}) collective-permute-start(bf16[256,384]{1,0:T(8,128)(2,1)S(1)} %get-tuple-element.130.refs_2_), channel_id=1, source_target_pairs={{0,2},{1,3},{2,0},{3,1},{4,6},{5,7},{6,4},{7,5},{8,10},{9,11},{10,... | collective-permute-start | bytes 589832 | tf_op jit(solution)/shard_map/ppermute | solution.py:746
  22.2 6.5 %collective-permute-start.7 = (bf16[144,768]{1,0:T(8,128)(2,1)S(1)}, bf16[144,768]{1,0:T(8,128)(2,1)S(1)}, u32[]{:S(2)}, u32[]{:S(2)}) collective-permute-start(bf16[144,768]{1,0:T(8,128)(2,1)S(1)} %get-tuple-element.144), channel_id=1, source_target_pairs={{0,4},{1,5},{2,6},{3,7},{4,0},{5,1},{6,2},{7,3},{8,12},{9,13},{10,... | collective-permute-start | bytes 663560 | tf_op jit(solution)/shard_map/ppermute | solution.py:754
  22.9 7.3 %collective-permute-start.9 = (bf16[2,144,768]{2,1,0:T(8,128)(2,1)S(1)}, bf16[2,144,768]{2,1,0:T(8,128)(2,1)S(1)}, u32[]{:S(2)}, u32[]{:S(2)}) collective-permute-start(bf16[2,144,768]{2,1,0:T(8,128)(2,1)S(1)} %get-tuple-element.143.refs_5_), channel_id=1, source_target_pairs={{0,1},{1,0},{2,3},{3,2},{4,5},{5,4},{6,7},{7,6},{8,9},{9,8},{10,11... | collective-permute-start | bytes 1327112 | tf_op jit(solution)/shard_map/ppermute | solution.py:743
  26.5 10.8 %collective-permute-start.11 = (bf16[256,384]{1,0:T(8,128)(2,1)S(1)}, bf16[256,384]{1,0:T(8,128)(2,1)S(1)}, u32[]{:S(2)}, u32[]{:S(2)}) collective-permute-start(bf16[256,384]{1,0:T(8,128)(2,1)S(1)} %get-tuple-element.137.refs_3_), channel_id=1, source_target_pairs={{0,2},{1,3},{2,0},{3,1},{4,6},{5,7},{6,4},{7,5},{8,10},{9,11},{10,... | collective-permute-start | bytes 589832 | tf_op jit(solution)/shard_map/ppermute | solution.py:746
  28.8 1.5 %collective-permute-start.10 = (bf16[144,768]{1,0:T(8,128)(2,1)S(1)}, bf16[144,768]{1,0:T(8,128)(2,1)S(1)}, u32[]{:S(2)}, u32[]{:S(2)}) collective-permute-start(bf16[144,768]{1,0:T(8,128)(2,1)S(1)} %collective-permute-done.7.refs_6_), channel_id=1, source_target_pairs={{0,1},{1,0},{2,3},{3,2},{4,5},{5,4},{6,7},{7,6},{8,9},{9,8},{10,11... | collective-permute-start | bytes 663560 | tf_op jit(solution)/shard_map/ppermute | solution.py:743
  39.1 2.6 %collective-permute-start.13 = (bf16[2,192,768]{2,1,0:T(8,128)(2,1)S(1)}, bf16[2,192,768]{2,1,0:T(8,128)(2,1)S(1)}, u32[]{:S(2)}, u32[]{:S(2)}) collective-permute-start(bf16[2,192,768]{2,1,0:T(8,128)(2,1)S(1)} %get-tuple-element.187), channel_id=1, source_target_pairs={{0,1},{1,0},{2,3},{3,2},{4,5},{5,4},{6,7},{7,6},{8,9},{9,8},{10,11... | collective-permute-start | bytes 1769480 | tf_op jit(solution)/shard_map/ppermute | solution.py:743
  42.2 5.5 %collective-permute-start.15 = (bf16[96,768]{1,0:T(8,128)(2,1)S(1)}, bf16[96,768]{1,0:T(8,128)(2,1)S(1)}, u32[]{:S(2)}, u32[]{:S(2)}) collective-permute-start(bf16[96,768]{1,0:T(8,128)(2,1)S(1)} %get-tuple-element.193), channel_id=1, source_target_pairs={{0,4},{1,9},{2,6},{3,11},{4,0},{5,13},{6,2},{7,15},{8,12},{9,1},{1... | collective-permute-start | bytes 442376 | tf_op jit(solution)/shard_map/ppermute | solution.py:754
  45.8 4.3 %collective-permute-start.14 = (bf16[4,192,768]{2,1,0:T(8,128)(2,1)S(1)}, bf16[4,192,768]{2,1,0:T(8,128)(2,1)S(1)}, u32[]{:S(2)}, u32[]{:S(2)}) collective-permute-start(bf16[4,192,768]{2,1,0:T(8,128)(2,1)S(1)} %get-tuple-element.192), channel_id=1, source_target_pairs={{0,1},{1,0},{2,3},{3,2},{4,5},{5,4},{6,7},{7,6},{8,9},{9,8},{10,11... | collective-permute-start | bytes 3538952 | tf_op jit(solution)/shard_map/ppermute | solution.py:743
  46.2 6.2 %collective-permute-start.17 = (bf16[96,768]{1,0:T(8,128)(2,1)S(1)}, bf16[96,768]{1,0:T(8,128)(2,1)S(1)}, u32[]{:S(2)}, u32[]{:S(2)}) collective-permute-start(bf16[96,768]{1,0:T(8,128)(2,1)S(1)} %get-tuple-element.197), channel_id=1, source_target_pairs={{0,4},{1,9},{2,6},{3,11},{4,0},{5,13},{6,2},{7,15},{8,12},{9,1},{1... | collective-permute-start | bytes 442376 | tf_op jit(solution)/shard_map/ppermute | solution.py:754
  48.3 6.2 %collective-permute-start.18 = (bf16[96,768]{1,0:T(8,128)(2,1)S(1)}, bf16[96,768]{1,0:T(8,128)(2,1)S(1)}, u32[]{:S(2)}, u32[]{:S(2)}) collective-permute-start(bf16[96,768]{1,0:T(8,128)(2,1)S(1)} %get-tuple-element.198), channel_id=1, source_target_pairs={{0,8},{1,5},{2,10},{3,7},{4,12},{5,1},{6,14},{7,3},{8,0},{9,13},{1... | collective-permute-start | bytes 442376 | tf_op jit(solution)/shard_map/ppermute | solution.py:754
  50.7 8.9 %collective-permute-start.16 = (bf16[192,768]{1,0:T(8,128)(2,1)S(1)}, bf16[192,768]{1,0:T(8,128)(2,1)S(1)}, u32[]{:S(2)}, u32[]{:S(2)}) collective-permute-start(bf16[192,768]{1,0:T(8,128)(2,1)S(1)} %get-tuple-element.196), channel_id=1, source_target_pairs={{0,4},{1,9},{2,6},{3,11},{4,0},{5,13},{6,2},{7,15},{8,12},{9,1},{1... | collective-permute-start | bytes 884744 | tf_op jit(solution)/shard_map/ppermute | solution.py:754
  55.2 10.1 %collective-permute-start.22 = (bf16[96,768]{1,0:T(8,128)(2,1)S(1)}, bf16[96,768]{1,0:T(8,128)(2,1)S(1)}, u32[]{:S(2)}, u32[]{:S(2)}) collective-permute-start(bf16[96,768]{1,0:T(8,128)(2,1)S(1)} %get-tuple-element.207.refs_0_), channel_id=1, source_target_pairs={{0,16},{1,17},{2,18},{3,19},{4,20},{5,21},{6,22},{7,23},{8,24},{9,... | collective-permute-start | bytes 442376 | tf_op jit(solution)/shard_map/ppermute | solution.py:754
  58.2 9.9 %collective-permute-start.20 = (bf16[192,768]{1,0:T(8,128)(2,1)S(1)}, bf16[192,768]{1,0:T(8,128)(2,1)S(1)}, u32[]{:S(2)}, u32[]{:S(2)}) collective-permute-start(bf16[192,768]{1,0:T(8,128)(2,1)S(1)} %get-tuple-element.205), channel_id=1, source_target_pairs={{0,4},{1,9},{2,6},{3,11},{4,0},{5,13},{6,2},{7,15},{8,12},{9,1},{1... | collective-permute-start | bytes 884744 | tf_op jit(solution)/shard_map/ppermute | solution.py:754
  60.3 7.8 %collective-permute-start.21 = (bf16[192,768]{1,0:T(8,128)(2,1)S(1)}, bf16[192,768]{1,0:T(8,128)(2,1)S(1)}, u32[]{:S(2)}, u32[]{:S(2)}) collective-permute-start(bf16[192,768]{1,0:T(8,128)(2,1)S(1)} %get-tuple-element.206), channel_id=1, source_target_pairs={{0,8},{1,5},{2,10},{3,7},{4,12},{5,1},{6,14},{7,3},{8,0},{9,13},{1... | collective-permute-start | bytes 884744 | tf_op jit(solution)/shard_map/ppermute | solution.py:754
  63.7 8.3 %collective-permute-start.19 = (bf16[272,768]{1,0:T(8,128)(2,1)S(1)}, bf16[272,768]{1,0:T(8,128)(2,1)S(1)}, u32[]{:S(2)}, u32[]{:S(2)}) collective-permute-start(bf16[272,768]{1,0:T(8,128)(2,1)S(1)} %get-tuple-element.203.refs_0_), channel_id=1, source_target_pairs={{0,2},{1,3},{2,0},{3,1},{4,6},{5,7},{6,4},{7,5},{8,10},{9,11},{10,... | collective-permute-start | bytes 1253384 | tf_op jit(solution)/shard_map/ppermute | solution.py:746
  65.4 6.6 %collective-permute-start.25 = (bf16[96,768]{1,0:T(8,128)(2,1)S(1)}, bf16[96,768]{1,0:T(8,128)(2,1)S(1)}, u32[]{:S(2)}, u32[]{:S(2)}) collective-permute-start(bf16[96,768]{1,0:T(8,128)(2,1)S(1)} %get-tuple-element.213.refs_1_), channel_id=1, source_target_pairs={{0,8},{1,5},{2,10},{3,7},{4,12},{5,1},{6,14},{7,3},{8,0},{9,13},{1... | collective-permute-start | bytes 442376 | tf_op jit(solution)/shard_map/ppermute | solution.py:754
  68.8 14.9 %collective-permute-start.23 = (bf16[192,768]{1,0:T(8,128)(2,1)S(1)}, bf16[192,768]{1,0:T(8,128)(2,1)S(1)}, u32[]{:S(2)}, u32[]{:S(2)}) collective-permute-start(bf16[192,768]{1,0:T(8,128)(2,1)S(1)} %get-tuple-element.210.refs_0_), channel_id=1, source_target_pairs={{0,16},{1,17},{2,18},{3,19},{4,20},{5,21},{6,22},{7,23},{8,24},{9,... | collective-permute-start | bytes 884744 | tf_op jit(solution)/shard_map/ppermute | solution.py:754
  69.7 5.1 %collective-permute-start.26 = (bf16[96,768]{1,0:T(8,128)(2,1)S(1)}, bf16[96,768]{1,0:T(8,128)(2,1)S(1)}, u32[]{:S(2)}, u32[]{:S(2)}) collective-permute-start(bf16[96,768]{1,0:T(8,128)(2,1)S(1)} %get-tuple-element.213.refs_1_), channel_id=1, source_target_pairs={{0,4},{1,9},{2,6},{3,11},{4,0},{5,13},{6,2},{7,15},{8,12},{9,1},{1... | collective-permute-start | bytes 442376 | tf_op jit(solution)/shard_map/ppermute | solution.py:754
  72.0 5.1 %collective-permute-start.27 = (bf16[96,768]{1,0:T(8,128)(2,1)S(1)}, bf16[96,768]{1,0:T(8,128)(2,1)S(1)}, u32[]{:S(2)}, u32[]{:S(2)}) collective-permute-start(bf16[96,768]{1,0:T(8,128)(2,1)S(1)} %collective-permute-done.25.refs_2_), channel_id=1, source_target_pairs={{0,4},{1,9},{2,6},{3,11},{4,0},{5,13},{6,2},{7,15},{8,12},{9,1},{1... | collective-permute-start | bytes 442376 | tf_op jit(solution)/shard_map/ppermute | solution.py:754
  72.0 6.8 %collective-permute-start.24 = (bf16[16,768]{1,0:T(8,128)(2,1)S(1)}, bf16[16,768]{1,0:T(8,128)(2,1)S(1)}, u32[]{:S(2)}, u32[]{:S(2)}) collective-permute-start(bf16[16,768]{1,0:T(8,128)(2,1)S(1)} %get-tuple-element.212.refs_0_), channel_id=1, source_target_pairs={{0,1},{1,0},{2,3},{3,2},{4,5},{5,4},{6,7},{7,6},{8,9},{9,8},{10,11... | collective-permute-start | bytes 73736 | tf_op jit(solution)/shard_map/ppermute | solution.py:743
  78.9 4.8 %collective-permute-start.28 = (bf16[16,768]{1,0:T(8,128)(2,1)S(1)}, bf16[16,768]{1,0:T(8,128)(2,1)S(1)}, u32[]{:S(2)}, u32[]{:S(2)}) collective-permute-start(bf16[16,768]{1,0:T(8,128)(2,1)S(1)} %get-tuple-element.216.refs_2_), channel_id=1, source_target_pairs={{0,16},{1,17},{2,18},{3,19},{4,20},{5,21},{6,22},{7,23},{8,24},{9,... | collective-permute-start | bytes 73736 | tf_op jit(solution)/shard_map/ppermute | solution.py:754
  83.8 7.1 %collective-permute-start.29 = (bf16[208,768]{1,0:T(8,128)(2,1)S(1)}, bf16[208,768]{1,0:T(8,128)(2,1)S(1)}, u32[]{:S(2)}, u32[]{:S(2)}) collective-permute-start(bf16[208,768]{1,0:T(8,128)(2,1)S(1)} %get-tuple-element.224.refs_1_), channel_id=1, source_target_pairs={{0,8},{1,5},{2,10},{3,7},{4,12},{5,1},{6,14},{7,3},{8,0},{9,13},{1... | collective-permute-start | bytes 958472 | tf_op jit(solution)/shard_map/ppermute | solution.py:754
  87.3 7.1 %collective-permute-start.30 = (bf16[208,768]{1,0:T(8,128)(2,1)S(1)}, bf16[208,768]{1,0:T(8,128)(2,1)S(1)}, u32[]{:S(2)}, u32[]{:S(2)}) collective-permute-start(bf16[208,768]{1,0:T(8,128)(2,1)S(1)} %get-tuple-element.224.refs_1_), channel_id=1, source_target_pairs={{0,4},{1,9},{2,6},{3,11},{4,0},{5,13},{6,2},{7,15},{8,12},{9,1},{1... | collective-permute-start | bytes 958472 | tf_op jit(solution)/shard_map/ppermute | solution.py:754
  90.8 7.0 %collective-permute-start.31 = (bf16[208,768]{1,0:T(8,128)(2,1)S(1)}, bf16[208,768]{1,0:T(8,128)(2,1)S(1)}, u32[]{:S(2)}, u32[]{:S(2)}) collective-permute-start(bf16[208,768]{1,0:T(8,128)(2,1)S(1)} %collective-permute-done.29.refs_2_), channel_id=1, source_target_pairs={{0,4},{1,9},{2,6},{3,11},{4,0},{5,13},{6,2},{7,15},{8,12},{9,1},{1... | collective-permute-start | bytes 958472 | tf_op jit(solution)/shard_map/ppermute | solution.py:754

commit v13 on v12

--- a/solution.py
+++ b/solution.py
@@ -72,7 +72,7 @@
 
 
 STRIP = 256
-COSTS = (0, 0, 100, 0, 0, 30, 30, 0, 0, 0, 0, 0, 100, 0, 0, 0, 200, 0, 30, 0, 0, 30, 0, 0, 0, 0, 0, 0, 0, 0, 0, 0)
+COSTS = (0, 0, 100, 0, 0, 30, 30, 0, 0, 0, 0, 0, 100, 0, 0, 0, 200, 0, 30, 0, 0, 30, 0, 0, 0, 0, 0, 0, 0, 0, 60, 0)
 
 
 class IO:

time: 99.7 us -> 99.7 us (level)
  no operation moved by 1% of the time
where the time goes in v13:
time: 99.7 us; the launch traced here: 99.5 us
  Pallas kernels  36 us (36%)
  starting transfers between devices  33.9 us (34%)
  waiting for transfers between devices  28.4 us (28%)
  between operations  1.13 us (1%)
    pallas_call x31, Pallas kernels, call(): pl.pallas_call(body, in_specs=[spec(kind) for kind in ins] + [vmem] * len...  36 us
    ppermute x18, waiting for transfers between devices, swap_dp(): return lax.ppermute(a, ('dp', 'tensor'), pairs)  25.6 us
    ppermute x18, starting transfers between devices, swap_dp(): return lax.ppermute(a, ('dp', 'tensor'), pairs)  24.4 us
    ppermute x6, starting transfers between devices, swap_y(): return lax.ppermute(a, 'tensor', [(t, t ^ 2) for t in range(n_tensor)])  8.19 us
  transfers between devices with their start and end apart: 32, of which 15 were waited for; matrix products, arithmetic and copies ran while one was open for 0% of the time, Pallas kernels for 32%

profile of v13, /device:TPU:0, one launch (start us, length us, event | category | flops | bytes accessed | tf_op | source)
XLA Modules:
  0.0 99.5 jit_solution(7437993757908750124)
XLA Ops:
  1.2 1.6 %pick.1 = (bf16[448,256]{1,0:T(8,128)(2,1)S(1)}, f32[8,128]{1,0:T(8,128)S(1)}) custom-call(s32[7]{0:T(128)S(1)} %stack.31.refs_0_, bf16[192,768]{1,0:T(8,128)(2,1)} %refs_0_.1, bf16[192,768]{1,0:T(8,128)(2,1)} %refs_1_.5, bf16[192,768]{1,0:T(8,128)(2,1)} %refs_2_.5, bf16[192]{0:T(256)(128)(2,1)} %refs_4_.2), custom_call_target="tpu_custom_call" | custom-call | bytes 100000000 | tf_op jit(solution)/shard_map/pick/pallas_call | solution.py:145
  2.8 2.6 %collective-permute-start.3 = (bf16[448,256]{1,0:T(8,128)(2,1)S(1)}, bf16[448,256]{1,0:T(8,128)(2,1)S(1)}, u32[]{:S(2)}, u32[]{:S(2)}) collective-permute-start(bf16[448,256]{1,0:T(8,128)(2,1)S(1)} %get-tuple-element.124.refs_3_), channel_id=1, source_target_pairs={{0,2},{1,3},{2,0},{3,1},{4,6},{5,7},{6,4},{7,5},{8,10},{9,11},{10,... | collective-permute-start | bytes 688136 | tf_op jit(solution)/shard_map/ppermute | solution.py:746
  5.6 1.5 %load.1 = (bf16[592,768]{1,0:T(8,128)(2,1)S(1)}, bf16[256,768]{1,0:T(8,128)(2,1)S(1)}, bf16[256,768]{1,0:T(8,128)(2,1)S(1)}, f32[768]{0:T(1024)S(1)}, f32[768]{0...) custom-call(bf16[192,768]{1,0:T(8,128)(2,1)} %refs_0_.1, bf16[192,768]{1,0:T(8,128)(2,1)} %refs_1_.5, ...), custom_call_target="tpu_custom_call" | custom-call | bytes 100000000 | tf_op jit(solution)/shard_map/load/pallas_call | solution.py:145
  7.3 4.0 %attention_forward.2 = (bf16[256,768]{1,0:T(8,128)(2,1)S(1)}, bf16[384,256]{1,0:T(8,128)(2,1)S(1)}, bf16[384,256]{1,0:T(8,128)(2,1)S(1)}, bf16[256,384]{1,0:T(8,...) custom-call(s32[7]{0:T(128)S(1)} %stack.31.refs_0_, ...), custom_call_target="tpu_custom_call" | custom-call | flops 10000000000 | bytes 100000000 | tf_op jit(solution)/shard_map/attention_forward/pallas_call | solution.py:145
  12.0 1.9 %collective-permute-start.4 = (bf16[144,768]{1,0:T(8,128)(2,1)S(1)}, bf16[144,768]{1,0:T(8,128)(2,1)S(1)}, u32[]{:S(2)}, u32[]{:S(2)}) collective-permute-start(bf16[144,768]{1,0:T(8,128)(2,1)S(1)} %get-tuple-element.134), channel_id=1, source_target_pairs={{0,4},{1,5},{2,6},{3,7},{4,0},{5,1},{6,2},{7,3},{8,12},{9,13},{10,... | collective-permute-start | bytes 663560 | tf_op jit(solution)/shard_map/ppermute | solution.py:754
  13.9 1.7 %collective-permute-start.5 = (bf16[144,768]{1,0:T(8,128)(2,1)S(1)}, bf16[144,768]{1,0:T(8,128)(2,1)S(1)}, u32[]{:S(2)}, u32[]{:S(2)}) collective-permute-start(bf16[144,768]{1,0:T(8,128)(2,1)S(1)} %get-tuple-element.134), channel_id=1, source_target_pairs={{0,8},{1,9},{2,10},{3,11},{4,12},{5,13},{6,14},{7,15},{8,0},{9,1},... | collective-permute-start | bytes 663560 | tf_op jit(solution)/shard_map/ppermute | solution.py:754
  15.5 1.5 %collective-permute-start.6 = (bf16[256,768]{1,0:T(8,128)(2,1)S(1)}, bf16[256,768]{1,0:T(8,128)(2,1)S(1)}, u32[]{:S(2)}, u32[]{:S(2)}) collective-permute-start(bf16[256,768]{1,0:T(8,128)(2,1)S(1)} %copy-done), channel_id=1, source_target_pairs={{0,2},{1,3},{2,0},{3,1},{4,6},{5,7},{6,4},{7,5},{8,10},{9,11},{10,... | collective-permute-start | bytes 1179656 | tf_op jit(solution)/shard_map/ppermute | solution.py:746
  17.1 2.1 %collective-permute-done.4.refs_0_ = bf16[144,768]{1,0:T(8,128)(2,1)S(1)} collective-permute-done((bf16[144,768]{1,0:T(8,128)(2,1)S(1)}, bf16[144,768]{1,0:T(8,128)(2,1)S(1)}, u32[]{:S(2)}, u32[]{:S(2)}) %collective-permute-start.4) | collective-permute-done | bytes 221216 | tf_op jit(solution)/shard_map/ppermute | solution.py:754
  19.2 1.5 %collective-permute-done.5.refs_1_ = bf16[144,768]{1,0:T(8,128)(2,1)S(1)} collective-permute-done((bf16[144,768]{1,0:T(8,128)(2,1)S(1)}, bf16[144,768]{1,0:T(8,128)(2,1)S(1)}, u32[]{:S(2)}, u32[]{:S(2)}) %collective-permute-start.5) | collective-permute-done | bytes 221216 | tf_op jit(solution)/shard_map/ppermute | solution.py:754
  20.6 1.5 %collective-permute-start.12 = (bf16[256,384]{1,0:T(8,128)(2,1)S(1)}, bf16[256,384]{1,0:T(8,128)(2,1)S(1)}, u32[]{:S(2)}, u32[]{:S(2)}) collective-permute-start(bf16[256,384]{1,0:T(8,128)(2,1)S(1)} %get-tuple-element.130.refs_2_), channel_id=1, source_target_pairs={{0,2},{1,3},{2,0},{3,1},{4,6},{5,7},{6,4},{7,5},{8,10},{9,11},{10,... | collective-permute-start | bytes 589832 | tf_op jit(solution)/shard_map/ppermute | solution.py:746
  22.9 3.5 %attention_forward.3 = (bf16[256,768]{1,0:T(8,128)(2,1)S(1)}, bf16[384,256]{1,0:T(8,128)(2,1)S(1)}, bf16[384,256]{1,0:T(8,128)(2,1)S(1)}, bf16[256,384]{1,0:T(8,...) custom-call(s32[7]{0:T(128)S(1)} %stack.31.refs_0_, ...), custom_call_target="tpu_custom_call" | custom-call | flops 3000000000 | bytes 100000000 | tf_op jit(solution)/shard_map/attention_forward/pallas_call | solution.py:145
  26.5 0.8 collective-permute-start.11
  27.3 1.5 %collective-permute-done.7.refs_6_ = bf16[144,768]{1,0:T(8,128)(2,1)S(1)} collective-permute-done((bf16[144,768]{1,0:T(8,128)(2,1)S(1)}, bf16[144,768]{1,0:T(8,128)(2,1)S(1)}, u32[]{:S(2)}, u32[]{:S(2)}) %collective-permute-start.7) | collective-permute-done | bytes 221216 | tf_op jit(solution)/shard_map/ppermute | solution.py:754
  28.8 1.5 %collective-permute-done.10.refs_9_ = bf16[144,768]{1,0:T(8,128)(2,1)S(1)} collective-permute-done((bf16[144,768]{1,0:T(8,128)(2,1)S(1)}, bf16[144,768]{1,0:T(8,128)(2,1)S(1)}, u32[]{:S(2)}, u32[]{:S(2)}) %collective-permute-start.10) | collective-permute-done | bytes 221216 | tf_op jit(solution)/shard_map/ppermute | solution.py:743
  30.2 0.9 pack_far.1
  31.1 1.2 %feed_in.1 = (f32[256,768]{1,0:T(8,128)S(1)}, f32[256,768]{1,0:T(8,128)S(1)}, f32[256,768]{1,0:T(8,128)S(1)}, f32[256,768]{1,0:T(8,128)S(1)}, f32[1,768]{1,0:T(1,128)S(1)}, /*index=5*/f32[8,128]{1,0:T(8,128)S(1)}) custom-call(bf16[256,768]{1,0:T(8,128)(2,1)S(1)} %get-tuple-element.126.refs_3_.refs_0_, ...), custom_call_target="tpu_custom_call" | custom-call | bytes 100000000 | tf_op jit(solution)/shard_map/feed_in/pallas_call | solution.py:145
  33.0 1.7 %feed_far.1 = (f32[256,768]{1,0:T(8,128)S(1)}, bf16[256,768]{1,0:T(8,128)(2,1)S(1)}, f32[384,768]{1,0:T(8,128)S(1)}, f32[384,768]{1,0:T(8,128)S(1)}, f32[8,128]{1,0:T(8,128)S(1)}) custom-call(f32[256,768]{1,0:T(8,128)S(1)} %get-tuple-element.155.refs_0_, bf16[256,384]{1,0:T(8,128)(2,1)S(1)} %collective-permute-done.12.refs_1_, ...), custom_call_target="tpu_custom_call" | custom-call | bytes 100000000 | tf_op jit(solution)/shard_map/feed_far/pallas_call | solution.py:145
  34.7 2.5 %attention_backward.2 = (bf16[256,768]{1,0:T(8,128)(2,1)S(1)}, bf16[1152,256]{1,0:T(8,128)(2,1)S(1)}, f32[8,128]{1,0:T(8,128)S(1)}) custom-call(bf16[256,768]{1,0:T(8,128)(2,1)S(1)} %get-tuple-element.158.refs_0_.refs_9_, bf16[768,768]{1,0:T(8,128)(2,1)S(1)} %get-tuple-element.153.refs_7_.refs_1_, f32[256,768]{1,0:T(8,128)S(1)} %get-tuple-element.161.refs_2_, ...), custom_call_target="tpu_custom_call" | custom-call | bytes 100000000 | tf_op jit(solution)/shard_map/attention_backward/pallas_call | solution.py:145
  37.3 1.8 %feed_own.1 = (f32[256,768]{1,0:T(8,128)S(1)}, bf16[256,768]{1,0:T(8,128)(2,1)S(1)}, bf16[256,768]{1,0:T(8,128)(2,1)S(1)}, bf16[2,192,768]{2,1,0:T(8,128)(2,1)S(...) custom-call(f32[256,768]{1,0:T(8,128)S(1)} %get-tuple-element.149.refs_0_, ...), custom_call_target="tpu_custom_call" | custom-call | bytes 100000000 | tf_op jit(solution)/shard_map/feed_own/pallas_call | solution.py:145
  39.2 2.5 %attention_backward.3 = (bf16[256,768]{1,0:T(8,128)(2,1)S(1)}, bf16[1152,256]{1,0:T(8,128)(2,1)S(1)}, f32[256,768]{1,0:T(8,128)S(1)}, f32[8,768]{1,0:T(8,128)S(1)}, f32[8,128]{1,0:T(8,128)S(1)}) custom-call(bf16[256,768]{1,0:T(8,128)(2,1)S(1)} %get-tuple-element.170.refs_0_, bf16[768,768]{1,0:T(8,128)(2,1)S(1)} %get-tuple-element.153.refs_7_.refs_1_, ...), custom_call_target="tpu_custom_call" | custom-call | flops 10000000000 | bytes 100000000 | tf_op jit(solution)/shard_map/attention_backward/pallas_call | solution.py:145
  42.2 1.9 %collective-permute-start.15 = (bf16[96,768]{1,0:T(8,128)(2,1)S(1)}, bf16[96,768]{1,0:T(8,128)(2,1)S(1)}, u32[]{:S(2)}, u32[]{:S(2)}) collective-permute-start(bf16[96,768]{1,0:T(8,128)(2,1)S(1)} %get-tuple-element.193), channel_id=1, source_target_pairs={{0,4},{1,9},{2,6},{3,11},{4,0},{5,13},{6,2},{7,15},{8,12},{9,1},{1... | collective-permute-start | bytes 442376 | tf_op jit(solution)/shard_map/ppermute | solution.py:754
  46.2 1.6 %collective-permute-start.17 = (bf16[96,768]{1,0:T(8,128)(2,1)S(1)}, bf16[96,768]{1,0:T(8,128)(2,1)S(1)}, u32[]{:S(2)}, u32[]{:S(2)}) collective-permute-start(bf16[96,768]{1,0:T(8,128)(2,1)S(1)} %get-tuple-element.197), channel_id=1, source_target_pairs={{0,4},{1,9},{2,6},{3,11},{4,0},{5,13},{6,2},{7,15},{8,12},{9,1},{1... | collective-permute-start | bytes 442376 | tf_op jit(solution)/shard_map/ppermute | solution.py:754
  48.3 1.7 %collective-permute-start.18 = (bf16[96,768]{1,0:T(8,128)(2,1)S(1)}, bf16[96,768]{1,0:T(8,128)(2,1)S(1)}, u32[]{:S(2)}, u32[]{:S(2)}) collective-permute-start(bf16[96,768]{1,0:T(8,128)(2,1)S(1)} %get-tuple-element.198), channel_id=1, source_target_pairs={{0,8},{1,5},{2,10},{3,7},{4,12},{5,1},{6,14},{7,3},{8,0},{9,13},{1... | collective-permute-start | bytes 442376 | tf_op jit(solution)/shard_map/ppermute | solution.py:754
  50.7 1.6 %collective-permute-start.16 = (bf16[192,768]{1,0:T(8,128)(2,1)S(1)}, bf16[192,768]{1,0:T(8,128)(2,1)S(1)}, u32[]{:S(2)}, u32[]{:S(2)}) collective-permute-start(bf16[192,768]{1,0:T(8,128)(2,1)S(1)} %get-tuple-element.196), channel_id=1, source_target_pairs={{0,4},{1,9},{2,6},{3,11},{4,0},{5,13},{6,2},{7,15},{8,12},{9,1},{1... | collective-permute-start | bytes 884744 | tf_op jit(solution)/shard_map/ppermute | solution.py:754
  52.3 2.2 %collective-permute-done.18.refs_4_ = bf16[96,768]{1,0:T(8,128)(2,1)S(1)} collective-permute-done((bf16[96,768]{1,0:T(8,128)(2,1)S(1)}, bf16[96,768]{1,0:T(8,128)(2,1)S(1)}, u32[]{:S(2)}, u32[]{:S(2)}) %collective-permute-start.18) | collective-permute-done | bytes 147488 | tf_op jit(solution)/shard_map/ppermute | solution.py:754
  55.2 3.0 %collective-permute-start.22 = (bf16[96,768]{1,0:T(8,128)(2,1)S(1)}, bf16[96,768]{1,0:T(8,128)(2,1)S(1)}, u32[]{:S(2)}, u32[]{:S(2)}) collective-permute-start(bf16[96,768]{1,0:T(8,128)(2,1)S(1)} %get-tuple-element.207.refs_0_), channel_id=1, source_target_pairs={{0,16},{1,17},{2,18},{3,19},{4,20},{5,21},{6,22},{7,23},{8,24},{9,... | collective-permute-start | bytes 442376 | tf_op jit(solution)/shard_map/ppermute | solution.py:754
  58.2 1.4 %collective-permute-start.20 = (bf16[192,768]{1,0:T(8,128)(2,1)S(1)}, bf16[192,768]{1,0:T(8,128)(2,1)S(1)}, u32[]{:S(2)}, u32[]{:S(2)}) collective-permute-start(bf16[192,768]{1,0:T(8,128)(2,1)S(1)} %get-tuple-element.205), channel_id=1, source_target_pairs={{0,4},{1,9},{2,6},{3,11},{4,0},{5,13},{6,2},{7,15},{8,12},{9,1},{1... | collective-permute-start | bytes 884744 | tf_op jit(solution)/shard_map/ppermute | solution.py:754
  60.3 2.0 %collective-permute-start.21 = (bf16[192,768]{1,0:T(8,128)(2,1)S(1)}, bf16[192,768]{1,0:T(8,128)(2,1)S(1)}, u32[]{:S(2)}, u32[]{:S(2)}) collective-permute-start(bf16[192,768]{1,0:T(8,128)(2,1)S(1)} %get-tuple-element.206), channel_id=1, source_target_pairs={{0,8},{1,5},{2,10},{3,7},{4,12},{5,1},{6,14},{7,3},{8,0},{9,13},{1... | collective-permute-start | bytes 884744 | tf_op jit(solution)/shard_map/ppermute | solution.py:754
  62.3 1.4 %input_grads.1 = (f32[256,768]{1,0:T(8,128)S(1)}, bf16[272,768]{1,0:T(8,128)(2,1)S(1)}, f32[8,128]{1,0:T(8,128)S(1)}) custom-call(bf16[1152,256]{1,0:T(8,128)(2,1)S(1)} %get-tuple-element.176.refs_0_.refs_4_.refs_8_, bf16[1152,256]{1,0:T(8,128)(2,1)S(1)} %get-tuple-element.177.refs_1_.refs_5_.refs_9_, ...), custom_call_target="tpu_custom_call" | custom-call | bytes 100000000 | tf_op jit(solution)/shard_map/input_grads/pallas_call | solution.py:145
  63.7 1.6 %collective-permute-start.19 = (bf16[272,768]{1,0:T(8,128)(2,1)S(1)}, bf16[272,768]{1,0:T(8,128)(2,1)S(1)}, u32[]{:S(2)}, u32[]{:S(2)}) collective-permute-start(bf16[272,768]{1,0:T(8,128)(2,1)S(1)} %get-tuple-element.203.refs_0_), channel_id=1, source_target_pairs={{0,2},{1,3},{2,0},{3,1},{4,6},{5,7},{6,4},{7,5},{8,10},{9,11},{10,... | collective-permute-start | bytes 1253384 | tf_op jit(solution)/shard_map/ppermute | solution.py:746
  65.5 2.6 %collective-permute-done.20.refs_3_ = bf16[192,768]{1,0:T(8,128)(2,1)S(1)} collective-permute-done((bf16[192,768]{1,0:T(8,128)(2,1)S(1)}, bf16[192,768]{1,0:T(8,128)(2,1)S(1)}, u32[]{:S(2)}, u32[]{:S(2)}) %collective-permute-start.20) | collective-permute-done | bytes 294944 | tf_op jit(solution)/shard_map/ppermute | solution.py:754
  68.8 0.9 collective-permute-start.23
  69.7 1.4 %collective-permute-start.26 = (bf16[96,768]{1,0:T(8,128)(2,1)S(1)}, bf16[96,768]{1,0:T(8,128)(2,1)S(1)}, u32[]{:S(2)}, u32[]{:S(2)}) collective-permute-start(bf16[96,768]{1,0:T(8,128)(2,1)S(1)} %get-tuple-element.213.refs_1_), channel_id=1, source_target_pairs={{0,4},{1,9},{2,6},{3,11},{4,0},{5,13},{6,2},{7,15},{8,12},{9,1},{1... | collective-permute-start | bytes 442376 | tf_op jit(solution)/shard_map/ppermute | solution.py:754
  71.1 0.9 collective-permute-done.25.refs_2_
  72.1 2.7 %collective-permute-done.26.refs_3_ = bf16[96,768]{1,0:T(8,128)(2,1)S(1)} collective-permute-done((bf16[96,768]{1,0:T(8,128)(2,1)S(1)}, bf16[96,768]{1,0:T(8,128)(2,1)S(1)}, u32[]{:S(2)}, u32[]{:S(2)}) %collective-permute-start.26) | collective-permute-done | bytes 147488 | tf_op jit(solution)/shard_map/ppermute | solution.py:754
  74.9 2.3 %collective-permute-done.27.refs_4_ = bf16[96,768]{1,0:T(8,128)(2,1)S(1)} collective-permute-done((bf16[96,768]{1,0:T(8,128)(2,1)S(1)}, bf16[96,768]{1,0:T(8,128)(2,1)S(1)}, u32[]{:S(2)}, u32[]{:S(2)}) %collective-permute-start.27) | collective-permute-done | bytes 147488 | tf_op jit(solution)/shard_map/ppermute | solution.py:754
  77.1 1.7 %place_sums.3 = (f32[192,768]{1,0:T(8,128)}, f32[192,768]{1,0:T(8,128)}, f32[8,128]{1,0:T(8,128)S(1)}) custom-call(s32[7]{0:T(128)S(1)} %stack.31.refs_0_, bf16[96,768]{1,0:T(8,128)(2,1)S(1)} %get-tuple-element.213.refs_1_, bf16[96,768]{1,0:T(8,128)(2,1)S(1)} %collective-permute-done.25.refs_2_, bf16[96,768]{1,0:T(8,128)(2,1)S(1)} %collective-permute-done.26.refs_3_, ...), custom_call_target="tpu_custom_call" | custom-call | bytes 100000000 | tf_op jit(solution)/shard_map/place_sums/pallas_call | solution.py:145
  78.9 1.4 %collective-permute-start.28 = (bf16[16,768]{1,0:T(8,128)(2,1)S(1)}, bf16[16,768]{1,0:T(8,128)(2,1)S(1)}, u32[]{:S(2)}, u32[]{:S(2)}) collective-permute-start(bf16[16,768]{1,0:T(8,128)(2,1)S(1)} %get-tuple-element.216.refs_2_), channel_id=1, source_target_pairs={{0,16},{1,17},{2,18},{3,19},{4,20},{5,21},{6,22},{7,23},{8,24},{9,... | collective-permute-start | bytes 73736 | tf_op jit(solution)/shard_map/ppermute | solution.py:754
  80.4 3.4 %collective-permute-done.28.refs_3_ = bf16[16,768]{1,0:T(8,128)(2,1)S(1)} collective-permute-done((bf16[16,768]{1,0:T(8,128)(2,1)S(1)}, bf16[16,768]{1,0:T(8,128)(2,1)S(1)}, u32[]{:S(2)}, u32[]{:S(2)}) %collective-permute-start.28) | collective-permute-done | bytes 24608 | tf_op jit(solution)/shard_map/ppermute | solution.py:754
  83.8 0.9 collective-permute-start.29
  84.7 1.3 %input_norm.1 = (bf16[256,768]{1,0:T(8,128)(2,1)}, f32[8,128]{1,0:T(8,128)S(1)}) custom-call(bf16[256,768]{1,0:T(8,128)(2,1)S(1)} %get-tuple-element.126.refs_3_.refs_0_, f32[768]{0:T(1024)S(1)} %get-tuple-element.127.refs_4_.refs_1_, f32[256,768]{1,0:T(8,128)S(1)} %get-tuple-element.202.refs_2_, ...), custom_call_target="tpu_custom_call" | custom-call | bytes 100000000 | tf_op jit(solution)/shard_map/input_norm/pallas_call | solution.py:145
  86.0 1.2 %feed_result.1 = (bf16[256,768]{1,0:T(8,128)(2,1)}, f32[8,128]{1,0:T(8,128)S(1)}) custom-call(bf16[256,768]{1,0:T(8,128)(2,1)S(1)} %get-tuple-element.168.refs_0_, bf16[768,768]{1,0:T(8,128)(2,1)S(1)} %get-tuple-element.147.refs_7_.refs_1_, f32[256,768]{1,0:T(8,128)S(1)} %get-tuple-element.169.refs_2_, f32[8,128]{1,0:T(8,128)S(1)} %get-tuple-element.219.refs_3_), custom_call_target="tpu_custom_call" | custom-call | bytes 100000000 | tf_op jit(solution)/shard_map/feed_result/pallas_call | solution.py:145
  87.3 1.4 %collective-permute-start.30 = (bf16[208,768]{1,0:T(8,128)(2,1)S(1)}, bf16[208,768]{1,0:T(8,128)(2,1)S(1)}, u32[]{:S(2)}, u32[]{:S(2)}) collective-permute-start(bf16[208,768]{1,0:T(8,128)(2,1)S(1)} %get-tuple-element.224.refs_1_), channel_id=1, source_target_pairs={{0,4},{1,9},{2,6},{3,11},{4,0},{5,13},{6,2},{7,15},{8,12},{9,1},{1... | collective-permute-start | bytes 958472 | tf_op jit(solution)/shard_map/ppermute | solution.py:754
  88.7 2.2 %collective-permute-done.29.refs_2_ = bf16[208,768]{1,0:T(8,128)(2,1)S(1)} collective-permute-done((bf16[208,768]{1,0:T(8,128)(2,1)S(1)}, bf16[208,768]{1,0:T(8,128)(2,1)S(1)}, u32[]{:S(2)}, u32[]{:S(2)}) %collective-permute-start.29) | collective-permute-done | bytes 319520 | tf_op jit(solution)/shard_map/ppermute | solution.py:754
  91.6 2.7 %collective-permute-done.30.refs_3_ = bf16[208,768]{1,0:T(8,128)(2,1)S(1)} collective-permute-done((bf16[208,768]{1,0:T(8,128)(2,1)S(1)}, bf16[208,768]{1,0:T(8,128)(2,1)S(1)}, u32[]{:S(2)}, u32[]{:S(2)}) %collective-permute-start.30) | collective-permute-done | bytes 319520 | tf_op jit(solution)/shard_map/ppermute | solution.py:754
  94.3 1.9 %place_sums.4 = (f32[3,192,768]{2,1,0:T(8,128)}, f32[192,768]{1,0:T(8,128)}, f32[8,128]{1,0:T(8,128)S(1)}) custom-call(s32[7]{0:T(128)S(1)} %stack.31.refs_0_, bf16[208,768]{1,0:T(8,128)(2,1)S(1)} %get-tuple-element.224.refs_1_, bf16[208,768]{1,0:T(8,128)(2,1)S(1)} %collective-permute-done.29.refs_2_, bf16[208,768]{1,0:T(8,128)(2,1)S(1)} %collective-permute-done.30.refs_3_, ...), custom_call_target="tpu_custom_call" | custom-call | bytes 100000000 | tf_op jit(solution)/shard_map/place_sums/pallas_call | solution.py:145
  96.2 1.6 %collective-permute-done.31.refs_4_ = bf16[208,768]{1,0:T(8,128)(2,1)S(1)} collective-permute-done((bf16[208,768]{1,0:T(8,128)(2,1)S(1)}, bf16[208,768]{1,0:T(8,128)(2,1)S(1)}, u32[]{:S(2)}, u32[]{:S(2)}) %collective-permute-start.31) | collective-permute-done | bytes 319520 | tf_op jit(solution)/shard_map/ppermute | solution.py:754
  97.8 1.5 %place_sums.5 = (f32[3,192,768]{2,1,0:T(8,128)}, f32[192,768]{1,0:T(8,128)}, f32[768]{0:T(1024)}, f32[768]{0:T(1024)}, f32[768]{0:T(1024)}, /*index=5*/f32[768]{0:T(1024)}, f32[192]{0:T(256)}) custom-call(s32[7]{0:T(128)S(1)} %stack.31.refs_0_, bf16[208,768]{1,0:T(8,128)(2,1)S(1)} %get-tuple-element.224.refs_1_, ...), custom_call_target="tpu_custom_call", output_to_operand_aliasing={{0}: (5, {}), {1}: (6, {})} | custom-call | flops 6000000000 | bytes 100000000 | tf_op jit(solution)/shard_map/place_sums/pallas_call | solution.py:145
  (50 shorter events, 10.1 us)
Async XLA Ops:
  0.6 6.6 %collective-permute-start.1 = (bf16[3,192,768]{2,1,0:T(8,128)(2,1)}, bf16[3,192,768]{2,1,0:T(8,128)(2,1)S(1)}, u32[]{:S(2)}, u32[]{:S(2)}) collective-permute-start(bf16[3,192,768]{2,1,0:T(8,128)(2,1)} %refs_6_.3), channel_id=1, source_target_pairs={{0,1},{1,0},{2,3},{3,2},{4,5},{5,4},{6,7},{7,6},{8,9},{9,8},{10,11... | collective-permute-start | bytes 2654216 | tf_op jit(solution)/shard_map/ppermute | solution.py:743
  2.8 9.1 %collective-permute-start.3 = (bf16[448,256]{1,0:T(8,128)(2,1)S(1)}, bf16[448,256]{1,0:T(8,128)(2,1)S(1)}, u32[]{:S(2)}, u32[]{:S(2)}) collective-permute-start(bf16[448,256]{1,0:T(8,128)(2,1)S(1)} %get-tuple-element.124.refs_3_), channel_id=1, source_target_pairs={{0,2},{1,3},{2,0},{3,1},{4,6},{5,7},{6,4},{7,5},{8,10},{9,11},{10,... | collective-permute-start | bytes 688136 | tf_op jit(solution)/shard_map/ppermute | solution.py:746
  5.5 16.7 %collective-permute-start = (bf16[256,768]{1,0:T(8,128)(2,1)}, bf16[256,768]{1,0:T(8,128)(2,1)S(1)}, u32[]{:S(2)}, u32[]{:S(2)}) collective-permute-start(bf16[256,768]{1,0:T(8,128)(2,1)} %refs_4_.3), channel_id=1, source_target_pairs={{0,2},{1,3},{2,0},{3,1},{4,6},{5,7},{6,4},{7,5},{8,10},{9,11},{10,... | collective-permute-start | bytes 1179656 | tf_op jit(solution)/shard_map/ppermute | solution.py:746
  7.1 15.9 %collective-permute-start.2 = (bf16[592,768]{1,0:T(8,128)(2,1)S(1)}, bf16[592,768]{1,0:T(8,128)(2,1)S(1)}, u32[]{:S(2)}, u32[]{:S(2)}) collective-permute-start(bf16[592,768]{1,0:T(8,128)(2,1)S(1)} %get-tuple-element.132.refs_7_.refs_8_), channel_id=1, source_target_pairs={{0,1},{1,0},{2,3},{3,2},{4,5},{5,4},{6,7},{7,6},{8,9},{9,8},{10,11... | collective-permute-start | bytes 2727944 | tf_op jit(solution)/shard_map/ppermute | solution.py:743
  7.3 8.3 %copy-start = (bf16[256,768]{1,0:T(8,128)(2,1)S(1)}, bf16[256,768]{1,0:T(8,128)(2,1)}, u32[]{:S(2)}) copy-start(bf16[256,768]{1,0:T(8,128)(2,1)} %refs_5_.1) | copy-start | bytes 1179652
  12.0 7.2 %collective-permute-start.4 = (bf16[144,768]{1,0:T(8,128)(2,1)S(1)}, bf16[144,768]{1,0:T(8,128)(2,1)S(1)}, u32[]{:S(2)}, u32[]{:S(2)}) collective-permute-start(bf16[144,768]{1,0:T(8,128)(2,1)S(1)} %get-tuple-element.134), channel_id=1, source_target_pairs={{0,4},{1,5},{2,6},{3,7},{4,0},{5,1},{6,2},{7,3},{8,12},{9,13},{10,... | collective-permute-start | bytes 663560 | tf_op jit(solution)/shard_map/ppermute | solution.py:754
  13.9 6.8 %collective-permute-start.5 = (bf16[144,768]{1,0:T(8,128)(2,1)S(1)}, bf16[144,768]{1,0:T(8,128)(2,1)S(1)}, u32[]{:S(2)}, u32[]{:S(2)}) collective-permute-start(bf16[144,768]{1,0:T(8,128)(2,1)S(1)} %get-tuple-element.134), channel_id=1, source_target_pairs={{0,8},{1,9},{2,10},{3,11},{4,12},{5,13},{6,14},{7,15},{8,0},{9,1},... | collective-permute-start | bytes 663560 | tf_op jit(solution)/shard_map/ppermute | solution.py:754
  15.5 15.6 %collective-permute-start.6 = (bf16[256,768]{1,0:T(8,128)(2,1)S(1)}, bf16[256,768]{1,0:T(8,128)(2,1)S(1)}, u32[]{:S(2)}, u32[]{:S(2)}) collective-permute-start(bf16[256,768]{1,0:T(8,128)(2,1)S(1)} %copy-done), channel_id=1, source_target_pairs={{0,2},{1,3},{2,0},{3,1},{4,6},{5,7},{6,4},{7,5},{8,10},{9,11},{10,... | collective-permute-start | bytes 1179656 | tf_op jit(solution)/shard_map/ppermute | solution.py:746
  19.2 7.3 %collective-permute-start.8 = (bf16[160,768]{1,0:T(8,128)(2,1)S(1)}, bf16[160,768]{1,0:T(8,128)(2,1)S(1)}, u32[]{:S(2)}, u32[]{:S(2)}) collective-permute-start(bf16[160,768]{1,0:T(8,128)(2,1)S(1)} %get-tuple-element.142.refs_4_.refs_10_), channel_id=1, source_target_pairs={{0,1},{1,0},{2,3},{3,2},{4,5},{5,4},{6,7},{7,6},{8,9},{9,8},{10,11... | collective-permute-start | bytes 737288 | tf_op jit(solution)/shard_map/ppermute | solution.py:743
  20.6 12.4 %collective-permute-start.12 = (bf16[256,384]{1,0:T(8,128)(2,1)S(1)}, bf16[256,384]{1,0:T(8,128)(2,1)S(1)}, u32[]{:S(2)}, u32[]{:S(2)}) collective-permute-start(bf16[256,384]{1,0:T(8,128)(2,1)S(1)} %get-tuple-element.130.refs_2_), channel_id=1, source_target_pairs={{0,2},{1,3},{2,0},{3,1},{4,6},{5,7},{6,4},{7,5},{8,10},{9,11},{10,... | collective-permute-start | bytes 589832 | tf_op jit(solution)/shard_map/ppermute | solution.py:746
  22.2 6.5 %collective-permute-start.7 = (bf16[144,768]{1,0:T(8,128)(2,1)S(1)}, bf16[144,768]{1,0:T(8,128)(2,1)S(1)}, u32[]{:S(2)}, u32[]{:S(2)}) collective-permute-start(bf16[144,768]{1,0:T(8,128)(2,1)S(1)} %get-tuple-element.144), channel_id=1, source_target_pairs={{0,4},{1,5},{2,6},{3,7},{4,0},{5,1},{6,2},{7,3},{8,12},{9,13},{10,... | collective-permute-start | bytes 663560 | tf_op jit(solution)/shard_map/ppermute | solution.py:754
  22.9 7.3 %collective-permute-start.9 = (bf16[2,144,768]{2,1,0:T(8,128)(2,1)S(1)}, bf16[2,144,768]{2,1,0:T(8,128)(2,1)S(1)}, u32[]{:S(2)}, u32[]{:S(2)}) collective-permute-start(bf16[2,144,768]{2,1,0:T(8,128)(2,1)S(1)} %get-tuple-element.143.refs_5_), channel_id=1, source_target_pairs={{0,1},{1,0},{2,3},{3,2},{4,5},{5,4},{6,7},{7,6},{8,9},{9,8},{10,11... | collective-permute-start | bytes 1327112 | tf_op jit(solution)/shard_map/ppermute | solution.py:743
  26.5 10.8 %collective-permute-start.11 = (bf16[256,384]{1,0:T(8,128)(2,1)S(1)}, bf16[256,384]{1,0:T(8,128)(2,1)S(1)}, u32[]{:S(2)}, u32[]{:S(2)}) collective-permute-start(bf16[256,384]{1,0:T(8,128)(2,1)S(1)} %get-tuple-element.137.refs_3_), channel_id=1, source_target_pairs={{0,2},{1,3},{2,0},{3,1},{4,6},{5,7},{6,4},{7,5},{8,10},{9,11},{10,... | collective-permute-start | bytes 589832 | tf_op jit(solution)/shard_map/ppermute | solution.py:746
  28.8 1.5 %collective-permute-start.10 = (bf16[144,768]{1,0:T(8,128)(2,1)S(1)}, bf16[144,768]{1,0:T(8,128)(2,1)S(1)}, u32[]{:S(2)}, u32[]{:S(2)}) collective-permute-start(bf16[144,768]{1,0:T(8,128)(2,1)S(1)} %collective-permute-done.7.refs_6_), channel_id=1, source_target_pairs={{0,1},{1,0},{2,3},{3,2},{4,5},{5,4},{6,7},{7,6},{8,9},{9,8},{10,11... | collective-permute-start | bytes 663560 | tf_op jit(solution)/shard_map/ppermute | solution.py:743
  39.1 2.6 %collective-permute-start.13 = (bf16[2,192,768]{2,1,0:T(8,128)(2,1)S(1)}, bf16[2,192,768]{2,1,0:T(8,128)(2,1)S(1)}, u32[]{:S(2)}, u32[]{:S(2)}) collective-permute-start(bf16[2,192,768]{2,1,0:T(8,128)(2,1)S(1)} %get-tuple-element.187), channel_id=1, source_target_pairs={{0,1},{1,0},{2,3},{3,2},{4,5},{5,4},{6,7},{7,6},{8,9},{9,8},{10,11... | collective-permute-start | bytes 1769480 | tf_op jit(solution)/shard_map/ppermute | solution.py:743
  42.2 5.5 %collective-permute-start.15 = (bf16[96,768]{1,0:T(8,128)(2,1)S(1)}, bf16[96,768]{1,0:T(8,128)(2,1)S(1)}, u32[]{:S(2)}, u32[]{:S(2)}) collective-permute-start(bf16[96,768]{1,0:T(8,128)(2,1)S(1)} %get-tuple-element.193), channel_id=1, source_target_pairs={{0,4},{1,9},{2,6},{3,11},{4,0},{5,13},{6,2},{7,15},{8,12},{9,1},{1... | collective-permute-start | bytes 442376 | tf_op jit(solution)/shard_map/ppermute | solution.py:754
  45.8 4.3 %collective-permute-start.14 = (bf16[4,192,768]{2,1,0:T(8,128)(2,1)S(1)}, bf16[4,192,768]{2,1,0:T(8,128)(2,1)S(1)}, u32[]{:S(2)}, u32[]{:S(2)}) collective-permute-start(bf16[4,192,768]{2,1,0:T(8,128)(2,1)S(1)} %get-tuple-element.192), channel_id=1, source_target_pairs={{0,1},{1,0},{2,3},{3,2},{4,5},{5,4},{6,7},{7,6},{8,9},{9,8},{10,11... | collective-permute-start | bytes 3538952 | tf_op jit(solution)/shard_map/ppermute | solution.py:743
  46.2 6.2 %collective-permute-start.17 = (bf16[96,768]{1,0:T(8,128)(2,1)S(1)}, bf16[96,768]{1,0:T(8,128)(2,1)S(1)}, u32[]{:S(2)}, u32[]{:S(2)}) collective-permute-start(bf16[96,768]{1,0:T(8,128)(2,1)S(1)} %get-tuple-element.197), channel_id=1, source_target_pairs={{0,4},{1,9},{2,6},{3,11},{4,0},{5,13},{6,2},{7,15},{8,12},{9,1},{1... | collective-permute-start | bytes 442376 | tf_op jit(solution)/shard_map/ppermute | solution.py:754
  48.3 6.2 %collective-permute-start.18 = (bf16[96,768]{1,0:T(8,128)(2,1)S(1)}, bf16[96,768]{1,0:T(8,128)(2,1)S(1)}, u32[]{:S(2)}, u32[]{:S(2)}) collective-permute-start(bf16[96,768]{1,0:T(8,128)(2,1)S(1)} %get-tuple-element.198), channel_id=1, source_target_pairs={{0,8},{1,5},{2,10},{3,7},{4,12},{5,1},{6,14},{7,3},{8,0},{9,13},{1... | collective-permute-start | bytes 442376 | tf_op jit(solution)/shard_map/ppermute | solution.py:754
  50.7 8.9 %collective-permute-start.16 = (bf16[192,768]{1,0:T(8,128)(2,1)S(1)}, bf16[192,768]{1,0:T(8,128)(2,1)S(1)}, u32[]{:S(2)}, u32[]{:S(2)}) collective-permute-start(bf16[192,768]{1,0:T(8,128)(2,1)S(1)} %get-tuple-element.196), channel_id=1, source_target_pairs={{0,4},{1,9},{2,6},{3,11},{4,0},{5,13},{6,2},{7,15},{8,12},{9,1},{1... | collective-permute-start | bytes 884744 | tf_op jit(solution)/shard_map/ppermute | solution.py:754
  55.2 10.1 %collective-permute-start.22 = (bf16[96,768]{1,0:T(8,128)(2,1)S(1)}, bf16[96,768]{1,0:T(8,128)(2,1)S(1)}, u32[]{:S(2)}, u32[]{:S(2)}) collective-permute-start(bf16[96,768]{1,0:T(8,128)(2,1)S(1)} %get-tuple-element.207.refs_0_), channel_id=1, source_target_pairs={{0,16},{1,17},{2,18},{3,19},{4,20},{5,21},{6,22},{7,23},{8,24},{9,... | collective-permute-start | bytes 442376 | tf_op jit(solution)/shard_map/ppermute | solution.py:754
  58.2 9.9 %collective-permute-start.20 = (bf16[192,768]{1,0:T(8,128)(2,1)S(1)}, bf16[192,768]{1,0:T(8,128)(2,1)S(1)}, u32[]{:S(2)}, u32[]{:S(2)}) collective-permute-start(bf16[192,768]{1,0:T(8,128)(2,1)S(1)} %get-tuple-element.205), channel_id=1, source_target_pairs={{0,4},{1,9},{2,6},{3,11},{4,0},{5,13},{6,2},{7,15},{8,12},{9,1},{1... | collective-permute-start | bytes 884744 | tf_op jit(solution)/shard_map/ppermute | solution.py:754
  60.3 7.8 %collective-permute-start.21 = (bf16[192,768]{1,0:T(8,128)(2,1)S(1)}, bf16[192,768]{1,0:T(8,128)(2,1)S(1)}, u32[]{:S(2)}, u32[]{:S(2)}) collective-permute-start(bf16[192,768]{1,0:T(8,128)(2,1)S(1)} %get-tuple-element.206), channel_id=1, source_target_pairs={{0,8},{1,5},{2,10},{3,7},{4,12},{5,1},{6,14},{7,3},{8,0},{9,13},{1... | collective-permute-start | bytes 884744 | tf_op jit(solution)/shard_map/ppermute | solution.py:754
  63.7 8.3 %collective-permute-start.19 = (bf16[272,768]{1,0:T(8,128)(2,1)S(1)}, bf16[272,768]{1,0:T(8,128)(2,1)S(1)}, u32[]{:S(2)}, u32[]{:S(2)}) collective-permute-start(bf16[272,768]{1,0:T(8,128)(2,1)S(1)} %get-tuple-element.203.refs_0_), channel_id=1, source_target_pairs={{0,2},{1,3},{2,0},{3,1},{4,6},{5,7},{6,4},{7,5},{8,10},{9,11},{10,... | collective-permute-start | bytes 1253384 | tf_op jit(solution)/shard_map/ppermute | solution.py:746
  65.4 6.6 %collective-permute-start.25 = (bf16[96,768]{1,0:T(8,128)(2,1)S(1)}, bf16[96,768]{1,0:T(8,128)(2,1)S(1)}, u32[]{:S(2)}, u32[]{:S(2)}) collective-permute-start(bf16[96,768]{1,0:T(8,128)(2,1)S(1)} %get-tuple-element.213.refs_1_), channel_id=1, source_target_pairs={{0,8},{1,5},{2,10},{3,7},{4,12},{5,1},{6,14},{7,3},{8,0},{9,13},{1... | collective-permute-start | bytes 442376 | tf_op jit(solution)/shard_map/ppermute | solution.py:754
  68.8 14.9 %collective-permute-start.23 = (bf16[192,768]{1,0:T(8,128)(2,1)S(1)}, bf16[192,768]{1,0:T(8,128)(2,1)S(1)}, u32[]{:S(2)}, u32[]{:S(2)}) collective-permute-start(bf16[192,768]{1,0:T(8,128)(2,1)S(1)} %get-tuple-element.210.refs_0_), channel_id=1, source_target_pairs={{0,16},{1,17},{2,18},{3,19},{4,20},{5,21},{6,22},{7,23},{8,24},{9,... | collective-permute-start | bytes 884744 | tf_op jit(solution)/shard_map/ppermute | solution.py:754
  69.7 5.1 %collective-permute-start.26 = (bf16[96,768]{1,0:T(8,128)(2,1)S(1)}, bf16[96,768]{1,0:T(8,128)(2,1)S(1)}, u32[]{:S(2)}, u32[]{:S(2)}) collective-permute-start(bf16[96,768]{1,0:T(8,128)(2,1)S(1)} %get-tuple-element.213.refs_1_), channel_id=1, source_target_pairs={{0,4},{1,9},{2,6},{3,11},{4,0},{5,13},{6,2},{7,15},{8,12},{9,1},{1... | collective-permute-start | bytes 442376 | tf_op jit(solution)/shard_map/ppermute | solution.py:754
  72.0 5.1 %collective-permute-start.27 = (bf16[96,768]{1,0:T(8,128)(2,1)S(1)}, bf16[96,768]{1,0:T(8,128)(2,1)S(1)}, u32[]{:S(2)}, u32[]{:S(2)}) collective-permute-start(bf16[96,768]{1,0:T(8,128)(2,1)S(1)} %collective-permute-done.25.refs_2_), channel_id=1, source_target_pairs={{0,4},{1,9},{2,6},{3,11},{4,0},{5,13},{6,2},{7,15},{8,12},{9,1},{1... | collective-permute-start | bytes 442376 | tf_op jit(solution)/shard_map/ppermute | solution.py:754
  72.0 6.8 %collective-permute-start.24 = (bf16[16,768]{1,0:T(8,128)(2,1)S(1)}, bf16[16,768]{1,0:T(8,128)(2,1)S(1)}, u32[]{:S(2)}, u32[]{:S(2)}) collective-permute-start(bf16[16,768]{1,0:T(8,128)(2,1)S(1)} %get-tuple-element.212.refs_0_), channel_id=1, source_target_pairs={{0,1},{1,0},{2,3},{3,2},{4,5},{5,4},{6,7},{7,6},{8,9},{9,8},{10,11... | collective-permute-start | bytes 73736 | tf_op jit(solution)/shard_map/ppermute | solution.py:743
  78.9 4.8 %collective-permute-start.28 = (bf16[16,768]{1,0:T(8,128)(2,1)S(1)}, bf16[16,768]{1,0:T(8,128)(2,1)S(1)}, u32[]{:S(2)}, u32[]{:S(2)}) collective-permute-start(bf16[16,768]{1,0:T(8,128)(2,1)S(1)} %get-tuple-element.216.refs_2_), channel_id=1, source_target_pairs={{0,16},{1,17},{2,18},{3,19},{4,20},{5,21},{6,22},{7,23},{8,24},{9,... | collective-permute-start | bytes 73736 | tf_op jit(solution)/shard_map/ppermute | solution.py:754
  83.8 7.1 %collective-permute-start.29 = (bf16[208,768]{1,0:T(8,128)(2,1)S(1)}, bf16[208,768]{1,0:T(8,128)(2,1)S(1)}, u32[]{:S(2)}, u32[]{:S(2)}) collective-permute-start(bf16[208,768]{1,0:T(8,128)(2,1)S(1)} %get-tuple-element.224.refs_1_), channel_id=1, source_target_pairs={{0,8},{1,5},{2,10},{3,7},{4,12},{5,1},{6,14},{7,3},{8,0},{9,13},{1... | collective-permute-start | bytes 958472 | tf_op jit(solution)/shard_map/ppermute | solution.py:754
  87.3 7.1 %collective-permute-start.30 = (bf16[208,768]{1,0:T(8,128)(2,1)S(1)}, bf16[208,768]{1,0:T(8,128)(2,1)S(1)}, u32[]{:S(2)}, u32[]{:S(2)}) collective-permute-start(bf16[208,768]{1,0:T(8,128)(2,1)S(1)} %get-tuple-element.224.refs_1_), channel_id=1, source_target_pairs={{0,4},{1,9},{2,6},{3,11},{4,0},{5,13},{6,2},{7,15},{8,12},{9,1},{1... | collective-permute-start | bytes 958472 | tf_op jit(solution)/shard_map/ppermute | solution.py:754
  90.8 7.0 %collective-permute-start.31 = (bf16[208,768]{1,0:T(8,128)(2,1)S(1)}, bf16[208,768]{1,0:T(8,128)(2,1)S(1)}, u32[]{:S(2)}, u32[]{:S(2)}) collective-permute-start(bf16[208,768]{1,0:T(8,128)(2,1)S(1)} %collective-permute-done.29.refs_2_), channel_id=1, source_target_pairs={{0,4},{1,9},{2,6},{3,11},{4,0},{5,13},{6,2},{7,15},{8,12},{9,1},{1... | collective-permute-start | bytes 958472 | tf_op jit(solution)/shard_map/ppermute | solution.py:754
